TPU v7x, 32 devices: a whole 2x2x4 slice. The times are simulated.
32 devices in a mesh: groups: 2 (over y), blk: 4 (over z), ops: 2 (over x), sub: 2 (over core).
Axes of the slice: x: 2, y: 2, z: 4, core: 2. Of those that a mesh axis runs over, the one named last changes fastest.
Arguments:
- theta: bfloat16 [4, 2048, 2048], P('groups', ('blk', 'sub')), parts along dimension 0, may hold values from -6 to 6
- hdiag: bfloat16 [4096, 2048], P(('groups', 'blk', 'sub')), parts along dimension 0, may hold values from -1 to 7
- pattern: int32 [32, 16], P('groups'), parts along dimension 0, may hold values 0 or 1
- left_blocks: bfloat16 [4, 16, 3, 128, 128], P(('groups', 'ops')), parts along dimension 0, may hold values from -0.21875 to 0.21875
- left_cols: int32 [4, 16, 3], P(('groups', 'ops')), parts along dimension 0, may hold values from 0 to 15, as said below
- right_blocks: bfloat16 [4, 16, 3, 128, 128], P(('groups', 'ops')), parts along dimension 0, may hold values from -0.3125 to 0.3125
- right_cols: int32 [4, 16, 3], P(('groups', 'ops')), parts along dimension 0, may hold values from 0 to 15, as said below
Outputs:
- correction: bfloat16 [4, 2048, 2048], P('groups', ('blk', 'sub')), parts along dimension 0
- sigma_two: bfloat16 [4, 2048, 2048], P('groups', ('blk', 'sub')), parts along dimension 0
- subspace: float32 [4, 4], P('groups'), parts along dimension 0
There are 2 independent parts, one for each index of `groups`. A program takes and returns all parts, laid end to end along the dimension named above; each array names one. Nothing has to cross between parts.
Inputs may be any that keep to these rules, and one draw needn't show every extreme that they name: pattern is 1 where a block of the wavefunction is allowed by the symmetry. `left_cols`: the 3 block columns of each block row of a term are distinct. `right_cols`: the 3 block columns of each block row of a term are distinct.
All inputs are finite; a program needn't handle non-finite values.
Results may differ from a plain program's by a relative error of at most 0.0048.
The roundings to bfloat16 on the way count: a program that leaves them out, or rounds other values in their place, can miss the bound.
Values may be sent and summed in bfloat16 or wider, within the bound.
No kernel may reach another device: no remote copies, remote signals or barrier semaphores. Data moves between devices by JAX's collectives and lax.ppermute only.
A program may use at most 128 MiB of HBM per device.

v0:
```python
import jax
import jax.numpy as jnp
from jax import lax
from jax.sharding import PartitionSpec as P


def apply_right(field_in, blocks, columns):
    roots_here, row_count, full_width = field_in.shape
    term_count, sectors, link_count = columns.shape
    block_size = full_width // sectors
    grouped = field_in.reshape(roots_here, row_count, sectors, block_size)
    picked = jnp.take(grouped, columns.reshape(-1), axis=2)
    picked = picked.reshape(roots_here, row_count, term_count, sectors, link_count, block_size)
    product = jnp.einsum("nrkbjq,kbjpq->knrbp", picked, blocks, preferred_element_type=jnp.float32)
    return product.reshape(term_count, roots_here, row_count, full_width).astype(jnp.bfloat16)


def take_rows(stacked, indices):
    return jnp.take(stacked, indices, axis=1)


def apply_left(arrived, blocks, columns):
    term_count, roots_here, full_width, col_count = arrived.shape
    sectors = columns.shape[1]
    link_count = columns.shape[2]
    block_size = full_width // sectors
    grouped = arrived.reshape(term_count, roots_here, sectors, block_size, col_count)
    picked = jax.vmap(take_rows)(grouped, columns.reshape(term_count, sectors * link_count))
    picked = picked.reshape(term_count, roots_here, sectors, link_count, block_size, col_count)
    product = jnp.einsum("kajpq,knajqc->napc", blocks, picked, preferred_element_type=jnp.float32)
    return product.reshape(roots_here, full_width, col_count)


def shards(theta, hdiag, pattern, left_blocks, left_cols, right_blocks, right_cols):
    roots_here, row_count, full_width = theta.shape
    sectors = pattern.shape[0]
    block_size = full_width // sectors
    first_row = lax.axis_index(("blk", "sub")) * row_count
    block_row = (first_row + jnp.arange(row_count, dtype=jnp.int32)) // block_size
    onehot = (block_row[:, None] == jnp.arange(sectors, dtype=jnp.int32)[None, :]).astype(
        jnp.float32
    )
    row_pattern = jnp.dot(onehot, pattern.astype(jnp.float32), preferred_element_type=jnp.float32)
    allowed = jnp.broadcast_to(row_pattern[:, :, None], (row_count, sectors, block_size))
    allowed = allowed.reshape(row_count, full_width).astype(jnp.bfloat16)
    diagonal = hdiag.astype(jnp.float32)
    peers = lax.axis_size("blk") * lax.axis_size("sub")

    def left_part(arrived):
        return apply_left(arrived, left_blocks, left_cols)

    def operate(field_in):
        images = apply_right(field_in, right_blocks, right_cols)
        partial_sum = left_part(
            lax.all_to_all(images, ("blk", "sub"), split_axis=3, concat_axis=2, tiled=True)
        )
        shares = lax.psum_scatter(partial_sum, "ops", scatter_dimension=2, tiled=True)
        returned = lax.all_to_all(
            shares.astype(jnp.bfloat16), ("blk", "sub"), split_axis=1, concat_axis=2, tiled=True
        )
        gathered = lax.all_gather(returned, "ops", axis=2, tiled=True)
        narrow = returned.shape[2] // peers
        gathered = gathered.reshape(roots_here, row_count, lax.axis_size("ops"), peers, narrow)
        offdiag = gathered.transpose(0, 1, 3, 2, 4).reshape(roots_here, row_count, full_width)
        offdiag = offdiag * allowed[None]
        return diagonal[None] * field_in.astype(jnp.float32) + offdiag.astype(jnp.float32)

    projected = theta * allowed[None]
    wave = projected.astype(jnp.float32)
    sigma_one = operate(projected)
    norm_sq, energy_sum = lax.psum(
        (jnp.sum(wave * wave, axis=(1, 2)), jnp.sum(wave * sigma_one, axis=(1, 2))), ("blk", "sub")
    )
    denominator = norm_sq + 1e-06
    energy = energy_sum / denominator
    shifted = diagonal[None] - energy[:, None, None]
    update = (sigma_one - energy[:, None, None] * wave) * shifted / (shifted * shifted + 1.0)
    correlation = lax.psum(jnp.sum(wave * update, axis=(1, 2)), ("blk", "sub"))
    factor = correlation / denominator
    orthogonal = update - factor[:, None, None] * wave
    length_sq = lax.psum(jnp.sum(orthogonal * orthogonal, axis=(1, 2)), ("blk", "sub"))
    correction = (orthogonal * jnp.sqrt(norm_sq / (length_sq + 1e-06))[:, None, None]).astype(
        jnp.bfloat16
    )
    sigma_two = operate(correction).astype(jnp.bfloat16)
    second = sigma_two.astype(jnp.float32)
    fixed = correction.astype(jnp.float32)
    cross_one, cross_two, cross_three = lax.psum(
        (
            jnp.sum(wave * second, axis=(1, 2)),
            jnp.sum(fixed * sigma_one, axis=(1, 2)),
            jnp.sum(fixed * second, axis=(1, 2)),
        ),
        ("blk", "sub"),
    )
    subspace = (
        jnp.stack([energy_sum, cross_one, cross_two, cross_three], axis=1) / denominator[:, None]
    )
    return (correction, sigma_two, subspace)


def solution(mesh):
    in_specs = (
        P("groups", ("blk", "sub"), None),
        P(("groups", "blk", "sub"), None),
        P("groups", None),
        P(("groups", "ops"), None, None, None, None),
        P(("groups", "ops"), None, None),
        P(("groups", "ops"), None, None, None, None),
        P(("groups", "ops"), None, None),
    )
    out_specs = (
        P("groups", ("blk", "sub"), None),
        P("groups", ("blk", "sub"), None),
        P("groups", None),
    )
    return jax.shard_map(shards, mesh=mesh, in_specs=in_specs, out_specs=out_specs, check_vma=False)
```

profile of v0, /device:TPU:0, one launch (start us, length us, event | category | flops | bytes accessed | tf_op | source)
XLA Modules:
  0.0 580.3 jit_solution(9859389454570310325)
XLA Ops:
  8.2 3.9 copy.89
  15.6 4.0 copy.92
  19.5 6.5 %gather_fusion = bf16[48,2,256,128]{3,2,1,0:T(8,128)(2,1)} fusion(bf16[2,256,16,128]{3,1,2,0:T(8,128)(2,1)} %copy.92, s32[1024]{0:T(1024)S(1)} %pad_clamp_fusion), kind=kCustom, calls=%fused_computation.clone | custom fusion | bytes 12583104 | tf_op jit(solution)/shard_map/jit(_take)/gather | solution.py:12
  31.8 14.0 %copy.96 = bf16[1,2,256,2048]{2,1,0,3:T(2,128)(2,1)} copy(bf16[1,2,256,2048]{2,3,1,0:T(8,128)(2,1)S(1)} %bitcast.156) | data formatting | bytes 4194304 | tf_op jit(solution)/shard_map/convert_element_type | solution.py:15
  45.8 6.3 %all-to-all-start = ((bf16[1,2,256,2048]{2,1,0,3:T(2,128)(2,1)}), bf16[1,2,256,2048]{2,1,0,3:T(2,128)(2,1)}, u32[]{:S(2)}, u32[]{:S(2)}) async-start(bf16[1,2,256,2048]{2,1,0,3:T(2,128)(2,1)} %copy.96), calls=%async_computation | async-start | bytes 4194304 | tf_op jit(solution)/shard_map/all_to_all | solution.py:55
  52.6 48.7 %all-to-all-done = bf16[1,2,256,2048]{2,1,0,3:T(2,128)(2,1)} async-done(((bf16[1,2,256,2048]{2,1,0,3:T(2,128)(2,1)}), bf16[1,2,256,2048]{2,1,0,3:T(2,128)(2,1)}, u32[]{:S(2)}, u32[]{:S(2)}) %all-to-all-start) | async-done | bytes 2097184 | tf_op jit(solution)/shard_map/all_to_all | solution.py:55
  104.5 3.9 copy.98
  108.5 6.6 %gather_fusion.1 = bf16[48,2,128,256]{3,2,1,0:T(8,128)(2,1)} fusion(bf16[1,2,16,128,256]{4,3,2,1,0:T(8,128)(2,1)} %bitcast.149, s32[48]{0:T(128)S(1)} %or_bitcast_fusion), kind=kCustom, calls=%fused_computation.1.clone | custom fusion | bytes 12583296 | tf_op jit(solution)/shard_map/vmap(jit(_take))/gather | solution.py:19
  122.3 53.3 %reduce-scatter.3.cloned.1.call-done = f32[2,2048,128]{2,1,0:T(8,128)} async-done(((f32[2,2048,256]{2,1,0:T(8,128)}), f32[2,2048,128]{2,1,0:T(8,128)}) %reduce-scatter.3.cloned.1.call-update) | async-done | bytes 2097168 | tf_op jit(solution)/shard_map/reduce_scatter | solution.py:57
  177.3 8.7 %copy.102 = bf16[2,2048,128]{2,0,1:T(2,128)(2,1)S(1)} copy(bf16[2,2048,128]{2,1,0:T(8,128)(2,1)S(1)} %convert_element_type.103) | data formatting | bytes 2097152 | tf_op jit(solution)/shard_map/convert_element_type | solution.py:59
  186.0 31.0 %all_to_all.66 = bf16[2,2048,128]{2,0,1:T(2,128)(2,1)S(1)} all-to-all(bf16[2,2048,128]{2,0,1:T(2,128)(2,1)S(1)} %copy.102), channel_id=1, replica_groups=mesh['groups'=2,'blk'=4,'ops'=2,'sub'=2] {'blk','sub'}, dimensions={1} | all-to-all | bytes 2097152 | tf_op jit(solution)/shard_map/all_to_all | solution.py:58
  223.1 28.6 %all-gather.3.cloned.1.call-done = bf16[2,256,2048]{1,2,0:T(8,128)(2,1)} async-done(((bf16[2,256,1024]{1,2,0:T(8,128)(2,1)}), bf16[2,256,2048]{1,2,0:T(8,128)(2,1)}) %all-gather.3.cloned.1.call-update) | async-done | bytes 2097168 | tf_op jit(solution)/shard_map/all_gather | solution.py:61
  256.7 16.5 %all-reduce.1 = (f32[2]{0:T(128)S(1)}, f32[2]{0:T(128)S(1)}) all-reduce(f32[2]{0:T(128)S(1)} %get-tuple-element.24, f32[2]{0:T(128)S(1)} %get-tuple-element.23), channel_id=1, replica_groups=mesh['groups'=2,'blk'=4,'ops'=2,'sub'=2] {'blk','sub'}, use_global_device_ids=true, to_apply=%region_2.5 | all-reduce | flops 4 | bytes 32 | tf_op jit(solution)/shard_map/psum | solution.py:71
  273.2 6.0 %fusion.10 = (f32[2]{0:T(128)S(1)}, f32[2,256,2048]{1,2,0:T(8,128)}) fusion(f32[2]{0:T(128)S(1)} %get-tuple-element.34, bf16[256,2048]{0,1:T(8,128)(2,1)S(1)} %bitcast.143, bf16[2,256,8,2,128]{1,4,3,2,0:T(8,128)(2,1)} %copy-done.5, f32[256,2048]{0,1:T(8,128)} %copy.88, bf16[2,256,2048]{1,2,0:T(8,128)(2,1)} %copy.89), kind=kLoop, calls=%fused_computation.30 | loop fusion | flops 15728638 | bytes 11534352 | tf_op jit(solution)/shard_map/reduce_sum | solution.py:78
  279.2 13.6 %psum.51 = f32[2]{0:T(128)S(1)} all-reduce(f32[2]{0:T(128)S(1)} %get-tuple-element.31), channel_id=1, replica_groups=mesh['groups'=2,'blk'=4,'ops'=2,'sub'=2] {'blk','sub'}, use_global_device_ids=true, to_apply=%region_6.9 | all-reduce | flops 2 | bytes 16 | tf_op jit(solution)/shard_map/psum | solution.py:78
  292.8 4.0 multiply_reduce_fusion
  296.8 13.6 %psum.52 = f32[2]{0:T(128)S(1)} all-reduce(f32[2]{0:T(128)S(1)} %multiply_reduce_fusion), channel_id=1, replica_groups=mesh['groups'=2,'blk'=4,'ops'=2,'sub'=2] {'blk','sub'}, use_global_device_ids=true, to_apply=%region_8.11 | all-reduce | flops 2 | bytes 16 | tf_op jit(solution)/shard_map/psum | solution.py:81
  310.4 5.1 multiply_convert_fusion
  315.5 3.9 copy.106
  319.4 6.5 %gather_fusion.2 = bf16[48,2,256,128]{3,2,1,0:T(8,128)(2,1)} fusion(bf16[2,256,16,128]{3,1,2,0:T(8,128)(2,1)} %copy.106, s32[1024]{0:T(1024)S(1)} %pad_clamp_fusion), kind=kCustom, calls=%fused_computation.2.clone | custom fusion | bytes 12583104 | tf_op jit(solution)/shard_map/jit(_take)/gather | solution.py:12
  331.7 12.8 %copy.110 = bf16[1,2,256,2048]{2,1,0,3:T(2,128)(2,1)S(1)} copy(bf16[1,2,256,2048]{2,3,1,0:T(8,128)(2,1)S(1)} %bitcast.158) | data formatting | bytes 4194304 | tf_op jit(solution)/shard_map/convert_element_type | solution.py:15
  344.5 51.5 %all_to_all.67 = bf16[1,2,256,2048]{2,1,0,3:T(2,128)(2,1)S(1)} all-to-all(bf16[1,2,256,2048]{2,1,0,3:T(2,128)(2,1)S(1)} %copy.110), channel_id=1, replica_groups=mesh['groups'=2,'blk'=4,'ops'=2,'sub'=2] {'blk','sub'}, dimensions={3} | all-to-all | bytes 4194304 | tf_op jit(solution)/shard_map/all_to_all | solution.py:55
  397.6 3.9 copy.112
  401.5 6.6 %gather_fusion.3 = bf16[48,2,128,256]{3,2,1,0:T(8,128)(2,1)} fusion(bf16[1,2,16,128,256]{4,3,2,1,0:T(8,128)(2,1)} %bitcast.148, s32[48]{0:T(128)S(1)} %or_bitcast_fusion), kind=kCustom, calls=%fused_computation.3.clone | custom fusion | bytes 12583296 | tf_op jit(solution)/shard_map/vmap(jit(_take))/gather | solution.py:19
  415.6 52.1 %reduce-scatter.5.cloned.1.call-done = f32[2,2048,128]{2,1,0:T(8,128)} async-done(((f32[2,2048,256]{2,1,0:T(8,128)}), f32[2,2048,128]{2,1,0:T(8,128)}) %reduce-scatter.5.cloned.1.call-update) | async-done | bytes 2097168 | tf_op jit(solution)/shard_map/reduce_scatter | solution.py:57
  469.4 8.7 %copy.116 = bf16[2,2048,128]{2,0,1:T(2,128)(2,1)S(1)} copy(bf16[2,2048,128]{2,1,0:T(8,128)(2,1)S(1)} %convert_element_type.112) | data formatting | bytes 2097152 | tf_op jit(solution)/shard_map/convert_element_type | solution.py:59
  478.1 31.0 %all_to_all.68 = bf16[2,2048,128]{2,0,1:T(2,128)(2,1)S(1)} all-to-all(bf16[2,2048,128]{2,0,1:T(2,128)(2,1)S(1)} %copy.116), channel_id=1, replica_groups=mesh['groups'=2,'blk'=4,'ops'=2,'sub'=2] {'blk','sub'}, dimensions={1} | all-to-all | bytes 2097152 | tf_op jit(solution)/shard_map/all_to_all | solution.py:58
  512.5 4.0 copy.120
  516.5 27.3 %all-gather.5.cloned.1.call-done = bf16[2,256,2048]{1,2,0:T(8,128)(2,1)} async-done(((bf16[2,256,1024]{1,2,0:T(8,128)(2,1)}), bf16[2,256,2048]{1,2,0:T(8,128)(2,1)}) %all-gather.5.cloned.1.call-update) | async-done | bytes 2097168 | tf_op jit(solution)/shard_map/all_gather | solution.py:61
  546.6 5.8 %fusion.12 = (f32[2]{0:T(128)S(1)}, f32[2]{0:T(128)S(1)}, f32[2]{0:T(128)S(1)}, bf16[2,256,2048]{1,2,0:T(8,128)(2,1)}) fusion(bf16[256,2048]{0,1:T(8,128)(2,1)S(1)} %bitcast.146, bf16[2,256,8,2,128]{1,4,3,2,0:T(8,128)(2,1)} %copy-done.5, f32[256,2048]{0,1:T(8,128)} %copy.88, bf16[2,256,2048]{1,2,0:T(8,128)(2,1)S(1)} %copy-done.3, ...), kind=kLoop, calls=%fused_computation.32 | loop fusion | flops 19922938 | bytes 13631512 | tf_op jit(solution)/shard_map/reduce_sum | solution.py:90
  552.4 16.3 %all-reduce = (f32[2,1]{0,1:T(1,128)S(1)}, f32[2,1]{0,1:T(1,128)S(1)}, f32[2,1]{0,1:T(1,128)S(1)}) all-reduce(f32[2,1]{0,1:T(1,128)S(1)} %bitcast.170, f32[2,1]{0,1:T(1,128)S(1)} %bitcast.169, f32[2,1]{0,1:T(1,128)S(1)} %bitcast.168), channel_id=1, replica_groups=mesh['groups'=2,'blk'=4,'ops'=2,'sub'=2] {'blk','sub'}, use_global_device_ids=true, to_apply=%region_15.18 | all-reduce | flops 6 | bytes 48 | tf_op jit(solution)/shard_map/psum | solution.py:88
  569.4 3.9 copy.121
  (72 shorter events, 57.1 us)
Async XLA Ops:
  7.2 22.4 %copy-start = (bf16[1,16,3,128,128]{4,3,2,1,0:T(8,128)(2,1)S(1)}, bf16[1,16,3,128,128]{4,3,2,1,0:T(8,128)(2,1)}, u32[]{:S(2)}) copy-start(bf16[1,16,3,128,128]{4,3,2,1,0:T(8,128)(2,1)} %param.16) | copy-start | bytes 4718596
  7.2 5.0 copy-start.9
  31.8 20.6 %copy-start.8 = (s32[1,16,3]{1,0,2:T(1,128)S(1)}, s32[1,16,3]{1,0,2:T(1,128)}, u32[]{:S(2)}) copy-start(s32[1,16,3]{1,0,2:T(1,128)} %param.15) | copy-start | bytes 580
  45.8 55.5 %all-to-all-start = ((bf16[1,2,256,2048]{2,1,0,3:T(2,128)(2,1)}), bf16[1,2,256,2048]{2,1,0,3:T(2,128)(2,1)}, u32[]{:S(2)}, u32[]{:S(2)}) async-start(bf16[1,2,256,2048]{2,1,0,3:T(2,128)(2,1)} %copy.96), calls=%async_computation | async-start | bytes 4194304 | tf_op jit(solution)/shard_map/all_to_all | solution.py:55
  52.2 123.4 %reduce-scatter.3.cloned.1.call-start = ((), (), s32[]{:S(2)}) async-start(), calls=%async_computation.6 | async-start | bytes 6291456 | tf_op jit(solution)/shard_map/reduce_scatter | solution.py:57
  115.1 3.6 copy-start.6
  122.2 129.4 %all-gather.3.cloned.1.call-start = ((), (), s32[]{:S(2)}) async-start(), calls=%async_computation.7 | async-start | bytes 3145728 | tf_op jit(solution)/shard_map/all_gather | solution.py:61
  220.4 247.3 %reduce-scatter.5.cloned.1.call-start = ((), (), s32[]{:S(2)}) async-start(), calls=%async_computation.8 | async-start | bytes 6291456 | tf_op jit(solution)/shard_map/reduce_scatter | solution.py:57
  251.6 2.2 copy-start.1
  251.6 2.9 copy-start.4
  254.5 2.2 copy-start.5
  408.1 3.6 copy-start.7
  415.3 128.4 %all-gather.5.cloned.1.call-start = ((), (), s32[]{:S(2)}) async-start(), calls=%async_computation.9 | async-start | bytes 3145728 | tf_op jit(solution)/shard_map/all_gather | solution.py:61
  543.7 2.2 copy-start.2
  543.7 2.9 copy-start.3
Sparse Core Ops, SparseCore 0:
  122.3 53.2 reduce-scatter.2
  220.5 31.0 all-gather.2
  415.4 52.2 reduce-scatter.4
  512.6 31.0 all-gather.4
where the time goes:
time: 587 us; the launch traced here: 580 us
  waiting for transfers between devices  210 us (36%)
  blocking collectives  174 us (30%)
  local copies, waits for them, and re-layouts  125 us (21%)
  other arithmetic  43.8 us (7%)
  between operations  14.5 us (2%)
  starting transfers between devices  6.92 us (1%)
  matrix products  6.85 us (1%)
    reduce_scatter x2, waiting for transfers between devices, operate(): lax.psum_scatter(partial_sum, 'ops', scatter_dimension=2, tiled=True)  105 us
    all_to_all x2, blocking collectives, operate(): lax.all_to_all(shares.astype(jnp.bfloat16), ('blk', 'sub'), split_axis=1,...  62 us
    all_gather x2, waiting for transfers between devices, operate(): gathered = lax.all_gather(returned, 'ops', axis=2, tiled=True)  55.8 us
    all_to_all x1, blocking collectives, operate(): lax.all_to_all(images, ('blk', 'sub'), split_axis=3, concat_axis=2, tiled...  51.5 us
    all_to_all x1, waiting for transfers between devices, operate(): lax.all_to_all(images, ('blk', 'sub'), split_axis=3, concat_axis=2, tiled...  48.7 us
    convert_element_type x4, local copies, waits for them, and re-layouts, apply_right(): product.reshape(term_count, roots_here, row_count, full_width)  27.2 us
    convert_element_type x2, local copies, waits for them, and re-layouts, operate(): shares.astype(jnp.bfloat16)  17.4 us
    psum x1, blocking collectives, shards(): lax.psum((jnp.sum(wave * wave, axis=(1, 2)), jnp.sum(wave * sigma_one, ax...  16.5 us
  transfers between devices with their start and end apart: 5, of which 5 were waited for; matrix products, arithmetic and copies ran while one was open for 1% of the time, Pallas kernels for 0%

commit v1 on v0

--- a/solution.py
+++ b/solution.py
@@ -1,7 +1,17 @@
+import functools
+
 import jax
 import jax.numpy as jnp
 from jax import lax
+from jax.experimental import pallas as pl
+from jax.experimental.pallas import tpu as pltpu
 from jax.sharding import PartitionSpec as P
+
+ANY = pl.BlockSpec(memory_space=pl.ANY)
+SMEM = pl.BlockSpec(memory_space=pltpu.SMEM)
+VMEM = pl.BlockSpec(memory_space=pltpu.VMEM)
+VMEM_LIMIT = 56 * 1024 * 1024
+LANES = 128
 
 
 def apply_right(field_in, blocks, columns):
@@ -31,7 +41,7 @@
     return product.reshape(roots_here, full_width, col_count)
 
 
-def shards(theta, hdiag, pattern, left_blocks, left_cols, right_blocks, right_cols):
+def general_shards(theta, hdiag, pattern, left_blocks, left_cols, right_blocks, right_cols):
     roots_here, row_count, full_width = theta.shape
     sectors = pattern.shape[0]
     block_size = full_width // sectors
@@ -99,6 +109,442 @@
     return (correction, sigma_two, subspace)
 
 
+def halves_fit(mesh):
+    sizes = dict(mesh.shape)
+    return sizes["blk"] == 4 and sizes["ops"] == 2 and sizes["sub"] == 2
+
+
+def across(value, axis, distance):
+    size = lax.axis_size(axis)
+    return lax.ppermute(value, axis, [(i, i ^ distance) for i in range(size)])
+
+
+def share(stats):
+    axes = ("blk", "ops", "sub")
+    count = lax.axis_size("blk") * lax.axis_size("ops") * lax.axis_size("sub")
+    found = [stats]
+    for distance in range(1, 8):
+        found.append(lax.ppermute(stats, axes, [(i, i ^ distance) for i in range(count)]))
+    return found
+
+
+def place():
+    return lax.axis_index("blk"), lax.axis_index("ops"), lax.axis_index("sub")
+
+
+def fold(value):
+    rows, width = value.shape
+    value = jnp.sum(value.reshape(rows // 8, 8, width), axis=0)
+    return sum(value[:, at : at + LANES] for at in range(0, width, LANES))
+
+
+def operate_kernel(
+    first, plan, cols, pattern, right_own, right_near, right_far, left_own, left_other, hd_own, hd_far, *refs
+):
+    count = len(plan)
+    pieces, refs = refs[:count], refs[count:]
+    if first:
+        psi_out, sigma_out, stats_out = refs[:3]
+        refs = refs[3:]
+    else:
+        psi_in, sigma_in, near_out, far_out, stats_out = refs[:5]
+        refs = refs[5:]
+    field, picked, images, right, left, diag, sems = refs
+    z, x, c = place()
+    sectors, block, width = field.shape
+    links = right.shape[2]
+    mine = 4 * z + 2 * c + x
+    rows = (mine, mine ^ 8)
+
+    copies = []
+
+    def begin(source, target):
+        copy = pltpu.make_async_copy(source, target, sems.at[len(copies)])
+        copy.start()
+        copies.append(copy)
+
+    for piece, offsets in zip(pieces, plan):
+        for at, (dz, dx, dc) in enumerate(offsets):
+            row = 4 * (z ^ dz) + 2 * (c ^ dc) + (x ^ dx if dx < 2 else dx - 2)
+            begin(piece.at[at], field.at[row])
+    part = right_near.shape[0]
+    begin(right_own.at[0], right.at[0])
+    begin(right_near, right.at[1, pl.ds(c * part, part)])
+    begin(right_far, right.at[1, pl.ds((1 - c) * part, part)])
+    for at in range(2):
+        begin(left_own.at[0, rows[at]], left.at[0, at])
+    begin(left_other, left.at[1])
+    begin(hd_own.at[x], diag.at[0])
+    begin(hd_far, diag.at[1])
+    for copy in copies:
+        copy.wait()
+
+    table = sectors * links
+
+    def right_col(term, b, j):
+        return cols[(2 * term) * table + b * links + j]
+
+    def left_col(term, a, j):
+        return cols[(2 * term + 1) * table + a * links + j]
+
+    def allowed(a, q, value):
+        return jnp.where(pattern[a * sectors + q] != 0, value, jnp.zeros_like(value))
+
+    for term in range(2):
+        for at in range(2):
+            for j in range(links):
+                source = left_col(term, rows[at], j)
+                spot = (at * links + j) * block
+                for q in range(sectors):
+                    span = slice(q * block, (q + 1) * block)
+                    value = field[source, :, span]
+                    if first:
+                        value = allowed(source, q, value)
+                    picked[term, spot : spot + block, span] = value
+
+    def image(b, carry):
+        for term in range(2):
+            lhs = []
+            for j in range(links):
+                start = pl.multiple_of(right_col(term, b, j) * block, block)
+                lhs.append(picked[term, :, pl.ds(start, block)])
+            rhs = [right[term, b, j] for j in range(links)]
+            product = lax.dot_general(
+                jnp.concatenate(lhs, axis=1),
+                jnp.concatenate(rhs, axis=1),
+                (((1,), (1,)), ((), ())),
+                preferred_element_type=jnp.float32,
+            )
+            images[term, :, pl.ds(pl.multiple_of(b * block, block), block)] = product.astype(jnp.bfloat16)
+        return carry
+
+    lax.fori_loop(0, sectors, image, 0)
+
+    step = 2
+    deep = links * block
+    zero = jnp.zeros((8, LANES), jnp.float32)
+
+    def column(n, sums):
+        start = pl.multiple_of(n * step * block, step * block)
+        span = pl.ds(start, step * block)
+        sums = list(sums)
+        for at in range(2):
+            total = None
+            for term in range(2):
+                weights = jnp.concatenate([left[term, at, j] for j in range(links)], axis=1)
+                product = jnp.dot(
+                    weights,
+                    images[term, at * deep : (at + 1) * deep, span],
+                    preferred_element_type=jnp.float32,
+                )
+                total = product if total is None else total + product
+            total = total.astype(jnp.bfloat16).astype(jnp.float32)
+            offdiag = jnp.concatenate(
+                [allowed(rows[at], n * step + i, total[:, i * block : (i + 1) * block]) for i in range(step)],
+                axis=1,
+            )
+            own = field[rows[at], :, span].astype(jnp.float32)
+            if first:
+                own = jnp.concatenate(
+                    [allowed(rows[at], n * step + i, own[:, i * block : (i + 1) * block]) for i in range(step)],
+                    axis=1,
+                )
+            result = diag[at, :, span].astype(jnp.float32) * own + offdiag
+            if first:
+                psi_out[at, :, span] = own.astype(jnp.bfloat16)
+                sigma_out[at, :, span] = result
+                sums[0] += fold(own * own)
+                sums[1] += fold(own * result)
+            else:
+                narrow = result.astype(jnp.bfloat16)
+                (near_out, far_out)[at][:, span] = narrow
+                second = narrow.astype(jnp.float32)
+                sums[0] += fold(psi_in[at, :, span].astype(jnp.float32) * second)
+                sums[1] += fold(own * sigma_in[at, :, span])
+                sums[2] += fold(own * second)
+        return tuple(sums)
+
+    sums = lax.fori_loop(0, sectors // step, column, (zero,) * (2 if first else 3))
+    stats_out[...] = jnp.zeros_like(stats_out)
+    for at, value in enumerate(sums):
+        stats_out[at : at + 1, :] = jnp.sum(value, axis=0, keepdims=True)
+
+
+def operate(first, plan, pieces, cols, pattern, right, left, diag, extra=()):
+    _, block, width = pieces[0].shape
+    right_own, right_near, right_far = right
+    _, sectors, links = right_own.shape[:3]
+    rows = jax.ShapeDtypeStruct((2, block, width), jnp.bfloat16)
+    one = jax.ShapeDtypeStruct((block, width), jnp.bfloat16)
+    stats = jax.ShapeDtypeStruct((8, LANES), jnp.float32)
+    if first:
+        out_shape = (rows, jax.ShapeDtypeStruct((2, block, width), jnp.float32), stats)
+    else:
+        out_shape = (one, one, stats)
+    copies = sum(len(offsets) for offsets in plan) + 8
+    inner = 2 * 2 * sectors * 2 * links * links * block * block * block
+    outer = 2 * 2 * 2 * links * block * block * width
+    return pl.pallas_call(
+        functools.partial(operate_kernel, first, plan),
+        out_shape=out_shape,
+        in_specs=[SMEM, SMEM] + [ANY] * (7 + len(pieces)) + [VMEM] * len(extra),
+        out_specs=(VMEM,) * len(out_shape),
+        scratch_shapes=[
+            pltpu.VMEM((sectors, block, width), jnp.bfloat16),
+            pltpu.VMEM((2, 2 * links * block, width), jnp.bfloat16),
+            pltpu.VMEM((2, 2 * links * block, width), jnp.bfloat16),
+            pltpu.VMEM((2, sectors, links, block, block), jnp.bfloat16),
+            pltpu.VMEM((2, 2, links, block, block), jnp.bfloat16),
+            pltpu.VMEM((2, block, width), jnp.bfloat16),
+            pltpu.SemaphoreType.DMA((copies,)),
+        ],
+        compiler_params=pltpu.CompilerParams(vmem_limit_bytes=VMEM_LIMIT),
+        cost_estimate=pl.CostEstimate(
+            flops=inner + outer, bytes_accessed=16 * 1024 * 1024, transcendentals=0
+        ),
+        name="operate_first" if first else "operate_second",
+    )(cols, pattern, right_own, right_near, right_far, *left, *diag, *pieces, *extra)
+
+
+def total_of(rows):
+    return jnp.sum(rows, axis=1, keepdims=True)
+
+
+def update_kernel(psi, sigma, hd_own, hd_far, *refs):
+    stats, (t_out, stats_out, diag, sems) = refs[:8], refs[8:]
+    z, x, c = place()
+    copies = [
+        pltpu.make_async_copy(hd_own.at[x], diag.at[0], sems.at[0]),
+        pltpu.make_async_copy(hd_far, diag.at[1], sems.at[1]),
+    ]
+    for copy in copies:
+        copy.start()
+    whole = sum(ref[0:2, :] for ref in stats)
+    norm_sq, energy_sum = total_of(whole[0:1, :]), total_of(whole[1:2, :])
+    energy = energy_sum / (norm_sq + 1e-06)
+    mine = total_of(stats[0][0:1, :])
+    for copy in copies:
+        copy.wait()
+    _, block, width = psi.shape
+    step = 16
+    zero = jnp.zeros((8, LANES), jnp.float32)
+
+    def chunk(n, total):
+        span = pl.ds(pl.multiple_of(n * step, step), step)
+        for at in range(2):
+            wave = psi[at, span, :].astype(jnp.float32)
+            shifted = diag[at, span, :].astype(jnp.float32) - energy
+            t = (sigma[at, span, :] - energy * wave) * shifted / (shifted * shifted + 1.0)
+            t_out[at, span, :] = t
+            total = total + fold(wave * t)
+        return total
+
+    lanes = jnp.sum(lax.fori_loop(0, block // step, chunk, zero), axis=0, keepdims=True)
+    correlation = total_of(lanes)
+    local = jnp.where(mine > 0.0, correlation / jnp.where(mine > 0.0, mine, 1.0), 0.0)
+
+    def within(n, total):
+        span = pl.ds(pl.multiple_of(n * step, step), step)
+        for at in range(2):
+            rest = t_out[at, span, :] - local * psi[at, span, :].astype(jnp.float32)
+            total = total + fold(rest * rest)
+        return total
+
+    spread = jnp.sum(lax.fori_loop(0, block // step, within, zero), axis=0, keepdims=True)
+    stats_out[...] = jnp.zeros_like(stats_out)
+    stats_out[0:1, :] = jnp.broadcast_to(correlation, (1, LANES))
+    stats_out[1:2, :] = jnp.broadcast_to(total_of(spread), (1, LANES))
+    stats_out[2:3, :] = jnp.broadcast_to(mine, (1, LANES))
+    stats_out[3:4, :] = jnp.broadcast_to(local, (1, LANES))
+    stats_out[4:5, :] = jnp.broadcast_to(norm_sq, (1, LANES))
+
+
+def correct_kernel(psi, t, *refs):
+    stats, (out,) = refs[:8], refs[8:]
+    norm_sq = stats[0][4:5, 0:1]
+    factor = sum(ref[0:1, 0:1] for ref in stats) / (norm_sq + 1e-06)
+    length_sq = jnp.zeros((1, 1), jnp.float32)
+    for ref in stats:
+        gap = factor - ref[3:4, 0:1]
+        length_sq = length_sq + (ref[1:2, 0:1] + gap * gap * ref[2:3, 0:1])
+    scale = jnp.sqrt(norm_sq / (length_sq + 1e-06))
+    _, block, width = psi.shape
+    step = 16
+
+    def chunk(n, carry):
+        span = pl.ds(pl.multiple_of(n * step, step), step)
+        for at in range(2):
+            wave = psi[at, span, :].astype(jnp.float32)
+            out[at, span, :] = ((t[at, span, :] - factor * wave) * scale).astype(jnp.bfloat16)
+        return carry
+
+    lax.fori_loop(0, block // step, chunk, 0)
+
+
+def assemble_kernel(near, near_x, far, far_x, out, sems):
+    z, x, c = place()
+    half = z // 2
+    copies = [
+        pltpu.make_async_copy(near, out.at[half, x], sems.at[0]),
+        pltpu.make_async_copy(near_x, out.at[half, 1 - x], sems.at[1]),
+        pltpu.make_async_copy(far, out.at[1 - half, x], sems.at[2]),
+        pltpu.make_async_copy(far_x, out.at[1 - half, 1 - x], sems.at[3]),
+    ]
+    for copy in copies:
+        copy.start()
+    for copy in copies:
+        copy.wait()
+
+
+def assemble(near, near_x, far, far_x):
+    block, width = near.shape
+    return pl.pallas_call(
+        assemble_kernel,
+        out_shape=jax.ShapeDtypeStruct((2, 2, block, width), near.dtype),
+        in_specs=[ANY] * 4,
+        out_specs=ANY,
+        scratch_shapes=[pltpu.SemaphoreType.DMA((4,))],
+        name="assemble",
+    )(near, near_x, far, far_x).reshape(2, 2 * block, width)
+
+
+def shards(theta, hdiag, pattern, left_blocks, left_cols, right_blocks, right_cols):
+    roots, row_count, width = theta.shape
+    sectors = pattern.shape[0]
+    block = width // sectors
+    links = left_cols.shape[2]
+    z, x, c = place()
+    half = z // 2
+    mine = 4 * z + 2 * c + x
+
+    halves = theta.reshape(roots, 2, block, width)
+    diag = hdiag.reshape(2, block, width)
+
+    own = lax.dynamic_index_in_dim(halves, half, 0, keepdims=False)
+    given = lax.dynamic_slice(halves, (1 - half, x, 0, 0), (1, 1, block, width))[0]
+    far = across(given, "blk", 2)
+    near_z = across(own, "blk", 1)
+    cols_own = jnp.stack([right_cols[0], left_cols[0]])
+    cols_other = across(cols_own, "ops", 1)
+    part = sectors // 2
+    right_near = across(lax.dynamic_slice_in_dim(right_blocks[0], c * part, part, 0), "ops", 1)
+    wanted = jnp.stack(
+        [
+            lax.dynamic_index_in_dim(left_blocks[0], mine ^ 1, 0, keepdims=False),
+            lax.dynamic_index_in_dim(left_blocks[0], mine ^ 9, 0, keepdims=False),
+        ]
+    )
+    left_other = across(wanted, "ops", 1)
+    own_core = across(own, "sub", 1)
+    right_far = across(right_near, "sub", 1)
+    near_z_core = across(near_z, "sub", 1)
+    far_z = across(far, "blk", 1)
+    far_x = across(far, "ops", 1)
+    far_core = across(far, "sub", 1)
+    far_zx = across(far_z, "ops", 1)
+    far_x_core = across(far_x, "sub", 1)
+    far_z_core = across(far_z, "sub", 1)
+    far_zx_core = across(far_zx, "sub", 1)
+    hd_far = across(lax.dynamic_index_in_dim(diag, x, 0, keepdims=False), "blk", 2)
+
+    cols = jnp.concatenate([cols_own.reshape(-1), cols_other.reshape(-1)])
+    allowed = pattern.reshape(-1)
+    right = (right_blocks, right_near, right_far)
+    left = (left_blocks, left_other)
+    pieces = [own, own_core, near_z, near_z_core]
+    plan = [
+        ((0, 2, 0), (0, 3, 0)),
+        ((0, 2, 1), (0, 3, 1)),
+        ((1, 2, 0), (1, 3, 0)),
+        ((1, 2, 1), (1, 3, 1)),
+    ]
+    for piece, offset in (
+        (far, (2, 0, 0)),
+        (far_x, (2, 1, 0)),
+        (far_z, (3, 0, 0)),
+        (far_zx, (3, 1, 0)),
+        (far_core, (2, 0, 1)),
+        (far_x_core, (2, 1, 1)),
+        (far_z_core, (3, 0, 1)),
+        (far_zx_core, (3, 1, 1)),
+    ):
+        pieces.append(piece)
+        plan.append((offset,))
+    pieces = [piece.reshape(-1, block, width) for piece in pieces]
+    psi, sigma_one, stats_one = operate(
+        True, tuple(plan), pieces, cols, allowed, right, left, (diag, hd_far)
+    )
+
+    found = share(stats_one)
+    t, stats_two = pl.pallas_call(
+        update_kernel,
+        out_shape=(
+            jax.ShapeDtypeStruct((2, block, width), jnp.float32),
+            jax.ShapeDtypeStruct((8, LANES), jnp.float32),
+        ),
+        in_specs=[VMEM, VMEM, ANY, ANY] + [VMEM] * 8,
+        out_specs=(VMEM, VMEM),
+        scratch_shapes=[
+            pltpu.VMEM((2, block, width), jnp.bfloat16),
+            pltpu.SemaphoreType.DMA((2,)),
+        ],
+        compiler_params=pltpu.CompilerParams(vmem_limit_bytes=VMEM_LIMIT),
+        name="update",
+    )(psi, sigma_one, diag, hd_far, *found)
+    found = share(stats_two)
+    changed = pl.pallas_call(
+        correct_kernel,
+        out_shape=jax.ShapeDtypeStruct((2, block, width), jnp.bfloat16),
+        in_specs=[VMEM, VMEM] + [VMEM] * 8,
+        out_specs=VMEM,
+        compiler_params=pltpu.CompilerParams(vmem_limit_bytes=VMEM_LIMIT),
+        name="correct",
+    )(psi, t, *found)
+
+    by_z = across(changed, "blk", 1)
+    by_x = across(changed, "ops", 1)
+    by_core = across(changed, "sub", 1)
+    by_zx_near = across(by_z[0], "ops", 1)
+    by_zx_far = across(by_x[1], "blk", 1)
+    by_z_core = across(by_z, "sub", 1)
+    by_x_core = across(by_x, "sub", 1)
+    by_zx_near_core = across(by_zx_near, "sub", 1)
+    by_zx_far_core = across(by_zx_far, "sub", 1)
+    pieces, plan = [], []
+    for piece, offset in (
+        (changed, (0, 0, 0)),
+        (by_z, (1, 0, 0)),
+        (by_x, (0, 1, 0)),
+        (by_core, (0, 0, 1)),
+        (by_z_core, (1, 0, 1)),
+        (by_x_core, (0, 1, 1)),
+    ):
+        pieces.append(piece)
+        plan.append((offset, (offset[0] ^ 2, offset[1], offset[2])))
+    for piece, offset in (
+        (by_zx_near, (1, 1, 0)),
+        (by_zx_far, (3, 1, 0)),
+        (by_zx_near_core, (1, 1, 1)),
+        (by_zx_far_core, (3, 1, 1)),
+    ):
+        pieces.append(piece[None])
+        plan.append((offset,))
+    two_near, two_far, stats_three = operate(
+        False, tuple(plan), pieces, cols, allowed, right, left, (diag, hd_far), (psi, sigma_one)
+    )
+
+    other = across(changed[1], "blk", 2)
+    correction = assemble(changed[0], by_x[0], other, across(other, "ops", 1))
+    other = across(two_far, "blk", 2)
+    sigma_two = assemble(two_near, across(two_near, "ops", 1), other, across(other, "ops", 1))
+
+    sums = jnp.concatenate([jnp.sum(stats_one[:2], axis=1), jnp.sum(stats_three[:3], axis=1)])
+    here = (jnp.arange(roots) == half)[:, None]
+    sums = lax.psum(jnp.where(here, sums[None, :], 0.0), ("blk", "ops", "sub"))
+    subspace = sums[:, 1:5] / (sums[:, 0:1] + 1e-06)
+    return correction, sigma_two, subspace
+
+
 def solution(mesh):
     in_specs = (
         P("groups", ("blk", "sub"), None),
@@ -114,4 +560,5 @@
         P("groups", ("blk", "sub"), None),
         P("groups", None),
     )
-    return jax.shard_map(shards, mesh=mesh, in_specs=in_specs, out_specs=out_specs, check_vma=False)
+    body = shards if halves_fit(mesh) else general_shards
+    return jax.shard_map(body, mesh=mesh, in_specs=in_specs, out_specs=out_specs, check_vma=False)

time: 587 us -> 384 us (0.65); the launches traced: 580 us -> 384 us
  Pallas kernels: 0 us -> 178 us
  blocking collectives: 174 us -> 30.2 us
  local copies, waits for them, and re-layouts: 125 us -> 14.1 us
  waiting for transfers between devices: 210 us -> 114 us
  other arithmetic: 43.8 us -> 3.15 us
  starting transfers between devices: 6.92 us -> 43.8 us
  between operations: 14.5 us -> 1.01 us
  matrix products: 6.85 us -> 0 us
    pallas_call x0 -> x6, Pallas kernels: none -> 178 us  [the longest x2 129 us: assemble(): pl.pallas_call(assemble_kernel, out_shape=jax.ShapeDtypeStruct((2, 2, blo...]
    ppermute x0 -> x44, waiting for transfers between devices: none -> 114 us  [the longest x30 107 us: across(): return lax.ppermute(value, axis, [(i, i ^ distance) for i in range(size)])]
    all_to_all x3 -> x0, blocking collectives: 114 us -> none  [the longest x2 62 us: operate(): lax.all_to_all(shares.astype(jnp.bfloat16), ('blk', 'sub'), split_axis=1,...]
    reduce_scatter x2 -> x0, waiting for transfers between devices: 105 us -> none  [operate(): lax.psum_scatter(partial_sum, 'ops', scatter_dimension=2, tiled=True)]
    all_gather x2 -> x0, waiting for transfers between devices: 55.8 us -> none  [operate(): gathered = lax.all_gather(returned, 'ops', axis=2, tiled=True)]
    all_to_all x1 -> x0, waiting for transfers between devices: 48.7 us -> none  [operate(): lax.all_to_all(images, ('blk', 'sub'), split_axis=3, concat_axis=2, tiled...]
    convert_element_type x7 -> x0, local copies, waits for them, and re-layouts: 47.2 us -> none  [the longest x4 27.2 us: apply_right(): product.reshape(term_count, roots_here, row_count, full_width)]
    ppermute x0 -> x44, starting transfers between devices: none -> 43.8 us  [the longest x30 30.5 us: across(): return lax.ppermute(value, axis, [(i, i ^ distance) for i in range(size)])]
  transfers between devices with their start and end apart: 5 -> 44, of which waited for: 5 -> 16; matrix products, arithmetic and copies ran while one was open for 1% -> 3% of each run, Pallas kernels for 0% -> 22%
where the time goes in v1:
time: 384 us
  Pallas kernels  178 us (46%)
  waiting for transfers between devices  114 us (30%)
  starting transfers between devices  43.8 us (11%)
  blocking collectives  30.2 us (8%)
  local copies, waits for them, and re-layouts  14.1 us (4%)
    pallas_call x2, Pallas kernels, assemble(): pl.pallas_call(assemble_kernel, out_shape=jax.ShapeDtypeStruct((2, 2, blo...  129 us
    ppermute x30, waiting for transfers between devices, across(): return lax.ppermute(value, axis, [(i, i ^ distance) for i in range(size)])  107 us
    pallas_call x2, Pallas kernels, operate(): pl.pallas_call(functools.partial(operate_kernel, first, plan), out_shape=...  39 us
    ppermute x30, starting transfers between devices, across(): return lax.ppermute(value, axis, [(i, i ^ distance) for i in range(size)])  30.5 us
    psum x1, blocking collectives, shards(): sums = lax.psum(jnp.where(here, sums[None, :], 0.0), ('blk', 'ops', 'sub'))  30.2 us
    ppermute x14, starting transfers between devices, share(): lax.ppermute(stats, axes, [(i, i ^ distance) for i in range(count)])  13.3 us
  transfers between devices with their start and end apart: 44, of which 16 were waited for; matrix products, arithmetic and copies ran while one was open for 3% of the time, Pallas kernels for 22%

profile of v1, /device:TPU:0, one launch (start us, length us, event | category | flops | bytes accessed | tf_op | source)
XLA Modules:
  0.0 383.8 jit_solution(6195099114168822406)
XLA Ops:
  0.7 1.5 copy-done
  3.3 3.0 collective-permute-start.6
  7.2 2.6 collective-permute-start.8
  11.0 2.1 dynamic-slice_bitcast_fusion.1
  16.1 15.6 %collective-permute-done = s32[2,16,3]{1,0,2:T(2,128)S(1)} collective-permute-done((s32[2,16,3]{1,0,2:T(2,128)S(1)}, s32[2,16,3]{1,0,2:T(2,128)S(1)}, u32[]{:S(2)}, u32[]{:S(2)}) %collective-permute-start) | collective-permute-done | bytes 416 | tf_op jit(solution)/shard_map/ppermute | solution.py:119
  33.3 4.2 %collective-permute-done.3.left_other = bf16[2,3,128,128]{3,2,1,0:T(8,128)(2,1)S(1)} collective-permute-done((bf16[2,3,128,128]{3,2,1,0:T(8,128)(2,1)S(1)}, bf16[2,3,128,128]{3,2,1,0:T(8,128)(2,1)S(1)}, u32[]{:S(2)}, u32[]{:S(2)}) %collective-permute-start.3) | collective-permute-done | bytes 196640 | tf_op jit(solution)/shard_map/ppermute | solution.py:119
  37.4 4.1 %collective-permute-done.8.refs_4_ = bf16[1,128,2048]{2,1,0:T(8,128)(2,1)} collective-permute-done((bf16[1,128,2048]{2,1,0:T(8,128)(2,1)}, bf16[1,128,2048]{2,1,0:T(8,128)(2,1)}, u32[]{:S(2)}, u32[]{:S(2)}) %collective-permute-start.8) | collective-permute-done | bytes 524320 | tf_op jit(solution)/shard_map/ppermute | solution.py:119
  41.5 3.5 collective-permute-start.10
  45.0 10.2 %collective-permute-done.4.hd_far = bf16[128,2048]{1,0:T(8,128)(2,1)S(1)} collective-permute-done((bf16[128,2048]{1,0:T(8,128)(2,1)}, bf16[128,2048]{1,0:T(8,128)(2,1)S(1)}, u32[]{:S(2)}, u32[]{:S(2)}) %collective-permute-start.4) | collective-permute-done | bytes 524320 | tf_op jit(solution)/shard_map/ppermute | solution.py:119
  57.3 6.2 %collective-permute-done.10.refs_6_ = bf16[1,128,2048]{2,1,0:T(8,128)(2,1)} collective-permute-done((bf16[1,128,2048]{2,1,0:T(8,128)(2,1)}, bf16[1,128,2048]{2,1,0:T(8,128)(2,1)}, u32[]{:S(2)}, u32[]{:S(2)}) %collective-permute-start.10) | collective-permute-done | bytes 524320 | tf_op jit(solution)/shard_map/ppermute | solution.py:119
  63.5 1.7 collective-permute-start.11
  65.8 11.2 %collective-permute-done.11.refs_7_ = bf16[1,128,2048]{2,1,0:T(8,128)(2,1)} collective-permute-done((bf16[1,128,2048]{2,1,0:T(8,128)(2,1)}, bf16[1,128,2048]{2,1,0:T(8,128)(2,1)}, u32[]{:S(2)}, u32[]{:S(2)}) %collective-permute-start.11) | collective-permute-done | bytes 524320 | tf_op jit(solution)/shard_map/ppermute | solution.py:119
  79.2 19.6 %operate_first.1 = (bf16[2,128,2048]{2,1,0:T(8,128)(2,1)}, f32[2,128,2048]{2,1,0:T(8,128)}, f32[8,128]{1,0:T(8,128)}) custom-call(s32[192]{0:T(256)} %pad_add_fusion.1.cols, s32[256]{0:T(256)} %reshape.37.pattern, bf16[1,16,3,128,128]{4,3,2,1,0:T(8,128)(2,1)} %right_own.3, bf16[8,3,128,128]{3,2,1,0:T(8,128)(2,1)} %copy-done.5, ...), custom_call_target="tpu_custom_call" | custom-call | flops 3221225472 | bytes 16777216 | tf_op jit(solution)/shard_map/operate_first/pallas_call | solution.py:287
  100.8 2.4 collective-permute-start.19
  103.2 2.6 collective-permute-start.21
  106.4 1.6 collective-permute-done.21.refs_6_
  107.9 2.1 collective-permute-done.22.refs_7_
  110.6 6.1 %update.1 = (f32[2,128,2048]{2,1,0:T(8,128)}, f32[8,128]{1,0:T(8,128)}) custom-call(bf16[2,128,2048]{2,1,0:T(8,128)(2,1)} %get-tuple-element.11.psi.refs_10_, f32[2,128,2048]{2,1,0:T(8,128)} %get-tuple-element.12.sigma.refs_11_, bf16[2,128,2048]{2,1,0:T(8,128)(2,1)} %bitcast.33, bf16[128,2048]{1,0:T(8,128)(2,1)} %copy-done.3, ...), custom_call_target="tpu_custom_call" | custom-call | tf_op jit(solution)/shard_map/update/pallas_call | solution.py:479
  120.9 2.1 collective-permute-start.29
  123.0 2.1 collective-permute-done.28.refs_6_
  125.7 3.5 correct.1.refs_0_
  130.4 1.7 collective-permute-start.33
  132.1 22.5 %collective-permute-done.30.refs_2_ = bf16[2,128,2048]{2,1,0:T(8,128)(2,1)S(1)} collective-permute-done((bf16[2,128,2048]{2,1,0:T(8,128)(2,1)}, bf16[2,128,2048]{2,1,0:T(8,128)(2,1)S(1)}, u32[]{:S(2)}, u32[]{:S(2)}) %collective-permute-start.30) | collective-permute-done | bytes 1048608 | tf_op jit(solution)/shard_map/ppermute | solution.py:119
  157.1 1.5 collective-permute-start.37
  159.1 9.6 %collective-permute-done.38 = bf16[128,2048]{1,0:T(8,128)(2,1)S(1)} collective-permute-done((bf16[128,2048]{1,0:T(8,128)(2,1)S(1)}, bf16[128,2048]{1,0:T(8,128)(2,1)S(1)}, u32[]{:S(2)}, u32[]{:S(2)}) %collective-permute-start.38) | collective-permute-done | bytes 524320 | tf_op jit(solution)/shard_map/ppermute | solution.py:119
  171.1 2.8 collective-permute-start.31
  175.6 19.4 %operate_second.1 = (bf16[128,2048]{1,0:T(8,128)(2,1)}, bf16[128,2048]{1,0:T(8,128)(2,1)}, f32[8,128]{1,0:T(8,128)}) custom-call(s32[192]{0:T(256)} %pad_add_fusion.1.cols, s32[256]{0:T(256)} %reshape.37.pattern, bf16[1,16,3,128,128]{4,3,2,1,0:T(8,128)(2,1)} %right_own.3, bf16[8,3,128,128]{3,2,1,0:T(8,128)(2,1)} %copy-done.5, ...), custom_call_target="tpu_custom_call" | custom-call | flops 3221225472 | bytes 16777216 | tf_op jit(solution)/shard_map/operate_second/pallas_call | solution.py:287
  195.6 2.4 collective-permute-done.31.far
  201.7 19.7 %collective-permute-done.42.far = bf16[128,2048]{1,0:T(8,128)(2,1)S(1)} collective-permute-done((bf16[128,2048]{1,0:T(8,128)(2,1)}, bf16[128,2048]{1,0:T(8,128)(2,1)S(1)}, u32[]{:S(2)}, u32[]{:S(2)}) %collective-permute-start.42) | collective-permute-done | bytes 524320 | tf_op jit(solution)/shard_map/ppermute | solution.py:119
  222.6 64.7 %assemble.2 = bf16[2,2,128,2048]{3,2,1,0:T(8,128)(2,1)} custom-call(bf16[128,2048]{1,0:T(8,128)(2,1)} %get-tuple-element.24.near, bf16[128,2048]{1,0:T(8,128)(2,1)} %get-tuple-element.22.near_x, bf16[128,2048]{1,0:T(8,128)(2,1)} %collective-permute-done.31.far, bf16[128,2048]{1,0:T(8,128)(2,1)} %collective-permute-done.32.far_x), custom_call_target="tpu_custom_call" | custom-call | tf_op jit(solution)/shard_map/assemble/pallas_call | solution.py:401
  287.3 30.2 %psum.7 = f32[2,5]{1,0:T(2,128)S(1)} all-reduce(f32[2,5]{1,0:T(2,128)S(1)} %broadcast_select_fusion), channel_id=1, replica_groups=mesh['groups'=2,'blk'=4,'ops'=2,'sub'=2] {'blk','ops','sub'}, use_global_device_ids=true, to_apply=%region_2.3 | all-reduce | flops 10 | bytes 80 | tf_op jit(solution)/shard_map/psum | solution.py:543
  319.1 64.7 %assemble.3 = bf16[2,2,128,2048]{3,2,1,0:T(8,128)(2,1)} custom-call(bf16[128,2048]{1,0:T(8,128)(2,1)} %get-tuple-element.16.near, bf16[128,2048]{1,0:T(8,128)(2,1)} %copy-done.16, bf16[128,2048]{1,0:T(8,128)(2,1)} %copy-done.15, bf16[128,2048]{1,0:T(8,128)(2,1)} %collective-permute-done.43.far_x), custom_call_target="tpu_custom_call" | custom-call | tf_op jit(solution)/shard_map/assemble/pallas_call | solution.py:401
  (154 shorter events, 35.9 us)
Async XLA Ops:
  3.3 53.5 %collective-permute-start.6 = (bf16[2,128,2048]{2,1,0:T(8,128)(2,1)}, bf16[2,128,2048]{2,1,0:T(8,128)(2,1)}, u32[]{:S(2)}, u32[]{:S(2)}) collective-permute-start(bf16[2,128,2048]{2,1,0:T(8,128)(2,1)} %dynamic-slice_bitcast_fusion.refs_0_), channel_id=1, source_target_pairs={{0,4},{4,0},{8,12},{12,8},{1,5},{5,1},{9,13},{13,9},{2,6},{6,2},{1... | collective-permute-start | bytes 3145736 | tf_op jit(solution)/shard_map/ppermute | solution.py:119
  7.2 34.3 %collective-permute-start.8 = (bf16[1,128,2048]{2,1,0:T(8,128)(2,1)}, bf16[1,128,2048]{2,1,0:T(8,128)(2,1)}, u32[]{:S(2)}, u32[]{:S(2)}) collective-permute-start(bf16[1,128,2048]{2,1,0:T(8,128)(2,1)} %dynamic-slice_bitcast_fusion.2), channel_id=1, source_target_pairs={{0,8},{4,12},{8,0},{12,4},{1,9},{5,13},{9,1},{13,5},{2,10},{6,14},... | collective-permute-start | bytes 1572872 | tf_op jit(solution)/shard_map/ppermute | solution.py:119
  10.6 44.7 %collective-permute-start.4 = (bf16[128,2048]{1,0:T(8,128)(2,1)}, bf16[128,2048]{1,0:T(8,128)(2,1)S(1)}, u32[]{:S(2)}, u32[]{:S(2)}) collective-permute-start(bf16[128,2048]{1,0:T(8,128)(2,1)} %dynamic-slice_bitcast_fusion.3), channel_id=1, source_target_pairs={{0,8},{4,12},{8,0},{12,4},{1,9},{5,13},{9,1},{13,5},{2,10},{6,14},... | collective-permute-start | bytes 1572872 | tf_op jit(solution)/shard_map/ppermute | solution.py:119
  13.0 43.7 %collective-permute-start.1 = (bf16[8,3,128,128]{3,2,1,0:T(8,128)(2,1)}, bf16[8,3,128,128]{3,2,1,0:T(8,128)(2,1)S(1)}, u32[]{:S(2)}, u32[]{:S(2)}) collective-permute-start(bf16[8,3,128,128]{3,2,1,0:T(8,128)(2,1)} %dynamic-slice_bitcast_fusion.1), channel_id=1, source_target_pairs={{0,2},{2,0},{1,3},{3,1},{4,6},{6,4},{5,7},{7,5},{8,10},{10,8},{9,1... | collective-permute-start | bytes 2359304 | tf_op jit(solution)/shard_map/ppermute | solution.py:119
  14.6 17.2 %collective-permute-start = (s32[2,16,3]{1,0,2:T(2,128)S(1)}, s32[2,16,3]{1,0,2:T(2,128)S(1)}, u32[]{:S(2)}, u32[]{:S(2)}) collective-permute-start(s32[2,16,3]{1,0,2:T(2,128)S(1)} %pad_add_fusion), channel_id=1, source_target_pairs={{0,2},{2,0},{1,3},{3,1},{4,6},{6,4},{5,7},{7,5},{8,10},{10,8},{9,1... | collective-permute-start | bytes 1160 | tf_op jit(solution)/shard_map/ppermute | solution.py:119
  31.8 5.7 %collective-permute-start.3 = (bf16[2,3,128,128]{3,2,1,0:T(8,128)(2,1)S(1)}, bf16[2,3,128,128]{3,2,1,0:T(8,128)(2,1)S(1)}, u32[]{:S(2)}, u32[]{:S(2)}) collective-permute-start(bf16[2,3,128,128]{3,2,1,0:T(8,128)(2,1)S(1)} %pad_maximum_fusion), channel_id=1, source_target_pairs={{0,2},{2,0},{1,3},{3,1},{4,6},{6,4},{5,7},{7,5},{8,10},{10,8},{9,1... | collective-permute-start | bytes 589832 | tf_op jit(solution)/shard_map/ppermute | solution.py:119
  37.4 27.8 %collective-permute-start.5 = (bf16[2,128,2048]{2,1,0:T(8,128)(2,1)}, bf16[2,128,2048]{2,1,0:T(8,128)(2,1)}, u32[]{:S(2)}, u32[]{:S(2)}) collective-permute-start(bf16[2,128,2048]{2,1,0:T(8,128)(2,1)} %dynamic-slice_bitcast_fusion.refs_0_), channel_id=1, source_target_pairs={{0,1},{1,0},{2,3},{3,2},{4,5},{5,4},{6,7},{7,6},{8,9},{9,8},{10,11... | collective-permute-start | bytes 3145736 | tf_op jit(solution)/shard_map/ppermute | solution.py:119
  41.5 22.0 %collective-permute-start.10 = (bf16[1,128,2048]{2,1,0:T(8,128)(2,1)}, bf16[1,128,2048]{2,1,0:T(8,128)(2,1)}, u32[]{:S(2)}, u32[]{:S(2)}) collective-permute-start(bf16[1,128,2048]{2,1,0:T(8,128)(2,1)} %collective-permute-done.8.refs_4_), channel_id=1, source_target_pairs={{0,4},{4,0},{8,12},{12,8},{1,5},{5,1},{9,13},{13,9},{2,6},{6,2},{1... | collective-permute-start | bytes 1572872 | tf_op jit(solution)/shard_map/ppermute | solution.py:119
  55.3 9.9 %collective-permute-start.9 = (bf16[1,128,2048]{2,1,0:T(8,128)(2,1)}, bf16[1,128,2048]{2,1,0:T(8,128)(2,1)}, u32[]{:S(2)}, u32[]{:S(2)}) collective-permute-start(bf16[1,128,2048]{2,1,0:T(8,128)(2,1)} %collective-permute-done.8.refs_4_), channel_id=1, source_target_pairs={{0,2},{2,0},{1,3},{3,1},{4,6},{6,4},{5,7},{7,5},{8,10},{10,8},{9,1... | collective-permute-start | bytes 1572872 | tf_op jit(solution)/shard_map/ppermute | solution.py:119
  56.8 8.9 %collective-permute-start.12 = (bf16[1,128,2048]{2,1,0:T(8,128)(2,1)}, bf16[1,128,2048]{2,1,0:T(8,128)(2,1)}, u32[]{:S(2)}, u32[]{:S(2)}) collective-permute-start(bf16[1,128,2048]{2,1,0:T(8,128)(2,1)} %collective-permute-done.8.refs_4_), channel_id=1, source_target_pairs={{0,1},{1,0},{2,3},{3,2},{4,5},{5,4},{6,7},{7,6},{8,9},{9,8},{10,11... | collective-permute-start | bytes 1572872 | tf_op jit(solution)/shard_map/ppermute | solution.py:119
  56.8 21.8 %collective-permute-start.7 = (bf16[2,128,2048]{2,1,0:T(8,128)(2,1)}, bf16[2,128,2048]{2,1,0:T(8,128)(2,1)}, u32[]{:S(2)}, u32[]{:S(2)}) collective-permute-start(bf16[2,128,2048]{2,1,0:T(8,128)(2,1)} %collective-permute-done.6.refs_2_), channel_id=1, source_target_pairs={{0,1},{1,0},{2,3},{3,2},{4,5},{5,4},{6,7},{7,6},{8,9},{9,8},{10,11... | collective-permute-start | bytes 3145736 | tf_op jit(solution)/shard_map/ppermute | solution.py:119
  63.5 13.4 %collective-permute-start.11 = (bf16[1,128,2048]{2,1,0:T(8,128)(2,1)}, bf16[1,128,2048]{2,1,0:T(8,128)(2,1)}, u32[]{:S(2)}, u32[]{:S(2)}) collective-permute-start(bf16[1,128,2048]{2,1,0:T(8,128)(2,1)} %collective-permute-done.10.refs_6_), channel_id=1, source_target_pairs={{0,2},{2,0},{1,3},{3,1},{4,6},{6,4},{5,7},{7,5},{8,10},{10,8},{9,1... | collective-permute-start | bytes 1572872 | tf_op jit(solution)/shard_map/ppermute | solution.py:119
  65.2 13.4 %collective-permute-start.2 = (bf16[8,3,128,128]{3,2,1,0:T(8,128)(2,1)S(1)}, bf16[8,3,128,128]{3,2,1,0:T(8,128)(2,1)}, u32[]{:S(2)}, u32[]{:S(2)}) collective-permute-start(bf16[8,3,128,128]{3,2,1,0:T(8,128)(2,1)S(1)} %collective-permute-done.1.right_near), channel_id=1, source_target_pairs={{0,1},{1,0},{2,3},{3,2},{4,5},{5,4},{6,7},{7,6},{8,9},{9,8},{10,11... | collective-permute-start | bytes 2359304 | tf_op jit(solution)/shard_map/ppermute | solution.py:119
  65.2 13.4 %collective-permute-start.13 = (bf16[1,128,2048]{2,1,0:T(8,128)(2,1)}, bf16[1,128,2048]{2,1,0:T(8,128)(2,1)}, u32[]{:S(2)}, u32[]{:S(2)}) collective-permute-start(bf16[1,128,2048]{2,1,0:T(8,128)(2,1)} %collective-permute-done.9.refs_5_), channel_id=1, source_target_pairs={{0,1},{1,0},{2,3},{3,2},{4,5},{5,4},{6,7},{7,6},{8,9},{9,8},{10,11... | collective-permute-start | bytes 1572872 | tf_op jit(solution)/shard_map/ppermute | solution.py:119
  65.7 12.9 %collective-permute-start.14 = (bf16[1,128,2048]{2,1,0:T(8,128)(2,1)}, bf16[1,128,2048]{2,1,0:T(8,128)(2,1)}, u32[]{:S(2)}, u32[]{:S(2)}) collective-permute-start(bf16[1,128,2048]{2,1,0:T(8,128)(2,1)} %collective-permute-done.10.refs_6_), channel_id=1, source_target_pairs={{0,1},{1,0},{2,3},{3,2},{4,5},{5,4},{6,7},{7,6},{8,9},{9,8},{10,11... | collective-permute-start | bytes 1572872 | tf_op jit(solution)/shard_map/ppermute | solution.py:119
  99.0 6.9 %collective-permute-start.17 = (f32[8,128]{1,0:T(8,128)}, f32[8,128]{1,0:T(8,128)S(1)}, u32[]{:S(2)}, u32[]{:S(2)}) collective-permute-start(f32[8,128]{1,0:T(8,128)} %get-tuple-element.13.refs_0_), channel_id=1, source_target_pairs={{0,2},{1,3},{2,0},{3,1},{4,6},{5,7},{6,4},{7,5},{8,10},{9,11},{10,... | collective-permute-start | bytes 12296 | tf_op jit(solution)/shard_map/ppermute | solution.py:127
  100.4 5.5 %collective-permute-start.18 = (f32[8,128]{1,0:T(8,128)}, f32[8,128]{1,0:T(8,128)S(1)}, u32[]{:S(2)}, u32[]{:S(2)}) collective-permute-start(f32[8,128]{1,0:T(8,128)} %get-tuple-element.13.refs_0_), channel_id=1, source_target_pairs={{0,3},{1,2},{2,1},{3,0},{4,7},{5,6},{6,5},{7,4},{8,11},{9,10},{10,... | collective-permute-start | bytes 12296 | tf_op jit(solution)/shard_map/ppermute | solution.py:127
  100.8 5.1 %collective-permute-start.19 = (f32[8,128]{1,0:T(8,128)}, f32[8,128]{1,0:T(8,128)S(1)}, u32[]{:S(2)}, u32[]{:S(2)}) collective-permute-start(f32[8,128]{1,0:T(8,128)} %get-tuple-element.13.refs_0_), channel_id=1, source_target_pairs={{0,4},{1,5},{2,6},{3,7},{4,0},{5,1},{6,2},{7,3},{8,12},{9,13},{10,... | collective-permute-start | bytes 12296 | tf_op jit(solution)/shard_map/ppermute | solution.py:127
  117.4 5.6 %collective-permute-start.25 = (f32[8,128]{1,0:T(8,128)}, f32[8,128]{1,0:T(8,128)S(1)}, u32[]{:S(2)}, u32[]{:S(2)}) collective-permute-start(f32[8,128]{1,0:T(8,128)} %get-tuple-element.15.refs_0_), channel_id=1, source_target_pairs={{0,3},{1,2},{2,1},{3,0},{4,7},{5,6},{6,5},{7,4},{8,11},{9,10},{10,... | collective-permute-start | bytes 12296 | tf_op jit(solution)/shard_map/ppermute | solution.py:127
  129.2 25.4 %collective-permute-start.30 = (bf16[2,128,2048]{2,1,0:T(8,128)(2,1)}, bf16[2,128,2048]{2,1,0:T(8,128)(2,1)S(1)}, u32[]{:S(2)}, u32[]{:S(2)}) collective-permute-start(bf16[2,128,2048]{2,1,0:T(8,128)(2,1)} %correct.1.refs_0_), channel_id=1, source_target_pairs={{0,2},{2,0},{1,3},{3,1},{4,6},{6,4},{5,7},{7,5},{8,10},{10,8},{9,1... | collective-permute-start | bytes 3145736 | tf_op jit(solution)/shard_map/ppermute | solution.py:119
  130.4 26.6 %collective-permute-start.33 = (bf16[2,128,2048]{2,1,0:T(8,128)(2,1)}, bf16[2,128,2048]{2,1,0:T(8,128)(2,1)S(1)}, u32[]{:S(2)}, u32[]{:S(2)}) collective-permute-start(bf16[2,128,2048]{2,1,0:T(8,128)(2,1)} %correct.1.refs_0_), channel_id=1, source_target_pairs={{0,4},{4,0},{8,12},{12,8},{1,5},{5,1},{9,13},{13,9},{2,6},{6,2},{1... | collective-permute-start | bytes 3145736 | tf_op jit(solution)/shard_map/ppermute | solution.py:119
  132.1 39.0 %collective-permute-start.34 = (bf16[2,128,2048]{2,1,0:T(8,128)(2,1)}, bf16[2,128,2048]{2,1,0:T(8,128)(2,1)S(1)}, u32[]{:S(2)}, u32[]{:S(2)}) collective-permute-start(bf16[2,128,2048]{2,1,0:T(8,128)(2,1)} %correct.1.refs_0_), channel_id=1, source_target_pairs={{0,1},{1,0},{2,3},{3,2},{4,5},{5,4},{6,7},{7,6},{8,9},{9,8},{10,11... | collective-permute-start | bytes 3145736 | tf_op jit(solution)/shard_map/ppermute | solution.py:119
  155.6 13.1 %collective-permute-start.38 = (bf16[128,2048]{1,0:T(8,128)(2,1)S(1)}, bf16[128,2048]{1,0:T(8,128)(2,1)S(1)}, u32[]{:S(2)}, u32[]{:S(2)}) collective-permute-start(bf16[128,2048]{1,0:T(8,128)(2,1)S(1)} %get-tuple-element.21), channel_id=1, source_target_pairs={{0,4},{4,0},{8,12},{12,8},{1,5},{5,1},{9,13},{13,9},{2,6},{6,2},{1... | collective-permute-start | bytes 1572872 | tf_op jit(solution)/shard_map/ppermute | solution.py:119
  157.1 12.9 %collective-permute-start.37 = (bf16[128,2048]{1,0:T(8,128)(2,1)S(1)}, bf16[128,2048]{1,0:T(8,128)(2,1)S(1)}, u32[]{:S(2)}, u32[]{:S(2)}) collective-permute-start(bf16[128,2048]{1,0:T(8,128)(2,1)S(1)} %slice_bitcast_fusion.1), channel_id=1, source_target_pairs={{0,2},{2,0},{1,3},{3,1},{4,6},{6,4},{5,7},{7,5},{8,10},{10,8},{9,1... | collective-permute-start | bytes 1572872 | tf_op jit(solution)/shard_map/ppermute | solution.py:119
  158.6 15.4 %collective-permute-start.35 = (bf16[2,128,2048]{2,1,0:T(8,128)(2,1)S(1)}, bf16[2,128,2048]{2,1,0:T(8,128)(2,1)S(1)}, u32[]{:S(2)}, u32[]{:S(2)}) collective-permute-start(bf16[2,128,2048]{2,1,0:T(8,128)(2,1)S(1)} %collective-permute-done.33.refs_1_), channel_id=1, source_target_pairs={{0,1},{1,0},{2,3},{3,2},{4,5},{5,4},{6,7},{7,6},{8,9},{9,8},{10,11... | collective-permute-start | bytes 3145736 | tf_op jit(solution)/shard_map/ppermute | solution.py:119
  158.6 15.4 %collective-permute-start.36 = (bf16[2,128,2048]{2,1,0:T(8,128)(2,1)S(1)}, bf16[2,128,2048]{2,1,0:T(8,128)(2,1)S(1)}, u32[]{:S(2)}, u32[]{:S(2)}) collective-permute-start(bf16[2,128,2048]{2,1,0:T(8,128)(2,1)S(1)} %collective-permute-done.30.refs_2_), channel_id=1, source_target_pairs={{0,1},{1,0},{2,3},{3,2},{4,5},{5,4},{6,7},{7,6},{8,9},{9,8},{10,11... | collective-permute-start | bytes 3145736 | tf_op jit(solution)/shard_map/ppermute | solution.py:119
  168.7 5.3 %collective-permute-start.40 = (bf16[128,2048]{1,0:T(8,128)(2,1)S(1)}, bf16[128,2048]{1,0:T(8,128)(2,1)S(1)}, u32[]{:S(2)}, u32[]{:S(2)}) collective-permute-start(bf16[128,2048]{1,0:T(8,128)(2,1)S(1)} %collective-permute-done.38), channel_id=1, source_target_pairs={{0,1},{1,0},{2,3},{3,2},{4,5},{5,4},{6,7},{7,6},{8,9},{9,8},{10,11... | collective-permute-start | bytes 1572872 | tf_op jit(solution)/shard_map/ppermute | solution.py:119
  171.1 26.9 %collective-permute-start.31 = (bf16[128,2048]{1,0:T(8,128)(2,1)}, bf16[128,2048]{1,0:T(8,128)(2,1)}, u32[]{:S(2)}, u32[]{:S(2)}) collective-permute-start(bf16[128,2048]{1,0:T(8,128)(2,1)} %get-tuple-element.23), channel_id=1, source_target_pairs={{0,8},{4,12},{8,0},{12,4},{1,9},{5,13},{9,1},{13,5},{2,10},{6,14},... | collective-permute-start | bytes 1572872 | tf_op jit(solution)/shard_map/ppermute | solution.py:119
  195.0 26.4 %collective-permute-start.42 = (bf16[128,2048]{1,0:T(8,128)(2,1)}, bf16[128,2048]{1,0:T(8,128)(2,1)S(1)}, u32[]{:S(2)}, u32[]{:S(2)}) collective-permute-start(bf16[128,2048]{1,0:T(8,128)(2,1)} %get-tuple-element.17), channel_id=1, source_target_pairs={{0,8},{4,12},{8,0},{12,4},{1,9},{5,13},{9,1},{13,5},{2,10},{6,14},... | collective-permute-start | bytes 1572872 | tf_op jit(solution)/shard_map/ppermute | solution.py:119
  198.0 24.7 %collective-permute-start.32 = (bf16[128,2048]{1,0:T(8,128)(2,1)}, bf16[128,2048]{1,0:T(8,128)(2,1)}, u32[]{:S(2)}, u32[]{:S(2)}) collective-permute-start(bf16[128,2048]{1,0:T(8,128)(2,1)} %collective-permute-done.31.far), channel_id=1, source_target_pairs={{0,2},{2,0},{1,3},{3,1},{4,6},{6,4},{5,7},{7,5},{8,10},{10,8},{9,1... | collective-permute-start | bytes 1572872 | tf_op jit(solution)/shard_map/ppermute | solution.py:119
  200.0 118.3 %collective-permute-start.41 = (bf16[128,2048]{1,0:T(8,128)(2,1)}, bf16[128,2048]{1,0:T(8,128)(2,1)S(1)}, u32[]{:S(2)}, u32[]{:S(2)}) collective-permute-start(bf16[128,2048]{1,0:T(8,128)(2,1)} %get-tuple-element.16.near), channel_id=1, source_target_pairs={{0,2},{2,0},{1,3},{3,1},{4,6},{6,4},{5,7},{7,5},{8,10},{10,8},{9,1... | collective-permute-start | bytes 1572872 | tf_op jit(solution)/shard_map/ppermute | solution.py:119
  221.4 97.0 %collective-permute-start.43 = (bf16[128,2048]{1,0:T(8,128)(2,1)S(1)}, bf16[128,2048]{1,0:T(8,128)(2,1)}, u32[]{:S(2)}, u32[]{:S(2)}) collective-permute-start(bf16[128,2048]{1,0:T(8,128)(2,1)S(1)} %collective-permute-done.42.far), channel_id=1, source_target_pairs={{0,2},{2,0},{1,3},{3,1},{4,6},{6,4},{5,7},{7,5},{8,10},{10,8},{9,1... | collective-permute-start | bytes 1572872 | tf_op jit(solution)/shard_map/ppermute | solution.py:119
  (46 other events, 428.7 us)

commit v2 on v1

--- a/solution.py
+++ b/solution.py
@@ -138,18 +138,21 @@
     return sum(value[:, at : at + LANES] for at in range(0, width, LANES))
 
 
-def operate_kernel(
-    first, plan, cols, pattern, right_own, right_near, right_far, left_own, left_other, hd_own, hd_far, *refs
-):
+def row_of(dz, dx, dc):
+    z, x, c = place()
+    return 4 * (z ^ dz) + 2 * (c ^ dc) + (x ^ dx if dx < 2 else dx - 2)
+
+
+def operate_kernel(first, plan, cols, pattern, right_own, right_near, right_far, left_own, *refs):
     count = len(plan)
     pieces, refs = refs[:count], refs[count:]
     if first:
-        psi_out, sigma_out, stats_out = refs[:3]
-        refs = refs[3:]
+        weight_own, weight_far, psi_out, off_out, stats_out = refs[:5]
+        refs = refs[5:]
     else:
-        psi_in, sigma_in, near_out, far_out, stats_out = refs[:5]
-        refs = refs[5:]
-    field, picked, images, right, left, diag, sems = refs
+        hd_own, hd_far, psi_in, off_in, near_out, far_out, late_out, stats_out = refs[:8]
+        refs = refs[8:]
+    field, images, right, left, diag, sems = refs
     z, x, c = place()
     sectors, block, width = field.shape
     links = right.shape[2]
@@ -163,20 +166,23 @@
         copy.start()
         copies.append(copy)
 
+    part = sectors // 2
+    near, far = pl.ds(c * part, part), pl.ds((1 - c) * part, part)
+    begin(right_own.at[0], right.at[x])
     for piece, offsets in zip(pieces, plan):
-        for at, (dz, dx, dc) in enumerate(offsets):
-            row = 4 * (z ^ dz) + 2 * (c ^ dc) + (x ^ dx if dx < 2 else dx - 2)
-            begin(piece.at[at], field.at[row])
-    part = right_near.shape[0]
-    begin(right_own.at[0], right.at[0])
-    begin(right_near, right.at[1, pl.ds(c * part, part)])
-    begin(right_far, right.at[1, pl.ds((1 - c) * part, part)])
+        tall = piece.shape[1]
+        for at, (dz, dx, dc, chunk) in enumerate(offsets):
+            begin(piece.at[at], field.at[row_of(dz, dx, dc), pl.ds(chunk * tall, tall)])
+    begin(right_near.at[pl.ds(0, part)], right.at[1 - x, near])
+    begin(right_far, right.at[1 - x, far])
+    early = len(copies)
     for at in range(2):
-        begin(left_own.at[0, rows[at]], left.at[0, at])
-    begin(left_other, left.at[1])
-    begin(hd_own.at[x], diag.at[0])
-    begin(hd_far, diag.at[1])
-    for copy in copies:
+        begin(left_own.at[0, rows[at]], left.at[x, at])
+    begin(right_near.at[pl.ds(part, 2)], left.at[1 - x])
+    if not first:
+        begin(hd_own.at[x], diag.at[0])
+        begin(hd_far, diag.at[1])
+    for copy in copies[:early]:
         copy.wait()
 
     table = sectors * links
@@ -190,27 +196,21 @@
     def allowed(a, q, value):
         return jnp.where(pattern[a * sectors + q] != 0, value, jnp.zeros_like(value))
 
-    for term in range(2):
-        for at in range(2):
-            for j in range(links):
-                source = left_col(term, rows[at], j)
-                spot = (at * links + j) * block
-                for q in range(sectors):
-                    span = slice(q * block, (q + 1) * block)
-                    value = field[source, :, span]
-                    if first:
-                        value = allowed(source, q, value)
-                    picked[term, spot : spot + block, span] = value
+    sources = [[left_col(term, rows[at], j) for at in range(2) for j in range(links)] for term in range(2)]
 
     def image(b, carry):
         for term in range(2):
+            found = [right_col(term, b, j) for j in range(links)]
             lhs = []
-            for j in range(links):
-                start = pl.multiple_of(right_col(term, b, j) * block, block)
-                lhs.append(picked[term, :, pl.ds(start, block)])
+            for source in sources[term]:
+                line = []
+                for col in found:
+                    value = field[source, :, pl.ds(pl.multiple_of(col * block, block), block)]
+                    line.append(allowed(source, col, value) if first else value)
+                lhs.append(jnp.concatenate(line, axis=1))
             rhs = [right[term, b, j] for j in range(links)]
             product = lax.dot_general(
-                jnp.concatenate(lhs, axis=1),
+                jnp.concatenate(lhs, axis=0),
                 jnp.concatenate(rhs, axis=1),
                 (((1,), (1,)), ((), ())),
                 preferred_element_type=jnp.float32,
@@ -219,15 +219,25 @@
         return carry
 
     lax.fori_loop(0, sectors, image, 0)
+    for copy in copies[early:]:
+        copy.wait()
 
     step = 2
     deep = links * block
+    half = block // 2
     zero = jnp.zeros((8, LANES), jnp.float32)
 
     def column(n, sums):
         start = pl.multiple_of(n * step * block, step * block)
         span = pl.ds(start, step * block)
         sums = list(sums)
+
+        def masked(a, value):
+            parts = [
+                allowed(a, n * step + i, value[:, i * block : (i + 1) * block]) for i in range(step)
+            ]
+            return jnp.concatenate(parts, axis=1)
+
         for at in range(2):
             total = None
             for term in range(2):
@@ -238,60 +248,58 @@
                     preferred_element_type=jnp.float32,
                 )
                 total = product if total is None else total + product
-            total = total.astype(jnp.bfloat16).astype(jnp.float32)
-            offdiag = jnp.concatenate(
-                [allowed(rows[at], n * step + i, total[:, i * block : (i + 1) * block]) for i in range(step)],
-                axis=1,
-            )
+            offdiag = masked(rows[at], total.astype(jnp.bfloat16).astype(jnp.float32))
             own = field[rows[at], :, span].astype(jnp.float32)
             if first:
-                own = jnp.concatenate(
-                    [allowed(rows[at], n * step + i, own[:, i * block : (i + 1) * block]) for i in range(step)],
-                    axis=1,
-                )
-            result = diag[at, :, span].astype(jnp.float32) * own + offdiag
-            if first:
+                own = masked(rows[at], own)
                 psi_out[at, :, span] = own.astype(jnp.bfloat16)
-                sigma_out[at, :, span] = result
+                off_out[at, :, span] = offdiag.astype(jnp.bfloat16)
                 sums[0] += fold(own * own)
-                sums[1] += fold(own * result)
+                sums[1] += fold(own * offdiag)
             else:
-                narrow = result.astype(jnp.bfloat16)
-                (near_out, far_out)[at][:, span] = narrow
+                weight = diag[at, :, span].astype(jnp.float32)
+                narrow = (weight * own + offdiag).astype(jnp.bfloat16)
+                if at == 0:
+                    near_out[:, span] = narrow
+                else:
+                    far_out[:, span] = narrow[:half]
+                    late_out[:, span] = narrow[half:]
                 second = narrow.astype(jnp.float32)
-                sums[0] += fold(psi_in[at, :, span].astype(jnp.float32) * second)
-                sums[1] += fold(own * sigma_in[at, :, span])
+                wave = psi_in[at, :, span].astype(jnp.float32)
+                sigma_one = weight * wave + off_in[at, :, span].astype(jnp.float32)
+                sums[0] += fold(wave * second)
+                sums[1] += fold(own * sigma_one)
                 sums[2] += fold(own * second)
         return tuple(sums)
 
-    sums = lax.fori_loop(0, sectors // step, column, (zero,) * (2 if first else 3))
+    sums = list(lax.fori_loop(0, sectors // step, column, (zero,) * (2 if first else 3)))
+    if first:
+        sums[1] += weight_own[...] + weight_far[...]
     stats_out[...] = jnp.zeros_like(stats_out)
     for at, value in enumerate(sums):
         stats_out[at : at + 1, :] = jnp.sum(value, axis=0, keepdims=True)
 
 
-def operate(first, plan, pieces, cols, pattern, right, left, diag, extra=()):
-    _, block, width = pieces[0].shape
+def operate(first, plan, pieces, cols, pattern, right, left, extra):
     right_own, right_near, right_far = right
-    _, sectors, links = right_own.shape[:3]
+    _, sectors, links, block = right_own.shape[:4]
+    width = sectors * block
     rows = jax.ShapeDtypeStruct((2, block, width), jnp.bfloat16)
     one = jax.ShapeDtypeStruct((block, width), jnp.bfloat16)
+    some = jax.ShapeDtypeStruct((block // 2, width), jnp.bfloat16)
     stats = jax.ShapeDtypeStruct((8, LANES), jnp.float32)
-    if first:
-        out_shape = (rows, jax.ShapeDtypeStruct((2, block, width), jnp.float32), stats)
-    else:
-        out_shape = (one, one, stats)
+    out_shape = (rows, rows, stats) if first else (one, some, some, stats)
+    extra_specs = [VMEM, VMEM] if first else [ANY, ANY, VMEM, VMEM]
     copies = sum(len(offsets) for offsets in plan) + 8
     inner = 2 * 2 * sectors * 2 * links * links * block * block * block
     outer = 2 * 2 * 2 * links * block * block * width
     return pl.pallas_call(
         functools.partial(operate_kernel, first, plan),
         out_shape=out_shape,
-        in_specs=[SMEM, SMEM] + [ANY] * (7 + len(pieces)) + [VMEM] * len(extra),
+        in_specs=[SMEM, SMEM] + [ANY] * (4 + len(pieces)) + extra_specs,
         out_specs=(VMEM,) * len(out_shape),
         scratch_shapes=[
             pltpu.VMEM((sectors, block, width), jnp.bfloat16),
-            pltpu.VMEM((2, 2 * links * block, width), jnp.bfloat16),
             pltpu.VMEM((2, 2 * links * block, width), jnp.bfloat16),
             pltpu.VMEM((2, sectors, links, block, block), jnp.bfloat16),
             pltpu.VMEM((2, 2, links, block, block), jnp.bfloat16),
@@ -303,14 +311,63 @@
             flops=inner + outer, bytes_accessed=16 * 1024 * 1024, transcendentals=0
         ),
         name="operate_first" if first else "operate_second",
-    )(cols, pattern, right_own, right_near, right_far, *left, *diag, *pieces, *extra)
+    )(cols, pattern, right_own, right_near, right_far, left, *pieces, *extra)
+
+
+def weigh_kernel(pattern, theta, hd, own_out, other_out, waves, diag, sems):
+    z, x, c = place()
+    copies = [
+        pltpu.make_async_copy(theta.at[0, x], waves.at[0], sems.at[0]),
+        pltpu.make_async_copy(theta.at[1, x], waves.at[1], sems.at[1]),
+        pltpu.make_async_copy(hd.at[x], diag, sems.at[2]),
+    ]
+    for copy in copies:
+        copy.start()
+    for copy in copies:
+        copy.wait()
+    block, width = diag.shape
+    sectors = width // block
+    mine = 4 * z + 2 * c + x
+    zero = jnp.zeros((8, LANES), jnp.float32)
+
+    def column(q, sums):
+        span = pl.ds(pl.multiple_of(q * block, block), block)
+        weight = diag[:, span].astype(jnp.float32)
+        weight = jnp.where(pattern[mine * sectors + q] != 0, weight, jnp.zeros_like(weight))
+        found = []
+        for root in range(2):
+            wave = waves[root, :, span].astype(jnp.float32)
+            found.append(sums[root] + fold(weight * wave * wave))
+        return tuple(found)
+
+    sums = lax.fori_loop(0, sectors, column, (zero, zero))
+    upper = z // 2 == 1
+    own_out[...] = jnp.where(upper, sums[1], sums[0])
+    other_out[...] = jnp.where(upper, sums[0], sums[1])
+
+
+def weigh(pattern, theta, hd):
+    _, _, block, width = theta.shape
+    stats = jax.ShapeDtypeStruct((8, LANES), jnp.float32)
+    return pl.pallas_call(
+        weigh_kernel,
+        out_shape=(stats, stats),
+        in_specs=[SMEM, ANY, ANY],
+        out_specs=(VMEM, VMEM),
+        scratch_shapes=[
+            pltpu.VMEM((2, block, width), theta.dtype),
+            pltpu.VMEM((block, width), hd.dtype),
+            pltpu.SemaphoreType.DMA((3,)),
+        ],
+        name="weigh",
+    )(pattern, theta, hd)
 
 
 def total_of(rows):
     return jnp.sum(rows, axis=1, keepdims=True)
 
 
-def update_kernel(psi, sigma, hd_own, hd_far, *refs):
+def update_kernel(psi, off, hd_own, hd_far, *refs):
     stats, (t_out, stats_out, diag, sems) = refs[:8], refs[8:]
     z, x, c = place()
     copies = [
@@ -333,8 +390,10 @@
         span = pl.ds(pl.multiple_of(n * step, step), step)
         for at in range(2):
             wave = psi[at, span, :].astype(jnp.float32)
-            shifted = diag[at, span, :].astype(jnp.float32) - energy
-            t = (sigma[at, span, :] - energy * wave) * shifted / (shifted * shifted + 1.0)
+            weight = diag[at, span, :].astype(jnp.float32)
+            sigma = weight * wave + off[at, span, :].astype(jnp.float32)
+            shifted = weight - energy
+            t = (sigma - energy * wave) * shifted / (shifted * shifted + 1.0)
             t_out[at, span, :] = t
             total = total + fold(wave * t)
         return total
@@ -360,7 +419,7 @@
 
 
 def correct_kernel(psi, t, *refs):
-    stats, (out,) = refs[:8], refs[8:]
+    stats, outs = refs[:8], refs[8:]
     norm_sq = stats[0][4:5, 0:1]
     factor = sum(ref[0:1, 0:1] for ref in stats) / (norm_sq + 1e-06)
     length_sq = jnp.zeros((1, 1), jnp.float32)
@@ -375,104 +434,127 @@
         span = pl.ds(pl.multiple_of(n * step, step), step)
         for at in range(2):
             wave = psi[at, span, :].astype(jnp.float32)
-            out[at, span, :] = ((t[at, span, :] - factor * wave) * scale).astype(jnp.bfloat16)
+            outs[at][span, :] = ((t[at, span, :] - factor * wave) * scale).astype(jnp.bfloat16)
         return carry
 
     lax.fori_loop(0, block // step, chunk, 0)
 
 
-def assemble_kernel(near, near_x, far, far_x, out, sems):
+def assemble_kernel(tall, *refs):
+    count = len(tall)
+    pieces, (out, sems) = refs[:count], refs[count:]
     z, x, c = place()
     half = z // 2
-    copies = [
-        pltpu.make_async_copy(near, out.at[half, x], sems.at[0]),
-        pltpu.make_async_copy(near_x, out.at[half, 1 - x], sems.at[1]),
-        pltpu.make_async_copy(far, out.at[1 - half, x], sems.at[2]),
-        pltpu.make_async_copy(far_x, out.at[1 - half, 1 - x], sems.at[3]),
-    ]
+    copies = []
+    for at, (root, flip, chunk) in enumerate(tall):
+        size = pieces[at].shape[0]
+        target = out.at[half ^ root, x ^ flip, pl.ds(chunk * size, size)]
+        copies.append(pltpu.make_async_copy(pieces[at], target, sems.at[at]))
     for copy in copies:
         copy.start()
     for copy in copies:
         copy.wait()
 
 
-def assemble(near, near_x, far, far_x):
-    block, width = near.shape
+def assemble(block, pieces, tall):
+    width = pieces[0].shape[1]
     return pl.pallas_call(
-        assemble_kernel,
-        out_shape=jax.ShapeDtypeStruct((2, 2, block, width), near.dtype),
-        in_specs=[ANY] * 4,
+        functools.partial(assemble_kernel, tall),
+        out_shape=jax.ShapeDtypeStruct((2, 2, block, width), pieces[0].dtype),
+        in_specs=[VMEM] * len(pieces),
         out_specs=ANY,
-        scratch_shapes=[pltpu.SemaphoreType.DMA((4,))],
+        scratch_shapes=[pltpu.SemaphoreType.DMA((len(pieces),))],
+        compiler_params=pltpu.CompilerParams(vmem_limit_bytes=VMEM_LIMIT),
         name="assemble",
-    )(near, near_x, far, far_x).reshape(2, 2 * block, width)
+    )(*pieces).reshape(2, 2 * block, width)
+
+
+def after(value, *others):
+    return lax.optimization_barrier((value, *others))[0]
 
 
 def shards(theta, hdiag, pattern, left_blocks, left_cols, right_blocks, right_cols):
     roots, row_count, width = theta.shape
     sectors = pattern.shape[0]
     block = width // sectors
-    links = left_cols.shape[2]
     z, x, c = place()
     half = z // 2
     mine = 4 * z + 2 * c + x
 
     halves = theta.reshape(roots, 2, block, width)
     diag = hdiag.reshape(2, block, width)
-
-    own = lax.dynamic_index_in_dim(halves, half, 0, keepdims=False)
-    given = lax.dynamic_slice(halves, (1 - half, x, 0, 0), (1, 1, block, width))[0]
-    far = across(given, "blk", 2)
-    near_z = across(own, "blk", 1)
-    cols_own = jnp.stack([right_cols[0], left_cols[0]])
-    cols_other = across(cols_own, "ops", 1)
+    allowed = pattern.reshape(-1)
+    chunk = block // 2
+
+    def given(at):
+        return lax.dynamic_slice(halves, (1 - half, x, at * chunk, 0), (1, 1, chunk, width))[0, 0]
+
+    far_a = across(given(0), "blk", 2)
+    own = [
+        lax.dynamic_slice(halves, (half, at, 0, 0), (1, 1, block, width))[0, 0] for at in range(2)
+    ]
+    near_a = across(own[0], "blk", 1)
     part = sectors // 2
-    right_near = across(lax.dynamic_slice_in_dim(right_blocks[0], c * part, part, 0), "ops", 1)
-    wanted = jnp.stack(
+    packed = jnp.concatenate(
         [
-            lax.dynamic_index_in_dim(left_blocks[0], mine ^ 1, 0, keepdims=False),
-            lax.dynamic_index_in_dim(left_blocks[0], mine ^ 9, 0, keepdims=False),
+            lax.dynamic_slice_in_dim(right_blocks[0], c * part, part, 0),
+            lax.dynamic_slice_in_dim(left_blocks[0], mine ^ 1, 1, 0),
+            lax.dynamic_slice_in_dim(left_blocks[0], mine ^ 9, 1, 0),
         ]
     )
-    left_other = across(wanted, "ops", 1)
-    own_core = across(own, "sub", 1)
-    right_far = across(right_near, "sub", 1)
-    near_z_core = across(near_z, "sub", 1)
-    far_z = across(far, "blk", 1)
-    far_x = across(far, "ops", 1)
-    far_core = across(far, "sub", 1)
-    far_zx = across(far_z, "ops", 1)
-    far_x_core = across(far_x, "sub", 1)
-    far_z_core = across(far_z, "sub", 1)
-    far_zx_core = across(far_zx, "sub", 1)
-    hd_far = across(lax.dynamic_index_in_dim(diag, x, 0, keepdims=False), "blk", 2)
-
-    cols = jnp.concatenate([cols_own.reshape(-1), cols_other.reshape(-1)])
-    allowed = pattern.reshape(-1)
-    right = (right_blocks, right_near, right_far)
-    left = (left_blocks, left_other)
-    pieces = [own, own_core, near_z, near_z_core]
-    plan = [
-        ((0, 2, 0), (0, 3, 0)),
-        ((0, 2, 1), (0, 3, 1)),
-        ((1, 2, 0), (1, 3, 0)),
-        ((1, 2, 1), (1, 3, 1)),
-    ]
-    for piece, offset in (
-        (far, (2, 0, 0)),
-        (far_x, (2, 1, 0)),
-        (far_z, (3, 0, 0)),
-        (far_zx, (3, 1, 0)),
-        (far_core, (2, 0, 1)),
-        (far_x_core, (2, 1, 1)),
-        (far_z_core, (3, 0, 1)),
-        (far_zx_core, (3, 1, 1)),
+    operators = across(packed, "ops", 1)
+    cols = jnp.concatenate([right_cols.reshape(-1), left_cols.reshape(-1)])
+    cols = lax.all_gather(cols, "ops").reshape(-1)
+    own_core = [across(value, "sub", 1) for value in own]
+    weight_own, weight_far = weigh(allowed, halves, diag)
+
+    far_b = across(after(given(1), far_a, *own_core), "blk", 2)
+    far_za = across(far_a, "blk", 1)
+    far_xa = across(far_a, "ops", 1)
+    operators_core = across(operators[:part], "sub", 1)
+    near_a_core = across(near_a, "sub", 1)
+
+    far_zb = across(far_b, "blk", 1)
+    far_xb = across(far_b, "ops", 1)
+    far_zxa = across(after(far_za, far_b), "ops", 1)
+    near_b = across(after(own[1], far_b), "blk", 1)
+    core_a = across(jnp.stack([far_a, far_b, far_xa, far_za]), "sub", 1)
+    far_zxb = across(after(far_zb, far_xb), "ops", 1)
+    weight_far = across(after(weight_far, far_zb), "blk", 2)
+    core_b = across(jnp.stack([far_xb, far_zxa, far_zb]), "sub", 1)
+    near_b_core = across(near_b, "sub", 1)
+    far_zxb_core = across(far_zxb, "sub", 1)
+    hd_far = lax.dynamic_index_in_dim(diag, x, 0, keepdims=False)
+    hd_far = across(after(hd_far, far_zb), "blk", 2)
+
+    right = (right_blocks, operators, operators_core)
+    pieces = []
+    plan = []
+    for piece, offsets in (
+        (own[0], ((0, 2, 0, 0),)),
+        (own[1], ((0, 3, 0, 0),)),
+        (own_core[0], ((0, 2, 1, 0),)),
+        (own_core[1], ((0, 3, 1, 0),)),
+        (near_a, ((1, 2, 0, 0),)),
+        (near_b, ((1, 3, 0, 0),)),
+        (near_a_core, ((1, 2, 1, 0),)),
+        (near_b_core, ((1, 3, 1, 0),)),
+        (far_a, ((2, 0, 0, 0),)),
+        (far_b, ((2, 0, 0, 1),)),
+        (far_xa, ((2, 1, 0, 0),)),
+        (far_xb, ((2, 1, 0, 1),)),
+        (far_za, ((3, 0, 0, 0),)),
+        (far_zb, ((3, 0, 0, 1),)),
+        (far_zxa, ((3, 1, 0, 0),)),
+        (far_zxb, ((3, 1, 0, 1),)),
+        (far_zxb_core, ((3, 1, 1, 1),)),
+        (core_a, ((2, 0, 1, 0), (2, 0, 1, 1), (2, 1, 1, 0), (3, 0, 1, 0))),
+        (core_b, ((2, 1, 1, 1), (3, 1, 1, 0), (3, 0, 1, 1))),
     ):
-        pieces.append(piece)
-        plan.append((offset,))
-    pieces = [piece.reshape(-1, block, width) for piece in pieces]
-    psi, sigma_one, stats_one = operate(
-        True, tuple(plan), pieces, cols, allowed, right, left, (diag, hd_far)
+        pieces.append(piece if piece.ndim == 3 else piece[None])
+        plan.append(offsets)
+    psi, off_one, stats_one = operate(
+        True, tuple(plan), pieces, cols, allowed, right, left_blocks, (weight_own, weight_far)
     )
 
     found = share(stats_one)
@@ -490,58 +572,72 @@
         ],
         compiler_params=pltpu.CompilerParams(vmem_limit_bytes=VMEM_LIMIT),
         name="update",
-    )(psi, sigma_one, diag, hd_far, *found)
+    )(psi, off_one, diag, hd_far, *found)
     found = share(stats_two)
-    changed = pl.pallas_call(
+    one = jax.ShapeDtypeStruct((block, width), jnp.bfloat16)
+    near, far = pl.pallas_call(
         correct_kernel,
-        out_shape=jax.ShapeDtypeStruct((2, block, width), jnp.bfloat16),
+        out_shape=(one, one),
         in_specs=[VMEM, VMEM] + [VMEM] * 8,
-        out_specs=VMEM,
+        out_specs=(VMEM, VMEM),
         compiler_params=pltpu.CompilerParams(vmem_limit_bytes=VMEM_LIMIT),
         name="correct",
     )(psi, t, *found)
 
-    by_z = across(changed, "blk", 1)
-    by_x = across(changed, "ops", 1)
-    by_core = across(changed, "sub", 1)
-    by_zx_near = across(by_z[0], "ops", 1)
-    by_zx_far = across(by_x[1], "blk", 1)
-    by_z_core = across(by_z, "sub", 1)
-    by_x_core = across(by_x, "sub", 1)
-    by_zx_near_core = across(by_zx_near, "sub", 1)
-    by_zx_far_core = across(by_zx_far, "sub", 1)
+    near_z = across(near, "blk", 1)
+    far_x = across(far, "ops", 1)
+    near_core = across(near, "sub", 1)
+    far_core = across(far, "sub", 1)
+    near_zx = across(after(near_z, far_x), "ops", 1)
+    far_xz = across(after(far_x, near_z), "blk", 1)
+    near_x = across(after(near, near_z, far_x), "ops", 1)
+    far_z = across(after(far, near_z, far_x), "blk", 1)
+    near_z_core = across(near_z, "sub", 1)
+    far_x_core = across(far_x, "sub", 1)
+    near_x_core = across(near_x, "sub", 1)
+    far_z_core = across(far_z, "sub", 1)
+    near_zx_core = across(near_zx, "sub", 1)
+    far_xz_core = across(far_xz, "sub", 1)
+    other = across(after(far, near_x, far_z), "blk", 2)
     pieces, plan = [], []
     for piece, offset in (
-        (changed, (0, 0, 0)),
-        (by_z, (1, 0, 0)),
-        (by_x, (0, 1, 0)),
-        (by_core, (0, 0, 1)),
-        (by_z_core, (1, 0, 1)),
-        (by_x_core, (0, 1, 1)),
-    ):
-        pieces.append(piece)
-        plan.append((offset, (offset[0] ^ 2, offset[1], offset[2])))
-    for piece, offset in (
-        (by_zx_near, (1, 1, 0)),
-        (by_zx_far, (3, 1, 0)),
-        (by_zx_near_core, (1, 1, 1)),
-        (by_zx_far_core, (3, 1, 1)),
+        (near, (0, 0, 0, 0)),
+        (far, (2, 0, 0, 0)),
+        (near_core, (0, 0, 1, 0)),
+        (far_core, (2, 0, 1, 0)),
+        (near_z, (1, 0, 0, 0)),
+        (far_z, (3, 0, 0, 0)),
+        (near_z_core, (1, 0, 1, 0)),
+        (far_z_core, (3, 0, 1, 0)),
+        (near_x, (0, 1, 0, 0)),
+        (far_x, (2, 1, 0, 0)),
+        (near_x_core, (0, 1, 1, 0)),
+        (far_x_core, (2, 1, 1, 0)),
+        (near_zx, (1, 1, 0, 0)),
+        (far_xz, (3, 1, 0, 0)),
+        (near_zx_core, (1, 1, 1, 0)),
+        (far_xz_core, (3, 1, 1, 0)),
     ):
         pieces.append(piece[None])
         plan.append((offset,))
-    two_near, two_far, stats_three = operate(
-        False, tuple(plan), pieces, cols, allowed, right, left, (diag, hd_far), (psi, sigma_one)
-    )
-
-    other = across(changed[1], "blk", 2)
-    correction = assemble(changed[0], by_x[0], other, across(other, "ops", 1))
-    other = across(two_far, "blk", 2)
-    sigma_two = assemble(two_near, across(two_near, "ops", 1), other, across(other, "ops", 1))
-
+    two_near, two_far, two_late, stats_three = operate(
+        False, tuple(plan), pieces, cols, allowed, right, left_blocks, (diag, hd_far, psi, off_one)
+    )
+
+    far_in = across(two_far, "blk", 2)
+    near_in = across(two_near, "ops", 1)
+    late_in = across(after(two_late, far_in), "blk", 2)
+    far_in_x = across(far_in, "ops", 1)
+    other_x = across(after(other, two_near), "ops", 1)
     sums = jnp.concatenate([jnp.sum(stats_one[:2], axis=1), jnp.sum(stats_three[:3], axis=1)])
     here = (jnp.arange(roots) == half)[:, None]
     sums = lax.psum(jnp.where(here, sums[None, :], 0.0), ("blk", "ops", "sub"))
     subspace = sums[:, 1:5] / (sums[:, 0:1] + 1e-06)
+    late_in_x = across(after(late_in, sums), "ops", 1)
+    places = ((0, 0, 0), (0, 1, 0), (1, 0, 0), (1, 1, 0))
+    correction = assemble(block, (near, near_x, other, other_x), places)
+    places = ((0, 0, 0), (0, 1, 0), (1, 0, 0), (1, 0, 1), (1, 1, 0), (1, 1, 1))
+    sigma_two = assemble(block, (two_near, near_in, far_in, late_in, far_in_x, late_in_x), places)
     return correction, sigma_two, subspace
 
 

time: 384 us -> 256 us (0.67)
  Pallas kernels: 178 us -> 54 us
  waiting for transfers between devices: 114 us -> 96.2 us
  blocking collectives: 30.2 us -> 38.2 us
    pallas_call x3 -> x4, Pallas kernels: 133 us -> 12.6 us  [the longest x2 5.72 us: assemble(): pl.pallas_call(functools.partial(assemble_kernel, tall), out_shape=jax.Sh...]
    ppermute x30 -> x42, waiting for transfers between devices: 107 us -> 90.3 us  [across(): return lax.ppermute(value, axis, [(i, i ^ distance) for i in range(size)])]
    unnamed x0 -> x1, blocking collectives: none -> 4.81 us
    ppermute x30 -> x42, starting transfers between devices: 30.5 us -> 34 us  [across(): return lax.ppermute(value, axis, [(i, i ^ distance) for i in range(size)])]
  transfers between devices with their start and end apart: 44 -> 56, of which waited for: 16 -> 23; matrix products, arithmetic and copies ran while one was open for 3% -> 4% of each run, Pallas kernels for 22% -> 16%
where the time goes in v2:
time: 256 us; the launch traced here: 255 us
  waiting for transfers between devices  96.2 us (38%)
  Pallas kernels  54 us (21%)
  starting transfers between devices  46.6 us (18%)
  blocking collectives  38.2 us (15%)
  local copies, waits for them, and re-layouts  13.5 us (5%)
  other arithmetic  4.86 us (2%)
    ppermute x42, waiting for transfers between devices, across(): return lax.ppermute(value, axis, [(i, i ^ distance) for i in range(size)])  90.3 us
    pallas_call x2, Pallas kernels, operate(): pl.pallas_call(functools.partial(operate_kernel, first, plan), out_shape=...  35.5 us
    ppermute x42, starting transfers between devices, across(): return lax.ppermute(value, axis, [(i, i ^ distance) for i in range(size)])  34 us
    psum x1, blocking collectives, shards(): sums = lax.psum(jnp.where(here, sums[None, :], 0.0), ('blk', 'ops', 'sub'))  33.4 us
    ppermute x14, starting transfers between devices, share(): lax.ppermute(stats, axes, [(i, i ^ distance) for i in range(count)])  12.6 us
    unnamed x114, local copies, waits for them, and re-layouts  5.99 us
    pallas_call x1, Pallas kernels, shards(): pl.pallas_call(update_kernel, out_shape=(jax.ShapeDtypeStruct((2, block,...  5.93 us
    ppermute x14, waiting for transfers between devices, share(): lax.ppermute(stats, axes, [(i, i ^ distance) for i in range(count)])  5.87 us
  transfers between devices with their start and end apart: 56, of which 23 were waited for; matrix products, arithmetic and copies ran while one was open for 4% of the time, Pallas kernels for 16%

profile of v2, /device:TPU:0, one launch (start us, length us, event | category | flops | bytes accessed | tf_op | source)
XLA Modules:
  0.0 255.2 jit_solution(6139339295904260983)
XLA Ops:
  0.7 2.8 %dynamic-slice_bitcast_fusion.2 = (bf16[128,2048]{1,0:T(8,128)(2,1)}, bf16[128,2048]{1,0:T(8,128)(2,1)}, bf16[1,128,2048]{2,1,0:T(8,128)(2,1)}, bf16[1,128,2048]{2,1,0:T(8,128)(2,1)}) fusion(bf16[2,2,128,2048]{3,2,1,0:T(8,128)(2,1)} %bitcast.60, s32[]{:T(128)S(6)} %select_n.36), kind=kLoop, calls=%fused_computation.5 | loop fusion | bytes 3145732 | tf_op jit(solution)/shard_map/squeeze | solution.py:494
  5.1 3.0 %collective-permute-start = (bf16[10,3,128,128]{3,2,1,0:T(8,128)(2,1)S(1)}, bf16[10,3,128,128]{3,2,1,0:T(8,128)(2,1)S(1)}, u32[]{:S(2)}, u32[]{:S(2)}) collective-permute-start(bf16[10,3,128,128]{3,2,1,0:T(8,128)(2,1)S(1)} %pad_maximum_fusion.1), channel_id=1, source_target_pairs={{0,2},{2,0},{1,3},{3,1},{4,6},{6,4},{5,7},{7,5},{8,10},{10,8},{9,1... | collective-permute-start | bytes 2949128 | tf_op jit(solution)/shard_map/ppermute | solution.py:119
  9.2 2.7 %collective-permute-start.5 = (bf16[64,2048]{1,0:T(8,128)(2,1)S(1)}, bf16[64,2048]{1,0:T(8,128)(2,1)S(1)}, u32[]{:S(2)}, u32[]{:S(2)}) collective-permute-start(bf16[64,2048]{1,0:T(8,128)(2,1)S(1)} %get-tuple-element.57), channel_id=1, source_target_pairs={{0,8},{4,12},{8,0},{12,4},{1,9},{5,13},{9,1},{13,5},{2,10},{6,14},... | collective-permute-start | bytes 786440 | tf_op jit(solution)/shard_map/ppermute | solution.py:119
  11.8 1.6 collective-permute-start.4
  13.4 10.4 %collective-permute-done.5 = bf16[64,2048]{1,0:T(8,128)(2,1)S(1)} collective-permute-done((bf16[64,2048]{1,0:T(8,128)(2,1)S(1)}, bf16[64,2048]{1,0:T(8,128)(2,1)S(1)}, u32[]{:S(2)}, u32[]{:S(2)}) %collective-permute-start.5) | collective-permute-done | bytes 262176 | tf_op jit(solution)/shard_map/ppermute | solution.py:119
  24.4 3.5 %collective-permute-start.6 = (bf16[64,2048]{1,0:T(8,128)(2,1)S(1)}, bf16[64,2048]{1,0:T(8,128)(2,1)S(1)}, u32[]{:S(2)}, u32[]{:S(2)}) collective-permute-start(bf16[64,2048]{1,0:T(8,128)(2,1)S(1)} %get-tuple-element.30), channel_id=1, source_target_pairs={{0,8},{4,12},{8,0},{12,4},{1,9},{5,13},{9,1},{13,5},{2,10},{6,14},... | collective-permute-start | bytes 786440 | tf_op jit(solution)/shard_map/ppermute | solution.py:119
  28.5 12.6 %collective-permute-done.12 = bf16[64,2048]{1,0:T(8,128)(2,1)S(1)} collective-permute-done((bf16[64,2048]{1,0:T(8,128)(2,1)S(1)}, bf16[64,2048]{1,0:T(8,128)(2,1)S(1)}, u32[]{:S(2)}, u32[]{:S(2)}) %collective-permute-start.12) | collective-permute-done | bytes 262176 | tf_op jit(solution)/shard_map/ppermute | solution.py:119
  45.3 5.1 %collective-permute-done.14 = bf16[64,2048]{1,0:T(8,128)(2,1)S(1)} collective-permute-done((bf16[64,2048]{1,0:T(8,128)(2,1)S(1)}, bf16[64,2048]{1,0:T(8,128)(2,1)S(1)}, u32[]{:S(2)}, u32[]{:S(2)}) %collective-permute-start.14) | collective-permute-done | bytes 262176 | tf_op jit(solution)/shard_map/ppermute | solution.py:119
  56.4 3.4 %weigh.1 = (f32[8,128]{1,0:T(8,128)}, f32[8,128]{1,0:T(8,128)}) custom-call(s32[256]{0:T(256)} %reshape.41.pattern, bf16[2,2,128,2048]{3,2,1,0:T(8,128)(2,1)} %bitcast.62, bf16[2,128,2048]{2,1,0:T(8,128)(2,1)} %bitcast.56), custom_call_target="tpu_custom_call" | custom-call | tf_op jit(solution)/shard_map/weigh/pallas_call | solution.py:352
  59.9 2.4 collective-permute-start.19
  62.3 2.4 collective-permute-done.19.refs_20_
  65.2 6.8 %collective-permute-done.15 = bf16[64,2048]{1,0:T(8,128)(2,1)S(1)} collective-permute-done((bf16[64,2048]{1,0:T(8,128)(2,1)}, bf16[64,2048]{1,0:T(8,128)(2,1)S(1)}, u32[]{:S(2)}, u32[]{:S(2)}) %collective-permute-start.15) | collective-permute-done | bytes 262176 | tf_op jit(solution)/shard_map/ppermute | solution.py:119
  73.7 2.4 collective-permute-start.20
  77.8 4.8 %all-reduce.cols = s32[192]{0:T(256)} all-reduce(s32[192]{0:T(256)S(1)} %add_dynamic-update-slice_fusion), channel_id=2, replica_groups=mesh['groups'=2,'blk'=4,'ops'=2,'sub'=2] {'ops'}, use_global_device_ids=true, to_apply=%add | all-reduce | flops 192 | bytes 1536
  83.7 17.4 %operate_first.1 = (bf16[2,128,2048]{2,1,0:T(8,128)(2,1)}, bf16[2,128,2048]{2,1,0:T(8,128)(2,1)}, f32[8,128]{1,0:T(8,128)}) custom-call(s32[192]{0:T(256)} %all-reduce.cols, s32[256]{0:T(256)} %reshape.41.pattern, bf16[1,16,3,128,128]{4,3,2,1,0:T(8,128)(2,1)} %right_own.3, bf16[10,3,128,128]{3,2,1,0:T(8,128)(2,1)} %copy-done.2, ...), custom_call_target="tpu_custom_call" | custom-call | flops 3221225472 | bytes 16777216 | tf_op jit(solution)/shard_map/operate_first/pallas_call | solution.py:296
  105.6 1.9 collective-permute-start.27
  107.5 2.0 collective-permute-done.26.refs_6_
  110.3 5.9 %update.1 = (f32[2,128,2048]{2,1,0:T(8,128)}, f32[8,128]{1,0:T(8,128)}) custom-call(bf16[2,128,2048]{2,1,0:T(8,128)(2,1)} %get-tuple-element.37.psi.refs_18_, bf16[2,128,2048]{2,1,0:T(8,128)(2,1)} %get-tuple-element.38.off.refs_19_, bf16[2,128,2048]{2,1,0:T(8,128)(2,1)} %bitcast.57, bf16[128,2048]{1,0:T(8,128)(2,1)} %copy-done.4, ...), custom_call_target="tpu_custom_call" | custom-call | tf_op jit(solution)/shard_map/update/pallas_call | solution.py:561
  120.0 2.1 collective-permute-start.33
  122.6 2.1 collective-permute-done.33.refs_6_
  126.8 3.5 %correct.1 = (bf16[128,2048]{1,0:T(8,128)(2,1)}, bf16[128,2048]{1,0:T(8,128)(2,1)}) custom-call(bf16[2,128,2048]{2,1,0:T(8,128)(2,1)} %get-tuple-element.37.psi.refs_18_, f32[2,128,2048]{2,1,0:T(8,128)} %get-tuple-element.41.t, f32[8,128]{1,0:T(8,128)} %get-tuple-element.42.refs_0_, f32[8,128]{1,0:T(8,128)} %copy-done.39, f32[8,128]{1,0:T(8,128)} %copy-done.41, ...), custom_call_target="tpu_custom_call" | custom-call | tf_op jit(solution)/shard_map/correct/pallas_call | solution.py:578
  132.2 12.3 %collective-permute-done.35 = bf16[128,2048]{1,0:T(8,128)(2,1)S(1)} collective-permute-done((bf16[128,2048]{1,0:T(8,128)(2,1)}, bf16[128,2048]{1,0:T(8,128)(2,1)S(1)}, u32[]{:S(2)}, u32[]{:S(2)}) %collective-permute-start.35) | collective-permute-done | bytes 524320 | tf_op jit(solution)/shard_map/ppermute | solution.py:119
  149.1 10.8 %collective-permute-done.47 = bf16[128,2048]{1,0:T(8,128)(2,1)S(1)} collective-permute-done((bf16[128,2048]{1,0:T(8,128)(2,1)S(1)}, bf16[128,2048]{1,0:T(8,128)(2,1)S(1)}, u32[]{:S(2)}, u32[]{:S(2)}) %collective-permute-start.47) | collective-permute-done | bytes 524320 | tf_op jit(solution)/shard_map/ppermute | solution.py:119
  161.1 7.9 %collective-permute-done.38 = bf16[128,2048]{1,0:T(8,128)(2,1)S(1)} collective-permute-done((bf16[128,2048]{1,0:T(8,128)(2,1)}, bf16[128,2048]{1,0:T(8,128)(2,1)S(1)}, u32[]{:S(2)}, u32[]{:S(2)}) %collective-permute-start.38) | collective-permute-done | bytes 524320 | tf_op jit(solution)/shard_map/ppermute | solution.py:119
  173.4 18.0 %operate_second.1 = (bf16[128,2048]{1,0:T(8,128)(2,1)}, bf16[64,2048]{1,0:T(8,128)(2,1)}, bf16[64,2048]{1,0:T(8,128)(2,1)}, f32[8,128]{1,0:T(8,128)}) custom-call(s32[192]{0:T(256)} %all-reduce.cols, s32[256]{0:T(256)} %reshape.41.pattern, bf16[1,16,3,128,128]{4,3,2,1,0:T(8,128)(2,1)} %right_own.3, bf16[10,3,128,128]{3,2,1,0:T(8,128)(2,1)} %copy-done.2, ...), custom_call_target="tpu_custom_call" | custom-call | flops 3221225472 | bytes 16777216 | tf_op jit(solution)/shard_map/operate_second/pallas_call | solution.py:296
  194.2 8.4 %collective-permute-done.39.refs_2_ = bf16[128,2048]{1,0:T(8,128)(2,1)S(1)} collective-permute-done((bf16[128,2048]{1,0:T(8,128)(2,1)}, bf16[128,2048]{1,0:T(8,128)(2,1)S(1)}, u32[]{:S(2)}, u32[]{:S(2)}) %collective-permute-start.39) | collective-permute-done | bytes 524320 | tf_op jit(solution)/shard_map/ppermute | solution.py:119
  204.0 3.9 %collective-permute-done.52.refs_2_ = bf16[64,2048]{1,0:T(8,128)(2,1)S(1)} collective-permute-done((bf16[64,2048]{1,0:T(8,128)(2,1)}, bf16[64,2048]{1,0:T(8,128)(2,1)S(1)}, u32[]{:S(2)}, u32[]{:S(2)}) %collective-permute-start.52) | collective-permute-done | bytes 262176 | tf_op jit(solution)/shard_map/ppermute | solution.py:119
  208.1 33.4 %psum.7 = f32[2,5]{1,0:T(2,128)S(1)} all-reduce(f32[2,5]{1,0:T(2,128)S(1)} %broadcast_select_fusion), channel_id=1, replica_groups=mesh['groups'=2,'blk'=4,'ops'=2,'sub'=2] {'blk','ops','sub'}, use_global_device_ids=true, to_apply=%region_2.3 | all-reduce | flops 10 | bytes 80 | tf_op jit(solution)/shard_map/psum | solution.py:634
  241.6 2.0 collective-permute-start.55
  245.2 2.9 %assemble.2 = bf16[2,2,128,2048]{3,2,1,0:T(8,128)(2,1)} custom-call(bf16[128,2048]{1,0:T(8,128)(2,1)} %get-tuple-element.45.refs_0_, bf16[128,2048]{1,0:T(8,128)(2,1)} %copy-done.5, bf16[128,2048]{1,0:T(8,128)(2,1)} %copy-done.28, bf16[128,2048]{1,0:T(8,128)(2,1)} %copy-done.30), custom_call_target="tpu_custom_call" | custom-call | tf_op jit(solution)/shard_map/assemble/pallas_call | solution.py:461
  248.8 2.8 %collective-permute-done.55.refs_5_ = bf16[64,2048]{1,0:T(8,128)(2,1)S(1)} collective-permute-done((bf16[64,2048]{1,0:T(8,128)(2,1)S(1)}, bf16[64,2048]{1,0:T(8,128)(2,1)S(1)}, u32[]{:S(2)}, u32[]{:S(2)}) %collective-permute-start.55) | collective-permute-done | bytes 262176 | tf_op jit(solution)/shard_map/ppermute | solution.py:119
  252.4 2.9 %assemble.3 = bf16[2,2,128,2048]{3,2,1,0:T(8,128)(2,1)} custom-call(bf16[128,2048]{1,0:T(8,128)(2,1)} %get-tuple-element.50.refs_0_, bf16[128,2048]{1,0:T(8,128)(2,1)} %copy-done.29, bf16[64,2048]{1,0:T(8,128)(2,1)} %copy-done.32, bf16[64,2048]{1,0:T(8,128)(2,1)} %copy-done.33, bf16[64,2048]{1,0:T(8,128)(2,1)} %copy-done.34, bf16[64,2048]{1,0:T(8,128)(2,1)} %copy-done.35), custom_call_target="tpu_custom_call" | custom-call | tf_op jit(solution)/shard_map/assemble/pallas_call | solution.py:461
  (223 shorter events, 49.5 us)
Async XLA Ops:
  3.4 21.0 %collective-permute-start.2 = (bf16[128,2048]{1,0:T(8,128)(2,1)}, bf16[128,2048]{1,0:T(8,128)(2,1)S(1)}, u32[]{:S(2)}, u32[]{:S(2)}) collective-permute-start(bf16[128,2048]{1,0:T(8,128)(2,1)} %get-tuple-element.60), channel_id=1, source_target_pairs={{0,1},{1,0},{2,3},{3,2},{4,5},{5,4},{6,7},{7,6},{8,9},{9,8},{10,11... | collective-permute-start | bytes 1572872 | tf_op jit(solution)/shard_map/ppermute | solution.py:119
  3.9 20.5 %collective-permute-start.3 = (bf16[128,2048]{1,0:T(8,128)(2,1)}, bf16[128,2048]{1,0:T(8,128)(2,1)}, u32[]{:S(2)}, u32[]{:S(2)}) collective-permute-start(bf16[128,2048]{1,0:T(8,128)(2,1)} %get-tuple-element.31), channel_id=1, source_target_pairs={{0,1},{1,0},{2,3},{3,2},{4,5},{5,4},{6,7},{7,6},{8,9},{9,8},{10,11... | collective-permute-start | bytes 1572872 | tf_op jit(solution)/shard_map/ppermute | solution.py:119
  5.1 40.2 %collective-permute-start = (bf16[10,3,128,128]{3,2,1,0:T(8,128)(2,1)S(1)}, bf16[10,3,128,128]{3,2,1,0:T(8,128)(2,1)S(1)}, u32[]{:S(2)}, u32[]{:S(2)}) collective-permute-start(bf16[10,3,128,128]{3,2,1,0:T(8,128)(2,1)S(1)} %pad_maximum_fusion.1), channel_id=1, source_target_pairs={{0,2},{2,0},{1,3},{3,1},{4,6},{6,4},{5,7},{7,5},{8,10},{10,8},{9,1... | collective-permute-start | bytes 2949128 | tf_op jit(solution)/shard_map/ppermute | solution.py:119
  9.2 14.6 %collective-permute-start.5 = (bf16[64,2048]{1,0:T(8,128)(2,1)S(1)}, bf16[64,2048]{1,0:T(8,128)(2,1)S(1)}, u32[]{:S(2)}, u32[]{:S(2)}) collective-permute-start(bf16[64,2048]{1,0:T(8,128)(2,1)S(1)} %get-tuple-element.57), channel_id=1, source_target_pairs={{0,8},{4,12},{8,0},{12,4},{1,9},{5,13},{9,1},{13,5},{2,10},{6,14},... | collective-permute-start | bytes 786440 | tf_op jit(solution)/shard_map/ppermute | solution.py:119
  11.8 29.8 %collective-permute-start.4 = (bf16[128,2048]{1,0:T(8,128)(2,1)}, bf16[128,2048]{1,0:T(8,128)(2,1)}, u32[]{:S(2)}, u32[]{:S(2)}) collective-permute-start(bf16[128,2048]{1,0:T(8,128)(2,1)} %get-tuple-element.60), channel_id=1, source_target_pairs={{0,4},{4,0},{8,12},{12,8},{1,5},{5,1},{9,13},{13,9},{2,6},{6,2},{1... | collective-permute-start | bytes 1572872 | tf_op jit(solution)/shard_map/ppermute | solution.py:119
  23.8 17.3 %collective-permute-start.12 = (bf16[64,2048]{1,0:T(8,128)(2,1)S(1)}, bf16[64,2048]{1,0:T(8,128)(2,1)S(1)}, u32[]{:S(2)}, u32[]{:S(2)}) collective-permute-start(bf16[64,2048]{1,0:T(8,128)(2,1)S(1)} %collective-permute-done.5), channel_id=1, source_target_pairs={{0,4},{4,0},{8,12},{12,8},{1,5},{5,1},{9,13},{13,9},{2,6},{6,2},{1... | collective-permute-start | bytes 786440 | tf_op jit(solution)/shard_map/ppermute | solution.py:119
  24.4 16.6 %collective-permute-start.6 = (bf16[64,2048]{1,0:T(8,128)(2,1)S(1)}, bf16[64,2048]{1,0:T(8,128)(2,1)S(1)}, u32[]{:S(2)}, u32[]{:S(2)}) collective-permute-start(bf16[64,2048]{1,0:T(8,128)(2,1)S(1)} %get-tuple-element.30), channel_id=1, source_target_pairs={{0,8},{4,12},{8,0},{12,4},{1,9},{5,13},{9,1},{13,5},{2,10},{6,14},... | collective-permute-start | bytes 786440 | tf_op jit(solution)/shard_map/ppermute | solution.py:119
  27.9 15.2 %collective-permute-start.10 = (bf16[64,2048]{1,0:T(8,128)(2,1)S(1)}, bf16[64,2048]{1,0:T(8,128)(2,1)S(1)}, u32[]{:S(2)}, u32[]{:S(2)}) collective-permute-start(bf16[64,2048]{1,0:T(8,128)(2,1)S(1)} %collective-permute-done.5), channel_id=1, source_target_pairs={{0,2},{2,0},{1,3},{3,1},{4,6},{6,4},{5,7},{7,5},{8,10},{10,8},{9,1... | collective-permute-start | bytes 786440 | tf_op jit(solution)/shard_map/ppermute | solution.py:119
  41.6 18.2 %collective-permute-start.8 = (bf16[128,2048]{1,0:T(8,128)(2,1)}, bf16[128,2048]{1,0:T(8,128)(2,1)}, u32[]{:S(2)}, u32[]{:S(2)}) collective-permute-start(bf16[128,2048]{1,0:T(8,128)(2,1)} %collective-permute-done.4), channel_id=1, source_target_pairs={{0,1},{1,0},{2,3},{3,2},{4,5},{5,4},{6,7},{7,6},{8,9},{9,8},{10,11... | collective-permute-start | bytes 1572872 | tf_op jit(solution)/shard_map/ppermute | solution.py:119
  41.6 11.9 %collective-permute-start.11 = (bf16[64,2048]{1,0:T(8,128)(2,1)S(1)}, bf16[64,2048]{1,0:T(8,128)(2,1)S(1)}, u32[]{:S(2)}, u32[]{:S(2)}) collective-permute-start(bf16[64,2048]{1,0:T(8,128)(2,1)S(1)} %collective-permute-done.6), channel_id=1, source_target_pairs={{0,2},{2,0},{1,3},{3,1},{4,6},{6,4},{5,7},{7,5},{8,10},{10,8},{9,1... | collective-permute-start | bytes 786440 | tf_op jit(solution)/shard_map/ppermute | solution.py:119
  43.2 10.3 %collective-permute-start.13 = (bf16[64,2048]{1,0:T(8,128)(2,1)S(1)}, bf16[64,2048]{1,0:T(8,128)(2,1)S(1)}, u32[]{:S(2)}, u32[]{:S(2)}) collective-permute-start(bf16[64,2048]{1,0:T(8,128)(2,1)S(1)} %collective-permute-done.6), channel_id=1, source_target_pairs={{0,4},{4,0},{8,12},{12,8},{1,5},{5,1},{9,13},{13,9},{2,6},{6,2},{1... | collective-permute-start | bytes 786440 | tf_op jit(solution)/shard_map/ppermute | solution.py:119
  45.3 37.3 %collective-permute-start.17 = (bf16[4,64,2048]{2,1,0:T(8,128)(2,1)}, bf16[4,64,2048]{2,1,0:T(8,128)(2,1)}, u32[]{:S(2)}, u32[]{:S(2)}) collective-permute-start(bf16[4,64,2048]{2,1,0:T(8,128)(2,1)} %pad_maximum_fusion), channel_id=1, source_target_pairs={{0,1},{1,0},{2,3},{3,2},{4,5},{5,4},{6,7},{7,6},{8,9},{9,8},{10,11... | collective-permute-start | bytes 3145736 | tf_op jit(solution)/shard_map/ppermute | solution.py:119
  50.4 14.8 %collective-permute-start.7 = (bf16[128,2048]{1,0:T(8,128)(2,1)}, bf16[128,2048]{1,0:T(8,128)(2,1)}, u32[]{:S(2)}, u32[]{:S(2)}) collective-permute-start(bf16[128,2048]{1,0:T(8,128)(2,1)} %get-tuple-element.31), channel_id=1, source_target_pairs={{0,4},{4,0},{8,12},{12,8},{1,5},{5,1},{9,13},{13,9},{2,6},{6,2},{1... | collective-permute-start | bytes 1572872 | tf_op jit(solution)/shard_map/ppermute | solution.py:119
  53.5 29.1 %collective-permute-start.1 = (bf16[8,3,128,128]{3,2,1,0:T(8,128)(2,1)}, bf16[8,3,128,128]{3,2,1,0:T(8,128)(2,1)S(1)}, u32[]{:S(2)}, u32[]{:S(2)}) collective-permute-start(bf16[8,3,128,128]{3,2,1,0:T(8,128)(2,1)} %slice.20), channel_id=1, source_target_pairs={{0,1},{1,0},{2,3},{3,2},{4,5},{5,4},{6,7},{7,6},{8,9},{9,8},{10,11... | collective-permute-start | bytes 2359304 | tf_op jit(solution)/shard_map/ppermute | solution.py:119
  55.2 27.4 %collective-permute-start.18 = (bf16[3,64,2048]{2,1,0:T(8,128)(2,1)}, bf16[3,64,2048]{2,1,0:T(8,128)(2,1)}, u32[]{:S(2)}, u32[]{:S(2)}) collective-permute-start(bf16[3,64,2048]{2,1,0:T(8,128)(2,1)} %pad_maximum_fusion.2), channel_id=1, source_target_pairs={{0,1},{1,0},{2,3},{3,2},{4,5},{5,4},{6,7},{7,6},{8,9},{9,8},{10,11... | collective-permute-start | bytes 2359304 | tf_op jit(solution)/shard_map/ppermute | solution.py:119
  65.2 17.5 %collective-permute-start.9 = (bf16[128,2048]{1,0:T(8,128)(2,1)}, bf16[128,2048]{1,0:T(8,128)(2,1)S(1)}, u32[]{:S(2)}, u32[]{:S(2)}) collective-permute-start(bf16[128,2048]{1,0:T(8,128)(2,1)} %collective-permute-done.7), channel_id=1, source_target_pairs={{0,1},{1,0},{2,3},{3,2},{4,5},{5,4},{6,7},{7,6},{8,9},{9,8},{10,11... | collective-permute-start | bytes 1572872 | tf_op jit(solution)/shard_map/ppermute | solution.py:119
  73.7 30.2 %collective-permute-start.20 = (bf16[128,2048]{1,0:T(8,128)(2,1)}, bf16[128,2048]{1,0:T(8,128)(2,1)S(1)}, u32[]{:S(2)}, u32[]{:S(2)}) collective-permute-start(bf16[128,2048]{1,0:T(8,128)(2,1)} %dynamic-slice_bitcast_fusion.1), channel_id=1, source_target_pairs={{0,8},{4,12},{8,0},{12,4},{1,9},{5,13},{9,1},{13,5},{2,10},{6,14},... | collective-permute-start | bytes 1572872 | tf_op jit(solution)/shard_map/ppermute | solution.py:119
  130.3 14.2 %collective-permute-start.35 = (bf16[128,2048]{1,0:T(8,128)(2,1)}, bf16[128,2048]{1,0:T(8,128)(2,1)S(1)}, u32[]{:S(2)}, u32[]{:S(2)}) collective-permute-start(bf16[128,2048]{1,0:T(8,128)(2,1)} %get-tuple-element.45.refs_0_), channel_id=1, source_target_pairs={{0,4},{4,0},{8,12},{12,8},{1,5},{5,1},{9,13},{13,9},{2,6},{6,2},{1... | collective-permute-start | bytes 1572872 | tf_op jit(solution)/shard_map/ppermute | solution.py:119
  131.1 13.9 %collective-permute-start.36 = (bf16[128,2048]{1,0:T(8,128)(2,1)}, bf16[128,2048]{1,0:T(8,128)(2,1)S(1)}, u32[]{:S(2)}, u32[]{:S(2)}) collective-permute-start(bf16[128,2048]{1,0:T(8,128)(2,1)} %get-tuple-element.47), channel_id=1, source_target_pairs={{0,2},{2,0},{1,3},{3,1},{4,6},{6,4},{5,7},{7,5},{8,10},{10,8},{9,1... | collective-permute-start | bytes 1572872 | tf_op jit(solution)/shard_map/ppermute | solution.py:119
  131.7 15.9 %collective-permute-start.40 = (bf16[128,2048]{1,0:T(8,128)(2,1)}, bf16[128,2048]{1,0:T(8,128)(2,1)S(1)}, u32[]{:S(2)}, u32[]{:S(2)}) collective-permute-start(bf16[128,2048]{1,0:T(8,128)(2,1)} %get-tuple-element.45.refs_0_), channel_id=1, source_target_pairs={{0,1},{1,0},{2,3},{3,2},{4,5},{5,4},{6,7},{7,6},{8,9},{9,8},{10,11... | collective-permute-start | bytes 1572872 | tf_op jit(solution)/shard_map/ppermute | solution.py:119
  131.7 17.4 %collective-permute-start.41 = (bf16[128,2048]{1,0:T(8,128)(2,1)}, bf16[128,2048]{1,0:T(8,128)(2,1)S(1)}, u32[]{:S(2)}, u32[]{:S(2)}) collective-permute-start(bf16[128,2048]{1,0:T(8,128)(2,1)} %get-tuple-element.47), channel_id=1, source_target_pairs={{0,1},{1,0},{2,3},{3,2},{4,5},{5,4},{6,7},{7,6},{8,9},{9,8},{10,11... | collective-permute-start | bytes 1572872 | tf_op jit(solution)/shard_map/ppermute | solution.py:119
  145.0 14.9 %collective-permute-start.47 = (bf16[128,2048]{1,0:T(8,128)(2,1)S(1)}, bf16[128,2048]{1,0:T(8,128)(2,1)S(1)}, u32[]{:S(2)}, u32[]{:S(2)}) collective-permute-start(bf16[128,2048]{1,0:T(8,128)(2,1)S(1)} %collective-permute-done.36), channel_id=1, source_target_pairs={{0,4},{4,0},{8,12},{12,8},{1,5},{5,1},{9,13},{13,9},{2,6},{6,2},{1... | collective-permute-start | bytes 1572872 | tf_op jit(solution)/shard_map/ppermute | solution.py:119
  146.2 14.9 %collective-permute-start.46 = (bf16[128,2048]{1,0:T(8,128)(2,1)S(1)}, bf16[128,2048]{1,0:T(8,128)(2,1)S(1)}, u32[]{:S(2)}, u32[]{:S(2)}) collective-permute-start(bf16[128,2048]{1,0:T(8,128)(2,1)S(1)} %collective-permute-done.35), channel_id=1, source_target_pairs={{0,2},{2,0},{1,3},{3,1},{4,6},{6,4},{5,7},{7,5},{8,10},{10,8},{9,1... | collective-permute-start | bytes 1572872 | tf_op jit(solution)/shard_map/ppermute | solution.py:119
  146.8 22.3 %collective-permute-start.38 = (bf16[128,2048]{1,0:T(8,128)(2,1)}, bf16[128,2048]{1,0:T(8,128)(2,1)S(1)}, u32[]{:S(2)}, u32[]{:S(2)}) collective-permute-start(bf16[128,2048]{1,0:T(8,128)(2,1)} %get-tuple-element.47), channel_id=1, source_target_pairs={{0,4},{4,0},{8,12},{12,8},{1,5},{5,1},{9,13},{13,9},{2,6},{6,2},{1... | collective-permute-start | bytes 1572872 | tf_op jit(solution)/shard_map/ppermute | solution.py:119
  147.6 22.4 %collective-permute-start.37 = (bf16[128,2048]{1,0:T(8,128)(2,1)}, bf16[128,2048]{1,0:T(8,128)(2,1)S(1)}, u32[]{:S(2)}, u32[]{:S(2)}) collective-permute-start(bf16[128,2048]{1,0:T(8,128)(2,1)} %get-tuple-element.45.refs_0_), channel_id=1, source_target_pairs={{0,2},{2,0},{1,3},{3,1},{4,6},{6,4},{5,7},{7,5},{8,10},{10,8},{9,1... | collective-permute-start | bytes 1572872 | tf_op jit(solution)/shard_map/ppermute | solution.py:119
  149.1 20.9 %collective-permute-start.42 = (bf16[128,2048]{1,0:T(8,128)(2,1)S(1)}, bf16[128,2048]{1,0:T(8,128)(2,1)S(1)}, u32[]{:S(2)}, u32[]{:S(2)}) collective-permute-start(bf16[128,2048]{1,0:T(8,128)(2,1)S(1)} %collective-permute-done.35), channel_id=1, source_target_pairs={{0,1},{1,0},{2,3},{3,2},{4,5},{5,4},{6,7},{7,6},{8,9},{9,8},{10,11... | collective-permute-start | bytes 1572872 | tf_op jit(solution)/shard_map/ppermute | solution.py:119
  159.9 10.6 %collective-permute-start.45 = (bf16[128,2048]{1,0:T(8,128)(2,1)S(1)}, bf16[128,2048]{1,0:T(8,128)(2,1)S(1)}, u32[]{:S(2)}, u32[]{:S(2)}) collective-permute-start(bf16[128,2048]{1,0:T(8,128)(2,1)S(1)} %collective-permute-done.36), channel_id=1, source_target_pairs={{0,1},{1,0},{2,3},{3,2},{4,5},{5,4},{6,7},{7,6},{8,9},{9,8},{10,11... | collective-permute-start | bytes 1572872 | tf_op jit(solution)/shard_map/ppermute | solution.py:119
  170.5 32.2 %collective-permute-start.39 = (bf16[128,2048]{1,0:T(8,128)(2,1)}, bf16[128,2048]{1,0:T(8,128)(2,1)S(1)}, u32[]{:S(2)}, u32[]{:S(2)}) collective-permute-start(bf16[128,2048]{1,0:T(8,128)(2,1)} %get-tuple-element.47), channel_id=1, source_target_pairs={{0,8},{4,12},{8,0},{12,4},{1,9},{5,13},{9,1},{13,5},{2,10},{6,14},... | collective-permute-start | bytes 1572872 | tf_op jit(solution)/shard_map/ppermute | solution.py:119
  191.5 16.5 %collective-permute-start.52 = (bf16[64,2048]{1,0:T(8,128)(2,1)}, bf16[64,2048]{1,0:T(8,128)(2,1)S(1)}, u32[]{:S(2)}, u32[]{:S(2)}) collective-permute-start(bf16[64,2048]{1,0:T(8,128)(2,1)} %get-tuple-element.52), channel_id=1, source_target_pairs={{0,8},{4,12},{8,0},{12,4},{1,9},{5,13},{9,1},{13,5},{2,10},{6,14},... | collective-permute-start | bytes 786440 | tf_op jit(solution)/shard_map/ppermute | solution.py:119
  193.6 54.4 %collective-permute-start.51 = (bf16[128,2048]{1,0:T(8,128)(2,1)}, bf16[128,2048]{1,0:T(8,128)(2,1)S(1)}, u32[]{:S(2)}, u32[]{:S(2)}) collective-permute-start(bf16[128,2048]{1,0:T(8,128)(2,1)} %get-tuple-element.50.refs_0_), channel_id=1, source_target_pairs={{0,2},{2,0},{1,3},{3,1},{4,6},{6,4},{5,7},{7,5},{8,10},{10,8},{9,1... | collective-permute-start | bytes 1572872 | tf_op jit(solution)/shard_map/ppermute | solution.py:119
  202.7 41.7 %collective-permute-start.50 = (bf16[128,2048]{1,0:T(8,128)(2,1)S(1)}, bf16[128,2048]{1,0:T(8,128)(2,1)S(1)}, u32[]{:S(2)}, u32[]{:S(2)}) collective-permute-start(bf16[128,2048]{1,0:T(8,128)(2,1)S(1)} %collective-permute-done.39.refs_2_), channel_id=1, source_target_pairs={{0,2},{2,0},{1,3},{3,1},{4,6},{6,4},{5,7},{7,5},{8,10},{10,8},{9,1... | collective-permute-start | bytes 1572872 | tf_op jit(solution)/shard_map/ppermute | solution.py:119
  208.0 33.6 %collective-permute-start.53 = (bf16[64,2048]{1,0:T(8,128)(2,1)}, bf16[64,2048]{1,0:T(8,128)(2,1)S(1)}, u32[]{:S(2)}, u32[]{:S(2)}) collective-permute-start(bf16[64,2048]{1,0:T(8,128)(2,1)} %get-tuple-element.54), channel_id=1, source_target_pairs={{0,8},{4,12},{8,0},{12,4},{1,9},{5,13},{9,1},{13,5},{2,10},{6,14},... | collective-permute-start | bytes 786440 | tf_op jit(solution)/shard_map/ppermute | solution.py:119
  (79 other events, 654.0 us)

commit v3 on v2

--- a/solution.py
+++ b/solution.py
@@ -120,11 +120,12 @@
 
 
 def share(stats):
-    axes = ("blk", "ops", "sub")
-    count = lax.axis_size("blk") * lax.axis_size("ops") * lax.axis_size("sub")
-    found = [stats]
-    for distance in range(1, 8):
-        found.append(lax.ppermute(stats, axes, [(i, i ^ distance) for i in range(count)]))
+    axes = ("blk", "ops")
+    count = lax.axis_size("blk") * lax.axis_size("ops")
+    pair = jnp.stack([stats, across(stats, "sub", 1)])
+    found = [pair]
+    for distance in (1, 2, 3):
+        found.append(lax.ppermute(pair, axes, [(i, i ^ distance) for i in range(count)]))
     return found
 
 
@@ -150,8 +151,8 @@
         weight_own, weight_far, psi_out, off_out, stats_out = refs[:5]
         refs = refs[5:]
     else:
-        hd_own, hd_far, psi_in, off_in, near_out, far_out, late_out, stats_out = refs[:8]
-        refs = refs[8:]
+        hd_own, hd_far, psi_in, off_in, stats_in, near_out, far_out, late_out, stats_out = refs[:9]
+        refs = refs[9:]
     field, images, right, left, diag, sems = refs
     z, x, c = place()
     sectors, block, width = field.shape
@@ -168,17 +169,17 @@
 
     part = sectors // 2
     near, far = pl.ds(c * part, part), pl.ds((1 - c) * part, part)
-    begin(right_own.at[0], right.at[x])
+    begin(right_own.at[0], right.at[0])
     for piece, offsets in zip(pieces, plan):
         tall = piece.shape[1]
         for at, (dz, dx, dc, chunk) in enumerate(offsets):
             begin(piece.at[at], field.at[row_of(dz, dx, dc), pl.ds(chunk * tall, tall)])
-    begin(right_near.at[pl.ds(0, part)], right.at[1 - x, near])
-    begin(right_far, right.at[1 - x, far])
+    begin(right_near.at[pl.ds(0, part)], right.at[1, near])
+    begin(right_far, right.at[1, far])
     early = len(copies)
     for at in range(2):
-        begin(left_own.at[0, rows[at]], left.at[x, at])
-    begin(right_near.at[pl.ds(part, 2)], left.at[1 - x])
+        begin(left_own.at[0, rows[at]], left.at[0, at])
+    begin(right_near.at[pl.ds(part, 2)], left.at[1])
     if not first:
         begin(hd_own.at[x], diag.at[0])
         begin(hd_far, diag.at[1])
@@ -197,6 +198,8 @@
         return jnp.where(pattern[a * sectors + q] != 0, value, jnp.zeros_like(value))
 
     sources = [[left_col(term, rows[at], j) for at in range(2) for j in range(links)] for term in range(2)]
+
+    deep = links * block
 
     def image(b, carry):
         for term in range(2):
@@ -215,15 +218,17 @@
                 (((1,), (1,)), ((), ())),
                 preferred_element_type=jnp.float32,
             )
-            images[term, :, pl.ds(pl.multiple_of(b * block, block), block)] = product.astype(jnp.bfloat16)
+            product = product.astype(jnp.bfloat16)
+            span = pl.ds(pl.multiple_of(b * block, block), block)
+            for at in range(2):
+                images[at, term * deep : (term + 1) * deep, span] = product[at * deep : (at + 1) * deep]
         return carry
 
-    lax.fori_loop(0, sectors, image, 0)
+    lax.fori_loop(0, sectors, image, 0, unroll=2)
     for copy in copies[early:]:
         copy.wait()
 
     step = 2
-    deep = links * block
     half = block // 2
     zero = jnp.zeros((8, LANES), jnp.float32)
 
@@ -239,15 +244,12 @@
             return jnp.concatenate(parts, axis=1)
 
         for at in range(2):
-            total = None
-            for term in range(2):
-                weights = jnp.concatenate([left[term, at, j] for j in range(links)], axis=1)
-                product = jnp.dot(
-                    weights,
-                    images[term, at * deep : (at + 1) * deep, span],
-                    preferred_element_type=jnp.float32,
-                )
-                total = product if total is None else total + product
+            weights = [left[term, at, j] for term in range(2) for j in range(links)]
+            total = jnp.dot(
+                jnp.concatenate(weights, axis=1),
+                images[at, :, span],
+                preferred_element_type=jnp.float32,
+            )
             offdiag = masked(rows[at], total.astype(jnp.bfloat16).astype(jnp.float32))
             own = field[rows[at], :, span].astype(jnp.float32)
             if first:
@@ -278,6 +280,8 @@
     stats_out[...] = jnp.zeros_like(stats_out)
     for at, value in enumerate(sums):
         stats_out[at : at + 1, :] = jnp.sum(value, axis=0, keepdims=True)
+    if not first:
+        stats_out[3:5, :] = stats_in[0:2, :]
 
 
 def operate(first, plan, pieces, cols, pattern, right, left, extra):
@@ -289,7 +293,7 @@
     some = jax.ShapeDtypeStruct((block // 2, width), jnp.bfloat16)
     stats = jax.ShapeDtypeStruct((8, LANES), jnp.float32)
     out_shape = (rows, rows, stats) if first else (one, some, some, stats)
-    extra_specs = [VMEM, VMEM] if first else [ANY, ANY, VMEM, VMEM]
+    extra_specs = [VMEM, VMEM] if first else [ANY, ANY, VMEM, VMEM, VMEM]
     copies = sum(len(offsets) for offsets in plan) + 8
     inner = 2 * 2 * sectors * 2 * links * links * block * block * block
     outer = 2 * 2 * 2 * links * block * block * width
@@ -368,7 +372,7 @@
 
 
 def update_kernel(psi, off, hd_own, hd_far, *refs):
-    stats, (t_out, stats_out, diag, sems) = refs[:8], refs[8:]
+    stats, (t_out, stats_out, diag, sems) = refs[:4], refs[4:]
     z, x, c = place()
     copies = [
         pltpu.make_async_copy(hd_own.at[x], diag.at[0], sems.at[0]),
@@ -376,10 +380,10 @@
     ]
     for copy in copies:
         copy.start()
-    whole = sum(ref[0:2, :] for ref in stats)
+    whole = sum(ref[at, 0:2, :] for ref in stats for at in range(2))
     norm_sq, energy_sum = total_of(whole[0:1, :]), total_of(whole[1:2, :])
     energy = energy_sum / (norm_sq + 1e-06)
-    mine = total_of(stats[0][0:1, :])
+    mine = total_of(stats[0][0, 0:1, :])
     for copy in copies:
         copy.wait()
     _, block, width = psi.shape
@@ -419,7 +423,8 @@
 
 
 def correct_kernel(psi, t, *refs):
-    stats, outs = refs[:8], refs[8:]
+    stats, outs = refs[:4], refs[4:]
+    stats = [ref.at[at] for ref in stats for at in range(2)]
     norm_sq = stats[0][4:5, 0:1]
     factor = sum(ref[0:1, 0:1] for ref in stats) / (norm_sq + 1e-06)
     length_sq = jnp.zeros((1, 1), jnp.float32)
@@ -489,11 +494,16 @@
     def given(at):
         return lax.dynamic_slice(halves, (1 - half, x, at * chunk, 0), (1, 1, chunk, width))[0, 0]
 
-    far_a = across(given(0), "blk", 2)
+    first = given(0)
+    far_a = across(first, "blk", 2)
+    halves = after(halves, first)
     own = [
         lax.dynamic_slice(halves, (half, at, 0, 0), (1, 1, block, width))[0, 0] for at in range(2)
     ]
     near_a = across(own[0], "blk", 1)
+    cols = jnp.concatenate([right_cols.reshape(-1), left_cols.reshape(-1)])
+    cols_other = across(cols, "ops", 1)
+    cols = jnp.concatenate([cols, cols_other])
     part = sectors // 2
     packed = jnp.concatenate(
         [
@@ -502,30 +512,30 @@
             lax.dynamic_slice_in_dim(left_blocks[0], mine ^ 9, 1, 0),
         ]
     )
-    operators = across(packed, "ops", 1)
-    cols = jnp.concatenate([right_cols.reshape(-1), left_cols.reshape(-1)])
-    cols = lax.all_gather(cols, "ops").reshape(-1)
+    operators = across(after(packed, cols_other), "ops", 1)
     own_core = [across(value, "sub", 1) for value in own]
     weight_own, weight_far = weigh(allowed, halves, diag)
 
-    far_b = across(after(given(1), far_a, *own_core), "blk", 2)
+    far_a, second = after((far_a, given(1)), weight_own, cols, *own_core)
+    far_b = across(after(second, far_a), "blk", 2)
     far_za = across(far_a, "blk", 1)
     far_xa = across(far_a, "ops", 1)
-    operators_core = across(operators[:part], "sub", 1)
-    near_a_core = across(near_a, "sub", 1)
-
-    far_zb = across(far_b, "blk", 1)
+    weight_far = across(weight_far, "blk", 2)
+
+    far_zb = across(after(far_b, far_za), "blk", 1)
+    near_b = across(after(own[1], far_b), "blk", 1)
+    far_zxa = across(after(far_za, far_b), "ops", 1)
     far_xb = across(far_b, "ops", 1)
-    far_zxa = across(after(far_za, far_b), "ops", 1)
-    near_b = across(after(own[1], far_b), "blk", 1)
+    operators_core = across(after(operators[:part], far_b), "sub", 1)
+    near_a_core = across(after(near_a, far_b), "sub", 1)
     core_a = across(jnp.stack([far_a, far_b, far_xa, far_za]), "sub", 1)
-    far_zxb = across(after(far_zb, far_xb), "ops", 1)
-    weight_far = across(after(weight_far, far_zb), "blk", 2)
+
+    far_zxb = across(after(far_zb, far_xb, far_zxa), "ops", 1)
     core_b = across(jnp.stack([far_xb, far_zxa, far_zb]), "sub", 1)
     near_b_core = across(near_b, "sub", 1)
-    far_zxb_core = across(far_zxb, "sub", 1)
     hd_far = lax.dynamic_index_in_dim(diag, x, 0, keepdims=False)
     hd_far = across(after(hd_far, far_zb), "blk", 2)
+    far_zxb_core = across(far_zxb, "sub", 1)
 
     right = (right_blocks, operators, operators_core)
     pieces = []
@@ -564,7 +574,7 @@
             jax.ShapeDtypeStruct((2, block, width), jnp.float32),
             jax.ShapeDtypeStruct((8, LANES), jnp.float32),
         ),
-        in_specs=[VMEM, VMEM, ANY, ANY] + [VMEM] * 8,
+        in_specs=[VMEM, VMEM, ANY, ANY] + [VMEM] * 4,
         out_specs=(VMEM, VMEM),
         scratch_shapes=[
             pltpu.VMEM((2, block, width), jnp.bfloat16),
@@ -578,7 +588,7 @@
     near, far = pl.pallas_call(
         correct_kernel,
         out_shape=(one, one),
-        in_specs=[VMEM, VMEM] + [VMEM] * 8,
+        in_specs=[VMEM, VMEM] + [VMEM] * 4,
         out_specs=(VMEM, VMEM),
         compiler_params=pltpu.CompilerParams(vmem_limit_bytes=VMEM_LIMIT),
         name="correct",
@@ -621,7 +631,7 @@
         pieces.append(piece[None])
         plan.append((offset,))
     two_near, two_far, two_late, stats_three = operate(
-        False, tuple(plan), pieces, cols, allowed, right, left_blocks, (diag, hd_far, psi, off_one)
+        False, tuple(plan), pieces, cols, allowed, right, left_blocks, (diag, hd_far, psi, off_one, stats_one)
     )
 
     far_in = across(two_far, "blk", 2)
@@ -629,11 +639,14 @@
     late_in = across(after(two_late, far_in), "blk", 2)
     far_in_x = across(far_in, "ops", 1)
     other_x = across(after(other, two_near), "ops", 1)
-    sums = jnp.concatenate([jnp.sum(stats_one[:2], axis=1), jnp.sum(stats_three[:3], axis=1)])
-    here = (jnp.arange(roots) == half)[:, None]
-    sums = lax.psum(jnp.where(here, sums[None, :], 0.0), ("blk", "ops", "sub"))
-    subspace = sums[:, 1:5] / (sums[:, 0:1] + 1e-06)
-    late_in_x = across(after(late_in, sums), "ops", 1)
+    late_in_x = across(late_in, "ops", 1)
+    sums = stats_three + across(stats_three, "sub", 1)
+    sums = sums + across(sums, "ops", 1)
+    sums = sums + across(sums, "blk", 1)
+    both = jnp.stack([sums, across(sums, "blk", 2)])
+    both = jnp.sum(jnp.where(half == 0, both, both[::-1])[:, :5], axis=2)
+    scale = both[:, 3:4] + 1e-06
+    subspace = jnp.concatenate([both[:, 4:5], both[:, 0:3]], axis=1) / scale
     places = ((0, 0, 0), (0, 1, 0), (1, 0, 0), (1, 1, 0))
     correction = assemble(block, (near, near_x, other, other_x), places)
     places = ((0, 0, 0), (0, 1, 0), (1, 0, 0), (1, 0, 1), (1, 1, 0), (1, 1, 1))

time: 256 us -> 247 us (0.965)
  blocking collectives: 38.2 us -> 0 us
  waiting for transfers between devices: 96.2 us -> 123 us
  starting transfers between devices: 46.6 us -> 54.4 us
  Pallas kernels: 54 us -> 50.4 us
    psum x1 -> x0, blocking collectives: 33.4 us -> none  [shards(): sums = lax.psum(jnp.where(here, sums[None, :], 0.0), ('blk', 'ops', 'sub'))]
    ppermute x42 -> x49, waiting for transfers between devices: 90.3 us -> 117 us  [across(): return lax.ppermute(value, axis, [(i, i ^ distance) for i in range(size)])]
    ppermute x42 -> x49, starting transfers between devices: 34 us -> 47.4 us  [across(): return lax.ppermute(value, axis, [(i, i ^ distance) for i in range(size)])]
    ppermute x14 -> x6, starting transfers between devices: 12.6 us -> 6.98 us  [share(): lax.ppermute(pair, axes, [(i, i ^ distance) for i in range(count)])]
    unnamed x1 -> x0, blocking collectives: 4.81 us -> none
    pallas_call x2, Pallas kernels: 35.5 us -> 32 us  [operate(): pl.pallas_call(functools.partial(operate_kernel, first, plan), out_shape=...]
    squeeze x1 -> x0, local copies, waits for them, and re-layouts: 2.77 us -> none  [shards(): lax.dynamic_slice(halves, (half, at, 0, 0), (1, 1, block, width))[0, 0]]
    another operation x0 -> x1, local copies, waits for them, and re-layouts: none -> 2.64 us  [shards(): pieces.append(piece if piece.ndim == 3 else piece[None])]
  transfers between devices with their start and end apart: 56 -> 55, of which waited for: 23 -> 31; matrix products, arithmetic and copies ran while one was open for 4% -> 3% of each run, Pallas kernels for 16% -> 15%
where the time goes in v3:
time: 247 us; the launch traced here: 246 us
  waiting for transfers between devices  123 us (50%)
  starting transfers between devices  54.4 us (22%)
  Pallas kernels  50.4 us (20%)
  local copies, waits for them, and re-layouts  12.4 us (5%)
  other arithmetic  5.13 us (2%)
    ppermute x49, waiting for transfers between devices, across(): return lax.ppermute(value, axis, [(i, i ^ distance) for i in range(size)])  117 us
    ppermute x49, starting transfers between devices, across(): return lax.ppermute(value, axis, [(i, i ^ distance) for i in range(size)])  47.4 us
    pallas_call x2, Pallas kernels, operate(): pl.pallas_call(functools.partial(operate_kernel, first, plan), out_shape=...  32 us
    ppermute x6, starting transfers between devices, share(): lax.ppermute(pair, axes, [(i, i ^ distance) for i in range(count)])  6.98 us
    pallas_call x1, Pallas kernels, shards(): pl.pallas_call(update_kernel, out_shape=(jax.ShapeDtypeStruct((2, block,...  5.92 us
    unnamed x114, local copies, waits for them, and re-layouts  5.74 us
    pallas_call x2, Pallas kernels, assemble(): pl.pallas_call(functools.partial(assemble_kernel, tall), out_shape=jax.Sh...  5.72 us
    ppermute x6, waiting for transfers between devices, share(): lax.ppermute(pair, axes, [(i, i ^ distance) for i in range(count)])  5.64 us
  transfers between devices with their start and end apart: 55, of which 31 were waited for; matrix products, arithmetic and copies ran while one was open for 3% of the time, Pallas kernels for 15%

profile of v3, /device:TPU:0, one launch (start us, length us, event | category | flops | bytes accessed | tf_op | source)
XLA Modules:
  0.0 246.3 jit_solution(5705168140058056677)
XLA Ops:
  1.8 2.6 %dynamic-slice_bitcast_fusion.2 = (bf16[1,128,2048]{2,1,0:T(8,128)(2,1)}, bf16[1,128,2048]{2,1,0:T(8,128)(2,1)}, bf16[128,2048]{1,0:T(8,128)(2,1)}, bf16[128,2048]{1,0:T(8,128)(2,1)}) fusion(bf16[2,2,128,2048]{3,2,1,0:T(8,128)(2,1)} %bitcast.67, s32[]{:T(128)S(6)} %select_n.42), kind=kLoop, calls=%fused_computation.5 | loop fusion | bytes 3145732 | tf_op jit(solution)/shard_map/broadcast_in_dim;squeeze | solution.py:564
  5.9 2.9 %collective-permute-start = (s32[96]{0:T(128)}, s32[96]{0:T(128)}, u32[]{:S(2)}, u32[]{:S(2)}) collective-permute-start(s32[96]{0:T(128)} %pad_add_fusion.1), channel_id=1, source_target_pairs={{0,2},{2,0},{1,3},{3,1},{4,6},{6,4},{5,7},{7,5},{8,10},{10,8},{9,1... | collective-permute-start | bytes 1160 | tf_op jit(solution)/shard_map/ppermute | solution.py:119
  10.6 2.0 collective-permute-start.1
  12.6 2.6 %collective-permute-start.2 = (bf16[64,2048]{1,0:T(8,128)(2,1)S(1)}, bf16[64,2048]{1,0:T(8,128)(2,1)S(1)}, u32[]{:S(2)}, u32[]{:S(2)}) collective-permute-start(bf16[64,2048]{1,0:T(8,128)(2,1)S(1)} %dynamic-slice_bitcast_fusion.7), channel_id=1, source_target_pairs={{0,8},{4,12},{8,0},{12,4},{1,9},{5,13},{9,1},{13,5},{2,10},{6,14},... | collective-permute-start | bytes 786440 | tf_op jit(solution)/shard_map/ppermute | solution.py:119
  15.9 3.3 %weigh.1 = (f32[8,128]{1,0:T(8,128)}, f32[8,128]{1,0:T(8,128)}) custom-call(s32[256]{0:T(256)} %reshape.32.pattern, bf16[2,2,128,2048]{3,2,1,0:T(8,128)(2,1)} %bitcast.68, bf16[2,128,2048]{2,1,0:T(8,128)(2,1)} %bitcast.62), custom_call_target="tpu_custom_call" | custom-call | tf_op jit(solution)/shard_map/weigh/pallas_call | solution.py:356
  21.4 4.5 %collective-permute-done.2 = bf16[64,2048]{1,0:T(8,128)(2,1)S(1)} collective-permute-done((bf16[64,2048]{1,0:T(8,128)(2,1)S(1)}, bf16[64,2048]{1,0:T(8,128)(2,1)S(1)}, u32[]{:S(2)}, u32[]{:S(2)}) %collective-permute-start.2) | collective-permute-done | bytes 262176 | tf_op jit(solution)/shard_map/ppermute | solution.py:119
  25.9 4.0 %collective-permute-start.13 = (bf16[64,2048]{1,0:T(8,128)(2,1)S(1)}, bf16[64,2048]{1,0:T(8,128)(2,1)S(1)}, u32[]{:S(2)}, u32[]{:S(2)}) collective-permute-start(bf16[64,2048]{1,0:T(8,128)(2,1)S(1)} %collective-permute-done.2), channel_id=1, source_target_pairs={{0,4},{4,0},{8,12},{12,8},{1,5},{5,1},{9,13},{13,9},{2,6},{6,2},{1... | collective-permute-start | bytes 786440 | tf_op jit(solution)/shard_map/ppermute | solution.py:119
  30.5 9.2 %collective-permute-done.5 = bf16[64,2048]{1,0:T(8,128)(2,1)S(1)} collective-permute-done((bf16[64,2048]{1,0:T(8,128)(2,1)S(1)}, bf16[64,2048]{1,0:T(8,128)(2,1)S(1)}, u32[]{:S(2)}, u32[]{:S(2)}) %collective-permute-start.5) | collective-permute-done | bytes 262176 | tf_op jit(solution)/shard_map/ppermute | solution.py:119
  43.0 5.7 %collective-permute-done.15 = bf16[64,2048]{1,0:T(8,128)(2,1)S(1)} collective-permute-done((bf16[64,2048]{1,0:T(8,128)(2,1)S(1)}, bf16[64,2048]{1,0:T(8,128)(2,1)S(1)}, u32[]{:S(2)}, u32[]{:S(2)}) %collective-permute-start.15) | collective-permute-done | bytes 262176 | tf_op jit(solution)/shard_map/ppermute | solution.py:119
  48.7 7.9 %collective-permute-done.14 = bf16[64,2048]{1,0:T(8,128)(2,1)S(1)} collective-permute-done((bf16[64,2048]{1,0:T(8,128)(2,1)S(1)}, bf16[64,2048]{1,0:T(8,128)(2,1)S(1)}, u32[]{:S(2)}, u32[]{:S(2)}) %collective-permute-start.14) | collective-permute-done | bytes 262176 | tf_op jit(solution)/shard_map/ppermute | solution.py:119
  57.2 4.2 %collective-permute-start.20 = (f32[8,128]{1,0:T(8,128)S(1)}, f32[8,128]{1,0:T(8,128)S(1)}, u32[]{:S(2)}, u32[]{:S(2)}) collective-permute-start(f32[8,128]{1,0:T(8,128)S(1)} %copy-done.55), channel_id=1, source_target_pairs={{0,8},{4,12},{8,0},{12,4},{1,9},{5,13},{9,1},{13,5},{2,10},{6,14},... | collective-permute-start | bytes 12296 | tf_op jit(solution)/shard_map/ppermute | solution.py:119
  61.6 6.4 %collective-permute-done.20.refs_20_ = f32[8,128]{1,0:T(8,128)S(1)} collective-permute-done((f32[8,128]{1,0:T(8,128)S(1)}, f32[8,128]{1,0:T(8,128)S(1)}, u32[]{:S(2)}, u32[]{:S(2)}) %collective-permute-start.20) | collective-permute-done | bytes 4128 | tf_op jit(solution)/shard_map/ppermute | solution.py:119
  72.6 3.3 %collective-permute-start.21 = (bf16[128,2048]{1,0:T(8,128)(2,1)S(1)}, bf16[128,2048]{1,0:T(8,128)(2,1)S(1)}, u32[]{:S(2)}, u32[]{:S(2)}) collective-permute-start(bf16[128,2048]{1,0:T(8,128)(2,1)S(1)} %dynamic-slice_bitcast_fusion.1), channel_id=1, source_target_pairs={{0,8},{4,12},{8,0},{12,4},{1,9},{5,13},{9,1},{13,5},{2,10},{6,14},... | collective-permute-start | bytes 1572872 | tf_op jit(solution)/shard_map/ppermute | solution.py:119
  77.6 15.6 %operate_first.1 = (bf16[2,128,2048]{2,1,0:T(8,128)(2,1)}, bf16[2,128,2048]{2,1,0:T(8,128)(2,1)}, f32[8,128]{1,0:T(8,128)}) custom-call(s32[192]{0:T(256)} %pad_add_fusion.cols, s32[256]{0:T(256)} %reshape.32.pattern, bf16[1,16,3,128,128]{4,3,2,1,0:T(8,128)(2,1)} %right_own.3, bf16[10,3,128,128]{3,2,1,0:T(8,128)(2,1)} %copy-done.2, ...), custom_call_target="tpu_custom_call" | custom-call | flops 3221225472 | bytes 16777216 | tf_op jit(solution)/shard_map/operate_first/pallas_call | solution.py:300
  100.6 2.5 %collective-permute-done.25.refs_3_ = f32[2,8,128]{2,1,0:T(8,128)S(1)} collective-permute-done((f32[2,8,128]{2,1,0:T(8,128)S(1)}, f32[2,8,128]{2,1,0:T(8,128)S(1)}, u32[]{:S(2)}, u32[]{:S(2)}) %collective-permute-start.25) | collective-permute-done | bytes 8224 | tf_op jit(solution)/shard_map/ppermute | solution.py:128
  103.6 5.9 %update.1 = (f32[2,128,2048]{2,1,0:T(8,128)}, f32[8,128]{1,0:T(8,128)}) custom-call(bf16[2,128,2048]{2,1,0:T(8,128)(2,1)} %get-tuple-element.48.psi.refs_18_, bf16[2,128,2048]{2,1,0:T(8,128)(2,1)} %get-tuple-element.49.off.refs_19_, bf16[2,128,2048]{2,1,0:T(8,128)(2,1)} %bitcast.63, bf16[128,2048]{1,0:T(8,128)(2,1)} %copy-done.4, f32[2,8,128]{2,1,0:T(8,128)} %copy-done.43, ...), custom_call_target="tpu_custom_call" | custom-call | tf_op jit(solution)/shard_map/update/pallas_call | solution.py:571
  112.6 2.6 %collective-permute-start.29 = (f32[2,8,128]{2,1,0:T(8,128)S(1)}, f32[2,8,128]{2,1,0:T(8,128)S(1)}, u32[]{:S(2)}, u32[]{:S(2)}) collective-permute-start(f32[2,8,128]{2,1,0:T(8,128)S(1)} %pad_maximum_fusion.5.refs_0_), channel_id=1, source_target_pairs={{0,6},{2,4},{4,2},{6,0},{8,14},{10,12},{12,10},{14,8},{1,7},{3,5},... | collective-permute-start | bytes 24584 | tf_op jit(solution)/shard_map/ppermute | solution.py:128
  117.8 3.5 %correct.1 = (bf16[128,2048]{1,0:T(8,128)(2,1)}, bf16[128,2048]{1,0:T(8,128)(2,1)}) custom-call(bf16[2,128,2048]{2,1,0:T(8,128)(2,1)} %get-tuple-element.48.psi.refs_18_, f32[2,128,2048]{2,1,0:T(8,128)} %get-tuple-element.52.t, f32[2,8,128]{2,1,0:T(8,128)} %copy-done.44, f32[2,8,128]{2,1,0:T(8,128)} %copy-done.47, f32[2,8,128]{2,1,0:T(8,128)} %copy-done.49, ...), custom_call_target="tpu_custom_call" | custom-call | tf_op jit(solution)/shard_map/correct/pallas_call | solution.py:588
  124.9 8.9 %collective-permute-done.30 = bf16[128,2048]{1,0:T(8,128)(2,1)S(1)} collective-permute-done((bf16[128,2048]{1,0:T(8,128)(2,1)}, bf16[128,2048]{1,0:T(8,128)(2,1)S(1)}, u32[]{:S(2)}, u32[]{:S(2)}) %collective-permute-start.30) | collective-permute-done | bytes 524320 | tf_op jit(solution)/shard_map/ppermute | solution.py:119
  139.1 10.8 %collective-permute-done.42 = bf16[128,2048]{1,0:T(8,128)(2,1)S(1)} collective-permute-done((bf16[128,2048]{1,0:T(8,128)(2,1)S(1)}, bf16[128,2048]{1,0:T(8,128)(2,1)S(1)}, u32[]{:S(2)}, u32[]{:S(2)}) %collective-permute-start.42) | collective-permute-done | bytes 524320 | tf_op jit(solution)/shard_map/ppermute | solution.py:119
  150.5 6.9 %collective-permute-done.33 = bf16[128,2048]{1,0:T(8,128)(2,1)S(1)} collective-permute-done((bf16[128,2048]{1,0:T(8,128)(2,1)}, bf16[128,2048]{1,0:T(8,128)(2,1)S(1)}, u32[]{:S(2)}, u32[]{:S(2)}) %collective-permute-start.33) | collective-permute-done | bytes 524320 | tf_op jit(solution)/shard_map/ppermute | solution.py:119
  158.3 2.9 %collective-permute-start.34 = (bf16[128,2048]{1,0:T(8,128)(2,1)}, bf16[128,2048]{1,0:T(8,128)(2,1)S(1)}, u32[]{:S(2)}, u32[]{:S(2)}) collective-permute-start(bf16[128,2048]{1,0:T(8,128)(2,1)} %get-tuple-element.58), channel_id=1, source_target_pairs={{0,8},{4,12},{8,0},{12,4},{1,9},{5,13},{9,1},{13,5},{2,10},{6,14},... | collective-permute-start | bytes 1572872 | tf_op jit(solution)/shard_map/ppermute | solution.py:119
  162.5 16.4 %operate_second.1 = (bf16[128,2048]{1,0:T(8,128)(2,1)}, bf16[64,2048]{1,0:T(8,128)(2,1)}, bf16[64,2048]{1,0:T(8,128)(2,1)}, f32[8,128]{1,0:T(8,128)}) custom-call(s32[192]{0:T(256)} %pad_add_fusion.cols, s32[256]{0:T(256)} %reshape.32.pattern, bf16[1,16,3,128,128]{4,3,2,1,0:T(8,128)(2,1)} %right_own.3, bf16[10,3,128,128]{3,2,1,0:T(8,128)(2,1)} %copy-done.2, ...), custom_call_target="tpu_custom_call" | custom-call | flops 3221225472 | bytes 16777216 | tf_op jit(solution)/shard_map/operate_second/pallas_call | solution.py:300
  178.9 2.0 collective-permute-start.47
  180.9 15.2 %collective-permute-done.47.refs_2_ = bf16[64,2048]{1,0:T(8,128)(2,1)S(1)} collective-permute-done((bf16[64,2048]{1,0:T(8,128)(2,1)}, bf16[64,2048]{1,0:T(8,128)(2,1)S(1)}, u32[]{:S(2)}, u32[]{:S(2)}) %collective-permute-start.47) | collective-permute-done | bytes 262176 | tf_op jit(solution)/shard_map/ppermute | solution.py:119
  199.6 2.1 collective-permute-done.52
  201.7 3.9 %collective-permute-start.53 = (f32[8,128]{1,0:T(8,128)S(1)}, f32[8,128]{1,0:T(8,128)S(1)}, u32[]{:S(2)}, u32[]{:S(2)}) collective-permute-start(f32[8,128]{1,0:T(8,128)S(1)} %add.52), channel_id=1, source_target_pairs={{0,4},{4,0},{8,12},{12,8},{1,5},{5,1},{9,13},{13,9},{2,6},{6,2},{1... | collective-permute-start | bytes 12296 | tf_op jit(solution)/shard_map/ppermute | solution.py:119
  205.7 2.0 collective-permute-done.53
  215.1 19.4 %collective-permute-done.45.refs_3_ = bf16[128,2048]{1,0:T(8,128)(2,1)S(1)} collective-permute-done((bf16[128,2048]{1,0:T(8,128)(2,1)S(1)}, bf16[128,2048]{1,0:T(8,128)(2,1)S(1)}, u32[]{:S(2)}, u32[]{:S(2)}) %collective-permute-start.45) | collective-permute-done | bytes 524320 | tf_op jit(solution)/shard_map/ppermute | solution.py:119
  235.4 2.9 %assemble.2 = bf16[2,2,128,2048]{3,2,1,0:T(8,128)(2,1)} custom-call(bf16[128,2048]{1,0:T(8,128)(2,1)} %get-tuple-element.56.refs_0_, bf16[128,2048]{1,0:T(8,128)(2,1)} %copy-done.5, bf16[128,2048]{1,0:T(8,128)(2,1)} %copy-done.34, bf16[128,2048]{1,0:T(8,128)(2,1)} %copy-done.36), custom_call_target="tpu_custom_call" | custom-call | tf_op jit(solution)/shard_map/assemble/pallas_call | solution.py:466
  239.9 2.8 %collective-permute-done.50.refs_5_ = bf16[64,2048]{1,0:T(8,128)(2,1)S(1)} collective-permute-done((bf16[64,2048]{1,0:T(8,128)(2,1)S(1)}, bf16[64,2048]{1,0:T(8,128)(2,1)S(1)}, u32[]{:S(2)}, u32[]{:S(2)}) %collective-permute-start.50) | collective-permute-done | bytes 262176 | tf_op jit(solution)/shard_map/ppermute | solution.py:119
  243.4 2.9 %assemble.3 = bf16[2,2,128,2048]{3,2,1,0:T(8,128)(2,1)} custom-call(bf16[128,2048]{1,0:T(8,128)(2,1)} %get-tuple-element.61.refs_0_, bf16[128,2048]{1,0:T(8,128)(2,1)} %copy-done.35, bf16[64,2048]{1,0:T(8,128)(2,1)} %copy-done.37, bf16[64,2048]{1,0:T(8,128)(2,1)} %copy-done.38, bf16[64,2048]{1,0:T(8,128)(2,1)} %copy-done.41, bf16[64,2048]{1,0:T(8,128)(2,1)} %copy-done.42), custom_call_target="tpu_custom_call" | custom-call | tf_op jit(solution)/shard_map/assemble/pallas_call | solution.py:466
  (224 shorter events, 57.1 us)
Async XLA Ops:
  4.4 21.4 %collective-permute-start.3 = (bf16[128,2048]{1,0:T(8,128)(2,1)}, bf16[128,2048]{1,0:T(8,128)(2,1)S(1)}, u32[]{:S(2)}, u32[]{:S(2)}) collective-permute-start(bf16[128,2048]{1,0:T(8,128)(2,1)} %get-tuple-element.70), channel_id=1, source_target_pairs={{0,1},{1,0},{2,3},{3,2},{4,5},{5,4},{6,7},{7,6},{8,9},{9,8},{10,11... | collective-permute-start | bytes 1572872 | tf_op jit(solution)/shard_map/ppermute | solution.py:119
  4.9 21.0 %collective-permute-start.4 = (bf16[128,2048]{1,0:T(8,128)(2,1)}, bf16[128,2048]{1,0:T(8,128)(2,1)S(1)}, u32[]{:S(2)}, u32[]{:S(2)}) collective-permute-start(bf16[128,2048]{1,0:T(8,128)(2,1)} %get-tuple-element.42), channel_id=1, source_target_pairs={{0,1},{1,0},{2,3},{3,2},{4,5},{5,4},{6,7},{7,6},{8,9},{9,8},{10,11... | collective-permute-start | bytes 1572872 | tf_op jit(solution)/shard_map/ppermute | solution.py:119
  10.6 50.8 %collective-permute-start.1 = (bf16[10,3,128,128]{3,2,1,0:T(8,128)(2,1)S(1)}, bf16[10,3,128,128]{3,2,1,0:T(8,128)(2,1)S(1)}, u32[]{:S(2)}, u32[]{:S(2)}) collective-permute-start(bf16[10,3,128,128]{3,2,1,0:T(8,128)(2,1)S(1)} %pad_maximum_fusion.1), channel_id=1, source_target_pairs={{0,2},{2,0},{1,3},{3,1},{4,6},{6,4},{5,7},{7,5},{8,10},{10,8},{9,1... | collective-permute-start | bytes 2949128 | tf_op jit(solution)/shard_map/ppermute | solution.py:119
  12.6 13.2 %collective-permute-start.2 = (bf16[64,2048]{1,0:T(8,128)(2,1)S(1)}, bf16[64,2048]{1,0:T(8,128)(2,1)S(1)}, u32[]{:S(2)}, u32[]{:S(2)}) collective-permute-start(bf16[64,2048]{1,0:T(8,128)(2,1)S(1)} %dynamic-slice_bitcast_fusion.7), channel_id=1, source_target_pairs={{0,8},{4,12},{8,0},{12,4},{1,9},{5,13},{9,1},{13,5},{2,10},{6,14},... | collective-permute-start | bytes 786440 | tf_op jit(solution)/shard_map/ppermute | solution.py:119
  25.9 13.8 %collective-permute-start.5 = (bf16[64,2048]{1,0:T(8,128)(2,1)S(1)}, bf16[64,2048]{1,0:T(8,128)(2,1)S(1)}, u32[]{:S(2)}, u32[]{:S(2)}) collective-permute-start(bf16[64,2048]{1,0:T(8,128)(2,1)S(1)} %dynamic-slice_bitcast_fusion.6), channel_id=1, source_target_pairs={{0,8},{4,12},{8,0},{12,4},{1,9},{5,13},{9,1},{13,5},{2,10},{6,14},... | collective-permute-start | bytes 786440 | tf_op jit(solution)/shard_map/ppermute | solution.py:119
  25.9 14.8 %collective-permute-start.13 = (bf16[64,2048]{1,0:T(8,128)(2,1)S(1)}, bf16[64,2048]{1,0:T(8,128)(2,1)S(1)}, u32[]{:S(2)}, u32[]{:S(2)}) collective-permute-start(bf16[64,2048]{1,0:T(8,128)(2,1)S(1)} %collective-permute-done.2), channel_id=1, source_target_pairs={{0,4},{4,0},{8,12},{12,8},{1,5},{5,1},{9,13},{13,9},{2,6},{6,2},{1... | collective-permute-start | bytes 786440 | tf_op jit(solution)/shard_map/ppermute | solution.py:119
  30.0 11.2 %collective-permute-start.11 = (bf16[64,2048]{1,0:T(8,128)(2,1)S(1)}, bf16[64,2048]{1,0:T(8,128)(2,1)S(1)}, u32[]{:S(2)}, u32[]{:S(2)}) collective-permute-start(bf16[64,2048]{1,0:T(8,128)(2,1)S(1)} %collective-permute-done.2), channel_id=1, source_target_pairs={{0,2},{2,0},{1,3},{3,1},{4,6},{6,4},{5,7},{7,5},{8,10},{10,8},{9,1... | collective-permute-start | bytes 786440 | tf_op jit(solution)/shard_map/ppermute | solution.py:119
  30.5 26.7 %collective-permute-start.7 = (bf16[128,2048]{1,0:T(8,128)(2,1)}, bf16[128,2048]{1,0:T(8,128)(2,1)S(1)}, u32[]{:S(2)}, u32[]{:S(2)}) collective-permute-start(bf16[128,2048]{1,0:T(8,128)(2,1)} %get-tuple-element.70), channel_id=1, source_target_pairs={{0,4},{4,0},{8,12},{12,8},{1,5},{5,1},{9,13},{13,9},{2,6},{6,2},{1... | collective-permute-start | bytes 1572872 | tf_op jit(solution)/shard_map/ppermute | solution.py:119
  41.2 15.4 %collective-permute-start.14 = (bf16[64,2048]{1,0:T(8,128)(2,1)S(1)}, bf16[64,2048]{1,0:T(8,128)(2,1)S(1)}, u32[]{:S(2)}, u32[]{:S(2)}) collective-permute-start(bf16[64,2048]{1,0:T(8,128)(2,1)S(1)} %collective-permute-done.5), channel_id=1, source_target_pairs={{0,4},{4,0},{8,12},{12,8},{1,5},{5,1},{9,13},{13,9},{2,6},{6,2},{1... | collective-permute-start | bytes 786440 | tf_op jit(solution)/shard_map/ppermute | solution.py:119
  41.2 15.4 %collective-permute-start.12 = (bf16[64,2048]{1,0:T(8,128)(2,1)S(1)}, bf16[64,2048]{1,0:T(8,128)(2,1)S(1)}, u32[]{:S(2)}, u32[]{:S(2)}) collective-permute-start(bf16[64,2048]{1,0:T(8,128)(2,1)S(1)} %collective-permute-done.5), channel_id=1, source_target_pairs={{0,2},{2,0},{1,3},{3,1},{4,6},{6,4},{5,7},{7,5},{8,10},{10,8},{9,1... | collective-permute-start | bytes 786440 | tf_op jit(solution)/shard_map/ppermute | solution.py:119
  48.7 27.3 %collective-permute-start.18 = (bf16[4,64,2048]{2,1,0:T(8,128)(2,1)S(1)}, bf16[4,64,2048]{2,1,0:T(8,128)(2,1)S(1)}, u32[]{:S(2)}, u32[]{:S(2)}) collective-permute-start(bf16[4,64,2048]{2,1,0:T(8,128)(2,1)S(1)} %pad_maximum_fusion), channel_id=1, source_target_pairs={{0,1},{1,0},{2,3},{3,2},{4,5},{5,4},{6,7},{7,6},{8,9},{9,8},{10,11... | collective-permute-start | bytes 3145736 | tf_op jit(solution)/shard_map/ppermute | solution.py:119
  56.6 11.5 %collective-permute-start.16 = (bf16[64,2048]{1,0:T(8,128)(2,1)S(1)}, bf16[64,2048]{1,0:T(8,128)(2,1)S(1)}, u32[]{:S(2)}, u32[]{:S(2)}) collective-permute-start(bf16[64,2048]{1,0:T(8,128)(2,1)S(1)} %collective-permute-done.14), channel_id=1, source_target_pairs={{0,2},{2,0},{1,3},{3,1},{4,6},{6,4},{5,7},{7,5},{8,10},{10,8},{9,1... | collective-permute-start | bytes 786440 | tf_op jit(solution)/shard_map/ppermute | solution.py:119
  57.2 13.0 %collective-permute-start.8 = (bf16[128,2048]{1,0:T(8,128)(2,1)}, bf16[128,2048]{1,0:T(8,128)(2,1)S(1)}, u32[]{:S(2)}, u32[]{:S(2)}) collective-permute-start(bf16[128,2048]{1,0:T(8,128)(2,1)} %get-tuple-element.42), channel_id=1, source_target_pairs={{0,4},{4,0},{8,12},{12,8},{1,5},{5,1},{9,13},{13,9},{2,6},{6,2},{1... | collective-permute-start | bytes 1572872 | tf_op jit(solution)/shard_map/ppermute | solution.py:119
  57.2 10.9 %collective-permute-start.20 = (f32[8,128]{1,0:T(8,128)S(1)}, f32[8,128]{1,0:T(8,128)S(1)}, u32[]{:S(2)}, u32[]{:S(2)}) collective-permute-start(f32[8,128]{1,0:T(8,128)S(1)} %copy-done.55), channel_id=1, source_target_pairs={{0,8},{4,12},{8,0},{12,4},{1,9},{5,13},{9,1},{13,5},{2,10},{6,14},... | collective-permute-start | bytes 12296 | tf_op jit(solution)/shard_map/ppermute | solution.py:119
  72.6 26.8 %collective-permute-start.21 = (bf16[128,2048]{1,0:T(8,128)(2,1)S(1)}, bf16[128,2048]{1,0:T(8,128)(2,1)S(1)}, u32[]{:S(2)}, u32[]{:S(2)}) collective-permute-start(bf16[128,2048]{1,0:T(8,128)(2,1)S(1)} %dynamic-slice_bitcast_fusion.1), channel_id=1, source_target_pairs={{0,8},{4,12},{8,0},{12,4},{1,9},{5,13},{9,1},{13,5},{2,10},{6,14},... | collective-permute-start | bytes 1572872 | tf_op jit(solution)/shard_map/ppermute | solution.py:119
  121.3 12.5 %collective-permute-start.30 = (bf16[128,2048]{1,0:T(8,128)(2,1)}, bf16[128,2048]{1,0:T(8,128)(2,1)S(1)}, u32[]{:S(2)}, u32[]{:S(2)}) collective-permute-start(bf16[128,2048]{1,0:T(8,128)(2,1)} %get-tuple-element.56.refs_0_), channel_id=1, source_target_pairs={{0,4},{4,0},{8,12},{12,8},{1,5},{5,1},{9,13},{13,9},{2,6},{6,2},{1... | collective-permute-start | bytes 1572872 | tf_op jit(solution)/shard_map/ppermute | solution.py:119
  122.9 12.2 %collective-permute-start.31 = (bf16[128,2048]{1,0:T(8,128)(2,1)}, bf16[128,2048]{1,0:T(8,128)(2,1)S(1)}, u32[]{:S(2)}, u32[]{:S(2)}) collective-permute-start(bf16[128,2048]{1,0:T(8,128)(2,1)} %get-tuple-element.58), channel_id=1, source_target_pairs={{0,2},{2,0},{1,3},{3,1},{4,6},{6,4},{5,7},{7,5},{8,10},{10,8},{9,1... | collective-permute-start | bytes 1572872 | tf_op jit(solution)/shard_map/ppermute | solution.py:119
  124.4 14.2 %collective-permute-start.35 = (bf16[128,2048]{1,0:T(8,128)(2,1)}, bf16[128,2048]{1,0:T(8,128)(2,1)S(1)}, u32[]{:S(2)}, u32[]{:S(2)}) collective-permute-start(bf16[128,2048]{1,0:T(8,128)(2,1)} %get-tuple-element.56.refs_0_), channel_id=1, source_target_pairs={{0,1},{1,0},{2,3},{3,2},{4,5},{5,4},{6,7},{7,6},{8,9},{9,8},{10,11... | collective-permute-start | bytes 1572872 | tf_op jit(solution)/shard_map/ppermute | solution.py:119
  124.4 14.8 %collective-permute-start.36 = (bf16[128,2048]{1,0:T(8,128)(2,1)}, bf16[128,2048]{1,0:T(8,128)(2,1)S(1)}, u32[]{:S(2)}, u32[]{:S(2)}) collective-permute-start(bf16[128,2048]{1,0:T(8,128)(2,1)} %get-tuple-element.58), channel_id=1, source_target_pairs={{0,1},{1,0},{2,3},{3,2},{4,5},{5,4},{6,7},{7,6},{8,9},{9,8},{10,11... | collective-permute-start | bytes 1572872 | tf_op jit(solution)/shard_map/ppermute | solution.py:119
  135.1 14.9 %collective-permute-start.42 = (bf16[128,2048]{1,0:T(8,128)(2,1)S(1)}, bf16[128,2048]{1,0:T(8,128)(2,1)S(1)}, u32[]{:S(2)}, u32[]{:S(2)}) collective-permute-start(bf16[128,2048]{1,0:T(8,128)(2,1)S(1)} %collective-permute-done.31), channel_id=1, source_target_pairs={{0,4},{4,0},{8,12},{12,8},{1,5},{5,1},{9,13},{13,9},{2,6},{6,2},{1... | collective-permute-start | bytes 1572872 | tf_op jit(solution)/shard_map/ppermute | solution.py:119
  135.5 14.9 %collective-permute-start.41 = (bf16[128,2048]{1,0:T(8,128)(2,1)S(1)}, bf16[128,2048]{1,0:T(8,128)(2,1)S(1)}, u32[]{:S(2)}, u32[]{:S(2)}) collective-permute-start(bf16[128,2048]{1,0:T(8,128)(2,1)S(1)} %collective-permute-done.30), channel_id=1, source_target_pairs={{0,2},{2,0},{1,3},{3,1},{4,6},{6,4},{5,7},{7,5},{8,10},{10,8},{9,1... | collective-permute-start | bytes 1572872 | tf_op jit(solution)/shard_map/ppermute | solution.py:119
  137.1 20.3 %collective-permute-start.33 = (bf16[128,2048]{1,0:T(8,128)(2,1)}, bf16[128,2048]{1,0:T(8,128)(2,1)S(1)}, u32[]{:S(2)}, u32[]{:S(2)}) collective-permute-start(bf16[128,2048]{1,0:T(8,128)(2,1)} %get-tuple-element.58), channel_id=1, source_target_pairs={{0,4},{4,0},{8,12},{12,8},{1,5},{5,1},{9,13},{13,9},{2,6},{6,2},{1... | collective-permute-start | bytes 1572872 | tf_op jit(solution)/shard_map/ppermute | solution.py:119
  138.6 19.1 %collective-permute-start.32 = (bf16[128,2048]{1,0:T(8,128)(2,1)}, bf16[128,2048]{1,0:T(8,128)(2,1)S(1)}, u32[]{:S(2)}, u32[]{:S(2)}) collective-permute-start(bf16[128,2048]{1,0:T(8,128)(2,1)} %get-tuple-element.56.refs_0_), channel_id=1, source_target_pairs={{0,2},{2,0},{1,3},{3,1},{4,6},{6,4},{5,7},{7,5},{8,10},{10,8},{9,1... | collective-permute-start | bytes 1572872 | tf_op jit(solution)/shard_map/ppermute | solution.py:119
  139.1 18.8 %collective-permute-start.37 = (bf16[128,2048]{1,0:T(8,128)(2,1)S(1)}, bf16[128,2048]{1,0:T(8,128)(2,1)S(1)}, u32[]{:S(2)}, u32[]{:S(2)}) collective-permute-start(bf16[128,2048]{1,0:T(8,128)(2,1)S(1)} %collective-permute-done.30), channel_id=1, source_target_pairs={{0,1},{1,0},{2,3},{3,2},{4,5},{5,4},{6,7},{7,6},{8,9},{9,8},{10,11... | collective-permute-start | bytes 1572872 | tf_op jit(solution)/shard_map/ppermute | solution.py:119
  150.4 10.8 %collective-permute-start.44 = (bf16[128,2048]{1,0:T(8,128)(2,1)S(1)}, bf16[128,2048]{1,0:T(8,128)(2,1)S(1)}, u32[]{:S(2)}, u32[]{:S(2)}) collective-permute-start(bf16[128,2048]{1,0:T(8,128)(2,1)S(1)} %collective-permute-done.42), channel_id=1, source_target_pairs={{0,1},{1,0},{2,3},{3,2},{4,5},{5,4},{6,7},{7,6},{8,9},{9,8},{10,11... | collective-permute-start | bytes 1572872 | tf_op jit(solution)/shard_map/ppermute | solution.py:119
  158.3 51.5 %collective-permute-start.34 = (bf16[128,2048]{1,0:T(8,128)(2,1)}, bf16[128,2048]{1,0:T(8,128)(2,1)S(1)}, u32[]{:S(2)}, u32[]{:S(2)}) collective-permute-start(bf16[128,2048]{1,0:T(8,128)(2,1)} %get-tuple-element.58), channel_id=1, source_target_pairs={{0,8},{4,12},{8,0},{12,4},{1,9},{5,13},{9,1},{13,5},{2,10},{6,14},... | collective-permute-start | bytes 1572872 | tf_op jit(solution)/shard_map/ppermute | solution.py:119
  178.9 17.2 %collective-permute-start.47 = (bf16[64,2048]{1,0:T(8,128)(2,1)}, bf16[64,2048]{1,0:T(8,128)(2,1)S(1)}, u32[]{:S(2)}, u32[]{:S(2)}) collective-permute-start(bf16[64,2048]{1,0:T(8,128)(2,1)} %get-tuple-element.63), channel_id=1, source_target_pairs={{0,8},{4,12},{8,0},{12,4},{1,9},{5,13},{9,1},{13,5},{2,10},{6,14},... | collective-permute-start | bytes 786440 | tf_op jit(solution)/shard_map/ppermute | solution.py:119
  196.0 17.8 %collective-permute-start.48 = (bf16[64,2048]{1,0:T(8,128)(2,1)}, bf16[64,2048]{1,0:T(8,128)(2,1)S(1)}, u32[]{:S(2)}, u32[]{:S(2)}) collective-permute-start(bf16[64,2048]{1,0:T(8,128)(2,1)} %get-tuple-element.65), channel_id=1, source_target_pairs={{0,8},{4,12},{8,0},{12,4},{1,9},{5,13},{9,1},{13,5},{2,10},{6,14},... | collective-permute-start | bytes 786440 | tf_op jit(solution)/shard_map/ppermute | solution.py:119
  208.3 30.0 %collective-permute-start.46 = (bf16[128,2048]{1,0:T(8,128)(2,1)}, bf16[128,2048]{1,0:T(8,128)(2,1)S(1)}, u32[]{:S(2)}, u32[]{:S(2)}) collective-permute-start(bf16[128,2048]{1,0:T(8,128)(2,1)} %get-tuple-element.61.refs_0_), channel_id=1, source_target_pairs={{0,2},{2,0},{1,3},{3,1},{4,6},{6,4},{5,7},{7,5},{8,10},{10,8},{9,1... | collective-permute-start | bytes 1572872 | tf_op jit(solution)/shard_map/ppermute | solution.py:119
  209.8 24.8 %collective-permute-start.45 = (bf16[128,2048]{1,0:T(8,128)(2,1)S(1)}, bf16[128,2048]{1,0:T(8,128)(2,1)S(1)}, u32[]{:S(2)}, u32[]{:S(2)}) collective-permute-start(bf16[128,2048]{1,0:T(8,128)(2,1)S(1)} %collective-permute-done.34.refs_2_), channel_id=1, source_target_pairs={{0,2},{2,0},{1,3},{3,1},{4,6},{6,4},{5,7},{7,5},{8,10},{10,8},{9,1... | collective-permute-start | bytes 1572872 | tf_op jit(solution)/shard_map/ppermute | solution.py:119
  212.3 27.6 %collective-permute-start.49 = (bf16[64,2048]{1,0:T(8,128)(2,1)S(1)}, bf16[64,2048]{1,0:T(8,128)(2,1)S(1)}, u32[]{:S(2)}, u32[]{:S(2)}) collective-permute-start(bf16[64,2048]{1,0:T(8,128)(2,1)S(1)} %collective-permute-done.47.refs_2_), channel_id=1, source_target_pairs={{0,2},{2,0},{1,3},{3,1},{4,6},{6,4},{5,7},{7,5},{8,10},{10,8},{9,1... | collective-permute-start | bytes 786440 | tf_op jit(solution)/shard_map/ppermute | solution.py:119
  213.8 28.9 %collective-permute-start.50 = (bf16[64,2048]{1,0:T(8,128)(2,1)S(1)}, bf16[64,2048]{1,0:T(8,128)(2,1)S(1)}, u32[]{:S(2)}, u32[]{:S(2)}) collective-permute-start(bf16[64,2048]{1,0:T(8,128)(2,1)S(1)} %collective-permute-done.48.refs_3_), channel_id=1, source_target_pairs={{0,2},{2,0},{1,3},{3,1},{4,6},{6,4},{5,7},{7,5},{8,10},{10,8},{9,1... | collective-permute-start | bytes 786440 | tf_op jit(solution)/shard_map/ppermute | solution.py:119
  (79 other events, 755.8 us)

commit v4 on v3

--- a/solution.py
+++ b/solution.py
@@ -148,12 +148,12 @@
     count = len(plan)
     pieces, refs = refs[:count], refs[count:]
     if first:
-        weight_own, weight_far, psi_out, off_out, stats_out = refs[:5]
-        refs = refs[5:]
+        weight_own, psi_out, off_out, stats_out = refs[:4]
+        refs = refs[4:]
     else:
         hd_own, hd_far, psi_in, off_in, stats_in, near_out, far_out, late_out, stats_out = refs[:9]
         refs = refs[9:]
-    field, images, right, left, diag, sems = refs
+    field, images, right, left, diag, parts, sems = refs
     z, x, c = place()
     sectors, block, width = field.shape
     links = right.shape[2]
@@ -171,9 +171,11 @@
     near, far = pl.ds(c * part, part), pl.ds((1 - c) * part, part)
     begin(right_own.at[0], right.at[0])
     for piece, offsets in zip(pieces, plan):
-        tall = piece.shape[1]
-        for at, (dz, dx, dc, chunk) in enumerate(offsets):
-            begin(piece.at[at], field.at[row_of(dz, dx, dc), pl.ds(chunk * tall, tall)])
+        for at, (dz, dx, dc, start, tall) in enumerate(offsets):
+            target = field.at[row_of(dz, dx, dc), pl.ds(start, tall)]
+            begin(piece.at[at, pl.ds(0, tall)], target)
+            if first and (dz, dx, dc, start) == (2, 0, 0, block - tall):
+                begin(piece.at[at, pl.ds(tall, parts.shape[0]), pl.ds(0, parts.shape[1])], parts)
     begin(right_near.at[pl.ds(0, part)], right.at[1, near])
     begin(right_far, right.at[1, far])
     early = len(copies)
@@ -276,7 +278,8 @@
 
     sums = list(lax.fori_loop(0, sectors // step, column, (zero,) * (2 if first else 3)))
     if first:
-        sums[1] += weight_own[...] + weight_far[...]
+        far_weight = parts[...].astype(jnp.float32)[:8]
+        sums[1] += weight_own[...] + sum(far_weight[:, i * LANES : (i + 1) * LANES] for i in range(3))
     stats_out[...] = jnp.zeros_like(stats_out)
     for at, value in enumerate(sums):
         stats_out[at : at + 1, :] = jnp.sum(value, axis=0, keepdims=True)
@@ -293,8 +296,8 @@
     some = jax.ShapeDtypeStruct((block // 2, width), jnp.bfloat16)
     stats = jax.ShapeDtypeStruct((8, LANES), jnp.float32)
     out_shape = (rows, rows, stats) if first else (one, some, some, stats)
-    extra_specs = [VMEM, VMEM] if first else [ANY, ANY, VMEM, VMEM, VMEM]
-    copies = sum(len(offsets) for offsets in plan) + 8
+    extra_specs = [VMEM] if first else [ANY, ANY, VMEM, VMEM, VMEM]
+    copies = sum(len(offsets) for offsets in plan) + 9
     inner = 2 * 2 * sectors * 2 * links * links * block * block * block
     outer = 2 * 2 * 2 * links * block * block * width
     return pl.pallas_call(
@@ -308,6 +311,7 @@
             pltpu.VMEM((2, sectors, links, block, block), jnp.bfloat16),
             pltpu.VMEM((2, 2, links, block, block), jnp.bfloat16),
             pltpu.VMEM((2, block, width), jnp.bfloat16),
+            pltpu.VMEM((16, 3 * LANES), jnp.bfloat16),
             pltpu.SemaphoreType.DMA((copies,)),
         ],
         compiler_params=pltpu.CompilerParams(vmem_limit_bytes=VMEM_LIMIT),
@@ -318,18 +322,61 @@
     )(cols, pattern, right_own, right_near, right_far, left, *pieces, *extra)
 
 
-def weigh_kernel(pattern, theta, hd, own_out, other_out, waves, diag, sems):
+def prepare_kernel(theta, right, left, first, own, packed, sems):
     z, x, c = place()
+    half = z // 2
+    mine = 4 * z + 2 * c + x
+    part = right.shape[1] // 2
+    tall = first.shape[0]
     copies = [
-        pltpu.make_async_copy(theta.at[0, x], waves.at[0], sems.at[0]),
-        pltpu.make_async_copy(theta.at[1, x], waves.at[1], sems.at[1]),
-        pltpu.make_async_copy(hd.at[x], diag, sems.at[2]),
+        pltpu.make_async_copy(theta.at[1 - half, x, pl.ds(0, tall)], first, sems.at[0]),
+        pltpu.make_async_copy(theta.at[half], own, sems.at[1]),
+        pltpu.make_async_copy(right.at[0, pl.ds(c * part, part)], packed.at[pl.ds(0, part)], sems.at[2]),
+        pltpu.make_async_copy(left.at[0, mine ^ 1], packed.at[part], sems.at[3]),
+        pltpu.make_async_copy(left.at[0, mine ^ 9], packed.at[part + 1], sems.at[4]),
     ]
     for copy in copies:
         copy.start()
     for copy in copies:
         copy.wait()
+
+
+def prepare(tall, theta, right, left):
+    _, _, block, width = theta.shape
+    _, sectors, links = right.shape[:3]
+    kind = jnp.bfloat16
+    return pl.pallas_call(
+        prepare_kernel,
+        out_shape=(
+            jax.ShapeDtypeStruct((tall, width), kind),
+            jax.ShapeDtypeStruct((2, block, width), kind),
+            jax.ShapeDtypeStruct((sectors // 2 + 2, links, block, block), kind),
+        ),
+        in_specs=[ANY] * 3,
+        out_specs=(VMEM,) * 3,
+        scratch_shapes=[pltpu.SemaphoreType.DMA((5,))],
+        compiler_params=pltpu.CompilerParams(vmem_limit_bytes=VMEM_LIMIT),
+        name="prepare",
+    )(theta, right, left)
+
+
+def weigh_kernel(pattern, theta, hd, own_out, second, waves, diag, sems):
+    z, x, c = place()
+    half = z // 2
     block, width = diag.shape
+    rest = second.shape[0] - 16
+    copies = [
+        pltpu.make_async_copy(theta.at[half, x], waves.at[0], sems.at[0]),
+        pltpu.make_async_copy(theta.at[1 - half, x], waves.at[1], sems.at[1]),
+        pltpu.make_async_copy(hd.at[x], diag, sems.at[2]),
+        pltpu.make_async_copy(
+            theta.at[1 - half, x, pl.ds(block - rest, rest)], second.at[pl.ds(0, rest)], sems.at[3]
+        ),
+    ]
+    for copy in copies:
+        copy.start()
+    for copy in copies:
+        copy.wait()
     sectors = width // block
     mine = 4 * z + 2 * c + x
     zero = jnp.zeros((8, LANES), jnp.float32)
@@ -344,25 +391,35 @@
             found.append(sums[root] + fold(weight * wave * wave))
         return tuple(found)
 
-    sums = lax.fori_loop(0, sectors, column, (zero, zero))
-    upper = z // 2 == 1
-    own_out[...] = jnp.where(upper, sums[1], sums[0])
-    other_out[...] = jnp.where(upper, sums[0], sums[1])
-
-
-def weigh(pattern, theta, hd):
+    near, far = lax.fori_loop(0, sectors, column, (zero, zero))
+    own_out[...] = near
+    left = jnp.concatenate([far, zero], axis=0)
+    parts = []
+    for _ in range(3):
+        part = left.astype(jnp.bfloat16)
+        parts.append(part)
+        left = left - part.astype(jnp.float32)
+    parts.append(jnp.zeros((16, width - 3 * LANES), jnp.bfloat16))
+    second[rest:, :] = jnp.concatenate(parts, axis=1)
+
+
+def weigh(rest, pattern, theta, hd):
     _, _, block, width = theta.shape
-    stats = jax.ShapeDtypeStruct((8, LANES), jnp.float32)
     return pl.pallas_call(
         weigh_kernel,
-        out_shape=(stats, stats),
+        out_shape=(
+            jax.ShapeDtypeStruct((8, LANES), jnp.float32),
+            jax.ShapeDtypeStruct((rest + 16, width), theta.dtype),
+        ),
         in_specs=[SMEM, ANY, ANY],
         out_specs=(VMEM, VMEM),
         scratch_shapes=[
             pltpu.VMEM((2, block, width), theta.dtype),
             pltpu.VMEM((block, width), hd.dtype),
-            pltpu.SemaphoreType.DMA((3,)),
+            pltpu.SemaphoreType.DMA((4,)),
         ],
+        cost_estimate=pl.CostEstimate(flops=0, bytes_accessed=64 * 1024 * 1024, transcendentals=0),
+        compiler_params=pltpu.CompilerParams(vmem_limit_bytes=VMEM_LIMIT),
         name="weigh",
     )(pattern, theta, hd)
 
@@ -445,15 +502,15 @@
     lax.fori_loop(0, block // step, chunk, 0)
 
 
-def assemble_kernel(tall, *refs):
-    count = len(tall)
-    pieces, (out, sems) = refs[:count], refs[count:]
+def assemble_kernel(places, based, *refs):
+    count = len(places)
+    pieces, (out, sems) = refs[:count], refs[count + based :]
     z, x, c = place()
     half = z // 2
     copies = []
-    for at, (root, flip, chunk) in enumerate(tall):
+    for at, (root, flip, start) in enumerate(places):
         size = pieces[at].shape[0]
-        target = out.at[half ^ root, x ^ flip, pl.ds(chunk * size, size)]
+        target = out.at[half ^ root, x ^ flip, pl.ds(start, size)]
         copies.append(pltpu.make_async_copy(pieces[at], target, sems.at[at]))
     for copy in copies:
         copy.start()
@@ -461,17 +518,19 @@
         copy.wait()
 
 
-def assemble(block, pieces, tall):
+def assemble(block, pieces, places, base=None):
     width = pieces[0].shape[1]
+    based = [] if base is None else [base]
     return pl.pallas_call(
-        functools.partial(assemble_kernel, tall),
+        functools.partial(assemble_kernel, places, len(based)),
         out_shape=jax.ShapeDtypeStruct((2, 2, block, width), pieces[0].dtype),
-        in_specs=[VMEM] * len(pieces),
+        in_specs=[VMEM] * len(pieces) + [ANY] * len(based),
         out_specs=ANY,
         scratch_shapes=[pltpu.SemaphoreType.DMA((len(pieces),))],
+        input_output_aliases={len(pieces): 0} if based else {},
         compiler_params=pltpu.CompilerParams(vmem_limit_bytes=VMEM_LIMIT),
         name="assemble",
-    )(*pieces).reshape(2, 2 * block, width)
+    )(*pieces, *based)
 
 
 def after(value, *others):
@@ -489,82 +548,80 @@
     halves = theta.reshape(roots, 2, block, width)
     diag = hdiag.reshape(2, block, width)
     allowed = pattern.reshape(-1)
-    chunk = block // 2
-
-    def given(at):
-        return lax.dynamic_slice(halves, (1 - half, x, at * chunk, 0), (1, 1, chunk, width))[0, 0]
-
-    first = given(0)
+    tall = block * 5 // 8
+    rest = block - tall
+
+    first, own, packed = prepare(tall, halves, right_blocks, left_blocks)
     far_a = across(first, "blk", 2)
-    halves = after(halves, first)
-    own = [
-        lax.dynamic_slice(halves, (half, at, 0, 0), (1, 1, block, width))[0, 0] for at in range(2)
-    ]
-    near_a = across(own[0], "blk", 1)
+    near = across(own, "blk", 1)
     cols = jnp.concatenate([right_cols.reshape(-1), left_cols.reshape(-1)])
     cols_other = across(cols, "ops", 1)
     cols = jnp.concatenate([cols, cols_other])
-    part = sectors // 2
-    packed = jnp.concatenate(
-        [
-            lax.dynamic_slice_in_dim(right_blocks[0], c * part, part, 0),
-            lax.dynamic_slice_in_dim(left_blocks[0], mine ^ 1, 1, 0),
-            lax.dynamic_slice_in_dim(left_blocks[0], mine ^ 9, 1, 0),
-        ]
-    )
-    operators = across(after(packed, cols_other), "ops", 1)
-    own_core = [across(value, "sub", 1) for value in own]
-    weight_own, weight_far = weigh(allowed, halves, diag)
-
-    far_a, second = after((far_a, given(1)), weight_own, cols, *own_core)
+    operators = across(packed, "ops", 1)
+    own_core = across(own, "sub", 1)
+    weight_own, second = weigh(rest, allowed, halves, diag)
+
+    far_a, second = after((far_a, second), cols, own_core)
     far_b = across(after(second, far_a), "blk", 2)
     far_za = across(far_a, "blk", 1)
     far_xa = across(far_a, "ops", 1)
-    weight_far = across(weight_far, "blk", 2)
 
     far_zb = across(after(far_b, far_za), "blk", 1)
-    near_b = across(after(own[1], far_b), "blk", 1)
     far_zxa = across(after(far_za, far_b), "ops", 1)
     far_xb = across(far_b, "ops", 1)
-    operators_core = across(after(operators[:part], far_b), "sub", 1)
-    near_a_core = across(after(near_a, far_b), "sub", 1)
-    core_a = across(jnp.stack([far_a, far_b, far_xa, far_za]), "sub", 1)
+    operators_core = across(after(operators, far_b)[: sectors // 2], "sub", 1)
+    near_core = across(after(near, far_b), "sub", 1)
+    core_a = across(jnp.stack([far_a, far_xa, far_za]), "sub", 1)
 
     far_zxb = across(after(far_zb, far_xb, far_zxa), "ops", 1)
-    core_b = across(jnp.stack([far_xb, far_zxa, far_zb]), "sub", 1)
-    near_b_core = across(near_b, "sub", 1)
+    core_b = across(jnp.stack([far_b, far_xb, far_zb]), "sub", 1)
+    far_zxa_core = across(far_zxa, "sub", 1)
+    far_zxb_core = across(far_zxb, "sub", 1)
     hd_far = lax.dynamic_index_in_dim(diag, x, 0, keepdims=False)
     hd_far = across(after(hd_far, far_zb), "blk", 2)
-    far_zxb_core = across(far_zxb, "sub", 1)
 
     right = (right_blocks, operators, operators_core)
     pieces = []
     plan = []
     for piece, offsets in (
-        (own[0], ((0, 2, 0, 0),)),
-        (own[1], ((0, 3, 0, 0),)),
-        (own_core[0], ((0, 2, 1, 0),)),
-        (own_core[1], ((0, 3, 1, 0),)),
-        (near_a, ((1, 2, 0, 0),)),
-        (near_b, ((1, 3, 0, 0),)),
-        (near_a_core, ((1, 2, 1, 0),)),
-        (near_b_core, ((1, 3, 1, 0),)),
-        (far_a, ((2, 0, 0, 0),)),
-        (far_b, ((2, 0, 0, 1),)),
-        (far_xa, ((2, 1, 0, 0),)),
-        (far_xb, ((2, 1, 0, 1),)),
-        (far_za, ((3, 0, 0, 0),)),
-        (far_zb, ((3, 0, 0, 1),)),
-        (far_zxa, ((3, 1, 0, 0),)),
-        (far_zxb, ((3, 1, 0, 1),)),
-        (far_zxb_core, ((3, 1, 1, 1),)),
-        (core_a, ((2, 0, 1, 0), (2, 0, 1, 1), (2, 1, 1, 0), (3, 0, 1, 0))),
-        (core_b, ((2, 1, 1, 1), (3, 1, 1, 0), (3, 0, 1, 1))),
+        (own, ((0, 2, 0), (0, 3, 0))),
+        (own_core, ((0, 2, 1), (0, 3, 1))),
+        (near, ((1, 2, 0), (1, 3, 0))),
+        (near_core, ((1, 2, 1), (1, 3, 1))),
     ):
-        pieces.append(piece if piece.ndim == 3 else piece[None])
-        plan.append(offsets)
+        pieces.append(piece)
+        plan.append(tuple(offset + (0, block) for offset in offsets))
+    for start, count, group in (
+        (
+            0,
+            tall,
+            (
+                (far_a, ((2, 0, 0),)),
+                (far_xa, ((2, 1, 0),)),
+                (far_za, ((3, 0, 0),)),
+                (far_zxa, ((3, 1, 0),)),
+                (core_a, ((2, 0, 1), (2, 1, 1), (3, 0, 1))),
+                (far_zxa_core, ((3, 1, 1),)),
+            ),
+        ),
+        (
+            tall,
+            rest,
+            (
+                (far_b, ((2, 0, 0),)),
+                (far_xb, ((2, 1, 0),)),
+                (far_zb, ((3, 0, 0),)),
+                (far_zxb, ((3, 1, 0),)),
+                (core_b, ((2, 0, 1), (2, 1, 1), (3, 0, 1))),
+                (far_zxb_core, ((3, 1, 1),)),
+            ),
+        ),
+    ):
+        for piece, offsets in group:
+            pieces.append(piece if piece.ndim == 3 else piece[None])
+            plan.append(tuple(offset + (start, count) for offset in offsets))
     psi, off_one, stats_one = operate(
-        True, tuple(plan), pieces, cols, allowed, right, left_blocks, (weight_own, weight_far)
+        True, tuple(plan), pieces, cols, allowed, right, left_blocks, (weight_own,)
     )
 
     found = share(stats_one)
@@ -585,7 +642,7 @@
     )(psi, off_one, diag, hd_far, *found)
     found = share(stats_two)
     one = jax.ShapeDtypeStruct((block, width), jnp.bfloat16)
-    near, far = pl.pallas_call(
+    changed_near, changed_far = pl.pallas_call(
         correct_kernel,
         out_shape=(one, one),
         in_specs=[VMEM, VMEM] + [VMEM] * 4,
@@ -594,64 +651,65 @@
         name="correct",
     )(psi, t, *found)
 
-    near_z = across(near, "blk", 1)
-    far_x = across(far, "ops", 1)
-    near_core = across(near, "sub", 1)
-    far_core = across(far, "sub", 1)
+    near_z = across(changed_near, "blk", 1)
+    far_x = across(changed_far, "ops", 1)
+    near_core = across(changed_near, "sub", 1)
+    far_core = across(changed_far, "sub", 1)
     near_zx = across(after(near_z, far_x), "ops", 1)
     far_xz = across(after(far_x, near_z), "blk", 1)
-    near_x = across(after(near, near_z, far_x), "ops", 1)
-    far_z = across(after(far, near_z, far_x), "blk", 1)
+    near_x = across(after(changed_near, near_z, far_x), "ops", 1)
+    far_z = across(after(changed_far, near_z, far_x), "blk", 1)
     near_z_core = across(near_z, "sub", 1)
     far_x_core = across(far_x, "sub", 1)
     near_x_core = across(near_x, "sub", 1)
     far_z_core = across(far_z, "sub", 1)
     near_zx_core = across(near_zx, "sub", 1)
     far_xz_core = across(far_xz, "sub", 1)
-    other = across(after(far, near_x, far_z), "blk", 2)
+    other = across(after(changed_far, near_z, far_x), "blk", 2)
     pieces, plan = [], []
     for piece, offset in (
-        (near, (0, 0, 0, 0)),
-        (far, (2, 0, 0, 0)),
-        (near_core, (0, 0, 1, 0)),
-        (far_core, (2, 0, 1, 0)),
-        (near_z, (1, 0, 0, 0)),
-        (far_z, (3, 0, 0, 0)),
-        (near_z_core, (1, 0, 1, 0)),
-        (far_z_core, (3, 0, 1, 0)),
-        (near_x, (0, 1, 0, 0)),
-        (far_x, (2, 1, 0, 0)),
-        (near_x_core, (0, 1, 1, 0)),
-        (far_x_core, (2, 1, 1, 0)),
-        (near_zx, (1, 1, 0, 0)),
-        (far_xz, (3, 1, 0, 0)),
-        (near_zx_core, (1, 1, 1, 0)),
-        (far_xz_core, (3, 1, 1, 0)),
+        (changed_near, (0, 0, 0)),
+        (changed_far, (2, 0, 0)),
+        (near_core, (0, 0, 1)),
+        (far_core, (2, 0, 1)),
+        (near_z, (1, 0, 0)),
+        (far_z, (3, 0, 0)),
+        (near_z_core, (1, 0, 1)),
+        (far_z_core, (3, 0, 1)),
+        (near_x, (0, 1, 0)),
+        (far_x, (2, 1, 0)),
+        (near_x_core, (0, 1, 1)),
+        (far_x_core, (2, 1, 1)),
+        (near_zx, (1, 1, 0)),
+        (far_xz, (3, 1, 0)),
+        (near_zx_core, (1, 1, 1)),
+        (far_xz_core, (3, 1, 1)),
     ):
         pieces.append(piece[None])
-        plan.append((offset,))
+        plan.append((offset + (0, block),))
     two_near, two_far, two_late, stats_three = operate(
         False, tuple(plan), pieces, cols, allowed, right, left_blocks, (diag, hd_far, psi, off_one, stats_one)
     )
 
     far_in = across(two_far, "blk", 2)
     near_in = across(two_near, "ops", 1)
-    late_in = across(after(two_late, far_in), "blk", 2)
-    far_in_x = across(far_in, "ops", 1)
-    other_x = across(after(other, two_near), "ops", 1)
-    late_in_x = across(late_in, "ops", 1)
+    late_in = across(after(two_late, far_in, near_in), "blk", 2)
+    far_in_x = across(after(far_in, near_in), "ops", 1)
+    other_x = across(after(other, near_in), "ops", 1)
+    late_in_x = across(after(late_in, other_x, far_in_x), "ops", 1)
     sums = stats_three + across(stats_three, "sub", 1)
-    sums = sums + across(sums, "ops", 1)
     sums = sums + across(sums, "blk", 1)
     both = jnp.stack([sums, across(sums, "blk", 2)])
+    both = both + across(after(both, near_in), "ops", 1)
     both = jnp.sum(jnp.where(half == 0, both, both[::-1])[:, :5], axis=2)
     scale = both[:, 3:4] + 1e-06
     subspace = jnp.concatenate([both[:, 4:5], both[:, 0:3]], axis=1) / scale
     places = ((0, 0, 0), (0, 1, 0), (1, 0, 0), (1, 1, 0))
-    correction = assemble(block, (near, near_x, other, other_x), places)
-    places = ((0, 0, 0), (0, 1, 0), (1, 0, 0), (1, 0, 1), (1, 1, 0), (1, 1, 1))
-    sigma_two = assemble(block, (two_near, near_in, far_in, late_in, far_in_x, late_in_x), places)
-    return correction, sigma_two, subspace
+    correction = assemble(block, (changed_near, near_x, other, other_x), places)
+    places = ((0, 0, 0), (0, 1, 0), (1, 0, 0), (1, 0, block // 2), (1, 1, 0))
+    sigma_two = assemble(block, (two_near, near_in, far_in, late_in, far_in_x), places)
+    sigma_two = assemble(block, (late_in_x,), ((1, 1, block // 2),), sigma_two)
+    return correction.reshape(theta.shape), sigma_two.reshape(theta.shape), subspace
 
 
 def solution(mesh):

time: 247 us -> 233 us (0.943)
  starting transfers between devices: 54.4 us -> 46.3 us
  local copies, waits for them, and re-layouts: 12.4 us -> 5.45 us
  Pallas kernels: 50.4 us -> 55.1 us
  waiting for transfers between devices: 123 us -> 119 us
    ppermute x49 -> x46, starting transfers between devices: 47.4 us -> 39.3 us  [across(): return lax.ppermute(value, axis, [(i, i ^ distance) for i in range(size)])]
    pallas_call x3 -> x5, Pallas kernels: 8.98 us -> 13.7 us  [the longest x3 7.21 us: assemble(): pl.pallas_call(functools.partial(assemble_kernel, places, len(based)), ou...]
    another operation x1 -> x0, local copies, waits for them, and re-layouts: 2.64 us -> none  [shards(): pieces.append(piece if piece.ndim == 3 else piece[None])]
    unnamed x114 -> x94, local copies, waits for them, and re-layouts: 5.74 us -> 3.53 us
    ppermute x49 -> x46, waiting for transfers between devices: 117 us -> 115 us  [across(): return lax.ppermute(value, axis, [(i, i ^ distance) for i in range(size)])]
  transfers between devices with their start and end apart: 55 -> 52, of which waited for: 31 -> 31; matrix products, arithmetic and copies ran while one was open for 3% -> 3% of each run, Pallas kernels for 15% -> 18%
where the time goes in v4:
time: 233 us
  waiting for transfers between devices  119 us (51%)
  Pallas kernels  55.1 us (24%)
  starting transfers between devices  46.3 us (20%)
  other arithmetic  5.75 us (2%)
  local copies, waits for them, and re-layouts  5.45 us (2%)
    ppermute x46, waiting for transfers between devices, across(): return lax.ppermute(value, axis, [(i, i ^ distance) for i in range(size)])  115 us
    ppermute x46, starting transfers between devices, across(): return lax.ppermute(value, axis, [(i, i ^ distance) for i in range(size)])  39.3 us
    pallas_call x2, Pallas kernels, operate(): pl.pallas_call(functools.partial(operate_kernel, first, plan), out_shape=...  32 us
    pallas_call x3, Pallas kernels, assemble(): pl.pallas_call(functools.partial(assemble_kernel, places, len(based)), ou...  7.21 us
    ppermute x6, starting transfers between devices, share(): lax.ppermute(pair, axes, [(i, i ^ distance) for i in range(count)])  6.98 us
    pallas_call x1, Pallas kernels, shards(): pl.pallas_call(update_kernel, out_shape=(jax.ShapeDtypeStruct((2, block,...  5.92 us
  transfers between devices with their start and end apart: 52, of which 31 were waited for; matrix products, arithmetic and copies ran while one was open for 3% of the time, Pallas kernels for 18%

profile of v4, /device:TPU:0, one launch (start us, length us, event | category | flops | bytes accessed | tf_op | source)
XLA Modules:
  0.0 232.7 jit_solution(11364788383355791636)
XLA Ops:
  0.7 3.0 %prepare.1 = (bf16[80,2048]{1,0:T(8,128)(2,1)}, bf16[2,128,2048]{2,1,0:T(8,128)(2,1)}, bf16[10,3,128,128]{3,2,1,0:T(8,128)(2,1)}) custom-call(bf16[2,2,128,2048]{3,2,1,0:T(8,128)(2,1)} %bitcast.43, bf16[1,16,3,128,128]{4,3,2,1,0:T(8,128)(2,1)} %right_own.3, bf16[1,16,3,128,128]{4,3,2,1,0:T(8,128)(2,1)} %left_own.3), custom_call_target="tpu_custom_call" | custom-call | tf_op jit(solution)/shard_map/prepare/pallas_call | solution.py:348
  4.2 2.6 %collective-permute-start.6 = (bf16[2,128,2048]{2,1,0:T(8,128)(2,1)}, bf16[2,128,2048]{2,1,0:T(8,128)(2,1)}, u32[]{:S(2)}, u32[]{:S(2)}) collective-permute-start(bf16[2,128,2048]{2,1,0:T(8,128)(2,1)} %get-tuple-element.40.refs_0_), channel_id=1, source_target_pairs={{0,4},{4,0},{8,12},{12,8},{1,5},{5,1},{9,13},{13,9},{2,6},{6,2},{1... | collective-permute-start | bytes 3145736 | tf_op jit(solution)/shard_map/ppermute | solution.py:119
  8.4 2.6 %collective-permute-start.2 = (bf16[80,2048]{1,0:T(8,128)(2,1)}, bf16[80,2048]{1,0:T(8,128)(2,1)S(1)}, u32[]{:S(2)}, u32[]{:S(2)}) collective-permute-start(bf16[80,2048]{1,0:T(8,128)(2,1)} %get-tuple-element.38), channel_id=1, source_target_pairs={{0,8},{4,12},{8,0},{12,4},{1,9},{5,13},{9,1},{13,5},{2,10},{6,14},... | collective-permute-start | bytes 983048 | tf_op jit(solution)/shard_map/ppermute | solution.py:119
  12.6 3.5 %weigh.1 = (f32[8,128]{1,0:T(8,128)}, bf16[64,2048]{1,0:T(8,128)(2,1)}) custom-call(s32[256]{0:T(256)} %reshape.29.pattern, bf16[2,2,128,2048]{3,2,1,0:T(8,128)(2,1)} %bitcast.44, bf16[2,128,2048]{2,1,0:T(8,128)(2,1)} %bitcast.39), custom_call_target="tpu_custom_call" | custom-call | bytes 67108864 | tf_op jit(solution)/shard_map/weigh/pallas_call | solution.py:408
  16.1 14.9 %collective-permute-done = s32[96]{0:T(128)S(1)} collective-permute-done((s32[96]{0:T(128)S(1)}, s32[96]{0:T(128)S(1)}, u32[]{:S(2)}, u32[]{:S(2)}) %collective-permute-start) | collective-permute-done | bytes 416 | tf_op jit(solution)/shard_map/ppermute | solution.py:119
  31.6 5.6 %collective-permute-done.2 = bf16[80,2048]{1,0:T(8,128)(2,1)S(1)} collective-permute-done((bf16[80,2048]{1,0:T(8,128)(2,1)}, bf16[80,2048]{1,0:T(8,128)(2,1)S(1)}, u32[]{:S(2)}, u32[]{:S(2)}) %collective-permute-start.2) | collective-permute-done | bytes 327712 | tf_op jit(solution)/shard_map/ppermute | solution.py:119
  37.3 3.4 %collective-permute-start.9 = (bf16[80,2048]{1,0:T(8,128)(2,1)S(1)}, bf16[80,2048]{1,0:T(8,128)(2,1)S(1)}, u32[]{:S(2)}, u32[]{:S(2)}) collective-permute-start(bf16[80,2048]{1,0:T(8,128)(2,1)S(1)} %collective-permute-done.2), channel_id=1, source_target_pairs={{0,4},{4,0},{8,12},{12,8},{1,5},{5,1},{9,13},{13,9},{2,6},{6,2},{1... | collective-permute-start | bytes 983048 | tf_op jit(solution)/shard_map/ppermute | solution.py:119
  42.2 12.9 %collective-permute-done.4 = bf16[64,2048]{1,0:T(8,128)(2,1)S(1)} collective-permute-done((bf16[64,2048]{1,0:T(8,128)(2,1)}, bf16[64,2048]{1,0:T(8,128)(2,1)S(1)}, u32[]{:S(2)}, u32[]{:S(2)}) %collective-permute-start.4) | collective-permute-done | bytes 262176 | tf_op jit(solution)/shard_map/ppermute | solution.py:119
  60.2 7.9 %collective-permute-done.13 = bf16[64,2048]{1,0:T(8,128)(2,1)S(1)} collective-permute-done((bf16[64,2048]{1,0:T(8,128)(2,1)S(1)}, bf16[64,2048]{1,0:T(8,128)(2,1)S(1)}, u32[]{:S(2)}, u32[]{:S(2)}) %collective-permute-start.13) | collective-permute-done | bytes 262176 | tf_op jit(solution)/shard_map/ppermute | solution.py:119
  68.2 1.6 collective-permute-start.15
  71.0 5.9 %collective-permute-done.15 = bf16[64,2048]{1,0:T(8,128)(2,1)S(1)} collective-permute-done((bf16[64,2048]{1,0:T(8,128)(2,1)S(1)}, bf16[64,2048]{1,0:T(8,128)(2,1)S(1)}, u32[]{:S(2)}, u32[]{:S(2)}) %collective-permute-start.15) | collective-permute-done | bytes 262176 | tf_op jit(solution)/shard_map/ppermute | solution.py:119
  77.0 1.8 collective-permute-done.12
  79.0 2.5 %collective-permute-start.18 = (bf16[128,2048]{1,0:T(8,128)(2,1)S(1)}, bf16[128,2048]{1,0:T(8,128)(2,1)S(1)}, u32[]{:S(2)}, u32[]{:S(2)}) collective-permute-start(bf16[128,2048]{1,0:T(8,128)(2,1)S(1)} %dynamic-slice_bitcast_fusion), channel_id=1, source_target_pairs={{0,8},{4,12},{8,0},{12,4},{1,9},{5,13},{9,1},{13,5},{2,10},{6,14},... | collective-permute-start | bytes 1572872 | tf_op jit(solution)/shard_map/ppermute | solution.py:119
  82.2 15.6 %operate_first.1 = (bf16[2,128,2048]{2,1,0:T(8,128)(2,1)}, bf16[2,128,2048]{2,1,0:T(8,128)(2,1)}, f32[8,128]{1,0:T(8,128)}) custom-call(s32[192]{0:T(256)} %pad_add_fusion.cols, s32[256]{0:T(256)} %reshape.29.pattern, bf16[1,16,3,128,128]{4,3,2,1,0:T(8,128)(2,1)} %right_own.3, bf16[10,3,128,128]{3,2,1,0:T(8,128)(2,1)} %copy-done.1, ...), custom_call_target="tpu_custom_call" | custom-call | flops 3221225472 | bytes 16777216 | tf_op jit(solution)/shard_map/operate_first/pallas_call | solution.py:303
  101.8 1.7 collective-permute-start.22
  103.5 2.0 collective-permute-done.18.hd_far.refs_17_
  107.3 5.9 %update.1 = (f32[2,128,2048]{2,1,0:T(8,128)}, f32[8,128]{1,0:T(8,128)}) custom-call(bf16[2,128,2048]{2,1,0:T(8,128)(2,1)} %get-tuple-element.50.psi.refs_18_, bf16[2,128,2048]{2,1,0:T(8,128)(2,1)} %get-tuple-element.51.off.refs_19_, bf16[2,128,2048]{2,1,0:T(8,128)(2,1)} %bitcast.40, bf16[128,2048]{1,0:T(8,128)(2,1)} %copy-done.3, f32[2,8,128]{2,1,0:T(8,128)} %copy-done.35, ...), custom_call_target="tpu_custom_call" | custom-call | tf_op jit(solution)/shard_map/update/pallas_call | solution.py:628
  117.2 1.6 collective-permute-start.26
  119.5 2.3 collective-permute-done.26.refs_3_
  122.4 3.5 %correct.1 = (bf16[128,2048]{1,0:T(8,128)(2,1)}, bf16[128,2048]{1,0:T(8,128)(2,1)}) custom-call(bf16[2,128,2048]{2,1,0:T(8,128)(2,1)} %get-tuple-element.50.psi.refs_18_, f32[2,128,2048]{2,1,0:T(8,128)} %get-tuple-element.54.t, f32[2,8,128]{2,1,0:T(8,128)} %copy-done.36, f32[2,8,128]{2,1,0:T(8,128)} %copy-done.39, f32[2,8,128]{2,1,0:T(8,128)} %copy-done.41, ...), custom_call_target="tpu_custom_call" | custom-call | tf_op jit(solution)/shard_map/correct/pallas_call | solution.py:645
  128.5 9.9 %collective-permute-done.27 = bf16[128,2048]{1,0:T(8,128)(2,1)S(1)} collective-permute-done((bf16[128,2048]{1,0:T(8,128)(2,1)}, bf16[128,2048]{1,0:T(8,128)(2,1)S(1)}, u32[]{:S(2)}, u32[]{:S(2)}) %collective-permute-start.27) | collective-permute-done | bytes 524320 | tf_op jit(solution)/shard_map/ppermute | solution.py:119
  142.8 10.8 %collective-permute-done.39 = bf16[128,2048]{1,0:T(8,128)(2,1)S(1)} collective-permute-done((bf16[128,2048]{1,0:T(8,128)(2,1)S(1)}, bf16[128,2048]{1,0:T(8,128)(2,1)S(1)}, u32[]{:S(2)}, u32[]{:S(2)}) %collective-permute-start.39) | collective-permute-done | bytes 524320 | tf_op jit(solution)/shard_map/ppermute | solution.py:119
  155.0 6.1 %collective-permute-done.33 = bf16[128,2048]{1,0:T(8,128)(2,1)S(1)} collective-permute-done((bf16[128,2048]{1,0:T(8,128)(2,1)}, bf16[128,2048]{1,0:T(8,128)(2,1)S(1)}, u32[]{:S(2)}, u32[]{:S(2)}) %collective-permute-start.33) | collective-permute-done | bytes 524320 | tf_op jit(solution)/shard_map/ppermute | solution.py:119
  165.7 16.3 %operate_second.1 = (bf16[128,2048]{1,0:T(8,128)(2,1)}, bf16[64,2048]{1,0:T(8,128)(2,1)}, bf16[64,2048]{1,0:T(8,128)(2,1)}, f32[8,128]{1,0:T(8,128)}) custom-call(s32[192]{0:T(256)} %pad_add_fusion.cols, s32[256]{0:T(256)} %reshape.29.pattern, bf16[1,16,3,128,128]{4,3,2,1,0:T(8,128)(2,1)} %right_own.3, bf16[10,3,128,128]{3,2,1,0:T(8,128)(2,1)} %copy-done.1, ...), custom_call_target="tpu_custom_call" | custom-call | flops 3221225472 | bytes 16777216 | tf_op jit(solution)/shard_map/operate_second/pallas_call | solution.py:303
  184.9 10.0 %collective-permute-done.30.refs_2_ = bf16[128,2048]{1,0:T(8,128)(2,1)S(1)} collective-permute-done((bf16[128,2048]{1,0:T(8,128)(2,1)}, bf16[128,2048]{1,0:T(8,128)(2,1)S(1)}, u32[]{:S(2)}, u32[]{:S(2)}) %collective-permute-start.30) | collective-permute-done | bytes 524320 | tf_op jit(solution)/shard_map/ppermute | solution.py:119
  200.9 2.6 %collective-permute-done.49 = f32[8,128]{1,0:T(8,128)S(1)} collective-permute-done((f32[8,128]{1,0:T(8,128)S(1)}, f32[8,128]{1,0:T(8,128)S(1)}, u32[]{:S(2)}, u32[]{:S(2)}) %collective-permute-start.49) | collective-permute-done | bytes 4128 | tf_op jit(solution)/shard_map/ppermute | solution.py:119
  204.7 3.3 %collective-permute-done.50 = f32[8,128]{1,0:T(8,128)S(1)} collective-permute-done((f32[8,128]{1,0:T(8,128)S(1)}, f32[8,128]{1,0:T(8,128)S(1)}, u32[]{:S(2)}, u32[]{:S(2)}) %collective-permute-start.50) | collective-permute-done | bytes 4128 | tf_op jit(solution)/shard_map/ppermute | solution.py:119
  211.9 3.4 %collective-permute-done.46.refs_4_ = bf16[64,2048]{1,0:T(8,128)(2,1)S(1)} collective-permute-done((bf16[64,2048]{1,0:T(8,128)(2,1)S(1)}, bf16[64,2048]{1,0:T(8,128)(2,1)S(1)}, u32[]{:S(2)}, u32[]{:S(2)}) %collective-permute-start.46) | collective-permute-done | bytes 262176 | tf_op jit(solution)/shard_map/ppermute | solution.py:119
  215.3 7.3 %collective-permute-done.45.refs_3_ = bf16[64,2048]{1,0:T(8,128)(2,1)S(1)} collective-permute-done((bf16[64,2048]{1,0:T(8,128)(2,1)}, bf16[64,2048]{1,0:T(8,128)(2,1)S(1)}, u32[]{:S(2)}, u32[]{:S(2)}) %collective-permute-start.45) | collective-permute-done | bytes 262176 | tf_op jit(solution)/shard_map/ppermute | solution.py:119
  224.0 2.7 %assemble.4.refs_1_ = bf16[2,2,128,2048]{3,2,1,0:T(8,128)(2,1)} custom-call(bf16[128,2048]{1,0:T(8,128)(2,1)} %get-tuple-element.62.refs_0_, bf16[128,2048]{1,0:T(8,128)(2,1)} %copy-done.12, bf16[64,2048]{1,0:T(8,128)(2,1)} %copy-done.32, bf16[64,2048]{1,0:T(8,128)(2,1)} %copy-done.33, bf16[64,2048]{1,0:T(8,128)(2,1)} %copy-done.34), custom_call_target="tpu_custom_call" | custom-call | tf_op jit(solution)/shard_map/assemble/pallas_call | solution.py:524
  226.7 2.9 %assemble.3 = bf16[2,2,128,2048]{3,2,1,0:T(8,128)(2,1)} custom-call(bf16[128,2048]{1,0:T(8,128)(2,1)} %get-tuple-element.58.refs_0_, bf16[128,2048]{1,0:T(8,128)(2,1)} %copy-done.4, bf16[128,2048]{1,0:T(8,128)(2,1)} %copy-done.26, bf16[128,2048]{1,0:T(8,128)(2,1)} %copy-done.27), custom_call_target="tpu_custom_call" | custom-call | tf_op jit(solution)/shard_map/assemble/pallas_call | solution.py:524
  231.0 1.7 assemble.5
  (194 shorter events, 53.9 us)
Async XLA Ops:
  3.7 33.5 %collective-permute-start.3 = (bf16[2,128,2048]{2,1,0:T(8,128)(2,1)}, bf16[2,128,2048]{2,1,0:T(8,128)(2,1)S(1)}, u32[]{:S(2)}, u32[]{:S(2)}) collective-permute-start(bf16[2,128,2048]{2,1,0:T(8,128)(2,1)} %get-tuple-element.40.refs_0_), channel_id=1, source_target_pairs={{0,1},{1,0},{2,3},{3,2},{4,5},{5,4},{6,7},{7,6},{8,9},{9,8},{10,11... | collective-permute-start | bytes 3145736 | tf_op jit(solution)/shard_map/ppermute | solution.py:119
  4.2 52.9 %collective-permute-start.6 = (bf16[2,128,2048]{2,1,0:T(8,128)(2,1)}, bf16[2,128,2048]{2,1,0:T(8,128)(2,1)}, u32[]{:S(2)}, u32[]{:S(2)}) collective-permute-start(bf16[2,128,2048]{2,1,0:T(8,128)(2,1)} %get-tuple-element.40.refs_0_), channel_id=1, source_target_pairs={{0,4},{4,0},{8,12},{12,8},{1,5},{5,1},{9,13},{13,9},{2,6},{6,2},{1... | collective-permute-start | bytes 3145736 | tf_op jit(solution)/shard_map/ppermute | solution.py:119
  6.9 50.8 %collective-permute-start.1 = (bf16[10,3,128,128]{3,2,1,0:T(8,128)(2,1)}, bf16[10,3,128,128]{3,2,1,0:T(8,128)(2,1)S(1)}, u32[]{:S(2)}, u32[]{:S(2)}) collective-permute-start(bf16[10,3,128,128]{3,2,1,0:T(8,128)(2,1)} %get-tuple-element.37), channel_id=1, source_target_pairs={{0,2},{2,0},{1,3},{3,1},{4,6},{6,4},{5,7},{7,5},{8,10},{10,8},{9,1... | collective-permute-start | bytes 2949128 | tf_op jit(solution)/shard_map/ppermute | solution.py:119
  8.4 28.9 %collective-permute-start.2 = (bf16[80,2048]{1,0:T(8,128)(2,1)}, bf16[80,2048]{1,0:T(8,128)(2,1)S(1)}, u32[]{:S(2)}, u32[]{:S(2)}) collective-permute-start(bf16[80,2048]{1,0:T(8,128)(2,1)} %get-tuple-element.38), channel_id=1, source_target_pairs={{0,8},{4,12},{8,0},{12,4},{1,9},{5,13},{9,1},{13,5},{2,10},{6,14},... | collective-permute-start | bytes 983048 | tf_op jit(solution)/shard_map/ppermute | solution.py:119
  11.4 19.6 %collective-permute-start = (s32[96]{0:T(128)S(1)}, s32[96]{0:T(128)S(1)}, u32[]{:S(2)}, u32[]{:S(2)}) collective-permute-start(s32[96]{0:T(128)S(1)} %pad_add_fusion.1), channel_id=1, source_target_pairs={{0,2},{2,0},{1,3},{3,1},{4,6},{6,4},{5,7},{7,5},{8,10},{10,8},{9,1... | collective-permute-start | bytes 1160 | tf_op jit(solution)/shard_map/ppermute | solution.py:119
  37.3 17.8 %collective-permute-start.9 = (bf16[80,2048]{1,0:T(8,128)(2,1)S(1)}, bf16[80,2048]{1,0:T(8,128)(2,1)S(1)}, u32[]{:S(2)}, u32[]{:S(2)}) collective-permute-start(bf16[80,2048]{1,0:T(8,128)(2,1)S(1)} %collective-permute-done.2), channel_id=1, source_target_pairs={{0,4},{4,0},{8,12},{12,8},{1,5},{5,1},{9,13},{13,9},{2,6},{6,2},{1... | collective-permute-start | bytes 983048 | tf_op jit(solution)/shard_map/ppermute | solution.py:119
  40.7 14.4 %collective-permute-start.4 = (bf16[64,2048]{1,0:T(8,128)(2,1)}, bf16[64,2048]{1,0:T(8,128)(2,1)S(1)}, u32[]{:S(2)}, u32[]{:S(2)}) collective-permute-start(bf16[64,2048]{1,0:T(8,128)(2,1)} %get-tuple-element.43), channel_id=1, source_target_pairs={{0,8},{4,12},{8,0},{12,4},{1,9},{5,13},{9,1},{13,5},{2,10},{6,14},... | collective-permute-start | bytes 786440 | tf_op jit(solution)/shard_map/ppermute | solution.py:119
  40.7 18.0 %collective-permute-start.8 = (bf16[80,2048]{1,0:T(8,128)(2,1)S(1)}, bf16[80,2048]{1,0:T(8,128)(2,1)S(1)}, u32[]{:S(2)}, u32[]{:S(2)}) collective-permute-start(bf16[80,2048]{1,0:T(8,128)(2,1)S(1)} %collective-permute-done.2), channel_id=1, source_target_pairs={{0,2},{2,0},{1,3},{3,1},{4,6},{6,4},{5,7},{7,5},{8,10},{10,8},{9,1... | collective-permute-start | bytes 983048 | tf_op jit(solution)/shard_map/ppermute | solution.py:119
  55.1 13.1 %collective-permute-start.10 = (bf16[80,2048]{1,0:T(8,128)(2,1)S(1)}, bf16[80,2048]{1,0:T(8,128)(2,1)}, u32[]{:S(2)}, u32[]{:S(2)}) collective-permute-start(bf16[80,2048]{1,0:T(8,128)(2,1)S(1)} %collective-permute-done.9), channel_id=1, source_target_pairs={{0,2},{2,0},{1,3},{3,1},{4,6},{6,4},{5,7},{7,5},{8,10},{10,8},{9,1... | collective-permute-start | bytes 983048 | tf_op jit(solution)/shard_map/ppermute | solution.py:119
  56.6 11.5 %collective-permute-start.13 = (bf16[64,2048]{1,0:T(8,128)(2,1)S(1)}, bf16[64,2048]{1,0:T(8,128)(2,1)S(1)}, u32[]{:S(2)}, u32[]{:S(2)}) collective-permute-start(bf16[64,2048]{1,0:T(8,128)(2,1)S(1)} %collective-permute-done.4), channel_id=1, source_target_pairs={{0,2},{2,0},{1,3},{3,1},{4,6},{6,4},{5,7},{7,5},{8,10},{10,8},{9,1... | collective-permute-start | bytes 786440 | tf_op jit(solution)/shard_map/ppermute | solution.py:119
  57.2 11.0 %collective-permute-start.14 = (bf16[64,2048]{1,0:T(8,128)(2,1)S(1)}, bf16[64,2048]{1,0:T(8,128)(2,1)S(1)}, u32[]{:S(2)}, u32[]{:S(2)}) collective-permute-start(bf16[64,2048]{1,0:T(8,128)(2,1)S(1)} %collective-permute-done.4), channel_id=1, source_target_pairs={{0,4},{4,0},{8,12},{12,8},{1,5},{5,1},{9,13},{13,9},{2,6},{6,2},{1... | collective-permute-start | bytes 786440 | tf_op jit(solution)/shard_map/ppermute | solution.py:119
  57.7 23.8 %collective-permute-start.7 = (bf16[2,128,2048]{2,1,0:T(8,128)(2,1)}, bf16[2,128,2048]{2,1,0:T(8,128)(2,1)}, u32[]{:S(2)}, u32[]{:S(2)}) collective-permute-start(bf16[2,128,2048]{2,1,0:T(8,128)(2,1)} %collective-permute-done.6.refs_2_), channel_id=1, source_target_pairs={{0,1},{1,0},{2,3},{3,2},{4,5},{5,4},{6,7},{7,6},{8,9},{9,8},{10,11... | collective-permute-start | bytes 3145736 | tf_op jit(solution)/shard_map/ppermute | solution.py:119
  58.8 20.2 %collective-permute-start.5 = (bf16[8,3,128,128]{3,2,1,0:T(8,128)(2,1)}, bf16[8,3,128,128]{3,2,1,0:T(8,128)(2,1)S(1)}, u32[]{:S(2)}, u32[]{:S(2)}) collective-permute-start(bf16[8,3,128,128]{3,2,1,0:T(8,128)(2,1)} %slice.15), channel_id=1, source_target_pairs={{0,1},{1,0},{2,3},{3,2},{4,5},{5,4},{6,7},{7,6},{8,9},{9,8},{10,11... | collective-permute-start | bytes 2359304 | tf_op jit(solution)/shard_map/ppermute | solution.py:119
  68.1 13.4 %collective-permute-start.11 = (bf16[3,80,2048]{2,1,0:T(8,128)(2,1)}, bf16[3,80,2048]{2,1,0:T(8,128)(2,1)}, u32[]{:S(2)}, u32[]{:S(2)}) collective-permute-start(bf16[3,80,2048]{2,1,0:T(8,128)(2,1)} %pad_maximum_fusion), channel_id=1, source_target_pairs={{0,1},{1,0},{2,3},{3,2},{4,5},{5,4},{6,7},{7,6},{8,9},{9,8},{10,11... | collective-permute-start | bytes 2949128 | tf_op jit(solution)/shard_map/ppermute | solution.py:119
  70.7 10.8 %collective-permute-start.16 = (bf16[3,64,2048]{2,1,0:T(8,128)(2,1)}, bf16[3,64,2048]{2,1,0:T(8,128)(2,1)}, u32[]{:S(2)}, u32[]{:S(2)}) collective-permute-start(bf16[3,64,2048]{2,1,0:T(8,128)(2,1)} %pad_maximum_fusion.1), channel_id=1, source_target_pairs={{0,1},{1,0},{2,3},{3,2},{4,5},{5,4},{6,7},{7,6},{8,9},{9,8},{10,11... | collective-permute-start | bytes 2359304 | tf_op jit(solution)/shard_map/ppermute | solution.py:119
  79.0 26.5 %collective-permute-start.18 = (bf16[128,2048]{1,0:T(8,128)(2,1)S(1)}, bf16[128,2048]{1,0:T(8,128)(2,1)S(1)}, u32[]{:S(2)}, u32[]{:S(2)}) collective-permute-start(bf16[128,2048]{1,0:T(8,128)(2,1)S(1)} %dynamic-slice_bitcast_fusion), channel_id=1, source_target_pairs={{0,8},{4,12},{8,0},{12,4},{1,9},{5,13},{9,1},{13,5},{2,10},{6,14},... | collective-permute-start | bytes 1572872 | tf_op jit(solution)/shard_map/ppermute | solution.py:119
  125.9 12.6 %collective-permute-start.27 = (bf16[128,2048]{1,0:T(8,128)(2,1)}, bf16[128,2048]{1,0:T(8,128)(2,1)S(1)}, u32[]{:S(2)}, u32[]{:S(2)}) collective-permute-start(bf16[128,2048]{1,0:T(8,128)(2,1)} %get-tuple-element.58.refs_0_), channel_id=1, source_target_pairs={{0,4},{4,0},{8,12},{12,8},{1,5},{5,1},{9,13},{13,9},{2,6},{6,2},{1... | collective-permute-start | bytes 1572872 | tf_op jit(solution)/shard_map/ppermute | solution.py:119
  126.5 12.2 %collective-permute-start.28 = (bf16[128,2048]{1,0:T(8,128)(2,1)}, bf16[128,2048]{1,0:T(8,128)(2,1)S(1)}, u32[]{:S(2)}, u32[]{:S(2)}) collective-permute-start(bf16[128,2048]{1,0:T(8,128)(2,1)} %get-tuple-element.59), channel_id=1, source_target_pairs={{0,2},{2,0},{1,3},{3,1},{4,6},{6,4},{5,7},{7,5},{8,10},{10,8},{9,1... | collective-permute-start | bytes 1572872 | tf_op jit(solution)/shard_map/ppermute | solution.py:119
  128.0 14.2 %collective-permute-start.31 = (bf16[128,2048]{1,0:T(8,128)(2,1)}, bf16[128,2048]{1,0:T(8,128)(2,1)S(1)}, u32[]{:S(2)}, u32[]{:S(2)}) collective-permute-start(bf16[128,2048]{1,0:T(8,128)(2,1)} %get-tuple-element.58.refs_0_), channel_id=1, source_target_pairs={{0,1},{1,0},{2,3},{3,2},{4,5},{5,4},{6,7},{7,6},{8,9},{9,8},{10,11... | collective-permute-start | bytes 1572872 | tf_op jit(solution)/shard_map/ppermute | solution.py:119
  128.0 14.8 %collective-permute-start.32 = (bf16[128,2048]{1,0:T(8,128)(2,1)}, bf16[128,2048]{1,0:T(8,128)(2,1)S(1)}, u32[]{:S(2)}, u32[]{:S(2)}) collective-permute-start(bf16[128,2048]{1,0:T(8,128)(2,1)} %get-tuple-element.59), channel_id=1, source_target_pairs={{0,1},{1,0},{2,3},{3,2},{4,5},{5,4},{6,7},{7,6},{8,9},{9,8},{10,11... | collective-permute-start | bytes 1572872 | tf_op jit(solution)/shard_map/ppermute | solution.py:119
  138.7 14.9 %collective-permute-start.39 = (bf16[128,2048]{1,0:T(8,128)(2,1)S(1)}, bf16[128,2048]{1,0:T(8,128)(2,1)S(1)}, u32[]{:S(2)}, u32[]{:S(2)}) collective-permute-start(bf16[128,2048]{1,0:T(8,128)(2,1)S(1)} %collective-permute-done.28), channel_id=1, source_target_pairs={{0,4},{4,0},{8,12},{12,8},{1,5},{5,1},{9,13},{13,9},{2,6},{6,2},{1... | collective-permute-start | bytes 1572872 | tf_op jit(solution)/shard_map/ppermute | solution.py:119
  140.2 14.9 %collective-permute-start.38 = (bf16[128,2048]{1,0:T(8,128)(2,1)S(1)}, bf16[128,2048]{1,0:T(8,128)(2,1)S(1)}, u32[]{:S(2)}, u32[]{:S(2)}) collective-permute-start(bf16[128,2048]{1,0:T(8,128)(2,1)S(1)} %collective-permute-done.27), channel_id=1, source_target_pairs={{0,2},{2,0},{1,3},{3,1},{4,6},{6,4},{5,7},{7,5},{8,10},{10,8},{9,1... | collective-permute-start | bytes 1572872 | tf_op jit(solution)/shard_map/ppermute | solution.py:119
  141.6 19.5 %collective-permute-start.33 = (bf16[128,2048]{1,0:T(8,128)(2,1)}, bf16[128,2048]{1,0:T(8,128)(2,1)S(1)}, u32[]{:S(2)}, u32[]{:S(2)}) collective-permute-start(bf16[128,2048]{1,0:T(8,128)(2,1)} %get-tuple-element.59), channel_id=1, source_target_pairs={{0,4},{4,0},{8,12},{12,8},{1,5},{5,1},{9,13},{13,9},{2,6},{6,2},{1... | collective-permute-start | bytes 1572872 | tf_op jit(solution)/shard_map/ppermute | solution.py:119
  142.3 20.0 %collective-permute-start.29 = (bf16[128,2048]{1,0:T(8,128)(2,1)}, bf16[128,2048]{1,0:T(8,128)(2,1)S(1)}, u32[]{:S(2)}, u32[]{:S(2)}) collective-permute-start(bf16[128,2048]{1,0:T(8,128)(2,1)} %get-tuple-element.58.refs_0_), channel_id=1, source_target_pairs={{0,2},{2,0},{1,3},{3,1},{4,6},{6,4},{5,7},{7,5},{8,10},{10,8},{9,1... | collective-permute-start | bytes 1572872 | tf_op jit(solution)/shard_map/ppermute | solution.py:119
  142.8 19.5 %collective-permute-start.34 = (bf16[128,2048]{1,0:T(8,128)(2,1)S(1)}, bf16[128,2048]{1,0:T(8,128)(2,1)S(1)}, u32[]{:S(2)}, u32[]{:S(2)}) collective-permute-start(bf16[128,2048]{1,0:T(8,128)(2,1)S(1)} %collective-permute-done.27), channel_id=1, source_target_pairs={{0,1},{1,0},{2,3},{3,2},{4,5},{5,4},{6,7},{7,6},{8,9},{9,8},{10,11... | collective-permute-start | bytes 1572872 | tf_op jit(solution)/shard_map/ppermute | solution.py:119
  153.6 9.2 %collective-permute-start.37 = (bf16[128,2048]{1,0:T(8,128)(2,1)S(1)}, bf16[128,2048]{1,0:T(8,128)(2,1)S(1)}, u32[]{:S(2)}, u32[]{:S(2)}) collective-permute-start(bf16[128,2048]{1,0:T(8,128)(2,1)S(1)} %collective-permute-done.28), channel_id=1, source_target_pairs={{0,1},{1,0},{2,3},{3,2},{4,5},{5,4},{6,7},{7,6},{8,9},{9,8},{10,11... | collective-permute-start | bytes 1572872 | tf_op jit(solution)/shard_map/ppermute | solution.py:119
  155.0 8.9 %collective-permute-start.41 = (bf16[128,2048]{1,0:T(8,128)(2,1)S(1)}, bf16[128,2048]{1,0:T(8,128)(2,1)S(1)}, u32[]{:S(2)}, u32[]{:S(2)}) collective-permute-start(bf16[128,2048]{1,0:T(8,128)(2,1)S(1)} %collective-permute-done.39), channel_id=1, source_target_pairs={{0,1},{1,0},{2,3},{3,2},{4,5},{5,4},{6,7},{7,6},{8,9},{9,8},{10,11... | collective-permute-start | bytes 1572872 | tf_op jit(solution)/shard_map/ppermute | solution.py:119
  162.8 32.1 %collective-permute-start.30 = (bf16[128,2048]{1,0:T(8,128)(2,1)}, bf16[128,2048]{1,0:T(8,128)(2,1)S(1)}, u32[]{:S(2)}, u32[]{:S(2)}) collective-permute-start(bf16[128,2048]{1,0:T(8,128)(2,1)} %get-tuple-element.59), channel_id=1, source_target_pairs={{0,8},{4,12},{8,0},{12,4},{1,9},{5,13},{9,1},{13,5},{2,10},{6,14},... | collective-permute-start | bytes 1572872 | tf_op jit(solution)/shard_map/ppermute | solution.py:119
  182.1 14.2 %collective-permute-start.42 = (bf16[128,2048]{1,0:T(8,128)(2,1)}, bf16[128,2048]{1,0:T(8,128)(2,1)S(1)}, u32[]{:S(2)}, u32[]{:S(2)}) collective-permute-start(bf16[128,2048]{1,0:T(8,128)(2,1)} %get-tuple-element.62.refs_0_), channel_id=1, source_target_pairs={{0,2},{2,0},{1,3},{3,1},{4,6},{6,4},{5,7},{7,5},{8,10},{10,8},{9,1... | collective-permute-start | bytes 1572872 | tf_op jit(solution)/shard_map/ppermute | solution.py:119
  183.6 25.0 %collective-permute-start.44 = (bf16[64,2048]{1,0:T(8,128)(2,1)}, bf16[64,2048]{1,0:T(8,128)(2,1)S(1)}, u32[]{:S(2)}, u32[]{:S(2)}) collective-permute-start(bf16[64,2048]{1,0:T(8,128)(2,1)} %get-tuple-element.65), channel_id=1, source_target_pairs={{0,8},{4,12},{8,0},{12,4},{1,9},{5,13},{9,1},{13,5},{2,10},{6,14},... | collective-permute-start | bytes 786440 | tf_op jit(solution)/shard_map/ppermute | solution.py:119
  196.3 26.2 %collective-permute-start.43 = (bf16[128,2048]{1,0:T(8,128)(2,1)S(1)}, bf16[128,2048]{1,0:T(8,128)(2,1)S(1)}, u32[]{:S(2)}, u32[]{:S(2)}) collective-permute-start(bf16[128,2048]{1,0:T(8,128)(2,1)S(1)} %collective-permute-done.30.refs_2_), channel_id=1, source_target_pairs={{0,2},{2,0},{1,3},{3,1},{4,6},{6,4},{5,7},{7,5},{8,10},{10,8},{9,1... | collective-permute-start | bytes 1572872 | tf_op jit(solution)/shard_map/ppermute | solution.py:119
  210.0 12.5 %collective-permute-start.45 = (bf16[64,2048]{1,0:T(8,128)(2,1)}, bf16[64,2048]{1,0:T(8,128)(2,1)S(1)}, u32[]{:S(2)}, u32[]{:S(2)}) collective-permute-start(bf16[64,2048]{1,0:T(8,128)(2,1)} %get-tuple-element.66), channel_id=1, source_target_pairs={{0,8},{4,12},{8,0},{12,4},{1,9},{5,13},{9,1},{13,5},{2,10},{6,14},... | collective-permute-start | bytes 786440 | tf_op jit(solution)/shard_map/ppermute | solution.py:119
  (66 other events, 515.8 us)

commit v5 on v4

--- a/solution.py
+++ b/solution.py
@@ -156,7 +156,8 @@
     field, images, right, left, diag, parts, sems = refs
     z, x, c = place()
     sectors, block, width = field.shape
-    links = right.shape[2]
+    table = right.shape[1]
+    links = table // sectors
     mine = 4 * z + 2 * c + x
     rows = (mine, mine ^ 8)
 
@@ -167,9 +168,9 @@
         copy.start()
         copies.append(copy)
 
-    part = sectors // 2
+    part = table // 2
     near, far = pl.ds(c * part, part), pl.ds((1 - c) * part, part)
-    begin(right_own.at[0], right.at[0])
+    begin(right_own, right.at[0])
     for piece, offsets in zip(pieces, plan):
         for at, (dz, dx, dc, start, tall) in enumerate(offsets):
             target = field.at[row_of(dz, dx, dc), pl.ds(start, tall)]
@@ -180,15 +181,13 @@
     begin(right_far, right.at[1, far])
     early = len(copies)
     for at in range(2):
-        begin(left_own.at[0, rows[at]], left.at[0, at])
-    begin(right_near.at[pl.ds(part, 2)], left.at[1])
+        begin(left_own.at[pl.ds(rows[at] * links, links)], left.at[0, pl.ds(at * links, links)])
+    begin(right_near.at[pl.ds(part, 2 * links)], left.at[1])
     if not first:
         begin(hd_own.at[x], diag.at[0])
         begin(hd_far, diag.at[1])
     for copy in copies[:early]:
         copy.wait()
-
-    table = sectors * links
 
     def right_col(term, b, j):
         return cols[(2 * term) * table + b * links + j]
@@ -213,7 +212,7 @@
                     value = field[source, :, pl.ds(pl.multiple_of(col * block, block), block)]
                     line.append(allowed(source, col, value) if first else value)
                 lhs.append(jnp.concatenate(line, axis=1))
-            rhs = [right[term, b, j] for j in range(links)]
+            rhs = [right[term, b * links + j] for j in range(links)]
             product = lax.dot_general(
                 jnp.concatenate(lhs, axis=0),
                 jnp.concatenate(rhs, axis=1),
@@ -246,7 +245,7 @@
             return jnp.concatenate(parts, axis=1)
 
         for at in range(2):
-            weights = [left[term, at, j] for term in range(2) for j in range(links)]
+            weights = [left[term, at * links + j] for term in range(2) for j in range(links)]
             total = jnp.dot(
                 jnp.concatenate(weights, axis=1),
                 images[at, :, span],
@@ -289,8 +288,10 @@
 
 def operate(first, plan, pieces, cols, pattern, right, left, extra):
     right_own, right_near, right_far = right
-    _, sectors, links, block = right_own.shape[:4]
-    width = sectors * block
+    table, block, _ = right_own.shape
+    width = pieces[0].shape[2]
+    sectors = width // block
+    links = table // sectors
     rows = jax.ShapeDtypeStruct((2, block, width), jnp.bfloat16)
     one = jax.ShapeDtypeStruct((block, width), jnp.bfloat16)
     some = jax.ShapeDtypeStruct((block // 2, width), jnp.bfloat16)
@@ -308,56 +309,65 @@
         scratch_shapes=[
             pltpu.VMEM((sectors, block, width), jnp.bfloat16),
             pltpu.VMEM((2, 2 * links * block, width), jnp.bfloat16),
-            pltpu.VMEM((2, sectors, links, block, block), jnp.bfloat16),
-            pltpu.VMEM((2, 2, links, block, block), jnp.bfloat16),
+            pltpu.VMEM((2, table, block, block), jnp.bfloat16),
+            pltpu.VMEM((2, 2 * links, block, block), jnp.bfloat16),
             pltpu.VMEM((2, block, width), jnp.bfloat16),
             pltpu.VMEM((16, 3 * LANES), jnp.bfloat16),
             pltpu.SemaphoreType.DMA((copies,)),
         ],
         compiler_params=pltpu.CompilerParams(vmem_limit_bytes=VMEM_LIMIT),
         cost_estimate=pl.CostEstimate(
-            flops=inner + outer, bytes_accessed=16 * 1024 * 1024, transcendentals=0
+            flops=inner + outer if first else 0,
+            bytes_accessed=16 * 1024 * 1024 if first else 1024,
+            transcendentals=0,
         ),
         name="operate_first" if first else "operate_second",
     )(cols, pattern, right_own, right_near, right_far, left, *pieces, *extra)
 
 
-def prepare_kernel(theta, right, left, first, own, packed, sems):
+def prepare_kernel(theta, right, left, cols, after_this, own_a, own_b, packed, sems):
     z, x, c = place()
     half = z // 2
     mine = 4 * z + 2 * c + x
-    part = right.shape[1] // 2
-    tall = first.shape[0]
+    block, width = own_a.shape
+    links = right.shape[0] * block // width
+    part = right.shape[0] // 2
+    sources = (
+        (theta.at[half, 0], own_a),
+        (theta.at[half, 1], own_b),
+        (right.at[pl.ds(c * part, part)], packed.at[pl.ds(0, part)]),
+        (left.at[pl.ds((mine ^ 1) * links, links)], packed.at[pl.ds(part, links)]),
+        (left.at[pl.ds((mine ^ 9) * links, links)], packed.at[pl.ds(part + links, links)]),
+    )
     copies = [
-        pltpu.make_async_copy(theta.at[1 - half, x, pl.ds(0, tall)], first, sems.at[0]),
-        pltpu.make_async_copy(theta.at[half], own, sems.at[1]),
-        pltpu.make_async_copy(right.at[0, pl.ds(c * part, part)], packed.at[pl.ds(0, part)], sems.at[2]),
-        pltpu.make_async_copy(left.at[0, mine ^ 1], packed.at[part], sems.at[3]),
-        pltpu.make_async_copy(left.at[0, mine ^ 9], packed.at[part + 1], sems.at[4]),
+        pltpu.make_async_copy(source, target, sems.at[at])
+        for at, (source, target) in enumerate(sources)
     ]
     for copy in copies:
         copy.start()
+    last = part + 2 * links
+    packed[last] = jnp.zeros_like(packed[last])
+    packed[last, 0 : cols.shape[0], :] = cols[...]
     for copy in copies:
         copy.wait()
 
 
-def prepare(tall, theta, right, left):
+def prepare(theta, right, left, cols, after_this):
     _, _, block, width = theta.shape
-    _, sectors, links = right.shape[:3]
-    kind = jnp.bfloat16
+    table = right.shape[0]
+    links = table * block // width
+    one = jax.ShapeDtypeStruct((block, width), jnp.bfloat16)
+    packed = jax.ShapeDtypeStruct((table // 2 + 2 * links + 1, block, block), jnp.bfloat16)
     return pl.pallas_call(
         prepare_kernel,
-        out_shape=(
-            jax.ShapeDtypeStruct((tall, width), kind),
-            jax.ShapeDtypeStruct((2, block, width), kind),
-            jax.ShapeDtypeStruct((sectors // 2 + 2, links, block, block), kind),
-        ),
-        in_specs=[ANY] * 3,
+        out_shape=(one, one, packed),
+        in_specs=[ANY, ANY, ANY, VMEM, ANY],
         out_specs=(VMEM,) * 3,
         scratch_shapes=[pltpu.SemaphoreType.DMA((5,))],
+        cost_estimate=pl.CostEstimate(flops=0, bytes_accessed=64 * 1024 * 1024, transcendentals=0),
         compiler_params=pltpu.CompilerParams(vmem_limit_bytes=VMEM_LIMIT),
         name="prepare",
-    )(theta, right, left)
+    )(theta, right, left, cols, after_this)
 
 
 def weigh_kernel(pattern, theta, hd, own_out, second, waves, diag, sems):
@@ -418,7 +428,6 @@
             pltpu.VMEM((block, width), hd.dtype),
             pltpu.SemaphoreType.DMA((4,)),
         ],
-        cost_estimate=pl.CostEstimate(flops=0, bytes_accessed=64 * 1024 * 1024, transcendentals=0),
         compiler_params=pltpu.CompilerParams(vmem_limit_bytes=VMEM_LIMIT),
         name="weigh",
     )(pattern, theta, hd)
@@ -479,9 +488,9 @@
     stats_out[4:5, :] = jnp.broadcast_to(norm_sq, (1, LANES))
 
 
-def correct_kernel(psi, t, *refs):
-    stats, outs = refs[:4], refs[4:]
-    stats = [ref.at[at] for ref in stats for at in range(2)]
+def correct_kernel(psi, t, found, *outs):
+    z, x, c = place()
+    stats = [found.at[8 * (z // 2) + at] for at in range(8)]
     norm_sq = stats[0][4:5, 0:1]
     factor = sum(ref[0:1, 0:1] for ref in stats) / (norm_sq + 1e-06)
     length_sq = jnp.zeros((1, 1), jnp.float32)
@@ -551,77 +560,69 @@
     tall = block * 5 // 8
     rest = block - tall
 
-    first, own, packed = prepare(tall, halves, right_blocks, left_blocks)
+    right = right_blocks.reshape(-1, block, block)
+    left = left_blocks.reshape(-1, block, block)
+    table = right.shape[0]
+    cols = jnp.concatenate([right_cols.reshape(-1), left_cols.reshape(-1)])
+
+    first = lax.dynamic_slice(halves, (1 - half, x, 0, 0), (1, 1, tall, width))[0, 0]
     far_a = across(first, "blk", 2)
-    near = across(own, "blk", 1)
-    cols = jnp.concatenate([right_cols.reshape(-1), left_cols.reshape(-1)])
-    cols_other = across(cols, "ops", 1)
-    cols = jnp.concatenate([cols, cols_other])
+    weight_own, second = weigh(rest, allowed, halves, diag)
+    far_b = across(second, "blk", 2)
+    spots = jnp.pad(cols, (0, 16 * LANES - cols.shape[0])).reshape(16, LANES).astype(jnp.bfloat16)
+    own_a, own_b, packed = prepare(halves, right, left, spots, weight_own)
     operators = across(packed, "ops", 1)
-    own_core = across(own, "sub", 1)
-    weight_own, second = weigh(rest, allowed, halves, diag)
-
-    far_a, second = after((far_a, second), cols, own_core)
-    far_b = across(after(second, far_a), "blk", 2)
+    own_core_a = across(own_a, "sub", 1)
+    own_core_b = across(own_b, "sub", 1)
+
+    far_a = after(far_a, own_core_a, own_core_b)
     far_za = across(far_a, "blk", 1)
     far_xa = across(far_a, "ops", 1)
 
-    far_zb = across(after(far_b, far_za), "blk", 1)
-    far_zxa = across(after(far_za, far_b), "ops", 1)
+    far_zb = across(far_b, "blk", 1)
     far_xb = across(far_b, "ops", 1)
-    operators_core = across(after(operators, far_b)[: sectors // 2], "sub", 1)
-    near_core = across(after(near, far_b), "sub", 1)
-    core_a = across(jnp.stack([far_a, far_xa, far_za]), "sub", 1)
-
-    far_zxb = across(after(far_zb, far_xb, far_zxa), "ops", 1)
-    core_b = across(jnp.stack([far_b, far_xb, far_zb]), "sub", 1)
-    far_zxa_core = across(far_zxa, "sub", 1)
-    far_zxb_core = across(far_zxb, "sub", 1)
+    far_zxa = across(far_za, "ops", 1)
+    near_a = across(after(own_a, far_za, far_b), "blk", 1)
+    near_b = across(after(own_b, far_za, far_b), "blk", 1)
+    operators_core = across(after(operators, far_b)[: table // 2], "sub", 1)
+    found = operators[-1].reshape(-1)[: cols.shape[0]].astype(jnp.int32)
+    cols = jnp.concatenate([cols, found])
+
+    far_zxb = across(after(far_zb, far_za), "ops", 1)
     hd_far = lax.dynamic_index_in_dim(diag, x, 0, keepdims=False)
     hd_far = across(after(hd_far, far_zb), "blk", 2)
-
-    right = (right_blocks, operators, operators_core)
+    core_a = across(jnp.stack([far_a, far_xa, far_za, far_zxa]), "sub", 1)
+    near_a_core = across(near_a, "sub", 1)
+    core_b = across(jnp.stack([far_b, far_xb, far_zb, far_zxb]), "sub", 1)
+    near_b_core = across(near_b, "sub", 1)
+
+    operators = (right, operators, operators_core)
     pieces = []
     plan = []
-    for piece, offsets in (
-        (own, ((0, 2, 0), (0, 3, 0))),
-        (own_core, ((0, 2, 1), (0, 3, 1))),
-        (near, ((1, 2, 0), (1, 3, 0))),
-        (near_core, ((1, 2, 1), (1, 3, 1))),
+    for piece, offset in (
+        (own_a, (0, 2, 0)),
+        (own_b, (0, 3, 0)),
+        (own_core_a, (0, 2, 1)),
+        (own_core_b, (0, 3, 1)),
+        (near_a, (1, 2, 0)),
+        (near_b, (1, 3, 0)),
+        (near_a_core, (1, 2, 1)),
+        (near_b_core, (1, 3, 1)),
     ):
-        pieces.append(piece)
-        plan.append(tuple(offset + (0, block) for offset in offsets))
-    for start, count, group in (
-        (
-            0,
-            tall,
-            (
-                (far_a, ((2, 0, 0),)),
-                (far_xa, ((2, 1, 0),)),
-                (far_za, ((3, 0, 0),)),
-                (far_zxa, ((3, 1, 0),)),
-                (core_a, ((2, 0, 1), (2, 1, 1), (3, 0, 1))),
-                (far_zxa_core, ((3, 1, 1),)),
-            ),
-        ),
-        (
-            tall,
-            rest,
-            (
-                (far_b, ((2, 0, 0),)),
-                (far_xb, ((2, 1, 0),)),
-                (far_zb, ((3, 0, 0),)),
-                (far_zxb, ((3, 1, 0),)),
-                (core_b, ((2, 0, 1), (2, 1, 1), (3, 0, 1))),
-                (far_zxb_core, ((3, 1, 1),)),
-            ),
-        ),
+        pieces.append(piece[None])
+        plan.append((offset + (0, block),))
+    crossed = ((2, 0), (2, 1), (3, 0), (3, 1))
+    for start, count, group, core in (
+        (0, tall, (far_a, far_xa, far_za, far_zxa), core_a),
+        (tall, rest, (far_b, far_xb, far_zb, far_zxb), core_b),
     ):
-        for piece, offsets in group:
-            pieces.append(piece if piece.ndim == 3 else piece[None])
-            plan.append(tuple(offset + (start, count) for offset in offsets))
+        for piece, offset in zip(group, crossed):
+            pieces.append(piece[None])
+            plan.append((offset + (0, start, count),))
+        pieces.append(core)
+        plan.append(tuple(offset + (1, start, count) for offset in crossed))
     psi, off_one, stats_one = operate(
-        True, tuple(plan), pieces, cols, allowed, right, left_blocks, (weight_own,)
+        True, tuple(plan), pieces, cols, allowed, operators, left, (weight_own,)
     )
 
     found = share(stats_one)
@@ -640,16 +641,16 @@
         compiler_params=pltpu.CompilerParams(vmem_limit_bytes=VMEM_LIMIT),
         name="update",
     )(psi, off_one, diag, hd_far, *found)
-    found = share(stats_two)
+    found = lax.all_gather(stats_two, ("blk", "ops", "sub"))
     one = jax.ShapeDtypeStruct((block, width), jnp.bfloat16)
     changed_near, changed_far = pl.pallas_call(
         correct_kernel,
         out_shape=(one, one),
-        in_specs=[VMEM, VMEM] + [VMEM] * 4,
+        in_specs=[VMEM, VMEM, VMEM],
         out_specs=(VMEM, VMEM),
         compiler_params=pltpu.CompilerParams(vmem_limit_bytes=VMEM_LIMIT),
         name="correct",
-    )(psi, t, *found)
+    )(psi, t, found)
 
     near_z = across(changed_near, "blk", 1)
     far_x = across(changed_far, "ops", 1)
@@ -688,7 +689,7 @@
         pieces.append(piece[None])
         plan.append((offset + (0, block),))
     two_near, two_far, two_late, stats_three = operate(
-        False, tuple(plan), pieces, cols, allowed, right, left_blocks, (diag, hd_far, psi, off_one, stats_one)
+        False, tuple(plan), pieces, cols, allowed, operators, left, (diag, hd_far, psi, off_one, stats_one)
     )
 
     far_in = across(two_far, "blk", 2)

time: 233 us -> 263 us (1.13)
  blocking collectives: 0 us -> 20.9 us
  waiting for transfers between devices: 119 us -> 133 us
  starting transfers between devices: 46.3 us -> 37.4 us
  local copies, waits for them, and re-layouts: 5.45 us -> 9.5 us
    all_gather x0 -> x1, blocking collectives: none -> 20.9 us  [shards(): found = lax.all_gather(stats_two, ('blk', 'ops', 'sub'))]
    ppermute x46 -> x45, waiting for transfers between devices: 115 us -> 131 us  [across(): return lax.ppermute(value, axis, [(i, i ^ distance) for i in range(size)])]
    ppermute x46 -> x45, starting transfers between devices: 39.3 us -> 33.9 us  [across(): return lax.ppermute(value, axis, [(i, i ^ distance) for i in range(size)])]
    ppermute x6 -> x3, starting transfers between devices: 6.98 us -> 3.49 us  [share(): lax.ppermute(pair, axes, [(i, i ^ distance) for i in range(count)])]
    unnamed x94 -> x96, local copies, waits for them, and re-layouts: 3.53 us -> 6.87 us
  transfers between devices with their start and end apart: 52 -> 48, of which waited for: 31 -> 29; matrix products, arithmetic and copies ran while one was open for 3% -> 2% of each run, Pallas kernels for 18% -> 14%
where the time goes in v5:
time: 263 us; the launch traced here: 262 us
  waiting for transfers between devices  133 us (51%)
  Pallas kernels  55.7 us (21%)
  starting transfers between devices  37.4 us (14%)
  blocking collectives  20.9 us (8%)
  local copies, waits for them, and re-layouts  9.5 us (4%)
  other arithmetic  3.95 us (2%)
    ppermute x45, waiting for transfers between devices, across(): return lax.ppermute(value, axis, [(i, i ^ distance) for i in range(size)])  131 us
    ppermute x45, starting transfers between devices, across(): return lax.ppermute(value, axis, [(i, i ^ distance) for i in range(size)])  33.9 us
    pallas_call x2, Pallas kernels, operate(): pl.pallas_call(functools.partial(operate_kernel, first, plan), out_shape=...  32.1 us
    all_gather x1, blocking collectives, shards(): found = lax.all_gather(stats_two, ('blk', 'ops', 'sub'))  20.9 us
    pallas_call x3, Pallas kernels, assemble(): pl.pallas_call(functools.partial(assemble_kernel, places, len(based)), ou...  7.21 us
    unnamed x96, local copies, waits for them, and re-layouts  6.87 us
    pallas_call x1, Pallas kernels, shards(): pl.pallas_call(update_kernel, out_shape=(jax.ShapeDtypeStruct((2, block,...  5.92 us
  transfers between devices with their start and end apart: 48, of which 29 were waited for; matrix products, arithmetic and copies ran while one was open for 2% of the time, Pallas kernels for 14%

profile of v5, /device:TPU:0, one launch (start us, length us, event | category | flops | bytes accessed | tf_op | source)
XLA Modules:
  0.0 261.9 jit_solution(15287969126844983355)
XLA Ops:
  4.4 3.4 %weigh.1 = (f32[8,128]{1,0:T(8,128)}, bf16[64,2048]{1,0:T(8,128)(2,1)}) custom-call(s32[256]{0:T(256)} %reshape.40.pattern, bf16[2,2,128,2048]{3,2,1,0:T(8,128)(2,1)} %bitcast.62, bf16[2,128,2048]{2,1,0:T(8,128)(2,1)} %bitcast.58), custom_call_target="tpu_custom_call" | custom-call | tf_op jit(solution)/shard_map/weigh/pallas_call | solution.py:418
  7.8 3.5 %prepare.1 = (bf16[128,2048]{1,0:T(8,128)(2,1)}, bf16[128,2048]{1,0:T(8,128)(2,1)}, bf16[31,128,128]{2,1,0:T(8,128)(2,1)}) custom-call(bf16[2,2,128,2048]{3,2,1,0:T(8,128)(2,1)} %bitcast.63, bf16[48,128,128]{2,1,0:T(8,128)(2,1)} %bitcast.52, bf16[48,128,128]{2,1,0:T(8,128)(2,1)} %bitcast.55, bf16[16,128]{1,0:T(8,128)(2,1)} %fusion.4.cols, ...), custom_call_target="tpu_custom_call" | custom-call | bytes 67108864 | tf_op jit(solution)/shard_map/prepare/pallas_call | solution.py:361
  13.0 4.1 %collective-permute-start.5 = (bf16[80,2048]{1,0:T(8,128)(2,1)S(1)}, bf16[80,2048]{1,0:T(8,128)(2,1)S(1)}, u32[]{:S(2)}, u32[]{:S(2)}) collective-permute-start(bf16[80,2048]{1,0:T(8,128)(2,1)S(1)} %dynamic-slice_bitcast_fusion.1), channel_id=1, source_target_pairs={{0,8},{4,12},{8,0},{12,4},{1,9},{5,13},{9,1},{13,5},{2,10},{6,14},... | collective-permute-start | bytes 983048 | tf_op jit(solution)/shard_map/ppermute | solution.py:119
  17.1 15.0 %collective-permute-done.5 = bf16[80,2048]{1,0:T(8,128)(2,1)S(1)} collective-permute-done((bf16[80,2048]{1,0:T(8,128)(2,1)S(1)}, bf16[80,2048]{1,0:T(8,128)(2,1)S(1)}, u32[]{:S(2)}, u32[]{:S(2)}) %collective-permute-start.5) | collective-permute-done | bytes 327712 | tf_op jit(solution)/shard_map/ppermute | solution.py:119
  32.9 3.4 %collective-permute-start.1 = (bf16[64,2048]{1,0:T(8,128)(2,1)S(1)}, bf16[64,2048]{1,0:T(8,128)(2,1)S(1)}, u32[]{:S(2)}, u32[]{:S(2)}) collective-permute-start(bf16[64,2048]{1,0:T(8,128)(2,1)S(1)} %copy-done.46), channel_id=1, source_target_pairs={{0,8},{4,12},{8,0},{12,4},{1,9},{5,13},{9,1},{13,5},{2,10},{6,14},... | collective-permute-start | bytes 786440 | tf_op jit(solution)/shard_map/ppermute | solution.py:119
  38.3 8.7 %collective-permute-done.6 = bf16[80,2048]{1,0:T(8,128)(2,1)S(1)} collective-permute-done((bf16[80,2048]{1,0:T(8,128)(2,1)S(1)}, bf16[80,2048]{1,0:T(8,128)(2,1)S(1)}, u32[]{:S(2)}, u32[]{:S(2)}) %collective-permute-start.6) | collective-permute-done | bytes 327712 | tf_op jit(solution)/shard_map/ppermute | solution.py:119
  51.2 4.5 %collective-permute-done.15 = bf16[64,2048]{1,0:T(8,128)(2,1)S(1)} collective-permute-done((bf16[64,2048]{1,0:T(8,128)(2,1)S(1)}, bf16[64,2048]{1,0:T(8,128)(2,1)S(1)}, u32[]{:S(2)}, u32[]{:S(2)}) %collective-permute-start.15) | collective-permute-done | bytes 262176 | tf_op jit(solution)/shard_map/ppermute | solution.py:119
  57.2 11.6 %collective-permute-done.11 = bf16[80,2048]{1,0:T(8,128)(2,1)S(1)} collective-permute-done((bf16[80,2048]{1,0:T(8,128)(2,1)S(1)}, bf16[80,2048]{1,0:T(8,128)(2,1)S(1)}, u32[]{:S(2)}, u32[]{:S(2)}) %collective-permute-start.11) | collective-permute-done | bytes 327712 | tf_op jit(solution)/shard_map/ppermute | solution.py:119
  69.6 6.3 %collective-permute-done.12 = bf16[80,2048]{1,0:T(8,128)(2,1)S(1)} collective-permute-done((bf16[80,2048]{1,0:T(8,128)(2,1)S(1)}, bf16[80,2048]{1,0:T(8,128)(2,1)S(1)}, u32[]{:S(2)}, u32[]{:S(2)}) %collective-permute-start.12) | collective-permute-done | bytes 327712 | tf_op jit(solution)/shard_map/ppermute | solution.py:119
  76.6 4.9 %collective-permute-done.14 = bf16[64,2048]{1,0:T(8,128)(2,1)S(1)} collective-permute-done((bf16[64,2048]{1,0:T(8,128)(2,1)S(1)}, bf16[64,2048]{1,0:T(8,128)(2,1)S(1)}, u32[]{:S(2)}, u32[]{:S(2)}) %collective-permute-start.14) | collective-permute-done | bytes 262176 | tf_op jit(solution)/shard_map/ppermute | solution.py:119
  82.2 3.3 %collective-permute-done.16 = bf16[64,2048]{1,0:T(8,128)(2,1)S(1)} collective-permute-done((bf16[64,2048]{1,0:T(8,128)(2,1)S(1)}, bf16[64,2048]{1,0:T(8,128)(2,1)S(1)}, u32[]{:S(2)}, u32[]{:S(2)}) %collective-permute-start.16) | collective-permute-done | bytes 262176 | tf_op jit(solution)/shard_map/ppermute | solution.py:119
  87.4 4.9 %collective-permute-done.7 = bf16[128,2048]{1,0:T(8,128)(2,1)S(1)} collective-permute-done((bf16[128,2048]{1,0:T(8,128)(2,1)S(1)}, bf16[128,2048]{1,0:T(8,128)(2,1)S(1)}, u32[]{:S(2)}, u32[]{:S(2)}) %collective-permute-start.7) | collective-permute-done | bytes 524320 | tf_op jit(solution)/shard_map/ppermute | solution.py:119
  95.8 15.7 %operate_first.1 = (bf16[2,128,2048]{2,1,0:T(8,128)(2,1)}, bf16[2,128,2048]{2,1,0:T(8,128)(2,1)}, f32[8,128]{1,0:T(8,128)}) custom-call(s32[192]{0:T(256)} %pad_add_fusion.cols, s32[256]{0:T(256)} %reshape.40.pattern, bf16[48,128,128]{2,1,0:T(8,128)(2,1)} %bitcast.53, bf16[31,128,128]{2,1,0:T(8,128)(2,1)} %copy-done.1, bf16[24,128,128]{2,1,0:T(8,128)(2,1)} %copy-done.2, ...), custom_call_target="tpu_custom_call" | custom-call | flops 3221225472 | bytes 16777216 | tf_op jit(solution)/shard_map/operate_first/pallas_call | solution.py:304
  117.1 1.9 collective-permute-done.18.hd_far.refs_17_
  119.2 1.9 collective-permute-done.22.refs_3_
  121.6 5.9 %update.1 = (f32[2,128,2048]{2,1,0:T(8,128)}, f32[8,128]{1,0:T(8,128)}) custom-call(bf16[2,128,2048]{2,1,0:T(8,128)(2,1)} %get-tuple-element.44.psi.refs_18_, bf16[2,128,2048]{2,1,0:T(8,128)(2,1)} %get-tuple-element.45.off.refs_19_, bf16[2,128,2048]{2,1,0:T(8,128)(2,1)} %bitcast.59, bf16[128,2048]{1,0:T(8,128)(2,1)} %copy-done.3, f32[2,8,128]{2,1,0:T(8,128)} %copy-done.42, ...), custom_call_target="tpu_custom_call" | custom-call | tf_op jit(solution)/shard_map/update/pallas_call | solution.py:629
  127.6 20.9 %all-gather = f32[128,128]{1,0:T(8,128)} all-gather(f32[8,128]{1,0:T(8,128)} %get-tuple-element.49), channel_id=2, replica_groups=mesh['groups'=2,'blk'=4,'ops'=2,'sub'=2] {'blk','ops','sub'}, dimensions={0}, use_global_device_ids=true | all-gather | bytes 69632 | tf_op jit(solution)/shard_map/all_gather | solution.py:644
  148.5 3.5 %correct.1 = (bf16[128,2048]{1,0:T(8,128)(2,1)}, bf16[128,2048]{1,0:T(8,128)(2,1)}) custom-call(bf16[2,128,2048]{2,1,0:T(8,128)(2,1)} %get-tuple-element.44.psi.refs_18_, f32[2,128,2048]{2,1,0:T(8,128)} %get-tuple-element.48.t, f32[16,8,128]{2,1,0:T(8,128)} %bitcast.107), custom_call_target="tpu_custom_call" | custom-call | tf_op jit(solution)/shard_map/correct/pallas_call | solution.py:646
  152.5 13.8 %collective-permute-done.23 = bf16[128,2048]{1,0:T(8,128)(2,1)S(1)} collective-permute-done((bf16[128,2048]{1,0:T(8,128)(2,1)}, bf16[128,2048]{1,0:T(8,128)(2,1)S(1)}, u32[]{:S(2)}, u32[]{:S(2)}) %collective-permute-start.23) | collective-permute-done | bytes 524320 | tf_op jit(solution)/shard_map/ppermute | solution.py:119
  166.4 1.7 collective-permute-start.35
  168.7 1.8 collective-permute-start.25
  170.5 10.8 %collective-permute-done.35 = bf16[128,2048]{1,0:T(8,128)(2,1)S(1)} collective-permute-done((bf16[128,2048]{1,0:T(8,128)(2,1)S(1)}, bf16[128,2048]{1,0:T(8,128)(2,1)S(1)}, u32[]{:S(2)}, u32[]{:S(2)}) %collective-permute-start.35) | collective-permute-done | bytes 524320 | tf_op jit(solution)/shard_map/ppermute | solution.py:119
  181.3 1.7 collective-permute-done.34
  183.0 8.1 %collective-permute-done.29 = bf16[128,2048]{1,0:T(8,128)(2,1)S(1)} collective-permute-done((bf16[128,2048]{1,0:T(8,128)(2,1)}, bf16[128,2048]{1,0:T(8,128)(2,1)S(1)}, u32[]{:S(2)}, u32[]{:S(2)}) %collective-permute-start.29) | collective-permute-done | bytes 524320 | tf_op jit(solution)/shard_map/ppermute | solution.py:119
  195.6 16.4 %operate_second.1 = (bf16[128,2048]{1,0:T(8,128)(2,1)}, bf16[64,2048]{1,0:T(8,128)(2,1)}, bf16[64,2048]{1,0:T(8,128)(2,1)}, f32[8,128]{1,0:T(8,128)}) custom-call(s32[192]{0:T(256)} %pad_add_fusion.cols, s32[256]{0:T(256)} %reshape.40.pattern, bf16[48,128,128]{2,1,0:T(8,128)(2,1)} %bitcast.54, bf16[31,128,128]{2,1,0:T(8,128)(2,1)} %copy-done.1, ...), custom_call_target="tpu_custom_call" | custom-call | bytes 1024 | tf_op jit(solution)/shard_map/operate_second/pallas_call | solution.py:304
  214.1 10.7 %collective-permute-done.26.refs_2_ = bf16[128,2048]{1,0:T(8,128)(2,1)S(1)} collective-permute-done((bf16[128,2048]{1,0:T(8,128)(2,1)}, bf16[128,2048]{1,0:T(8,128)(2,1)S(1)}, u32[]{:S(2)}, u32[]{:S(2)}) %collective-permute-start.26) | collective-permute-done | bytes 524320 | tf_op jit(solution)/shard_map/ppermute | solution.py:119
  229.9 2.6 collective-permute-done.45
  233.6 3.5 %collective-permute-done.46 = f32[8,128]{1,0:T(8,128)S(1)} collective-permute-done((f32[8,128]{1,0:T(8,128)S(1)}, f32[8,128]{1,0:T(8,128)S(1)}, u32[]{:S(2)}, u32[]{:S(2)}) %collective-permute-start.46) | collective-permute-done | bytes 4128 | tf_op jit(solution)/shard_map/ppermute | solution.py:119
  240.9 4.2 %collective-permute-done.42.refs_4_ = bf16[64,2048]{1,0:T(8,128)(2,1)S(1)} collective-permute-done((bf16[64,2048]{1,0:T(8,128)(2,1)S(1)}, bf16[64,2048]{1,0:T(8,128)(2,1)S(1)}, u32[]{:S(2)}, u32[]{:S(2)}) %collective-permute-start.42) | collective-permute-done | bytes 262176 | tf_op jit(solution)/shard_map/ppermute | solution.py:119
  245.1 6.4 %collective-permute-done.41.refs_3_ = bf16[64,2048]{1,0:T(8,128)(2,1)S(1)} collective-permute-done((bf16[64,2048]{1,0:T(8,128)(2,1)}, bf16[64,2048]{1,0:T(8,128)(2,1)S(1)}, u32[]{:S(2)}, u32[]{:S(2)}) %collective-permute-start.41) | collective-permute-done | bytes 262176 | tf_op jit(solution)/shard_map/ppermute | solution.py:119
  253.9 2.7 %assemble.4.refs_1_ = bf16[2,2,128,2048]{3,2,1,0:T(8,128)(2,1)} custom-call(bf16[128,2048]{1,0:T(8,128)(2,1)} %get-tuple-element.56.refs_0_, bf16[128,2048]{1,0:T(8,128)(2,1)} %copy-done.22, bf16[64,2048]{1,0:T(8,128)(2,1)} %copy-done.39, bf16[64,2048]{1,0:T(8,128)(2,1)} %copy-done.40, bf16[64,2048]{1,0:T(8,128)(2,1)} %copy-done.41), custom_call_target="tpu_custom_call" | custom-call | tf_op jit(solution)/shard_map/assemble/pallas_call | solution.py:533
  256.6 2.9 %assemble.3 = bf16[2,2,128,2048]{3,2,1,0:T(8,128)(2,1)} custom-call(bf16[128,2048]{1,0:T(8,128)(2,1)} %get-tuple-element.52.refs_0_, bf16[128,2048]{1,0:T(8,128)(2,1)} %copy-done.4, bf16[128,2048]{1,0:T(8,128)(2,1)} %copy-done.36, bf16[128,2048]{1,0:T(8,128)(2,1)} %copy-done.37), custom_call_target="tpu_custom_call" | custom-call | tf_op jit(solution)/shard_map/assemble/pallas_call | solution.py:533
  (193 shorter events, 50.1 us)
Async XLA Ops:
  11.4 20.7 %collective-permute-start.3 = (bf16[128,2048]{1,0:T(8,128)(2,1)}, bf16[128,2048]{1,0:T(8,128)(2,1)S(1)}, u32[]{:S(2)}, u32[]{:S(2)}) collective-permute-start(bf16[128,2048]{1,0:T(8,128)(2,1)} %get-tuple-element.41), channel_id=1, source_target_pairs={{0,1},{1,0},{2,3},{3,2},{4,5},{5,4},{6,7},{7,6},{8,9},{9,8},{10,11... | collective-permute-start | bytes 1572872 | tf_op jit(solution)/shard_map/ppermute | solution.py:119
  11.9 20.1 %collective-permute-start.4 = (bf16[128,2048]{1,0:T(8,128)(2,1)}, bf16[128,2048]{1,0:T(8,128)(2,1)S(1)}, u32[]{:S(2)}, u32[]{:S(2)}) collective-permute-start(bf16[128,2048]{1,0:T(8,128)(2,1)} %get-tuple-element.42), channel_id=1, source_target_pairs={{0,1},{1,0},{2,3},{3,2},{4,5},{5,4},{6,7},{7,6},{8,9},{9,8},{10,11... | collective-permute-start | bytes 1572872 | tf_op jit(solution)/shard_map/ppermute | solution.py:119
  13.0 19.1 %collective-permute-start.5 = (bf16[80,2048]{1,0:T(8,128)(2,1)S(1)}, bf16[80,2048]{1,0:T(8,128)(2,1)S(1)}, u32[]{:S(2)}, u32[]{:S(2)}) collective-permute-start(bf16[80,2048]{1,0:T(8,128)(2,1)S(1)} %dynamic-slice_bitcast_fusion.1), channel_id=1, source_target_pairs={{0,8},{4,12},{8,0},{12,4},{1,9},{5,13},{9,1},{13,5},{2,10},{6,14},... | collective-permute-start | bytes 983048 | tf_op jit(solution)/shard_map/ppermute | solution.py:119
  32.1 14.9 %collective-permute-start.6 = (bf16[80,2048]{1,0:T(8,128)(2,1)S(1)}, bf16[80,2048]{1,0:T(8,128)(2,1)S(1)}, u32[]{:S(2)}, u32[]{:S(2)}) collective-permute-start(bf16[80,2048]{1,0:T(8,128)(2,1)S(1)} %collective-permute-done.5), channel_id=1, source_target_pairs={{0,4},{4,0},{8,12},{12,8},{1,5},{5,1},{9,13},{13,9},{2,6},{6,2},{1... | collective-permute-start | bytes 983048 | tf_op jit(solution)/shard_map/ppermute | solution.py:119
  32.9 15.3 %collective-permute-start.1 = (bf16[64,2048]{1,0:T(8,128)(2,1)S(1)}, bf16[64,2048]{1,0:T(8,128)(2,1)S(1)}, u32[]{:S(2)}, u32[]{:S(2)}) collective-permute-start(bf16[64,2048]{1,0:T(8,128)(2,1)S(1)} %copy-done.46), channel_id=1, source_target_pairs={{0,8},{4,12},{8,0},{12,4},{1,9},{5,13},{9,1},{13,5},{2,10},{6,14},... | collective-permute-start | bytes 786440 | tf_op jit(solution)/shard_map/ppermute | solution.py:119
  36.2 49.6 %collective-permute-start = (bf16[31,128,128]{2,1,0:T(8,128)(2,1)}, bf16[31,128,128]{2,1,0:T(8,128)(2,1)S(1)}, u32[]{:S(2)}, u32[]{:S(2)}) collective-permute-start(bf16[31,128,128]{2,1,0:T(8,128)(2,1)} %get-tuple-element.35), channel_id=1, source_target_pairs={{0,2},{2,0},{1,3},{3,1},{4,6},{6,4},{5,7},{7,5},{8,10},{10,8},{9,1... | collective-permute-start | bytes 3047432 | tf_op jit(solution)/shard_map/ppermute | solution.py:119
  37.7 31.1 %collective-permute-start.11 = (bf16[80,2048]{1,0:T(8,128)(2,1)S(1)}, bf16[80,2048]{1,0:T(8,128)(2,1)S(1)}, u32[]{:S(2)}, u32[]{:S(2)}) collective-permute-start(bf16[80,2048]{1,0:T(8,128)(2,1)S(1)} %collective-permute-done.5), channel_id=1, source_target_pairs={{0,2},{2,0},{1,3},{3,1},{4,6},{6,4},{5,7},{7,5},{8,10},{10,8},{9,1... | collective-permute-start | bytes 983048 | tf_op jit(solution)/shard_map/ppermute | solution.py:119
  46.9 29.0 %collective-permute-start.12 = (bf16[80,2048]{1,0:T(8,128)(2,1)S(1)}, bf16[80,2048]{1,0:T(8,128)(2,1)S(1)}, u32[]{:S(2)}, u32[]{:S(2)}) collective-permute-start(bf16[80,2048]{1,0:T(8,128)(2,1)S(1)} %collective-permute-done.6), channel_id=1, source_target_pairs={{0,2},{2,0},{1,3},{3,1},{4,6},{6,4},{5,7},{7,5},{8,10},{10,8},{9,1... | collective-permute-start | bytes 983048 | tf_op jit(solution)/shard_map/ppermute | solution.py:119
  49.7 31.7 %collective-permute-start.14 = (bf16[64,2048]{1,0:T(8,128)(2,1)S(1)}, bf16[64,2048]{1,0:T(8,128)(2,1)S(1)}, u32[]{:S(2)}, u32[]{:S(2)}) collective-permute-start(bf16[64,2048]{1,0:T(8,128)(2,1)S(1)} %collective-permute-done.1), channel_id=1, source_target_pairs={{0,2},{2,0},{1,3},{3,1},{4,6},{6,4},{5,7},{7,5},{8,10},{10,8},{9,1... | collective-permute-start | bytes 786440 | tf_op jit(solution)/shard_map/ppermute | solution.py:119
  55.7 29.8 %collective-permute-start.16 = (bf16[64,2048]{1,0:T(8,128)(2,1)S(1)}, bf16[64,2048]{1,0:T(8,128)(2,1)S(1)}, u32[]{:S(2)}, u32[]{:S(2)}) collective-permute-start(bf16[64,2048]{1,0:T(8,128)(2,1)S(1)} %collective-permute-done.15), channel_id=1, source_target_pairs={{0,2},{2,0},{1,3},{3,1},{4,6},{6,4},{5,7},{7,5},{8,10},{10,8},{9,1... | collective-permute-start | bytes 786440 | tf_op jit(solution)/shard_map/ppermute | solution.py:119
  68.9 18.4 %collective-permute-start.8 = (bf16[128,2048]{1,0:T(8,128)(2,1)}, bf16[128,2048]{1,0:T(8,128)(2,1)S(1)}, u32[]{:S(2)}, u32[]{:S(2)}) collective-permute-start(bf16[128,2048]{1,0:T(8,128)(2,1)} %get-tuple-element.42), channel_id=1, source_target_pairs={{0,4},{4,0},{8,12},{12,8},{1,5},{5,1},{9,13},{13,9},{2,6},{6,2},{1... | collective-permute-start | bytes 1572872 | tf_op jit(solution)/shard_map/ppermute | solution.py:119
  76.6 17.6 %collective-permute-start.13 = (bf16[4,80,2048]{2,1,0:T(8,128)(2,1)S(1)}, bf16[4,80,2048]{2,1,0:T(8,128)(2,1)S(1)}, u32[]{:S(2)}, u32[]{:S(2)}) collective-permute-start(bf16[4,80,2048]{2,1,0:T(8,128)(2,1)S(1)} %pad_maximum_fusion), channel_id=1, source_target_pairs={{0,1},{1,0},{2,3},{3,2},{4,5},{5,4},{6,7},{7,6},{8,9},{9,8},{10,11... | collective-permute-start | bytes 3932168 | tf_op jit(solution)/shard_map/ppermute | solution.py:119
  81.5 10.8 %collective-permute-start.7 = (bf16[128,2048]{1,0:T(8,128)(2,1)S(1)}, bf16[128,2048]{1,0:T(8,128)(2,1)S(1)}, u32[]{:S(2)}, u32[]{:S(2)}) collective-permute-start(bf16[128,2048]{1,0:T(8,128)(2,1)S(1)} %copy-done.15), channel_id=1, source_target_pairs={{0,4},{4,0},{8,12},{12,8},{1,5},{5,1},{9,13},{13,9},{2,6},{6,2},{1... | collective-permute-start | bytes 1572872 | tf_op jit(solution)/shard_map/ppermute | solution.py:119
  85.7 8.5 %collective-permute-start.17 = (bf16[4,64,2048]{2,1,0:T(8,128)(2,1)S(1)}, bf16[4,64,2048]{2,1,0:T(8,128)(2,1)S(1)}, u32[]{:S(2)}, u32[]{:S(2)}) collective-permute-start(bf16[4,64,2048]{2,1,0:T(8,128)(2,1)S(1)} %pad_maximum_fusion.1), channel_id=1, source_target_pairs={{0,1},{1,0},{2,3},{3,2},{4,5},{5,4},{6,7},{7,6},{8,9},{9,8},{10,11... | collective-permute-start | bytes 3145736 | tf_op jit(solution)/shard_map/ppermute | solution.py:119
  92.4 26.6 %collective-permute-start.18 = (bf16[128,2048]{1,0:T(8,128)(2,1)S(1)}, bf16[128,2048]{1,0:T(8,128)(2,1)S(1)}, u32[]{:S(2)}, u32[]{:S(2)}) collective-permute-start(bf16[128,2048]{1,0:T(8,128)(2,1)S(1)} %dynamic-slice_bitcast_fusion), channel_id=1, source_target_pairs={{0,8},{4,12},{8,0},{12,4},{1,9},{5,13},{9,1},{13,5},{2,10},{6,14},... | collective-permute-start | bytes 1572872 | tf_op jit(solution)/shard_map/ppermute | solution.py:119
  152.0 14.4 %collective-permute-start.23 = (bf16[128,2048]{1,0:T(8,128)(2,1)}, bf16[128,2048]{1,0:T(8,128)(2,1)S(1)}, u32[]{:S(2)}, u32[]{:S(2)}) collective-permute-start(bf16[128,2048]{1,0:T(8,128)(2,1)} %get-tuple-element.52.refs_0_), channel_id=1, source_target_pairs={{0,4},{4,0},{8,12},{12,8},{1,5},{5,1},{9,13},{13,9},{2,6},{6,2},{1... | collective-permute-start | bytes 1572872 | tf_op jit(solution)/shard_map/ppermute | solution.py:119
  152.0 14.4 %collective-permute-start.24 = (bf16[128,2048]{1,0:T(8,128)(2,1)}, bf16[128,2048]{1,0:T(8,128)(2,1)S(1)}, u32[]{:S(2)}, u32[]{:S(2)}) collective-permute-start(bf16[128,2048]{1,0:T(8,128)(2,1)} %get-tuple-element.53), channel_id=1, source_target_pairs={{0,2},{2,0},{1,3},{3,1},{4,6},{6,4},{5,7},{7,5},{8,10},{10,8},{9,1... | collective-permute-start | bytes 1572872 | tf_op jit(solution)/shard_map/ppermute | solution.py:119
  152.0 16.7 %collective-permute-start.27 = (bf16[128,2048]{1,0:T(8,128)(2,1)}, bf16[128,2048]{1,0:T(8,128)(2,1)S(1)}, u32[]{:S(2)}, u32[]{:S(2)}) collective-permute-start(bf16[128,2048]{1,0:T(8,128)(2,1)} %get-tuple-element.52.refs_0_), channel_id=1, source_target_pairs={{0,1},{1,0},{2,3},{3,2},{4,5},{5,4},{6,7},{7,6},{8,9},{9,8},{10,11... | collective-permute-start | bytes 1572872 | tf_op jit(solution)/shard_map/ppermute | solution.py:119
  152.4 18.1 %collective-permute-start.28 = (bf16[128,2048]{1,0:T(8,128)(2,1)}, bf16[128,2048]{1,0:T(8,128)(2,1)S(1)}, u32[]{:S(2)}, u32[]{:S(2)}) collective-permute-start(bf16[128,2048]{1,0:T(8,128)(2,1)} %get-tuple-element.53), channel_id=1, source_target_pairs={{0,1},{1,0},{2,3},{3,2},{4,5},{5,4},{6,7},{7,6},{8,9},{9,8},{10,11... | collective-permute-start | bytes 1572872 | tf_op jit(solution)/shard_map/ppermute | solution.py:119
  166.4 14.9 %collective-permute-start.35 = (bf16[128,2048]{1,0:T(8,128)(2,1)S(1)}, bf16[128,2048]{1,0:T(8,128)(2,1)S(1)}, u32[]{:S(2)}, u32[]{:S(2)}) collective-permute-start(bf16[128,2048]{1,0:T(8,128)(2,1)S(1)} %collective-permute-done.24), channel_id=1, source_target_pairs={{0,4},{4,0},{8,12},{12,8},{1,5},{5,1},{9,13},{13,9},{2,6},{6,2},{1... | collective-permute-start | bytes 1572872 | tf_op jit(solution)/shard_map/ppermute | solution.py:119
  168.1 14.9 %collective-permute-start.34 = (bf16[128,2048]{1,0:T(8,128)(2,1)S(1)}, bf16[128,2048]{1,0:T(8,128)(2,1)S(1)}, u32[]{:S(2)}, u32[]{:S(2)}) collective-permute-start(bf16[128,2048]{1,0:T(8,128)(2,1)S(1)} %collective-permute-done.23), channel_id=1, source_target_pairs={{0,2},{2,0},{1,3},{3,1},{4,6},{6,4},{5,7},{7,5},{8,10},{10,8},{9,1... | collective-permute-start | bytes 1572872 | tf_op jit(solution)/shard_map/ppermute | solution.py:119
  168.4 22.6 %collective-permute-start.29 = (bf16[128,2048]{1,0:T(8,128)(2,1)}, bf16[128,2048]{1,0:T(8,128)(2,1)S(1)}, u32[]{:S(2)}, u32[]{:S(2)}) collective-permute-start(bf16[128,2048]{1,0:T(8,128)(2,1)} %get-tuple-element.53), channel_id=1, source_target_pairs={{0,4},{4,0},{8,12},{12,8},{1,5},{5,1},{9,13},{13,9},{2,6},{6,2},{1... | collective-permute-start | bytes 1572872 | tf_op jit(solution)/shard_map/ppermute | solution.py:119
  168.7 23.4 %collective-permute-start.25 = (bf16[128,2048]{1,0:T(8,128)(2,1)}, bf16[128,2048]{1,0:T(8,128)(2,1)S(1)}, u32[]{:S(2)}, u32[]{:S(2)}) collective-permute-start(bf16[128,2048]{1,0:T(8,128)(2,1)} %get-tuple-element.52.refs_0_), channel_id=1, source_target_pairs={{0,2},{2,0},{1,3},{3,1},{4,6},{6,4},{5,7},{7,5},{8,10},{10,8},{9,1... | collective-permute-start | bytes 1572872 | tf_op jit(solution)/shard_map/ppermute | solution.py:119
  170.5 21.6 %collective-permute-start.30 = (bf16[128,2048]{1,0:T(8,128)(2,1)S(1)}, bf16[128,2048]{1,0:T(8,128)(2,1)S(1)}, u32[]{:S(2)}, u32[]{:S(2)}) collective-permute-start(bf16[128,2048]{1,0:T(8,128)(2,1)S(1)} %collective-permute-done.23), channel_id=1, source_target_pairs={{0,1},{1,0},{2,3},{3,2},{4,5},{5,4},{6,7},{7,6},{8,9},{9,8},{10,11... | collective-permute-start | bytes 1572872 | tf_op jit(solution)/shard_map/ppermute | solution.py:119
  181.3 11.4 %collective-permute-start.33 = (bf16[128,2048]{1,0:T(8,128)(2,1)S(1)}, bf16[128,2048]{1,0:T(8,128)(2,1)S(1)}, u32[]{:S(2)}, u32[]{:S(2)}) collective-permute-start(bf16[128,2048]{1,0:T(8,128)(2,1)S(1)} %collective-permute-done.24), channel_id=1, source_target_pairs={{0,1},{1,0},{2,3},{3,2},{4,5},{5,4},{6,7},{7,6},{8,9},{9,8},{10,11... | collective-permute-start | bytes 1572872 | tf_op jit(solution)/shard_map/ppermute | solution.py:119
  183.0 9.7 %collective-permute-start.37 = (bf16[128,2048]{1,0:T(8,128)(2,1)S(1)}, bf16[128,2048]{1,0:T(8,128)(2,1)S(1)}, u32[]{:S(2)}, u32[]{:S(2)}) collective-permute-start(bf16[128,2048]{1,0:T(8,128)(2,1)S(1)} %collective-permute-done.35), channel_id=1, source_target_pairs={{0,1},{1,0},{2,3},{3,2},{4,5},{5,4},{6,7},{7,6},{8,9},{9,8},{10,11... | collective-permute-start | bytes 1572872 | tf_op jit(solution)/shard_map/ppermute | solution.py:119
  192.6 32.1 %collective-permute-start.26 = (bf16[128,2048]{1,0:T(8,128)(2,1)}, bf16[128,2048]{1,0:T(8,128)(2,1)S(1)}, u32[]{:S(2)}, u32[]{:S(2)}) collective-permute-start(bf16[128,2048]{1,0:T(8,128)(2,1)} %get-tuple-element.53), channel_id=1, source_target_pairs={{0,8},{4,12},{8,0},{12,4},{1,9},{5,13},{9,1},{13,5},{2,10},{6,14},... | collective-permute-start | bytes 1572872 | tf_op jit(solution)/shard_map/ppermute | solution.py:119
  212.0 14.2 %collective-permute-start.38 = (bf16[128,2048]{1,0:T(8,128)(2,1)}, bf16[128,2048]{1,0:T(8,128)(2,1)S(1)}, u32[]{:S(2)}, u32[]{:S(2)}) collective-permute-start(bf16[128,2048]{1,0:T(8,128)(2,1)} %get-tuple-element.56.refs_0_), channel_id=1, source_target_pairs={{0,2},{2,0},{1,3},{3,1},{4,6},{6,4},{5,7},{7,5},{8,10},{10,8},{9,1... | collective-permute-start | bytes 1572872 | tf_op jit(solution)/shard_map/ppermute | solution.py:119
  212.7 25.7 %collective-permute-start.40 = (bf16[64,2048]{1,0:T(8,128)(2,1)}, bf16[64,2048]{1,0:T(8,128)(2,1)S(1)}, u32[]{:S(2)}, u32[]{:S(2)}) collective-permute-start(bf16[64,2048]{1,0:T(8,128)(2,1)} %get-tuple-element.59), channel_id=1, source_target_pairs={{0,8},{4,12},{8,0},{12,4},{1,9},{5,13},{9,1},{13,5},{2,10},{6,14},... | collective-permute-start | bytes 786440 | tf_op jit(solution)/shard_map/ppermute | solution.py:119
  226.2 25.4 %collective-permute-start.39 = (bf16[128,2048]{1,0:T(8,128)(2,1)S(1)}, bf16[128,2048]{1,0:T(8,128)(2,1)S(1)}, u32[]{:S(2)}, u32[]{:S(2)}) collective-permute-start(bf16[128,2048]{1,0:T(8,128)(2,1)S(1)} %collective-permute-done.26.refs_2_), channel_id=1, source_target_pairs={{0,2},{2,0},{1,3},{3,1},{4,6},{6,4},{5,7},{7,5},{8,10},{10,8},{9,1... | collective-permute-start | bytes 1572872 | tf_op jit(solution)/shard_map/ppermute | solution.py:119
  239.0 12.5 %collective-permute-start.41 = (bf16[64,2048]{1,0:T(8,128)(2,1)}, bf16[64,2048]{1,0:T(8,128)(2,1)S(1)}, u32[]{:S(2)}, u32[]{:S(2)}) collective-permute-start(bf16[64,2048]{1,0:T(8,128)(2,1)} %get-tuple-element.60), channel_id=1, source_target_pairs={{0,8},{4,12},{8,0},{12,4},{1,9},{5,13},{9,1},{13,5},{2,10},{6,14},... | collective-permute-start | bytes 786440 | tf_op jit(solution)/shard_map/ppermute | solution.py:119
  251.6 7.9 %collective-permute-start.43 = (bf16[64,2048]{1,0:T(8,128)(2,1)S(1)}, bf16[64,2048]{1,0:T(8,128)(2,1)S(1)}, u32[]{:S(2)}, u32[]{:S(2)}) collective-permute-start(bf16[64,2048]{1,0:T(8,128)(2,1)S(1)} %collective-permute-done.41.refs_3_), channel_id=1, source_target_pairs={{0,2},{2,0},{1,3},{3,1},{4,6},{6,4},{5,7},{7,5},{8,10},{10,8},{9,1... | collective-permute-start | bytes 786440 | tf_op jit(solution)/shard_map/ppermute | solution.py:119
  (63 other events, 571.8 us)

commit v6 on v5

--- a/solution.py
+++ b/solution.py
@@ -109,6 +109,9 @@
     return (correction, sigma_two, subspace)
 
 
+MIX_A, MIX_B = 4, 5
+
+
 def halves_fit(mesh):
     sizes = dict(mesh.shape)
     return sizes["blk"] == 4 and sizes["ops"] == 2 and sizes["sub"] == 2
@@ -139,8 +142,15 @@
     return sum(value[:, at : at + LANES] for at in range(0, width, LANES))
 
 
+def in_middle(z):
+    return jnp.logical_or(z == 1, z == 2)
+
+
 def row_of(dz, dx, dc):
     z, x, c = place()
+    if dz in (MIX_A, MIX_B):
+        far = in_middle(z) if dz == MIX_A else jnp.logical_not(in_middle(z))
+        return jnp.where(far, row_of(2, 0, dc), row_of(1, 2, dc))
     return 4 * (z ^ dz) + 2 * (c ^ dc) + (x ^ dx if dx < 2 else dx - 2)
 
 
@@ -174,9 +184,15 @@
     for piece, offsets in zip(pieces, plan):
         for at, (dz, dx, dc, start, tall) in enumerate(offsets):
             target = field.at[row_of(dz, dx, dc), pl.ds(start, tall)]
-            begin(piece.at[at, pl.ds(0, tall)], target)
-            if first and (dz, dx, dc, start) == (2, 0, 0, block - tall):
-                begin(piece.at[at, pl.ds(tall, parts.shape[0]), pl.ds(0, parts.shape[1])], parts)
+            if dz in (MIX_A, MIX_B):
+                begin(piece.at[at, :, pl.ds(0, width)], target)
+                if dc == 0:
+                    begin(
+                        piece.at[at, pl.ds(0, parts.shape[1]), pl.ds(width, LANES)],
+                        parts.at[dz - MIX_A],
+                    )
+            else:
+                begin(piece.at[at], target)
     begin(right_near.at[pl.ds(0, part)], right.at[1, near])
     begin(right_far, right.at[1, far])
     early = len(copies)
@@ -277,8 +293,8 @@
 
     sums = list(lax.fori_loop(0, sectors // step, column, (zero,) * (2 if first else 3)))
     if first:
-        far_weight = parts[...].astype(jnp.float32)[:8]
-        sums[1] += weight_own[...] + sum(far_weight[:, i * LANES : (i + 1) * LANES] for i in range(3))
+        far_weight = (parts[0] + parts[1]).astype(jnp.float32)
+        sums[1] += weight_own[...] + (far_weight[0:8] + far_weight[16:24] + far_weight[32:40])
     stats_out[...] = jnp.zeros_like(stats_out)
     for at, value in enumerate(sums):
         stats_out[at : at + 1, :] = jnp.sum(value, axis=0, keepdims=True)
@@ -312,7 +328,7 @@
             pltpu.VMEM((2, table, block, block), jnp.bfloat16),
             pltpu.VMEM((2, 2 * links, block, block), jnp.bfloat16),
             pltpu.VMEM((2, block, width), jnp.bfloat16),
-            pltpu.VMEM((16, 3 * LANES), jnp.bfloat16),
+            pltpu.VMEM((2, 48, LANES), jnp.bfloat16),
             pltpu.SemaphoreType.DMA((copies,)),
         ],
         compiler_params=pltpu.CompilerParams(vmem_limit_bytes=VMEM_LIMIT),
@@ -325,14 +341,26 @@
     )(cols, pattern, right_own, right_near, right_far, left, *pieces, *extra)
 
 
-def prepare_kernel(theta, right, left, cols, after_this, own_a, own_b, packed, sems):
+def prepare_kernel(
+    pattern, theta, hd, right, left, cols, mix_a, mix_b, own_a, own_b, packed, own_out, waves, diag, sems
+):
     z, x, c = place()
     half = z // 2
+    middle = in_middle(z)
     mine = 4 * z + 2 * c + x
     block, width = own_a.shape
-    links = right.shape[0] * block // width
+    sectors = width // block
+    links = right.shape[0] // sectors
     part = right.shape[0] // 2
+    root_a = jnp.where(middle, half, 1 - half)
+    last = part + 2 * links
+    rows = pl.ds(0, width)
     sources = (
+        (theta.at[half, x], waves.at[0]),
+        (theta.at[1 - half, x], waves.at[1]),
+        (hd.at[x], diag),
+        (theta.at[root_a, jnp.where(middle, 0, x)], mix_a.at[:, rows]),
+        (theta.at[1 - root_a, jnp.where(middle, x, 0)], mix_b.at[:, rows]),
         (theta.at[half, 0], own_a),
         (theta.at[half, 1], own_b),
         (right.at[pl.ds(c * part, part)], packed.at[pl.ds(0, part)]),
@@ -345,50 +373,10 @@
     ]
     for copy in copies:
         copy.start()
-    last = part + 2 * links
     packed[last] = jnp.zeros_like(packed[last])
     packed[last, 0 : cols.shape[0], :] = cols[...]
-    for copy in copies:
+    for copy in copies[:3]:
         copy.wait()
-
-
-def prepare(theta, right, left, cols, after_this):
-    _, _, block, width = theta.shape
-    table = right.shape[0]
-    links = table * block // width
-    one = jax.ShapeDtypeStruct((block, width), jnp.bfloat16)
-    packed = jax.ShapeDtypeStruct((table // 2 + 2 * links + 1, block, block), jnp.bfloat16)
-    return pl.pallas_call(
-        prepare_kernel,
-        out_shape=(one, one, packed),
-        in_specs=[ANY, ANY, ANY, VMEM, ANY],
-        out_specs=(VMEM,) * 3,
-        scratch_shapes=[pltpu.SemaphoreType.DMA((5,))],
-        cost_estimate=pl.CostEstimate(flops=0, bytes_accessed=64 * 1024 * 1024, transcendentals=0),
-        compiler_params=pltpu.CompilerParams(vmem_limit_bytes=VMEM_LIMIT),
-        name="prepare",
-    )(theta, right, left, cols, after_this)
-
-
-def weigh_kernel(pattern, theta, hd, own_out, second, waves, diag, sems):
-    z, x, c = place()
-    half = z // 2
-    block, width = diag.shape
-    rest = second.shape[0] - 16
-    copies = [
-        pltpu.make_async_copy(theta.at[half, x], waves.at[0], sems.at[0]),
-        pltpu.make_async_copy(theta.at[1 - half, x], waves.at[1], sems.at[1]),
-        pltpu.make_async_copy(hd.at[x], diag, sems.at[2]),
-        pltpu.make_async_copy(
-            theta.at[1 - half, x, pl.ds(block - rest, rest)], second.at[pl.ds(0, rest)], sems.at[3]
-        ),
-    ]
-    for copy in copies:
-        copy.start()
-    for copy in copies:
-        copy.wait()
-    sectors = width // block
-    mine = 4 * z + 2 * c + x
     zero = jnp.zeros((8, LANES), jnp.float32)
 
     def column(q, sums):
@@ -401,36 +389,44 @@
             found.append(sums[root] + fold(weight * wave * wave))
         return tuple(found)
 
-    near, far = lax.fori_loop(0, sectors, column, (zero, zero))
+    near, far = lax.fori_loop(0, sectors, column, (zero, zero), unroll=4)
     own_out[...] = near
-    left = jnp.concatenate([far, zero], axis=0)
+    left_over = jnp.concatenate([far, zero], axis=0)
     parts = []
     for _ in range(3):
-        part = left.astype(jnp.bfloat16)
-        parts.append(part)
-        left = left - part.astype(jnp.float32)
-    parts.append(jnp.zeros((16, width - 3 * LANES), jnp.bfloat16))
-    second[rest:, :] = jnp.concatenate(parts, axis=1)
-
-
-def weigh(rest, pattern, theta, hd):
+        piece = left_over.astype(jnp.bfloat16)
+        parts.append(piece)
+        left_over = left_over - piece.astype(jnp.float32)
+    parts.append(jnp.zeros((block - 48, LANES), jnp.bfloat16))
+    tail = jnp.concatenate(parts, axis=0)
+    none = jnp.zeros_like(tail)
+    mix_a[:, width:] = jnp.where(middle, none, tail)
+    mix_b[:, width:] = jnp.where(middle, tail, none)
+    for copy in copies[3:]:
+        copy.wait()
+
+
+def prepare(pattern, theta, hd, right, left, cols):
     _, _, block, width = theta.shape
+    table = right.shape[0]
+    links = table * block // width
+    kind = jnp.bfloat16
+    mix = jax.ShapeDtypeStruct((block, width + LANES), kind)
+    one = jax.ShapeDtypeStruct((block, width), kind)
+    packed = jax.ShapeDtypeStruct((table // 2 + 2 * links + 1, block, block), kind)
     return pl.pallas_call(
-        weigh_kernel,
-        out_shape=(
-            jax.ShapeDtypeStruct((8, LANES), jnp.float32),
-            jax.ShapeDtypeStruct((rest + 16, width), theta.dtype),
-        ),
-        in_specs=[SMEM, ANY, ANY],
-        out_specs=(VMEM, VMEM),
+        prepare_kernel,
+        out_shape=(mix, mix, one, one, packed, jax.ShapeDtypeStruct((8, LANES), jnp.float32)),
+        in_specs=[SMEM, ANY, ANY, ANY, ANY, VMEM],
+        out_specs=(VMEM,) * 6,
         scratch_shapes=[
-            pltpu.VMEM((2, block, width), theta.dtype),
-            pltpu.VMEM((block, width), hd.dtype),
-            pltpu.SemaphoreType.DMA((4,)),
+            pltpu.VMEM((2, block, width), kind),
+            pltpu.VMEM((block, width), kind),
+            pltpu.SemaphoreType.DMA((10,)),
         ],
         compiler_params=pltpu.CompilerParams(vmem_limit_bytes=VMEM_LIMIT),
-        name="weigh",
-    )(pattern, theta, hd)
+        name="prepare",
+    )(pattern, theta, hd, right, left, cols)
 
 
 def total_of(rows):
@@ -488,9 +484,9 @@
     stats_out[4:5, :] = jnp.broadcast_to(norm_sq, (1, LANES))
 
 
-def correct_kernel(psi, t, found, *outs):
-    z, x, c = place()
-    stats = [found.at[8 * (z // 2) + at] for at in range(8)]
+def correct_kernel(psi, t, *refs):
+    stats, outs = refs[:4], refs[4:]
+    stats = [ref.at[at] for ref in stats for at in range(2)]
     norm_sq = stats[0][4:5, 0:1]
     factor = sum(ref[0:1, 0:1] for ref in stats) / (norm_sq + 1e-06)
     length_sq = jnp.zeros((1, 1), jnp.float32)
@@ -557,43 +553,39 @@
     halves = theta.reshape(roots, 2, block, width)
     diag = hdiag.reshape(2, block, width)
     allowed = pattern.reshape(-1)
-    tall = block * 5 // 8
-    rest = block - tall
-
+    chunk = block // 2
     right = right_blocks.reshape(-1, block, block)
     left = left_blocks.reshape(-1, block, block)
     table = right.shape[0]
     cols = jnp.concatenate([right_cols.reshape(-1), left_cols.reshape(-1)])
-
-    first = lax.dynamic_slice(halves, (1 - half, x, 0, 0), (1, 1, tall, width))[0, 0]
-    far_a = across(first, "blk", 2)
-    weight_own, second = weigh(rest, allowed, halves, diag)
-    far_b = across(second, "blk", 2)
     spots = jnp.pad(cols, (0, 16 * LANES - cols.shape[0])).reshape(16, LANES).astype(jnp.bfloat16)
-    own_a, own_b, packed = prepare(halves, right, left, spots, weight_own)
+
+    mix_a, mix_b, own_a, own_b, packed, weight_own = prepare(allowed, halves, diag, right, left, spots)
+    mix_a = lax.ppermute(mix_a, "blk", [(0, 2), (2, 3), (3, 1), (1, 0)])
+    mix_b = lax.ppermute(mix_b, "blk", [(0, 1), (1, 3), (3, 2), (2, 0)])
     operators = across(packed, "ops", 1)
     own_core_a = across(own_a, "sub", 1)
     own_core_b = across(own_b, "sub", 1)
 
-    far_a = after(far_a, own_core_a, own_core_b)
-    far_za = across(far_a, "blk", 1)
-    far_xa = across(far_a, "ops", 1)
-
-    far_zb = across(far_b, "blk", 1)
-    far_xb = across(far_b, "ops", 1)
-    far_zxa = across(far_za, "ops", 1)
-    near_a = across(after(own_a, far_za, far_b), "blk", 1)
-    near_b = across(after(own_b, far_za, far_b), "blk", 1)
-    operators_core = across(after(operators, far_b)[: table // 2], "sub", 1)
+    mix_a, mix_b = after((mix_a, mix_b), own_core_a, own_core_b)
+    far = [
+        jnp.where(in_middle(z), mix_a[at : at + chunk, :width], mix_b[at : at + chunk, :width])
+        for at in (0, chunk)
+    ]
+    far_z = [across(value, "blk", 1) for value in far]
+    far_x = [across(value, "ops", 1) for value in far]
+    mix_a_core = across(mix_a, "sub", 1)
+    mix_b_core = across(mix_b, "sub", 1)
+    operators_core = across(after(operators, mix_b_core)[: table // 2], "sub", 1)
     found = operators[-1].reshape(-1)[: cols.shape[0]].astype(jnp.int32)
     cols = jnp.concatenate([cols, found])
 
-    far_zxb = across(after(far_zb, far_za), "ops", 1)
+    near_b = across(after(own_b, far_z[0]), "blk", 1)
+    far_zx = [across(far_z[0], "ops", 1), across(after(far_z[1], far_x[1]), "ops", 1)]
+    crossed_core = across(jnp.stack([*far_x, *far_z]), "sub", 1)
     hd_far = lax.dynamic_index_in_dim(diag, x, 0, keepdims=False)
-    hd_far = across(after(hd_far, far_zb), "blk", 2)
-    core_a = across(jnp.stack([far_a, far_xa, far_za, far_zxa]), "sub", 1)
-    near_a_core = across(near_a, "sub", 1)
-    core_b = across(jnp.stack([far_b, far_xb, far_zb, far_zxb]), "sub", 1)
+    hd_far = across(after(hd_far, far_z[1]), "blk", 2)
+    far_zx_core = [across(value, "sub", 1) for value in far_zx]
     near_b_core = across(near_b, "sub", 1)
 
     operators = (right, operators, operators_core)
@@ -604,23 +596,28 @@
         (own_b, (0, 3, 0)),
         (own_core_a, (0, 2, 1)),
         (own_core_b, (0, 3, 1)),
-        (near_a, (1, 2, 0)),
+        (mix_a, (MIX_A, 0, 0)),
+        (mix_b, (MIX_B, 0, 0)),
+        (mix_a_core, (MIX_A, 0, 1)),
+        (mix_b_core, (MIX_B, 0, 1)),
         (near_b, (1, 3, 0)),
-        (near_a_core, (1, 2, 1)),
         (near_b_core, (1, 3, 1)),
     ):
         pieces.append(piece[None])
         plan.append((offset + (0, block),))
-    crossed = ((2, 0), (2, 1), (3, 0), (3, 1))
-    for start, count, group, core in (
-        (0, tall, (far_a, far_xa, far_za, far_zxa), core_a),
-        (tall, rest, (far_b, far_xb, far_zb, far_zxb), core_b),
-    ):
-        for piece, offset in zip(group, crossed):
+    for at in range(2):
+        for piece, offset in (
+            (far_x[at], (2, 1, 0)),
+            (far_z[at], (3, 0, 0)),
+            (far_zx[at], (3, 1, 0)),
+            (far_zx_core[at], (3, 1, 1)),
+        ):
             pieces.append(piece[None])
-            plan.append((offset + (0, start, count),))
-        pieces.append(core)
-        plan.append(tuple(offset + (1, start, count) for offset in crossed))
+            plan.append((offset + (at * chunk, chunk),))
+    pieces.append(crossed_core)
+    plan.append(
+        tuple((*offset, 1, at * chunk, chunk) for offset in ((2, 1), (3, 0)) for at in range(2))
+    )
     psi, off_one, stats_one = operate(
         True, tuple(plan), pieces, cols, allowed, operators, left, (weight_own,)
     )
@@ -641,16 +638,16 @@
         compiler_params=pltpu.CompilerParams(vmem_limit_bytes=VMEM_LIMIT),
         name="update",
     )(psi, off_one, diag, hd_far, *found)
-    found = lax.all_gather(stats_two, ("blk", "ops", "sub"))
+    found = share(stats_two)
     one = jax.ShapeDtypeStruct((block, width), jnp.bfloat16)
     changed_near, changed_far = pl.pallas_call(
         correct_kernel,
         out_shape=(one, one),
-        in_specs=[VMEM, VMEM, VMEM],
+        in_specs=[VMEM, VMEM] + [VMEM] * 4,
         out_specs=(VMEM, VMEM),
         compiler_params=pltpu.CompilerParams(vmem_limit_bytes=VMEM_LIMIT),
         name="correct",
-    )(psi, t, found)
+    )(psi, t, *found)
 
     near_z = across(changed_near, "blk", 1)
     far_x = across(changed_far, "ops", 1)

time: 263 us -> 229 us (0.87)
  blocking collectives: 20.9 us -> 0 us
  waiting for transfers between devices: 133 us -> 119 us
  starting transfers between devices: 37.4 us -> 41.5 us
    ppermute x45, waiting for transfers between devices: 131 us -> 91.5 us  [across(): return lax.ppermute(value, axis, [(i, i ^ distance) for i in range(size)])]
    ppermute x0 -> x2, waiting for transfers between devices: none -> 22.8 us  [the longest x1 12.5 us: shards(): mix_b = lax.ppermute(mix_b, 'blk', [(0, 1), (1, 3), (3, 2), (2, 0)])]
    all_gather x1 -> x0, blocking collectives: 20.9 us -> none  [shards(): found = lax.all_gather(stats_two, ('blk', 'ops', 'sub'))]
    ppermute x0 -> x2, starting transfers between devices: none -> 4.1 us  [the longest x1 4.1 us: shards(): mix_a = lax.ppermute(mix_a, 'blk', [(0, 2), (2, 3), (3, 1), (1, 0)])]
    ppermute x3 -> x6, starting transfers between devices: 3.49 us -> 6.98 us  [share(): lax.ppermute(pair, axes, [(i, i ^ distance) for i in range(count)])]
    ppermute x45, starting transfers between devices: 33.9 us -> 30.5 us  [across(): return lax.ppermute(value, axis, [(i, i ^ distance) for i in range(size)])]
    pallas_call x2 -> x1, Pallas kernels: 6.99 us -> 4.72 us  [prepare(): pl.pallas_call(prepare_kernel, out_shape=(mix, mix, one, one, packed, jax...]
    unnamed x96 -> x86, local copies, waits for them, and re-layouts: 6.87 us -> 5.27 us
  transfers between devices with their start and end apart: 48 -> 53, of which waited for: 29 -> 35; matrix products, arithmetic and copies ran while one was open for 2% -> 2% of each run, Pallas kernels for 14% -> 17%
where the time goes in v6:
time: 229 us; the launch traced here: 228 us
  waiting for transfers between devices  119 us (52%)
  Pallas kernels  53.4 us (23%)
  starting transfers between devices  41.5 us (18%)
  local copies, waits for them, and re-layouts  6.88 us (3%)
  other arithmetic  6.45 us (3%)
    ppermute x45, waiting for transfers between devices, across(): return lax.ppermute(value, axis, [(i, i ^ distance) for i in range(size)])  91.5 us
    pallas_call x2, Pallas kernels, operate(): pl.pallas_call(functools.partial(operate_kernel, first, plan), out_shape=...  32.1 us
    ppermute x45, starting transfers between devices, across(): return lax.ppermute(value, axis, [(i, i ^ distance) for i in range(size)])  30.5 us
    ppermute x1, waiting for transfers between devices, shards(): mix_b = lax.ppermute(mix_b, 'blk', [(0, 1), (1, 3), (3, 2), (2, 0)])  12.5 us
    ppermute x1, waiting for transfers between devices, shards(): mix_a = lax.ppermute(mix_a, 'blk', [(0, 2), (2, 3), (3, 1), (1, 0)])  10.4 us
    pallas_call x3, Pallas kernels, assemble(): pl.pallas_call(functools.partial(assemble_kernel, places, len(based)), ou...  7.21 us
    ppermute x6, starting transfers between devices, share(): lax.ppermute(pair, axes, [(i, i ^ distance) for i in range(count)])  6.98 us
    pallas_call x1, Pallas kernels, shards(): pl.pallas_call(update_kernel, out_shape=(jax.ShapeDtypeStruct((2, block,...  5.92 us
  transfers between devices with their start and end apart: 53, of which 35 were waited for; matrix products, arithmetic and copies ran while one was open for 2% of the time, Pallas kernels for 17%

profile of v6, /device:TPU:0, one launch (start us, length us, event | category | flops | bytes accessed | tf_op | source)
XLA Modules:
  0.0 228.1 jit_solution(17115212878094853757)
XLA Ops:
  4.4 4.7 %prepare.1 = (bf16[128,2176]{1,0:T(8,128)(2,1)}, bf16[128,2176]{1,0:T(8,128)(2,1)}, bf16[128,2048]{1,0:T(8,128)(2,1)}, bf16[128,2048]{1,0:T(8,128)(2,1)}, bf16[3...) custom-call(s32[256]{0:T(256)} %reshape.37.pattern, bf16[2,2,128,2048]{3,2,1,0:T(8,128)(2,1)} %bitcast.66, ...), custom_call_target="tpu_custom_call" | custom-call | tf_op jit(solution)/shard_map/prepare/pallas_call | solution.py:417
  9.1 4.1 %collective-permute-start.1 = (bf16[128,2176]{1,0:T(8,128)(2,1)}, bf16[128,2176]{1,0:T(8,128)(2,1)S(1)}, u32[]{:S(2)}, u32[]{:S(2)}) collective-permute-start(bf16[128,2176]{1,0:T(8,128)(2,1)} %get-tuple-element.36), channel_id=1, source_target_pairs={{0,8},{8,12},{12,4},{4,0},{1,9},{9,13},{13,5},{5,1},{2,10},{10,14}... | collective-permute-start | bytes 1671176 | tf_op jit(solution)/shard_map/ppermute | solution.py:564
  13.7 1.5 collective-permute-start
  16.2 10.4 %collective-permute-done.1 = bf16[128,2176]{1,0:T(8,128)(2,1)S(1)} collective-permute-done((bf16[128,2176]{1,0:T(8,128)(2,1)}, bf16[128,2176]{1,0:T(8,128)(2,1)S(1)}, u32[]{:S(2)}, u32[]{:S(2)}) %collective-permute-start.1) | collective-permute-done | bytes 557088 | tf_op jit(solution)/shard_map/ppermute | solution.py:564
  26.6 12.5 %collective-permute-done.2 = bf16[128,2176]{1,0:T(8,128)(2,1)S(1)} collective-permute-done((bf16[128,2176]{1,0:T(8,128)(2,1)}, bf16[128,2176]{1,0:T(8,128)(2,1)S(1)}, u32[]{:S(2)}, u32[]{:S(2)}) %collective-permute-start.2) | collective-permute-done | bytes 557088 | tf_op jit(solution)/shard_map/ppermute | solution.py:565
  42.7 5.7 %collective-permute-done.8 = bf16[64,2048]{1,0:T(8,128)(2,1)S(1)} collective-permute-done((bf16[64,2048]{1,0:T(8,128)(2,1)S(1)}, bf16[64,2048]{1,0:T(8,128)(2,1)S(1)}, u32[]{:S(2)}, u32[]{:S(2)}) %collective-permute-start.8) | collective-permute-done | bytes 262176 | tf_op jit(solution)/shard_map/ppermute | solution.py:122
  49.8 3.3 %collective-permute-done.15 = bf16[64,2048]{1,0:T(8,128)(2,1)} collective-permute-done((bf16[64,2048]{1,0:T(8,128)(2,1)S(1)}, bf16[64,2048]{1,0:T(8,128)(2,1)}, u32[]{:S(2)}, u32[]{:S(2)}) %collective-permute-start.15) | collective-permute-done | bytes 262176 | tf_op jit(solution)/shard_map/ppermute | solution.py:122
  53.4 1.8 collective-permute-done.11
  55.3 2.1 pad_maximum_fusion
  59.7 7.2 %collective-permute-done.16 = bf16[64,2048]{1,0:T(8,128)(2,1)} collective-permute-done((bf16[64,2048]{1,0:T(8,128)(2,1)}, bf16[64,2048]{1,0:T(8,128)(2,1)}, u32[]{:S(2)}, u32[]{:S(2)}) %collective-permute-start.16) | collective-permute-done | bytes 262176 | tf_op jit(solution)/shard_map/ppermute | solution.py:122
  66.8 5.2 %collective-permute-done.12 = bf16[64,2048]{1,0:T(8,128)(2,1)} collective-permute-done((bf16[64,2048]{1,0:T(8,128)(2,1)S(1)}, bf16[64,2048]{1,0:T(8,128)(2,1)}, u32[]{:S(2)}, u32[]{:S(2)}) %collective-permute-start.12) | collective-permute-done | bytes 262176 | tf_op jit(solution)/shard_map/ppermute | solution.py:122
  76.9 15.7 %operate_first.1 = (bf16[2,128,2048]{2,1,0:T(8,128)(2,1)}, bf16[2,128,2048]{2,1,0:T(8,128)(2,1)}, f32[8,128]{1,0:T(8,128)}) custom-call(s32[192]{0:T(256)} %pad_add_fusion.cols, s32[256]{0:T(256)} %reshape.37.pattern, bf16[48,128,128]{2,1,0:T(8,128)(2,1)} %bitcast.54, bf16[31,128,128]{2,1,0:T(8,128)(2,1)} %copy-done.1, bf16[24,128,128]{2,1,0:T(8,128)(2,1)} %copy-done.2, ...), custom_call_target="tpu_custom_call" | custom-call | flops 3221225472 | bytes 16777216 | tf_op jit(solution)/shard_map/operate_first/pallas_call | solution.py:320
  96.2 1.7 collective-permute-start.22
  98.2 1.8 collective-permute-done.19.hd_far.refs_17_
  100.1 2.4 %collective-permute-done.23.refs_3_ = f32[2,8,128]{2,1,0:T(8,128)S(1)} collective-permute-done((f32[2,8,128]{2,1,0:T(8,128)S(1)}, f32[2,8,128]{2,1,0:T(8,128)S(1)}, u32[]{:S(2)}, u32[]{:S(2)}) %collective-permute-start.23) | collective-permute-done | bytes 8224 | tf_op jit(solution)/shard_map/ppermute | solution.py:131
  103.1 5.9 %update.1 = (f32[2,128,2048]{2,1,0:T(8,128)}, f32[8,128]{1,0:T(8,128)}) custom-call(bf16[2,128,2048]{2,1,0:T(8,128)(2,1)} %get-tuple-element.46.psi.refs_18_, bf16[2,128,2048]{2,1,0:T(8,128)(2,1)} %get-tuple-element.47.off.refs_19_, bf16[2,128,2048]{2,1,0:T(8,128)(2,1)} %bitcast.60, bf16[128,2048]{1,0:T(8,128)(2,1)} %copy-done.5, f32[2,8,128]{2,1,0:T(8,128)} %copy-done.34, ...), custom_call_target="tpu_custom_call" | custom-call | tf_op jit(solution)/shard_map/update/pallas_call | solution.py:626
  112.0 2.6 %collective-permute-start.27 = (f32[2,8,128]{2,1,0:T(8,128)S(1)}, f32[2,8,128]{2,1,0:T(8,128)S(1)}, u32[]{:S(2)}, u32[]{:S(2)}) collective-permute-start(f32[2,8,128]{2,1,0:T(8,128)S(1)} %pad_maximum_fusion.2.refs_0_), channel_id=1, source_target_pairs={{0,6},{2,4},{4,2},{6,0},{8,14},{10,12},{12,10},{14,8},{1,7},{3,5},... | collective-permute-start | bytes 24584 | tf_op jit(solution)/shard_map/ppermute | solution.py:131
  117.1 3.5 %correct.1 = (bf16[128,2048]{1,0:T(8,128)(2,1)}, bf16[128,2048]{1,0:T(8,128)(2,1)}) custom-call(bf16[2,128,2048]{2,1,0:T(8,128)(2,1)} %get-tuple-element.46.psi.refs_18_, f32[2,128,2048]{2,1,0:T(8,128)} %get-tuple-element.50.t, f32[2,8,128]{2,1,0:T(8,128)} %copy-done.35, f32[2,8,128]{2,1,0:T(8,128)} %copy-done.38, f32[2,8,128]{2,1,0:T(8,128)} %copy-done.40, ...), custom_call_target="tpu_custom_call" | custom-call | tf_op jit(solution)/shard_map/correct/pallas_call | solution.py:643
  120.6 1.7 collective-permute-start.28
  124.3 8.9 %collective-permute-done.28 = bf16[128,2048]{1,0:T(8,128)(2,1)S(1)} collective-permute-done((bf16[128,2048]{1,0:T(8,128)(2,1)}, bf16[128,2048]{1,0:T(8,128)(2,1)S(1)}, u32[]{:S(2)}, u32[]{:S(2)}) %collective-permute-start.28) | collective-permute-done | bytes 524320 | tf_op jit(solution)/shard_map/ppermute | solution.py:122
  136.4 1.7 collective-permute-start.34
  138.6 10.8 %collective-permute-done.40 = bf16[128,2048]{1,0:T(8,128)(2,1)S(1)} collective-permute-done((bf16[128,2048]{1,0:T(8,128)(2,1)S(1)}, bf16[128,2048]{1,0:T(8,128)(2,1)S(1)}, u32[]{:S(2)}, u32[]{:S(2)}) %collective-permute-start.40) | collective-permute-done | bytes 524320 | tf_op jit(solution)/shard_map/ppermute | solution.py:122
  149.9 6.9 %collective-permute-done.34 = bf16[128,2048]{1,0:T(8,128)(2,1)S(1)} collective-permute-done((bf16[128,2048]{1,0:T(8,128)(2,1)}, bf16[128,2048]{1,0:T(8,128)(2,1)S(1)}, u32[]{:S(2)}, u32[]{:S(2)}) %collective-permute-start.34) | collective-permute-done | bytes 524320 | tf_op jit(solution)/shard_map/ppermute | solution.py:122
  161.1 16.4 %operate_second.1 = (bf16[128,2048]{1,0:T(8,128)(2,1)}, bf16[64,2048]{1,0:T(8,128)(2,1)}, bf16[64,2048]{1,0:T(8,128)(2,1)}, f32[8,128]{1,0:T(8,128)}) custom-call(s32[192]{0:T(256)} %pad_add_fusion.cols, s32[256]{0:T(256)} %reshape.37.pattern, bf16[48,128,128]{2,1,0:T(8,128)(2,1)} %bitcast.55, bf16[31,128,128]{2,1,0:T(8,128)(2,1)} %copy-done.1, ...), custom_call_target="tpu_custom_call" | custom-call | bytes 1024 | tf_op jit(solution)/shard_map/operate_second/pallas_call | solution.py:320
  180.0 10.5 %collective-permute-done.31.refs_2_ = bf16[128,2048]{1,0:T(8,128)(2,1)S(1)} collective-permute-done((bf16[128,2048]{1,0:T(8,128)(2,1)}, bf16[128,2048]{1,0:T(8,128)(2,1)S(1)}, u32[]{:S(2)}, u32[]{:S(2)}) %collective-permute-start.31) | collective-permute-done | bytes 524320 | tf_op jit(solution)/shard_map/ppermute | solution.py:122
  196.3 2.6 %collective-permute-done.50 = f32[8,128]{1,0:T(8,128)S(1)} collective-permute-done((f32[8,128]{1,0:T(8,128)S(1)}, f32[8,128]{1,0:T(8,128)S(1)}, u32[]{:S(2)}, u32[]{:S(2)}) %collective-permute-start.50) | collective-permute-done | bytes 4128 | tf_op jit(solution)/shard_map/ppermute | solution.py:122
  199.7 3.6 %collective-permute-done.51 = f32[8,128]{1,0:T(8,128)S(1)} collective-permute-done((f32[8,128]{1,0:T(8,128)S(1)}, f32[8,128]{1,0:T(8,128)S(1)}, u32[]{:S(2)}, u32[]{:S(2)}) %collective-permute-start.51) | collective-permute-done | bytes 4128 | tf_op jit(solution)/shard_map/ppermute | solution.py:122
  207.3 3.4 %collective-permute-done.47.refs_4_ = bf16[64,2048]{1,0:T(8,128)(2,1)S(1)} collective-permute-done((bf16[64,2048]{1,0:T(8,128)(2,1)S(1)}, bf16[64,2048]{1,0:T(8,128)(2,1)S(1)}, u32[]{:S(2)}, u32[]{:S(2)}) %collective-permute-start.47) | collective-permute-done | bytes 262176 | tf_op jit(solution)/shard_map/ppermute | solution.py:122
  210.7 7.3 %collective-permute-done.46.refs_3_ = bf16[64,2048]{1,0:T(8,128)(2,1)S(1)} collective-permute-done((bf16[64,2048]{1,0:T(8,128)(2,1)}, bf16[64,2048]{1,0:T(8,128)(2,1)S(1)}, u32[]{:S(2)}, u32[]{:S(2)}) %collective-permute-start.46) | collective-permute-done | bytes 262176 | tf_op jit(solution)/shard_map/ppermute | solution.py:122
  219.4 2.7 %assemble.4.refs_1_ = bf16[2,2,128,2048]{3,2,1,0:T(8,128)(2,1)} custom-call(bf16[128,2048]{1,0:T(8,128)(2,1)} %get-tuple-element.58.refs_0_, bf16[128,2048]{1,0:T(8,128)(2,1)} %copy-done.11, bf16[64,2048]{1,0:T(8,128)(2,1)} %copy-done.29, bf16[64,2048]{1,0:T(8,128)(2,1)} %copy-done.30, bf16[64,2048]{1,0:T(8,128)(2,1)} %copy-done.31), custom_call_target="tpu_custom_call" | custom-call | tf_op jit(solution)/shard_map/assemble/pallas_call | solution.py:529
  222.1 2.9 %assemble.3 = bf16[2,2,128,2048]{3,2,1,0:T(8,128)(2,1)} custom-call(bf16[128,2048]{1,0:T(8,128)(2,1)} %get-tuple-element.54.refs_0_, bf16[128,2048]{1,0:T(8,128)(2,1)} %copy-done.6, bf16[128,2048]{1,0:T(8,128)(2,1)} %copy-done.25, bf16[128,2048]{1,0:T(8,128)(2,1)} %copy-done.26), custom_call_target="tpu_custom_call" | custom-call | tf_op jit(solution)/shard_map/assemble/pallas_call | solution.py:529
  226.4 1.7 assemble.5
  (191 shorter events, 53.8 us)
Async XLA Ops:
  9.1 17.5 %collective-permute-start.1 = (bf16[128,2176]{1,0:T(8,128)(2,1)}, bf16[128,2176]{1,0:T(8,128)(2,1)S(1)}, u32[]{:S(2)}, u32[]{:S(2)}) collective-permute-start(bf16[128,2176]{1,0:T(8,128)(2,1)} %get-tuple-element.36), channel_id=1, source_target_pairs={{0,8},{8,12},{12,4},{4,0},{1,9},{9,13},{13,5},{5,1},{2,10},{10,14}... | collective-permute-start | bytes 1671176 | tf_op jit(solution)/shard_map/ppermute | solution.py:564
  13.2 25.9 %collective-permute-start.2 = (bf16[128,2176]{1,0:T(8,128)(2,1)}, bf16[128,2176]{1,0:T(8,128)(2,1)S(1)}, u32[]{:S(2)}, u32[]{:S(2)}) collective-permute-start(bf16[128,2176]{1,0:T(8,128)(2,1)} %get-tuple-element.37), channel_id=1, source_target_pairs={{0,4},{4,12},{12,8},{8,0},{1,5},{5,13},{13,9},{9,1},{2,6},{6,14},{... | collective-permute-start | bytes 1671176 | tf_op jit(solution)/shard_map/ppermute | solution.py:565
  13.7 45.2 %collective-permute-start = (bf16[31,128,128]{2,1,0:T(8,128)(2,1)}, bf16[31,128,128]{2,1,0:T(8,128)(2,1)S(1)}, u32[]{:S(2)}, u32[]{:S(2)}) collective-permute-start(bf16[31,128,128]{2,1,0:T(8,128)(2,1)} %get-tuple-element.35), channel_id=1, source_target_pairs={{0,2},{2,0},{1,3},{3,1},{4,6},{6,4},{5,7},{7,5},{8,10},{10,8},{9,1... | collective-permute-start | bytes 3047432 | tf_op jit(solution)/shard_map/ppermute | solution.py:122
  39.1 9.2 %collective-permute-start.8 = (bf16[64,2048]{1,0:T(8,128)(2,1)S(1)}, bf16[64,2048]{1,0:T(8,128)(2,1)S(1)}, u32[]{:S(2)}, u32[]{:S(2)}) collective-permute-start(bf16[64,2048]{1,0:T(8,128)(2,1)S(1)} %get-tuple-element.68), channel_id=1, source_target_pairs={{0,4},{4,0},{8,12},{12,8},{1,5},{5,1},{9,13},{13,9},{2,6},{6,2},{1... | collective-permute-start | bytes 786440 | tf_op jit(solution)/shard_map/ppermute | solution.py:122
  39.9 19.6 %collective-permute-start.5 = (bf16[128,2176]{1,0:T(8,128)(2,1)S(1)}, bf16[128,2176]{1,0:T(8,128)(2,1)}, u32[]{:S(2)}, u32[]{:S(2)}) collective-permute-start(bf16[128,2176]{1,0:T(8,128)(2,1)S(1)} %collective-permute-done.2), channel_id=1, source_target_pairs={{0,1},{1,0},{2,3},{3,2},{4,5},{5,4},{6,7},{7,6},{8,9},{9,8},{10,11... | collective-permute-start | bytes 1671176 | tf_op jit(solution)/shard_map/ppermute | solution.py:122
  39.9 13.2 %collective-permute-start.15 = (bf16[64,2048]{1,0:T(8,128)(2,1)S(1)}, bf16[64,2048]{1,0:T(8,128)(2,1)}, u32[]{:S(2)}, u32[]{:S(2)}) collective-permute-start(bf16[64,2048]{1,0:T(8,128)(2,1)S(1)} %get-tuple-element.67), channel_id=1, source_target_pairs={{0,4},{4,0},{8,12},{12,8},{1,5},{5,1},{9,13},{13,9},{2,6},{6,2},{1... | collective-permute-start | bytes 786440 | tf_op jit(solution)/shard_map/ppermute | solution.py:122
  41.2 12.2 %collective-permute-start.14 = (bf16[64,2048]{1,0:T(8,128)(2,1)S(1)}, bf16[64,2048]{1,0:T(8,128)(2,1)S(1)}, u32[]{:S(2)}, u32[]{:S(2)}) collective-permute-start(bf16[64,2048]{1,0:T(8,128)(2,1)S(1)} %get-tuple-element.67), channel_id=1, source_target_pairs={{0,2},{2,0},{1,3},{3,1},{4,6},{6,4},{5,7},{7,5},{8,10},{10,8},{9,1... | collective-permute-start | bytes 786440 | tf_op jit(solution)/shard_map/ppermute | solution.py:122
  48.4 6.9 %collective-permute-start.11 = (bf16[64,2048]{1,0:T(8,128)(2,1)S(1)}, bf16[64,2048]{1,0:T(8,128)(2,1)S(1)}, u32[]{:S(2)}, u32[]{:S(2)}) collective-permute-start(bf16[64,2048]{1,0:T(8,128)(2,1)S(1)} %get-tuple-element.68), channel_id=1, source_target_pairs={{0,2},{2,0},{1,3},{3,1},{4,6},{6,4},{5,7},{7,5},{8,10},{10,8},{9,1... | collective-permute-start | bytes 786440 | tf_op jit(solution)/shard_map/ppermute | solution.py:122
  53.1 18.9 %collective-permute-start.9 = (bf16[128,2048]{1,0:T(8,128)(2,1)}, bf16[128,2048]{1,0:T(8,128)(2,1)}, u32[]{:S(2)}, u32[]{:S(2)}) collective-permute-start(bf16[128,2048]{1,0:T(8,128)(2,1)} %get-tuple-element.43), channel_id=1, source_target_pairs={{0,4},{4,0},{8,12},{12,8},{1,5},{5,1},{9,13},{13,9},{2,6},{6,2},{1... | collective-permute-start | bytes 1572872 | tf_op jit(solution)/shard_map/ppermute | solution.py:122
  57.4 18.3 %collective-permute-start.18 = (bf16[4,64,2048]{2,1,0:T(8,128)(2,1)}, bf16[4,64,2048]{2,1,0:T(8,128)(2,1)}, u32[]{:S(2)}, u32[]{:S(2)}) collective-permute-start(bf16[4,64,2048]{2,1,0:T(8,128)(2,1)} %pad_maximum_fusion), channel_id=1, source_target_pairs={{0,1},{1,0},{2,3},{3,2},{4,5},{5,4},{6,7},{7,6},{8,9},{9,8},{10,11... | collective-permute-start | bytes 3145736 | tf_op jit(solution)/shard_map/ppermute | solution.py:122
  57.4 9.4 %collective-permute-start.16 = (bf16[64,2048]{1,0:T(8,128)(2,1)}, bf16[64,2048]{1,0:T(8,128)(2,1)}, u32[]{:S(2)}, u32[]{:S(2)}) collective-permute-start(bf16[64,2048]{1,0:T(8,128)(2,1)} %collective-permute-done.15), channel_id=1, source_target_pairs={{0,2},{2,0},{1,3},{3,1},{4,6},{6,4},{5,7},{7,5},{8,10},{10,8},{9,1... | collective-permute-start | bytes 786440 | tf_op jit(solution)/shard_map/ppermute | solution.py:122
  58.9 13.2 %collective-permute-start.12 = (bf16[64,2048]{1,0:T(8,128)(2,1)S(1)}, bf16[64,2048]{1,0:T(8,128)(2,1)}, u32[]{:S(2)}, u32[]{:S(2)}) collective-permute-start(bf16[64,2048]{1,0:T(8,128)(2,1)S(1)} %collective-permute-done.8), channel_id=1, source_target_pairs={{0,2},{2,0},{1,3},{3,1},{4,6},{6,4},{5,7},{7,5},{8,10},{10,8},{9,1... | collective-permute-start | bytes 786440 | tf_op jit(solution)/shard_map/ppermute | solution.py:122
  59.5 13.1 %collective-permute-start.7 = (bf16[128,2176]{1,0:T(8,128)(2,1)S(1)}, bf16[128,2176]{1,0:T(8,128)(2,1)S(1)}, u32[]{:S(2)}, u32[]{:S(2)}) collective-permute-start(bf16[128,2176]{1,0:T(8,128)(2,1)S(1)} %collective-permute-done.1), channel_id=1, source_target_pairs={{0,1},{1,0},{2,3},{3,2},{4,5},{5,4},{6,7},{7,6},{8,9},{9,8},{10,11... | collective-permute-start | bytes 1671176 | tf_op jit(solution)/shard_map/ppermute | solution.py:122
  66.8 8.9 %collective-permute-start.6 = (bf16[24,128,128]{2,1,0:T(8,128)(2,1)S(1)}, bf16[24,128,128]{2,1,0:T(8,128)(2,1)S(1)}, u32[]{:S(2)}, u32[]{:S(2)}) collective-permute-start(bf16[24,128,128]{2,1,0:T(8,128)(2,1)S(1)} %slice.35), channel_id=1, source_target_pairs={{0,1},{1,0},{2,3},{3,2},{4,5},{5,4},{6,7},{7,6},{8,9},{9,8},{10,11... | collective-permute-start | bytes 2359304 | tf_op jit(solution)/shard_map/ppermute | solution.py:122
  73.8 26.2 %collective-permute-start.19 = (bf16[128,2048]{1,0:T(8,128)(2,1)S(1)}, bf16[128,2048]{1,0:T(8,128)(2,1)S(1)}, u32[]{:S(2)}, u32[]{:S(2)}) collective-permute-start(bf16[128,2048]{1,0:T(8,128)(2,1)S(1)} %dynamic-slice_bitcast_fusion), channel_id=1, source_target_pairs={{0,8},{4,12},{8,0},{12,4},{1,9},{5,13},{9,1},{13,5},{2,10},{6,14},... | collective-permute-start | bytes 1572872 | tf_op jit(solution)/shard_map/ppermute | solution.py:122
  120.6 12.6 %collective-permute-start.28 = (bf16[128,2048]{1,0:T(8,128)(2,1)}, bf16[128,2048]{1,0:T(8,128)(2,1)S(1)}, u32[]{:S(2)}, u32[]{:S(2)}) collective-permute-start(bf16[128,2048]{1,0:T(8,128)(2,1)} %get-tuple-element.54.refs_0_), channel_id=1, source_target_pairs={{0,4},{4,0},{8,12},{12,8},{1,5},{5,1},{9,13},{13,9},{2,6},{6,2},{1... | collective-permute-start | bytes 1572872 | tf_op jit(solution)/shard_map/ppermute | solution.py:122
  122.3 12.2 %collective-permute-start.29 = (bf16[128,2048]{1,0:T(8,128)(2,1)}, bf16[128,2048]{1,0:T(8,128)(2,1)S(1)}, u32[]{:S(2)}, u32[]{:S(2)}) collective-permute-start(bf16[128,2048]{1,0:T(8,128)(2,1)} %get-tuple-element.55), channel_id=1, source_target_pairs={{0,2},{2,0},{1,3},{3,1},{4,6},{6,4},{5,7},{7,5},{8,10},{10,8},{9,1... | collective-permute-start | bytes 1572872 | tf_op jit(solution)/shard_map/ppermute | solution.py:122
  123.8 14.2 %collective-permute-start.32 = (bf16[128,2048]{1,0:T(8,128)(2,1)}, bf16[128,2048]{1,0:T(8,128)(2,1)S(1)}, u32[]{:S(2)}, u32[]{:S(2)}) collective-permute-start(bf16[128,2048]{1,0:T(8,128)(2,1)} %get-tuple-element.54.refs_0_), channel_id=1, source_target_pairs={{0,1},{1,0},{2,3},{3,2},{4,5},{5,4},{6,7},{7,6},{8,9},{9,8},{10,11... | collective-permute-start | bytes 1572872 | tf_op jit(solution)/shard_map/ppermute | solution.py:122
  123.8 14.8 %collective-permute-start.33 = (bf16[128,2048]{1,0:T(8,128)(2,1)}, bf16[128,2048]{1,0:T(8,128)(2,1)S(1)}, u32[]{:S(2)}, u32[]{:S(2)}) collective-permute-start(bf16[128,2048]{1,0:T(8,128)(2,1)} %get-tuple-element.55), channel_id=1, source_target_pairs={{0,1},{1,0},{2,3},{3,2},{4,5},{5,4},{6,7},{7,6},{8,9},{9,8},{10,11... | collective-permute-start | bytes 1572872 | tf_op jit(solution)/shard_map/ppermute | solution.py:122
  134.6 14.9 %collective-permute-start.40 = (bf16[128,2048]{1,0:T(8,128)(2,1)S(1)}, bf16[128,2048]{1,0:T(8,128)(2,1)S(1)}, u32[]{:S(2)}, u32[]{:S(2)}) collective-permute-start(bf16[128,2048]{1,0:T(8,128)(2,1)S(1)} %collective-permute-done.29), channel_id=1, source_target_pairs={{0,4},{4,0},{8,12},{12,8},{1,5},{5,1},{9,13},{13,9},{2,6},{6,2},{1... | collective-permute-start | bytes 1572872 | tf_op jit(solution)/shard_map/ppermute | solution.py:122
  134.9 14.9 %collective-permute-start.39 = (bf16[128,2048]{1,0:T(8,128)(2,1)S(1)}, bf16[128,2048]{1,0:T(8,128)(2,1)S(1)}, u32[]{:S(2)}, u32[]{:S(2)}) collective-permute-start(bf16[128,2048]{1,0:T(8,128)(2,1)S(1)} %collective-permute-done.28), channel_id=1, source_target_pairs={{0,2},{2,0},{1,3},{3,1},{4,6},{6,4},{5,7},{7,5},{8,10},{10,8},{9,1... | collective-permute-start | bytes 1572872 | tf_op jit(solution)/shard_map/ppermute | solution.py:122
  136.4 20.5 %collective-permute-start.34 = (bf16[128,2048]{1,0:T(8,128)(2,1)}, bf16[128,2048]{1,0:T(8,128)(2,1)S(1)}, u32[]{:S(2)}, u32[]{:S(2)}) collective-permute-start(bf16[128,2048]{1,0:T(8,128)(2,1)} %get-tuple-element.55), channel_id=1, source_target_pairs={{0,4},{4,0},{8,12},{12,8},{1,5},{5,1},{9,13},{13,9},{2,6},{6,2},{1... | collective-permute-start | bytes 1572872 | tf_op jit(solution)/shard_map/ppermute | solution.py:122
  138.1 19.2 %collective-permute-start.30 = (bf16[128,2048]{1,0:T(8,128)(2,1)}, bf16[128,2048]{1,0:T(8,128)(2,1)S(1)}, u32[]{:S(2)}, u32[]{:S(2)}) collective-permute-start(bf16[128,2048]{1,0:T(8,128)(2,1)} %get-tuple-element.54.refs_0_), channel_id=1, source_target_pairs={{0,2},{2,0},{1,3},{3,1},{4,6},{6,4},{5,7},{7,5},{8,10},{10,8},{9,1... | collective-permute-start | bytes 1572872 | tf_op jit(solution)/shard_map/ppermute | solution.py:122
  138.6 18.8 %collective-permute-start.35 = (bf16[128,2048]{1,0:T(8,128)(2,1)S(1)}, bf16[128,2048]{1,0:T(8,128)(2,1)S(1)}, u32[]{:S(2)}, u32[]{:S(2)}) collective-permute-start(bf16[128,2048]{1,0:T(8,128)(2,1)S(1)} %collective-permute-done.28), channel_id=1, source_target_pairs={{0,1},{1,0},{2,3},{3,2},{4,5},{5,4},{6,7},{7,6},{8,9},{9,8},{10,11... | collective-permute-start | bytes 1572872 | tf_op jit(solution)/shard_map/ppermute | solution.py:122
  149.4 8.3 %collective-permute-start.38 = (bf16[128,2048]{1,0:T(8,128)(2,1)S(1)}, bf16[128,2048]{1,0:T(8,128)(2,1)S(1)}, u32[]{:S(2)}, u32[]{:S(2)}) collective-permute-start(bf16[128,2048]{1,0:T(8,128)(2,1)S(1)} %collective-permute-done.29), channel_id=1, source_target_pairs={{0,1},{1,0},{2,3},{3,2},{4,5},{5,4},{6,7},{7,6},{8,9},{9,8},{10,11... | collective-permute-start | bytes 1572872 | tf_op jit(solution)/shard_map/ppermute | solution.py:122
  149.8 9.2 %collective-permute-start.42 = (bf16[128,2048]{1,0:T(8,128)(2,1)S(1)}, bf16[128,2048]{1,0:T(8,128)(2,1)S(1)}, u32[]{:S(2)}, u32[]{:S(2)}) collective-permute-start(bf16[128,2048]{1,0:T(8,128)(2,1)S(1)} %collective-permute-done.40), channel_id=1, source_target_pairs={{0,1},{1,0},{2,3},{3,2},{4,5},{5,4},{6,7},{7,6},{8,9},{9,8},{10,11... | collective-permute-start | bytes 1572872 | tf_op jit(solution)/shard_map/ppermute | solution.py:122
  157.7 32.7 %collective-permute-start.31 = (bf16[128,2048]{1,0:T(8,128)(2,1)}, bf16[128,2048]{1,0:T(8,128)(2,1)S(1)}, u32[]{:S(2)}, u32[]{:S(2)}) collective-permute-start(bf16[128,2048]{1,0:T(8,128)(2,1)} %get-tuple-element.55), channel_id=1, source_target_pairs={{0,8},{4,12},{8,0},{12,4},{1,9},{5,13},{9,1},{13,5},{2,10},{6,14},... | collective-permute-start | bytes 1572872 | tf_op jit(solution)/shard_map/ppermute | solution.py:122
  177.5 14.2 %collective-permute-start.43 = (bf16[128,2048]{1,0:T(8,128)(2,1)}, bf16[128,2048]{1,0:T(8,128)(2,1)S(1)}, u32[]{:S(2)}, u32[]{:S(2)}) collective-permute-start(bf16[128,2048]{1,0:T(8,128)(2,1)} %get-tuple-element.58.refs_0_), channel_id=1, source_target_pairs={{0,2},{2,0},{1,3},{3,1},{4,6},{6,4},{5,7},{7,5},{8,10},{10,8},{9,1... | collective-permute-start | bytes 1572872 | tf_op jit(solution)/shard_map/ppermute | solution.py:122
  179.0 24.9 %collective-permute-start.45 = (bf16[64,2048]{1,0:T(8,128)(2,1)}, bf16[64,2048]{1,0:T(8,128)(2,1)S(1)}, u32[]{:S(2)}, u32[]{:S(2)}) collective-permute-start(bf16[64,2048]{1,0:T(8,128)(2,1)} %get-tuple-element.61), channel_id=1, source_target_pairs={{0,8},{4,12},{8,0},{12,4},{1,9},{5,13},{9,1},{13,5},{2,10},{6,14},... | collective-permute-start | bytes 786440 | tf_op jit(solution)/shard_map/ppermute | solution.py:122
  191.7 26.2 %collective-permute-start.44 = (bf16[128,2048]{1,0:T(8,128)(2,1)S(1)}, bf16[128,2048]{1,0:T(8,128)(2,1)S(1)}, u32[]{:S(2)}, u32[]{:S(2)}) collective-permute-start(bf16[128,2048]{1,0:T(8,128)(2,1)S(1)} %collective-permute-done.31.refs_2_), channel_id=1, source_target_pairs={{0,2},{2,0},{1,3},{3,1},{4,6},{6,4},{5,7},{7,5},{8,10},{10,8},{9,1... | collective-permute-start | bytes 1572872 | tf_op jit(solution)/shard_map/ppermute | solution.py:122
  205.4 12.5 %collective-permute-start.46 = (bf16[64,2048]{1,0:T(8,128)(2,1)}, bf16[64,2048]{1,0:T(8,128)(2,1)S(1)}, u32[]{:S(2)}, u32[]{:S(2)}) collective-permute-start(bf16[64,2048]{1,0:T(8,128)(2,1)} %get-tuple-element.62), channel_id=1, source_target_pairs={{0,8},{4,12},{8,0},{12,4},{1,9},{5,13},{9,1},{13,5},{2,10},{6,14},... | collective-permute-start | bytes 786440 | tf_op jit(solution)/shard_map/ppermute | solution.py:122
  218.0 7.8 %collective-permute-start.48 = (bf16[64,2048]{1,0:T(8,128)(2,1)S(1)}, bf16[64,2048]{1,0:T(8,128)(2,1)S(1)}, u32[]{:S(2)}, u32[]{:S(2)}) collective-permute-start(bf16[64,2048]{1,0:T(8,128)(2,1)S(1)} %collective-permute-done.46.refs_3_), channel_id=1, source_target_pairs={{0,2},{2,0},{1,3},{3,1},{4,6},{6,4},{5,7},{7,5},{8,10},{10,8},{9,1... | collective-permute-start | bytes 786440 | tf_op jit(solution)/shard_map/ppermute | solution.py:122
  (63 other events, 468.2 us)

commit v7 on v6

--- a/solution.py
+++ b/solution.py
@@ -154,7 +154,7 @@
     return 4 * (z ^ dz) + 2 * (c ^ dc) + (x ^ dx if dx < 2 else dx - 2)
 
 
-def operate_kernel(first, plan, cols, pattern, right_own, right_near, right_far, left_own, *refs):
+def operate_kernel(first, plan, cols, pattern, right_all, left_own, left_other, *refs):
     count = len(plan)
     pieces, refs = refs[:count], refs[count:]
     if first:
@@ -169,7 +169,8 @@
     table = right.shape[1]
     links = table // sectors
     mine = 4 * z + 2 * c + x
-    rows = (mine, mine ^ 8)
+    rows = (mine, mine ^ 12)
+    half = z // 2
 
     copies = []
 
@@ -178,10 +179,9 @@
         copy.start()
         copies.append(copy)
 
-    part = table // 2
-    near, far = pl.ds(c * part, part), pl.ds((1 - c) * part, part)
-    begin(right_own, right.at[0])
+    begin(right_all, right)
     for piece, offsets in zip(pieces, plan):
+        base = 2 * half if piece.shape[0] == 4 else 0
         for at, (dz, dx, dc, start, tall) in enumerate(offsets):
             target = field.at[row_of(dz, dx, dc), pl.ds(start, tall)]
             if dz in (MIX_A, MIX_B):
@@ -192,13 +192,11 @@
                         parts.at[dz - MIX_A],
                     )
             else:
-                begin(piece.at[at], target)
-    begin(right_near.at[pl.ds(0, part)], right.at[1, near])
-    begin(right_far, right.at[1, far])
+                begin(piece.at[base + at], target)
     early = len(copies)
     for at in range(2):
         begin(left_own.at[pl.ds(rows[at] * links, links)], left.at[0, pl.ds(at * links, links)])
-    begin(right_near.at[pl.ds(part, 2 * links)], left.at[1])
+    begin(left_other.at[pl.ds(table // 2, 2 * links)], left.at[1])
     if not first:
         begin(hd_own.at[x], diag.at[0])
         begin(hd_far, diag.at[1])
@@ -212,15 +210,19 @@
         return cols[(2 * term + 1) * table + a * links + j]
 
     def allowed(a, q, value):
-        return jnp.where(pattern[a * sectors + q] != 0, value, jnp.zeros_like(value))
+        return jnp.where(pattern[a, q] != 0, value, jnp.zeros_like(value))
 
     sources = [[left_col(term, rows[at], j) for at in range(2) for j in range(links)] for term in range(2)]
 
     deep = links * block
 
-    def image(b, carry):
+    none = jnp.zeros((block, block), jnp.bfloat16)
+    pair = 2
+
+    def image(n, carry):
+        picks = [(i, j) for i in range(pair) for j in range(links)]
         for term in range(2):
-            found = [right_col(term, b, j) for j in range(links)]
+            found = [right_col(term, n * pair + i, j) for i, j in picks]
             lhs = []
             for source in sources[term]:
                 line = []
@@ -228,25 +230,27 @@
                     value = field[source, :, pl.ds(pl.multiple_of(col * block, block), block)]
                     line.append(allowed(source, col, value) if first else value)
                 lhs.append(jnp.concatenate(line, axis=1))
-            rhs = [right[term, b * links + j] for j in range(links)]
-            product = lax.dot_general(
+            rhs = []
+            for i, j in picks:
+                tile = right[term, (n * pair + i) * links + j]
+                rhs.append(jnp.concatenate([tile if i == at else none for at in range(pair)], axis=1))
+            product = jnp.dot(
                 jnp.concatenate(lhs, axis=0),
-                jnp.concatenate(rhs, axis=1),
-                (((1,), (1,)), ((), ())),
+                jnp.concatenate(rhs, axis=0),
                 preferred_element_type=jnp.float32,
             )
             product = product.astype(jnp.bfloat16)
-            span = pl.ds(pl.multiple_of(b * block, block), block)
+            span = pl.ds(pl.multiple_of(n * pair * block, pair * block), pair * block)
             for at in range(2):
                 images[at, term * deep : (term + 1) * deep, span] = product[at * deep : (at + 1) * deep]
         return carry
 
-    lax.fori_loop(0, sectors, image, 0, unroll=2)
+    lax.fori_loop(0, sectors // pair, image, 0, unroll=2)
     for copy in copies[early:]:
         copy.wait()
 
     step = 2
-    half = block // 2
+    early_rows = block // 2
     zero = jnp.zeros((8, LANES), jnp.float32)
 
     def column(n, sums):
@@ -281,8 +285,8 @@
                 if at == 0:
                     near_out[:, span] = narrow
                 else:
-                    far_out[:, span] = narrow[:half]
-                    late_out[:, span] = narrow[half:]
+                    far_out[:, span] = narrow[:early_rows]
+                    late_out[:, span] = narrow[early_rows:]
                 second = narrow.astype(jnp.float32)
                 wave = psi_in[at, :, span].astype(jnp.float32)
                 sigma_one = weight * wave + off_in[at, :, span].astype(jnp.float32)
@@ -303,8 +307,7 @@
 
 
 def operate(first, plan, pieces, cols, pattern, right, left, extra):
-    right_own, right_near, right_far = right
-    table, block, _ = right_own.shape
+    _, table, block, _ = right.shape
     width = pieces[0].shape[2]
     sectors = width // block
     links = table // sectors
@@ -320,7 +323,7 @@
     return pl.pallas_call(
         functools.partial(operate_kernel, first, plan),
         out_shape=out_shape,
-        in_specs=[SMEM, SMEM] + [ANY] * (4 + len(pieces)) + extra_specs,
+        in_specs=[SMEM, SMEM] + [ANY] * (3 + len(pieces)) + extra_specs,
         out_specs=(VMEM,) * len(out_shape),
         scratch_shapes=[
             pltpu.VMEM((sectors, block, width), jnp.bfloat16),
@@ -338,22 +341,53 @@
             transcendentals=0,
         ),
         name="operate_first" if first else "operate_second",
-    )(cols, pattern, right_own, right_near, right_far, left, *pieces, *extra)
-
-
-def prepare_kernel(
-    pattern, theta, hd, right, left, cols, mix_a, mix_b, own_a, own_b, packed, own_out, waves, diag, sems
-):
+    )(cols, pattern, right, *left, *pieces, *extra)
+
+
+def arrange_kernel(own, near, far, out, found, sems):
+    _, _, c = place()
+    part = far.shape[0]
+    copies = [
+        pltpu.make_async_copy(own, found.at[0], sems.at[0]),
+        pltpu.make_async_copy(near.at[pl.ds(0, part)], found.at[1, pl.ds(c * part, part)], sems.at[1]),
+        pltpu.make_async_copy(far, found.at[1, pl.ds((1 - c) * part, part)], sems.at[2]),
+    ]
+    for copy in copies:
+        copy.start()
+    for copy in copies:
+        copy.wait()
+
+    def turn(at, carry):
+        for term in range(2):
+            out[term, at] = found[term, at].T
+        return carry
+
+    lax.fori_loop(0, found.shape[1], turn, 0, unroll=4)
+
+
+def arrange(own, near, far):
+    shape = (2, *own.shape)
+    return pl.pallas_call(
+        arrange_kernel,
+        out_shape=jax.ShapeDtypeStruct(shape, own.dtype),
+        in_specs=[ANY] * 3,
+        out_specs=VMEM,
+        scratch_shapes=[pltpu.VMEM(shape, own.dtype), pltpu.SemaphoreType.DMA((3,))],
+        compiler_params=pltpu.CompilerParams(vmem_limit_bytes=VMEM_LIMIT),
+        name="arrange",
+    )(own, near, far)
+
+
+def prepare_kernel(pattern, theta, hd, right, left, mix_a, mix_b, packed, own_out, waves, diag, sems):
     z, x, c = place()
     half = z // 2
     middle = in_middle(z)
     mine = 4 * z + 2 * c + x
-    block, width = own_a.shape
+    block, width = diag.shape
     sectors = width // block
     links = right.shape[0] // sectors
     part = right.shape[0] // 2
     root_a = jnp.where(middle, half, 1 - half)
-    last = part + 2 * links
     rows = pl.ds(0, width)
     sources = (
         (theta.at[half, x], waves.at[0]),
@@ -361,11 +395,9 @@
         (hd.at[x], diag),
         (theta.at[root_a, jnp.where(middle, 0, x)], mix_a.at[:, rows]),
         (theta.at[1 - root_a, jnp.where(middle, x, 0)], mix_b.at[:, rows]),
-        (theta.at[half, 0], own_a),
-        (theta.at[half, 1], own_b),
         (right.at[pl.ds(c * part, part)], packed.at[pl.ds(0, part)]),
         (left.at[pl.ds((mine ^ 1) * links, links)], packed.at[pl.ds(part, links)]),
-        (left.at[pl.ds((mine ^ 9) * links, links)], packed.at[pl.ds(part + links, links)]),
+        (left.at[pl.ds((mine ^ 13) * links, links)], packed.at[pl.ds(part + links, links)]),
     )
     copies = [
         pltpu.make_async_copy(source, target, sems.at[at])
@@ -373,8 +405,6 @@
     ]
     for copy in copies:
         copy.start()
-    packed[last] = jnp.zeros_like(packed[last])
-    packed[last, 0 : cols.shape[0], :] = cols[...]
     for copy in copies[:3]:
         copy.wait()
     zero = jnp.zeros((8, LANES), jnp.float32)
@@ -382,7 +412,7 @@
     def column(q, sums):
         span = pl.ds(pl.multiple_of(q * block, block), block)
         weight = diag[:, span].astype(jnp.float32)
-        weight = jnp.where(pattern[mine * sectors + q] != 0, weight, jnp.zeros_like(weight))
+        weight = jnp.where(pattern[mine, q] != 0, weight, jnp.zeros_like(weight))
         found = []
         for root in range(2):
             wave = waves[root, :, span].astype(jnp.float32)
@@ -406,27 +436,26 @@
         copy.wait()
 
 
-def prepare(pattern, theta, hd, right, left, cols):
+def prepare(pattern, theta, hd, right, left):
     _, _, block, width = theta.shape
     table = right.shape[0]
     links = table * block // width
     kind = jnp.bfloat16
     mix = jax.ShapeDtypeStruct((block, width + LANES), kind)
-    one = jax.ShapeDtypeStruct((block, width), kind)
-    packed = jax.ShapeDtypeStruct((table // 2 + 2 * links + 1, block, block), kind)
+    packed = jax.ShapeDtypeStruct((table // 2 + 2 * links, block, block), kind)
     return pl.pallas_call(
         prepare_kernel,
-        out_shape=(mix, mix, one, one, packed, jax.ShapeDtypeStruct((8, LANES), jnp.float32)),
-        in_specs=[SMEM, ANY, ANY, ANY, ANY, VMEM],
-        out_specs=(VMEM,) * 6,
+        out_shape=(mix, mix, packed, jax.ShapeDtypeStruct((8, LANES), jnp.float32)),
+        in_specs=[SMEM, ANY, ANY, ANY, ANY],
+        out_specs=(VMEM,) * 4,
         scratch_shapes=[
             pltpu.VMEM((2, block, width), kind),
             pltpu.VMEM((block, width), kind),
-            pltpu.SemaphoreType.DMA((10,)),
+            pltpu.SemaphoreType.DMA((8,)),
         ],
         compiler_params=pltpu.CompilerParams(vmem_limit_bytes=VMEM_LIMIT),
         name="prepare",
-    )(pattern, theta, hd, right, left, cols)
+    )(pattern, theta, hd, right, left)
 
 
 def total_of(rows):
@@ -552,74 +581,68 @@
 
     halves = theta.reshape(roots, 2, block, width)
     diag = hdiag.reshape(2, block, width)
-    allowed = pattern.reshape(-1)
     chunk = block // 2
+    middle = in_middle(z)
     right = right_blocks.reshape(-1, block, block)
     left = left_blocks.reshape(-1, block, block)
-    table = right.shape[0]
     cols = jnp.concatenate([right_cols.reshape(-1), left_cols.reshape(-1)])
-    spots = jnp.pad(cols, (0, 16 * LANES - cols.shape[0])).reshape(16, LANES).astype(jnp.bfloat16)
-
-    mix_a, mix_b, own_a, own_b, packed, weight_own = prepare(allowed, halves, diag, right, left, spots)
+
+    mix_a, mix_b, packed, weight_own = prepare(pattern, halves, diag, right, left)
     mix_a = lax.ppermute(mix_a, "blk", [(0, 2), (2, 3), (3, 1), (1, 0)])
     mix_b = lax.ppermute(mix_b, "blk", [(0, 1), (1, 3), (3, 2), (2, 0)])
     operators = across(packed, "ops", 1)
-    own_core_a = across(own_a, "sub", 1)
-    own_core_b = across(own_b, "sub", 1)
-
-    mix_a, mix_b = after((mix_a, mix_b), own_core_a, own_core_b)
-    far = [
-        jnp.where(in_middle(z), mix_a[at : at + chunk, :width], mix_b[at : at + chunk, :width])
-        for at in (0, chunk)
-    ]
-    far_z = [across(value, "blk", 1) for value in far]
-    far_x = [across(value, "ops", 1) for value in far]
+    theta_core = across(theta, "sub", 1)
+
+    mix_a, mix_b = after((mix_a, mix_b), theta_core)
+    far = jnp.where(middle, mix_a[:, :width], mix_b[:, :width])
+    far_z = [across(far[at : at + chunk], "blk", 1) for at in (0, chunk)]
+    far_x = across(far, "ops", 1)
     mix_a_core = across(mix_a, "sub", 1)
     mix_b_core = across(mix_b, "sub", 1)
-    operators_core = across(after(operators, mix_b_core)[: table // 2], "sub", 1)
-    found = operators[-1].reshape(-1)[: cols.shape[0]].astype(jnp.int32)
-    cols = jnp.concatenate([cols, found])
-
-    near_b = across(after(own_b, far_z[0]), "blk", 1)
-    far_zx = [across(far_z[0], "ops", 1), across(after(far_z[1], far_x[1]), "ops", 1)]
-    crossed_core = across(jnp.stack([*far_x, *far_z]), "sub", 1)
+
+    own_b = lax.dynamic_slice(halves, (half, 1, 0, 0), (1, 1, block, width))[0, 0]
+    near_b = across(after(own_b, far_z[0], mix_a_core, mix_b_core), "blk", 1)
+    far_zx = [across(value, "ops", 1) for value in far_z]
+    cols_other = across(after(cols, mix_a_core, mix_b_core), "ops", 1)
+    cols = jnp.concatenate([cols, cols_other])
+    operators_core = across(after(operators, far_z[0])[: right.shape[0] // 2], "sub", 1)
+    far_x_core = across(far_x, "sub", 1)
+    far_z_core = [across(value, "sub", 1) for value in far_z]
     hd_far = lax.dynamic_index_in_dim(diag, x, 0, keepdims=False)
-    hd_far = across(after(hd_far, far_z[1]), "blk", 2)
+    hd_far = across(after(hd_far, far_z[1]), "blk", 3)
     far_zx_core = [across(value, "sub", 1) for value in far_zx]
     near_b_core = across(near_b, "sub", 1)
 
-    operators = (right, operators, operators_core)
-    pieces = []
-    plan = []
+    turned = arrange(right, operators, operators_core)
+    left = (left, operators)
+    pieces = [halves.reshape(4, block, width), theta_core.reshape(4, block, width)]
+    plan = [
+        ((0, 2, 0, 0, block), (0, 3, 0, 0, block)),
+        ((0, 2, 1, 0, block), (0, 3, 1, 0, block)),
+    ]
     for piece, offset in (
-        (own_a, (0, 2, 0)),
-        (own_b, (0, 3, 0)),
-        (own_core_a, (0, 2, 1)),
-        (own_core_b, (0, 3, 1)),
         (mix_a, (MIX_A, 0, 0)),
         (mix_b, (MIX_B, 0, 0)),
         (mix_a_core, (MIX_A, 0, 1)),
         (mix_b_core, (MIX_B, 0, 1)),
         (near_b, (1, 3, 0)),
         (near_b_core, (1, 3, 1)),
+        (far_x, (2, 1, 0)),
+        (far_x_core, (2, 1, 1)),
     ):
         pieces.append(piece[None])
         plan.append((offset + (0, block),))
     for at in range(2):
         for piece, offset in (
-            (far_x[at], (2, 1, 0)),
             (far_z[at], (3, 0, 0)),
+            (far_z_core[at], (3, 0, 1)),
             (far_zx[at], (3, 1, 0)),
             (far_zx_core[at], (3, 1, 1)),
         ):
             pieces.append(piece[None])
             plan.append((offset + (at * chunk, chunk),))
-    pieces.append(crossed_core)
-    plan.append(
-        tuple((*offset, 1, at * chunk, chunk) for offset in ((2, 1), (3, 0)) for at in range(2))
-    )
     psi, off_one, stats_one = operate(
-        True, tuple(plan), pieces, cols, allowed, operators, left, (weight_own,)
+        True, tuple(plan), pieces, cols, pattern, turned, left, (weight_own,)
     )
 
     found = share(stats_one)
@@ -653,8 +676,10 @@
     far_x = across(changed_far, "ops", 1)
     near_core = across(changed_near, "sub", 1)
     far_core = across(changed_far, "sub", 1)
-    near_zx = across(after(near_z, far_x), "ops", 1)
-    far_xz = across(after(far_x, near_z), "blk", 1)
+    other_middle = lax.ppermute(changed_far, "blk", [(1, 2), (2, 1)])
+    near_z, far_x = after((near_z, far_x), other_middle)
+    near_zx = across(near_z, "ops", 1)
+    far_xz = across(far_x, "blk", 1)
     near_x = across(after(changed_near, near_z, far_x), "ops", 1)
     far_z = across(after(changed_far, near_z, far_x), "blk", 1)
     near_z_core = across(near_z, "sub", 1)
@@ -663,37 +688,38 @@
     far_z_core = across(far_z, "sub", 1)
     near_zx_core = across(near_zx, "sub", 1)
     far_xz_core = across(far_xz, "sub", 1)
-    other = across(after(changed_far, near_z, far_x), "blk", 2)
+    other_end = lax.ppermute(after(changed_far, near_z, far_x), "blk", [(0, 3), (3, 0)])
     pieces, plan = [], []
     for piece, offset in (
         (changed_near, (0, 0, 0)),
-        (changed_far, (2, 0, 0)),
+        (changed_far, (3, 0, 0)),
         (near_core, (0, 0, 1)),
-        (far_core, (2, 0, 1)),
+        (far_core, (3, 0, 1)),
         (near_z, (1, 0, 0)),
-        (far_z, (3, 0, 0)),
+        (far_z, (2, 0, 0)),
         (near_z_core, (1, 0, 1)),
-        (far_z_core, (3, 0, 1)),
+        (far_z_core, (2, 0, 1)),
         (near_x, (0, 1, 0)),
-        (far_x, (2, 1, 0)),
+        (far_x, (3, 1, 0)),
         (near_x_core, (0, 1, 1)),
-        (far_x_core, (2, 1, 1)),
+        (far_x_core, (3, 1, 1)),
         (near_zx, (1, 1, 0)),
-        (far_xz, (3, 1, 0)),
+        (far_xz, (2, 1, 0)),
         (near_zx_core, (1, 1, 1)),
-        (far_xz_core, (3, 1, 1)),
+        (far_xz_core, (2, 1, 1)),
     ):
         pieces.append(piece[None])
         plan.append((offset + (0, block),))
     two_near, two_far, two_late, stats_three = operate(
-        False, tuple(plan), pieces, cols, allowed, operators, left, (diag, hd_far, psi, off_one, stats_one)
-    )
-
-    far_in = across(two_far, "blk", 2)
+        False, tuple(plan), pieces, cols, pattern, turned, left, (diag, hd_far, psi, off_one, stats_one)
+    )
+
+    other = jnp.where(middle, other_middle, other_end)
+    far_in = across(two_far, "blk", 3)
     near_in = across(two_near, "ops", 1)
-    late_in = across(after(two_late, far_in, near_in), "blk", 2)
+    late_in = across(after(two_late, far_in), "blk", 3)
+    other_x = across(other, "ops", 1)
     far_in_x = across(after(far_in, near_in), "ops", 1)
-    other_x = across(after(other, near_in), "ops", 1)
     late_in_x = across(after(late_in, other_x, far_in_x), "ops", 1)
     sums = stats_three + across(stats_three, "sub", 1)
     sums = sums + across(sums, "blk", 1)

time: 229 us -> 236 us (1.031)
  starting transfers between devices: 41.5 us -> 48.6 us
  waiting for transfers between devices: 119 us -> 115 us
  Pallas kernels: 53.4 us -> 56.3 us
  local copies, waits for them, and re-layouts: 6.88 us -> 9.27 us
    ppermute x45, waiting for transfers between devices: 91.5 us -> 84.1 us  [across(): return lax.ppermute(value, axis, [(i, i ^ distance) for i in range(size)])]
    pallas_call x1 -> x2, Pallas kernels: 4.72 us -> 9.27 us  [the longest x1 4.98 us: arrange(): pl.pallas_call(arrange_kernel, out_shape=jax.ShapeDtypeStruct(shape, own....]
    ppermute x0 -> x2, starting transfers between devices: none -> 3.85 us  [the longest x1 3.17 us: shards(): lax.ppermute(after(changed_far, near_z, far_x), 'blk', [(0, 3), (3, 0)])]
    ppermute x45, starting transfers between devices: 30.5 us -> 34.2 us  [across(): return lax.ppermute(value, axis, [(i, i ^ distance) for i in range(size)])]
    unnamed x86 -> x92, local copies, waits for them, and re-layouts: 5.27 us -> 6.13 us
  transfers between devices with their start and end apart: 53 -> 55, of which waited for: 35 -> 27; matrix products, arithmetic and copies ran while one was open for 2% -> 3% of each run, Pallas kernels for 17% -> 19%
where the time goes in v7:
time: 236 us; the launch traced here: 235 us
  waiting for transfers between devices  115 us (49%)
  Pallas kernels  56.3 us (24%)
  starting transfers between devices  48.6 us (21%)
  local copies, waits for them, and re-layouts  9.27 us (4%)
  other arithmetic  4.82 us (2%)
    ppermute x45, waiting for transfers between devices, across(): return lax.ppermute(value, axis, [(i, i ^ distance) for i in range(size)])  84.1 us
    ppermute x45, starting transfers between devices, across(): return lax.ppermute(value, axis, [(i, i ^ distance) for i in range(size)])  34.2 us
    pallas_call x2, Pallas kernels, operate(): pl.pallas_call(functools.partial(operate_kernel, first, plan), out_shape=...  30.4 us
    ppermute x1, waiting for transfers between devices, shards(): mix_b = lax.ppermute(mix_b, 'blk', [(0, 1), (1, 3), (3, 2), (2, 0)])  13.2 us
    ppermute x1, waiting for transfers between devices, shards(): mix_a = lax.ppermute(mix_a, 'blk', [(0, 2), (2, 3), (3, 1), (1, 0)])  11.9 us
    pallas_call x3, Pallas kernels, assemble(): pl.pallas_call(functools.partial(assemble_kernel, places, len(based)), ou...  7.2 us
    ppermute x6, starting transfers between devices, share(): lax.ppermute(pair, axes, [(i, i ^ distance) for i in range(count)])  6.98 us
    ppermute x6, waiting for transfers between devices, share(): lax.ppermute(pair, axes, [(i, i ^ distance) for i in range(count)])  6.16 us
  transfers between devices with their start and end apart: 55, of which 27 were waited for; matrix products, arithmetic and copies ran while one was open for 3% of the time, Pallas kernels for 19%

profile of v7, /device:TPU:0, one launch (start us, length us, event | category | flops | bytes accessed | tf_op | source)
XLA Modules:
  0.0 235.5 jit_solution(13698369711472090736)
XLA Ops:
  1.1 4.3 %prepare.1 = (bf16[128,2176]{1,0:T(8,128)(2,1)}, bf16[128,2176]{1,0:T(8,128)(2,1)}, bf16[30,128,128]{2,1,0:T(8,128)(2,1)}, f32[8,128]{1,0:T(8,128)}) custom-call(s32[16,16]{1,0:T(8,128)} %pattern.5, bf16[2,2,128,2048]{3,2,1,0:T(8,128)(2,1)} %bitcast.58, bf16[2,128,2048]{2,1,0:T(8,128)(2,1)} %bitcast.54, bf16[48,128,128]{2,1,0:T(8,128)(2,1)} %bitcast.62, ...), custom_call_target="tpu_custom_call" | custom-call | tf_op jit(solution)/shard_map/prepare/pallas_call | solution.py:446
  5.4 3.6 %collective-permute-start = (bf16[128,2176]{1,0:T(8,128)(2,1)}, bf16[128,2176]{1,0:T(8,128)(2,1)S(1)}, u32[]{:S(2)}, u32[]{:S(2)}) collective-permute-start(bf16[128,2176]{1,0:T(8,128)(2,1)} %get-tuple-element.32), channel_id=1, source_target_pairs={{0,8},{8,12},{12,4},{4,0},{1,9},{9,13},{13,5},{5,1},{2,10},{10,14}... | collective-permute-start | bytes 1671176 | tf_op jit(solution)/shard_map/ppermute | solution.py:591
  10.4 11.9 %collective-permute-done = bf16[128,2176]{1,0:T(8,128)(2,1)S(1)} collective-permute-done((bf16[128,2176]{1,0:T(8,128)(2,1)}, bf16[128,2176]{1,0:T(8,128)(2,1)S(1)}, u32[]{:S(2)}, u32[]{:S(2)}) %collective-permute-start) | collective-permute-done | bytes 557088 | tf_op jit(solution)/shard_map/ppermute | solution.py:591
  22.4 13.2 %collective-permute-done.1 = bf16[128,2176]{1,0:T(8,128)(2,1)S(1)} collective-permute-done((bf16[128,2176]{1,0:T(8,128)(2,1)}, bf16[128,2176]{1,0:T(8,128)(2,1)S(1)}, u32[]{:S(2)}, u32[]{:S(2)}) %collective-permute-start.1) | collective-permute-done | bytes 557088 | tf_op jit(solution)/shard_map/ppermute | solution.py:592
  40.9 6.3 %collective-permute-done.7 = bf16[64,2048]{1,0:T(8,128)(2,1)S(1)} collective-permute-done((bf16[64,2048]{1,0:T(8,128)(2,1)}, bf16[64,2048]{1,0:T(8,128)(2,1)S(1)}, u32[]{:S(2)}, u32[]{:S(2)}) %collective-permute-start.7) | collective-permute-done | bytes 262176 | tf_op jit(solution)/shard_map/ppermute | solution.py:122
  54.3 13.6 %collective-permute-done.14 = bf16[64,2048]{1,0:T(8,128)(2,1)S(1)} collective-permute-done((bf16[64,2048]{1,0:T(8,128)(2,1)S(1)}, bf16[64,2048]{1,0:T(8,128)(2,1)S(1)}, u32[]{:S(2)}, u32[]{:S(2)}) %collective-permute-start.14) | collective-permute-done | bytes 262176 | tf_op jit(solution)/shard_map/ppermute | solution.py:122
  67.9 2.9 %collective-permute-done.18 = bf16[64,2048]{1,0:T(8,128)(2,1)S(1)} collective-permute-done((bf16[64,2048]{1,0:T(8,128)(2,1)}, bf16[64,2048]{1,0:T(8,128)(2,1)S(1)}, u32[]{:S(2)}, u32[]{:S(2)}) %collective-permute-start.18) | collective-permute-done | bytes 262176 | tf_op jit(solution)/shard_map/ppermute | solution.py:122
  75.5 2.5 %collective-permute-start.20 = (bf16[128,2048]{1,0:T(8,128)(2,1)S(1)}, bf16[128,2048]{1,0:T(8,128)(2,1)S(1)}, u32[]{:S(2)}, u32[]{:S(2)}) collective-permute-start(bf16[128,2048]{1,0:T(8,128)(2,1)S(1)} %dynamic-slice_bitcast_fusion), channel_id=1, source_target_pairs={{0,12},{4,8},{8,4},{12,0},{1,13},{5,9},{9,5},{13,1},{2,14},{6,10},... | collective-permute-start | bytes 1572872 | tf_op jit(solution)/shard_map/ppermute | solution.py:122
  78.7 5.0 %arrange.1.right_all = bf16[2,48,128,128]{3,2,1,0:T(8,128)(2,1)} custom-call(bf16[48,128,128]{2,1,0:T(8,128)(2,1)} %bitcast.63, bf16[30,128,128]{2,1,0:T(8,128)(2,1)} %copy-done, bf16[24,128,128]{2,1,0:T(8,128)(2,1)} %collective-permute-done.8.far), custom_call_target="tpu_custom_call" | custom-call | tf_op jit(solution)/shard_map/arrange/pallas_call | solution.py:370
  84.9 14.8 %operate_first.1 = (bf16[2,128,2048]{2,1,0:T(8,128)(2,1)}, bf16[2,128,2048]{2,1,0:T(8,128)(2,1)}, f32[8,128]{1,0:T(8,128)}) custom-call(s32[192]{0:T(256)} %pad_add_fusion.cols, s32[16,16]{1,0:T(8,128)} %pattern.5, bf16[2,48,128,128]{3,2,1,0:T(8,128)(2,1)} %arrange.1.right_all, bf16[48,128,128]{2,1,0:T(8,128)(2,1)} %bitcast.52, ...), custom_call_target="tpu_custom_call" | custom-call | flops 3221225472 | bytes 16777216 | tf_op jit(solution)/shard_map/operate_first/pallas_call | solution.py:323
  103.3 2.0 collective-permute-start.24
  108.4 5.9 %update.1 = (f32[2,128,2048]{2,1,0:T(8,128)}, f32[8,128]{1,0:T(8,128)}) custom-call(bf16[2,128,2048]{2,1,0:T(8,128)(2,1)} %get-tuple-element.41.psi.refs_18_, bf16[2,128,2048]{2,1,0:T(8,128)(2,1)} %get-tuple-element.42.off.refs_19_, bf16[2,128,2048]{2,1,0:T(8,128)(2,1)} %bitcast.55, bf16[128,2048]{1,0:T(8,128)(2,1)} %copy-done.4, f32[2,8,128]{2,1,0:T(8,128)} %copy-done.34, ...), custom_call_target="tpu_custom_call" | custom-call | tf_op jit(solution)/shard_map/update/pallas_call | solution.py:649
  117.1 1.9 collective-permute-start.27
  120.8 2.8 %collective-permute-done.28.refs_3_ = f32[2,8,128]{2,1,0:T(8,128)S(1)} collective-permute-done((f32[2,8,128]{2,1,0:T(8,128)S(1)}, f32[2,8,128]{2,1,0:T(8,128)S(1)}, u32[]{:S(2)}, u32[]{:S(2)}) %collective-permute-start.28) | collective-permute-done | bytes 8224 | tf_op jit(solution)/shard_map/ppermute | solution.py:131
  124.2 3.4 %correct.1 = (bf16[128,2048]{1,0:T(8,128)(2,1)}, bf16[128,2048]{1,0:T(8,128)(2,1)}) custom-call(bf16[2,128,2048]{2,1,0:T(8,128)(2,1)} %get-tuple-element.41.psi.refs_18_, f32[2,128,2048]{2,1,0:T(8,128)} %get-tuple-element.45.t, f32[2,8,128]{2,1,0:T(8,128)} %copy-done.35, f32[2,8,128]{2,1,0:T(8,128)} %copy-done.38, f32[2,8,128]{2,1,0:T(8,128)} %copy-done.40, ...), custom_call_target="tpu_custom_call" | custom-call | tf_op jit(solution)/shard_map/correct/pallas_call | solution.py:666
  130.4 9.8 %collective-permute-done.29 = bf16[128,2048]{1,0:T(8,128)(2,1)S(1)} collective-permute-done((bf16[128,2048]{1,0:T(8,128)(2,1)}, bf16[128,2048]{1,0:T(8,128)(2,1)S(1)}, u32[]{:S(2)}, u32[]{:S(2)}) %collective-permute-start.29) | collective-permute-done | bytes 524320 | tf_op jit(solution)/shard_map/ppermute | solution.py:122
  140.2 4.7 %collective-permute-start.37 = (bf16[128,2048]{1,0:T(8,128)(2,1)}, bf16[128,2048]{1,0:T(8,128)(2,1)S(1)}, u32[]{:S(2)}, u32[]{:S(2)}) collective-permute-start(bf16[128,2048]{1,0:T(8,128)(2,1)} %get-tuple-element.52), channel_id=1, source_target_pairs={{0,4},{4,0},{8,12},{12,8},{1,5},{5,1},{9,13},{13,9},{2,6},{6,2},{1... | collective-permute-start | bytes 1572872 | tf_op jit(solution)/shard_map/ppermute | solution.py:122
  147.1 10.9 %collective-permute-done.37 = bf16[128,2048]{1,0:T(8,128)(2,1)S(1)} collective-permute-done((bf16[128,2048]{1,0:T(8,128)(2,1)}, bf16[128,2048]{1,0:T(8,128)(2,1)S(1)}, u32[]{:S(2)}, u32[]{:S(2)}) %collective-permute-start.37) | collective-permute-done | bytes 524320 | tf_op jit(solution)/shard_map/ppermute | solution.py:122
  158.0 2.0 collective-permute-done.32.refs_1_
  160.0 6.9 %collective-permute-done.42 = bf16[128,2048]{1,0:T(8,128)(2,1)S(1)} collective-permute-done((bf16[128,2048]{1,0:T(8,128)(2,1)S(1)}, bf16[128,2048]{1,0:T(8,128)(2,1)S(1)}, u32[]{:S(2)}, u32[]{:S(2)}) %collective-permute-start.42) | collective-permute-done | bytes 524320 | tf_op jit(solution)/shard_map/ppermute | solution.py:122
  167.5 3.2 %collective-permute-start.33 = (bf16[128,2048]{1,0:T(8,128)(2,1)}, bf16[128,2048]{1,0:T(8,128)(2,1)}, u32[]{:S(2)}, u32[]{:S(2)}) collective-permute-start(bf16[128,2048]{1,0:T(8,128)(2,1)} %get-tuple-element.52), channel_id=1, source_target_pairs={{0,12},{12,0},{1,13},{13,1},{2,14},{14,2},{3,15},{15,3},{16,28},{2... | collective-permute-start | bytes 1572872 | tf_op jit(solution)/shard_map/ppermute | solution.py:691
  172.0 15.6 %operate_second.1 = (bf16[128,2048]{1,0:T(8,128)(2,1)}, bf16[64,2048]{1,0:T(8,128)(2,1)}, bf16[64,2048]{1,0:T(8,128)(2,1)}, f32[8,128]{1,0:T(8,128)}) custom-call(s32[192]{0:T(256)} %pad_add_fusion.cols, s32[16,16]{1,0:T(8,128)} %pattern.5, bf16[2,48,128,128]{3,2,1,0:T(8,128)(2,1)} %arrange.1.right_all, bf16[48,128,128]{2,1,0:T(8,128)(2,1)} %bitcast.53, ...), custom_call_target="tpu_custom_call" | custom-call | bytes 1024 | tf_op jit(solution)/shard_map/operate_second/pallas_call | solution.py:323
  190.9 2.6 %collective-permute-start.46 = (bf16[64,2048]{1,0:T(8,128)(2,1)}, bf16[64,2048]{1,0:T(8,128)(2,1)S(1)}, u32[]{:S(2)}, u32[]{:S(2)}) collective-permute-start(bf16[64,2048]{1,0:T(8,128)(2,1)} %get-tuple-element.54), channel_id=1, source_target_pairs={{0,12},{4,8},{8,4},{12,0},{1,13},{5,9},{9,5},{13,1},{2,14},{6,10},... | collective-permute-start | bytes 786440 | tf_op jit(solution)/shard_map/ppermute | solution.py:122
  195.6 3.9 %collective-permute-done.52 = f32[8,128]{1,0:T(8,128)S(1)} collective-permute-done((f32[8,128]{1,0:T(8,128)S(1)}, f32[8,128]{1,0:T(8,128)S(1)}, u32[]{:S(2)}, u32[]{:S(2)}) %collective-permute-start.52) | collective-permute-done | bytes 4128 | tf_op jit(solution)/shard_map/ppermute | solution.py:122
  199.5 2.0 collective-permute-start.53
  201.5 2.5 %collective-permute-done.53 = f32[8,128]{1,0:T(8,128)S(1)} collective-permute-done((f32[8,128]{1,0:T(8,128)S(1)}, f32[8,128]{1,0:T(8,128)S(1)}, u32[]{:S(2)}, u32[]{:S(2)}) %collective-permute-start.53) | collective-permute-done | bytes 4128 | tf_op jit(solution)/shard_map/ppermute | solution.py:122
  204.6 8.6 %collective-permute-done.34.refs_3_ = bf16[128,2048]{1,0:T(8,128)(2,1)S(1)} collective-permute-done((bf16[128,2048]{1,0:T(8,128)(2,1)S(1)}, bf16[128,2048]{1,0:T(8,128)(2,1)S(1)}, u32[]{:S(2)}, u32[]{:S(2)}) %collective-permute-start.34) | collective-permute-done | bytes 524320 | tf_op jit(solution)/shard_map/ppermute | solution.py:122
  214.1 2.9 %assemble.3 = bf16[2,2,128,2048]{3,2,1,0:T(8,128)(2,1)} custom-call(bf16[128,2048]{1,0:T(8,128)(2,1)} %get-tuple-element.51.refs_0_, bf16[128,2048]{1,0:T(8,128)(2,1)} %copy-done.6, bf16[128,2048]{1,0:T(8,128)(2,1)} %copy-done.7, bf16[128,2048]{1,0:T(8,128)(2,1)} %copy-done.24), custom_call_target="tpu_custom_call" | custom-call | tf_op jit(solution)/shard_map/assemble/pallas_call | solution.py:558
  217.0 2.6 %collective-permute-start.47 = (bf16[64,2048]{1,0:T(8,128)(2,1)S(1)}, bf16[64,2048]{1,0:T(8,128)(2,1)S(1)}, u32[]{:S(2)}, u32[]{:S(2)}) collective-permute-start(bf16[64,2048]{1,0:T(8,128)(2,1)S(1)} %copy-done.44), channel_id=1, source_target_pairs={{0,12},{4,8},{8,4},{12,0},{1,13},{5,9},{9,5},{13,1},{2,14},{6,10},... | collective-permute-start | bytes 786440 | tf_op jit(solution)/shard_map/ppermute | solution.py:122
  220.2 6.2 %collective-permute-done.47.refs_3_ = bf16[64,2048]{1,0:T(8,128)(2,1)S(1)} collective-permute-done((bf16[64,2048]{1,0:T(8,128)(2,1)S(1)}, bf16[64,2048]{1,0:T(8,128)(2,1)S(1)}, u32[]{:S(2)}, u32[]{:S(2)}) %collective-permute-start.47) | collective-permute-done | bytes 262176 | tf_op jit(solution)/shard_map/ppermute | solution.py:122
  228.1 2.7 %assemble.4.refs_1_ = bf16[2,2,128,2048]{3,2,1,0:T(8,128)(2,1)} custom-call(bf16[128,2048]{1,0:T(8,128)(2,1)} %get-tuple-element.56.refs_0_, bf16[128,2048]{1,0:T(8,128)(2,1)} %copy-done.10, bf16[64,2048]{1,0:T(8,128)(2,1)} %copy-done.31, bf16[64,2048]{1,0:T(8,128)(2,1)} %copy-done.32, bf16[64,2048]{1,0:T(8,128)(2,1)} %copy-done.33), custom_call_target="tpu_custom_call" | custom-call | tf_op jit(solution)/shard_map/assemble/pallas_call | solution.py:558
  230.8 2.3 collective-permute-done.50.refs_0_
  (199 shorter events, 50.8 us)
Async XLA Ops:
  0.6 34.9 %collective-permute-start.2 = (bf16[2,256,2048]{2,1,0:T(8,128)(2,1)}, bf16[2,256,2048]{2,1,0:T(8,128)(2,1)}, u32[]{:S(2)}, u32[]{:S(2)}) collective-permute-start(bf16[2,256,2048]{2,1,0:T(8,128)(2,1)} %param.7), channel_id=1, source_target_pairs={{0,1},{1,0},{2,3},{3,2},{4,5},{5,4},{6,7},{7,6},{8,9},{9,8},{10,11... | collective-permute-start | bytes 6291464 | tf_op jit(solution)/shard_map/ppermute | solution.py:122
  5.4 16.9 %collective-permute-start = (bf16[128,2176]{1,0:T(8,128)(2,1)}, bf16[128,2176]{1,0:T(8,128)(2,1)S(1)}, u32[]{:S(2)}, u32[]{:S(2)}) collective-permute-start(bf16[128,2176]{1,0:T(8,128)(2,1)} %get-tuple-element.32), channel_id=1, source_target_pairs={{0,8},{8,12},{12,4},{4,0},{1,9},{9,13},{13,5},{5,1},{2,10},{10,14}... | collective-permute-start | bytes 1671176 | tf_op jit(solution)/shard_map/ppermute | solution.py:591
  9.1 26.5 %collective-permute-start.1 = (bf16[128,2176]{1,0:T(8,128)(2,1)}, bf16[128,2176]{1,0:T(8,128)(2,1)S(1)}, u32[]{:S(2)}, u32[]{:S(2)}) collective-permute-start(bf16[128,2176]{1,0:T(8,128)(2,1)} %get-tuple-element.33), channel_id=1, source_target_pairs={{0,4},{4,12},{12,8},{8,0},{1,5},{5,13},{13,9},{9,1},{2,6},{6,14},{... | collective-permute-start | bytes 1671176 | tf_op jit(solution)/shard_map/ppermute | solution.py:592
  9.1 40.3 %collective-permute-start.6 = (bf16[30,128,128]{2,1,0:T(8,128)(2,1)}, bf16[30,128,128]{2,1,0:T(8,128)(2,1)S(1)}, u32[]{:S(2)}, u32[]{:S(2)}) collective-permute-start(bf16[30,128,128]{2,1,0:T(8,128)(2,1)} %get-tuple-element.37), channel_id=1, source_target_pairs={{0,2},{2,0},{1,3},{3,1},{4,6},{6,4},{5,7},{7,5},{8,10},{10,8},{9,1... | collective-permute-start | bytes 2949128 | tf_op jit(solution)/shard_map/ppermute | solution.py:122
  35.6 13.0 %collective-permute-start.3 = (bf16[128,2176]{1,0:T(8,128)(2,1)S(1)}, bf16[128,2176]{1,0:T(8,128)(2,1)}, u32[]{:S(2)}, u32[]{:S(2)}) collective-permute-start(bf16[128,2176]{1,0:T(8,128)(2,1)S(1)} %collective-permute-done), channel_id=1, source_target_pairs={{0,1},{1,0},{2,3},{3,2},{4,5},{5,4},{6,7},{7,6},{8,9},{9,8},{10,11... | collective-permute-start | bytes 1671176 | tf_op jit(solution)/shard_map/ppermute | solution.py:122
  35.6 13.0 %collective-permute-start.4 = (bf16[128,2176]{1,0:T(8,128)(2,1)S(1)}, bf16[128,2176]{1,0:T(8,128)(2,1)}, u32[]{:S(2)}, u32[]{:S(2)}) collective-permute-start(bf16[128,2176]{1,0:T(8,128)(2,1)S(1)} %collective-permute-done.1), channel_id=1, source_target_pairs={{0,1},{1,0},{2,3},{3,2},{4,5},{5,4},{6,7},{7,6},{8,9},{9,8},{10,11... | collective-permute-start | bytes 1671176 | tf_op jit(solution)/shard_map/ppermute | solution.py:122
  38.5 14.4 %collective-permute-start.16 = (bf16[64,2048]{1,0:T(8,128)(2,1)}, bf16[64,2048]{1,0:T(8,128)(2,1)}, u32[]{:S(2)}, u32[]{:S(2)}) collective-permute-start(bf16[64,2048]{1,0:T(8,128)(2,1)} %get-tuple-element.61), channel_id=1, source_target_pairs={{0,4},{4,0},{8,12},{12,8},{1,5},{5,1},{9,13},{13,9},{2,6},{6,2},{1... | collective-permute-start | bytes 786440 | tf_op jit(solution)/shard_map/ppermute | solution.py:122
  47.2 23.6 %collective-permute-start.11 = (bf16[128,2048]{1,0:T(8,128)(2,1)}, bf16[128,2048]{1,0:T(8,128)(2,1)}, u32[]{:S(2)}, u32[]{:S(2)}) collective-permute-start(bf16[128,2048]{1,0:T(8,128)(2,1)} %copy-done.5), channel_id=1, source_target_pairs={{0,2},{2,0},{1,3},{3,1},{4,6},{6,4},{5,7},{7,5},{8,10},{10,8},{9,1... | collective-permute-start | bytes 1572872 | tf_op jit(solution)/shard_map/ppermute | solution.py:122
  48.6 22.7 %collective-permute-start.9 = (bf16[128,2048]{1,0:T(8,128)(2,1)S(1)}, bf16[128,2048]{1,0:T(8,128)(2,1)}, u32[]{:S(2)}, u32[]{:S(2)}) collective-permute-start(bf16[128,2048]{1,0:T(8,128)(2,1)S(1)} %dynamic-slice_bitcast_fusion.1), channel_id=1, source_target_pairs={{0,4},{4,0},{8,12},{12,8},{1,5},{5,1},{9,13},{13,9},{2,6},{6,2},{1... | collective-permute-start | bytes 1572872 | tf_op jit(solution)/shard_map/ppermute | solution.py:122
  50.4 25.2 %collective-permute-start.8 = (bf16[24,128,128]{2,1,0:T(8,128)(2,1)}, bf16[24,128,128]{2,1,0:T(8,128)(2,1)}, u32[]{:S(2)}, u32[]{:S(2)}) collective-permute-start(bf16[24,128,128]{2,1,0:T(8,128)(2,1)} %slice.30), channel_id=1, source_target_pairs={{0,1},{1,0},{2,3},{3,2},{4,5},{5,4},{6,7},{7,6},{8,9},{9,8},{10,11... | collective-permute-start | bytes 2359304 | tf_op jit(solution)/shard_map/ppermute | solution.py:122
  50.4 17.5 %collective-permute-start.14 = (bf16[64,2048]{1,0:T(8,128)(2,1)S(1)}, bf16[64,2048]{1,0:T(8,128)(2,1)S(1)}, u32[]{:S(2)}, u32[]{:S(2)}) collective-permute-start(bf16[64,2048]{1,0:T(8,128)(2,1)S(1)} %collective-permute-done.7), channel_id=1, source_target_pairs={{0,2},{2,0},{1,3},{3,1},{4,6},{6,4},{5,7},{7,5},{8,10},{10,8},{9,1... | collective-permute-start | bytes 786440 | tf_op jit(solution)/shard_map/ppermute | solution.py:122
  52.9 17.9 %collective-permute-start.18 = (bf16[64,2048]{1,0:T(8,128)(2,1)}, bf16[64,2048]{1,0:T(8,128)(2,1)S(1)}, u32[]{:S(2)}, u32[]{:S(2)}) collective-permute-start(bf16[64,2048]{1,0:T(8,128)(2,1)} %collective-permute-done.16), channel_id=1, source_target_pairs={{0,2},{2,0},{1,3},{3,1},{4,6},{6,4},{5,7},{7,5},{8,10},{10,8},{9,1... | collective-permute-start | bytes 786440 | tf_op jit(solution)/shard_map/ppermute | solution.py:122
  70.8 13.0 %collective-permute-start.12 = (bf16[128,2048]{1,0:T(8,128)(2,1)}, bf16[128,2048]{1,0:T(8,128)(2,1)S(1)}, u32[]{:S(2)}, u32[]{:S(2)}) collective-permute-start(bf16[128,2048]{1,0:T(8,128)(2,1)} %collective-permute-done.11), channel_id=1, source_target_pairs={{0,1},{1,0},{2,3},{3,2},{4,5},{5,4},{6,7},{7,6},{8,9},{9,8},{10,11... | collective-permute-start | bytes 1572872 | tf_op jit(solution)/shard_map/ppermute | solution.py:122
  71.5 12.3 %collective-permute-start.10 = (bf16[128,2048]{1,0:T(8,128)(2,1)}, bf16[128,2048]{1,0:T(8,128)(2,1)S(1)}, u32[]{:S(2)}, u32[]{:S(2)}) collective-permute-start(bf16[128,2048]{1,0:T(8,128)(2,1)} %collective-permute-done.9), channel_id=1, source_target_pairs={{0,1},{1,0},{2,3},{3,2},{4,5},{5,4},{6,7},{7,6},{8,9},{9,8},{10,11... | collective-permute-start | bytes 1572872 | tf_op jit(solution)/shard_map/ppermute | solution.py:122
  73.4 10.4 %collective-permute-start.15 = (bf16[64,2048]{1,0:T(8,128)(2,1)}, bf16[64,2048]{1,0:T(8,128)(2,1)S(1)}, u32[]{:S(2)}, u32[]{:S(2)}) collective-permute-start(bf16[64,2048]{1,0:T(8,128)(2,1)} %copy-done.26), channel_id=1, source_target_pairs={{0,1},{1,0},{2,3},{3,2},{4,5},{5,4},{6,7},{7,6},{8,9},{9,8},{10,11... | collective-permute-start | bytes 786440 | tf_op jit(solution)/shard_map/ppermute | solution.py:122
  75.5 29.7 %collective-permute-start.20 = (bf16[128,2048]{1,0:T(8,128)(2,1)S(1)}, bf16[128,2048]{1,0:T(8,128)(2,1)S(1)}, u32[]{:S(2)}, u32[]{:S(2)}) collective-permute-start(bf16[128,2048]{1,0:T(8,128)(2,1)S(1)} %dynamic-slice_bitcast_fusion), channel_id=1, source_target_pairs={{0,12},{4,8},{8,4},{12,0},{1,13},{5,9},{9,5},{13,1},{2,14},{6,10},... | collective-permute-start | bytes 1572872 | tf_op jit(solution)/shard_map/ppermute | solution.py:122
  127.6 12.5 %collective-permute-start.29 = (bf16[128,2048]{1,0:T(8,128)(2,1)}, bf16[128,2048]{1,0:T(8,128)(2,1)S(1)}, u32[]{:S(2)}, u32[]{:S(2)}) collective-permute-start(bf16[128,2048]{1,0:T(8,128)(2,1)} %get-tuple-element.51.refs_0_), channel_id=1, source_target_pairs={{0,4},{4,0},{8,12},{12,8},{1,5},{5,1},{9,13},{13,9},{2,6},{6,2},{1... | collective-permute-start | bytes 1572872 | tf_op jit(solution)/shard_map/ppermute | solution.py:122
  127.7 12.5 %collective-permute-start.30 = (bf16[128,2048]{1,0:T(8,128)(2,1)}, bf16[128,2048]{1,0:T(8,128)(2,1)S(1)}, u32[]{:S(2)}, u32[]{:S(2)}) collective-permute-start(bf16[128,2048]{1,0:T(8,128)(2,1)} %get-tuple-element.52), channel_id=1, source_target_pairs={{0,2},{2,0},{1,3},{3,1},{4,6},{6,4},{5,7},{7,5},{8,10},{10,8},{9,1... | collective-permute-start | bytes 1572872 | tf_op jit(solution)/shard_map/ppermute | solution.py:122
  129.1 11.1 %collective-permute-start.31 = (bf16[128,2048]{1,0:T(8,128)(2,1)}, bf16[128,2048]{1,0:T(8,128)(2,1)S(1)}, u32[]{:S(2)}, u32[]{:S(2)}) collective-permute-start(bf16[128,2048]{1,0:T(8,128)(2,1)} %get-tuple-element.52), channel_id=1, source_target_pairs={{4,8},{8,4},{5,9},{9,5},{6,10},{10,6},{7,11},{11,7},{20,24},{24,20... | collective-permute-start | bytes 1572872 | tf_op jit(solution)/shard_map/ppermute | solution.py:679
  129.8 17.2 %collective-permute-start.35 = (bf16[128,2048]{1,0:T(8,128)(2,1)}, bf16[128,2048]{1,0:T(8,128)(2,1)S(1)}, u32[]{:S(2)}, u32[]{:S(2)}) collective-permute-start(bf16[128,2048]{1,0:T(8,128)(2,1)} %get-tuple-element.51.refs_0_), channel_id=1, source_target_pairs={{0,1},{1,0},{2,3},{3,2},{4,5},{5,4},{6,7},{7,6},{8,9},{9,8},{10,11... | collective-permute-start | bytes 1572872 | tf_op jit(solution)/shard_map/ppermute | solution.py:122
  129.9 17.1 %collective-permute-start.36 = (bf16[128,2048]{1,0:T(8,128)(2,1)}, bf16[128,2048]{1,0:T(8,128)(2,1)S(1)}, u32[]{:S(2)}, u32[]{:S(2)}) collective-permute-start(bf16[128,2048]{1,0:T(8,128)(2,1)} %get-tuple-element.52), channel_id=1, source_target_pairs={{0,1},{1,0},{2,3},{3,2},{4,5},{5,4},{6,7},{7,6},{8,9},{9,8},{10,11... | collective-permute-start | bytes 1572872 | tf_op jit(solution)/shard_map/ppermute | solution.py:122
  140.2 17.8 %collective-permute-start.37 = (bf16[128,2048]{1,0:T(8,128)(2,1)}, bf16[128,2048]{1,0:T(8,128)(2,1)S(1)}, u32[]{:S(2)}, u32[]{:S(2)}) collective-permute-start(bf16[128,2048]{1,0:T(8,128)(2,1)} %get-tuple-element.52), channel_id=1, source_target_pairs={{0,4},{4,0},{8,12},{12,8},{1,5},{5,1},{9,13},{13,9},{2,6},{6,2},{1... | collective-permute-start | bytes 1572872 | tf_op jit(solution)/shard_map/ppermute | solution.py:122
  144.9 15.1 %collective-permute-start.32 = (bf16[128,2048]{1,0:T(8,128)(2,1)}, bf16[128,2048]{1,0:T(8,128)(2,1)S(1)}, u32[]{:S(2)}, u32[]{:S(2)}) collective-permute-start(bf16[128,2048]{1,0:T(8,128)(2,1)} %get-tuple-element.51.refs_0_), channel_id=1, source_target_pairs={{0,2},{2,0},{1,3},{3,1},{4,6},{6,4},{5,7},{7,5},{8,10},{10,8},{9,1... | collective-permute-start | bytes 1572872 | tf_op jit(solution)/shard_map/ppermute | solution.py:122
  145.5 21.4 %collective-permute-start.42 = (bf16[128,2048]{1,0:T(8,128)(2,1)S(1)}, bf16[128,2048]{1,0:T(8,128)(2,1)S(1)}, u32[]{:S(2)}, u32[]{:S(2)}) collective-permute-start(bf16[128,2048]{1,0:T(8,128)(2,1)S(1)} %collective-permute-done.29), channel_id=1, source_target_pairs={{0,2},{2,0},{1,3},{3,1},{4,6},{6,4},{5,7},{7,5},{8,10},{10,8},{9,1... | collective-permute-start | bytes 1572872 | tf_op jit(solution)/shard_map/ppermute | solution.py:122
  147.0 19.9 %collective-permute-start.43 = (bf16[128,2048]{1,0:T(8,128)(2,1)S(1)}, bf16[128,2048]{1,0:T(8,128)(2,1)S(1)}, u32[]{:S(2)}, u32[]{:S(2)}) collective-permute-start(bf16[128,2048]{1,0:T(8,128)(2,1)S(1)} %collective-permute-done.30), channel_id=1, source_target_pairs={{0,4},{4,0},{8,12},{12,8},{1,5},{5,1},{9,13},{13,9},{2,6},{6,2},{1... | collective-permute-start | bytes 1572872 | tf_op jit(solution)/shard_map/ppermute | solution.py:122
  147.0 20.4 %collective-permute-start.38 = (bf16[128,2048]{1,0:T(8,128)(2,1)S(1)}, bf16[128,2048]{1,0:T(8,128)(2,1)S(1)}, u32[]{:S(2)}, u32[]{:S(2)}) collective-permute-start(bf16[128,2048]{1,0:T(8,128)(2,1)S(1)} %collective-permute-done.29), channel_id=1, source_target_pairs={{0,1},{1,0},{2,3},{3,2},{4,5},{5,4},{6,7},{7,6},{8,9},{9,8},{10,11... | collective-permute-start | bytes 1572872 | tf_op jit(solution)/shard_map/ppermute | solution.py:122
  160.0 10.7 %collective-permute-start.39 = (bf16[128,2048]{1,0:T(8,128)(2,1)S(1)}, bf16[128,2048]{1,0:T(8,128)(2,1)S(1)}, u32[]{:S(2)}, u32[]{:S(2)}) collective-permute-start(bf16[128,2048]{1,0:T(8,128)(2,1)S(1)} %collective-permute-done.37), channel_id=1, source_target_pairs={{0,1},{1,0},{2,3},{3,2},{4,5},{5,4},{6,7},{7,6},{8,9},{9,8},{10,11... | collective-permute-start | bytes 1572872 | tf_op jit(solution)/shard_map/ppermute | solution.py:122
  167.5 20.9 %collective-permute-start.33 = (bf16[128,2048]{1,0:T(8,128)(2,1)}, bf16[128,2048]{1,0:T(8,128)(2,1)}, u32[]{:S(2)}, u32[]{:S(2)}) collective-permute-start(bf16[128,2048]{1,0:T(8,128)(2,1)} %get-tuple-element.52), channel_id=1, source_target_pairs={{0,12},{12,0},{1,13},{13,1},{2,14},{14,2},{3,15},{15,3},{16,28},{2... | collective-permute-start | bytes 1572872 | tf_op jit(solution)/shard_map/ppermute | solution.py:691
  187.7 16.4 %collective-permute-start.48 = (bf16[128,2048]{1,0:T(8,128)(2,1)}, bf16[128,2048]{1,0:T(8,128)(2,1)S(1)}, u32[]{:S(2)}, u32[]{:S(2)}) collective-permute-start(bf16[128,2048]{1,0:T(8,128)(2,1)} %get-tuple-element.56.refs_0_), channel_id=1, source_target_pairs={{0,2},{2,0},{1,3},{3,1},{4,6},{6,4},{5,7},{7,5},{8,10},{10,8},{9,1... | collective-permute-start | bytes 1572872 | tf_op jit(solution)/shard_map/ppermute | solution.py:122
  189.5 23.8 %collective-permute-start.34 = (bf16[128,2048]{1,0:T(8,128)(2,1)S(1)}, bf16[128,2048]{1,0:T(8,128)(2,1)S(1)}, u32[]{:S(2)}, u32[]{:S(2)}) collective-permute-start(bf16[128,2048]{1,0:T(8,128)(2,1)S(1)} %broadcast_select_fusion.refs_2_), channel_id=1, source_target_pairs={{0,2},{2,0},{1,3},{3,1},{4,6},{6,4},{5,7},{7,5},{8,10},{10,8},{9,1... | collective-permute-start | bytes 1572872 | tf_op jit(solution)/shard_map/ppermute | solution.py:122
  190.9 26.0 %collective-permute-start.46 = (bf16[64,2048]{1,0:T(8,128)(2,1)}, bf16[64,2048]{1,0:T(8,128)(2,1)S(1)}, u32[]{:S(2)}, u32[]{:S(2)}) collective-permute-start(bf16[64,2048]{1,0:T(8,128)(2,1)} %get-tuple-element.54), channel_id=1, source_target_pairs={{0,12},{4,8},{8,4},{12,0},{1,13},{5,9},{9,5},{13,1},{2,14},{6,10},... | collective-permute-start | bytes 786440 | tf_op jit(solution)/shard_map/ppermute | solution.py:122
  204.0 16.1 %collective-permute-start.54 = (f32[2,8,128]{2,1,0:T(8,128)S(1)}, f32[2,8,128]{2,1,0:T(8,128)S(1)}, u32[]{:S(2)}, u32[]{:S(2)}) collective-permute-start(f32[2,8,128]{2,1,0:T(8,128)S(1)} %pad_maximum_fusion.2), channel_id=1, source_target_pairs={{0,2},{2,0},{1,3},{3,1},{4,6},{6,4},{5,7},{7,5},{8,10},{10,8},{9,1... | collective-permute-start | bytes 24584 | tf_op jit(solution)/shard_map/ppermute | solution.py:122
  (68 other events, 575.4 us)

commit v8 on v7

--- a/solution.py
+++ b/solution.py
@@ -10,7 +10,8 @@
 ANY = pl.BlockSpec(memory_space=pl.ANY)
 SMEM = pl.BlockSpec(memory_space=pltpu.SMEM)
 VMEM = pl.BlockSpec(memory_space=pltpu.VMEM)
-VMEM_LIMIT = 56 * 1024 * 1024
+VMEM_LIMIT = 24 * 1024 * 1024
+OPERATE_LIMIT = 44 * 1024 * 1024
 LANES = 128
 
 
@@ -110,6 +111,7 @@
 
 
 MIX_A, MIX_B = 4, 5
+MIXES = ((MIX_A, 0, 0), (MIX_B, 0, 0))
 
 
 def halves_fit(mesh):
@@ -154,7 +156,7 @@
     return 4 * (z ^ dz) + 2 * (c ^ dc) + (x ^ dx if dx < 2 else dx - 2)
 
 
-def operate_kernel(first, plan, cols, pattern, right_all, left_own, left_other, *refs):
+def operate_kernel(first, plan, cols, pattern, right, left_own, left_other, *refs):
     count = len(plan)
     pieces, refs = refs[:count], refs[count:]
     if first:
@@ -163,7 +165,7 @@
     else:
         hd_own, hd_far, psi_in, off_in, stats_in, near_out, far_out, late_out, stats_out = refs[:9]
         refs = refs[9:]
-    field, images, right, left, diag, parts, sems = refs
+    field, images, left, diag, sems = refs
     z, x, c = place()
     sectors, block, width = field.shape
     table = right.shape[1]
@@ -179,38 +181,30 @@
         copy.start()
         copies.append(copy)
 
-    begin(right_all, right)
-    for piece, offsets in zip(pieces, plan):
-        base = 2 * half if piece.shape[0] == 4 else 0
-        for at, (dz, dx, dc, start, tall) in enumerate(offsets):
-            target = field.at[row_of(dz, dx, dc), pl.ds(start, tall)]
-            if dz in (MIX_A, MIX_B):
-                begin(piece.at[at, :, pl.ds(0, width)], target)
-                if dc == 0:
-                    begin(
-                        piece.at[at, pl.ds(0, parts.shape[1]), pl.ds(width, LANES)],
-                        parts.at[dz - MIX_A],
-                    )
-            else:
-                begin(piece.at[base + at], target)
-    early = len(copies)
     for at in range(2):
         begin(left_own.at[pl.ds(rows[at] * links, links)], left.at[0, pl.ds(at * links, links)])
     begin(left_other.at[pl.ds(table // 2, 2 * links)], left.at[1])
     if not first:
         begin(hd_own.at[x], diag.at[0])
         begin(hd_far, diag.at[1])
-    for copy in copies[:early]:
-        copy.wait()
+
+    def allowed(a, q, value):
+        return jnp.where(pattern[a, q] != 0, value, jnp.zeros_like(value))
+
+    for piece, offsets in zip(pieces, plan):
+        base = 2 * half if piece.shape[0] == 4 else 0
+        for at, (dz, dx, dc, start, tall) in enumerate(offsets):
+            row = row_of(dz, dx, dc)
+            for q in range(sectors):
+                span = slice(q * block, (q + 1) * block)
+                value = piece[base + at, :, span]
+                field[row, start : start + tall, span] = allowed(row, q, value) if first else value
 
     def right_col(term, b, j):
         return cols[(2 * term) * table + b * links + j]
 
     def left_col(term, a, j):
         return cols[(2 * term + 1) * table + a * links + j]
-
-    def allowed(a, q, value):
-        return jnp.where(pattern[a, q] != 0, value, jnp.zeros_like(value))
 
     sources = [[left_col(term, rows[at], j) for at in range(2) for j in range(links)] for term in range(2)]
 
@@ -228,7 +222,7 @@
                 line = []
                 for col in found:
                     value = field[source, :, pl.ds(pl.multiple_of(col * block, block), block)]
-                    line.append(allowed(source, col, value) if first else value)
+                    line.append(value)
                 lhs.append(jnp.concatenate(line, axis=1))
             rhs = []
             for i, j in picks:
@@ -246,7 +240,7 @@
         return carry
 
     lax.fori_loop(0, sectors // pair, image, 0, unroll=2)
-    for copy in copies[early:]:
+    for copy in copies:
         copy.wait()
 
     step = 2
@@ -274,7 +268,6 @@
             offdiag = masked(rows[at], total.astype(jnp.bfloat16).astype(jnp.float32))
             own = field[rows[at], :, span].astype(jnp.float32)
             if first:
-                own = masked(rows[at], own)
                 psi_out[at, :, span] = own.astype(jnp.bfloat16)
                 off_out[at, :, span] = offdiag.astype(jnp.bfloat16)
                 sums[0] += fold(own * own)
@@ -297,7 +290,10 @@
 
     sums = list(lax.fori_loop(0, sectors // step, column, (zero,) * (2 if first else 3)))
     if first:
-        far_weight = (parts[0] + parts[1]).astype(jnp.float32)
+        parts = [
+            piece[0, 0:48, width:] for piece, offsets in zip(pieces, plan) if offsets[0][:3] in MIXES
+        ]
+        far_weight = sum(part.astype(jnp.float32) for part in parts)
         sums[1] += weight_own[...] + (far_weight[0:8] + far_weight[16:24] + far_weight[32:40])
     stats_out[...] = jnp.zeros_like(stats_out)
     for at, value in enumerate(sums):
@@ -317,24 +313,21 @@
     stats = jax.ShapeDtypeStruct((8, LANES), jnp.float32)
     out_shape = (rows, rows, stats) if first else (one, some, some, stats)
     extra_specs = [VMEM] if first else [ANY, ANY, VMEM, VMEM, VMEM]
-    copies = sum(len(offsets) for offsets in plan) + 9
     inner = 2 * 2 * sectors * 2 * links * links * block * block * block
     outer = 2 * 2 * 2 * links * block * block * width
     return pl.pallas_call(
         functools.partial(operate_kernel, first, plan),
         out_shape=out_shape,
-        in_specs=[SMEM, SMEM] + [ANY] * (3 + len(pieces)) + extra_specs,
+        in_specs=[SMEM, SMEM, VMEM, ANY, ANY] + [VMEM] * len(pieces) + extra_specs,
         out_specs=(VMEM,) * len(out_shape),
         scratch_shapes=[
             pltpu.VMEM((sectors, block, width), jnp.bfloat16),
             pltpu.VMEM((2, 2 * links * block, width), jnp.bfloat16),
-            pltpu.VMEM((2, table, block, block), jnp.bfloat16),
             pltpu.VMEM((2, 2 * links, block, block), jnp.bfloat16),
             pltpu.VMEM((2, block, width), jnp.bfloat16),
-            pltpu.VMEM((2, 48, LANES), jnp.bfloat16),
-            pltpu.SemaphoreType.DMA((copies,)),
+            pltpu.SemaphoreType.DMA((5,)),
         ],
-        compiler_params=pltpu.CompilerParams(vmem_limit_bytes=VMEM_LIMIT),
+        compiler_params=pltpu.CompilerParams(vmem_limit_bytes=OPERATE_LIMIT),
         cost_estimate=pl.CostEstimate(
             flops=inner + outer if first else 0,
             bytes_accessed=16 * 1024 * 1024 if first else 1024,
@@ -593,19 +586,21 @@
     operators = across(packed, "ops", 1)
     theta_core = across(theta, "sub", 1)
 
-    mix_a, mix_b = after((mix_a, mix_b), theta_core)
+    cols_other = across(after(cols, mix_a), "ops", 1)
+    cols = jnp.concatenate([cols, cols_other])
+    mix_a_core = across(mix_a, "sub", 1)
+    operators_core = across(after(operators, cols_other)[: right.shape[0] // 2], "sub", 1)
+
+    mix_b = after(mix_b, theta_core, mix_a_core, operators_core)
     far = jnp.where(middle, mix_a[:, :width], mix_b[:, :width])
     far_z = [across(far[at : at + chunk], "blk", 1) for at in (0, chunk)]
     far_x = across(far, "ops", 1)
-    mix_a_core = across(mix_a, "sub", 1)
     mix_b_core = across(mix_b, "sub", 1)
+    turned = arrange(right, operators, operators_core)
 
     own_b = lax.dynamic_slice(halves, (half, 1, 0, 0), (1, 1, block, width))[0, 0]
-    near_b = across(after(own_b, far_z[0], mix_a_core, mix_b_core), "blk", 1)
+    near_b = across(after(own_b, far_z[0], mix_b_core, turned), "blk", 1)
     far_zx = [across(value, "ops", 1) for value in far_z]
-    cols_other = across(after(cols, mix_a_core, mix_b_core), "ops", 1)
-    cols = jnp.concatenate([cols, cols_other])
-    operators_core = across(after(operators, far_z[0])[: right.shape[0] // 2], "sub", 1)
     far_x_core = across(far_x, "sub", 1)
     far_z_core = [across(value, "sub", 1) for value in far_z]
     hd_far = lax.dynamic_index_in_dim(diag, x, 0, keepdims=False)
@@ -613,7 +608,6 @@
     far_zx_core = [across(value, "sub", 1) for value in far_zx]
     near_b_core = across(near_b, "sub", 1)
 
-    turned = arrange(right, operators, operators_core)
     left = (left, operators)
     pieces = [halves.reshape(4, block, width), theta_core.reshape(4, block, width)]
     plan = [
@@ -714,17 +708,18 @@
         False, tuple(plan), pieces, cols, pattern, turned, left, (diag, hd_far, psi, off_one, stats_one)
     )
 
-    other = jnp.where(middle, other_middle, other_end)
     far_in = across(two_far, "blk", 3)
     near_in = across(two_near, "ops", 1)
-    late_in = across(after(two_late, far_in), "blk", 3)
+    sums = stats_three + across(stats_three, "sub", 1)
+    other = jnp.where(middle, other_middle, after(other_end, sums))
     other_x = across(other, "ops", 1)
-    far_in_x = across(after(far_in, near_in), "ops", 1)
-    late_in_x = across(after(late_in, other_x, far_in_x), "ops", 1)
-    sums = stats_three + across(stats_three, "sub", 1)
     sums = sums + across(sums, "blk", 1)
     both = jnp.stack([sums, across(sums, "blk", 2)])
-    both = both + across(after(both, near_in), "ops", 1)
+    late_in = across(after(two_late, far_in), "blk", 3)
+    far_in_x = across(after(far_in, near_in), "ops", 1)
+    both = both + across(after(both, far_in), "ops", 1)
+    other, other_x = after((other, other_x), late_in)
+    late_in_x = across(late_in, "ops", 1)
     both = jnp.sum(jnp.where(half == 0, both, both[::-1])[:, :5], axis=2)
     scale = both[:, 3:4] + 1e-06
     subspace = jnp.concatenate([both[:, 4:5], both[:, 0:3]], axis=1) / scale

time: 236 us -> 234 us (level)
  Pallas kernels: 56.3 us -> 39.1 us
  local copies, waits for them, and re-layouts: 9.27 us -> 18 us
  waiting for transfers between devices: 115 us -> 122 us
  other arithmetic: 4.82 us -> 2.24 us
    unnamed x92 -> x50, local copies, waits for them, and re-layouts: 6.13 us -> 14.7 us
    ppermute x45, waiting for transfers between devices: 84.1 us -> 89.7 us  [across(): return lax.ppermute(value, axis, [(i, i ^ distance) for i in range(size)])]
    pallas_call x1, Pallas kernels: 5.92 us -> 2.13 us  [shards(): pl.pallas_call(update_kernel, out_shape=(jax.ShapeDtypeStruct((2, block,...]
    pallas_call x1, Pallas kernels: 4.98 us -> 1.72 us  [arrange(): pl.pallas_call(arrange_kernel, out_shape=jax.ShapeDtypeStruct(shape, own....]
    pallas_call x3, Pallas kernels: 7.2 us -> 4.26 us  [assemble(): pl.pallas_call(functools.partial(assemble_kernel, places, len(based)), ou...]
    pallas_call x1, Pallas kernels: 3.43 us -> 0.62 us  [shards(): pl.pallas_call(correct_kernel, out_shape=(one, one), in_specs=[VMEM, VMEM...]
    pallas_call x1, Pallas kernels: 4.29 us -> 1.73 us  [prepare(): pl.pallas_call(prepare_kernel, out_shape=(mix, mix, packed, jax.ShapeDtyp...]
  transfers between devices with their start and end apart: 55 -> 55, of which waited for: 27 -> 25; matrix products, arithmetic and copies ran while one was open for 3% -> 2% of each run, Pallas kernels for 19% -> 15%
where the time goes in v8:
time: 234 us; the launch traced here: 233 us
  waiting for transfers between devices  122 us (52%)
  starting transfers between devices  50.5 us (22%)
  Pallas kernels  39.1 us (17%)
  local copies, waits for them, and re-layouts  18 us (8%)
    ppermute x45, waiting for transfers between devices, across(): return lax.ppermute(value, axis, [(i, i ^ distance) for i in range(size)])  89.7 us
    ppermute x45, starting transfers between devices, across(): return lax.ppermute(value, axis, [(i, i ^ distance) for i in range(size)])  34.9 us
    pallas_call x2, Pallas kernels, operate(): pl.pallas_call(functools.partial(operate_kernel, first, plan), out_shape=...  28.6 us
    unnamed x50, local copies, waits for them, and re-layouts  14.7 us
    ppermute x1, waiting for transfers between devices, shards(): mix_b = lax.ppermute(mix_b, 'blk', [(0, 1), (1, 3), (3, 2), (2, 0)])  14.3 us
    ppermute x1, waiting for transfers between devices, shards(): mix_a = lax.ppermute(mix_a, 'blk', [(0, 2), (2, 3), (3, 1), (1, 0)])  11.8 us
    ppermute x6, starting transfers between devices, share(): lax.ppermute(pair, axes, [(i, i ^ distance) for i in range(count)])  6.98 us
    ppermute x6, waiting for transfers between devices, share(): lax.ppermute(pair, axes, [(i, i ^ distance) for i in range(count)])  6.17 us
  transfers between devices with their start and end apart: 55, of which 25 were waited for; matrix products, arithmetic and copies ran while one was open for 2% of the time, Pallas kernels for 15%

profile of v8, /device:TPU:0, one launch (start us, length us, event | category | flops | bytes accessed | tf_op | source)
XLA Modules:
  0.0 233.0 jit_solution(11936159956849426628)
XLA Ops:
  3.8 1.6 copy-done.5
  7.5 1.7 prepare.1
  10.0 2.5 %collective-permute-start.2 = (bf16[30,128,128]{2,1,0:T(8,128)(2,1)S(1)}, bf16[30,128,128]{2,1,0:T(8,128)(2,1)S(1)}, u32[]{:S(2)}, u32[]{:S(2)}) collective-permute-start(bf16[30,128,128]{2,1,0:T(8,128)(2,1)S(1)} %get-tuple-element.35), channel_id=1, source_target_pairs={{0,2},{2,0},{1,3},{3,1},{4,6},{6,4},{5,7},{7,5},{8,10},{10,8},{9,1... | collective-permute-start | bytes 2949128 | tf_op jit(solution)/shard_map/ppermute | solution.py:124
  12.5 2.6 %collective-permute-start = (bf16[128,2176]{1,0:T(8,128)(2,1)S(1)}, bf16[128,2176]{1,0:T(8,128)(2,1)S(1)}, u32[]{:S(2)}, u32[]{:S(2)}) collective-permute-start(bf16[128,2176]{1,0:T(8,128)(2,1)S(1)} %get-tuple-element.33), channel_id=1, source_target_pairs={{0,8},{8,12},{12,4},{4,0},{1,9},{9,13},{13,5},{5,1},{2,10},{10,14}... | collective-permute-start | bytes 1671176 | tf_op jit(solution)/shard_map/ppermute | solution.py:584
  15.6 11.8 %collective-permute-done = bf16[128,2176]{1,0:T(8,128)(2,1)S(1)} collective-permute-done((bf16[128,2176]{1,0:T(8,128)(2,1)S(1)}, bf16[128,2176]{1,0:T(8,128)(2,1)S(1)}, u32[]{:S(2)}, u32[]{:S(2)}) %collective-permute-start) | collective-permute-done | bytes 557088 | tf_op jit(solution)/shard_map/ppermute | solution.py:584
  27.9 7.1 %collective-permute-done.1 = s32[96]{0:T(128)S(1)} collective-permute-done((s32[96]{0:T(128)S(1)}, s32[96]{0:T(128)S(1)}, u32[]{:S(2)}, u32[]{:S(2)}) %collective-permute-start.1) | collective-permute-done | bytes 416 | tf_op jit(solution)/shard_map/ppermute | solution.py:124
  36.0 1.8 collective-permute-start.5
  38.1 14.3 %collective-permute-done.5 = bf16[128,2176]{1,0:T(8,128)(2,1)S(1)} collective-permute-done((bf16[128,2176]{1,0:T(8,128)(2,1)}, bf16[128,2176]{1,0:T(8,128)(2,1)S(1)}, u32[]{:S(2)}, u32[]{:S(2)}) %collective-permute-start.5) | collective-permute-done | bytes 557088 | tf_op jit(solution)/shard_map/ppermute | solution.py:585
  58.2 1.7 arrange.1.right
  60.0 1.6 copy-done
  66.0 16.5 %collective-permute-done.16 = bf16[64,2048]{1,0:T(8,128)(2,1)} collective-permute-done((bf16[64,2048]{1,0:T(8,128)(2,1)S(1)}, bf16[64,2048]{1,0:T(8,128)(2,1)}, u32[]{:S(2)}, u32[]{:S(2)}) %collective-permute-start.16) | collective-permute-done | bytes 262176 | tf_op jit(solution)/shard_map/ppermute | solution.py:124
  84.8 5.1 %collective-permute-done.18 = bf16[64,2048]{1,0:T(8,128)(2,1)} collective-permute-done((bf16[64,2048]{1,0:T(8,128)(2,1)}, bf16[64,2048]{1,0:T(8,128)(2,1)}, u32[]{:S(2)}, u32[]{:S(2)}) %collective-permute-start.18) | collective-permute-done | bytes 262176 | tf_op jit(solution)/shard_map/ppermute | solution.py:124
  90.5 3.1 %collective-permute-start.20 = (bf16[128,2048]{1,0:T(8,128)(2,1)S(1)}, bf16[128,2048]{1,0:T(8,128)(2,1)S(1)}, u32[]{:S(2)}, u32[]{:S(2)}) collective-permute-start(bf16[128,2048]{1,0:T(8,128)(2,1)S(1)} %dynamic-slice_bitcast_fusion), channel_id=1, source_target_pairs={{0,12},{4,8},{8,4},{12,0},{1,13},{5,9},{9,5},{13,1},{2,14},{6,10},... | collective-permute-start | bytes 1572872 | tf_op jit(solution)/shard_map/ppermute | solution.py:124
  94.7 15.9 %operate_first.1 = (bf16[2,128,2048]{2,1,0:T(8,128)(2,1)S(1)}, bf16[2,128,2048]{2,1,0:T(8,128)(2,1)S(1)}, f32[8,128]{1,0:T(8,128)S(1)}) custom-call(s32[192]{0:T(256)S(1)} %pad_add_fusion.cols, s32[16,16]{1,0:T(8,128)S(1)} %copy-done.15, bf16[2,48,128,128]{3,2,1,0:T(8,128)(2,1)} %copy-done, bf16[48,128,128]{2,1,0:T(8,128)(2,1)} %bitcast.51, ...), custom_call_target="tpu_custom_call" | custom-call | flops 3221225472 | bytes 16777216 | tf_op jit(solution)/shard_map/operate_first/pallas_call | solution.py:318
  113.2 2.2 collective-permute-start.24
  117.7 2.1 update.1
  126.3 2.1 collective-permute-done.28.refs_3_
  131.7 9.7 %collective-permute-done.29 = bf16[128,2048]{1,0:T(8,128)(2,1)S(1)} collective-permute-done((bf16[128,2048]{1,0:T(8,128)(2,1)S(1)}, bf16[128,2048]{1,0:T(8,128)(2,1)S(1)}, u32[]{:S(2)}, u32[]{:S(2)}) %collective-permute-start.29) | collective-permute-done | bytes 524320 | tf_op jit(solution)/shard_map/ppermute | solution.py:124
  142.8 3.6 %collective-permute-start.36 = (bf16[128,2048]{1,0:T(8,128)(2,1)S(1)}, bf16[128,2048]{1,0:T(8,128)(2,1)S(1)}, u32[]{:S(2)}, u32[]{:S(2)}) collective-permute-start(bf16[128,2048]{1,0:T(8,128)(2,1)S(1)} %get-tuple-element.52), channel_id=1, source_target_pairs={{0,4},{4,0},{8,12},{12,8},{1,5},{5,1},{9,13},{13,9},{2,6},{6,2},{1... | collective-permute-start | bytes 1572872 | tf_op jit(solution)/shard_map/ppermute | solution.py:124
  148.5 10.7 %collective-permute-done.36 = bf16[128,2048]{1,0:T(8,128)(2,1)S(1)} collective-permute-done((bf16[128,2048]{1,0:T(8,128)(2,1)S(1)}, bf16[128,2048]{1,0:T(8,128)(2,1)S(1)}, u32[]{:S(2)}, u32[]{:S(2)}) %collective-permute-start.36) | collective-permute-done | bytes 524320 | tf_op jit(solution)/shard_map/ppermute | solution.py:124
  159.3 2.0 collective-permute-done.32.refs_1_
  161.3 6.9 %collective-permute-done.41 = bf16[128,2048]{1,0:T(8,128)(2,1)S(1)} collective-permute-done((bf16[128,2048]{1,0:T(8,128)(2,1)S(1)}, bf16[128,2048]{1,0:T(8,128)(2,1)S(1)}, u32[]{:S(2)}, u32[]{:S(2)}) %collective-permute-start.41) | collective-permute-done | bytes 524320 | tf_op jit(solution)/shard_map/ppermute | solution.py:124
  168.8 3.5 %collective-permute-start.33 = (bf16[128,2048]{1,0:T(8,128)(2,1)S(1)}, bf16[128,2048]{1,0:T(8,128)(2,1)}, u32[]{:S(2)}, u32[]{:S(2)}) collective-permute-start(bf16[128,2048]{1,0:T(8,128)(2,1)S(1)} %get-tuple-element.52), channel_id=1, source_target_pairs={{0,12},{12,0},{1,13},{13,1},{2,14},{14,2},{3,15},{15,3},{16,28},{2... | collective-permute-start | bytes 1572872 | tf_op jit(solution)/shard_map/ppermute | solution.py:685
  172.3 12.7 %operate_second.1 = (bf16[128,2048]{1,0:T(8,128)(2,1)S(1)}, bf16[64,2048]{1,0:T(8,128)(2,1)S(1)}, bf16[64,2048]{1,0:T(8,128)(2,1)S(1)}, f32[8,128]{1,0:T(8,128)S(1)}) custom-call(s32[192]{0:T(256)S(1)} %pad_add_fusion.cols, s32[16,16]{1,0:T(8,128)S(1)} %copy-done.15, bf16[2,48,128,128]{3,2,1,0:T(8,128)(2,1)} %copy-done, bf16[48,128,128]{2,1,0:T(8,128)(2,1)} %bitcast.52, ...), custom_call_target="tpu_custom_call" | custom-call | bytes 1024 | tf_op jit(solution)/shard_map/operate_second/pallas_call | solution.py:318
  185.7 2.4 %collective-permute-start.47 = (bf16[64,2048]{1,0:T(8,128)(2,1)S(1)}, bf16[64,2048]{1,0:T(8,128)(2,1)S(1)}, u32[]{:S(2)}, u32[]{:S(2)}) collective-permute-start(bf16[64,2048]{1,0:T(8,128)(2,1)S(1)} %get-tuple-element.56), channel_id=1, source_target_pairs={{0,12},{4,8},{8,4},{12,0},{1,13},{5,9},{9,5},{13,1},{2,14},{6,10},... | collective-permute-start | bytes 786440 | tf_op jit(solution)/shard_map/ppermute | solution.py:124
  189.3 4.9 %collective-permute-done.52 = f32[8,128]{1,0:T(8,128)S(1)} collective-permute-done((f32[8,128]{1,0:T(8,128)S(1)}, f32[8,128]{1,0:T(8,128)S(1)}, u32[]{:S(2)}, u32[]{:S(2)}) %collective-permute-start.52) | collective-permute-done | bytes 4128 | tf_op jit(solution)/shard_map/ppermute | solution.py:124
  194.2 2.4 %collective-permute-start.53 = (f32[8,128]{1,0:T(8,128)S(1)}, f32[8,128]{1,0:T(8,128)S(1)}, u32[]{:S(2)}, u32[]{:S(2)}) collective-permute-start(f32[8,128]{1,0:T(8,128)S(1)} %add.23), channel_id=1, source_target_pairs={{0,8},{4,12},{8,0},{12,4},{1,9},{5,13},{9,1},{13,5},{2,10},{6,14},... | collective-permute-start | bytes 12296 | tf_op jit(solution)/shard_map/ppermute | solution.py:124
  201.9 1.9 collective-permute-start.48
  203.8 7.8 %collective-permute-done.54 = f32[2,8,128]{2,1,0:T(8,128)S(1)} collective-permute-done((f32[2,8,128]{2,1,0:T(8,128)S(1)}, f32[2,8,128]{2,1,0:T(8,128)S(1)}, u32[]{:S(2)}, u32[]{:S(2)}) %collective-permute-start.54) | collective-permute-done | bytes 8224 | tf_op jit(solution)/shard_map/ppermute | solution.py:124
  214.6 8.3 %collective-permute-done.46.refs_3_ = bf16[128,2048]{1,0:T(8,128)(2,1)S(1)} collective-permute-done((bf16[128,2048]{1,0:T(8,128)(2,1)S(1)}, bf16[128,2048]{1,0:T(8,128)(2,1)S(1)}, u32[]{:S(2)}, u32[]{:S(2)}) %collective-permute-start.46) | collective-permute-done | bytes 524320 | tf_op jit(solution)/shard_map/ppermute | solution.py:124
  224.2 4.3 %collective-permute-done.51.refs_4_ = bf16[64,2048]{1,0:T(8,128)(2,1)S(1)} collective-permute-done((bf16[64,2048]{1,0:T(8,128)(2,1)S(1)}, bf16[64,2048]{1,0:T(8,128)(2,1)S(1)}, u32[]{:S(2)}, u32[]{:S(2)}) %collective-permute-start.51) | collective-permute-done | bytes 262176 | tf_op jit(solution)/shard_map/ppermute | solution.py:124
  228.5 2.2 assemble.4.refs_1_
  (157 shorter events, 54.6 us)
Async XLA Ops:
  0.6 51.7 %collective-permute-start.4 = (bf16[2,256,2048]{2,1,0:T(8,128)(2,1)}, bf16[2,256,2048]{2,1,0:T(8,128)(2,1)}, u32[]{:S(2)}, u32[]{:S(2)}) collective-permute-start(bf16[2,256,2048]{2,1,0:T(8,128)(2,1)} %param.7), channel_id=1, source_target_pairs={{0,1},{1,0},{2,3},{3,2},{4,5},{5,4},{6,7},{7,6},{8,9},{9,8},{10,11... | collective-permute-start | bytes 6291464 | tf_op jit(solution)/shard_map/ppermute | solution.py:124
  10.0 25.0 %collective-permute-start.2 = (bf16[30,128,128]{2,1,0:T(8,128)(2,1)S(1)}, bf16[30,128,128]{2,1,0:T(8,128)(2,1)S(1)}, u32[]{:S(2)}, u32[]{:S(2)}) collective-permute-start(bf16[30,128,128]{2,1,0:T(8,128)(2,1)S(1)} %get-tuple-element.35), channel_id=1, source_target_pairs={{0,2},{2,0},{1,3},{3,1},{4,6},{6,4},{5,7},{7,5},{8,10},{10,8},{9,1... | collective-permute-start | bytes 2949128 | tf_op jit(solution)/shard_map/ppermute | solution.py:124
  12.5 14.8 %collective-permute-start = (bf16[128,2176]{1,0:T(8,128)(2,1)S(1)}, bf16[128,2176]{1,0:T(8,128)(2,1)S(1)}, u32[]{:S(2)}, u32[]{:S(2)}) collective-permute-start(bf16[128,2176]{1,0:T(8,128)(2,1)S(1)} %get-tuple-element.33), channel_id=1, source_target_pairs={{0,8},{8,12},{12,4},{4,0},{1,9},{9,13},{13,5},{5,1},{2,10},{10,14}... | collective-permute-start | bytes 1671176 | tf_op jit(solution)/shard_map/ppermute | solution.py:584
  36.0 16.4 %collective-permute-start.3 = (bf16[24,128,128]{2,1,0:T(8,128)(2,1)}, bf16[24,128,128]{2,1,0:T(8,128)(2,1)S(1)}, u32[]{:S(2)}, u32[]{:S(2)}) collective-permute-start(bf16[24,128,128]{2,1,0:T(8,128)(2,1)} %slice.27), channel_id=1, source_target_pairs={{0,1},{1,0},{2,3},{3,2},{4,5},{5,4},{6,7},{7,6},{8,9},{9,8},{10,11... | collective-permute-start | bytes 2359304 | tf_op jit(solution)/shard_map/ppermute | solution.py:124
  36.0 16.3 %collective-permute-start.5 = (bf16[128,2176]{1,0:T(8,128)(2,1)}, bf16[128,2176]{1,0:T(8,128)(2,1)S(1)}, u32[]{:S(2)}, u32[]{:S(2)}) collective-permute-start(bf16[128,2176]{1,0:T(8,128)(2,1)} %copy-done.16), channel_id=1, source_target_pairs={{0,4},{4,12},{12,8},{8,0},{1,5},{5,13},{13,9},{9,1},{2,6},{6,14},{... | collective-permute-start | bytes 1671176 | tf_op jit(solution)/shard_map/ppermute | solution.py:585
  37.8 14.5 %collective-permute-start.6 = (bf16[128,2176]{1,0:T(8,128)(2,1)S(1)}, bf16[128,2176]{1,0:T(8,128)(2,1)}, u32[]{:S(2)}, u32[]{:S(2)}) collective-permute-start(bf16[128,2176]{1,0:T(8,128)(2,1)S(1)} %collective-permute-done), channel_id=1, source_target_pairs={{0,1},{1,0},{2,3},{3,2},{4,5},{5,4},{6,7},{7,6},{8,9},{9,8},{10,11... | collective-permute-start | bytes 1671176 | tf_op jit(solution)/shard_map/ppermute | solution.py:124
  52.4 10.7 %collective-permute-start.7 = (bf16[128,2176]{1,0:T(8,128)(2,1)S(1)}, bf16[128,2176]{1,0:T(8,128)(2,1)}, u32[]{:S(2)}, u32[]{:S(2)}) collective-permute-start(bf16[128,2176]{1,0:T(8,128)(2,1)S(1)} %collective-permute-done.5), channel_id=1, source_target_pairs={{0,1},{1,0},{2,3},{3,2},{4,5},{5,4},{6,7},{7,6},{8,9},{9,8},{10,11... | collective-permute-start | bytes 1671176 | tf_op jit(solution)/shard_map/ppermute | solution.py:124
  61.6 21.5 %collective-permute-start.11 = (bf16[128,2048]{1,0:T(8,128)(2,1)S(1)}, bf16[128,2048]{1,0:T(8,128)(2,1)}, u32[]{:S(2)}, u32[]{:S(2)}) collective-permute-start(bf16[128,2048]{1,0:T(8,128)(2,1)S(1)} %copy-done.19), channel_id=1, source_target_pairs={{0,2},{2,0},{1,3},{3,1},{4,6},{6,4},{5,7},{7,5},{8,10},{10,8},{9,1... | collective-permute-start | bytes 1572872 | tf_op jit(solution)/shard_map/ppermute | solution.py:124
  63.1 20.5 %collective-permute-start.9 = (bf16[128,2048]{1,0:T(8,128)(2,1)S(1)}, bf16[128,2048]{1,0:T(8,128)(2,1)}, u32[]{:S(2)}, u32[]{:S(2)}) collective-permute-start(bf16[128,2048]{1,0:T(8,128)(2,1)S(1)} %dynamic-slice_bitcast_fusion.1), channel_id=1, source_target_pairs={{0,4},{4,0},{8,12},{12,8},{1,5},{5,1},{9,13},{13,9},{2,6},{6,2},{1... | collective-permute-start | bytes 1572872 | tf_op jit(solution)/shard_map/ppermute | solution.py:124
  64.3 18.2 %collective-permute-start.16 = (bf16[64,2048]{1,0:T(8,128)(2,1)S(1)}, bf16[64,2048]{1,0:T(8,128)(2,1)}, u32[]{:S(2)}, u32[]{:S(2)}) collective-permute-start(bf16[64,2048]{1,0:T(8,128)(2,1)S(1)} %copy-done.21), channel_id=1, source_target_pairs={{0,4},{4,0},{8,12},{12,8},{1,5},{5,1},{9,13},{13,9},{2,6},{6,2},{1... | collective-permute-start | bytes 786440 | tf_op jit(solution)/shard_map/ppermute | solution.py:124
  65.1 18.5 %collective-permute-start.14 = (bf16[64,2048]{1,0:T(8,128)(2,1)S(1)}, bf16[64,2048]{1,0:T(8,128)(2,1)S(1)}, u32[]{:S(2)}, u32[]{:S(2)}) collective-permute-start(bf16[64,2048]{1,0:T(8,128)(2,1)S(1)} %collective-permute-done.8), channel_id=1, source_target_pairs={{0,2},{2,0},{1,3},{3,1},{4,6},{6,4},{5,7},{7,5},{8,10},{10,8},{9,1... | collective-permute-start | bytes 786440 | tf_op jit(solution)/shard_map/ppermute | solution.py:124
  83.1 10.6 %collective-permute-start.12 = (bf16[128,2048]{1,0:T(8,128)(2,1)}, bf16[128,2048]{1,0:T(8,128)(2,1)}, u32[]{:S(2)}, u32[]{:S(2)}) collective-permute-start(bf16[128,2048]{1,0:T(8,128)(2,1)} %collective-permute-done.11), channel_id=1, source_target_pairs={{0,1},{1,0},{2,3},{3,2},{4,5},{5,4},{6,7},{7,6},{8,9},{9,8},{10,11... | collective-permute-start | bytes 1572872 | tf_op jit(solution)/shard_map/ppermute | solution.py:124
  90.5 24.9 %collective-permute-start.20 = (bf16[128,2048]{1,0:T(8,128)(2,1)S(1)}, bf16[128,2048]{1,0:T(8,128)(2,1)S(1)}, u32[]{:S(2)}, u32[]{:S(2)}) collective-permute-start(bf16[128,2048]{1,0:T(8,128)(2,1)S(1)} %dynamic-slice_bitcast_fusion), channel_id=1, source_target_pairs={{0,12},{4,8},{8,4},{12,0},{1,13},{5,9},{9,5},{13,1},{2,14},{6,10},... | collective-permute-start | bytes 1572872 | tf_op jit(solution)/shard_map/ppermute | solution.py:124
  129.0 12.4 %collective-permute-start.29 = (bf16[128,2048]{1,0:T(8,128)(2,1)S(1)}, bf16[128,2048]{1,0:T(8,128)(2,1)S(1)}, u32[]{:S(2)}, u32[]{:S(2)}) collective-permute-start(bf16[128,2048]{1,0:T(8,128)(2,1)S(1)} %get-tuple-element.51.refs_0_), channel_id=1, source_target_pairs={{0,4},{4,0},{8,12},{12,8},{1,5},{5,1},{9,13},{13,9},{2,6},{6,2},{1... | collective-permute-start | bytes 1572872 | tf_op jit(solution)/shard_map/ppermute | solution.py:124
  129.9 12.1 %collective-permute-start.30 = (bf16[128,2048]{1,0:T(8,128)(2,1)S(1)}, bf16[128,2048]{1,0:T(8,128)(2,1)S(1)}, u32[]{:S(2)}, u32[]{:S(2)}) collective-permute-start(bf16[128,2048]{1,0:T(8,128)(2,1)S(1)} %get-tuple-element.52), channel_id=1, source_target_pairs={{0,2},{2,0},{1,3},{3,1},{4,6},{6,4},{5,7},{7,5},{8,10},{10,8},{9,1... | collective-permute-start | bytes 1572872 | tf_op jit(solution)/shard_map/ppermute | solution.py:124
  130.4 11.6 %collective-permute-start.31 = (bf16[128,2048]{1,0:T(8,128)(2,1)S(1)}, bf16[128,2048]{1,0:T(8,128)(2,1)S(1)}, u32[]{:S(2)}, u32[]{:S(2)}) collective-permute-start(bf16[128,2048]{1,0:T(8,128)(2,1)S(1)} %get-tuple-element.52), channel_id=1, source_target_pairs={{4,8},{8,4},{5,9},{9,5},{6,10},{10,6},{7,11},{11,7},{20,24},{24,20... | collective-permute-start | bytes 1572872 | tf_op jit(solution)/shard_map/ppermute | solution.py:673
  131.1 17.3 %collective-permute-start.34 = (bf16[128,2048]{1,0:T(8,128)(2,1)S(1)}, bf16[128,2048]{1,0:T(8,128)(2,1)S(1)}, u32[]{:S(2)}, u32[]{:S(2)}) collective-permute-start(bf16[128,2048]{1,0:T(8,128)(2,1)S(1)} %get-tuple-element.51.refs_0_), channel_id=1, source_target_pairs={{0,1},{1,0},{2,3},{3,2},{4,5},{5,4},{6,7},{7,6},{8,9},{9,8},{10,11... | collective-permute-start | bytes 1572872 | tf_op jit(solution)/shard_map/ppermute | solution.py:124
  131.2 17.3 %collective-permute-start.35 = (bf16[128,2048]{1,0:T(8,128)(2,1)S(1)}, bf16[128,2048]{1,0:T(8,128)(2,1)S(1)}, u32[]{:S(2)}, u32[]{:S(2)}) collective-permute-start(bf16[128,2048]{1,0:T(8,128)(2,1)S(1)} %get-tuple-element.52), channel_id=1, source_target_pairs={{0,1},{1,0},{2,3},{3,2},{4,5},{5,4},{6,7},{7,6},{8,9},{9,8},{10,11... | collective-permute-start | bytes 1572872 | tf_op jit(solution)/shard_map/ppermute | solution.py:124
  142.8 16.5 %collective-permute-start.36 = (bf16[128,2048]{1,0:T(8,128)(2,1)S(1)}, bf16[128,2048]{1,0:T(8,128)(2,1)S(1)}, u32[]{:S(2)}, u32[]{:S(2)}) collective-permute-start(bf16[128,2048]{1,0:T(8,128)(2,1)S(1)} %get-tuple-element.52), channel_id=1, source_target_pairs={{0,4},{4,0},{8,12},{12,8},{1,5},{5,1},{9,13},{13,9},{2,6},{6,2},{1... | collective-permute-start | bytes 1572872 | tf_op jit(solution)/shard_map/ppermute | solution.py:124
  146.4 14.9 %collective-permute-start.32 = (bf16[128,2048]{1,0:T(8,128)(2,1)S(1)}, bf16[128,2048]{1,0:T(8,128)(2,1)S(1)}, u32[]{:S(2)}, u32[]{:S(2)}) collective-permute-start(bf16[128,2048]{1,0:T(8,128)(2,1)S(1)} %get-tuple-element.51.refs_0_), channel_id=1, source_target_pairs={{0,2},{2,0},{1,3},{3,1},{4,6},{6,4},{5,7},{7,5},{8,10},{10,8},{9,1... | collective-permute-start | bytes 1572872 | tf_op jit(solution)/shard_map/ppermute | solution.py:124
  147.6 20.6 %collective-permute-start.41 = (bf16[128,2048]{1,0:T(8,128)(2,1)S(1)}, bf16[128,2048]{1,0:T(8,128)(2,1)S(1)}, u32[]{:S(2)}, u32[]{:S(2)}) collective-permute-start(bf16[128,2048]{1,0:T(8,128)(2,1)S(1)} %collective-permute-done.29), channel_id=1, source_target_pairs={{0,2},{2,0},{1,3},{3,1},{4,6},{6,4},{5,7},{7,5},{8,10},{10,8},{9,1... | collective-permute-start | bytes 1572872 | tf_op jit(solution)/shard_map/ppermute | solution.py:124
  148.4 19.7 %collective-permute-start.42 = (bf16[128,2048]{1,0:T(8,128)(2,1)S(1)}, bf16[128,2048]{1,0:T(8,128)(2,1)S(1)}, u32[]{:S(2)}, u32[]{:S(2)}) collective-permute-start(bf16[128,2048]{1,0:T(8,128)(2,1)S(1)} %collective-permute-done.30), channel_id=1, source_target_pairs={{0,4},{4,0},{8,12},{12,8},{1,5},{5,1},{9,13},{13,9},{2,6},{6,2},{1... | collective-permute-start | bytes 1572872 | tf_op jit(solution)/shard_map/ppermute | solution.py:124
  148.5 20.2 %collective-permute-start.37 = (bf16[128,2048]{1,0:T(8,128)(2,1)S(1)}, bf16[128,2048]{1,0:T(8,128)(2,1)S(1)}, u32[]{:S(2)}, u32[]{:S(2)}) collective-permute-start(bf16[128,2048]{1,0:T(8,128)(2,1)S(1)} %collective-permute-done.29), channel_id=1, source_target_pairs={{0,1},{1,0},{2,3},{3,2},{4,5},{5,4},{6,7},{7,6},{8,9},{9,8},{10,11... | collective-permute-start | bytes 1572872 | tf_op jit(solution)/shard_map/ppermute | solution.py:124
  161.3 11.0 %collective-permute-start.38 = (bf16[128,2048]{1,0:T(8,128)(2,1)S(1)}, bf16[128,2048]{1,0:T(8,128)(2,1)S(1)}, u32[]{:S(2)}, u32[]{:S(2)}) collective-permute-start(bf16[128,2048]{1,0:T(8,128)(2,1)S(1)} %collective-permute-done.36), channel_id=1, source_target_pairs={{0,1},{1,0},{2,3},{3,2},{4,5},{5,4},{6,7},{7,6},{8,9},{9,8},{10,11... | collective-permute-start | bytes 1572872 | tf_op jit(solution)/shard_map/ppermute | solution.py:124
  168.8 29.1 %collective-permute-start.33 = (bf16[128,2048]{1,0:T(8,128)(2,1)S(1)}, bf16[128,2048]{1,0:T(8,128)(2,1)}, u32[]{:S(2)}, u32[]{:S(2)}) collective-permute-start(bf16[128,2048]{1,0:T(8,128)(2,1)S(1)} %get-tuple-element.52), channel_id=1, source_target_pairs={{0,12},{12,0},{1,13},{13,1},{2,14},{14,2},{3,15},{15,3},{16,28},{2... | collective-permute-start | bytes 1572872 | tf_op jit(solution)/shard_map/ppermute | solution.py:685
  185.7 13.0 %collective-permute-start.47 = (bf16[64,2048]{1,0:T(8,128)(2,1)S(1)}, bf16[64,2048]{1,0:T(8,128)(2,1)S(1)}, u32[]{:S(2)}, u32[]{:S(2)}) collective-permute-start(bf16[64,2048]{1,0:T(8,128)(2,1)S(1)} %get-tuple-element.56), channel_id=1, source_target_pairs={{0,12},{4,8},{8,4},{12,0},{1,13},{5,9},{9,5},{13,1},{2,14},{6,10},... | collective-permute-start | bytes 786440 | tf_op jit(solution)/shard_map/ppermute | solution.py:124
  196.6 15.1 %collective-permute-start.50 = (bf16[128,2048]{1,0:T(8,128)(2,1)S(1)}, bf16[128,2048]{1,0:T(8,128)(2,1)S(1)}, u32[]{:S(2)}, u32[]{:S(2)}) collective-permute-start(bf16[128,2048]{1,0:T(8,128)(2,1)S(1)} %get-tuple-element.60.refs_0_), channel_id=1, source_target_pairs={{0,2},{2,0},{1,3},{3,1},{4,6},{6,4},{5,7},{7,5},{8,10},{10,8},{9,1... | collective-permute-start | bytes 1572872 | tf_op jit(solution)/shard_map/ppermute | solution.py:124
  198.7 12.9 %collective-permute-start.54 = (f32[2,8,128]{2,1,0:T(8,128)S(1)}, f32[2,8,128]{2,1,0:T(8,128)S(1)}, u32[]{:S(2)}, u32[]{:S(2)}) collective-permute-start(f32[2,8,128]{2,1,0:T(8,128)S(1)} %pad_maximum_fusion.2), channel_id=1, source_target_pairs={{0,2},{2,0},{1,3},{3,1},{4,6},{6,4},{5,7},{7,5},{8,10},{10,8},{9,1... | collective-permute-start | bytes 24584 | tf_op jit(solution)/shard_map/ppermute | solution.py:124
  201.0 21.9 %collective-permute-start.46 = (bf16[128,2048]{1,0:T(8,128)(2,1)S(1)}, bf16[128,2048]{1,0:T(8,128)(2,1)S(1)}, u32[]{:S(2)}, u32[]{:S(2)}) collective-permute-start(bf16[128,2048]{1,0:T(8,128)(2,1)S(1)} %broadcast_select_fusion.refs_2_), channel_id=1, source_target_pairs={{0,2},{2,0},{1,3},{3,1},{4,6},{6,4},{5,7},{7,5},{8,10},{10,8},{9,1... | collective-permute-start | bytes 1572872 | tf_op jit(solution)/shard_map/ppermute | solution.py:124
  201.9 11.0 %collective-permute-start.48 = (bf16[64,2048]{1,0:T(8,128)(2,1)}, bf16[64,2048]{1,0:T(8,128)(2,1)}, u32[]{:S(2)}, u32[]{:S(2)}) collective-permute-start(bf16[64,2048]{1,0:T(8,128)(2,1)} %copy-done.17), channel_id=1, source_target_pairs={{0,12},{4,8},{8,4},{12,0},{1,13},{5,9},{9,5},{13,1},{2,14},{6,10},... | collective-permute-start | bytes 786440 | tf_op jit(solution)/shard_map/ppermute | solution.py:124
  211.8 16.7 %collective-permute-start.51 = (bf16[64,2048]{1,0:T(8,128)(2,1)S(1)}, bf16[64,2048]{1,0:T(8,128)(2,1)S(1)}, u32[]{:S(2)}, u32[]{:S(2)}) collective-permute-start(bf16[64,2048]{1,0:T(8,128)(2,1)S(1)} %collective-permute-done.47.refs_2_), channel_id=1, source_target_pairs={{0,2},{2,0},{1,3},{3,1},{4,6},{6,4},{5,7},{7,5},{8,10},{10,8},{9,1... | collective-permute-start | bytes 786440 | tf_op jit(solution)/shard_map/ppermute | solution.py:124
  213.0 19.2 %collective-permute-start.49 = (bf16[64,2048]{1,0:T(8,128)(2,1)}, bf16[64,2048]{1,0:T(8,128)(2,1)S(1)}, u32[]{:S(2)}, u32[]{:S(2)}) collective-permute-start(bf16[64,2048]{1,0:T(8,128)(2,1)} %collective-permute-done.48.refs_3_), channel_id=1, source_target_pairs={{0,2},{2,0},{1,3},{3,1},{4,6},{6,4},{5,7},{7,5},{8,10},{10,8},{9,1... | collective-permute-start | bytes 786440 | tf_op jit(solution)/shard_map/ppermute | solution.py:124
  (47 other events, 319.1 us)

commit v9 on v8

--- a/solution.py
+++ b/solution.py
@@ -12,6 +12,7 @@
 VMEM = pl.BlockSpec(memory_space=pltpu.VMEM)
 VMEM_LIMIT = 24 * 1024 * 1024
 OPERATE_LIMIT = 44 * 1024 * 1024
+PREPARE_LIMIT = 56 * 1024 * 1024
 LANES = 128
 
 
@@ -156,7 +157,7 @@
     return 4 * (z ^ dz) + 2 * (c ^ dc) + (x ^ dx if dx < 2 else dx - 2)
 
 
-def operate_kernel(first, plan, cols, pattern, right, left_own, left_other, *refs):
+def operate_kernel(first, plan, right_cols, left_cols, cols_other, pattern, right, left_own, left_other, *refs):
     count = len(plan)
     pieces, refs = refs[:count], refs[count:]
     if first:
@@ -189,7 +190,7 @@
         begin(hd_far, diag.at[1])
 
     def allowed(a, q, value):
-        return jnp.where(pattern[a, q] != 0, value, jnp.zeros_like(value))
+        return lax.select(pattern[a, q] != 0, value, jnp.zeros_like(value))
 
     for piece, offsets in zip(pieces, plan):
         base = 2 * half if piece.shape[0] == 4 else 0
@@ -201,10 +202,10 @@
                 field[row, start : start + tall, span] = allowed(row, q, value) if first else value
 
     def right_col(term, b, j):
-        return cols[(2 * term) * table + b * links + j]
+        return cols_other[j, b] if term else right_cols[j, 0, b]
 
     def left_col(term, a, j):
-        return cols[(2 * term + 1) * table + a * links + j]
+        return cols_other[8 + j, a] if term else left_cols[j, 0, a]
 
     sources = [[left_col(term, rows[at], j) for at in range(2) for j in range(links)] for term in range(2)]
 
@@ -318,7 +319,7 @@
     return pl.pallas_call(
         functools.partial(operate_kernel, first, plan),
         out_shape=out_shape,
-        in_specs=[SMEM, SMEM, VMEM, ANY, ANY] + [VMEM] * len(pieces) + extra_specs,
+        in_specs=[SMEM, SMEM, SMEM, SMEM, VMEM, ANY, ANY] + [VMEM] * len(pieces) + extra_specs,
         out_specs=(VMEM,) * len(out_shape),
         scratch_shapes=[
             pltpu.VMEM((sectors, block, width), jnp.bfloat16),
@@ -334,7 +335,7 @@
             transcendentals=0,
         ),
         name="operate_first" if first else "operate_second",
-    )(cols, pattern, right, *left, *pieces, *extra)
+    )(*cols, pattern, right, *left, *pieces, *extra)
 
 
 def arrange_kernel(own, near, far, out, found, sems):
@@ -371,7 +372,9 @@
     )(own, near, far)
 
 
-def prepare_kernel(pattern, theta, hd, right, left, mix_a, mix_b, packed, own_out, waves, diag, sems):
+def prepare_kernel(
+    pattern, theta, hd, right, left, right_cols, left_cols, mix_a, mix_b, packed, own_out, waves, diag, spots, sems
+):
     z, x, c = place()
     half = z // 2
     middle = in_middle(z)
@@ -398,6 +401,12 @@
     ]
     for copy in copies:
         copy.start()
+    last = part + 2 * links
+    spots[...] = jnp.zeros_like(spots)
+    spots[0:links, 0:sectors] = right_cols[:, 0, :].astype(jnp.float32)
+    spots[8 : 8 + links, 0:sectors] = left_cols[:, 0, :].astype(jnp.float32)
+    packed[last] = jnp.zeros_like(packed[last])
+    packed[last, 0:16, :] = spots[...].astype(jnp.bfloat16)
     for copy in copies[:3]:
         copy.wait()
     zero = jnp.zeros((8, LANES), jnp.float32)
@@ -429,26 +438,27 @@
         copy.wait()
 
 
-def prepare(pattern, theta, hd, right, left):
+def prepare(pattern, theta, hd, right, left, *cols):
     _, _, block, width = theta.shape
     table = right.shape[0]
     links = table * block // width
     kind = jnp.bfloat16
     mix = jax.ShapeDtypeStruct((block, width + LANES), kind)
-    packed = jax.ShapeDtypeStruct((table // 2 + 2 * links, block, block), kind)
+    packed = jax.ShapeDtypeStruct((table // 2 + 2 * links + 1, block, block), kind)
     return pl.pallas_call(
         prepare_kernel,
         out_shape=(mix, mix, packed, jax.ShapeDtypeStruct((8, LANES), jnp.float32)),
-        in_specs=[SMEM, ANY, ANY, ANY, ANY],
+        in_specs=[SMEM, ANY, ANY, ANY, ANY, VMEM, VMEM],
         out_specs=(VMEM,) * 4,
         scratch_shapes=[
             pltpu.VMEM((2, block, width), kind),
             pltpu.VMEM((block, width), kind),
+            pltpu.VMEM((16, LANES), jnp.float32),
             pltpu.SemaphoreType.DMA((8,)),
         ],
-        compiler_params=pltpu.CompilerParams(vmem_limit_bytes=VMEM_LIMIT),
+        compiler_params=pltpu.CompilerParams(vmem_limit_bytes=PREPARE_LIMIT),
         name="prepare",
-    )(pattern, theta, hd, right, left)
+    )(pattern, theta, hd, right, left, *cols)
 
 
 def total_of(rows):
@@ -578,28 +588,27 @@
     middle = in_middle(z)
     right = right_blocks.reshape(-1, block, block)
     left = left_blocks.reshape(-1, block, block)
-    cols = jnp.concatenate([right_cols.reshape(-1), left_cols.reshape(-1)])
-
-    mix_a, mix_b, packed, weight_own = prepare(pattern, halves, diag, right, left)
+    cols = (right_cols.transpose(2, 0, 1), left_cols.transpose(2, 0, 1))
+
+    mix_a, mix_b, packed, weight_own = prepare(pattern, halves, diag, right, left, *cols)
     mix_a = lax.ppermute(mix_a, "blk", [(0, 2), (2, 3), (3, 1), (1, 0)])
     mix_b = lax.ppermute(mix_b, "blk", [(0, 1), (1, 3), (3, 2), (2, 0)])
     operators = across(packed, "ops", 1)
     theta_core = across(theta, "sub", 1)
 
-    cols_other = across(after(cols, mix_a), "ops", 1)
-    cols = jnp.concatenate([cols, cols_other])
-    mix_a_core = across(mix_a, "sub", 1)
-    operators_core = across(after(operators, cols_other)[: right.shape[0] // 2], "sub", 1)
-
-    mix_b = after(mix_b, theta_core, mix_a_core, operators_core)
+    mix_a, mix_b = after((mix_a, mix_b), theta_core)
     far = jnp.where(middle, mix_a[:, :width], mix_b[:, :width])
     far_z = [across(far[at : at + chunk], "blk", 1) for at in (0, chunk)]
     far_x = across(far, "ops", 1)
+    mix_a_core = across(mix_a, "sub", 1)
     mix_b_core = across(mix_b, "sub", 1)
+    operators = after(operators, mix_b)
+    operators_core = across(operators[: right.shape[0] // 2], "sub", 1)
     turned = arrange(right, operators, operators_core)
+    cols = (*cols, operators[-1, :16, :sectors].astype(jnp.int32))
 
     own_b = lax.dynamic_slice(halves, (half, 1, 0, 0), (1, 1, block, width))[0, 0]
-    near_b = across(after(own_b, far_z[0], mix_b_core, turned), "blk", 1)
+    near_b = across(after(own_b, far_z[0], mix_a_core, mix_b_core, turned), "blk", 1)
     far_zx = [across(value, "ops", 1) for value in far_z]
     far_x_core = across(far_x, "sub", 1)
     far_z_core = [across(value, "sub", 1) for value in far_z]
@@ -710,14 +719,15 @@
 
     far_in = across(two_far, "blk", 3)
     near_in = across(two_near, "ops", 1)
-    sums = stats_three + across(stats_three, "sub", 1)
-    other = jnp.where(middle, other_middle, after(other_end, sums))
+    late_in = across(after(two_late, far_in, near_in), "blk", 3)
+    far_in_x = across(after(far_in, near_in), "ops", 1)
+    other = jnp.where(middle, other_middle, after(other_end, near_in))
     other_x = across(other, "ops", 1)
+    sums = after(stats_three, far_in, near_in)
+    sums = sums + across(sums, "sub", 1)
     sums = sums + across(sums, "blk", 1)
     both = jnp.stack([sums, across(sums, "blk", 2)])
-    late_in = across(after(two_late, far_in), "blk", 3)
-    far_in_x = across(after(far_in, near_in), "ops", 1)
-    both = both + across(after(both, far_in), "ops", 1)
+    both = both + across(both, "ops", 1)
     other, other_x = after((other, other_x), late_in)
     late_in_x = across(late_in, "ops", 1)
     both = jnp.sum(jnp.where(half == 0, both, both[::-1])[:, :5], axis=2)

time: 234 us -> 228 us (0.974)
  local copies, waits for them, and re-layouts: 18 us -> 7.83 us
  Pallas kernels: 39.1 us -> 43.4 us
    unnamed x50 -> x28, local copies, waits for them, and re-layouts: 14.7 us -> 4.72 us
    ppermute x45 -> x44, starting transfers between devices: 34.9 us -> 37.8 us  [across(): return lax.ppermute(value, axis, [(i, i ^ distance) for i in range(size)])]
    pallas_call x1, Pallas kernels: 1.73 us -> 4.18 us  [prepare(): pl.pallas_call(prepare_kernel, out_shape=(mix, mix, packed, jax.ShapeDtyp...]
    ppermute x45 -> x44, waiting for transfers between devices: 89.7 us -> 89.1 us  [across(): return lax.ppermute(value, axis, [(i, i ^ distance) for i in range(size)])]
  transfers between devices with their start and end apart: 55 -> 54, of which waited for: 25 -> 28; matrix products, arithmetic and copies ran while one was open for 2% -> 2% of each run, Pallas kernels for 15% -> 11%
where the time goes in v9:
time: 228 us
  waiting for transfers between devices  121 us (53%)
  starting transfers between devices  51.7 us (23%)
  Pallas kernels  43.4 us (19%)
  local copies, waits for them, and re-layouts  7.83 us (3%)
    ppermute x44, waiting for transfers between devices, across(): return lax.ppermute(value, axis, [(i, i ^ distance) for i in range(size)])  89.1 us
    ppermute x44, starting transfers between devices, across(): return lax.ppermute(value, axis, [(i, i ^ distance) for i in range(size)])  37.8 us
    pallas_call x2, Pallas kernels, operate(): pl.pallas_call(functools.partial(operate_kernel, first, plan), out_shape=...  29.3 us
    ppermute x1, waiting for transfers between devices, shards(): mix_a = lax.ppermute(mix_a, 'blk', [(0, 2), (2, 3), (3, 1), (1, 0)])  13.3 us
    ppermute x1, waiting for transfers between devices, shards(): mix_b = lax.ppermute(mix_b, 'blk', [(0, 1), (1, 3), (3, 2), (2, 0)])  12.8 us
    ppermute x6, starting transfers between devices, share(): lax.ppermute(pair, axes, [(i, i ^ distance) for i in range(count)])  6.98 us
    ppermute x6, waiting for transfers between devices, share(): lax.ppermute(pair, axes, [(i, i ^ distance) for i in range(count)])  6.17 us
    unnamed x28, local copies, waits for them, and re-layouts  4.72 us
  transfers between devices with their start and end apart: 54, of which 28 were waited for; matrix products, arithmetic and copies ran while one was open for 2% of the time, Pallas kernels for 11%

profile of v9, /device:TPU:0, one launch (start us, length us, event | category | flops | bytes accessed | tf_op | source)
XLA Modules:
  0.0 227.6 jit_solution(14969127507510481371)
XLA Ops:
  1.1 4.2 %prepare.1 = (bf16[128,2176]{1,0:T(8,128)(2,1)}, bf16[128,2176]{1,0:T(8,128)(2,1)}, bf16[31,128,128]{2,1,0:T(8,128)(2,1)}, f32[8,128]{1,0:T(8,128)}) custom-call(s32[16,16]{1,0:T(8,128)} %pattern.5, bf16[2,2,128,2048]{3,2,1,0:T(8,128)(2,1)} %bitcast.95, bf16[2,128,2048]{2,1,0:T(8,128)(2,1)} %bitcast.56, bf16[48,128,128]{2,1,0:T(8,128)(2,1)} %bitcast.60, ...), custom_call_target="tpu_custom_call" | custom-call | tf_op jit(solution)/shard_map/prepare/pallas_call | solution.py:448
  5.3 2.5 %collective-permute-start = (bf16[31,128,128]{2,1,0:T(8,128)(2,1)}, bf16[31,128,128]{2,1,0:T(8,128)(2,1)S(1)}, u32[]{:S(2)}, u32[]{:S(2)}) collective-permute-start(bf16[31,128,128]{2,1,0:T(8,128)(2,1)} %get-tuple-element.33), channel_id=1, source_target_pairs={{0,2},{2,0},{1,3},{3,1},{4,6},{6,4},{5,7},{7,5},{8,10},{10,8},{9,1... | collective-permute-start | bytes 3047432 | tf_op jit(solution)/shard_map/ppermute | solution.py:125
  7.9 2.6 %collective-permute-start.1 = (bf16[128,2176]{1,0:T(8,128)(2,1)}, bf16[128,2176]{1,0:T(8,128)(2,1)S(1)}, u32[]{:S(2)}, u32[]{:S(2)}) collective-permute-start(bf16[128,2176]{1,0:T(8,128)(2,1)} %get-tuple-element.34), channel_id=1, source_target_pairs={{0,8},{8,12},{12,4},{4,0},{1,9},{9,13},{13,5},{5,1},{2,10},{10,14}... | collective-permute-start | bytes 1671176 | tf_op jit(solution)/shard_map/ppermute | solution.py:594
  10.5 13.3 %collective-permute-done.1 = bf16[128,2176]{1,0:T(8,128)(2,1)S(1)} collective-permute-done((bf16[128,2176]{1,0:T(8,128)(2,1)}, bf16[128,2176]{1,0:T(8,128)(2,1)S(1)}, u32[]{:S(2)}, u32[]{:S(2)}) %collective-permute-start.1) | collective-permute-done | bytes 557088 | tf_op jit(solution)/shard_map/ppermute | solution.py:594
  23.8 12.8 %collective-permute-done.2 = bf16[128,2176]{1,0:T(8,128)(2,1)S(1)} collective-permute-done((bf16[128,2176]{1,0:T(8,128)(2,1)}, bf16[128,2176]{1,0:T(8,128)(2,1)S(1)}, u32[]{:S(2)}, u32[]{:S(2)}) %collective-permute-start.2) | collective-permute-done | bytes 557088 | tf_op jit(solution)/shard_map/ppermute | solution.py:595
  43.2 2.8 %arrange.1.right = bf16[2,48,128,128]{3,2,1,0:T(8,128)(2,1)S(1)} custom-call(bf16[48,128,128]{2,1,0:T(8,128)(2,1)S(1)} %bitcast.61, bf16[31,128,128]{2,1,0:T(8,128)(2,1)S(1)} %collective-permute-done.near.left_other, bf16[24,128,128]{2,1,0:T(8,128)(2,1)} %collective-permute-done.4.far), custom_call_target="tpu_custom_call" | custom-call | tf_op jit(solution)/shard_map/arrange/pallas_call | solution.py:364
  46.0 1.6 copy-done
  51.2 16.4 %collective-permute-done.15 = bf16[64,2048]{1,0:T(8,128)(2,1)} collective-permute-done((bf16[64,2048]{1,0:T(8,128)(2,1)S(1)}, bf16[64,2048]{1,0:T(8,128)(2,1)}, u32[]{:S(2)}, u32[]{:S(2)}) %collective-permute-start.15) | collective-permute-done | bytes 262176 | tf_op jit(solution)/shard_map/ppermute | solution.py:125
  70.4 4.7 %collective-permute-done.17 = bf16[64,2048]{1,0:T(8,128)(2,1)} collective-permute-done((bf16[64,2048]{1,0:T(8,128)(2,1)}, bf16[64,2048]{1,0:T(8,128)(2,1)}, u32[]{:S(2)}, u32[]{:S(2)}) %collective-permute-start.17) | collective-permute-done | bytes 262176 | tf_op jit(solution)/shard_map/ppermute | solution.py:125
  75.6 2.6 %collective-permute-start.19 = (bf16[128,2048]{1,0:T(8,128)(2,1)S(1)}, bf16[128,2048]{1,0:T(8,128)(2,1)S(1)}, u32[]{:S(2)}, u32[]{:S(2)}) collective-permute-start(bf16[128,2048]{1,0:T(8,128)(2,1)S(1)} %dynamic-slice_bitcast_fusion), channel_id=1, source_target_pairs={{0,12},{4,8},{8,4},{12,0},{1,13},{5,9},{9,5},{13,1},{2,14},{6,10},... | collective-permute-start | bytes 1572872 | tf_op jit(solution)/shard_map/ppermute | solution.py:125
  79.2 15.9 %operate_first.1 = (bf16[2,128,2048]{2,1,0:T(8,128)(2,1)S(1)}, bf16[2,128,2048]{2,1,0:T(8,128)(2,1)S(1)}, f32[8,128]{1,0:T(8,128)S(1)}) custom-call(s32[3,1,16]{2,1,0:T(1,128)S(1)} %bitcast.86, s32[3,1,16]{2,1,0:T(1,128)S(1)} %bitcast.89, s32[16,16]{1,0:T(8,128)S(1)} %bitcast_convert_fusion.cols_other, s32[16,16]{1,0:T(8,128)S(1)} %copy-done.8, ...), custom_call_target="tpu_custom_call" | custom-call | flops 3221225472 | bytes 16777216 | tf_op jit(solution)/shard_map/operate_first/pallas_call | solution.py:319
  97.9 1.9 collective-permute-start.23
  100.8 1.7 collective-permute-done.23.refs_3_
  102.5 2.2 update.1
  106.4 1.9 collective-permute-start.26
  110.1 2.8 %collective-permute-done.27.refs_3_ = f32[2,8,128]{2,1,0:T(8,128)S(1)} collective-permute-done((f32[2,8,128]{2,1,0:T(8,128)S(1)}, f32[2,8,128]{2,1,0:T(8,128)S(1)}, u32[]{:S(2)}, u32[]{:S(2)}) %collective-permute-start.27) | collective-permute-done | bytes 8224 | tf_op jit(solution)/shard_map/ppermute | solution.py:134
  116.7 9.2 %collective-permute-done.28 = bf16[128,2048]{1,0:T(8,128)(2,1)S(1)} collective-permute-done((bf16[128,2048]{1,0:T(8,128)(2,1)S(1)}, bf16[128,2048]{1,0:T(8,128)(2,1)S(1)}, u32[]{:S(2)}, u32[]{:S(2)}) %collective-permute-start.28) | collective-permute-done | bytes 524320 | tf_op jit(solution)/shard_map/ppermute | solution.py:125
  126.0 4.1 %collective-permute-start.35 = (bf16[128,2048]{1,0:T(8,128)(2,1)S(1)}, bf16[128,2048]{1,0:T(8,128)(2,1)S(1)}, u32[]{:S(2)}, u32[]{:S(2)}) collective-permute-start(bf16[128,2048]{1,0:T(8,128)(2,1)S(1)} %get-tuple-element.52), channel_id=1, source_target_pairs={{0,4},{4,0},{8,12},{12,8},{1,5},{5,1},{9,13},{13,9},{2,6},{6,2},{1... | collective-permute-start | bytes 1572872 | tf_op jit(solution)/shard_map/ppermute | solution.py:125
  132.2 10.7 %collective-permute-done.35 = bf16[128,2048]{1,0:T(8,128)(2,1)S(1)} collective-permute-done((bf16[128,2048]{1,0:T(8,128)(2,1)S(1)}, bf16[128,2048]{1,0:T(8,128)(2,1)S(1)}, u32[]{:S(2)}, u32[]{:S(2)}) %collective-permute-start.35) | collective-permute-done | bytes 524320 | tf_op jit(solution)/shard_map/ppermute | solution.py:125
  142.9 2.0 collective-permute-done.31.refs_1_
  145.0 6.9 %collective-permute-done.40 = bf16[128,2048]{1,0:T(8,128)(2,1)S(1)} collective-permute-done((bf16[128,2048]{1,0:T(8,128)(2,1)S(1)}, bf16[128,2048]{1,0:T(8,128)(2,1)S(1)}, u32[]{:S(2)}, u32[]{:S(2)}) %collective-permute-start.40) | collective-permute-done | bytes 524320 | tf_op jit(solution)/shard_map/ppermute | solution.py:125
  155.3 13.4 %operate_second.1 = (bf16[128,2048]{1,0:T(8,128)(2,1)S(1)}, bf16[64,2048]{1,0:T(8,128)(2,1)S(1)}, bf16[64,2048]{1,0:T(8,128)(2,1)}, f32[8,128]{1,0:T(8,128)S(1)}) custom-call(s32[3,1,16]{2,1,0:T(1,128)S(1)} %bitcast.87, s32[3,1,16]{2,1,0:T(1,128)S(1)} %bitcast.90, s32[16,16]{1,0:T(8,128)S(1)} %bitcast_convert_fusion.cols_other, s32[16,16]{1,0:T(8,128)S(1)} %copy-done.8, ...), custom_call_target="tpu_custom_call" | custom-call | bytes 1024 | tf_op jit(solution)/shard_map/operate_second/pallas_call | solution.py:319
  169.9 3.4 %collective-permute-start.32 = (bf16[128,2048]{1,0:T(8,128)(2,1)S(1)}, bf16[128,2048]{1,0:T(8,128)(2,1)}, u32[]{:S(2)}, u32[]{:S(2)}) collective-permute-start(bf16[128,2048]{1,0:T(8,128)(2,1)S(1)} %get-tuple-element.52), channel_id=1, source_target_pairs={{0,12},{12,0},{1,13},{13,1},{2,14},{14,2},{3,15},{15,3},{16,28},{2... | collective-permute-start | bytes 1572872 | tf_op jit(solution)/shard_map/ppermute | solution.py:694
  173.3 2.4 %collective-permute-start.46 = (bf16[64,2048]{1,0:T(8,128)(2,1)S(1)}, bf16[64,2048]{1,0:T(8,128)(2,1)S(1)}, u32[]{:S(2)}, u32[]{:S(2)}) collective-permute-start(bf16[64,2048]{1,0:T(8,128)(2,1)S(1)} %get-tuple-element.56), channel_id=1, source_target_pairs={{0,12},{4,8},{8,4},{12,0},{1,13},{5,9},{9,5},{13,1},{2,14},{6,10},... | collective-permute-start | bytes 786440 | tf_op jit(solution)/shard_map/ppermute | solution.py:125
  175.7 17.3 %collective-permute-done.46.refs_2_ = bf16[64,2048]{1,0:T(8,128)(2,1)S(1)} collective-permute-done((bf16[64,2048]{1,0:T(8,128)(2,1)S(1)}, bf16[64,2048]{1,0:T(8,128)(2,1)S(1)}, u32[]{:S(2)}, u32[]{:S(2)}) %collective-permute-start.46) | collective-permute-done | bytes 262176 | tf_op jit(solution)/shard_map/ppermute | solution.py:125
  194.2 3.6 %collective-permute-start.51 = (f32[8,128]{1,0:T(8,128)S(1)}, f32[8,128]{1,0:T(8,128)S(1)}, u32[]{:S(2)}, u32[]{:S(2)}) collective-permute-start(f32[8,128]{1,0:T(8,128)S(1)} %add.22), channel_id=1, source_target_pairs={{0,4},{4,0},{8,12},{12,8},{1,5},{5,1},{9,13},{13,9},{2,6},{6,2},{1... | collective-permute-start | bytes 12296 | tf_op jit(solution)/shard_map/ppermute | solution.py:125
  199.3 2.0 collective-permute-start.52
  202.5 2.1 collective-permute-start.47
  209.5 1.8 collective-permute-done.47.refs_3_
  213.1 2.3 %assemble.4.refs_1_ = bf16[2,2,128,2048]{3,2,1,0:T(8,128)(2,1)} custom-call(bf16[128,2048]{1,0:T(8,128)(2,1)S(1)} %get-tuple-element.53.refs_0_, bf16[128,2048]{1,0:T(8,128)(2,1)S(1)} %collective-permute-done.44.refs_1_, bf16[64,2048]{1,0:T(8,128)(2,1)S(1)} %collective-permute-done.46.refs_2_, bf16[64,2048]{1,0:T(8,128)(2,1)} %collective-permute-done.47.refs_3_, ...), custom_call_target="tpu_custom_call" | custom-call | tf_op jit(solution)/shard_map/assemble/pallas_call | solution.py:561
  215.4 6.5 %collective-permute-done.45.refs_3_ = bf16[128,2048]{1,0:T(8,128)(2,1)S(1)} collective-permute-done((bf16[128,2048]{1,0:T(8,128)(2,1)S(1)}, bf16[128,2048]{1,0:T(8,128)(2,1)S(1)}, u32[]{:S(2)}, u32[]{:S(2)}) %collective-permute-start.45) | collective-permute-done | bytes 524320 | tf_op jit(solution)/shard_map/ppermute | solution.py:125
  221.8 3.5 %collective-permute-done.48.refs_0_ = bf16[64,2048]{1,0:T(8,128)(2,1)S(1)} collective-permute-done((bf16[64,2048]{1,0:T(8,128)(2,1)}, bf16[64,2048]{1,0:T(8,128)(2,1)S(1)}, u32[]{:S(2)}, u32[]{:S(2)}) %collective-permute-start.48) | collective-permute-done | bytes 262176 | tf_op jit(solution)/shard_map/ppermute | solution.py:125
  (130 shorter events, 45.4 us)
Async XLA Ops:
  0.6 36.1 %collective-permute-start.3 = (bf16[2,256,2048]{2,1,0:T(8,128)(2,1)}, bf16[2,256,2048]{2,1,0:T(8,128)(2,1)}, u32[]{:S(2)}, u32[]{:S(2)}) collective-permute-start(bf16[2,256,2048]{2,1,0:T(8,128)(2,1)} %param.7), channel_id=1, source_target_pairs={{0,1},{1,0},{2,3},{3,2},{4,5},{5,4},{6,7},{7,6},{8,9},{9,8},{10,11... | collective-permute-start | bytes 6291464 | tf_op jit(solution)/shard_map/ppermute | solution.py:125
  5.3 31.4 %collective-permute-start = (bf16[31,128,128]{2,1,0:T(8,128)(2,1)}, bf16[31,128,128]{2,1,0:T(8,128)(2,1)S(1)}, u32[]{:S(2)}, u32[]{:S(2)}) collective-permute-start(bf16[31,128,128]{2,1,0:T(8,128)(2,1)} %get-tuple-element.33), channel_id=1, source_target_pairs={{0,2},{2,0},{1,3},{3,1},{4,6},{6,4},{5,7},{7,5},{8,10},{10,8},{9,1... | collective-permute-start | bytes 3047432 | tf_op jit(solution)/shard_map/ppermute | solution.py:125
  7.9 15.9 %collective-permute-start.1 = (bf16[128,2176]{1,0:T(8,128)(2,1)}, bf16[128,2176]{1,0:T(8,128)(2,1)S(1)}, u32[]{:S(2)}, u32[]{:S(2)}) collective-permute-start(bf16[128,2176]{1,0:T(8,128)(2,1)} %get-tuple-element.34), channel_id=1, source_target_pairs={{0,8},{8,12},{12,4},{4,0},{1,9},{9,13},{13,5},{5,1},{2,10},{10,14}... | collective-permute-start | bytes 1671176 | tf_op jit(solution)/shard_map/ppermute | solution.py:594
  10.5 26.2 %collective-permute-start.2 = (bf16[128,2176]{1,0:T(8,128)(2,1)}, bf16[128,2176]{1,0:T(8,128)(2,1)S(1)}, u32[]{:S(2)}, u32[]{:S(2)}) collective-permute-start(bf16[128,2176]{1,0:T(8,128)(2,1)} %get-tuple-element.35), channel_id=1, source_target_pairs={{0,4},{4,12},{12,8},{8,0},{1,5},{5,13},{13,9},{9,1},{2,6},{6,14},{... | collective-permute-start | bytes 1671176 | tf_op jit(solution)/shard_map/ppermute | solution.py:595
  36.7 11.5 %collective-permute-start.6 = (bf16[128,2176]{1,0:T(8,128)(2,1)S(1)}, bf16[128,2176]{1,0:T(8,128)(2,1)}, u32[]{:S(2)}, u32[]{:S(2)}) collective-permute-start(bf16[128,2176]{1,0:T(8,128)(2,1)S(1)} %collective-permute-done.2), channel_id=1, source_target_pairs={{0,1},{1,0},{2,3},{3,2},{4,5},{5,4},{6,7},{7,6},{8,9},{9,8},{10,11... | collective-permute-start | bytes 1671176 | tf_op jit(solution)/shard_map/ppermute | solution.py:125
  38.2 10.0 %collective-permute-start.5 = (bf16[128,2176]{1,0:T(8,128)(2,1)S(1)}, bf16[128,2176]{1,0:T(8,128)(2,1)}, u32[]{:S(2)}, u32[]{:S(2)}) collective-permute-start(bf16[128,2176]{1,0:T(8,128)(2,1)S(1)} %collective-permute-done.1), channel_id=1, source_target_pairs={{0,1},{1,0},{2,3},{3,2},{4,5},{5,4},{6,7},{7,6},{8,9},{9,8},{10,11... | collective-permute-start | bytes 1671176 | tf_op jit(solution)/shard_map/ppermute | solution.py:125
  39.2 8.9 %collective-permute-start.7 = (bf16[64,2048]{1,0:T(8,128)(2,1)}, bf16[64,2048]{1,0:T(8,128)(2,1)S(1)}, u32[]{:S(2)}, u32[]{:S(2)}) collective-permute-start(bf16[64,2048]{1,0:T(8,128)(2,1)} %get-tuple-element.64), channel_id=1, source_target_pairs={{0,4},{4,0},{8,12},{12,8},{1,5},{5,1},{9,13},{13,9},{2,6},{6,2},{1... | collective-permute-start | bytes 786440 | tf_op jit(solution)/shard_map/ppermute | solution.py:125
  41.1 27.5 %collective-permute-start.10 = (bf16[128,2048]{1,0:T(8,128)(2,1)}, bf16[128,2048]{1,0:T(8,128)(2,1)}, u32[]{:S(2)}, u32[]{:S(2)}) collective-permute-start(bf16[128,2048]{1,0:T(8,128)(2,1)} %copy-done.12), channel_id=1, source_target_pairs={{0,2},{2,0},{1,3},{3,1},{4,6},{6,4},{5,7},{7,5},{8,10},{10,8},{9,1... | collective-permute-start | bytes 1572872 | tf_op jit(solution)/shard_map/ppermute | solution.py:125
  48.2 21.0 %collective-permute-start.8 = (bf16[128,2048]{1,0:T(8,128)(2,1)S(1)}, bf16[128,2048]{1,0:T(8,128)(2,1)}, u32[]{:S(2)}, u32[]{:S(2)}) collective-permute-start(bf16[128,2048]{1,0:T(8,128)(2,1)S(1)} %dynamic-slice_bitcast_fusion.1), channel_id=1, source_target_pairs={{0,4},{4,0},{8,12},{12,8},{1,5},{5,1},{9,13},{13,9},{2,6},{6,2},{1... | collective-permute-start | bytes 1572872 | tf_op jit(solution)/shard_map/ppermute | solution.py:125
  49.0 18.6 %collective-permute-start.15 = (bf16[64,2048]{1,0:T(8,128)(2,1)S(1)}, bf16[64,2048]{1,0:T(8,128)(2,1)}, u32[]{:S(2)}, u32[]{:S(2)}) collective-permute-start(bf16[64,2048]{1,0:T(8,128)(2,1)S(1)} %copy-done.13), channel_id=1, source_target_pairs={{0,4},{4,0},{8,12},{12,8},{1,5},{5,1},{9,13},{13,9},{2,6},{6,2},{1... | collective-permute-start | bytes 786440 | tf_op jit(solution)/shard_map/ppermute | solution.py:125
  50.2 19.0 %collective-permute-start.13 = (bf16[64,2048]{1,0:T(8,128)(2,1)S(1)}, bf16[64,2048]{1,0:T(8,128)(2,1)S(1)}, u32[]{:S(2)}, u32[]{:S(2)}) collective-permute-start(bf16[64,2048]{1,0:T(8,128)(2,1)S(1)} %collective-permute-done.7), channel_id=1, source_target_pairs={{0,2},{2,0},{1,3},{3,1},{4,6},{6,4},{5,7},{7,5},{8,10},{10,8},{9,1... | collective-permute-start | bytes 786440 | tf_op jit(solution)/shard_map/ppermute | solution.py:125
  68.6 9.5 %collective-permute-start.11 = (bf16[128,2048]{1,0:T(8,128)(2,1)}, bf16[128,2048]{1,0:T(8,128)(2,1)}, u32[]{:S(2)}, u32[]{:S(2)}) collective-permute-start(bf16[128,2048]{1,0:T(8,128)(2,1)} %collective-permute-done.10), channel_id=1, source_target_pairs={{0,1},{1,0},{2,3},{3,2},{4,5},{5,4},{6,7},{7,6},{8,9},{9,8},{10,11... | collective-permute-start | bytes 1572872 | tf_op jit(solution)/shard_map/ppermute | solution.py:125
  69.1 9.0 %collective-permute-start.9 = (bf16[128,2048]{1,0:T(8,128)(2,1)}, bf16[128,2048]{1,0:T(8,128)(2,1)}, u32[]{:S(2)}, u32[]{:S(2)}) collective-permute-start(bf16[128,2048]{1,0:T(8,128)(2,1)} %collective-permute-done.8), channel_id=1, source_target_pairs={{0,1},{1,0},{2,3},{3,2},{4,5},{5,4},{6,7},{7,6},{8,9},{9,8},{10,11... | collective-permute-start | bytes 1572872 | tf_op jit(solution)/shard_map/ppermute | solution.py:125
  75.6 24.2 %collective-permute-start.19 = (bf16[128,2048]{1,0:T(8,128)(2,1)S(1)}, bf16[128,2048]{1,0:T(8,128)(2,1)S(1)}, u32[]{:S(2)}, u32[]{:S(2)}) collective-permute-start(bf16[128,2048]{1,0:T(8,128)(2,1)S(1)} %dynamic-slice_bitcast_fusion), channel_id=1, source_target_pairs={{0,12},{4,8},{8,4},{12,0},{1,13},{5,9},{9,5},{13,1},{2,14},{6,10},... | collective-permute-start | bytes 1572872 | tf_op jit(solution)/shard_map/ppermute | solution.py:125
  113.5 12.4 %collective-permute-start.28 = (bf16[128,2048]{1,0:T(8,128)(2,1)S(1)}, bf16[128,2048]{1,0:T(8,128)(2,1)S(1)}, u32[]{:S(2)}, u32[]{:S(2)}) collective-permute-start(bf16[128,2048]{1,0:T(8,128)(2,1)S(1)} %get-tuple-element.51.refs_0_), channel_id=1, source_target_pairs={{0,4},{4,0},{8,12},{12,8},{1,5},{5,1},{9,13},{13,9},{2,6},{6,2},{1... | collective-permute-start | bytes 1572872 | tf_op jit(solution)/shard_map/ppermute | solution.py:125
  113.7 12.2 %collective-permute-start.29 = (bf16[128,2048]{1,0:T(8,128)(2,1)S(1)}, bf16[128,2048]{1,0:T(8,128)(2,1)S(1)}, u32[]{:S(2)}, u32[]{:S(2)}) collective-permute-start(bf16[128,2048]{1,0:T(8,128)(2,1)S(1)} %get-tuple-element.52), channel_id=1, source_target_pairs={{0,2},{2,0},{1,3},{3,1},{4,6},{6,4},{5,7},{7,5},{8,10},{10,8},{9,1... | collective-permute-start | bytes 1572872 | tf_op jit(solution)/shard_map/ppermute | solution.py:125
  115.2 10.8 %collective-permute-start.30 = (bf16[128,2048]{1,0:T(8,128)(2,1)S(1)}, bf16[128,2048]{1,0:T(8,128)(2,1)S(1)}, u32[]{:S(2)}, u32[]{:S(2)}) collective-permute-start(bf16[128,2048]{1,0:T(8,128)(2,1)S(1)} %get-tuple-element.52), channel_id=1, source_target_pairs={{4,8},{8,4},{5,9},{9,5},{6,10},{10,6},{7,11},{11,7},{20,24},{24,20... | collective-permute-start | bytes 1572872 | tf_op jit(solution)/shard_map/ppermute | solution.py:682
  116.1 16.0 %collective-permute-start.33 = (bf16[128,2048]{1,0:T(8,128)(2,1)S(1)}, bf16[128,2048]{1,0:T(8,128)(2,1)S(1)}, u32[]{:S(2)}, u32[]{:S(2)}) collective-permute-start(bf16[128,2048]{1,0:T(8,128)(2,1)S(1)} %get-tuple-element.51.refs_0_), channel_id=1, source_target_pairs={{0,1},{1,0},{2,3},{3,2},{4,5},{5,4},{6,7},{7,6},{8,9},{9,8},{10,11... | collective-permute-start | bytes 1572872 | tf_op jit(solution)/shard_map/ppermute | solution.py:125
  116.2 16.0 %collective-permute-start.34 = (bf16[128,2048]{1,0:T(8,128)(2,1)S(1)}, bf16[128,2048]{1,0:T(8,128)(2,1)S(1)}, u32[]{:S(2)}, u32[]{:S(2)}) collective-permute-start(bf16[128,2048]{1,0:T(8,128)(2,1)S(1)} %get-tuple-element.52), channel_id=1, source_target_pairs={{0,1},{1,0},{2,3},{3,2},{4,5},{5,4},{6,7},{7,6},{8,9},{9,8},{10,11... | collective-permute-start | bytes 1572872 | tf_op jit(solution)/shard_map/ppermute | solution.py:125
  126.0 17.0 %collective-permute-start.35 = (bf16[128,2048]{1,0:T(8,128)(2,1)S(1)}, bf16[128,2048]{1,0:T(8,128)(2,1)S(1)}, u32[]{:S(2)}, u32[]{:S(2)}) collective-permute-start(bf16[128,2048]{1,0:T(8,128)(2,1)S(1)} %get-tuple-element.52), channel_id=1, source_target_pairs={{0,4},{4,0},{8,12},{12,8},{1,5},{5,1},{9,13},{13,9},{2,6},{6,2},{1... | collective-permute-start | bytes 1572872 | tf_op jit(solution)/shard_map/ppermute | solution.py:125
  130.1 14.9 %collective-permute-start.31 = (bf16[128,2048]{1,0:T(8,128)(2,1)S(1)}, bf16[128,2048]{1,0:T(8,128)(2,1)S(1)}, u32[]{:S(2)}, u32[]{:S(2)}) collective-permute-start(bf16[128,2048]{1,0:T(8,128)(2,1)S(1)} %get-tuple-element.51.refs_0_), channel_id=1, source_target_pairs={{0,2},{2,0},{1,3},{3,1},{4,6},{6,4},{5,7},{7,5},{8,10},{10,8},{9,1... | collective-permute-start | bytes 1572872 | tf_op jit(solution)/shard_map/ppermute | solution.py:125
  131.3 20.6 %collective-permute-start.40 = (bf16[128,2048]{1,0:T(8,128)(2,1)S(1)}, bf16[128,2048]{1,0:T(8,128)(2,1)S(1)}, u32[]{:S(2)}, u32[]{:S(2)}) collective-permute-start(bf16[128,2048]{1,0:T(8,128)(2,1)S(1)} %collective-permute-done.28), channel_id=1, source_target_pairs={{0,2},{2,0},{1,3},{3,1},{4,6},{6,4},{5,7},{7,5},{8,10},{10,8},{9,1... | collective-permute-start | bytes 1572872 | tf_op jit(solution)/shard_map/ppermute | solution.py:125
  132.1 19.7 %collective-permute-start.41 = (bf16[128,2048]{1,0:T(8,128)(2,1)S(1)}, bf16[128,2048]{1,0:T(8,128)(2,1)S(1)}, u32[]{:S(2)}, u32[]{:S(2)}) collective-permute-start(bf16[128,2048]{1,0:T(8,128)(2,1)S(1)} %collective-permute-done.29), channel_id=1, source_target_pairs={{0,4},{4,0},{8,12},{12,8},{1,5},{5,1},{9,13},{13,9},{2,6},{6,2},{1... | collective-permute-start | bytes 1572872 | tf_op jit(solution)/shard_map/ppermute | solution.py:125
  132.1 20.2 %collective-permute-start.36 = (bf16[128,2048]{1,0:T(8,128)(2,1)S(1)}, bf16[128,2048]{1,0:T(8,128)(2,1)S(1)}, u32[]{:S(2)}, u32[]{:S(2)}) collective-permute-start(bf16[128,2048]{1,0:T(8,128)(2,1)S(1)} %collective-permute-done.28), channel_id=1, source_target_pairs={{0,1},{1,0},{2,3},{3,2},{4,5},{5,4},{6,7},{7,6},{8,9},{9,8},{10,11... | collective-permute-start | bytes 1572872 | tf_op jit(solution)/shard_map/ppermute | solution.py:125
  142.9 9.5 %collective-permute-start.39 = (bf16[128,2048]{1,0:T(8,128)(2,1)S(1)}, bf16[128,2048]{1,0:T(8,128)(2,1)S(1)}, u32[]{:S(2)}, u32[]{:S(2)}) collective-permute-start(bf16[128,2048]{1,0:T(8,128)(2,1)S(1)} %collective-permute-done.29), channel_id=1, source_target_pairs={{0,1},{1,0},{2,3},{3,2},{4,5},{5,4},{6,7},{7,6},{8,9},{9,8},{10,11... | collective-permute-start | bytes 1572872 | tf_op jit(solution)/shard_map/ppermute | solution.py:125
  168.7 24.3 %collective-permute-start.44 = (bf16[128,2048]{1,0:T(8,128)(2,1)S(1)}, bf16[128,2048]{1,0:T(8,128)(2,1)S(1)}, u32[]{:S(2)}, u32[]{:S(2)}) collective-permute-start(bf16[128,2048]{1,0:T(8,128)(2,1)S(1)} %get-tuple-element.53.refs_0_), channel_id=1, source_target_pairs={{0,2},{2,0},{1,3},{3,1},{4,6},{6,4},{5,7},{7,5},{8,10},{10,8},{9,1... | collective-permute-start | bytes 1572872 | tf_op jit(solution)/shard_map/ppermute | solution.py:125
  169.9 34.7 %collective-permute-start.32 = (bf16[128,2048]{1,0:T(8,128)(2,1)S(1)}, bf16[128,2048]{1,0:T(8,128)(2,1)}, u32[]{:S(2)}, u32[]{:S(2)}) collective-permute-start(bf16[128,2048]{1,0:T(8,128)(2,1)S(1)} %get-tuple-element.52), channel_id=1, source_target_pairs={{0,12},{12,0},{1,13},{13,1},{2,14},{14,2},{3,15},{15,3},{16,28},{2... | collective-permute-start | bytes 1572872 | tf_op jit(solution)/shard_map/ppermute | solution.py:694
  173.3 19.7 %collective-permute-start.46 = (bf16[64,2048]{1,0:T(8,128)(2,1)S(1)}, bf16[64,2048]{1,0:T(8,128)(2,1)S(1)}, u32[]{:S(2)}, u32[]{:S(2)}) collective-permute-start(bf16[64,2048]{1,0:T(8,128)(2,1)S(1)} %get-tuple-element.56), channel_id=1, source_target_pairs={{0,12},{4,8},{8,4},{12,0},{1,13},{5,9},{9,5},{13,1},{2,14},{6,10},... | collective-permute-start | bytes 786440 | tf_op jit(solution)/shard_map/ppermute | solution.py:125
  201.4 11.7 %collective-permute-start.49 = (bf16[64,2048]{1,0:T(8,128)(2,1)S(1)}, bf16[64,2048]{1,0:T(8,128)(2,1)}, u32[]{:S(2)}, u32[]{:S(2)}) collective-permute-start(bf16[64,2048]{1,0:T(8,128)(2,1)S(1)} %collective-permute-done.46.refs_2_), channel_id=1, source_target_pairs={{0,2},{2,0},{1,3},{3,1},{4,6},{6,4},{5,7},{7,5},{8,10},{10,8},{9,1... | collective-permute-start | bytes 786440 | tf_op jit(solution)/shard_map/ppermute | solution.py:125
  202.5 8.8 %collective-permute-start.47 = (bf16[64,2048]{1,0:T(8,128)(2,1)}, bf16[64,2048]{1,0:T(8,128)(2,1)}, u32[]{:S(2)}, u32[]{:S(2)}) collective-permute-start(bf16[64,2048]{1,0:T(8,128)(2,1)} %get-tuple-element.57), channel_id=1, source_target_pairs={{0,12},{4,8},{8,4},{12,0},{1,13},{5,9},{9,5},{13,1},{2,14},{6,10},... | collective-permute-start | bytes 786440 | tf_op jit(solution)/shard_map/ppermute | solution.py:125
  206.9 14.9 %collective-permute-start.45 = (bf16[128,2048]{1,0:T(8,128)(2,1)S(1)}, bf16[128,2048]{1,0:T(8,128)(2,1)S(1)}, u32[]{:S(2)}, u32[]{:S(2)}) collective-permute-start(bf16[128,2048]{1,0:T(8,128)(2,1)S(1)} %broadcast_select_fusion.refs_2_), channel_id=1, source_target_pairs={{0,2},{2,0},{1,3},{3,1},{4,6},{6,4},{5,7},{7,5},{8,10},{10,8},{9,1... | collective-permute-start | bytes 1572872 | tf_op jit(solution)/shard_map/ppermute | solution.py:125
  211.3 14.0 %collective-permute-start.48 = (bf16[64,2048]{1,0:T(8,128)(2,1)}, bf16[64,2048]{1,0:T(8,128)(2,1)S(1)}, u32[]{:S(2)}, u32[]{:S(2)}) collective-permute-start(bf16[64,2048]{1,0:T(8,128)(2,1)} %collective-permute-done.47.refs_3_), channel_id=1, source_target_pairs={{0,2},{2,0},{1,3},{3,1},{4,6},{6,4},{5,7},{7,5},{8,10},{10,8},{9,1... | collective-permute-start | bytes 786440 | tf_op jit(solution)/shard_map/ppermute | solution.py:125
  (36 other events, 367.7 us)

commit v10 on v9

--- a/solution.py
+++ b/solution.py
@@ -161,8 +161,8 @@
     count = len(plan)
     pieces, refs = refs[:count], refs[count:]
     if first:
-        weight_own, psi_out, off_out, stats_out = refs[:4]
-        refs = refs[4:]
+        masks, weight_own, psi_out, off_out, stats_out = refs[:5]
+        refs = refs[5:]
     else:
         hd_own, hd_far, psi_in, off_in, stats_in, near_out, far_out, late_out, stats_out = refs[:9]
         refs = refs[9:]
@@ -196,10 +196,11 @@
         base = 2 * half if piece.shape[0] == 4 else 0
         for at, (dz, dx, dc, start, tall) in enumerate(offsets):
             row = row_of(dz, dx, dc)
-            for q in range(sectors):
-                span = slice(q * block, (q + 1) * block)
-                value = piece[base + at, :, span]
-                field[row, start : start + tall, span] = allowed(row, q, value) if first else value
+            for line in range(0, tall, 16):
+                value = piece[base + at, line : line + 16, 0:width]
+                if first:
+                    value = value * masks[row]
+                field[row, start + line : start + line + 16, :] = value
 
     def right_col(term, b, j):
         return cols_other[j, b] if term else right_cols[j, 0, b]
@@ -313,7 +314,7 @@
     some = jax.ShapeDtypeStruct((block // 2, width), jnp.bfloat16)
     stats = jax.ShapeDtypeStruct((8, LANES), jnp.float32)
     out_shape = (rows, rows, stats) if first else (one, some, some, stats)
-    extra_specs = [VMEM] if first else [ANY, ANY, VMEM, VMEM, VMEM]
+    extra_specs = [VMEM, VMEM] if first else [ANY, ANY, VMEM, VMEM, VMEM]
     inner = 2 * 2 * sectors * 2 * links * links * block * block * block
     outer = 2 * 2 * 2 * links * block * block * width
     return pl.pallas_call(
@@ -340,11 +341,11 @@
 
 def arrange_kernel(own, near, far, out, found, sems):
     _, _, c = place()
-    part = far.shape[0]
+    part = own.shape[0] // 2
     copies = [
         pltpu.make_async_copy(own, found.at[0], sems.at[0]),
         pltpu.make_async_copy(near.at[pl.ds(0, part)], found.at[1, pl.ds(c * part, part)], sems.at[1]),
-        pltpu.make_async_copy(far, found.at[1, pl.ds((1 - c) * part, part)], sems.at[2]),
+        pltpu.make_async_copy(far.at[pl.ds(0, part)], found.at[1, pl.ds((1 - c) * part, part)], sems.at[2]),
     ]
     for copy in copies:
         copy.start()
@@ -584,7 +585,6 @@
 
     halves = theta.reshape(roots, 2, block, width)
     diag = hdiag.reshape(2, block, width)
-    chunk = block // 2
     middle = in_middle(z)
     right = right_blocks.reshape(-1, block, block)
     left = left_blocks.reshape(-1, block, block)
@@ -598,23 +598,25 @@
 
     mix_a, mix_b = after((mix_a, mix_b), theta_core)
     far = jnp.where(middle, mix_a[:, :width], mix_b[:, :width])
-    far_z = [across(far[at : at + chunk], "blk", 1) for at in (0, chunk)]
+    far_z = across(far, "blk", 1)
     far_x = across(far, "ops", 1)
     mix_a_core = across(mix_a, "sub", 1)
     mix_b_core = across(mix_b, "sub", 1)
     operators = after(operators, mix_b)
-    operators_core = across(operators[: right.shape[0] // 2], "sub", 1)
+    operators_core = across(operators, "sub", 1)
     turned = arrange(right, operators, operators_core)
     cols = (*cols, operators[-1, :16, :sectors].astype(jnp.int32))
+    masks = jnp.repeat(pattern.astype(jnp.bfloat16), block, axis=1)
+    masks = jnp.broadcast_to(masks[:, None, :], (sectors, 16, width))
 
     own_b = lax.dynamic_slice(halves, (half, 1, 0, 0), (1, 1, block, width))[0, 0]
-    near_b = across(after(own_b, far_z[0], mix_a_core, mix_b_core, turned), "blk", 1)
-    far_zx = [across(value, "ops", 1) for value in far_z]
+    near_b = across(after(own_b, mix_a_core, mix_b_core, turned), "blk", 1)
+    far_zx = across(far_z, "ops", 1)
     far_x_core = across(far_x, "sub", 1)
-    far_z_core = [across(value, "sub", 1) for value in far_z]
+    far_z_core = across(far_z, "sub", 1)
     hd_far = lax.dynamic_index_in_dim(diag, x, 0, keepdims=False)
-    hd_far = across(after(hd_far, far_z[1]), "blk", 3)
-    far_zx_core = [across(value, "sub", 1) for value in far_zx]
+    hd_far = across(after(hd_far, far_z), "blk", 3)
+    far_zx_core = across(far_zx, "sub", 1)
     near_b_core = across(near_b, "sub", 1)
 
     left = (left, operators)
@@ -632,20 +634,15 @@
         (near_b_core, (1, 3, 1)),
         (far_x, (2, 1, 0)),
         (far_x_core, (2, 1, 1)),
+        (far_z, (3, 0, 0)),
+        (far_z_core, (3, 0, 1)),
+        (far_zx, (3, 1, 0)),
+        (far_zx_core, (3, 1, 1)),
     ):
         pieces.append(piece[None])
         plan.append((offset + (0, block),))
-    for at in range(2):
-        for piece, offset in (
-            (far_z[at], (3, 0, 0)),
-            (far_z_core[at], (3, 0, 1)),
-            (far_zx[at], (3, 1, 0)),
-            (far_zx_core[at], (3, 1, 1)),
-        ):
-            pieces.append(piece[None])
-            plan.append((offset + (at * chunk, chunk),))
     psi, off_one, stats_one = operate(
-        True, tuple(plan), pieces, cols, pattern, turned, left, (weight_own,)
+        True, tuple(plan), pieces, cols, pattern, turned, left, (masks, weight_own)
     )
 
     found = share(stats_one)
@@ -719,14 +716,14 @@
 
     far_in = across(two_far, "blk", 3)
     near_in = across(two_near, "ops", 1)
-    late_in = across(after(two_late, far_in, near_in), "blk", 3)
+    late_in = across(after(two_late, far_in), "blk", 3)
     far_in_x = across(after(far_in, near_in), "ops", 1)
-    other = jnp.where(middle, other_middle, after(other_end, near_in))
+    sums = stats_three + across(stats_three, "sub", 1)
+    other = jnp.where(middle, other_middle, after(other_end, sums))
     other_x = across(other, "ops", 1)
-    sums = after(stats_three, far_in, near_in)
-    sums = sums + across(sums, "sub", 1)
-    sums = sums + across(sums, "blk", 1)
-    both = jnp.stack([sums, across(sums, "blk", 2)])
+    sums = after(sums, far_in)
+    both = jnp.stack([sums + across(sums, "blk", 1), across(sums, "blk", 2) + across(sums, "blk", 3)])
+    both = after(both, late_in)
     both = both + across(both, "ops", 1)
     other, other_x = after((other, other_x), late_in)
     late_in_x = across(late_in, "ops", 1)

time: 228 us -> 209 us (0.917)
  waiting for transfers between devices: 121 us -> 109 us
  starting transfers between devices: 51.7 us -> 48 us
  Pallas kernels: 43.4 us -> 40.1 us
    ppermute x44 -> x41, waiting for transfers between devices: 89.1 us -> 76.1 us  [across(): return lax.ppermute(value, axis, [(i, i ^ distance) for i in range(size)])]
    ppermute x44 -> x41, starting transfers between devices: 37.8 us -> 34 us  [across(): return lax.ppermute(value, axis, [(i, i ^ distance) for i in range(size)])]
    pallas_call x2, Pallas kernels: 29.3 us -> 26 us  [operate(): pl.pallas_call(functools.partial(operate_kernel, first, plan), out_shape=...]
    unnamed x28 -> x23, local copies, waits for them, and re-layouts: 4.72 us -> 4.39 us
  transfers between devices with their start and end apart: 54 -> 51, of which waited for: 28 -> 24; matrix products, arithmetic and copies ran while one was open for 2% -> 2% of each run, Pallas kernels for 11% -> 18%
where the time goes in v10:
time: 209 us; the launch traced here: 206 us
  waiting for transfers between devices  109 us (52%)
  starting transfers between devices  48 us (23%)
  Pallas kernels  40.1 us (19%)
  local copies, waits for them, and re-layouts  6.72 us (3%)
    ppermute x41, waiting for transfers between devices, across(): return lax.ppermute(value, axis, [(i, i ^ distance) for i in range(size)])  76.1 us
    ppermute x41, starting transfers between devices, across(): return lax.ppermute(value, axis, [(i, i ^ distance) for i in range(size)])  34 us
    pallas_call x2, Pallas kernels, operate(): pl.pallas_call(functools.partial(operate_kernel, first, plan), out_shape=...  26 us
    ppermute x1, waiting for transfers between devices, shards(): mix_a = lax.ppermute(mix_a, 'blk', [(0, 2), (2, 3), (3, 1), (1, 0)])  13.3 us
    ppermute x1, waiting for transfers between devices, shards(): mix_b = lax.ppermute(mix_b, 'blk', [(0, 1), (1, 3), (3, 2), (2, 0)])  12.9 us
    ppermute x6, starting transfers between devices, share(): lax.ppermute(pair, axes, [(i, i ^ distance) for i in range(count)])  6.98 us
    ppermute x6, waiting for transfers between devices, share(): lax.ppermute(pair, axes, [(i, i ^ distance) for i in range(count)])  6.32 us
    pallas_call x3, Pallas kernels, assemble(): pl.pallas_call(functools.partial(assemble_kernel, places, len(based)), ou...  4.42 us
  transfers between devices with their start and end apart: 51, of which 24 were waited for; matrix products, arithmetic and copies ran while one was open for 2% of the time, Pallas kernels for 18%

profile of v10, /device:TPU:0, one launch (start us, length us, event | category | flops | bytes accessed | tf_op | source)
XLA Modules:
  0.0 206.4 jit_solution(3083888487192533663)
XLA Ops:
  1.1 4.2 %prepare.1 = (bf16[128,2176]{1,0:T(8,128)(2,1)}, bf16[128,2176]{1,0:T(8,128)(2,1)}, bf16[31,128,128]{2,1,0:T(8,128)(2,1)}, f32[8,128]{1,0:T(8,128)}) custom-call(s32[16,16]{1,0:T(8,128)} %pattern.5, bf16[2,2,128,2048]{3,2,1,0:T(8,128)(2,1)} %bitcast.93, bf16[2,128,2048]{2,1,0:T(8,128)(2,1)} %bitcast.58, bf16[48,128,128]{2,1,0:T(8,128)(2,1)} %bitcast.62, ...), custom_call_target="tpu_custom_call" | custom-call | tf_op jit(solution)/shard_map/prepare/pallas_call | solution.py:449
  5.3 2.6 %collective-permute-start = (bf16[31,128,128]{2,1,0:T(8,128)(2,1)}, bf16[31,128,128]{2,1,0:T(8,128)(2,1)S(1)}, u32[]{:S(2)}, u32[]{:S(2)}) collective-permute-start(bf16[31,128,128]{2,1,0:T(8,128)(2,1)} %get-tuple-element.34), channel_id=1, source_target_pairs={{0,2},{2,0},{1,3},{3,1},{4,6},{6,4},{5,7},{7,5},{8,10},{10,8},{9,1... | collective-permute-start | bytes 3047432 | tf_op jit(solution)/shard_map/ppermute | solution.py:125
  7.9 2.6 %collective-permute-start.1 = (bf16[128,2176]{1,0:T(8,128)(2,1)}, bf16[128,2176]{1,0:T(8,128)(2,1)S(1)}, u32[]{:S(2)}, u32[]{:S(2)}) collective-permute-start(bf16[128,2176]{1,0:T(8,128)(2,1)} %get-tuple-element.35), channel_id=1, source_target_pairs={{0,8},{8,12},{12,4},{4,0},{1,9},{9,13},{13,5},{5,1},{2,10},{10,14}... | collective-permute-start | bytes 1671176 | tf_op jit(solution)/shard_map/ppermute | solution.py:594
  10.5 13.3 %collective-permute-done.1 = bf16[128,2176]{1,0:T(8,128)(2,1)S(1)} collective-permute-done((bf16[128,2176]{1,0:T(8,128)(2,1)}, bf16[128,2176]{1,0:T(8,128)(2,1)S(1)}, u32[]{:S(2)}, u32[]{:S(2)}) %collective-permute-start.1) | collective-permute-done | bytes 557088 | tf_op jit(solution)/shard_map/ppermute | solution.py:594
  23.8 12.9 %collective-permute-done.2 = bf16[128,2176]{1,0:T(8,128)(2,1)S(1)} collective-permute-done((bf16[128,2176]{1,0:T(8,128)(2,1)}, bf16[128,2176]{1,0:T(8,128)(2,1)S(1)}, u32[]{:S(2)}, u32[]{:S(2)}) %collective-permute-start.2) | collective-permute-done | bytes 557088 | tf_op jit(solution)/shard_map/ppermute | solution.py:595
  41.8 12.2 %collective-permute-done.11 = bf16[128,2048]{1,0:T(8,128)(2,1)} collective-permute-done((bf16[128,2048]{1,0:T(8,128)(2,1)}, bf16[128,2048]{1,0:T(8,128)(2,1)}, u32[]{:S(2)}, u32[]{:S(2)}) %collective-permute-start.11) | collective-permute-done | bytes 524320 | tf_op jit(solution)/shard_map/ppermute | solution.py:125
  56.0 2.8 %arrange.1.right = bf16[2,48,128,128]{3,2,1,0:T(8,128)(2,1)S(1)} custom-call(bf16[48,128,128]{2,1,0:T(8,128)(2,1)S(1)} %bitcast.63, bf16[31,128,128]{2,1,0:T(8,128)(2,1)S(1)} %collective-permute-done.near.left_other, bf16[31,128,128]{2,1,0:T(8,128)(2,1)} %collective-permute-done.4.far), custom_call_target="tpu_custom_call" | custom-call | tf_op jit(solution)/shard_map/arrange/pallas_call | solution.py:365
  58.8 1.6 copy-done
  61.7 6.2 %collective-permute-done.13 = bf16[128,2048]{1,0:T(8,128)(2,1)} collective-permute-done((bf16[128,2048]{1,0:T(8,128)(2,1)}, bf16[128,2048]{1,0:T(8,128)(2,1)}, u32[]{:S(2)}, u32[]{:S(2)}) %collective-permute-start.13) | collective-permute-done | bytes 524320 | tf_op jit(solution)/shard_map/ppermute | solution.py:125
  67.9 5.9 %collective-permute-done.7 = bf16[128,2048]{1,0:T(8,128)(2,1)} collective-permute-done((bf16[128,2048]{1,0:T(8,128)(2,1)S(1)}, bf16[128,2048]{1,0:T(8,128)(2,1)}, u32[]{:S(2)}, u32[]{:S(2)}) %collective-permute-start.7) | collective-permute-done | bytes 524320 | tf_op jit(solution)/shard_map/ppermute | solution.py:125
  74.1 2.5 %collective-permute-start.15 = (bf16[128,2048]{1,0:T(8,128)(2,1)S(1)}, bf16[128,2048]{1,0:T(8,128)(2,1)S(1)}, u32[]{:S(2)}, u32[]{:S(2)}) collective-permute-start(bf16[128,2048]{1,0:T(8,128)(2,1)S(1)} %dynamic-slice_bitcast_fusion), channel_id=1, source_target_pairs={{0,12},{4,8},{8,4},{12,0},{1,13},{5,9},{9,5},{13,1},{2,14},{6,10},... | collective-permute-start | bytes 1572872 | tf_op jit(solution)/shard_map/ppermute | solution.py:125
  77.8 14.1 %operate_first.1 = (bf16[2,128,2048]{2,1,0:T(8,128)(2,1)S(1)}, bf16[2,128,2048]{2,1,0:T(8,128)(2,1)S(1)}, f32[8,128]{1,0:T(8,128)S(1)}) custom-call(s32[3,1,16]{2,1,0:T(1,128)S(1)} %bitcast.84, s32[3,1,16]{2,1,0:T(1,128)S(1)} %bitcast.87, s32[16,16]{1,0:T(8,128)S(1)} %bitcast_convert_fusion.cols_other, s32[16,16]{1,0:T(8,128)S(1)} %copy-done.6, ...), custom_call_target="tpu_custom_call" | custom-call | flops 3221225472 | bytes 16777216 | tf_op jit(solution)/shard_map/operate_first/pallas_call | solution.py:320
  94.8 1.8 collective-permute-start.19
  99.4 2.2 %update.1 = (f32[2,128,2048]{2,1,0:T(8,128)S(1)}, f32[8,128]{1,0:T(8,128)S(1)}) custom-call(bf16[2,128,2048]{2,1,0:T(8,128)(2,1)S(1)} %get-tuple-element.42.psi.refs_18_, bf16[2,128,2048]{2,1,0:T(8,128)(2,1)S(1)} %get-tuple-element.43.off.refs_19_, bf16[2,128,2048]{2,1,0:T(8,128)(2,1)S(1)} %bitcast.61, ...), custom_call_target="tpu_custom_call" | custom-call | tf_op jit(solution)/shard_map/update/pallas_call | solution.py:649
  103.3 2.0 collective-permute-start.22
  107.0 2.9 %collective-permute-done.23.refs_3_ = f32[2,8,128]{2,1,0:T(8,128)S(1)} collective-permute-done((f32[2,8,128]{2,1,0:T(8,128)S(1)}, f32[2,8,128]{2,1,0:T(8,128)S(1)}, u32[]{:S(2)}, u32[]{:S(2)}) %collective-permute-start.23) | collective-permute-done | bytes 8224 | tf_op jit(solution)/shard_map/ppermute | solution.py:134
  113.4 9.5 %collective-permute-done.24 = bf16[128,2048]{1,0:T(8,128)(2,1)S(1)} collective-permute-done((bf16[128,2048]{1,0:T(8,128)(2,1)S(1)}, bf16[128,2048]{1,0:T(8,128)(2,1)S(1)}, u32[]{:S(2)}, u32[]{:S(2)}) %collective-permute-start.24) | collective-permute-done | bytes 524320 | tf_op jit(solution)/shard_map/ppermute | solution.py:125
  123.0 4.6 %collective-permute-start.31 = (bf16[128,2048]{1,0:T(8,128)(2,1)S(1)}, bf16[128,2048]{1,0:T(8,128)(2,1)S(1)}, u32[]{:S(2)}, u32[]{:S(2)}) collective-permute-start(bf16[128,2048]{1,0:T(8,128)(2,1)S(1)} %get-tuple-element.53), channel_id=1, source_target_pairs={{0,4},{4,0},{8,12},{12,8},{1,5},{5,1},{9,13},{13,9},{2,6},{6,2},{1... | collective-permute-start | bytes 1572872 | tf_op jit(solution)/shard_map/ppermute | solution.py:125
  129.7 10.7 %collective-permute-done.31 = bf16[128,2048]{1,0:T(8,128)(2,1)S(1)} collective-permute-done((bf16[128,2048]{1,0:T(8,128)(2,1)S(1)}, bf16[128,2048]{1,0:T(8,128)(2,1)S(1)}, u32[]{:S(2)}, u32[]{:S(2)}) %collective-permute-start.31) | collective-permute-done | bytes 524320 | tf_op jit(solution)/shard_map/ppermute | solution.py:125
  140.4 2.0 collective-permute-done.27.refs_1_
  142.4 6.9 %collective-permute-done.36 = bf16[128,2048]{1,0:T(8,128)(2,1)S(1)} collective-permute-done((bf16[128,2048]{1,0:T(8,128)(2,1)S(1)}, bf16[128,2048]{1,0:T(8,128)(2,1)S(1)}, u32[]{:S(2)}, u32[]{:S(2)}) %collective-permute-start.36) | collective-permute-done | bytes 524320 | tf_op jit(solution)/shard_map/ppermute | solution.py:125
  149.9 3.8 %collective-permute-start.28 = (bf16[128,2048]{1,0:T(8,128)(2,1)S(1)}, bf16[128,2048]{1,0:T(8,128)(2,1)S(1)}, u32[]{:S(2)}, u32[]{:S(2)}) collective-permute-start(bf16[128,2048]{1,0:T(8,128)(2,1)S(1)} %get-tuple-element.53), channel_id=1, source_target_pairs={{0,12},{12,0},{1,13},{13,1},{2,14},{14,2},{3,15},{15,3},{16,28},{2... | collective-permute-start | bytes 1572872 | tf_op jit(solution)/shard_map/ppermute | solution.py:691
  153.8 11.8 %operate_second.1 = (bf16[128,2048]{1,0:T(8,128)(2,1)S(1)}, bf16[64,2048]{1,0:T(8,128)(2,1)S(1)}, bf16[64,2048]{1,0:T(8,128)(2,1)S(1)}, f32[8,128]{1,0:T(8,128)S(1)}) custom-call(s32[3,1,16]{2,1,0:T(1,128)S(1)} %bitcast.85, s32[3,1,16]{2,1,0:T(1,128)S(1)} %bitcast.88, s32[16,16]{1,0:T(8,128)S(1)} %bitcast_convert_fusion.cols_other, s32[16,16]{1,0:T(8,128)S(1)} %copy-done.6, ...), custom_call_target="tpu_custom_call" | custom-call | bytes 1024 | tf_op jit(solution)/shard_map/operate_second/pallas_call | solution.py:320
  165.6 1.9 collective-permute-start.42
  168.7 7.3 %collective-permute-done.42.refs_2_ = bf16[64,2048]{1,0:T(8,128)(2,1)} collective-permute-done((bf16[64,2048]{1,0:T(8,128)(2,1)S(1)}, bf16[64,2048]{1,0:T(8,128)(2,1)}, u32[]{:S(2)}, u32[]{:S(2)}) %collective-permute-start.42) | collective-permute-done | bytes 262176 | tf_op jit(solution)/shard_map/ppermute | solution.py:125
  176.1 3.7 %collective-permute-start.47 = (f32[8,128]{1,0:T(8,128)S(1)}, f32[8,128]{1,0:T(8,128)S(1)}, u32[]{:S(2)}, u32[]{:S(2)}) collective-permute-start(f32[8,128]{1,0:T(8,128)S(1)} %add.25), channel_id=1, source_target_pairs={{0,4},{4,0},{8,12},{12,8},{1,5},{5,1},{9,13},{13,9},{2,6},{6,2},{1... | collective-permute-start | bytes 12296 | tf_op jit(solution)/shard_map/ppermute | solution.py:125
  181.4 1.6 collective-permute-start.49
  183.0 2.2 %collective-permute-start.43 = (bf16[64,2048]{1,0:T(8,128)(2,1)S(1)}, bf16[64,2048]{1,0:T(8,128)(2,1)}, u32[]{:S(2)}, u32[]{:S(2)}) collective-permute-start(bf16[64,2048]{1,0:T(8,128)(2,1)S(1)} %get-tuple-element.58), channel_id=1, source_target_pairs={{0,12},{4,8},{8,4},{12,0},{1,13},{5,9},{9,5},{13,1},{2,14},{6,10},... | collective-permute-start | bytes 786440 | tf_op jit(solution)/shard_map/ppermute | solution.py:125
  185.2 1.7 collective-permute-done.49
  186.9 5.5 %collective-permute-done.43.refs_3_ = bf16[64,2048]{1,0:T(8,128)(2,1)} collective-permute-done((bf16[64,2048]{1,0:T(8,128)(2,1)S(1)}, bf16[64,2048]{1,0:T(8,128)(2,1)}, u32[]{:S(2)}, u32[]{:S(2)}) %collective-permute-start.43) | collective-permute-done | bytes 262176 | tf_op jit(solution)/shard_map/ppermute | solution.py:125
  198.0 5.0 %collective-permute-done.46.refs_4_ = bf16[64,2048]{1,0:T(8,128)(2,1)} collective-permute-done((bf16[64,2048]{1,0:T(8,128)(2,1)}, bf16[64,2048]{1,0:T(8,128)(2,1)}, u32[]{:S(2)}, u32[]{:S(2)}) %collective-permute-start.46) | collective-permute-done | bytes 262176 | tf_op jit(solution)/shard_map/ppermute | solution.py:125
  203.0 2.4 %assemble.4.refs_1_ = bf16[2,2,128,2048]{3,2,1,0:T(8,128)(2,1)} custom-call(bf16[128,2048]{1,0:T(8,128)(2,1)S(1)} %get-tuple-element.61.refs_0_, bf16[128,2048]{1,0:T(8,128)(2,1)S(1)} %collective-permute-done.45.refs_1_, bf16[64,2048]{1,0:T(8,128)(2,1)} %collective-permute-done.42.refs_2_, bf16[64,2048]{1,0:T(8,128)(2,1)} %collective-permute-done.43.refs_3_, ...), custom_call_target="tpu_custom_call" | custom-call | tf_op jit(solution)/shard_map/assemble/pallas_call | solution.py:562
  (121 shorter events, 34.8 us)
Async XLA Ops:
  0.6 36.1 %collective-permute-start.3 = (bf16[2,256,2048]{2,1,0:T(8,128)(2,1)}, bf16[2,256,2048]{2,1,0:T(8,128)(2,1)S(1)}, u32[]{:S(2)}, u32[]{:S(2)}) collective-permute-start(bf16[2,256,2048]{2,1,0:T(8,128)(2,1)} %param.7), channel_id=1, source_target_pairs={{0,1},{1,0},{2,3},{3,2},{4,5},{5,4},{6,7},{7,6},{8,9},{9,8},{10,11... | collective-permute-start | bytes 6291464 | tf_op jit(solution)/shard_map/ppermute | solution.py:125
  5.3 31.4 %collective-permute-start = (bf16[31,128,128]{2,1,0:T(8,128)(2,1)}, bf16[31,128,128]{2,1,0:T(8,128)(2,1)S(1)}, u32[]{:S(2)}, u32[]{:S(2)}) collective-permute-start(bf16[31,128,128]{2,1,0:T(8,128)(2,1)} %get-tuple-element.34), channel_id=1, source_target_pairs={{0,2},{2,0},{1,3},{3,1},{4,6},{6,4},{5,7},{7,5},{8,10},{10,8},{9,1... | collective-permute-start | bytes 3047432 | tf_op jit(solution)/shard_map/ppermute | solution.py:125
  7.9 15.9 %collective-permute-start.1 = (bf16[128,2176]{1,0:T(8,128)(2,1)}, bf16[128,2176]{1,0:T(8,128)(2,1)S(1)}, u32[]{:S(2)}, u32[]{:S(2)}) collective-permute-start(bf16[128,2176]{1,0:T(8,128)(2,1)} %get-tuple-element.35), channel_id=1, source_target_pairs={{0,8},{8,12},{12,4},{4,0},{1,9},{9,13},{13,5},{5,1},{2,10},{10,14}... | collective-permute-start | bytes 1671176 | tf_op jit(solution)/shard_map/ppermute | solution.py:594
  10.5 26.3 %collective-permute-start.2 = (bf16[128,2176]{1,0:T(8,128)(2,1)}, bf16[128,2176]{1,0:T(8,128)(2,1)S(1)}, u32[]{:S(2)}, u32[]{:S(2)}) collective-permute-start(bf16[128,2176]{1,0:T(8,128)(2,1)} %get-tuple-element.36), channel_id=1, source_target_pairs={{0,4},{4,12},{12,8},{8,0},{1,5},{5,13},{13,9},{9,1},{2,6},{6,14},{... | collective-permute-start | bytes 1671176 | tf_op jit(solution)/shard_map/ppermute | solution.py:595
  38.1 16.5 %collective-permute-start.4 = (bf16[31,128,128]{2,1,0:T(8,128)(2,1)S(1)}, bf16[31,128,128]{2,1,0:T(8,128)(2,1)}, u32[]{:S(2)}, u32[]{:S(2)}) collective-permute-start(bf16[31,128,128]{2,1,0:T(8,128)(2,1)S(1)} %collective-permute-done.near.left_other), channel_id=1, source_target_pairs={{0,1},{1,0},{2,3},{3,2},{4,5},{5,4},{6,7},{7,6},{8,9},{9,8},{10,11... | collective-permute-start | bytes 3047432 | tf_op jit(solution)/shard_map/ppermute | solution.py:125
  38.1 22.3 %collective-permute-start.6 = (bf16[128,2176]{1,0:T(8,128)(2,1)S(1)}, bf16[128,2176]{1,0:T(8,128)(2,1)}, u32[]{:S(2)}, u32[]{:S(2)}) collective-permute-start(bf16[128,2176]{1,0:T(8,128)(2,1)S(1)} %collective-permute-done.2), channel_id=1, source_target_pairs={{0,1},{1,0},{2,3},{3,2},{4,5},{5,4},{6,7},{7,6},{8,9},{9,8},{10,11... | collective-permute-start | bytes 1671176 | tf_op jit(solution)/shard_map/ppermute | solution.py:125
  38.6 21.9 %collective-permute-start.5 = (bf16[128,2176]{1,0:T(8,128)(2,1)S(1)}, bf16[128,2176]{1,0:T(8,128)(2,1)}, u32[]{:S(2)}, u32[]{:S(2)}) collective-permute-start(bf16[128,2176]{1,0:T(8,128)(2,1)S(1)} %collective-permute-done.1), channel_id=1, source_target_pairs={{0,1},{1,0},{2,3},{3,2},{4,5},{5,4},{6,7},{7,6},{8,9},{9,8},{10,11... | collective-permute-start | bytes 1671176 | tf_op jit(solution)/shard_map/ppermute | solution.py:125
  39.4 14.6 %collective-permute-start.11 = (bf16[128,2048]{1,0:T(8,128)(2,1)}, bf16[128,2048]{1,0:T(8,128)(2,1)}, u32[]{:S(2)}, u32[]{:S(2)}) collective-permute-start(bf16[128,2048]{1,0:T(8,128)(2,1)} %slice_select_fusion), channel_id=1, source_target_pairs={{0,4},{4,0},{8,12},{12,8},{1,5},{5,1},{9,13},{13,9},{2,6},{6,2},{1... | collective-permute-start | bytes 1572872 | tf_op jit(solution)/shard_map/ppermute | solution.py:125
  41.2 20.0 %collective-permute-start.9 = (bf16[128,2048]{1,0:T(8,128)(2,1)}, bf16[128,2048]{1,0:T(8,128)(2,1)}, u32[]{:S(2)}, u32[]{:S(2)}) collective-permute-start(bf16[128,2048]{1,0:T(8,128)(2,1)} %slice_select_fusion), channel_id=1, source_target_pairs={{0,2},{2,0},{1,3},{3,1},{4,6},{6,4},{5,7},{7,5},{8,10},{10,8},{9,1... | collective-permute-start | bytes 1572872 | tf_op jit(solution)/shard_map/ppermute | solution.py:125
  54.1 13.9 %collective-permute-start.13 = (bf16[128,2048]{1,0:T(8,128)(2,1)}, bf16[128,2048]{1,0:T(8,128)(2,1)}, u32[]{:S(2)}, u32[]{:S(2)}) collective-permute-start(bf16[128,2048]{1,0:T(8,128)(2,1)} %collective-permute-done.11), channel_id=1, source_target_pairs={{0,2},{2,0},{1,3},{3,1},{4,6},{6,4},{5,7},{7,5},{8,10},{10,8},{9,1... | collective-permute-start | bytes 1572872 | tf_op jit(solution)/shard_map/ppermute | solution.py:125
  60.4 13.4 %collective-permute-start.7 = (bf16[128,2048]{1,0:T(8,128)(2,1)S(1)}, bf16[128,2048]{1,0:T(8,128)(2,1)}, u32[]{:S(2)}, u32[]{:S(2)}) collective-permute-start(bf16[128,2048]{1,0:T(8,128)(2,1)S(1)} %dynamic-slice_bitcast_fusion.1), channel_id=1, source_target_pairs={{0,4},{4,0},{8,12},{12,8},{1,5},{5,1},{9,13},{13,9},{2,6},{6,2},{1... | collective-permute-start | bytes 1572872 | tf_op jit(solution)/shard_map/ppermute | solution.py:125
  61.2 15.4 %collective-permute-start.12 = (bf16[128,2048]{1,0:T(8,128)(2,1)}, bf16[128,2048]{1,0:T(8,128)(2,1)}, u32[]{:S(2)}, u32[]{:S(2)}) collective-permute-start(bf16[128,2048]{1,0:T(8,128)(2,1)} %collective-permute-done.11), channel_id=1, source_target_pairs={{0,1},{1,0},{2,3},{3,2},{4,5},{5,4},{6,7},{7,6},{8,9},{9,8},{10,11... | collective-permute-start | bytes 1572872 | tf_op jit(solution)/shard_map/ppermute | solution.py:125
  61.2 15.4 %collective-permute-start.10 = (bf16[128,2048]{1,0:T(8,128)(2,1)}, bf16[128,2048]{1,0:T(8,128)(2,1)}, u32[]{:S(2)}, u32[]{:S(2)}) collective-permute-start(bf16[128,2048]{1,0:T(8,128)(2,1)} %collective-permute-done.9), channel_id=1, source_target_pairs={{0,1},{1,0},{2,3},{3,2},{4,5},{5,4},{6,7},{7,6},{8,9},{9,8},{10,11... | collective-permute-start | bytes 1572872 | tf_op jit(solution)/shard_map/ppermute | solution.py:125
  74.1 22.6 %collective-permute-start.15 = (bf16[128,2048]{1,0:T(8,128)(2,1)S(1)}, bf16[128,2048]{1,0:T(8,128)(2,1)S(1)}, u32[]{:S(2)}, u32[]{:S(2)}) collective-permute-start(bf16[128,2048]{1,0:T(8,128)(2,1)S(1)} %dynamic-slice_bitcast_fusion), channel_id=1, source_target_pairs={{0,12},{4,8},{8,4},{12,0},{1,13},{5,9},{9,5},{13,1},{2,14},{6,10},... | collective-permute-start | bytes 1572872 | tf_op jit(solution)/shard_map/ppermute | solution.py:125
  110.5 12.4 %collective-permute-start.24 = (bf16[128,2048]{1,0:T(8,128)(2,1)S(1)}, bf16[128,2048]{1,0:T(8,128)(2,1)S(1)}, u32[]{:S(2)}, u32[]{:S(2)}) collective-permute-start(bf16[128,2048]{1,0:T(8,128)(2,1)S(1)} %get-tuple-element.52.refs_0_), channel_id=1, source_target_pairs={{0,4},{4,0},{8,12},{12,8},{1,5},{5,1},{9,13},{13,9},{2,6},{6,2},{1... | collective-permute-start | bytes 1572872 | tf_op jit(solution)/shard_map/ppermute | solution.py:125
  110.6 12.3 %collective-permute-start.25 = (bf16[128,2048]{1,0:T(8,128)(2,1)S(1)}, bf16[128,2048]{1,0:T(8,128)(2,1)S(1)}, u32[]{:S(2)}, u32[]{:S(2)}) collective-permute-start(bf16[128,2048]{1,0:T(8,128)(2,1)S(1)} %get-tuple-element.53), channel_id=1, source_target_pairs={{0,2},{2,0},{1,3},{3,1},{4,6},{6,4},{5,7},{7,5},{8,10},{10,8},{9,1... | collective-permute-start | bytes 1572872 | tf_op jit(solution)/shard_map/ppermute | solution.py:125
  112.1 10.9 %collective-permute-start.26 = (bf16[128,2048]{1,0:T(8,128)(2,1)S(1)}, bf16[128,2048]{1,0:T(8,128)(2,1)S(1)}, u32[]{:S(2)}, u32[]{:S(2)}) collective-permute-start(bf16[128,2048]{1,0:T(8,128)(2,1)S(1)} %get-tuple-element.53), channel_id=1, source_target_pairs={{4,8},{8,4},{5,9},{9,5},{6,10},{10,6},{7,11},{11,7},{20,24},{24,20... | collective-permute-start | bytes 1572872 | tf_op jit(solution)/shard_map/ppermute | solution.py:679
  112.8 16.8 %collective-permute-start.29 = (bf16[128,2048]{1,0:T(8,128)(2,1)S(1)}, bf16[128,2048]{1,0:T(8,128)(2,1)S(1)}, u32[]{:S(2)}, u32[]{:S(2)}) collective-permute-start(bf16[128,2048]{1,0:T(8,128)(2,1)S(1)} %get-tuple-element.52.refs_0_), channel_id=1, source_target_pairs={{0,1},{1,0},{2,3},{3,2},{4,5},{5,4},{6,7},{7,6},{8,9},{9,8},{10,11... | collective-permute-start | bytes 1572872 | tf_op jit(solution)/shard_map/ppermute | solution.py:125
  112.9 16.7 %collective-permute-start.30 = (bf16[128,2048]{1,0:T(8,128)(2,1)S(1)}, bf16[128,2048]{1,0:T(8,128)(2,1)S(1)}, u32[]{:S(2)}, u32[]{:S(2)}) collective-permute-start(bf16[128,2048]{1,0:T(8,128)(2,1)S(1)} %get-tuple-element.53), channel_id=1, source_target_pairs={{0,1},{1,0},{2,3},{3,2},{4,5},{5,4},{6,7},{7,6},{8,9},{9,8},{10,11... | collective-permute-start | bytes 1572872 | tf_op jit(solution)/shard_map/ppermute | solution.py:125
  123.0 17.4 %collective-permute-start.31 = (bf16[128,2048]{1,0:T(8,128)(2,1)S(1)}, bf16[128,2048]{1,0:T(8,128)(2,1)S(1)}, u32[]{:S(2)}, u32[]{:S(2)}) collective-permute-start(bf16[128,2048]{1,0:T(8,128)(2,1)S(1)} %get-tuple-element.53), channel_id=1, source_target_pairs={{0,4},{4,0},{8,12},{12,8},{1,5},{5,1},{9,13},{13,9},{2,6},{6,2},{1... | collective-permute-start | bytes 1572872 | tf_op jit(solution)/shard_map/ppermute | solution.py:125
  127.5 14.9 %collective-permute-start.27 = (bf16[128,2048]{1,0:T(8,128)(2,1)S(1)}, bf16[128,2048]{1,0:T(8,128)(2,1)S(1)}, u32[]{:S(2)}, u32[]{:S(2)}) collective-permute-start(bf16[128,2048]{1,0:T(8,128)(2,1)S(1)} %get-tuple-element.52.refs_0_), channel_id=1, source_target_pairs={{0,2},{2,0},{1,3},{3,1},{4,6},{6,4},{5,7},{7,5},{8,10},{10,8},{9,1... | collective-permute-start | bytes 1572872 | tf_op jit(solution)/shard_map/ppermute | solution.py:125
  128.3 21.0 %collective-permute-start.36 = (bf16[128,2048]{1,0:T(8,128)(2,1)S(1)}, bf16[128,2048]{1,0:T(8,128)(2,1)S(1)}, u32[]{:S(2)}, u32[]{:S(2)}) collective-permute-start(bf16[128,2048]{1,0:T(8,128)(2,1)S(1)} %collective-permute-done.24), channel_id=1, source_target_pairs={{0,2},{2,0},{1,3},{3,1},{4,6},{6,4},{5,7},{7,5},{8,10},{10,8},{9,1... | collective-permute-start | bytes 1572872 | tf_op jit(solution)/shard_map/ppermute | solution.py:125
  129.6 19.7 %collective-permute-start.37 = (bf16[128,2048]{1,0:T(8,128)(2,1)S(1)}, bf16[128,2048]{1,0:T(8,128)(2,1)S(1)}, u32[]{:S(2)}, u32[]{:S(2)}) collective-permute-start(bf16[128,2048]{1,0:T(8,128)(2,1)S(1)} %collective-permute-done.25), channel_id=1, source_target_pairs={{0,4},{4,0},{8,12},{12,8},{1,5},{5,1},{9,13},{13,9},{2,6},{6,2},{1... | collective-permute-start | bytes 1572872 | tf_op jit(solution)/shard_map/ppermute | solution.py:125
  129.6 20.2 %collective-permute-start.32 = (bf16[128,2048]{1,0:T(8,128)(2,1)S(1)}, bf16[128,2048]{1,0:T(8,128)(2,1)S(1)}, u32[]{:S(2)}, u32[]{:S(2)}) collective-permute-start(bf16[128,2048]{1,0:T(8,128)(2,1)S(1)} %collective-permute-done.24), channel_id=1, source_target_pairs={{0,1},{1,0},{2,3},{3,2},{4,5},{5,4},{6,7},{7,6},{8,9},{9,8},{10,11... | collective-permute-start | bytes 1572872 | tf_op jit(solution)/shard_map/ppermute | solution.py:125
  140.4 9.5 %collective-permute-start.35 = (bf16[128,2048]{1,0:T(8,128)(2,1)S(1)}, bf16[128,2048]{1,0:T(8,128)(2,1)S(1)}, u32[]{:S(2)}, u32[]{:S(2)}) collective-permute-start(bf16[128,2048]{1,0:T(8,128)(2,1)S(1)} %collective-permute-done.25), channel_id=1, source_target_pairs={{0,1},{1,0},{2,3},{3,2},{4,5},{5,4},{6,7},{7,6},{8,9},{9,8},{10,11... | collective-permute-start | bytes 1572872 | tf_op jit(solution)/shard_map/ppermute | solution.py:125
  142.4 11.3 %collective-permute-start.33 = (bf16[128,2048]{1,0:T(8,128)(2,1)S(1)}, bf16[128,2048]{1,0:T(8,128)(2,1)S(1)}, u32[]{:S(2)}, u32[]{:S(2)}) collective-permute-start(bf16[128,2048]{1,0:T(8,128)(2,1)S(1)} %collective-permute-done.31), channel_id=1, source_target_pairs={{0,1},{1,0},{2,3},{3,2},{4,5},{5,4},{6,7},{7,6},{8,9},{9,8},{10,11... | collective-permute-start | bytes 1572872 | tf_op jit(solution)/shard_map/ppermute | solution.py:125
  149.9 18.8 %collective-permute-start.28 = (bf16[128,2048]{1,0:T(8,128)(2,1)S(1)}, bf16[128,2048]{1,0:T(8,128)(2,1)S(1)}, u32[]{:S(2)}, u32[]{:S(2)}) collective-permute-start(bf16[128,2048]{1,0:T(8,128)(2,1)S(1)} %get-tuple-element.53), channel_id=1, source_target_pairs={{0,12},{12,0},{1,13},{13,1},{2,14},{14,2},{3,15},{15,3},{16,28},{2... | collective-permute-start | bytes 1572872 | tf_op jit(solution)/shard_map/ppermute | solution.py:691
  165.6 10.5 %collective-permute-start.42 = (bf16[64,2048]{1,0:T(8,128)(2,1)S(1)}, bf16[64,2048]{1,0:T(8,128)(2,1)}, u32[]{:S(2)}, u32[]{:S(2)}) collective-permute-start(bf16[64,2048]{1,0:T(8,128)(2,1)S(1)} %get-tuple-element.57), channel_id=1, source_target_pairs={{0,12},{4,8},{8,4},{12,0},{1,13},{5,9},{9,5},{13,1},{2,14},{6,10},... | collective-permute-start | bytes 786440 | tf_op jit(solution)/shard_map/ppermute | solution.py:125
  167.6 26.1 %collective-permute-start.45 = (bf16[128,2048]{1,0:T(8,128)(2,1)S(1)}, bf16[128,2048]{1,0:T(8,128)(2,1)S(1)}, u32[]{:S(2)}, u32[]{:S(2)}) collective-permute-start(bf16[128,2048]{1,0:T(8,128)(2,1)S(1)} %get-tuple-element.61.refs_0_), channel_id=1, source_target_pairs={{0,2},{2,0},{1,3},{3,1},{4,6},{6,4},{5,7},{7,5},{8,10},{10,8},{9,1... | collective-permute-start | bytes 1572872 | tf_op jit(solution)/shard_map/ppermute | solution.py:125
  179.8 15.9 %collective-permute-start.41 = (bf16[128,2048]{1,0:T(8,128)(2,1)S(1)}, bf16[128,2048]{1,0:T(8,128)(2,1)S(1)}, u32[]{:S(2)}, u32[]{:S(2)}) collective-permute-start(bf16[128,2048]{1,0:T(8,128)(2,1)S(1)} %broadcast_select_fusion.refs_2_), channel_id=1, source_target_pairs={{0,2},{2,0},{1,3},{3,1},{4,6},{6,4},{5,7},{7,5},{8,10},{10,8},{9,1... | collective-permute-start | bytes 1572872 | tf_op jit(solution)/shard_map/ppermute | solution.py:125
  183.0 9.5 %collective-permute-start.43 = (bf16[64,2048]{1,0:T(8,128)(2,1)S(1)}, bf16[64,2048]{1,0:T(8,128)(2,1)}, u32[]{:S(2)}, u32[]{:S(2)}) collective-permute-start(bf16[64,2048]{1,0:T(8,128)(2,1)S(1)} %get-tuple-element.58), channel_id=1, source_target_pairs={{0,12},{4,8},{8,4},{12,0},{1,13},{5,9},{9,5},{13,1},{2,14},{6,10},... | collective-permute-start | bytes 786440 | tf_op jit(solution)/shard_map/ppermute | solution.py:125
  194.4 11.2 %collective-permute-start.44 = (bf16[64,2048]{1,0:T(8,128)(2,1)}, bf16[64,2048]{1,0:T(8,128)(2,1)S(1)}, u32[]{:S(2)}, u32[]{:S(2)}) collective-permute-start(bf16[64,2048]{1,0:T(8,128)(2,1)} %collective-permute-done.43.refs_3_), channel_id=1, source_target_pairs={{0,2},{2,0},{1,3},{3,1},{4,6},{6,4},{5,7},{7,5},{8,10},{10,8},{9,1... | collective-permute-start | bytes 786440 | tf_op jit(solution)/shard_map/ppermute | solution.py:125
  (30 other events, 282.5 us)

commit v11 on v10

--- a/solution.py
+++ b/solution.py
@@ -157,15 +157,15 @@
     return 4 * (z ^ dz) + 2 * (c ^ dc) + (x ^ dx if dx < 2 else dx - 2)
 
 
-def operate_kernel(first, plan, right_cols, left_cols, cols_other, pattern, right, left_own, left_other, *refs):
+def operate_kernel(first, ats, plan, right_cols, left_cols, cols_other, pattern, right, left_own, left_other, *refs):
     count = len(plan)
     pieces, refs = refs[:count], refs[count:]
     if first:
         masks, weight_own, psi_out, off_out, stats_out = refs[:5]
         refs = refs[5:]
     else:
-        hd_own, hd_far, psi_in, off_in, stats_in, near_out, far_out, late_out, stats_out = refs[:9]
-        refs = refs[9:]
+        hd_own, hd_far, psi_in, off_in, stats_in = refs[:5]
+        result_outs, stats_out, refs = refs[5:-6], refs[-6], refs[-5:]
     field, images, left, diag, sems = refs
     z, x, c = place()
     sectors, block, width = field.shape
@@ -182,7 +182,7 @@
         copy.start()
         copies.append(copy)
 
-    for at in range(2):
+    for at in ats:
         begin(left_own.at[pl.ds(rows[at] * links, links)], left.at[0, pl.ds(at * links, links)])
     begin(left_other.at[pl.ds(table // 2, 2 * links)], left.at[1])
     if not first:
@@ -208,7 +208,7 @@
     def left_col(term, a, j):
         return cols_other[8 + j, a] if term else left_cols[j, 0, a]
 
-    sources = [[left_col(term, rows[at], j) for at in range(2) for j in range(links)] for term in range(2)]
+    sources = [[left_col(term, rows[at], j) for at in ats for j in range(links)] for term in range(2)]
 
     deep = links * block
 
@@ -237,7 +237,7 @@
             )
             product = product.astype(jnp.bfloat16)
             span = pl.ds(pl.multiple_of(n * pair * block, pair * block), pair * block)
-            for at in range(2):
+            for at in range(len(ats)):
                 images[at, term * deep : (term + 1) * deep, span] = product[at * deep : (at + 1) * deep]
         return carry
 
@@ -246,7 +246,6 @@
         copy.wait()
 
     step = 2
-    early_rows = block // 2
     zero = jnp.zeros((8, LANES), jnp.float32)
 
     def column(n, sums):
@@ -260,11 +259,11 @@
             ]
             return jnp.concatenate(parts, axis=1)
 
-        for at in range(2):
+        for spot, at in enumerate(ats):
             weights = [left[term, at * links + j] for term in range(2) for j in range(links)]
             total = jnp.dot(
                 jnp.concatenate(weights, axis=1),
-                images[at, :, span],
+                images[spot, :, span],
                 preferred_element_type=jnp.float32,
             )
             offdiag = masked(rows[at], total.astype(jnp.bfloat16).astype(jnp.float32))
@@ -277,11 +276,9 @@
             else:
                 weight = diag[at, :, span].astype(jnp.float32)
                 narrow = (weight * own + offdiag).astype(jnp.bfloat16)
-                if at == 0:
-                    near_out[:, span] = narrow
-                else:
-                    far_out[:, span] = narrow[:early_rows]
-                    late_out[:, span] = narrow[early_rows:]
+                tall = block // len(result_outs)
+                for part, out in enumerate(result_outs):
+                    out[:, span] = narrow[part * tall : (part + 1) * tall]
                 second = narrow.astype(jnp.float32)
                 wave = psi_in[at, :, span].astype(jnp.float32)
                 sigma_one = weight * wave + off_in[at, :, span].astype(jnp.float32)
@@ -301,10 +298,13 @@
     for at, value in enumerate(sums):
         stats_out[at : at + 1, :] = jnp.sum(value, axis=0, keepdims=True)
     if not first:
-        stats_out[3:5, :] = stats_in[0:2, :]
-
-
-def operate(first, plan, pieces, cols, pattern, right, left, extra):
+        if len(result_outs) == 2:
+            stats_out[3:5, :] = stats_in[0:2, :]
+        else:
+            stats_out[...] = stats_out[...] + stats_in[...]
+
+
+def operate(first, ats, plan, pieces, cols, pattern, right, left, extra):
     _, table, block, _ = right.shape
     width = pieces[0].shape[2]
     sectors = width // block
@@ -313,26 +313,26 @@
     one = jax.ShapeDtypeStruct((block, width), jnp.bfloat16)
     some = jax.ShapeDtypeStruct((block // 2, width), jnp.bfloat16)
     stats = jax.ShapeDtypeStruct((8, LANES), jnp.float32)
-    out_shape = (rows, rows, stats) if first else (one, some, some, stats)
+    out_shape = (rows, rows, stats) if first else ((some, some, stats) if ats == (1,) else (one, stats))
     extra_specs = [VMEM, VMEM] if first else [ANY, ANY, VMEM, VMEM, VMEM]
     inner = 2 * 2 * sectors * 2 * links * links * block * block * block
     outer = 2 * 2 * 2 * links * block * block * width
     return pl.pallas_call(
-        functools.partial(operate_kernel, first, plan),
+        functools.partial(operate_kernel, first, ats, plan),
         out_shape=out_shape,
         in_specs=[SMEM, SMEM, SMEM, SMEM, VMEM, ANY, ANY] + [VMEM] * len(pieces) + extra_specs,
         out_specs=(VMEM,) * len(out_shape),
         scratch_shapes=[
             pltpu.VMEM((sectors, block, width), jnp.bfloat16),
-            pltpu.VMEM((2, 2 * links * block, width), jnp.bfloat16),
+            pltpu.VMEM((len(ats), 2 * links * block, width), jnp.bfloat16),
             pltpu.VMEM((2, 2 * links, block, block), jnp.bfloat16),
             pltpu.VMEM((2, block, width), jnp.bfloat16),
             pltpu.SemaphoreType.DMA((5,)),
         ],
         compiler_params=pltpu.CompilerParams(vmem_limit_bytes=OPERATE_LIMIT),
         cost_estimate=pl.CostEstimate(
-            flops=inner + outer if first else 0,
-            bytes_accessed=16 * 1024 * 1024 if first else 1024,
+            flops=inner + outer if 0 in ats else 0,
+            bytes_accessed=64 * 1024 * 1024 if 0 in ats else 1024,
             transcendentals=0,
         ),
         name="operate_first" if first else "operate_second",
@@ -586,6 +586,7 @@
     halves = theta.reshape(roots, 2, block, width)
     diag = hdiag.reshape(2, block, width)
     middle = in_middle(z)
+    chunk = block // 2
     right = right_blocks.reshape(-1, block, block)
     left = left_blocks.reshape(-1, block, block)
     cols = (right_cols.transpose(2, 0, 1), left_cols.transpose(2, 0, 1))
@@ -598,26 +599,25 @@
 
     mix_a, mix_b = after((mix_a, mix_b), theta_core)
     far = jnp.where(middle, mix_a[:, :width], mix_b[:, :width])
-    far_z = across(far, "blk", 1)
+    far_z = [across(far[at : at + chunk], "blk", 1) for at in (0, chunk)]
     far_x = across(far, "ops", 1)
-    mix_a_core = across(mix_a, "sub", 1)
-    mix_b_core = across(mix_b, "sub", 1)
-    operators = after(operators, mix_b)
+    masks = jnp.repeat(pattern.astype(jnp.bfloat16), block, axis=1)
+    masks = jnp.broadcast_to(masks[:, None, :], (sectors, 16, width))
+    own_b = lax.dynamic_slice(halves, (half, 1, 0, 0), (1, 1, block, width))[0, 0]
+    near_b = across(after(own_b, far_z[0], masks), "blk", 1)
+    far_zx = [across(value, "ops", 1) for value in far_z]
+    mix_a_core = across(after(mix_a, far_z[0]), "sub", 1)
+    mix_b_core = across(after(mix_b, far_z[0]), "sub", 1)
+    operators = after(operators, far_z[0])
     operators_core = across(operators, "sub", 1)
     turned = arrange(right, operators, operators_core)
     cols = (*cols, operators[-1, :16, :sectors].astype(jnp.int32))
-    masks = jnp.repeat(pattern.astype(jnp.bfloat16), block, axis=1)
-    masks = jnp.broadcast_to(masks[:, None, :], (sectors, 16, width))
-
-    own_b = lax.dynamic_slice(halves, (half, 1, 0, 0), (1, 1, block, width))[0, 0]
-    near_b = across(after(own_b, mix_a_core, mix_b_core, turned), "blk", 1)
-    far_zx = across(far_z, "ops", 1)
     far_x_core = across(far_x, "sub", 1)
-    far_z_core = across(far_z, "sub", 1)
+    far_z_core = [across(value, "sub", 1) for value in far_z]
     hd_far = lax.dynamic_index_in_dim(diag, x, 0, keepdims=False)
-    hd_far = across(after(hd_far, far_z), "blk", 3)
-    far_zx_core = across(far_zx, "sub", 1)
-    near_b_core = across(near_b, "sub", 1)
+    hd_far = across(after(hd_far, far_z[1]), "blk", 3)
+    far_zx_core = [across(value, "sub", 1) for value in far_zx]
+    near_b_core = across(after(near_b, turned), "sub", 1)
 
     left = (left, operators)
     pieces = [halves.reshape(4, block, width), theta_core.reshape(4, block, width)]
@@ -634,15 +634,20 @@
         (near_b_core, (1, 3, 1)),
         (far_x, (2, 1, 0)),
         (far_x_core, (2, 1, 1)),
-        (far_z, (3, 0, 0)),
-        (far_z_core, (3, 0, 1)),
-        (far_zx, (3, 1, 0)),
-        (far_zx_core, (3, 1, 1)),
     ):
         pieces.append(piece[None])
         plan.append((offset + (0, block),))
+    for at in range(2):
+        for piece, offset in (
+            (far_z[at], (3, 0, 0)),
+            (far_z_core[at], (3, 0, 1)),
+            (far_zx[at], (3, 1, 0)),
+            (far_zx_core[at], (3, 1, 1)),
+        ):
+            pieces.append(piece[None])
+            plan.append((offset + (at * chunk, chunk),))
     psi, off_one, stats_one = operate(
-        True, tuple(plan), pieces, cols, pattern, turned, left, (masks, weight_own)
+        True, (0, 1), tuple(plan), pieces, cols, pattern, turned, left, (masks, weight_own)
     )
 
     found = share(stats_one)
@@ -710,17 +715,21 @@
     ):
         pieces.append(piece[None])
         plan.append((offset + (0, block),))
-    two_near, two_far, two_late, stats_three = operate(
-        False, tuple(plan), pieces, cols, pattern, turned, left, (diag, hd_far, psi, off_one, stats_one)
-    )
-
+    extra = (diag, hd_far, psi, off_one)
+    two_far, two_late, stats_far = operate(
+        False, (1,), tuple(plan), pieces, cols, pattern, turned, left, (*extra, stats_one)
+    )
     far_in = across(two_far, "blk", 3)
+    other = jnp.where(middle, other_middle, after(other_end, two_far))
+    other_x = across(other, "ops", 1)
+    pieces[0] = after(pieces[0], other)
+    two_near, stats_three = operate(
+        False, (0,), tuple(plan), pieces, cols, pattern, turned, left, (*extra, stats_far)
+    )
     near_in = across(two_near, "ops", 1)
     late_in = across(after(two_late, far_in), "blk", 3)
-    far_in_x = across(after(far_in, near_in), "ops", 1)
+    far_in_x = across(far_in, "ops", 1)
     sums = stats_three + across(stats_three, "sub", 1)
-    other = jnp.where(middle, other_middle, after(other_end, sums))
-    other_x = across(other, "ops", 1)
     sums = after(sums, far_in)
     both = jnp.stack([sums + across(sums, "blk", 1), across(sums, "blk", 2) + across(sums, "blk", 3)])
     both = after(both, late_in)

time: 209 us -> 228 us (1.091)
  waiting for transfers between devices: 109 us -> 120 us
  Pallas kernels: 40.1 us -> 45 us
  local copies, waits for them, and re-layouts: 6.72 us -> 11.3 us
    ppermute x41 -> x45, waiting for transfers between devices: 76.1 us -> 85.5 us  [across(): return lax.ppermute(value, axis, [(i, i ^ distance) for i in range(size)])]
    pallas_call x2 -> x3, Pallas kernels: 26 us -> 30.8 us  [operate(): pl.pallas_call(functools.partial(operate_kernel, first, ats, plan), out_s...]
    unnamed x23 -> x41, local copies, waits for them, and re-layouts: 4.39 us -> 9 us
    ppermute x1, waiting for transfers between devices: 0.01 us -> 3.75 us  [shards(): lax.ppermute(after(changed_far, near_z, far_x), 'blk', [(0, 3), (3, 0)])]
    ppermute x41 -> x45, starting transfers between devices: 34 us -> 33.2 us  [across(): return lax.ppermute(value, axis, [(i, i ^ distance) for i in range(size)])]
  transfers between devices with their start and end apart: 51 -> 55, of which waited for: 24 -> 26; matrix products, arithmetic and copies ran while one was open for 2% -> 2% of each run, Pallas kernels for 18% -> 18%
where the time goes in v11:
time: 228 us; the launch traced here: 227 us
  waiting for transfers between devices  120 us (53%)
  starting transfers between devices  49.1 us (22%)
  Pallas kernels  45 us (20%)
  local copies, waits for them, and re-layouts  11.3 us (5%)
    ppermute x45, waiting for transfers between devices, across(): return lax.ppermute(value, axis, [(i, i ^ distance) for i in range(size)])  85.5 us
    ppermute x45, starting transfers between devices, across(): return lax.ppermute(value, axis, [(i, i ^ distance) for i in range(size)])  33.2 us
    pallas_call x3, Pallas kernels, operate(): pl.pallas_call(functools.partial(operate_kernel, first, ats, plan), out_s...  30.8 us
    ppermute x1, waiting for transfers between devices, shards(): mix_b = lax.ppermute(mix_b, 'blk', [(0, 1), (1, 3), (3, 2), (2, 0)])  13.2 us
    ppermute x1, waiting for transfers between devices, shards(): mix_a = lax.ppermute(mix_a, 'blk', [(0, 2), (2, 3), (3, 1), (1, 0)])  11.8 us
    unnamed x41, local copies, waits for them, and re-layouts  9 us
    ppermute x6, starting transfers between devices, share(): lax.ppermute(pair, axes, [(i, i ^ distance) for i in range(count)])  6.98 us
    ppermute x6, waiting for transfers between devices, share(): lax.ppermute(pair, axes, [(i, i ^ distance) for i in range(count)])  5.27 us
  transfers between devices with their start and end apart: 55, of which 26 were waited for; matrix products, arithmetic and copies ran while one was open for 2% of the time, Pallas kernels for 18%

profile of v11, /device:TPU:0, one launch (start us, length us, event | category | flops | bytes accessed | tf_op | source)
XLA Modules:
  0.0 227.3 jit_solution(8731128045183971065)
XLA Ops:
  1.1 4.2 %prepare.1 = (bf16[128,2176]{1,0:T(8,128)(2,1)}, bf16[128,2176]{1,0:T(8,128)(2,1)}, bf16[31,128,128]{2,1,0:T(8,128)(2,1)}, f32[8,128]{1,0:T(8,128)}) custom-call(s32[16,16]{1,0:T(8,128)} %pattern.7, bf16[2,2,128,2048]{3,2,1,0:T(8,128)(2,1)} %bitcast.122, bf16[2,128,2048]{2,1,0:T(8,128)(2,1)} %bitcast.62, bf16[48,128,128]{2,1,0:T(8,128)(2,1)} %bitcast.67, ...), custom_call_target="tpu_custom_call" | custom-call | tf_op jit(solution)/shard_map/prepare/pallas_call | solution.py:449
  5.3 3.7 %collective-permute-start.1 = (bf16[128,2176]{1,0:T(8,128)(2,1)}, bf16[128,2176]{1,0:T(8,128)(2,1)S(1)}, u32[]{:S(2)}, u32[]{:S(2)}) collective-permute-start(bf16[128,2176]{1,0:T(8,128)(2,1)} %get-tuple-element.39), channel_id=1, source_target_pairs={{0,8},{8,12},{12,4},{4,0},{1,9},{9,13},{13,5},{5,1},{2,10},{10,14}... | collective-permute-start | bytes 1671176 | tf_op jit(solution)/shard_map/ppermute | solution.py:595
  10.5 11.8 %collective-permute-done.1 = bf16[128,2176]{1,0:T(8,128)(2,1)S(1)} collective-permute-done((bf16[128,2176]{1,0:T(8,128)(2,1)}, bf16[128,2176]{1,0:T(8,128)(2,1)S(1)}, u32[]{:S(2)}, u32[]{:S(2)}) %collective-permute-start.1) | collective-permute-done | bytes 557088 | tf_op jit(solution)/shard_map/ppermute | solution.py:595
  22.3 13.2 %collective-permute-done.2 = bf16[128,2176]{1,0:T(8,128)(2,1)S(1)} collective-permute-done((bf16[128,2176]{1,0:T(8,128)(2,1)}, bf16[128,2176]{1,0:T(8,128)(2,1)S(1)}, u32[]{:S(2)}, u32[]{:S(2)}) %collective-permute-start.2) | collective-permute-done | bytes 557088 | tf_op jit(solution)/shard_map/ppermute | solution.py:596
  37.7 7.1 %collective-permute-done.4 = bf16[64,2048]{1,0:T(8,128)(2,1)S(1)} collective-permute-done((bf16[64,2048]{1,0:T(8,128)(2,1)S(1)}, bf16[64,2048]{1,0:T(8,128)(2,1)S(1)}, u32[]{:S(2)}, u32[]{:S(2)}) %collective-permute-start.4) | collective-permute-done | bytes 262176 | tf_op jit(solution)/shard_map/ppermute | solution.py:125
  45.0 4.6 %collective-permute-done.15 = bf16[64,2048]{1,0:T(8,128)(2,1)} collective-permute-done((bf16[64,2048]{1,0:T(8,128)(2,1)S(1)}, bf16[64,2048]{1,0:T(8,128)(2,1)}, u32[]{:S(2)}, u32[]{:S(2)}) %collective-permute-start.15) | collective-permute-done | bytes 262176 | tf_op jit(solution)/shard_map/ppermute | solution.py:125
  54.3 4.8 %collective-permute-done.17 = bf16[64,2048]{1,0:T(8,128)(2,1)S(1)} collective-permute-done((bf16[64,2048]{1,0:T(8,128)(2,1)}, bf16[64,2048]{1,0:T(8,128)(2,1)S(1)}, u32[]{:S(2)}, u32[]{:S(2)}) %collective-permute-start.17) | collective-permute-done | bytes 262176 | tf_op jit(solution)/shard_map/ppermute | solution.py:125
  61.3 13.0 %collective-permute-done.13 = bf16[64,2048]{1,0:T(8,128)(2,1)} collective-permute-done((bf16[64,2048]{1,0:T(8,128)(2,1)S(1)}, bf16[64,2048]{1,0:T(8,128)(2,1)}, u32[]{:S(2)}, u32[]{:S(2)}) %collective-permute-start.13) | collective-permute-done | bytes 262176 | tf_op jit(solution)/shard_map/ppermute | solution.py:125
  76.2 2.8 %arrange.1.right = bf16[2,48,128,128]{3,2,1,0:T(8,128)(2,1)S(1)} custom-call(bf16[48,128,128]{2,1,0:T(8,128)(2,1)S(1)} %bitcast.68, bf16[31,128,128]{2,1,0:T(8,128)(2,1)S(1)} %collective-permute-done.near.left_other, bf16[31,128,128]{2,1,0:T(8,128)(2,1)} %collective-permute-done.5.far), custom_call_target="tpu_custom_call" | custom-call | tf_op jit(solution)/shard_map/arrange/pallas_call | solution.py:365
  79.0 1.6 copy-done
  84.5 2.5 %collective-permute-start.19 = (bf16[128,2048]{1,0:T(8,128)(2,1)S(1)}, bf16[128,2048]{1,0:T(8,128)(2,1)S(1)}, u32[]{:S(2)}, u32[]{:S(2)}) collective-permute-start(bf16[128,2048]{1,0:T(8,128)(2,1)S(1)} %dynamic-slice_bitcast_fusion), channel_id=1, source_target_pairs={{0,12},{4,8},{8,4},{12,0},{1,13},{5,9},{9,5},{13,1},{2,14},{6,10},... | collective-permute-start | bytes 1572872 | tf_op jit(solution)/shard_map/ppermute | solution.py:125
  90.9 13.7 %operate_first.1 = (bf16[2,128,2048]{2,1,0:T(8,128)(2,1)S(1)}, bf16[2,128,2048]{2,1,0:T(8,128)(2,1)S(1)}, f32[8,128]{1,0:T(8,128)S(1)}) custom-call(s32[3,1,16]{2,1,0:T(1,128)S(1)} %bitcast.109, s32[3,1,16]{2,1,0:T(1,128)S(1)} %bitcast.113, s32[16,16]{1,0:T(8,128)S(1)} %bitcast_convert_fusion.cols_other, s32[16,16]{1,0:T(8,128)S(1)} %copy-done.14, ...), custom_call_target="tpu_custom_call" | custom-call | flops 3221225472 | bytes 67108864 | tf_op jit(solution)/shard_map/operate_first/pallas_call | solution.py:320
  106.5 2.3 %collective-permute-start.22 = (f32[2,8,128]{2,1,0:T(8,128)S(1)}, f32[2,8,128]{2,1,0:T(8,128)S(1)}, u32[]{:S(2)}, u32[]{:S(2)}) collective-permute-start(f32[2,8,128]{2,1,0:T(8,128)S(1)} %pad_maximum_fusion.refs_0_), channel_id=1, source_target_pairs={{0,4},{2,6},{4,0},{6,2},{8,12},{10,14},{12,8},{14,10},{1,5},{3,7},... | collective-permute-start | bytes 24584 | tf_op jit(solution)/shard_map/ppermute | solution.py:134
  110.6 1.9 collective-permute-done.21.refs_1_
  112.5 2.2 update.1
  115.9 2.0 collective-permute-start.26
  125.1 9.8 %collective-permute-done.28 = bf16[128,2048]{1,0:T(8,128)(2,1)S(1)} collective-permute-done((bf16[128,2048]{1,0:T(8,128)(2,1)S(1)}, bf16[128,2048]{1,0:T(8,128)(2,1)S(1)}, u32[]{:S(2)}, u32[]{:S(2)}) %collective-permute-start.28) | collective-permute-done | bytes 524320 | tf_op jit(solution)/shard_map/ppermute | solution.py:125
  136.8 3.4 %collective-permute-start.35 = (bf16[128,2048]{1,0:T(8,128)(2,1)S(1)}, bf16[128,2048]{1,0:T(8,128)(2,1)S(1)}, u32[]{:S(2)}, u32[]{:S(2)}) collective-permute-start(bf16[128,2048]{1,0:T(8,128)(2,1)S(1)} %get-tuple-element.60), channel_id=1, source_target_pairs={{0,4},{4,0},{8,12},{12,8},{1,5},{5,1},{9,13},{13,9},{2,6},{6,2},{1... | collective-permute-start | bytes 1572872 | tf_op jit(solution)/shard_map/ppermute | solution.py:125
  140.9 9.6 %collective-permute-done.31.refs_1_ = bf16[128,2048]{1,0:T(8,128)(2,1)S(1)} collective-permute-done((bf16[128,2048]{1,0:T(8,128)(2,1)S(1)}, bf16[128,2048]{1,0:T(8,128)(2,1)S(1)}, u32[]{:S(2)}, u32[]{:S(2)}) %collective-permute-start.31) | collective-permute-done | bytes 524320 | tf_op jit(solution)/shard_map/ppermute | solution.py:125
  150.5 2.6 %collective-permute-done.35 = bf16[128,2048]{1,0:T(8,128)(2,1)S(1)} collective-permute-done((bf16[128,2048]{1,0:T(8,128)(2,1)S(1)}, bf16[128,2048]{1,0:T(8,128)(2,1)S(1)}, u32[]{:S(2)}, u32[]{:S(2)}) %collective-permute-start.35) | collective-permute-done | bytes 524320 | tf_op jit(solution)/shard_map/ppermute | solution.py:125
  153.1 5.5 %collective-permute-done.40 = bf16[128,2048]{1,0:T(8,128)(2,1)S(1)} collective-permute-done((bf16[128,2048]{1,0:T(8,128)(2,1)S(1)}, bf16[128,2048]{1,0:T(8,128)(2,1)S(1)}, u32[]{:S(2)}, u32[]{:S(2)}) %collective-permute-start.40) | collective-permute-done | bytes 524320 | tf_op jit(solution)/shard_map/ppermute | solution.py:125
  160.0 4.5 %collective-permute-start.32 = (bf16[128,2048]{1,0:T(8,128)(2,1)S(1)}, bf16[128,2048]{1,0:T(8,128)(2,1)S(1)}, u32[]{:S(2)}, u32[]{:S(2)}) collective-permute-start(bf16[128,2048]{1,0:T(8,128)(2,1)S(1)} %get-tuple-element.60), channel_id=1, source_target_pairs={{0,12},{12,0},{1,13},{13,1},{2,14},{14,2},{3,15},{15,3},{16,28},{2... | collective-permute-start | bytes 1572872 | tf_op jit(solution)/shard_map/ppermute | solution.py:696
  164.6 8.5 %operate_second.2 = (bf16[64,2048]{1,0:T(8,128)(2,1)S(1)}, bf16[64,2048]{1,0:T(8,128)(2,1)S(1)}, f32[8,128]{1,0:T(8,128)S(1)}) custom-call(s32[3,1,16]{2,1,0:T(1,128)S(1)} %bitcast.110, s32[3,1,16]{2,1,0:T(1,128)S(1)} %bitcast.114, s32[16,16]{1,0:T(8,128)S(1)} %bitcast_convert_fusion.cols_other, s32[16,16]{1,0:T(8,128)S(1)} %copy-done.14, ...), custom_call_target="tpu_custom_call" | custom-call | bytes 1024 | tf_op jit(solution)/shard_map/operate_second/pallas_call | solution.py:320
  174.5 3.8 %collective-permute-done.32 = bf16[128,2048]{1,0:T(8,128)(2,1)S(1)} collective-permute-done((bf16[128,2048]{1,0:T(8,128)(2,1)S(1)}, bf16[128,2048]{1,0:T(8,128)(2,1)S(1)}, u32[]{:S(2)}, u32[]{:S(2)}) %collective-permute-start.32) | collective-permute-done | bytes 524320 | tf_op jit(solution)/shard_map/ppermute | solution.py:696
  178.4 8.5 %operate_second.3 = (bf16[128,2048]{1,0:T(8,128)(2,1)S(1)}, f32[8,128]{1,0:T(8,128)S(1)}) custom-call(s32[3,1,16]{2,1,0:T(1,128)S(1)} %bitcast.111, s32[3,1,16]{2,1,0:T(1,128)S(1)} %bitcast.115, s32[16,16]{1,0:T(8,128)S(1)} %bitcast_convert_fusion.cols_other, s32[16,16]{1,0:T(8,128)S(1)} %copy-done.14, bf16[2,48,128,128]{3,2,1,0:T(8,128)(2,1)} %copy-done, ...), custom_call_target="tpu_custom_call" | custom-call | flops 3221225472 | bytes 67108864 | tf_op jit(solution)/shard_map/operate_second/pallas_call | solution.py:320
  188.1 1.8 collective-permute-start.51
  191.9 2.4 %collective-permute-start.53 = (f32[8,128]{1,0:T(8,128)S(1)}, f32[8,128]{1,0:T(8,128)S(1)}, u32[]{:S(2)}, u32[]{:S(2)}) collective-permute-start(f32[8,128]{1,0:T(8,128)S(1)} %add.25), channel_id=1, source_target_pairs={{0,12},{4,8},{8,4},{12,0},{1,13},{5,9},{9,5},{13,1},{2,14},{6,10},... | collective-permute-start | bytes 12296 | tf_op jit(solution)/shard_map/ppermute | solution.py:125
  194.4 1.9 collective-permute-start.46
  198.6 5.0 %collective-permute-done.52 = f32[8,128]{1,0:T(8,128)S(1)} collective-permute-done((f32[8,128]{1,0:T(8,128)S(1)}, f32[8,128]{1,0:T(8,128)S(1)}, u32[]{:S(2)}, u32[]{:S(2)}) %collective-permute-start.52) | collective-permute-done | bytes 4128 | tf_op jit(solution)/shard_map/ppermute | solution.py:125
  205.9 10.1 %collective-permute-done.48.refs_1_ = bf16[128,2048]{1,0:T(8,128)(2,1)S(1)} collective-permute-done((bf16[128,2048]{1,0:T(8,128)(2,1)S(1)}, bf16[128,2048]{1,0:T(8,128)(2,1)S(1)}, u32[]{:S(2)}, u32[]{:S(2)}) %collective-permute-start.48) | collective-permute-done | bytes 524320 | tf_op jit(solution)/shard_map/ppermute | solution.py:125
  216.0 5.7 %collective-permute-done.49.refs_4_ = bf16[64,2048]{1,0:T(8,128)(2,1)} collective-permute-done((bf16[64,2048]{1,0:T(8,128)(2,1)}, bf16[64,2048]{1,0:T(8,128)(2,1)}, u32[]{:S(2)}, u32[]{:S(2)}) %collective-permute-start.49) | collective-permute-done | bytes 262176 | tf_op jit(solution)/shard_map/ppermute | solution.py:125
  221.7 2.4 %assemble.4.refs_1_ = bf16[2,2,128,2048]{3,2,1,0:T(8,128)(2,1)} custom-call(bf16[128,2048]{1,0:T(8,128)(2,1)S(1)} %get-tuple-element.69.refs_0_, bf16[128,2048]{1,0:T(8,128)(2,1)S(1)} %collective-permute-done.48.refs_1_, bf16[64,2048]{1,0:T(8,128)(2,1)} %collective-permute-done.45.refs_2_, bf16[64,2048]{1,0:T(8,128)(2,1)} %collective-permute-done.46.refs_3_, ...), custom_call_target="tpu_custom_call" | custom-call | tf_op jit(solution)/shard_map/assemble/pallas_call | solution.py:562
  (149 shorter events, 49.1 us)
Async XLA Ops:
  0.6 34.9 %collective-permute-start.3 = (bf16[2,256,2048]{2,1,0:T(8,128)(2,1)}, bf16[2,256,2048]{2,1,0:T(8,128)(2,1)}, u32[]{:S(2)}, u32[]{:S(2)}) collective-permute-start(bf16[2,256,2048]{2,1,0:T(8,128)(2,1)} %param.7), channel_id=1, source_target_pairs={{0,1},{1,0},{2,3},{3,2},{4,5},{5,4},{6,7},{7,6},{8,9},{9,8},{10,11... | collective-permute-start | bytes 6291464 | tf_op jit(solution)/shard_map/ppermute | solution.py:125
  5.3 17.0 %collective-permute-start.1 = (bf16[128,2176]{1,0:T(8,128)(2,1)}, bf16[128,2176]{1,0:T(8,128)(2,1)S(1)}, u32[]{:S(2)}, u32[]{:S(2)}) collective-permute-start(bf16[128,2176]{1,0:T(8,128)(2,1)} %get-tuple-element.39), channel_id=1, source_target_pairs={{0,8},{8,12},{12,4},{4,0},{1,9},{9,13},{13,5},{5,1},{2,10},{10,14}... | collective-permute-start | bytes 1671176 | tf_op jit(solution)/shard_map/ppermute | solution.py:595
  9.0 26.5 %collective-permute-start.2 = (bf16[128,2176]{1,0:T(8,128)(2,1)}, bf16[128,2176]{1,0:T(8,128)(2,1)S(1)}, u32[]{:S(2)}, u32[]{:S(2)}) collective-permute-start(bf16[128,2176]{1,0:T(8,128)(2,1)} %get-tuple-element.40), channel_id=1, source_target_pairs={{0,4},{4,12},{12,8},{8,0},{1,5},{5,13},{13,9},{9,1},{2,6},{6,14},{... | collective-permute-start | bytes 1671176 | tf_op jit(solution)/shard_map/ppermute | solution.py:596
  9.0 28.7 %collective-permute-start = (bf16[31,128,128]{2,1,0:T(8,128)(2,1)}, bf16[31,128,128]{2,1,0:T(8,128)(2,1)S(1)}, u32[]{:S(2)}, u32[]{:S(2)}) collective-permute-start(bf16[31,128,128]{2,1,0:T(8,128)(2,1)} %get-tuple-element.38), channel_id=1, source_target_pairs={{0,2},{2,0},{1,3},{3,1},{4,6},{6,4},{5,7},{7,5},{8,10},{10,8},{9,1... | collective-permute-start | bytes 3047432 | tf_op jit(solution)/shard_map/ppermute | solution.py:125
  36.4 13.3 %collective-permute-start.15 = (bf16[64,2048]{1,0:T(8,128)(2,1)S(1)}, bf16[64,2048]{1,0:T(8,128)(2,1)}, u32[]{:S(2)}, u32[]{:S(2)}) collective-permute-start(bf16[64,2048]{1,0:T(8,128)(2,1)S(1)} %get-tuple-element.73), channel_id=1, source_target_pairs={{0,4},{4,0},{8,12},{12,8},{1,5},{5,1},{9,13},{13,9},{2,6},{6,2},{1... | collective-permute-start | bytes 786440 | tf_op jit(solution)/shard_map/ppermute | solution.py:125
  44.9 29.9 %collective-permute-start.5 = (bf16[31,128,128]{2,1,0:T(8,128)(2,1)S(1)}, bf16[31,128,128]{2,1,0:T(8,128)(2,1)}, u32[]{:S(2)}, u32[]{:S(2)}) collective-permute-start(bf16[31,128,128]{2,1,0:T(8,128)(2,1)S(1)} %collective-permute-done.near.left_other), channel_id=1, source_target_pairs={{0,1},{1,0},{2,3},{3,2},{4,5},{5,4},{6,7},{7,6},{8,9},{9,8},{10,11... | collective-permute-start | bytes 3047432 | tf_op jit(solution)/shard_map/ppermute | solution.py:125
  53.3 20.9 %collective-permute-start.8 = (bf16[128,2048]{1,0:T(8,128)(2,1)S(1)}, bf16[128,2048]{1,0:T(8,128)(2,1)}, u32[]{:S(2)}, u32[]{:S(2)}) collective-permute-start(bf16[128,2048]{1,0:T(8,128)(2,1)S(1)} %dynamic-slice_bitcast_fusion.1), channel_id=1, source_target_pairs={{0,4},{4,0},{8,12},{12,8},{1,5},{5,1},{9,13},{13,9},{2,6},{6,2},{1... | collective-permute-start | bytes 1572872 | tf_op jit(solution)/shard_map/ppermute | solution.py:125
  53.7 26.9 %collective-permute-start.10 = (bf16[128,2048]{1,0:T(8,128)(2,1)S(1)}, bf16[128,2048]{1,0:T(8,128)(2,1)}, u32[]{:S(2)}, u32[]{:S(2)}) collective-permute-start(bf16[128,2048]{1,0:T(8,128)(2,1)S(1)} %copy-done.19), channel_id=1, source_target_pairs={{0,2},{2,0},{1,3},{3,1},{4,6},{6,4},{5,7},{7,5},{8,10},{10,8},{9,1... | collective-permute-start | bytes 1572872 | tf_op jit(solution)/shard_map/ppermute | solution.py:125
  59.1 15.1 %collective-permute-start.13 = (bf16[64,2048]{1,0:T(8,128)(2,1)S(1)}, bf16[64,2048]{1,0:T(8,128)(2,1)}, u32[]{:S(2)}, u32[]{:S(2)}) collective-permute-start(bf16[64,2048]{1,0:T(8,128)(2,1)S(1)} %collective-permute-done.4), channel_id=1, source_target_pairs={{0,2},{2,0},{1,3},{3,1},{4,6},{6,4},{5,7},{7,5},{8,10},{10,8},{9,1... | collective-permute-start | bytes 786440 | tf_op jit(solution)/shard_map/ppermute | solution.py:125
  61.3 19.8 %collective-permute-start.12 = (bf16[64,2048]{1,0:T(8,128)(2,1)S(1)}, bf16[64,2048]{1,0:T(8,128)(2,1)S(1)}, u32[]{:S(2)}, u32[]{:S(2)}) collective-permute-start(bf16[64,2048]{1,0:T(8,128)(2,1)S(1)} %collective-permute-done.4), channel_id=1, source_target_pairs={{0,1},{1,0},{2,3},{3,2},{4,5},{5,4},{6,7},{7,6},{8,9},{9,8},{10,11... | collective-permute-start | bytes 786440 | tf_op jit(solution)/shard_map/ppermute | solution.py:125
  74.2 12.8 %collective-permute-start.6 = (bf16[128,2176]{1,0:T(8,128)(2,1)S(1)}, bf16[128,2176]{1,0:T(8,128)(2,1)}, u32[]{:S(2)}, u32[]{:S(2)}) collective-permute-start(bf16[128,2176]{1,0:T(8,128)(2,1)S(1)} %collective-permute-done.1), channel_id=1, source_target_pairs={{0,1},{1,0},{2,3},{3,2},{4,5},{5,4},{6,7},{7,6},{8,9},{9,8},{10,11... | collective-permute-start | bytes 1671176 | tf_op jit(solution)/shard_map/ppermute | solution.py:125
  74.8 12.3 %collective-permute-start.7 = (bf16[128,2176]{1,0:T(8,128)(2,1)S(1)}, bf16[128,2176]{1,0:T(8,128)(2,1)}, u32[]{:S(2)}, u32[]{:S(2)}) collective-permute-start(bf16[128,2176]{1,0:T(8,128)(2,1)S(1)} %collective-permute-done.2), channel_id=1, source_target_pairs={{0,1},{1,0},{2,3},{3,2},{4,5},{5,4},{6,7},{7,6},{8,9},{9,8},{10,11... | collective-permute-start | bytes 1671176 | tf_op jit(solution)/shard_map/ppermute | solution.py:125
  84.5 24.9 %collective-permute-start.19 = (bf16[128,2048]{1,0:T(8,128)(2,1)S(1)}, bf16[128,2048]{1,0:T(8,128)(2,1)S(1)}, u32[]{:S(2)}, u32[]{:S(2)}) collective-permute-start(bf16[128,2048]{1,0:T(8,128)(2,1)S(1)} %dynamic-slice_bitcast_fusion), channel_id=1, source_target_pairs={{0,12},{4,8},{8,4},{12,0},{1,13},{5,9},{9,5},{13,1},{2,14},{6,10},... | collective-permute-start | bytes 1572872 | tf_op jit(solution)/shard_map/ppermute | solution.py:125
  122.2 12.6 %collective-permute-start.28 = (bf16[128,2048]{1,0:T(8,128)(2,1)S(1)}, bf16[128,2048]{1,0:T(8,128)(2,1)S(1)}, u32[]{:S(2)}, u32[]{:S(2)}) collective-permute-start(bf16[128,2048]{1,0:T(8,128)(2,1)S(1)} %get-tuple-element.59.refs_0_), channel_id=1, source_target_pairs={{0,4},{4,0},{8,12},{12,8},{1,5},{5,1},{9,13},{13,9},{2,6},{6,2},{1... | collective-permute-start | bytes 1572872 | tf_op jit(solution)/shard_map/ppermute | solution.py:125
  122.3 12.6 %collective-permute-start.30 = (bf16[128,2048]{1,0:T(8,128)(2,1)S(1)}, bf16[128,2048]{1,0:T(8,128)(2,1)S(1)}, u32[]{:S(2)}, u32[]{:S(2)}) collective-permute-start(bf16[128,2048]{1,0:T(8,128)(2,1)S(1)} %get-tuple-element.60), channel_id=1, source_target_pairs={{4,8},{8,4},{5,9},{9,5},{6,10},{10,6},{7,11},{11,7},{20,24},{24,20... | collective-permute-start | bytes 1572872 | tf_op jit(solution)/shard_map/ppermute | solution.py:684
  123.0 12.6 %collective-permute-start.29 = (bf16[128,2048]{1,0:T(8,128)(2,1)S(1)}, bf16[128,2048]{1,0:T(8,128)(2,1)S(1)}, u32[]{:S(2)}, u32[]{:S(2)}) collective-permute-start(bf16[128,2048]{1,0:T(8,128)(2,1)S(1)} %get-tuple-element.60), channel_id=1, source_target_pairs={{0,2},{2,0},{1,3},{3,1},{4,6},{6,4},{5,7},{7,5},{8,10},{10,8},{9,1... | collective-permute-start | bytes 1572872 | tf_op jit(solution)/shard_map/ppermute | solution.py:125
  124.5 16.3 %collective-permute-start.33 = (bf16[128,2048]{1,0:T(8,128)(2,1)S(1)}, bf16[128,2048]{1,0:T(8,128)(2,1)S(1)}, u32[]{:S(2)}, u32[]{:S(2)}) collective-permute-start(bf16[128,2048]{1,0:T(8,128)(2,1)S(1)} %get-tuple-element.59.refs_0_), channel_id=1, source_target_pairs={{0,1},{1,0},{2,3},{3,2},{4,5},{5,4},{6,7},{7,6},{8,9},{9,8},{10,11... | collective-permute-start | bytes 1572872 | tf_op jit(solution)/shard_map/ppermute | solution.py:125
  124.5 16.3 %collective-permute-start.34 = (bf16[128,2048]{1,0:T(8,128)(2,1)S(1)}, bf16[128,2048]{1,0:T(8,128)(2,1)S(1)}, u32[]{:S(2)}, u32[]{:S(2)}) collective-permute-start(bf16[128,2048]{1,0:T(8,128)(2,1)S(1)} %get-tuple-element.60), channel_id=1, source_target_pairs={{0,1},{1,0},{2,3},{3,2},{4,5},{5,4},{6,7},{7,6},{8,9},{9,8},{10,11... | collective-permute-start | bytes 1572872 | tf_op jit(solution)/shard_map/ppermute | solution.py:125
  135.7 14.9 %collective-permute-start.31 = (bf16[128,2048]{1,0:T(8,128)(2,1)S(1)}, bf16[128,2048]{1,0:T(8,128)(2,1)S(1)}, u32[]{:S(2)}, u32[]{:S(2)}) collective-permute-start(bf16[128,2048]{1,0:T(8,128)(2,1)S(1)} %get-tuple-element.59.refs_0_), channel_id=1, source_target_pairs={{0,2},{2,0},{1,3},{3,1},{4,6},{6,4},{5,7},{7,5},{8,10},{10,8},{9,1... | collective-permute-start | bytes 1572872 | tf_op jit(solution)/shard_map/ppermute | solution.py:125
  136.8 16.2 %collective-permute-start.35 = (bf16[128,2048]{1,0:T(8,128)(2,1)S(1)}, bf16[128,2048]{1,0:T(8,128)(2,1)S(1)}, u32[]{:S(2)}, u32[]{:S(2)}) collective-permute-start(bf16[128,2048]{1,0:T(8,128)(2,1)S(1)} %get-tuple-element.60), channel_id=1, source_target_pairs={{0,4},{4,0},{8,12},{12,8},{1,5},{5,1},{9,13},{13,9},{2,6},{6,2},{1... | collective-permute-start | bytes 1572872 | tf_op jit(solution)/shard_map/ppermute | solution.py:125
  140.2 18.3 %collective-permute-start.40 = (bf16[128,2048]{1,0:T(8,128)(2,1)S(1)}, bf16[128,2048]{1,0:T(8,128)(2,1)S(1)}, u32[]{:S(2)}, u32[]{:S(2)}) collective-permute-start(bf16[128,2048]{1,0:T(8,128)(2,1)S(1)} %collective-permute-done.28), channel_id=1, source_target_pairs={{0,2},{2,0},{1,3},{3,1},{4,6},{6,4},{5,7},{7,5},{8,10},{10,8},{9,1... | collective-permute-start | bytes 1572872 | tf_op jit(solution)/shard_map/ppermute | solution.py:125
  140.8 17.7 %collective-permute-start.36 = (bf16[128,2048]{1,0:T(8,128)(2,1)S(1)}, bf16[128,2048]{1,0:T(8,128)(2,1)S(1)}, u32[]{:S(2)}, u32[]{:S(2)}) collective-permute-start(bf16[128,2048]{1,0:T(8,128)(2,1)S(1)} %collective-permute-done.28), channel_id=1, source_target_pairs={{0,1},{1,0},{2,3},{3,2},{4,5},{5,4},{6,7},{7,6},{8,9},{9,8},{10,11... | collective-permute-start | bytes 1572872 | tf_op jit(solution)/shard_map/ppermute | solution.py:125
  140.8 19.1 %collective-permute-start.41 = (bf16[128,2048]{1,0:T(8,128)(2,1)S(1)}, bf16[128,2048]{1,0:T(8,128)(2,1)S(1)}, u32[]{:S(2)}, u32[]{:S(2)}) collective-permute-start(bf16[128,2048]{1,0:T(8,128)(2,1)S(1)} %collective-permute-done.29), channel_id=1, source_target_pairs={{0,4},{4,0},{8,12},{12,8},{1,5},{5,1},{9,13},{13,9},{2,6},{6,2},{1... | collective-permute-start | bytes 1572872 | tf_op jit(solution)/shard_map/ppermute | solution.py:125
  150.5 9.5 %collective-permute-start.39 = (bf16[128,2048]{1,0:T(8,128)(2,1)S(1)}, bf16[128,2048]{1,0:T(8,128)(2,1)S(1)}, u32[]{:S(2)}, u32[]{:S(2)}) collective-permute-start(bf16[128,2048]{1,0:T(8,128)(2,1)S(1)} %collective-permute-done.29), channel_id=1, source_target_pairs={{0,1},{1,0},{2,3},{3,2},{4,5},{5,4},{6,7},{7,6},{8,9},{9,8},{10,11... | collective-permute-start | bytes 1572872 | tf_op jit(solution)/shard_map/ppermute | solution.py:125
  153.1 11.5 %collective-permute-start.38 = (bf16[128,2048]{1,0:T(8,128)(2,1)S(1)}, bf16[128,2048]{1,0:T(8,128)(2,1)S(1)}, u32[]{:S(2)}, u32[]{:S(2)}) collective-permute-start(bf16[128,2048]{1,0:T(8,128)(2,1)S(1)} %collective-permute-done.31.refs_1_), channel_id=1, source_target_pairs={{0,1},{1,0},{2,3},{3,2},{4,5},{5,4},{6,7},{7,6},{8,9},{9,8},{10,11... | collective-permute-start | bytes 1572872 | tf_op jit(solution)/shard_map/ppermute | solution.py:125
  160.0 18.3 %collective-permute-start.32 = (bf16[128,2048]{1,0:T(8,128)(2,1)S(1)}, bf16[128,2048]{1,0:T(8,128)(2,1)S(1)}, u32[]{:S(2)}, u32[]{:S(2)}) collective-permute-start(bf16[128,2048]{1,0:T(8,128)(2,1)S(1)} %get-tuple-element.60), channel_id=1, source_target_pairs={{0,12},{12,0},{1,13},{13,1},{2,14},{14,2},{3,15},{15,3},{16,28},{2... | collective-permute-start | bytes 1572872 | tf_op jit(solution)/shard_map/ppermute | solution.py:696
  173.1 15.0 %collective-permute-start.45 = (bf16[64,2048]{1,0:T(8,128)(2,1)S(1)}, bf16[64,2048]{1,0:T(8,128)(2,1)}, u32[]{:S(2)}, u32[]{:S(2)}) collective-permute-start(bf16[64,2048]{1,0:T(8,128)(2,1)S(1)} %get-tuple-element.61), channel_id=1, source_target_pairs={{0,12},{4,8},{8,4},{12,0},{1,13},{5,9},{9,5},{13,1},{2,14},{6,10},... | collective-permute-start | bytes 786440 | tf_op jit(solution)/shard_map/ppermute | solution.py:125
  189.9 14.9 %collective-permute-start.44 = (bf16[128,2048]{1,0:T(8,128)(2,1)S(1)}, bf16[128,2048]{1,0:T(8,128)(2,1)S(1)}, u32[]{:S(2)}, u32[]{:S(2)}) collective-permute-start(bf16[128,2048]{1,0:T(8,128)(2,1)S(1)} %broadcast_select_fusion.refs_2_), channel_id=1, source_target_pairs={{0,2},{2,0},{1,3},{3,1},{4,6},{6,4},{5,7},{7,5},{8,10},{10,8},{9,1... | collective-permute-start | bytes 1572872 | tf_op jit(solution)/shard_map/ppermute | solution.py:125
  191.1 24.9 %collective-permute-start.48 = (bf16[128,2048]{1,0:T(8,128)(2,1)S(1)}, bf16[128,2048]{1,0:T(8,128)(2,1)S(1)}, u32[]{:S(2)}, u32[]{:S(2)}) collective-permute-start(bf16[128,2048]{1,0:T(8,128)(2,1)S(1)} %get-tuple-element.69.refs_0_), channel_id=1, source_target_pairs={{0,2},{2,0},{1,3},{3,1},{4,6},{6,4},{5,7},{7,5},{8,10},{10,8},{9,1... | collective-permute-start | bytes 1572872 | tf_op jit(solution)/shard_map/ppermute | solution.py:125
  197.4 24.2 %collective-permute-start.49 = (bf16[64,2048]{1,0:T(8,128)(2,1)}, bf16[64,2048]{1,0:T(8,128)(2,1)}, u32[]{:S(2)}, u32[]{:S(2)}) collective-permute-start(bf16[64,2048]{1,0:T(8,128)(2,1)} %collective-permute-done.45.refs_2_), channel_id=1, source_target_pairs={{0,2},{2,0},{1,3},{3,1},{4,6},{6,4},{5,7},{7,5},{8,10},{10,8},{9,1... | collective-permute-start | bytes 786440 | tf_op jit(solution)/shard_map/ppermute | solution.py:125
  203.6 21.9 %collective-permute-start.54 = (f32[2,8,128]{2,1,0:T(8,128)S(1)}, f32[2,8,128]{2,1,0:T(8,128)S(1)}, u32[]{:S(2)}, u32[]{:S(2)}) collective-permute-start(f32[2,8,128]{2,1,0:T(8,128)S(1)} %pad_maximum_fusion.2), channel_id=1, source_target_pairs={{0,2},{2,0},{1,3},{3,1},{4,6},{6,4},{5,7},{7,5},{8,10},{10,8},{9,1... | collective-permute-start | bytes 24584 | tf_op jit(solution)/shard_map/ppermute | solution.py:125
  204.8 21.6 %collective-permute-start.47 = (bf16[64,2048]{1,0:T(8,128)(2,1)}, bf16[64,2048]{1,0:T(8,128)(2,1)S(1)}, u32[]{:S(2)}, u32[]{:S(2)}) collective-permute-start(bf16[64,2048]{1,0:T(8,128)(2,1)} %collective-permute-done.46.refs_3_), channel_id=1, source_target_pairs={{0,2},{2,0},{1,3},{3,1},{4,6},{6,4},{5,7},{7,5},{8,10},{10,8},{9,1... | collective-permute-start | bytes 786440 | tf_op jit(solution)/shard_map/ppermute | solution.py:125
  (43 other events, 426.7 us)

commit v12 on v10

--- a/solution.py
+++ b/solution.py
@@ -111,10 +111,6 @@
     return (correction, sigma_two, subspace)
 
 
-MIX_A, MIX_B = 4, 5
-MIXES = ((MIX_A, 0, 0), (MIX_B, 0, 0))
-
-
 def halves_fit(mesh):
     sizes = dict(mesh.shape)
     return sizes["blk"] == 4 and sizes["ops"] == 2 and sizes["sub"] == 2
@@ -151,9 +147,6 @@
 
 def row_of(dz, dx, dc):
     z, x, c = place()
-    if dz in (MIX_A, MIX_B):
-        far = in_middle(z) if dz == MIX_A else jnp.logical_not(in_middle(z))
-        return jnp.where(far, row_of(2, 0, dc), row_of(1, 2, dc))
     return 4 * (z ^ dz) + 2 * (c ^ dc) + (x ^ dx if dx < 2 else dx - 2)
 
 
@@ -161,8 +154,8 @@
     count = len(plan)
     pieces, refs = refs[:count], refs[count:]
     if first:
-        masks, weight_own, psi_out, off_out, stats_out = refs[:5]
-        refs = refs[5:]
+        mix_a, mix_b, weight_own, psi_out, off_out, stats_out = refs[:6]
+        refs = refs[6:]
     else:
         hd_own, hd_far, psi_in, off_in, stats_in, near_out, far_out, late_out, stats_out = refs[:9]
         refs = refs[9:]
@@ -173,7 +166,6 @@
     links = table // sectors
     mine = 4 * z + 2 * c + x
     rows = (mine, mine ^ 12)
-    half = z // 2
 
     copies = []
 
@@ -193,13 +185,10 @@
         return lax.select(pattern[a, q] != 0, value, jnp.zeros_like(value))
 
     for piece, offsets in zip(pieces, plan):
-        base = 2 * half if piece.shape[0] == 4 else 0
         for at, (dz, dx, dc, start, tall) in enumerate(offsets):
             row = row_of(dz, dx, dc)
             for line in range(0, tall, 16):
-                value = piece[base + at, line : line + 16, 0:width]
-                if first:
-                    value = value * masks[row]
+                value = piece[at, line : line + 16, :]
                 field[row, start + line : start + line + 16, :] = value
 
     def right_col(term, b, j):
@@ -292,10 +281,7 @@
 
     sums = list(lax.fori_loop(0, sectors // step, column, (zero,) * (2 if first else 3)))
     if first:
-        parts = [
-            piece[0, 0:48, width:] for piece, offsets in zip(pieces, plan) if offsets[0][:3] in MIXES
-        ]
-        far_weight = sum(part.astype(jnp.float32) for part in parts)
+        far_weight = sum(mix[0:48, width:].astype(jnp.float32) for mix in (mix_a, mix_b))
         sums[1] += weight_own[...] + (far_weight[0:8] + far_weight[16:24] + far_weight[32:40])
     stats_out[...] = jnp.zeros_like(stats_out)
     for at, value in enumerate(sums):
@@ -314,7 +300,7 @@
     some = jax.ShapeDtypeStruct((block // 2, width), jnp.bfloat16)
     stats = jax.ShapeDtypeStruct((8, LANES), jnp.float32)
     out_shape = (rows, rows, stats) if first else (one, some, some, stats)
-    extra_specs = [VMEM, VMEM] if first else [ANY, ANY, VMEM, VMEM, VMEM]
+    extra_specs = [VMEM] * 3 if first else [ANY, ANY, VMEM, VMEM, VMEM]
     inner = 2 * 2 * sectors * 2 * links * links * block * block * block
     outer = 2 * 2 * 2 * links * block * block * width
     return pl.pallas_call(
@@ -594,24 +580,31 @@
     mix_a = lax.ppermute(mix_a, "blk", [(0, 2), (2, 3), (3, 1), (1, 0)])
     mix_b = lax.ppermute(mix_b, "blk", [(0, 1), (1, 3), (3, 2), (2, 0)])
     operators = across(packed, "ops", 1)
-    theta_core = across(theta, "sub", 1)
-
-    mix_a, mix_b = after((mix_a, mix_b), theta_core)
-    far = jnp.where(middle, mix_a[:, :width], mix_b[:, :width])
+
+    def masked(row, value):
+        line = lax.dynamic_index_in_dim(pattern, row, 0, keepdims=False).astype(jnp.bfloat16)
+        return value * jnp.repeat(line, block)[None, :]
+
+    own = [
+        masked(row_of(0, 2 + at, 0), lax.dynamic_slice(halves, (half, at, 0, 0), (1, 1, block, width))[0, 0])
+        for at in range(2)
+    ]
+    own_core = [across(value, "sub", 1) for value in own]
+
+    mix_a, mix_b = after((mix_a, mix_b), *own_core)
+    far = masked(row_of(2, 0, 0), jnp.where(middle, mix_a[:, :width], mix_b[:, :width]))
     far_z = across(far, "blk", 1)
     far_x = across(far, "ops", 1)
-    mix_a_core = across(mix_a, "sub", 1)
-    mix_b_core = across(mix_b, "sub", 1)
-    operators = after(operators, mix_b)
+    near_a = masked(row_of(1, 2, 0), jnp.where(middle, mix_b[:, :width], mix_a[:, :width]))
+    far_core = across(far, "sub", 1)
+    near_a_core = across(near_a, "sub", 1)
+
+    near_b = across(after(own[1], far_z, far_core, near_a_core), "blk", 1)
+    far_zx = across(far_z, "ops", 1)
+    operators = after(operators, far_z)
     operators_core = across(operators, "sub", 1)
     turned = arrange(right, operators, operators_core)
     cols = (*cols, operators[-1, :16, :sectors].astype(jnp.int32))
-    masks = jnp.repeat(pattern.astype(jnp.bfloat16), block, axis=1)
-    masks = jnp.broadcast_to(masks[:, None, :], (sectors, 16, width))
-
-    own_b = lax.dynamic_slice(halves, (half, 1, 0, 0), (1, 1, block, width))[0, 0]
-    near_b = across(after(own_b, mix_a_core, mix_b_core, turned), "blk", 1)
-    far_zx = across(far_z, "ops", 1)
     far_x_core = across(far_x, "sub", 1)
     far_z_core = across(far_z, "sub", 1)
     hd_far = lax.dynamic_index_in_dim(diag, x, 0, keepdims=False)
@@ -620,18 +613,19 @@
     near_b_core = across(near_b, "sub", 1)
 
     left = (left, operators)
-    pieces = [halves.reshape(4, block, width), theta_core.reshape(4, block, width)]
-    plan = [
-        ((0, 2, 0, 0, block), (0, 3, 0, 0, block)),
-        ((0, 2, 1, 0, block), (0, 3, 1, 0, block)),
-    ]
+    pieces = []
+    plan = []
     for piece, offset in (
-        (mix_a, (MIX_A, 0, 0)),
-        (mix_b, (MIX_B, 0, 0)),
-        (mix_a_core, (MIX_A, 0, 1)),
-        (mix_b_core, (MIX_B, 0, 1)),
+        (own[0], (0, 2, 0)),
+        (own[1], (0, 3, 0)),
+        (own_core[0], (0, 2, 1)),
+        (own_core[1], (0, 3, 1)),
+        (near_a, (1, 2, 0)),
         (near_b, (1, 3, 0)),
+        (near_a_core, (1, 2, 1)),
         (near_b_core, (1, 3, 1)),
+        (far, (2, 0, 0)),
+        (far_core, (2, 0, 1)),
         (far_x, (2, 1, 0)),
         (far_x_core, (2, 1, 1)),
         (far_z, (3, 0, 0)),
@@ -642,7 +636,7 @@
         pieces.append(piece[None])
         plan.append((offset + (0, block),))
     psi, off_one, stats_one = operate(
-        True, tuple(plan), pieces, cols, pattern, turned, left, (masks, weight_own)
+        True, tuple(plan), pieces, cols, pattern, turned, left, (mix_a, mix_b, weight_own)
     )
 
     found = share(stats_one)

time: 209 us -> 207 us (level)
  waiting for transfers between devices: 109 us -> 99.7 us
  local copies, waits for them, and re-layouts: 6.72 us -> 10.5 us
  starting transfers between devices: 48 us -> 50.6 us
    unnamed x23 -> x52, local copies, waits for them, and re-layouts: 4.39 us -> 10.3 us
    ppermute x1, waiting for transfers between devices: 13.3 us -> 8.52 us  [shards(): mix_a = lax.ppermute(mix_a, 'blk', [(0, 2), (2, 3), (3, 1), (1, 0)])]
    ppermute x41 -> x42, waiting for transfers between devices: 76.1 us -> 72.5 us  [across(): return lax.ppermute(value, axis, [(i, i ^ distance) for i in range(size)])]
    mul x0 -> x3, other arithmetic: none -> 2.18 us  [masked(): return value * jnp.repeat(line, block)[None, :]]
    ppermute x41 -> x42, starting transfers between devices: 34 us -> 35.6 us  [across(): return lax.ppermute(value, axis, [(i, i ^ distance) for i in range(size)])]
  transfers between devices with their start and end apart: 51 -> 52, of which waited for: 24 -> 25; matrix products, arithmetic and copies ran while one was open for 2% -> 2% of each run, Pallas kernels for 18% -> 15%
where the time goes in v12:
time: 207 us; the launch traced here: 204 us
  waiting for transfers between devices  99.7 us (48%)
  starting transfers between devices  50.6 us (24%)
  Pallas kernels  39.3 us (19%)
  local copies, waits for them, and re-layouts  10.5 us (5%)
  other arithmetic  3.2 us (2%)
    ppermute x42, waiting for transfers between devices, across(): return lax.ppermute(value, axis, [(i, i ^ distance) for i in range(size)])  72.5 us
    ppermute x42, starting transfers between devices, across(): return lax.ppermute(value, axis, [(i, i ^ distance) for i in range(size)])  35.6 us
    pallas_call x2, Pallas kernels, operate(): pl.pallas_call(functools.partial(operate_kernel, first, plan), out_shape=...  24.9 us
    ppermute x1, waiting for transfers between devices, shards(): mix_b = lax.ppermute(mix_b, 'blk', [(0, 1), (1, 3), (3, 2), (2, 0)])  12.4 us
    unnamed x52, local copies, waits for them, and re-layouts  10.3 us
    ppermute x1, waiting for transfers between devices, shards(): mix_a = lax.ppermute(mix_a, 'blk', [(0, 2), (2, 3), (3, 1), (1, 0)])  8.52 us
    ppermute x6, starting transfers between devices, share(): lax.ppermute(pair, axes, [(i, i ^ distance) for i in range(count)])  6.98 us
    ppermute x6, waiting for transfers between devices, share(): lax.ppermute(pair, axes, [(i, i ^ distance) for i in range(count)])  6.17 us
  transfers between devices with their start and end apart: 52, of which 25 were waited for; matrix products, arithmetic and copies ran while one was open for 2% of the time, Pallas kernels for 15%

profile of v12, /device:TPU:0, one launch (start us, length us, event | category | flops | bytes accessed | tf_op | source)
XLA Modules:
  0.0 204.4 jit_solution(2085475988241719750)
XLA Ops:
  0.7 4.3 %prepare.1 = (bf16[128,2176]{1,0:T(8,128)(2,1)}, bf16[128,2176]{1,0:T(8,128)(2,1)}, bf16[31,128,128]{2,1,0:T(8,128)(2,1)}, f32[8,128]{1,0:T(8,128)}) custom-call(s32[16,16]{1,0:T(8,128)} %pattern.5, bf16[2,2,128,2048]{3,2,1,0:T(8,128)(2,1)} %bitcast.115, bf16[2,128,2048]{2,1,0:T(8,128)(2,1)} %bitcast.76, bf16[48,128,128]{2,1,0:T(8,128)(2,1)} %bitcast.80, ...), custom_call_target="tpu_custom_call" | custom-call | tf_op jit(solution)/shard_map/prepare/pallas_call | solution.py:435
  5.0 4.1 %collective-permute-start.1 = (bf16[128,2176]{1,0:T(8,128)(2,1)}, bf16[128,2176]{1,0:T(8,128)(2,1)S(1)}, u32[]{:S(2)}, u32[]{:S(2)}) collective-permute-start(bf16[128,2176]{1,0:T(8,128)(2,1)} %get-tuple-element.35), channel_id=1, source_target_pairs={{0,8},{8,12},{12,4},{4,0},{1,9},{9,13},{13,5},{5,1},{2,10},{10,14}... | collective-permute-start | bytes 1671176 | tf_op jit(solution)/shard_map/ppermute | solution.py:580
  13.9 8.5 %collective-permute-done.1.refs_16_ = bf16[128,2176]{1,0:T(8,128)(2,1)S(1)} collective-permute-done((bf16[128,2176]{1,0:T(8,128)(2,1)}, bf16[128,2176]{1,0:T(8,128)(2,1)S(1)}, u32[]{:S(2)}, u32[]{:S(2)}) %collective-permute-start.1) | collective-permute-done | bytes 557088 | tf_op jit(solution)/shard_map/ppermute | solution.py:580
  22.5 12.4 %collective-permute-done.2.refs_17_ = bf16[128,2176]{1,0:T(8,128)(2,1)S(1)} collective-permute-done((bf16[128,2176]{1,0:T(8,128)(2,1)}, bf16[128,2176]{1,0:T(8,128)(2,1)S(1)}, u32[]{:S(2)}, u32[]{:S(2)}) %collective-permute-start.2) | collective-permute-done | bytes 557088 | tf_op jit(solution)/shard_map/ppermute | solution.py:581
  39.4 9.6 %collective-permute-done.5 = bf16[128,2048]{1,0:T(8,128)(2,1)} collective-permute-done((bf16[128,2048]{1,0:T(8,128)(2,1)S(1)}, bf16[128,2048]{1,0:T(8,128)(2,1)}, u32[]{:S(2)}, u32[]{:S(2)}) %collective-permute-start.5) | collective-permute-done | bytes 524320 | tf_op jit(solution)/shard_map/ppermute | solution.py:121
  53.0 11.0 %collective-permute-done.9 = bf16[128,2048]{1,0:T(8,128)(2,1)} collective-permute-done((bf16[128,2048]{1,0:T(8,128)(2,1)}, bf16[128,2048]{1,0:T(8,128)(2,1)}, u32[]{:S(2)}, u32[]{:S(2)}) %collective-permute-start.9) | collective-permute-done | bytes 524320 | tf_op jit(solution)/shard_map/ppermute | solution.py:121
  65.6 2.5 %collective-permute-start.16 = (bf16[128,2048]{1,0:T(8,128)(2,1)S(1)}, bf16[128,2048]{1,0:T(8,128)(2,1)S(1)}, u32[]{:S(2)}, u32[]{:S(2)}) collective-permute-start(bf16[128,2048]{1,0:T(8,128)(2,1)S(1)} %dynamic-slice_bitcast_fusion), channel_id=1, source_target_pairs={{0,12},{4,8},{8,4},{12,0},{1,13},{5,9},{9,5},{13,1},{2,14},{6,10},... | collective-permute-start | bytes 1572872 | tf_op jit(solution)/shard_map/ppermute | solution.py:121
  69.6 2.9 %arrange.1.right = bf16[2,48,128,128]{3,2,1,0:T(8,128)(2,1)S(1)} custom-call(bf16[48,128,128]{2,1,0:T(8,128)(2,1)S(1)} %bitcast.81, bf16[31,128,128]{2,1,0:T(8,128)(2,1)S(1)} %collective-permute-done.near.left_other, bf16[31,128,128]{2,1,0:T(8,128)(2,1)} %collective-permute-done.6.far), custom_call_target="tpu_custom_call" | custom-call | tf_op jit(solution)/shard_map/arrange/pallas_call | solution.py:351
  72.6 1.6 copy-done
  74.3 13.1 %operate_first.1 = (bf16[2,128,2048]{2,1,0:T(8,128)(2,1)}, bf16[2,128,2048]{2,1,0:T(8,128)(2,1)}, f32[8,128]{1,0:T(8,128)S(1)}) custom-call(s32[3,1,16]{2,1,0:T(1,128)S(1)} %bitcast.106, s32[3,1,16]{2,1,0:T(1,128)S(1)} %bitcast.109, s32[16,16]{1,0:T(8,128)S(1)} %bitcast_convert_fusion.cols_other, s32[16,16]{1,0:T(8,128)S(1)} %copy-done.20, ...), custom_call_target="tpu_custom_call" | custom-call | flops 3221225472 | bytes 16777216 | tf_op jit(solution)/shard_map/operate_first/pallas_call | solution.py:306
  90.5 1.7 collective-permute-start.20
  92.3 1.5 collective-permute-done.19.refs_2_
  97.5 2.2 %update.1 = (f32[2,128,2048]{2,1,0:T(8,128)S(1)}, f32[8,128]{1,0:T(8,128)S(1)}) custom-call(bf16[2,128,2048]{2,1,0:T(8,128)(2,1)S(1)} %copy-done.2, bf16[2,128,2048]{2,1,0:T(8,128)(2,1)S(1)} %copy-done.5, bf16[2,128,2048]{2,1,0:T(8,128)(2,1)S(1)} %bitcast.79, bf16[128,2048]{1,0:T(8,128)(2,1)S(1)} %collective-permute-done.16.hd_far.refs_17_, ...), custom_call_target="tpu_custom_call" | custom-call | tf_op jit(solution)/shard_map/update/pallas_call | solution.py:643
  101.4 1.7 collective-permute-start.23
  105.1 2.6 %collective-permute-done.24.refs_3_ = f32[2,8,128]{2,1,0:T(8,128)S(1)} collective-permute-done((f32[2,8,128]{2,1,0:T(8,128)S(1)}, f32[2,8,128]{2,1,0:T(8,128)S(1)}, u32[]{:S(2)}, u32[]{:S(2)}) %collective-permute-start.24) | collective-permute-done | bytes 8224 | tf_op jit(solution)/shard_map/ppermute | solution.py:130
  111.4 9.2 %collective-permute-done.25 = bf16[128,2048]{1,0:T(8,128)(2,1)S(1)} collective-permute-done((bf16[128,2048]{1,0:T(8,128)(2,1)S(1)}, bf16[128,2048]{1,0:T(8,128)(2,1)S(1)}, u32[]{:S(2)}, u32[]{:S(2)}) %collective-permute-start.25) | collective-permute-done | bytes 524320 | tf_op jit(solution)/shard_map/ppermute | solution.py:121
  120.8 4.7 %collective-permute-start.32 = (bf16[128,2048]{1,0:T(8,128)(2,1)S(1)}, bf16[128,2048]{1,0:T(8,128)(2,1)S(1)}, u32[]{:S(2)}, u32[]{:S(2)}) collective-permute-start(bf16[128,2048]{1,0:T(8,128)(2,1)S(1)} %get-tuple-element.53), channel_id=1, source_target_pairs={{0,4},{4,0},{8,12},{12,8},{1,5},{5,1},{9,13},{13,9},{2,6},{6,2},{1... | collective-permute-start | bytes 1572872 | tf_op jit(solution)/shard_map/ppermute | solution.py:121
  126.0 1.5 collective-permute-start.37
  127.6 10.7 %collective-permute-done.32 = bf16[128,2048]{1,0:T(8,128)(2,1)S(1)} collective-permute-done((bf16[128,2048]{1,0:T(8,128)(2,1)S(1)}, bf16[128,2048]{1,0:T(8,128)(2,1)S(1)}, u32[]{:S(2)}, u32[]{:S(2)}) %collective-permute-start.32) | collective-permute-done | bytes 524320 | tf_op jit(solution)/shard_map/ppermute | solution.py:121
  138.3 2.0 collective-permute-done.28.refs_1_
  140.4 6.9 %collective-permute-done.37 = bf16[128,2048]{1,0:T(8,128)(2,1)S(1)} collective-permute-done((bf16[128,2048]{1,0:T(8,128)(2,1)S(1)}, bf16[128,2048]{1,0:T(8,128)(2,1)S(1)}, u32[]{:S(2)}, u32[]{:S(2)}) %collective-permute-start.37) | collective-permute-done | bytes 524320 | tf_op jit(solution)/shard_map/ppermute | solution.py:121
  147.8 3.2 %collective-permute-start.29 = (bf16[128,2048]{1,0:T(8,128)(2,1)S(1)}, bf16[128,2048]{1,0:T(8,128)(2,1)S(1)}, u32[]{:S(2)}, u32[]{:S(2)}) collective-permute-start(bf16[128,2048]{1,0:T(8,128)(2,1)S(1)} %get-tuple-element.53), channel_id=1, source_target_pairs={{0,12},{12,0},{1,13},{13,1},{2,14},{14,2},{3,15},{15,3},{16,28},{2... | collective-permute-start | bytes 1572872 | tf_op jit(solution)/shard_map/ppermute | solution.py:685
  151.1 11.8 %operate_second.1 = (bf16[128,2048]{1,0:T(8,128)(2,1)S(1)}, bf16[64,2048]{1,0:T(8,128)(2,1)S(1)}, bf16[64,2048]{1,0:T(8,128)(2,1)S(1)}, f32[8,128]{1,0:T(8,128)S(1)}) custom-call(s32[3,1,16]{2,1,0:T(1,128)S(1)} %bitcast.107, s32[3,1,16]{2,1,0:T(1,128)S(1)} %bitcast.110, s32[16,16]{1,0:T(8,128)S(1)} %bitcast_convert_fusion.cols_other, ...), custom_call_target="tpu_custom_call" | custom-call | bytes 1024 | tf_op jit(solution)/shard_map/operate_second/pallas_call | solution.py:306
  162.9 2.6 %collective-permute-start.43 = (bf16[64,2048]{1,0:T(8,128)(2,1)S(1)}, bf16[64,2048]{1,0:T(8,128)(2,1)}, u32[]{:S(2)}, u32[]{:S(2)}) collective-permute-start(bf16[64,2048]{1,0:T(8,128)(2,1)S(1)} %get-tuple-element.57), channel_id=1, source_target_pairs={{0,12},{4,8},{8,4},{12,0},{1,13},{5,9},{9,5},{13,1},{2,14},{6,10},... | collective-permute-start | bytes 786440 | tf_op jit(solution)/shard_map/ppermute | solution.py:121
  166.6 6.7 %collective-permute-done.43.refs_2_ = bf16[64,2048]{1,0:T(8,128)(2,1)} collective-permute-done((bf16[64,2048]{1,0:T(8,128)(2,1)S(1)}, bf16[64,2048]{1,0:T(8,128)(2,1)}, u32[]{:S(2)}, u32[]{:S(2)}) %collective-permute-start.43) | collective-permute-done | bytes 262176 | tf_op jit(solution)/shard_map/ppermute | solution.py:121
  173.4 4.3 %collective-permute-start.48 = (f32[8,128]{1,0:T(8,128)S(1)}, f32[8,128]{1,0:T(8,128)S(1)}, u32[]{:S(2)}, u32[]{:S(2)}) collective-permute-start(f32[8,128]{1,0:T(8,128)S(1)} %add.66), channel_id=1, source_target_pairs={{0,4},{4,0},{8,12},{12,8},{1,5},{5,1},{9,13},{13,9},{2,6},{6,2},{1... | collective-permute-start | bytes 12296 | tf_op jit(solution)/shard_map/ppermute | solution.py:121
  178.4 2.4 %collective-permute-start.50 = (f32[8,128]{1,0:T(8,128)S(1)}, f32[8,128]{1,0:T(8,128)S(1)}, u32[]{:S(2)}, u32[]{:S(2)}) collective-permute-start(f32[8,128]{1,0:T(8,128)S(1)} %add.66), channel_id=1, source_target_pairs={{0,12},{4,8},{8,4},{12,0},{1,13},{5,9},{9,5},{13,1},{2,14},{6,10},... | collective-permute-start | bytes 12296 | tf_op jit(solution)/shard_map/ppermute | solution.py:121
  183.9 6.2 %collective-permute-done.44.refs_3_ = bf16[64,2048]{1,0:T(8,128)(2,1)} collective-permute-done((bf16[64,2048]{1,0:T(8,128)(2,1)S(1)}, bf16[64,2048]{1,0:T(8,128)(2,1)}, u32[]{:S(2)}, u32[]{:S(2)}) %collective-permute-start.44) | collective-permute-done | bytes 262176 | tf_op jit(solution)/shard_map/ppermute | solution.py:121
  190.1 1.5 collective-permute-start.51
  192.1 1.5 collective-permute-start.45
  195.9 5.0 %collective-permute-done.47.refs_4_ = bf16[64,2048]{1,0:T(8,128)(2,1)} collective-permute-done((bf16[64,2048]{1,0:T(8,128)(2,1)}, bf16[64,2048]{1,0:T(8,128)(2,1)}, u32[]{:S(2)}, u32[]{:S(2)}) %collective-permute-start.47) | collective-permute-done | bytes 262176 | tf_op jit(solution)/shard_map/ppermute | solution.py:121
  200.9 2.4 %assemble.4.refs_1_ = bf16[2,2,128,2048]{3,2,1,0:T(8,128)(2,1)} custom-call(bf16[128,2048]{1,0:T(8,128)(2,1)S(1)} %get-tuple-element.61.refs_0_, bf16[128,2048]{1,0:T(8,128)(2,1)S(1)} %collective-permute-done.46.refs_1_, bf16[64,2048]{1,0:T(8,128)(2,1)} %collective-permute-done.43.refs_2_, bf16[64,2048]{1,0:T(8,128)(2,1)} %collective-permute-done.44.refs_3_, ...), custom_call_target="tpu_custom_call" | custom-call | tf_op jit(solution)/shard_map/assemble/pallas_call | solution.py:548
  (153 shorter events, 40.9 us)
Async XLA Ops:
  5.0 17.5 %collective-permute-start.1 = (bf16[128,2176]{1,0:T(8,128)(2,1)}, bf16[128,2176]{1,0:T(8,128)(2,1)S(1)}, u32[]{:S(2)}, u32[]{:S(2)}) collective-permute-start(bf16[128,2176]{1,0:T(8,128)(2,1)} %get-tuple-element.35), channel_id=1, source_target_pairs={{0,8},{8,12},{12,4},{4,0},{1,9},{9,13},{13,5},{5,1},{2,10},{10,14}... | collective-permute-start | bytes 1671176 | tf_op jit(solution)/shard_map/ppermute | solution.py:580
  9.1 25.8 %collective-permute-start.2 = (bf16[128,2176]{1,0:T(8,128)(2,1)}, bf16[128,2176]{1,0:T(8,128)(2,1)S(1)}, u32[]{:S(2)}, u32[]{:S(2)}) collective-permute-start(bf16[128,2176]{1,0:T(8,128)(2,1)} %get-tuple-element.36), channel_id=1, source_target_pairs={{0,4},{4,12},{12,8},{8,0},{1,5},{5,13},{13,9},{9,1},{2,6},{6,14},{... | collective-permute-start | bytes 1671176 | tf_op jit(solution)/shard_map/ppermute | solution.py:581
  10.7 41.6 %collective-permute-start = (bf16[31,128,128]{2,1,0:T(8,128)(2,1)}, bf16[31,128,128]{2,1,0:T(8,128)(2,1)S(1)}, u32[]{:S(2)}, u32[]{:S(2)}) collective-permute-start(bf16[31,128,128]{2,1,0:T(8,128)(2,1)} %get-tuple-element.34), channel_id=1, source_target_pairs={{0,2},{2,0},{1,3},{3,1},{4,6},{6,4},{5,7},{7,5},{8,10},{10,8},{9,1... | collective-permute-start | bytes 3047432 | tf_op jit(solution)/shard_map/ppermute | solution.py:121
  35.0 14.0 %collective-permute-start.5 = (bf16[128,2048]{1,0:T(8,128)(2,1)S(1)}, bf16[128,2048]{1,0:T(8,128)(2,1)}, u32[]{:S(2)}, u32[]{:S(2)}) collective-permute-start(bf16[128,2048]{1,0:T(8,128)(2,1)S(1)} %get-tuple-element.70), channel_id=1, source_target_pairs={{0,4},{4,0},{8,12},{12,8},{1,5},{5,1},{9,13},{13,9},{2,6},{6,2},{1... | collective-permute-start | bytes 1572872 | tf_op jit(solution)/shard_map/ppermute | solution.py:121
  35.8 13.2 %collective-permute-start.7 = (bf16[128,2048]{1,0:T(8,128)(2,1)S(1)}, bf16[128,2048]{1,0:T(8,128)(2,1)S(1)}, u32[]{:S(2)}, u32[]{:S(2)}) collective-permute-start(bf16[128,2048]{1,0:T(8,128)(2,1)S(1)} %get-tuple-element.70), channel_id=1, source_target_pairs={{0,1},{1,0},{2,3},{3,2},{4,5},{5,4},{6,7},{7,6},{8,9},{9,8},{10,11... | collective-permute-start | bytes 1572872 | tf_op jit(solution)/shard_map/ppermute | solution.py:121
  35.8 14.0 %collective-permute-start.8 = (bf16[128,2048]{1,0:T(8,128)(2,1)S(1)}, bf16[128,2048]{1,0:T(8,128)(2,1)S(1)}, u32[]{:S(2)}, u32[]{:S(2)}) collective-permute-start(bf16[128,2048]{1,0:T(8,128)(2,1)S(1)} %get-tuple-element.69), channel_id=1, source_target_pairs={{0,1},{1,0},{2,3},{3,2},{4,5},{5,4},{6,7},{7,6},{8,9},{9,8},{10,11... | collective-permute-start | bytes 1572872 | tf_op jit(solution)/shard_map/ppermute | solution.py:121
  37.1 15.8 %collective-permute-start.11 = (bf16[128,2048]{1,0:T(8,128)(2,1)S(1)}, bf16[128,2048]{1,0:T(8,128)(2,1)}, u32[]{:S(2)}, u32[]{:S(2)}) collective-permute-start(bf16[128,2048]{1,0:T(8,128)(2,1)S(1)} %get-tuple-element.70), channel_id=1, source_target_pairs={{0,2},{2,0},{1,3},{3,1},{4,6},{6,4},{5,7},{7,5},{8,10},{10,8},{9,1... | collective-permute-start | bytes 1572872 | tf_op jit(solution)/shard_map/ppermute | solution.py:121
  50.6 13.3 %collective-permute-start.9 = (bf16[128,2048]{1,0:T(8,128)(2,1)}, bf16[128,2048]{1,0:T(8,128)(2,1)}, u32[]{:S(2)}, u32[]{:S(2)}) collective-permute-start(bf16[128,2048]{1,0:T(8,128)(2,1)} %get-tuple-element.40), channel_id=1, source_target_pairs={{0,4},{4,0},{8,12},{12,8},{1,5},{5,1},{9,13},{13,9},{2,6},{6,2},{1... | collective-permute-start | bytes 1572872 | tf_op jit(solution)/shard_map/ppermute | solution.py:121
  50.9 13.0 %collective-permute-start.14 = (bf16[128,2048]{1,0:T(8,128)(2,1)}, bf16[128,2048]{1,0:T(8,128)(2,1)}, u32[]{:S(2)}, u32[]{:S(2)}) collective-permute-start(bf16[128,2048]{1,0:T(8,128)(2,1)} %collective-permute-done.5), channel_id=1, source_target_pairs={{0,2},{2,0},{1,3},{3,1},{4,6},{6,4},{5,7},{7,5},{8,10},{10,8},{9,1... | collective-permute-start | bytes 1572872 | tf_op jit(solution)/shard_map/ppermute | solution.py:121
  52.4 13.2 %collective-permute-start.6 = (bf16[31,128,128]{2,1,0:T(8,128)(2,1)S(1)}, bf16[31,128,128]{2,1,0:T(8,128)(2,1)}, u32[]{:S(2)}, u32[]{:S(2)}) collective-permute-start(bf16[31,128,128]{2,1,0:T(8,128)(2,1)S(1)} %collective-permute-done.near.left_other), channel_id=1, source_target_pairs={{0,1},{1,0},{2,3},{3,2},{4,5},{5,4},{6,7},{7,6},{8,9},{9,8},{10,11... | collective-permute-start | bytes 3047432 | tf_op jit(solution)/shard_map/ppermute | solution.py:121
  52.4 21.8 %collective-permute-start.13 = (bf16[128,2048]{1,0:T(8,128)(2,1)}, bf16[128,2048]{1,0:T(8,128)(2,1)}, u32[]{:S(2)}, u32[]{:S(2)}) collective-permute-start(bf16[128,2048]{1,0:T(8,128)(2,1)} %collective-permute-done.5), channel_id=1, source_target_pairs={{0,1},{1,0},{2,3},{3,2},{4,5},{5,4},{6,7},{7,6},{8,9},{9,8},{10,11... | collective-permute-start | bytes 1572872 | tf_op jit(solution)/shard_map/ppermute | solution.py:121
  52.9 21.3 %collective-permute-start.12 = (bf16[128,2048]{1,0:T(8,128)(2,1)}, bf16[128,2048]{1,0:T(8,128)(2,1)}, u32[]{:S(2)}, u32[]{:S(2)}) collective-permute-start(bf16[128,2048]{1,0:T(8,128)(2,1)} %collective-permute-done.11), channel_id=1, source_target_pairs={{0,1},{1,0},{2,3},{3,2},{4,5},{5,4},{6,7},{7,6},{8,9},{9,8},{10,11... | collective-permute-start | bytes 1572872 | tf_op jit(solution)/shard_map/ppermute | solution.py:121
  63.9 10.3 %collective-permute-start.10 = (bf16[128,2048]{1,0:T(8,128)(2,1)}, bf16[128,2048]{1,0:T(8,128)(2,1)}, u32[]{:S(2)}, u32[]{:S(2)}) collective-permute-start(bf16[128,2048]{1,0:T(8,128)(2,1)} %collective-permute-done.9), channel_id=1, source_target_pairs={{0,1},{1,0},{2,3},{3,2},{4,5},{5,4},{6,7},{7,6},{8,9},{9,8},{10,11... | collective-permute-start | bytes 1572872 | tf_op jit(solution)/shard_map/ppermute | solution.py:121
  64.0 10.3 %collective-permute-start.15 = (bf16[128,2048]{1,0:T(8,128)(2,1)}, bf16[128,2048]{1,0:T(8,128)(2,1)}, u32[]{:S(2)}, u32[]{:S(2)}) collective-permute-start(bf16[128,2048]{1,0:T(8,128)(2,1)} %collective-permute-done.14), channel_id=1, source_target_pairs={{0,1},{1,0},{2,3},{3,2},{4,5},{5,4},{6,7},{7,6},{8,9},{9,8},{10,11... | collective-permute-start | bytes 1572872 | tf_op jit(solution)/shard_map/ppermute | solution.py:121
  65.6 26.6 %collective-permute-start.16 = (bf16[128,2048]{1,0:T(8,128)(2,1)S(1)}, bf16[128,2048]{1,0:T(8,128)(2,1)S(1)}, u32[]{:S(2)}, u32[]{:S(2)}) collective-permute-start(bf16[128,2048]{1,0:T(8,128)(2,1)S(1)} %dynamic-slice_bitcast_fusion), channel_id=1, source_target_pairs={{0,12},{4,8},{8,4},{12,0},{1,13},{5,9},{9,5},{13,1},{2,14},{6,10},... | collective-permute-start | bytes 1572872 | tf_op jit(solution)/shard_map/ppermute | solution.py:121
  108.3 12.4 %collective-permute-start.25 = (bf16[128,2048]{1,0:T(8,128)(2,1)S(1)}, bf16[128,2048]{1,0:T(8,128)(2,1)S(1)}, u32[]{:S(2)}, u32[]{:S(2)}) collective-permute-start(bf16[128,2048]{1,0:T(8,128)(2,1)S(1)} %get-tuple-element.52.refs_0_), channel_id=1, source_target_pairs={{0,4},{4,0},{8,12},{12,8},{1,5},{5,1},{9,13},{13,9},{2,6},{6,2},{1... | collective-permute-start | bytes 1572872 | tf_op jit(solution)/shard_map/ppermute | solution.py:121
  108.7 12.0 %collective-permute-start.26 = (bf16[128,2048]{1,0:T(8,128)(2,1)S(1)}, bf16[128,2048]{1,0:T(8,128)(2,1)S(1)}, u32[]{:S(2)}, u32[]{:S(2)}) collective-permute-start(bf16[128,2048]{1,0:T(8,128)(2,1)S(1)} %get-tuple-element.53), channel_id=1, source_target_pairs={{0,2},{2,0},{1,3},{3,1},{4,6},{6,4},{5,7},{7,5},{8,10},{10,8},{9,1... | collective-permute-start | bytes 1572872 | tf_op jit(solution)/shard_map/ppermute | solution.py:121
  110.2 10.6 %collective-permute-start.27 = (bf16[128,2048]{1,0:T(8,128)(2,1)S(1)}, bf16[128,2048]{1,0:T(8,128)(2,1)S(1)}, u32[]{:S(2)}, u32[]{:S(2)}) collective-permute-start(bf16[128,2048]{1,0:T(8,128)(2,1)S(1)} %get-tuple-element.53), channel_id=1, source_target_pairs={{4,8},{8,4},{5,9},{9,5},{6,10},{10,6},{7,11},{11,7},{20,24},{24,20... | collective-permute-start | bytes 1572872 | tf_op jit(solution)/shard_map/ppermute | solution.py:673
  110.9 16.6 %collective-permute-start.30 = (bf16[128,2048]{1,0:T(8,128)(2,1)S(1)}, bf16[128,2048]{1,0:T(8,128)(2,1)S(1)}, u32[]{:S(2)}, u32[]{:S(2)}) collective-permute-start(bf16[128,2048]{1,0:T(8,128)(2,1)S(1)} %get-tuple-element.52.refs_0_), channel_id=1, source_target_pairs={{0,1},{1,0},{2,3},{3,2},{4,5},{5,4},{6,7},{7,6},{8,9},{9,8},{10,11... | collective-permute-start | bytes 1572872 | tf_op jit(solution)/shard_map/ppermute | solution.py:121
  111.0 16.6 %collective-permute-start.31 = (bf16[128,2048]{1,0:T(8,128)(2,1)S(1)}, bf16[128,2048]{1,0:T(8,128)(2,1)S(1)}, u32[]{:S(2)}, u32[]{:S(2)}) collective-permute-start(bf16[128,2048]{1,0:T(8,128)(2,1)S(1)} %get-tuple-element.53), channel_id=1, source_target_pairs={{0,1},{1,0},{2,3},{3,2},{4,5},{5,4},{6,7},{7,6},{8,9},{9,8},{10,11... | collective-permute-start | bytes 1572872 | tf_op jit(solution)/shard_map/ppermute | solution.py:121
  120.8 17.6 %collective-permute-start.32 = (bf16[128,2048]{1,0:T(8,128)(2,1)S(1)}, bf16[128,2048]{1,0:T(8,128)(2,1)S(1)}, u32[]{:S(2)}, u32[]{:S(2)}) collective-permute-start(bf16[128,2048]{1,0:T(8,128)(2,1)S(1)} %get-tuple-element.53), channel_id=1, source_target_pairs={{0,4},{4,0},{8,12},{12,8},{1,5},{5,1},{9,13},{13,9},{2,6},{6,2},{1... | collective-permute-start | bytes 1572872 | tf_op jit(solution)/shard_map/ppermute | solution.py:121
  125.5 14.9 %collective-permute-start.28 = (bf16[128,2048]{1,0:T(8,128)(2,1)S(1)}, bf16[128,2048]{1,0:T(8,128)(2,1)S(1)}, u32[]{:S(2)}, u32[]{:S(2)}) collective-permute-start(bf16[128,2048]{1,0:T(8,128)(2,1)S(1)} %get-tuple-element.52.refs_0_), channel_id=1, source_target_pairs={{0,2},{2,0},{1,3},{3,1},{4,6},{6,4},{5,7},{7,5},{8,10},{10,8},{9,1... | collective-permute-start | bytes 1572872 | tf_op jit(solution)/shard_map/ppermute | solution.py:121
  126.0 21.2 %collective-permute-start.37 = (bf16[128,2048]{1,0:T(8,128)(2,1)S(1)}, bf16[128,2048]{1,0:T(8,128)(2,1)S(1)}, u32[]{:S(2)}, u32[]{:S(2)}) collective-permute-start(bf16[128,2048]{1,0:T(8,128)(2,1)S(1)} %collective-permute-done.25), channel_id=1, source_target_pairs={{0,2},{2,0},{1,3},{3,1},{4,6},{6,4},{5,7},{7,5},{8,10},{10,8},{9,1... | collective-permute-start | bytes 1572872 | tf_op jit(solution)/shard_map/ppermute | solution.py:121
  127.5 19.7 %collective-permute-start.38 = (bf16[128,2048]{1,0:T(8,128)(2,1)S(1)}, bf16[128,2048]{1,0:T(8,128)(2,1)S(1)}, u32[]{:S(2)}, u32[]{:S(2)}) collective-permute-start(bf16[128,2048]{1,0:T(8,128)(2,1)S(1)} %collective-permute-done.26), channel_id=1, source_target_pairs={{0,4},{4,0},{8,12},{12,8},{1,5},{5,1},{9,13},{13,9},{2,6},{6,2},{1... | collective-permute-start | bytes 1572872 | tf_op jit(solution)/shard_map/ppermute | solution.py:121
  127.5 20.2 %collective-permute-start.33 = (bf16[128,2048]{1,0:T(8,128)(2,1)S(1)}, bf16[128,2048]{1,0:T(8,128)(2,1)S(1)}, u32[]{:S(2)}, u32[]{:S(2)}) collective-permute-start(bf16[128,2048]{1,0:T(8,128)(2,1)S(1)} %collective-permute-done.25), channel_id=1, source_target_pairs={{0,1},{1,0},{2,3},{3,2},{4,5},{5,4},{6,7},{7,6},{8,9},{9,8},{10,11... | collective-permute-start | bytes 1572872 | tf_op jit(solution)/shard_map/ppermute | solution.py:121
  138.3 9.5 %collective-permute-start.36 = (bf16[128,2048]{1,0:T(8,128)(2,1)S(1)}, bf16[128,2048]{1,0:T(8,128)(2,1)S(1)}, u32[]{:S(2)}, u32[]{:S(2)}) collective-permute-start(bf16[128,2048]{1,0:T(8,128)(2,1)S(1)} %collective-permute-done.26), channel_id=1, source_target_pairs={{0,1},{1,0},{2,3},{3,2},{4,5},{5,4},{6,7},{7,6},{8,9},{9,8},{10,11... | collective-permute-start | bytes 1572872 | tf_op jit(solution)/shard_map/ppermute | solution.py:121
  140.3 10.7 %collective-permute-start.34 = (bf16[128,2048]{1,0:T(8,128)(2,1)S(1)}, bf16[128,2048]{1,0:T(8,128)(2,1)S(1)}, u32[]{:S(2)}, u32[]{:S(2)}) collective-permute-start(bf16[128,2048]{1,0:T(8,128)(2,1)S(1)} %collective-permute-done.32), channel_id=1, source_target_pairs={{0,1},{1,0},{2,3},{3,2},{4,5},{5,4},{6,7},{7,6},{8,9},{9,8},{10,11... | collective-permute-start | bytes 1572872 | tf_op jit(solution)/shard_map/ppermute | solution.py:121
  147.8 18.8 %collective-permute-start.29 = (bf16[128,2048]{1,0:T(8,128)(2,1)S(1)}, bf16[128,2048]{1,0:T(8,128)(2,1)S(1)}, u32[]{:S(2)}, u32[]{:S(2)}) collective-permute-start(bf16[128,2048]{1,0:T(8,128)(2,1)S(1)} %get-tuple-element.53), channel_id=1, source_target_pairs={{0,12},{12,0},{1,13},{13,1},{2,14},{14,2},{3,15},{15,3},{16,28},{2... | collective-permute-start | bytes 1572872 | tf_op jit(solution)/shard_map/ppermute | solution.py:685
  162.9 10.5 %collective-permute-start.43 = (bf16[64,2048]{1,0:T(8,128)(2,1)S(1)}, bf16[64,2048]{1,0:T(8,128)(2,1)}, u32[]{:S(2)}, u32[]{:S(2)}) collective-permute-start(bf16[64,2048]{1,0:T(8,128)(2,1)S(1)} %get-tuple-element.57), channel_id=1, source_target_pairs={{0,12},{4,8},{8,4},{12,0},{1,13},{5,9},{9,5},{13,1},{2,14},{6,10},... | collective-permute-start | bytes 786440 | tf_op jit(solution)/shard_map/ppermute | solution.py:121
  165.5 26.1 %collective-permute-start.46 = (bf16[128,2048]{1,0:T(8,128)(2,1)S(1)}, bf16[128,2048]{1,0:T(8,128)(2,1)S(1)}, u32[]{:S(2)}, u32[]{:S(2)}) collective-permute-start(bf16[128,2048]{1,0:T(8,128)(2,1)S(1)} %get-tuple-element.61.refs_0_), channel_id=1, source_target_pairs={{0,2},{2,0},{1,3},{3,1},{4,6},{6,4},{5,7},{7,5},{8,10},{10,8},{9,1... | collective-permute-start | bytes 1572872 | tf_op jit(solution)/shard_map/ppermute | solution.py:121
  177.8 15.9 %collective-permute-start.42 = (bf16[128,2048]{1,0:T(8,128)(2,1)S(1)}, bf16[128,2048]{1,0:T(8,128)(2,1)S(1)}, u32[]{:S(2)}, u32[]{:S(2)}) collective-permute-start(bf16[128,2048]{1,0:T(8,128)(2,1)S(1)} %broadcast_select_fusion.refs_2_), channel_id=1, source_target_pairs={{0,2},{2,0},{1,3},{3,1},{4,6},{6,4},{5,7},{7,5},{8,10},{10,8},{9,1... | collective-permute-start | bytes 1572872 | tf_op jit(solution)/shard_map/ppermute | solution.py:121
  192.1 11.5 %collective-permute-start.45 = (bf16[64,2048]{1,0:T(8,128)(2,1)}, bf16[64,2048]{1,0:T(8,128)(2,1)S(1)}, u32[]{:S(2)}, u32[]{:S(2)}) collective-permute-start(bf16[64,2048]{1,0:T(8,128)(2,1)} %collective-permute-done.44.refs_3_), channel_id=1, source_target_pairs={{0,2},{2,0},{1,3},{3,1},{4,6},{6,4},{5,7},{7,5},{8,10},{10,8},{9,1... | collective-permute-start | bytes 786440 | tf_op jit(solution)/shard_map/ppermute | solution.py:121
  (46 other events, 266.7 us)

commit v13 on v12

--- a/solution.py
+++ b/solution.py
@@ -11,7 +11,7 @@
 SMEM = pl.BlockSpec(memory_space=pltpu.SMEM)
 VMEM = pl.BlockSpec(memory_space=pltpu.VMEM)
 VMEM_LIMIT = 24 * 1024 * 1024
-OPERATE_LIMIT = 44 * 1024 * 1024
+OPERATE_LIMIT = 32 * 1024 * 1024
 PREPARE_LIMIT = 56 * 1024 * 1024
 LANES = 128
 
@@ -159,7 +159,7 @@
     else:
         hd_own, hd_far, psi_in, off_in, stats_in, near_out, far_out, late_out, stats_out = refs[:9]
         refs = refs[9:]
-    field, images, left, diag, sems = refs
+    field, images, left, diag, parts, sems = refs
     z, x, c = place()
     sectors, block, width = field.shape
     table = right.shape[1]
@@ -177,19 +177,20 @@
     for at in range(2):
         begin(left_own.at[pl.ds(rows[at] * links, links)], left.at[0, pl.ds(at * links, links)])
     begin(left_other.at[pl.ds(table // 2, 2 * links)], left.at[1])
-    if not first:
+    if first:
+        for at, mix in enumerate((mix_a, mix_b)):
+            begin(mix.at[pl.ds(0, parts.shape[1]), pl.ds(width, LANES)], parts.at[at])
+    else:
         begin(hd_own.at[x], diag.at[0])
         begin(hd_far, diag.at[1])
 
     def allowed(a, q, value):
         return lax.select(pattern[a, q] != 0, value, jnp.zeros_like(value))
 
-    for piece, offsets in zip(pieces, plan):
-        for at, (dz, dx, dc, start, tall) in enumerate(offsets):
-            row = row_of(dz, dx, dc)
-            for line in range(0, tall, 16):
-                value = piece[at, line : line + 16, :]
-                field[row, start + line : start + line + 16, :] = value
+    for piece, offset in zip(pieces, plan):
+        row = row_of(*offset)
+        for line in range(0, block, 16):
+            field[row, line : line + 16, :] = piece[line : line + 16, :]
 
     def right_col(term, b, j):
         return cols_other[j, b] if term else right_cols[j, 0, b]
@@ -281,7 +282,7 @@
 
     sums = list(lax.fori_loop(0, sectors // step, column, (zero,) * (2 if first else 3)))
     if first:
-        far_weight = sum(mix[0:48, width:].astype(jnp.float32) for mix in (mix_a, mix_b))
+        far_weight = (parts[0] + parts[1]).astype(jnp.float32)
         sums[1] += weight_own[...] + (far_weight[0:8] + far_weight[16:24] + far_weight[32:40])
     stats_out[...] = jnp.zeros_like(stats_out)
     for at, value in enumerate(sums):
@@ -292,7 +293,7 @@
 
 def operate(first, plan, pieces, cols, pattern, right, left, extra):
     _, table, block, _ = right.shape
-    width = pieces[0].shape[2]
+    width = pieces[0].shape[1]
     sectors = width // block
     links = table // sectors
     rows = jax.ShapeDtypeStruct((2, block, width), jnp.bfloat16)
@@ -300,7 +301,7 @@
     some = jax.ShapeDtypeStruct((block // 2, width), jnp.bfloat16)
     stats = jax.ShapeDtypeStruct((8, LANES), jnp.float32)
     out_shape = (rows, rows, stats) if first else (one, some, some, stats)
-    extra_specs = [VMEM] * 3 if first else [ANY, ANY, VMEM, VMEM, VMEM]
+    extra_specs = [ANY, ANY, VMEM] if first else [ANY, ANY, VMEM, VMEM, VMEM]
     inner = 2 * 2 * sectors * 2 * links * links * block * block * block
     outer = 2 * 2 * 2 * links * block * block * width
     return pl.pallas_call(
@@ -313,6 +314,7 @@
             pltpu.VMEM((2, 2 * links * block, width), jnp.bfloat16),
             pltpu.VMEM((2, 2 * links, block, block), jnp.bfloat16),
             pltpu.VMEM((2, block, width), jnp.bfloat16),
+            pltpu.VMEM((2, 48, LANES), jnp.bfloat16),
             pltpu.SemaphoreType.DMA((5,)),
         ],
         compiler_params=pltpu.CompilerParams(vmem_limit_bytes=OPERATE_LIMIT),
@@ -610,7 +612,7 @@
     hd_far = lax.dynamic_index_in_dim(diag, x, 0, keepdims=False)
     hd_far = across(after(hd_far, far_z), "blk", 3)
     far_zx_core = across(far_zx, "sub", 1)
-    near_b_core = across(near_b, "sub", 1)
+    near_b_core = across(after(near_b, turned), "sub", 1)
 
     left = (left, operators)
     pieces = []
@@ -633,8 +635,8 @@
         (far_zx, (3, 1, 0)),
         (far_zx_core, (3, 1, 1)),
     ):
-        pieces.append(piece[None])
-        plan.append((offset + (0, block),))
+        pieces.append(piece)
+        plan.append(offset)
     psi, off_one, stats_one = operate(
         True, tuple(plan), pieces, cols, pattern, turned, left, (mix_a, mix_b, weight_own)
     )
@@ -702,8 +704,8 @@
         (near_zx_core, (1, 1, 1)),
         (far_xz_core, (2, 1, 1)),
     ):
-        pieces.append(piece[None])
-        plan.append((offset + (0, block),))
+        pieces.append(piece)
+        plan.append(offset)
     two_near, two_far, two_late, stats_three = operate(
         False, tuple(plan), pieces, cols, pattern, turned, left, (diag, hd_far, psi, off_one, stats_one)
     )
@@ -711,14 +713,13 @@
     far_in = across(two_far, "blk", 3)
     near_in = across(two_near, "ops", 1)
     late_in = across(after(two_late, far_in), "blk", 3)
-    far_in_x = across(after(far_in, near_in), "ops", 1)
+    far_in_x = across(far_in, "ops", 1)
+    other = jnp.where(middle, other_middle, after(other_end, two_near))
+    other_x = across(other, "ops", 1)
     sums = stats_three + across(stats_three, "sub", 1)
-    other = jnp.where(middle, other_middle, after(other_end, sums))
-    other_x = across(other, "ops", 1)
-    sums = after(sums, far_in)
+    sums = sums + across(sums, "ops", 1)
+    sums = after(sums, late_in)
     both = jnp.stack([sums + across(sums, "blk", 1), across(sums, "blk", 2) + across(sums, "blk", 3)])
-    both = after(both, late_in)
-    both = both + across(both, "ops", 1)
     other, other_x = after((other, other_x), late_in)
     late_in_x = across(late_in, "ops", 1)
     both = jnp.sum(jnp.where(half == 0, both, both[::-1])[:, :5], axis=2)

time: 207 us -> 227 us (1.097)
  waiting for transfers between devices: 99.7 us -> 117 us
  local copies, waits for them, and re-layouts: 10.5 us -> 19.9 us
  starting transfers between devices: 50.6 us -> 47.5 us
  Pallas kernels: 39.3 us -> 36.6 us
    ppermute x42, waiting for transfers between devices: 72.5 us -> 89.8 us  [across(): return lax.ppermute(value, axis, [(i, i ^ distance) for i in range(size)])]
    unnamed x52 -> x62, local copies, waits for them, and re-layouts: 10.3 us -> 18.7 us
    ppermute x42, starting transfers between devices: 35.6 us -> 32.4 us  [across(): return lax.ppermute(value, axis, [(i, i ^ distance) for i in range(size)])]
  transfers between devices with their start and end apart: 52 -> 52, of which waited for: 25 -> 24; matrix products, arithmetic and copies ran while one was open for 2% -> 2% of each run, Pallas kernels for 15% -> 13%
where the time goes in v13:
time: 227 us; the launch traced here: 226 us
  waiting for transfers between devices  117 us (52%)
  starting transfers between devices  47.5 us (21%)
  Pallas kernels  36.6 us (16%)
  local copies, waits for them, and re-layouts  19.9 us (9%)
  other arithmetic  3.86 us (2%)
    ppermute x42, waiting for transfers between devices, across(): return lax.ppermute(value, axis, [(i, i ^ distance) for i in range(size)])  89.8 us
    ppermute x42, starting transfers between devices, across(): return lax.ppermute(value, axis, [(i, i ^ distance) for i in range(size)])  32.4 us
    pallas_call x2, Pallas kernels, operate(): pl.pallas_call(functools.partial(operate_kernel, first, plan), out_shape=...  23.5 us
    unnamed x62, local copies, waits for them, and re-layouts  18.7 us
    ppermute x1, waiting for transfers between devices, shards(): mix_b = lax.ppermute(mix_b, 'blk', [(0, 1), (1, 3), (3, 2), (2, 0)])  12.5 us
    ppermute x1, waiting for transfers between devices, shards(): mix_a = lax.ppermute(mix_a, 'blk', [(0, 2), (2, 3), (3, 1), (1, 0)])  7.81 us
    ppermute x6, starting transfers between devices, share(): lax.ppermute(pair, axes, [(i, i ^ distance) for i in range(count)])  6.98 us
    ppermute x6, waiting for transfers between devices, share(): lax.ppermute(pair, axes, [(i, i ^ distance) for i in range(count)])  6.17 us
  transfers between devices with their start and end apart: 52, of which 24 were waited for; matrix products, arithmetic and copies ran while one was open for 2% of the time, Pallas kernels for 13%

profile of v13, /device:TPU:0, one launch (start us, length us, event | category | flops | bytes accessed | tf_op | source)
XLA Modules:
  0.0 225.9 jit_solution(5146493280491348905)
XLA Ops:
  0.6 4.2 %prepare.1 = (bf16[128,2176]{1,0:T(8,128)(2,1)}, bf16[128,2176]{1,0:T(8,128)(2,1)}, bf16[31,128,128]{2,1,0:T(8,128)(2,1)}, f32[8,128]{1,0:T(8,128)}) custom-call(s32[16,16]{1,0:T(8,128)} %pattern.5, bf16[2,2,128,2048]{3,2,1,0:T(8,128)(2,1)} %bitcast.60, bf16[2,128,2048]{2,1,0:T(8,128)(2,1)} %bitcast.45, bf16[48,128,128]{2,1,0:T(8,128)(2,1)} %bitcast.49, ...), custom_call_target="tpu_custom_call" | custom-call | tf_op jit(solution)/shard_map/prepare/pallas_call | solution.py:437
  4.9 4.1 %collective-permute-start.1 = (bf16[128,2176]{1,0:T(8,128)(2,1)}, bf16[128,2176]{1,0:T(8,128)(2,1)S(1)}, u32[]{:S(2)}, u32[]{:S(2)}) collective-permute-start(bf16[128,2176]{1,0:T(8,128)(2,1)} %get-tuple-element.34), channel_id=1, source_target_pairs={{0,8},{8,12},{12,4},{4,0},{1,9},{9,13},{13,5},{5,1},{2,10},{10,14}... | collective-permute-start | bytes 1671176 | tf_op jit(solution)/shard_map/ppermute | solution.py:582
  9.1 2.1 bitcast_multiply_fusion
  11.6 1.5 collective-permute-start
  14.5 7.8 %collective-permute-done.1.refs_16_ = bf16[128,2176]{1,0:T(8,128)(2,1)S(1)} collective-permute-done((bf16[128,2176]{1,0:T(8,128)(2,1)}, bf16[128,2176]{1,0:T(8,128)(2,1)S(1)}, u32[]{:S(2)}, u32[]{:S(2)}) %collective-permute-start.1) | collective-permute-done | bytes 557088 | tf_op jit(solution)/shard_map/ppermute | solution.py:582
  22.3 12.5 %collective-permute-done.2.refs_17_ = bf16[128,2176]{1,0:T(8,128)(2,1)S(1)} collective-permute-done((bf16[128,2176]{1,0:T(8,128)(2,1)}, bf16[128,2176]{1,0:T(8,128)(2,1)S(1)}, u32[]{:S(2)}, u32[]{:S(2)}) %collective-permute-start.2) | collective-permute-done | bytes 557088 | tf_op jit(solution)/shard_map/ppermute | solution.py:583
  37.1 11.8 %collective-permute-done.5.refs_12_ = bf16[128,2048]{1,0:T(8,128)(2,1)} collective-permute-done((bf16[128,2048]{1,0:T(8,128)(2,1)S(1)}, bf16[128,2048]{1,0:T(8,128)(2,1)}, u32[]{:S(2)}, u32[]{:S(2)}) %collective-permute-start.5) | collective-permute-done | bytes 524320 | tf_op jit(solution)/shard_map/ppermute | solution.py:121
  49.9 1.5 collective-permute-start.11
  54.7 10.0 %collective-permute-done.11.refs_10_ = bf16[128,2048]{1,0:T(8,128)(2,1)} collective-permute-done((bf16[128,2048]{1,0:T(8,128)(2,1)S(1)}, bf16[128,2048]{1,0:T(8,128)(2,1)}, u32[]{:S(2)}, u32[]{:S(2)}) %collective-permute-start.11) | collective-permute-done | bytes 524320 | tf_op jit(solution)/shard_map/ppermute | solution.py:121
  64.7 10.8 %collective-permute-done.14.refs_14_ = bf16[128,2048]{1,0:T(8,128)(2,1)} collective-permute-done((bf16[128,2048]{1,0:T(8,128)(2,1)}, bf16[128,2048]{1,0:T(8,128)(2,1)}, u32[]{:S(2)}, u32[]{:S(2)}) %collective-permute-start.14) | collective-permute-done | bytes 524320 | tf_op jit(solution)/shard_map/ppermute | solution.py:121
  78.2 1.7 arrange.1.right
  81.6 2.5 %collective-permute-start.16 = (bf16[128,2048]{1,0:T(8,128)(2,1)S(1)}, bf16[128,2048]{1,0:T(8,128)(2,1)S(1)}, u32[]{:S(2)}, u32[]{:S(2)}) collective-permute-start(bf16[128,2048]{1,0:T(8,128)(2,1)S(1)} %dynamic-slice_bitcast_fusion), channel_id=1, source_target_pairs={{0,12},{4,8},{8,4},{12,0},{1,13},{5,9},{9,5},{13,1},{2,14},{6,10},... | collective-permute-start | bytes 1572872 | tf_op jit(solution)/shard_map/ppermute | solution.py:121
  95.9 12.0 %operate_first.1 = (bf16[2,128,2048]{2,1,0:T(8,128)(2,1)S(1)}, bf16[2,128,2048]{2,1,0:T(8,128)(2,1)S(1)}, f32[8,128]{1,0:T(8,128)S(1)}) custom-call(s32[3,1,16]{2,1,0:T(1,128)S(1)} %bitcast.53, s32[3,1,16]{2,1,0:T(1,128)S(1)} %bitcast.56, s32[16,16]{1,0:T(8,128)S(1)} %bitcast_convert_fusion.cols_other, s32[16,16]{1,0:T(8,128)S(1)} %copy-done.27, ...), custom_call_target="tpu_custom_call" | custom-call | flops 3221225472 | bytes 16777216 | tf_op jit(solution)/shard_map/operate_first/pallas_call | solution.py:307
  110.6 2.0 collective-permute-start.20
  115.1 2.1 update.1
  119.2 1.9 collective-permute-start.23
  122.8 2.8 %collective-permute-done.24.refs_3_ = f32[2,8,128]{2,1,0:T(8,128)S(1)} collective-permute-done((f32[2,8,128]{2,1,0:T(8,128)S(1)}, f32[2,8,128]{2,1,0:T(8,128)S(1)}, u32[]{:S(2)}, u32[]{:S(2)}) %collective-permute-start.24) | collective-permute-done | bytes 8224 | tf_op jit(solution)/shard_map/ppermute | solution.py:130
  129.2 9.5 %collective-permute-done.25.refs_4_ = bf16[128,2048]{1,0:T(8,128)(2,1)S(1)} collective-permute-done((bf16[128,2048]{1,0:T(8,128)(2,1)S(1)}, bf16[128,2048]{1,0:T(8,128)(2,1)S(1)}, u32[]{:S(2)}, u32[]{:S(2)}) %collective-permute-start.25) | collective-permute-done | bytes 524320 | tf_op jit(solution)/shard_map/ppermute | solution.py:121
  138.8 4.7 %collective-permute-start.32 = (bf16[128,2048]{1,0:T(8,128)(2,1)S(1)}, bf16[128,2048]{1,0:T(8,128)(2,1)S(1)}, u32[]{:S(2)}, u32[]{:S(2)}) collective-permute-start(bf16[128,2048]{1,0:T(8,128)(2,1)S(1)} %get-tuple-element.53.refs_1_), channel_id=1, source_target_pairs={{0,4},{4,0},{8,12},{12,8},{1,5},{5,1},{9,13},{13,9},{2,6},{6,2},{1... | collective-permute-start | bytes 1572872 | tf_op jit(solution)/shard_map/ppermute | solution.py:121
  145.6 10.7 %collective-permute-done.32.refs_5_ = bf16[128,2048]{1,0:T(8,128)(2,1)S(1)} collective-permute-done((bf16[128,2048]{1,0:T(8,128)(2,1)S(1)}, bf16[128,2048]{1,0:T(8,128)(2,1)S(1)}, u32[]{:S(2)}, u32[]{:S(2)}) %collective-permute-start.32) | collective-permute-done | bytes 524320 | tf_op jit(solution)/shard_map/ppermute | solution.py:121
  156.3 2.0 collective-permute-done.28.refs_8_.refs_1_
  158.3 6.9 %collective-permute-done.37.refs_12_ = bf16[128,2048]{1,0:T(8,128)(2,1)S(1)} collective-permute-done((bf16[128,2048]{1,0:T(8,128)(2,1)S(1)}, bf16[128,2048]{1,0:T(8,128)(2,1)S(1)}, u32[]{:S(2)}, u32[]{:S(2)}) %collective-permute-start.37) | collective-permute-done | bytes 524320 | tf_op jit(solution)/shard_map/ppermute | solution.py:121
  165.8 3.3 %collective-permute-start.29 = (bf16[128,2048]{1,0:T(8,128)(2,1)S(1)}, bf16[128,2048]{1,0:T(8,128)(2,1)S(1)}, u32[]{:S(2)}, u32[]{:S(2)}) collective-permute-start(bf16[128,2048]{1,0:T(8,128)(2,1)S(1)} %get-tuple-element.53.refs_1_), channel_id=1, source_target_pairs={{0,12},{12,0},{1,13},{13,1},{2,14},{14,2},{3,15},{15,3},{16,28},{2... | collective-permute-start | bytes 1572872 | tf_op jit(solution)/shard_map/ppermute | solution.py:687
  169.2 11.5 %operate_second.1 = (bf16[128,2048]{1,0:T(8,128)(2,1)}, bf16[64,2048]{1,0:T(8,128)(2,1)S(1)}, bf16[64,2048]{1,0:T(8,128)(2,1)S(1)}, f32[8,128]{1,0:T(8,128)S(1)}) custom-call(s32[3,1,16]{2,1,0:T(1,128)S(1)} %bitcast.54, s32[3,1,16]{2,1,0:T(1,128)S(1)} %bitcast.57, s32[16,16]{1,0:T(8,128)S(1)} %bitcast_convert_fusion.cols_other, s32[16,16]{1,0:T(8,128)S(1)} %copy-done.27, ...), custom_call_target="tpu_custom_call" | custom-call | bytes 1024 | tf_op jit(solution)/shard_map/operate_second/pallas_call | solution.py:307
  180.7 2.5 %collective-permute-start.42 = (bf16[64,2048]{1,0:T(8,128)(2,1)S(1)}, bf16[64,2048]{1,0:T(8,128)(2,1)S(1)}, u32[]{:S(2)}, u32[]{:S(2)}) collective-permute-start(bf16[64,2048]{1,0:T(8,128)(2,1)S(1)} %get-tuple-element.57), channel_id=1, source_target_pairs={{0,12},{4,8},{8,4},{12,0},{1,13},{5,9},{9,5},{13,1},{2,14},{6,10},... | collective-permute-start | bytes 786440 | tf_op jit(solution)/shard_map/ppermute | solution.py:121
  186.1 5.0 %collective-permute-done.42.refs_2_ = bf16[64,2048]{1,0:T(8,128)(2,1)S(1)} collective-permute-done((bf16[64,2048]{1,0:T(8,128)(2,1)S(1)}, bf16[64,2048]{1,0:T(8,128)(2,1)S(1)}, u32[]{:S(2)}, u32[]{:S(2)}) %collective-permute-start.42) | collective-permute-done | bytes 262176 | tf_op jit(solution)/shard_map/ppermute | solution.py:121
  191.1 2.4 %collective-permute-start.43 = (bf16[64,2048]{1,0:T(8,128)(2,1)S(1)}, bf16[64,2048]{1,0:T(8,128)(2,1)S(1)}, u32[]{:S(2)}, u32[]{:S(2)}) collective-permute-start(bf16[64,2048]{1,0:T(8,128)(2,1)S(1)} %get-tuple-element.58), channel_id=1, source_target_pairs={{0,12},{4,8},{8,4},{12,0},{1,13},{5,9},{9,5},{13,1},{2,14},{6,10},... | collective-permute-start | bytes 786440 | tf_op jit(solution)/shard_map/ppermute | solution.py:121
  195.2 1.5 collective-permute-start.48
  196.7 17.7 %collective-permute-done.48 = f32[8,128]{1,0:T(8,128)S(1)} collective-permute-done((f32[8,128]{1,0:T(8,128)S(1)}, f32[8,128]{1,0:T(8,128)S(1)}, u32[]{:S(2)}, u32[]{:S(2)}) %collective-permute-start.48) | collective-permute-done | bytes 4128 | tf_op jit(solution)/shard_map/ppermute | solution.py:121
  214.4 2.0 collective-permute-start.50
  216.4 2.4 %collective-permute-start.51 = (f32[8,128]{1,0:T(8,128)S(1)}, f32[8,128]{1,0:T(8,128)S(1)}, u32[]{:S(2)}, u32[]{:S(2)}) collective-permute-start(f32[8,128]{1,0:T(8,128)S(1)} %add.67), channel_id=1, source_target_pairs={{0,12},{4,8},{8,4},{12,0},{1,13},{5,9},{9,5},{13,1},{2,14},{6,10},... | collective-permute-start | bytes 12296 | tf_op jit(solution)/shard_map/ppermute | solution.py:121
  219.4 2.4 %assemble.4.refs_1_ = bf16[2,2,128,2048]{3,2,1,0:T(8,128)(2,1)} custom-call(bf16[128,2048]{1,0:T(8,128)(2,1)} %get-tuple-element.54.refs_0_, bf16[128,2048]{1,0:T(8,128)(2,1)S(1)} %collective-permute-done.45.refs_1_, bf16[64,2048]{1,0:T(8,128)(2,1)S(1)} %collective-permute-done.42.refs_2_, bf16[64,2048]{1,0:T(8,128)(2,1)S(1)} %collective-permute-done.43.refs_3_, ...), custom_call_target="tpu_custom_call" | custom-call | tf_op jit(solution)/shard_map/assemble/pallas_call | solution.py:550
  (162 shorter events, 48.7 us)
Async XLA Ops:
  4.9 17.5 %collective-permute-start.1 = (bf16[128,2176]{1,0:T(8,128)(2,1)}, bf16[128,2176]{1,0:T(8,128)(2,1)S(1)}, u32[]{:S(2)}, u32[]{:S(2)}) collective-permute-start(bf16[128,2176]{1,0:T(8,128)(2,1)} %get-tuple-element.34), channel_id=1, source_target_pairs={{0,8},{8,12},{12,4},{4,0},{1,9},{9,13},{13,5},{5,1},{2,10},{10,14}... | collective-permute-start | bytes 1671176 | tf_op jit(solution)/shard_map/ppermute | solution.py:582
  9.0 25.9 %collective-permute-start.2 = (bf16[128,2176]{1,0:T(8,128)(2,1)}, bf16[128,2176]{1,0:T(8,128)(2,1)S(1)}, u32[]{:S(2)}, u32[]{:S(2)}) collective-permute-start(bf16[128,2176]{1,0:T(8,128)(2,1)} %get-tuple-element.35), channel_id=1, source_target_pairs={{0,4},{4,12},{12,8},{8,0},{1,5},{5,13},{13,9},{9,1},{2,6},{6,14},{... | collective-permute-start | bytes 1671176 | tf_op jit(solution)/shard_map/ppermute | solution.py:583
  11.6 25.5 %collective-permute-start = (bf16[31,128,128]{2,1,0:T(8,128)(2,1)}, bf16[31,128,128]{2,1,0:T(8,128)(2,1)S(1)}, u32[]{:S(2)}, u32[]{:S(2)}) collective-permute-start(bf16[31,128,128]{2,1,0:T(8,128)(2,1)} %get-tuple-element.33), channel_id=1, source_target_pairs={{0,2},{2,0},{1,3},{3,1},{4,6},{6,4},{5,7},{7,5},{8,10},{10,8},{9,1... | collective-permute-start | bytes 3047432 | tf_op jit(solution)/shard_map/ppermute | solution.py:121
  34.9 14.0 %collective-permute-start.5 = (bf16[128,2048]{1,0:T(8,128)(2,1)S(1)}, bf16[128,2048]{1,0:T(8,128)(2,1)}, u32[]{:S(2)}, u32[]{:S(2)}) collective-permute-start(bf16[128,2048]{1,0:T(8,128)(2,1)S(1)} %get-tuple-element.66.refs_8_), channel_id=1, source_target_pairs={{0,4},{4,0},{8,12},{12,8},{1,5},{5,1},{9,13},{13,9},{2,6},{6,2},{1... | collective-permute-start | bytes 1572872 | tf_op jit(solution)/shard_map/ppermute | solution.py:121
  35.7 17.0 %collective-permute-start.7 = (bf16[128,2048]{1,0:T(8,128)(2,1)S(1)}, bf16[128,2048]{1,0:T(8,128)(2,1)S(1)}, u32[]{:S(2)}, u32[]{:S(2)}) collective-permute-start(bf16[128,2048]{1,0:T(8,128)(2,1)S(1)} %get-tuple-element.66.refs_8_), channel_id=1, source_target_pairs={{0,1},{1,0},{2,3},{3,2},{4,5},{5,4},{6,7},{7,6},{8,9},{9,8},{10,11... | collective-permute-start | bytes 1572872 | tf_op jit(solution)/shard_map/ppermute | solution.py:121
  35.7 17.8 %collective-permute-start.8 = (bf16[128,2048]{1,0:T(8,128)(2,1)S(1)}, bf16[128,2048]{1,0:T(8,128)(2,1)S(1)}, u32[]{:S(2)}, u32[]{:S(2)}) collective-permute-start(bf16[128,2048]{1,0:T(8,128)(2,1)S(1)} %get-tuple-element.65.refs_4_), channel_id=1, source_target_pairs={{0,1},{1,0},{2,3},{3,2},{4,5},{5,4},{6,7},{7,6},{8,9},{9,8},{10,11... | collective-permute-start | bytes 1572872 | tf_op jit(solution)/shard_map/ppermute | solution.py:121
  48.9 26.7 %collective-permute-start.6 = (bf16[31,128,128]{2,1,0:T(8,128)(2,1)S(1)}, bf16[31,128,128]{2,1,0:T(8,128)(2,1)S(1)}, u32[]{:S(2)}, u32[]{:S(2)}) collective-permute-start(bf16[31,128,128]{2,1,0:T(8,128)(2,1)S(1)} %collective-permute-done.near.left_other), channel_id=1, source_target_pairs={{0,1},{1,0},{2,3},{3,2},{4,5},{5,4},{6,7},{7,6},{8,9},{9,8},{10,11... | collective-permute-start | bytes 3047432 | tf_op jit(solution)/shard_map/ppermute | solution.py:121
  49.9 14.8 %collective-permute-start.11 = (bf16[128,2048]{1,0:T(8,128)(2,1)S(1)}, bf16[128,2048]{1,0:T(8,128)(2,1)}, u32[]{:S(2)}, u32[]{:S(2)}) collective-permute-start(bf16[128,2048]{1,0:T(8,128)(2,1)S(1)} %get-tuple-element.66.refs_8_), channel_id=1, source_target_pairs={{0,2},{2,0},{1,3},{3,1},{4,6},{6,4},{5,7},{7,5},{8,10},{10,8},{9,1... | collective-permute-start | bytes 1572872 | tf_op jit(solution)/shard_map/ppermute | solution.py:121
  52.2 23.4 %collective-permute-start.14 = (bf16[128,2048]{1,0:T(8,128)(2,1)}, bf16[128,2048]{1,0:T(8,128)(2,1)}, u32[]{:S(2)}, u32[]{:S(2)}) collective-permute-start(bf16[128,2048]{1,0:T(8,128)(2,1)} %collective-permute-done.5.refs_12_), channel_id=1, source_target_pairs={{0,2},{2,0},{1,3},{3,1},{4,6},{6,4},{5,7},{7,5},{8,10},{10,8},{9,1... | collective-permute-start | bytes 1572872 | tf_op jit(solution)/shard_map/ppermute | solution.py:121
  54.4 25.6 %collective-permute-start.9 = (bf16[128,2048]{1,0:T(8,128)(2,1)}, bf16[128,2048]{1,0:T(8,128)(2,1)}, u32[]{:S(2)}, u32[]{:S(2)}) collective-permute-start(bf16[128,2048]{1,0:T(8,128)(2,1)} %get-tuple-element.39.refs_1_), channel_id=1, source_target_pairs={{0,4},{4,0},{8,12},{12,8},{1,5},{5,1},{9,13},{13,9},{2,6},{6,2},{1... | collective-permute-start | bytes 1572872 | tf_op jit(solution)/shard_map/ppermute | solution.py:121
  54.7 30.2 %collective-permute-start.13 = (bf16[128,2048]{1,0:T(8,128)(2,1)}, bf16[128,2048]{1,0:T(8,128)(2,1)}, u32[]{:S(2)}, u32[]{:S(2)}) collective-permute-start(bf16[128,2048]{1,0:T(8,128)(2,1)} %collective-permute-done.5.refs_12_), channel_id=1, source_target_pairs={{0,1},{1,0},{2,3},{3,2},{4,5},{5,4},{6,7},{7,6},{8,9},{9,8},{10,11... | collective-permute-start | bytes 1572872 | tf_op jit(solution)/shard_map/ppermute | solution.py:121
  64.7 20.1 %collective-permute-start.12 = (bf16[128,2048]{1,0:T(8,128)(2,1)}, bf16[128,2048]{1,0:T(8,128)(2,1)}, u32[]{:S(2)}, u32[]{:S(2)}) collective-permute-start(bf16[128,2048]{1,0:T(8,128)(2,1)} %collective-permute-done.11.refs_10_), channel_id=1, source_target_pairs={{0,1},{1,0},{2,3},{3,2},{4,5},{5,4},{6,7},{7,6},{8,9},{9,8},{10,11... | collective-permute-start | bytes 1572872 | tf_op jit(solution)/shard_map/ppermute | solution.py:121
  81.6 31.0 %collective-permute-start.16 = (bf16[128,2048]{1,0:T(8,128)(2,1)S(1)}, bf16[128,2048]{1,0:T(8,128)(2,1)S(1)}, u32[]{:S(2)}, u32[]{:S(2)}) collective-permute-start(bf16[128,2048]{1,0:T(8,128)(2,1)S(1)} %dynamic-slice_bitcast_fusion), channel_id=1, source_target_pairs={{0,12},{4,8},{8,4},{12,0},{1,13},{5,9},{9,5},{13,1},{2,14},{6,10},... | collective-permute-start | bytes 1572872 | tf_op jit(solution)/shard_map/ppermute | solution.py:121
  126.3 12.4 %collective-permute-start.25 = (bf16[128,2048]{1,0:T(8,128)(2,1)S(1)}, bf16[128,2048]{1,0:T(8,128)(2,1)S(1)}, u32[]{:S(2)}, u32[]{:S(2)}) collective-permute-start(bf16[128,2048]{1,0:T(8,128)(2,1)S(1)} %get-tuple-element.52.refs_0_), channel_id=1, source_target_pairs={{0,4},{4,0},{8,12},{12,8},{1,5},{5,1},{9,13},{13,9},{2,6},{6,2},{1... | collective-permute-start | bytes 1572872 | tf_op jit(solution)/shard_map/ppermute | solution.py:121
  126.5 12.3 %collective-permute-start.26 = (bf16[128,2048]{1,0:T(8,128)(2,1)S(1)}, bf16[128,2048]{1,0:T(8,128)(2,1)S(1)}, u32[]{:S(2)}, u32[]{:S(2)}) collective-permute-start(bf16[128,2048]{1,0:T(8,128)(2,1)S(1)} %get-tuple-element.53.refs_1_), channel_id=1, source_target_pairs={{0,2},{2,0},{1,3},{3,1},{4,6},{6,4},{5,7},{7,5},{8,10},{10,8},{9,1... | collective-permute-start | bytes 1572872 | tf_op jit(solution)/shard_map/ppermute | solution.py:121
  127.9 10.8 %collective-permute-start.27 = (bf16[128,2048]{1,0:T(8,128)(2,1)S(1)}, bf16[128,2048]{1,0:T(8,128)(2,1)S(1)}, u32[]{:S(2)}, u32[]{:S(2)}) collective-permute-start(bf16[128,2048]{1,0:T(8,128)(2,1)S(1)} %get-tuple-element.53.refs_1_), channel_id=1, source_target_pairs={{4,8},{8,4},{5,9},{9,5},{6,10},{10,6},{7,11},{11,7},{20,24},{24,20... | collective-permute-start | bytes 1572872 | tf_op jit(solution)/shard_map/ppermute | solution.py:675
  128.6 16.9 %collective-permute-start.30 = (bf16[128,2048]{1,0:T(8,128)(2,1)S(1)}, bf16[128,2048]{1,0:T(8,128)(2,1)S(1)}, u32[]{:S(2)}, u32[]{:S(2)}) collective-permute-start(bf16[128,2048]{1,0:T(8,128)(2,1)S(1)} %get-tuple-element.52.refs_0_), channel_id=1, source_target_pairs={{0,1},{1,0},{2,3},{3,2},{4,5},{5,4},{6,7},{7,6},{8,9},{9,8},{10,11... | collective-permute-start | bytes 1572872 | tf_op jit(solution)/shard_map/ppermute | solution.py:121
  128.7 16.8 %collective-permute-start.31 = (bf16[128,2048]{1,0:T(8,128)(2,1)S(1)}, bf16[128,2048]{1,0:T(8,128)(2,1)S(1)}, u32[]{:S(2)}, u32[]{:S(2)}) collective-permute-start(bf16[128,2048]{1,0:T(8,128)(2,1)S(1)} %get-tuple-element.53.refs_1_), channel_id=1, source_target_pairs={{0,1},{1,0},{2,3},{3,2},{4,5},{5,4},{6,7},{7,6},{8,9},{9,8},{10,11... | collective-permute-start | bytes 1572872 | tf_op jit(solution)/shard_map/ppermute | solution.py:121
  138.8 17.6 %collective-permute-start.32 = (bf16[128,2048]{1,0:T(8,128)(2,1)S(1)}, bf16[128,2048]{1,0:T(8,128)(2,1)S(1)}, u32[]{:S(2)}, u32[]{:S(2)}) collective-permute-start(bf16[128,2048]{1,0:T(8,128)(2,1)S(1)} %get-tuple-element.53.refs_1_), channel_id=1, source_target_pairs={{0,4},{4,0},{8,12},{12,8},{1,5},{5,1},{9,13},{13,9},{2,6},{6,2},{1... | collective-permute-start | bytes 1572872 | tf_op jit(solution)/shard_map/ppermute | solution.py:121
  143.5 14.9 %collective-permute-start.28 = (bf16[128,2048]{1,0:T(8,128)(2,1)S(1)}, bf16[128,2048]{1,0:T(8,128)(2,1)S(1)}, u32[]{:S(2)}, u32[]{:S(2)}) collective-permute-start(bf16[128,2048]{1,0:T(8,128)(2,1)S(1)} %get-tuple-element.52.refs_0_), channel_id=1, source_target_pairs={{0,2},{2,0},{1,3},{3,1},{4,6},{6,4},{5,7},{7,5},{8,10},{10,8},{9,1... | collective-permute-start | bytes 1572872 | tf_op jit(solution)/shard_map/ppermute | solution.py:121
  144.0 21.2 %collective-permute-start.37 = (bf16[128,2048]{1,0:T(8,128)(2,1)S(1)}, bf16[128,2048]{1,0:T(8,128)(2,1)S(1)}, u32[]{:S(2)}, u32[]{:S(2)}) collective-permute-start(bf16[128,2048]{1,0:T(8,128)(2,1)S(1)} %collective-permute-done.25.refs_4_), channel_id=1, source_target_pairs={{0,2},{2,0},{1,3},{3,1},{4,6},{6,4},{5,7},{7,5},{8,10},{10,8},{9,1... | collective-permute-start | bytes 1572872 | tf_op jit(solution)/shard_map/ppermute | solution.py:121
  145.5 19.7 %collective-permute-start.38 = (bf16[128,2048]{1,0:T(8,128)(2,1)S(1)}, bf16[128,2048]{1,0:T(8,128)(2,1)S(1)}, u32[]{:S(2)}, u32[]{:S(2)}) collective-permute-start(bf16[128,2048]{1,0:T(8,128)(2,1)S(1)} %collective-permute-done.26.refs_9_), channel_id=1, source_target_pairs={{0,4},{4,0},{8,12},{12,8},{1,5},{5,1},{9,13},{13,9},{2,6},{6,2},{1... | collective-permute-start | bytes 1572872 | tf_op jit(solution)/shard_map/ppermute | solution.py:121
  145.5 20.2 %collective-permute-start.33 = (bf16[128,2048]{1,0:T(8,128)(2,1)S(1)}, bf16[128,2048]{1,0:T(8,128)(2,1)S(1)}, u32[]{:S(2)}, u32[]{:S(2)}) collective-permute-start(bf16[128,2048]{1,0:T(8,128)(2,1)S(1)} %collective-permute-done.25.refs_4_), channel_id=1, source_target_pairs={{0,1},{1,0},{2,3},{3,2},{4,5},{5,4},{6,7},{7,6},{8,9},{9,8},{10,11... | collective-permute-start | bytes 1572872 | tf_op jit(solution)/shard_map/ppermute | solution.py:121
  156.3 9.5 %collective-permute-start.36 = (bf16[128,2048]{1,0:T(8,128)(2,1)S(1)}, bf16[128,2048]{1,0:T(8,128)(2,1)S(1)}, u32[]{:S(2)}, u32[]{:S(2)}) collective-permute-start(bf16[128,2048]{1,0:T(8,128)(2,1)S(1)} %collective-permute-done.26.refs_9_), channel_id=1, source_target_pairs={{0,1},{1,0},{2,3},{3,2},{4,5},{5,4},{6,7},{7,6},{8,9},{9,8},{10,11... | collective-permute-start | bytes 1572872 | tf_op jit(solution)/shard_map/ppermute | solution.py:121
  158.3 10.8 %collective-permute-start.34 = (bf16[128,2048]{1,0:T(8,128)(2,1)S(1)}, bf16[128,2048]{1,0:T(8,128)(2,1)S(1)}, u32[]{:S(2)}, u32[]{:S(2)}) collective-permute-start(bf16[128,2048]{1,0:T(8,128)(2,1)S(1)} %collective-permute-done.32.refs_5_), channel_id=1, source_target_pairs={{0,1},{1,0},{2,3},{3,2},{4,5},{5,4},{6,7},{7,6},{8,9},{9,8},{10,11... | collective-permute-start | bytes 1572872 | tf_op jit(solution)/shard_map/ppermute | solution.py:121
  165.8 18.1 %collective-permute-start.29 = (bf16[128,2048]{1,0:T(8,128)(2,1)S(1)}, bf16[128,2048]{1,0:T(8,128)(2,1)S(1)}, u32[]{:S(2)}, u32[]{:S(2)}) collective-permute-start(bf16[128,2048]{1,0:T(8,128)(2,1)S(1)} %get-tuple-element.53.refs_1_), channel_id=1, source_target_pairs={{0,12},{12,0},{1,13},{13,1},{2,14},{14,2},{3,15},{15,3},{16,28},{2... | collective-permute-start | bytes 1572872 | tf_op jit(solution)/shard_map/ppermute | solution.py:687
  180.7 10.4 %collective-permute-start.42 = (bf16[64,2048]{1,0:T(8,128)(2,1)S(1)}, bf16[64,2048]{1,0:T(8,128)(2,1)S(1)}, u32[]{:S(2)}, u32[]{:S(2)}) collective-permute-start(bf16[64,2048]{1,0:T(8,128)(2,1)S(1)} %get-tuple-element.57), channel_id=1, source_target_pairs={{0,12},{4,8},{8,4},{12,0},{1,13},{5,9},{9,5},{13,1},{2,14},{6,10},... | collective-permute-start | bytes 786440 | tf_op jit(solution)/shard_map/ppermute | solution.py:121
  184.0 32.4 %collective-permute-start.41 = (bf16[128,2048]{1,0:T(8,128)(2,1)S(1)}, bf16[128,2048]{1,0:T(8,128)(2,1)S(1)}, u32[]{:S(2)}, u32[]{:S(2)}) collective-permute-start(bf16[128,2048]{1,0:T(8,128)(2,1)S(1)} %broadcast_select_fusion.refs_2_), channel_id=1, source_target_pairs={{0,2},{2,0},{1,3},{3,1},{4,6},{6,4},{5,7},{7,5},{8,10},{10,8},{9,1... | collective-permute-start | bytes 1572872 | tf_op jit(solution)/shard_map/ppermute | solution.py:121
  184.6 34.2 %collective-permute-start.45 = (bf16[128,2048]{1,0:T(8,128)(2,1)}, bf16[128,2048]{1,0:T(8,128)(2,1)S(1)}, u32[]{:S(2)}, u32[]{:S(2)}) collective-permute-start(bf16[128,2048]{1,0:T(8,128)(2,1)} %get-tuple-element.54.refs_0_), channel_id=1, source_target_pairs={{0,2},{2,0},{1,3},{3,1},{4,6},{6,4},{5,7},{7,5},{8,10},{10,8},{9,1... | collective-permute-start | bytes 1572872 | tf_op jit(solution)/shard_map/ppermute | solution.py:121
  191.1 23.4 %collective-permute-start.43 = (bf16[64,2048]{1,0:T(8,128)(2,1)S(1)}, bf16[64,2048]{1,0:T(8,128)(2,1)S(1)}, u32[]{:S(2)}, u32[]{:S(2)}) collective-permute-start(bf16[64,2048]{1,0:T(8,128)(2,1)S(1)} %get-tuple-element.58), channel_id=1, source_target_pairs={{0,12},{4,8},{8,4},{12,0},{1,13},{5,9},{9,5},{13,1},{2,14},{6,10},... | collective-permute-start | bytes 786440 | tf_op jit(solution)/shard_map/ppermute | solution.py:121
  193.5 25.9 %collective-permute-start.46 = (bf16[64,2048]{1,0:T(8,128)(2,1)S(1)}, bf16[64,2048]{1,0:T(8,128)(2,1)}, u32[]{:S(2)}, u32[]{:S(2)}) collective-permute-start(bf16[64,2048]{1,0:T(8,128)(2,1)S(1)} %collective-permute-done.42.refs_2_), channel_id=1, source_target_pairs={{0,2},{2,0},{1,3},{3,1},{4,6},{6,4},{5,7},{7,5},{8,10},{10,8},{9,1... | collective-permute-start | bytes 786440 | tf_op jit(solution)/shard_map/ppermute | solution.py:121
  195.2 19.2 %collective-permute-start.48 = (f32[8,128]{1,0:T(8,128)S(1)}, f32[8,128]{1,0:T(8,128)S(1)}, u32[]{:S(2)}, u32[]{:S(2)}) collective-permute-start(f32[8,128]{1,0:T(8,128)S(1)} %add.66), channel_id=1, source_target_pairs={{0,2},{2,0},{1,3},{3,1},{4,6},{6,4},{5,7},{7,5},{8,10},{10,8},{9,1... | collective-permute-start | bytes 12296 | tf_op jit(solution)/shard_map/ppermute | solution.py:121
  (51 other events, 647.6 us)

commit v14 on v12

--- a/solution.py
+++ b/solution.py
@@ -589,6 +589,7 @@
         masked(row_of(0, 2 + at, 0), lax.dynamic_slice(halves, (half, at, 0, 0), (1, 1, block, width))[0, 0])
         for at in range(2)
     ]
+    own = list(lax.optimization_barrier(tuple(own)))
     own_core = [across(value, "sub", 1) for value in own]
 
     mix_a, mix_b = after((mix_a, mix_b), *own_core)
@@ -599,11 +600,11 @@
     far_core = across(far, "sub", 1)
     near_a_core = across(near_a, "sub", 1)
 
-    near_b = across(after(own[1], far_z, far_core, near_a_core), "blk", 1)
-    far_zx = across(far_z, "ops", 1)
-    operators = after(operators, far_z)
+    operators = after(operators, mix_b)
     operators_core = across(operators, "sub", 1)
     turned = arrange(right, operators, operators_core)
+    near_b = across(after(own[1], far_z, far_core, near_a_core, turned), "blk", 1)
+    far_zx = across(far_z, "ops", 1)
     cols = (*cols, operators[-1, :16, :sectors].astype(jnp.int32))
     far_x_core = across(far_x, "sub", 1)
     far_z_core = across(far_z, "sub", 1)
@@ -711,13 +712,12 @@
     far_in = across(two_far, "blk", 3)
     near_in = across(two_near, "ops", 1)
     late_in = across(after(two_late, far_in), "blk", 3)
-    far_in_x = across(after(far_in, near_in), "ops", 1)
+    far_in_x = across(far_in, "ops", 1)
+    other = jnp.where(middle, other_middle, after(other_end, two_near))
+    other_x = across(other, "ops", 1)
     sums = stats_three + across(stats_three, "sub", 1)
-    other = jnp.where(middle, other_middle, after(other_end, sums))
-    other_x = across(other, "ops", 1)
-    sums = after(sums, far_in)
+    sums = after(sums, late_in)
     both = jnp.stack([sums + across(sums, "blk", 1), across(sums, "blk", 2) + across(sums, "blk", 3)])
-    both = after(both, late_in)
     both = both + across(both, "ops", 1)
     other, other_x = after((other, other_x), late_in)
     late_in_x = across(late_in, "ops", 1)

time: 207 us -> 222 us (1.072)
  waiting for transfers between devices: 99.7 us -> 111 us
  local copies, waits for them, and re-layouts: 10.5 us -> 14.5 us
  starting transfers between devices: 50.6 us -> 53.5 us
    ppermute x42, waiting for transfers between devices: 72.5 us -> 85.2 us  [across(): return lax.ppermute(value, axis, [(i, i ^ distance) for i in range(size)])]
    unnamed x52 -> x50, local copies, waits for them, and re-layouts: 10.3 us -> 14.3 us
  transfers between devices with their start and end apart: 52 -> 52, of which waited for: 25 -> 26; matrix products, arithmetic and copies ran while one was open for 2% -> 1% of each run, Pallas kernels for 15% -> 14%
where the time goes in v14:
time: 222 us; the launch traced here: 221 us
  waiting for transfers between devices  111 us (50%)
  starting transfers between devices  53.5 us (24%)
  Pallas kernels  38.3 us (17%)
  local copies, waits for them, and re-layouts  14.5 us (7%)
  other arithmetic  2.39 us (1%)
    ppermute x42, waiting for transfers between devices, across(): return lax.ppermute(value, axis, [(i, i ^ distance) for i in range(size)])  85.2 us
    ppermute x42, starting transfers between devices, across(): return lax.ppermute(value, axis, [(i, i ^ distance) for i in range(size)])  37.8 us
    pallas_call x2, Pallas kernels, operate(): pl.pallas_call(functools.partial(operate_kernel, first, plan), out_shape=...  25.2 us
    unnamed x50, local copies, waits for them, and re-layouts  14.3 us
    ppermute x1, waiting for transfers between devices, shards(): mix_b = lax.ppermute(mix_b, 'blk', [(0, 1), (1, 3), (3, 2), (2, 0)])  12.4 us
    ppermute x1, waiting for transfers between devices, shards(): mix_a = lax.ppermute(mix_a, 'blk', [(0, 2), (2, 3), (3, 1), (1, 0)])  7.66 us
    ppermute x6, starting transfers between devices, share(): lax.ppermute(pair, axes, [(i, i ^ distance) for i in range(count)])  6.98 us
    ppermute x6, waiting for transfers between devices, share(): lax.ppermute(pair, axes, [(i, i ^ distance) for i in range(count)])  6.17 us
  transfers between devices with their start and end apart: 52, of which 26 were waited for; matrix products, arithmetic and copies ran while one was open for 1% of the time, Pallas kernels for 14%

profile of v14, /device:TPU:0, one launch (start us, length us, event | category | flops | bytes accessed | tf_op | source)
XLA Modules:
  0.0 221.2 jit_solution(15076749167430667338)
XLA Ops:
  0.6 4.2 %prepare.1 = (bf16[128,2176]{1,0:T(8,128)(2,1)}, bf16[128,2176]{1,0:T(8,128)(2,1)}, bf16[31,128,128]{2,1,0:T(8,128)(2,1)}, f32[8,128]{1,0:T(8,128)}) custom-call(s32[16,16]{1,0:T(8,128)} %pattern.5, bf16[2,2,128,2048]{3,2,1,0:T(8,128)(2,1)} %bitcast.114, bf16[2,128,2048]{2,1,0:T(8,128)(2,1)} %bitcast.74, bf16[48,128,128]{2,1,0:T(8,128)(2,1)} %bitcast.78, ...), custom_call_target="tpu_custom_call" | custom-call | tf_op jit(solution)/shard_map/prepare/pallas_call | solution.py:435
  4.9 4.1 %collective-permute-start.1 = (bf16[128,2176]{1,0:T(8,128)(2,1)}, bf16[128,2176]{1,0:T(8,128)(2,1)S(1)}, u32[]{:S(2)}, u32[]{:S(2)}) collective-permute-start(bf16[128,2176]{1,0:T(8,128)(2,1)} %get-tuple-element.35), channel_id=1, source_target_pairs={{0,8},{8,12},{12,4},{4,0},{1,9},{9,13},{13,5},{5,1},{2,10},{10,14}... | collective-permute-start | bytes 1671176 | tf_op jit(solution)/shard_map/ppermute | solution.py:580
  14.7 7.7 %collective-permute-done.1.refs_16_ = bf16[128,2176]{1,0:T(8,128)(2,1)S(1)} collective-permute-done((bf16[128,2176]{1,0:T(8,128)(2,1)}, bf16[128,2176]{1,0:T(8,128)(2,1)S(1)}, u32[]{:S(2)}, u32[]{:S(2)}) %collective-permute-start.1) | collective-permute-done | bytes 557088 | tf_op jit(solution)/shard_map/ppermute | solution.py:580
  22.4 12.4 %collective-permute-done.2.refs_17_ = bf16[128,2176]{1,0:T(8,128)(2,1)S(1)} collective-permute-done((bf16[128,2176]{1,0:T(8,128)(2,1)}, bf16[128,2176]{1,0:T(8,128)(2,1)S(1)}, u32[]{:S(2)}, u32[]{:S(2)}) %collective-permute-start.2) | collective-permute-done | bytes 557088 | tf_op jit(solution)/shard_map/ppermute | solution.py:581
  37.8 11.6 %collective-permute-done.6 = bf16[128,2048]{1,0:T(8,128)(2,1)} collective-permute-done((bf16[128,2048]{1,0:T(8,128)(2,1)S(1)}, bf16[128,2048]{1,0:T(8,128)(2,1)}, u32[]{:S(2)}, u32[]{:S(2)}) %collective-permute-start.6) | collective-permute-done | bytes 524320 | tf_op jit(solution)/shard_map/ppermute | solution.py:121
  52.3 1.7 arrange.1.right
  54.1 1.6 copy-done
  58.6 4.7 %collective-permute-done.14 = bf16[128,2048]{1,0:T(8,128)(2,1)} collective-permute-done((bf16[128,2048]{1,0:T(8,128)(2,1)}, bf16[128,2048]{1,0:T(8,128)(2,1)}, u32[]{:S(2)}, u32[]{:S(2)}) %collective-permute-start.14) | collective-permute-done | bytes 524320 | tf_op jit(solution)/shard_map/ppermute | solution.py:121
  63.3 7.4 %collective-permute-done.9 = bf16[128,2048]{1,0:T(8,128)(2,1)} collective-permute-done((bf16[128,2048]{1,0:T(8,128)(2,1)S(1)}, bf16[128,2048]{1,0:T(8,128)(2,1)}, u32[]{:S(2)}, u32[]{:S(2)}) %collective-permute-start.9) | collective-permute-done | bytes 524320 | tf_op jit(solution)/shard_map/ppermute | solution.py:121
  70.7 2.6 %collective-permute-start.16 = (bf16[128,2048]{1,0:T(8,128)(2,1)S(1)}, bf16[128,2048]{1,0:T(8,128)(2,1)S(1)}, u32[]{:S(2)}, u32[]{:S(2)}) collective-permute-start(bf16[128,2048]{1,0:T(8,128)(2,1)S(1)} %dynamic-slice_bitcast_fusion), channel_id=1, source_target_pairs={{0,12},{4,8},{8,4},{12,0},{1,13},{5,9},{9,5},{13,1},{2,14},{6,10},... | collective-permute-start | bytes 1572872 | tf_op jit(solution)/shard_map/ppermute | solution.py:121
  79.6 13.4 %operate_first.1 = (bf16[2,128,2048]{2,1,0:T(8,128)(2,1)}, bf16[2,128,2048]{2,1,0:T(8,128)(2,1)}, f32[8,128]{1,0:T(8,128)S(1)}) custom-call(s32[3,1,16]{2,1,0:T(1,128)S(1)} %bitcast.104, s32[3,1,16]{2,1,0:T(1,128)S(1)} %bitcast.107, s32[16,16]{1,0:T(8,128)S(1)} %bitcast_convert_fusion.cols_other, s32[16,16]{1,0:T(8,128)S(1)} %copy-done.21, ...), custom_call_target="tpu_custom_call" | custom-call | flops 3221225472 | bytes 16777216 | tf_op jit(solution)/shard_map/operate_first/pallas_call | solution.py:306
  95.2 2.6 %collective-permute-start.20 = (f32[2,8,128]{2,1,0:T(8,128)S(1)}, f32[2,8,128]{2,1,0:T(8,128)S(1)}, u32[]{:S(2)}, u32[]{:S(2)}) collective-permute-start(f32[2,8,128]{2,1,0:T(8,128)S(1)} %pad_maximum_fusion.refs_0_), channel_id=1, source_target_pairs={{0,6},{2,4},{4,2},{6,0},{8,14},{10,12},{12,10},{14,8},{1,7},{3,5},... | collective-permute-start | bytes 24584 | tf_op jit(solution)/shard_map/ppermute | solution.py:130
  102.2 2.1 update.1
  107.1 1.7 collective-permute-start.23
  110.7 2.6 %collective-permute-done.24.refs_3_ = f32[2,8,128]{2,1,0:T(8,128)S(1)} collective-permute-done((f32[2,8,128]{2,1,0:T(8,128)S(1)}, f32[2,8,128]{2,1,0:T(8,128)S(1)}, u32[]{:S(2)}, u32[]{:S(2)}) %collective-permute-start.24) | collective-permute-done | bytes 8224 | tf_op jit(solution)/shard_map/ppermute | solution.py:130
  116.1 10.2 %collective-permute-done.25 = bf16[128,2048]{1,0:T(8,128)(2,1)S(1)} collective-permute-done((bf16[128,2048]{1,0:T(8,128)(2,1)S(1)}, bf16[128,2048]{1,0:T(8,128)(2,1)S(1)}, u32[]{:S(2)}, u32[]{:S(2)}) %collective-permute-start.25) | collective-permute-done | bytes 524320 | tf_op jit(solution)/shard_map/ppermute | solution.py:121
  126.4 3.8 %collective-permute-start.32 = (bf16[128,2048]{1,0:T(8,128)(2,1)S(1)}, bf16[128,2048]{1,0:T(8,128)(2,1)S(1)}, u32[]{:S(2)}, u32[]{:S(2)}) collective-permute-start(bf16[128,2048]{1,0:T(8,128)(2,1)S(1)} %get-tuple-element.55), channel_id=1, source_target_pairs={{0,4},{4,0},{8,12},{12,8},{1,5},{5,1},{9,13},{13,9},{2,6},{6,2},{1... | collective-permute-start | bytes 1572872 | tf_op jit(solution)/shard_map/ppermute | solution.py:121
  132.3 10.7 %collective-permute-done.32 = bf16[128,2048]{1,0:T(8,128)(2,1)S(1)} collective-permute-done((bf16[128,2048]{1,0:T(8,128)(2,1)S(1)}, bf16[128,2048]{1,0:T(8,128)(2,1)S(1)}, u32[]{:S(2)}, u32[]{:S(2)}) %collective-permute-start.32) | collective-permute-done | bytes 524320 | tf_op jit(solution)/shard_map/ppermute | solution.py:121
  143.0 2.0 collective-permute-done.28.refs_1_
  145.0 6.9 %collective-permute-done.37 = bf16[128,2048]{1,0:T(8,128)(2,1)S(1)} collective-permute-done((bf16[128,2048]{1,0:T(8,128)(2,1)S(1)}, bf16[128,2048]{1,0:T(8,128)(2,1)S(1)}, u32[]{:S(2)}, u32[]{:S(2)}) %collective-permute-start.37) | collective-permute-done | bytes 524320 | tf_op jit(solution)/shard_map/ppermute | solution.py:121
  152.5 4.0 %collective-permute-start.29 = (bf16[128,2048]{1,0:T(8,128)(2,1)S(1)}, bf16[128,2048]{1,0:T(8,128)(2,1)S(1)}, u32[]{:S(2)}, u32[]{:S(2)}) collective-permute-start(bf16[128,2048]{1,0:T(8,128)(2,1)S(1)} %get-tuple-element.55), channel_id=1, source_target_pairs={{0,12},{12,0},{1,13},{13,1},{2,14},{14,2},{3,15},{15,3},{16,28},{2... | collective-permute-start | bytes 1572872 | tf_op jit(solution)/shard_map/ppermute | solution.py:686
  156.6 11.8 %operate_second.1 = (bf16[128,2048]{1,0:T(8,128)(2,1)S(1)}, bf16[64,2048]{1,0:T(8,128)(2,1)S(1)}, bf16[64,2048]{1,0:T(8,128)(2,1)S(1)}, f32[8,128]{1,0:T(8,128)S(1)}) custom-call(s32[3,1,16]{2,1,0:T(1,128)S(1)} %bitcast.105, s32[3,1,16]{2,1,0:T(1,128)S(1)} %bitcast.108, s32[16,16]{1,0:T(8,128)S(1)} %bitcast_convert_fusion.cols_other, ...), custom_call_target="tpu_custom_call" | custom-call | bytes 1024 | tf_op jit(solution)/shard_map/operate_second/pallas_call | solution.py:306
  168.4 1.8 collective-permute-start.42
  170.2 8.6 %collective-permute-done.42.refs_2_ = bf16[64,2048]{1,0:T(8,128)(2,1)} collective-permute-done((bf16[64,2048]{1,0:T(8,128)(2,1)S(1)}, bf16[64,2048]{1,0:T(8,128)(2,1)}, u32[]{:S(2)}, u32[]{:S(2)}) %collective-permute-start.42) | collective-permute-done | bytes 262176 | tf_op jit(solution)/shard_map/ppermute | solution.py:121
  178.8 1.8 collective-permute-start.43
  182.0 6.1 %collective-permute-done.43.refs_3_ = bf16[64,2048]{1,0:T(8,128)(2,1)S(1)} collective-permute-done((bf16[64,2048]{1,0:T(8,128)(2,1)S(1)}, bf16[64,2048]{1,0:T(8,128)(2,1)S(1)}, u32[]{:S(2)}, u32[]{:S(2)}) %collective-permute-start.43) | collective-permute-done | bytes 262176 | tf_op jit(solution)/shard_map/ppermute | solution.py:121
  188.2 6.1 %collective-permute-start.48 = (f32[8,128]{1,0:T(8,128)S(1)}, f32[8,128]{1,0:T(8,128)S(1)}, u32[]{:S(2)}, u32[]{:S(2)}) collective-permute-start(f32[8,128]{1,0:T(8,128)S(1)} %add.66), channel_id=1, source_target_pairs={{0,4},{4,0},{8,12},{12,8},{1,5},{5,1},{9,13},{13,9},{2,6},{6,2},{1... | collective-permute-start | bytes 12296 | tf_op jit(solution)/shard_map/ppermute | solution.py:121
  197.4 2.0 collective-permute-start.50
  200.9 1.9 collective-permute-done.50
  204.3 4.9 %collective-permute-done.41.refs_3_ = bf16[128,2048]{1,0:T(8,128)(2,1)S(1)} collective-permute-done((bf16[128,2048]{1,0:T(8,128)(2,1)S(1)}, bf16[128,2048]{1,0:T(8,128)(2,1)S(1)}, u32[]{:S(2)}, u32[]{:S(2)}) %collective-permute-start.41) | collective-permute-done | bytes 524320 | tf_op jit(solution)/shard_map/ppermute | solution.py:121
  210.7 4.2 %collective-permute-done.46.refs_4_ = bf16[64,2048]{1,0:T(8,128)(2,1)} collective-permute-done((bf16[64,2048]{1,0:T(8,128)(2,1)}, bf16[64,2048]{1,0:T(8,128)(2,1)}, u32[]{:S(2)}, u32[]{:S(2)}) %collective-permute-start.46) | collective-permute-done | bytes 262176 | tf_op jit(solution)/shard_map/ppermute | solution.py:121
  215.9 2.3 %assemble.4.refs_1_ = bf16[2,2,128,2048]{3,2,1,0:T(8,128)(2,1)} custom-call(bf16[128,2048]{1,0:T(8,128)(2,1)S(1)} %get-tuple-element.56.refs_0_, bf16[128,2048]{1,0:T(8,128)(2,1)S(1)} %collective-permute-done.45.refs_1_, bf16[64,2048]{1,0:T(8,128)(2,1)} %collective-permute-done.42.refs_2_, bf16[64,2048]{1,0:T(8,128)(2,1)S(1)} %copy-done.20, ...), custom_call_target="tpu_custom_call" | custom-call | tf_op jit(solution)/shard_map/assemble/pallas_call | solution.py:548
  (150 shorter events, 50.5 us)
Async XLA Ops:
  4.9 17.5 %collective-permute-start.1 = (bf16[128,2176]{1,0:T(8,128)(2,1)}, bf16[128,2176]{1,0:T(8,128)(2,1)S(1)}, u32[]{:S(2)}, u32[]{:S(2)}) collective-permute-start(bf16[128,2176]{1,0:T(8,128)(2,1)} %get-tuple-element.35), channel_id=1, source_target_pairs={{0,8},{8,12},{12,4},{4,0},{1,9},{9,13},{13,5},{5,1},{2,10},{10,14}... | collective-permute-start | bytes 1671176 | tf_op jit(solution)/shard_map/ppermute | solution.py:580
  9.0 25.8 %collective-permute-start.2 = (bf16[128,2176]{1,0:T(8,128)(2,1)}, bf16[128,2176]{1,0:T(8,128)(2,1)S(1)}, u32[]{:S(2)}, u32[]{:S(2)}) collective-permute-start(bf16[128,2176]{1,0:T(8,128)(2,1)} %get-tuple-element.36), channel_id=1, source_target_pairs={{0,4},{4,12},{12,8},{8,0},{1,5},{5,13},{13,9},{9,1},{2,6},{6,14},{... | collective-permute-start | bytes 1671176 | tf_op jit(solution)/shard_map/ppermute | solution.py:581
  9.0 25.8 %collective-permute-start = (bf16[31,128,128]{2,1,0:T(8,128)(2,1)}, bf16[31,128,128]{2,1,0:T(8,128)(2,1)S(1)}, u32[]{:S(2)}, u32[]{:S(2)}) collective-permute-start(bf16[31,128,128]{2,1,0:T(8,128)(2,1)} %get-tuple-element.34), channel_id=1, source_target_pairs={{0,2},{2,0},{1,3},{3,1},{4,6},{6,4},{5,7},{7,5},{8,10},{10,8},{9,1... | collective-permute-start | bytes 3047432 | tf_op jit(solution)/shard_map/ppermute | solution.py:121
  34.8 16.1 %collective-permute-start.5 = (bf16[31,128,128]{2,1,0:T(8,128)(2,1)S(1)}, bf16[31,128,128]{2,1,0:T(8,128)(2,1)S(1)}, u32[]{:S(2)}, u32[]{:S(2)}) collective-permute-start(bf16[31,128,128]{2,1,0:T(8,128)(2,1)S(1)} %collective-permute-done.near.left_other), channel_id=1, source_target_pairs={{0,1},{1,0},{2,3},{3,2},{4,5},{5,4},{6,7},{7,6},{8,9},{9,8},{10,11... | collective-permute-start | bytes 3047432 | tf_op jit(solution)/shard_map/ppermute | solution.py:121
  35.0 14.5 %collective-permute-start.6 = (bf16[128,2048]{1,0:T(8,128)(2,1)S(1)}, bf16[128,2048]{1,0:T(8,128)(2,1)}, u32[]{:S(2)}, u32[]{:S(2)}) collective-permute-start(bf16[128,2048]{1,0:T(8,128)(2,1)S(1)} %get-tuple-element.67), channel_id=1, source_target_pairs={{0,4},{4,0},{8,12},{12,8},{1,5},{5,1},{9,13},{13,9},{2,6},{6,2},{1... | collective-permute-start | bytes 1572872 | tf_op jit(solution)/shard_map/ppermute | solution.py:121
  35.8 20.0 %collective-permute-start.7 = (bf16[128,2048]{1,0:T(8,128)(2,1)S(1)}, bf16[128,2048]{1,0:T(8,128)(2,1)S(1)}, u32[]{:S(2)}, u32[]{:S(2)}) collective-permute-start(bf16[128,2048]{1,0:T(8,128)(2,1)S(1)} %get-tuple-element.67), channel_id=1, source_target_pairs={{0,1},{1,0},{2,3},{3,2},{4,5},{5,4},{6,7},{7,6},{8,9},{9,8},{10,11... | collective-permute-start | bytes 1572872 | tf_op jit(solution)/shard_map/ppermute | solution.py:121
  36.0 20.5 %collective-permute-start.8 = (bf16[128,2048]{1,0:T(8,128)(2,1)S(1)}, bf16[128,2048]{1,0:T(8,128)(2,1)S(1)}, u32[]{:S(2)}, u32[]{:S(2)}) collective-permute-start(bf16[128,2048]{1,0:T(8,128)(2,1)S(1)} %get-tuple-element.68), channel_id=1, source_target_pairs={{0,1},{1,0},{2,3},{3,2},{4,5},{5,4},{6,7},{7,6},{8,9},{9,8},{10,11... | collective-permute-start | bytes 1572872 | tf_op jit(solution)/shard_map/ppermute | solution.py:121
  36.3 21.7 %collective-permute-start.11 = (bf16[128,2048]{1,0:T(8,128)(2,1)S(1)}, bf16[128,2048]{1,0:T(8,128)(2,1)}, u32[]{:S(2)}, u32[]{:S(2)}) collective-permute-start(bf16[128,2048]{1,0:T(8,128)(2,1)S(1)} %get-tuple-element.67), channel_id=1, source_target_pairs={{0,2},{2,0},{1,3},{3,1},{4,6},{6,4},{5,7},{7,5},{8,10},{10,8},{9,1... | collective-permute-start | bytes 1572872 | tf_op jit(solution)/shard_map/ppermute | solution.py:121
  49.5 13.9 %collective-permute-start.14 = (bf16[128,2048]{1,0:T(8,128)(2,1)}, bf16[128,2048]{1,0:T(8,128)(2,1)}, u32[]{:S(2)}, u32[]{:S(2)}) collective-permute-start(bf16[128,2048]{1,0:T(8,128)(2,1)} %collective-permute-done.6), channel_id=1, source_target_pairs={{0,2},{2,0},{1,3},{3,1},{4,6},{6,4},{5,7},{7,5},{8,10},{10,8},{9,1... | collective-permute-start | bytes 1572872 | tf_op jit(solution)/shard_map/ppermute | solution.py:121
  57.3 13.4 %collective-permute-start.9 = (bf16[128,2048]{1,0:T(8,128)(2,1)S(1)}, bf16[128,2048]{1,0:T(8,128)(2,1)}, u32[]{:S(2)}, u32[]{:S(2)}) collective-permute-start(bf16[128,2048]{1,0:T(8,128)(2,1)S(1)} %copy-done.7), channel_id=1, source_target_pairs={{0,4},{4,0},{8,12},{12,8},{1,5},{5,1},{9,13},{13,9},{2,6},{6,2},{1... | collective-permute-start | bytes 1572872 | tf_op jit(solution)/shard_map/ppermute | solution.py:121
  58.1 15.2 %collective-permute-start.13 = (bf16[128,2048]{1,0:T(8,128)(2,1)}, bf16[128,2048]{1,0:T(8,128)(2,1)}, u32[]{:S(2)}, u32[]{:S(2)}) collective-permute-start(bf16[128,2048]{1,0:T(8,128)(2,1)} %collective-permute-done.6), channel_id=1, source_target_pairs={{0,1},{1,0},{2,3},{3,2},{4,5},{5,4},{6,7},{7,6},{8,9},{9,8},{10,11... | collective-permute-start | bytes 1572872 | tf_op jit(solution)/shard_map/ppermute | solution.py:121
  58.1 15.2 %collective-permute-start.12 = (bf16[128,2048]{1,0:T(8,128)(2,1)}, bf16[128,2048]{1,0:T(8,128)(2,1)}, u32[]{:S(2)}, u32[]{:S(2)}) collective-permute-start(bf16[128,2048]{1,0:T(8,128)(2,1)} %collective-permute-done.11), channel_id=1, source_target_pairs={{0,1},{1,0},{2,3},{3,2},{4,5},{5,4},{6,7},{7,6},{8,9},{9,8},{10,11... | collective-permute-start | bytes 1572872 | tf_op jit(solution)/shard_map/ppermute | solution.py:121
  63.3 10.0 %collective-permute-start.15 = (bf16[128,2048]{1,0:T(8,128)(2,1)}, bf16[128,2048]{1,0:T(8,128)(2,1)}, u32[]{:S(2)}, u32[]{:S(2)}) collective-permute-start(bf16[128,2048]{1,0:T(8,128)(2,1)} %collective-permute-done.14), channel_id=1, source_target_pairs={{0,1},{1,0},{2,3},{3,2},{4,5},{5,4},{6,7},{7,6},{8,9},{9,8},{10,11... | collective-permute-start | bytes 1572872 | tf_op jit(solution)/shard_map/ppermute | solution.py:121
  70.7 27.1 %collective-permute-start.16 = (bf16[128,2048]{1,0:T(8,128)(2,1)S(1)}, bf16[128,2048]{1,0:T(8,128)(2,1)S(1)}, u32[]{:S(2)}, u32[]{:S(2)}) collective-permute-start(bf16[128,2048]{1,0:T(8,128)(2,1)S(1)} %dynamic-slice_bitcast_fusion), channel_id=1, source_target_pairs={{0,12},{4,8},{8,4},{12,0},{1,13},{5,9},{9,5},{13,1},{2,14},{6,10},... | collective-permute-start | bytes 1572872 | tf_op jit(solution)/shard_map/ppermute | solution.py:121
  113.9 12.4 %collective-permute-start.25 = (bf16[128,2048]{1,0:T(8,128)(2,1)S(1)}, bf16[128,2048]{1,0:T(8,128)(2,1)S(1)}, u32[]{:S(2)}, u32[]{:S(2)}) collective-permute-start(bf16[128,2048]{1,0:T(8,128)(2,1)S(1)} %get-tuple-element.54.refs_0_), channel_id=1, source_target_pairs={{0,4},{4,0},{8,12},{12,8},{1,5},{5,1},{9,13},{13,9},{2,6},{6,2},{1... | collective-permute-start | bytes 1572872 | tf_op jit(solution)/shard_map/ppermute | solution.py:121
  114.3 12.0 %collective-permute-start.26 = (bf16[128,2048]{1,0:T(8,128)(2,1)S(1)}, bf16[128,2048]{1,0:T(8,128)(2,1)S(1)}, u32[]{:S(2)}, u32[]{:S(2)}) collective-permute-start(bf16[128,2048]{1,0:T(8,128)(2,1)S(1)} %get-tuple-element.55), channel_id=1, source_target_pairs={{0,2},{2,0},{1,3},{3,1},{4,6},{6,4},{5,7},{7,5},{8,10},{10,8},{9,1... | collective-permute-start | bytes 1572872 | tf_op jit(solution)/shard_map/ppermute | solution.py:121
  114.9 11.5 %collective-permute-start.27 = (bf16[128,2048]{1,0:T(8,128)(2,1)S(1)}, bf16[128,2048]{1,0:T(8,128)(2,1)S(1)}, u32[]{:S(2)}, u32[]{:S(2)}) collective-permute-start(bf16[128,2048]{1,0:T(8,128)(2,1)S(1)} %get-tuple-element.55), channel_id=1, source_target_pairs={{4,8},{8,4},{5,9},{9,5},{6,10},{10,6},{7,11},{11,7},{20,24},{24,20... | collective-permute-start | bytes 1572872 | tf_op jit(solution)/shard_map/ppermute | solution.py:674
  115.6 16.7 %collective-permute-start.30 = (bf16[128,2048]{1,0:T(8,128)(2,1)S(1)}, bf16[128,2048]{1,0:T(8,128)(2,1)S(1)}, u32[]{:S(2)}, u32[]{:S(2)}) collective-permute-start(bf16[128,2048]{1,0:T(8,128)(2,1)S(1)} %get-tuple-element.54.refs_0_), channel_id=1, source_target_pairs={{0,1},{1,0},{2,3},{3,2},{4,5},{5,4},{6,7},{7,6},{8,9},{9,8},{10,11... | collective-permute-start | bytes 1572872 | tf_op jit(solution)/shard_map/ppermute | solution.py:121
  115.6 16.6 %collective-permute-start.31 = (bf16[128,2048]{1,0:T(8,128)(2,1)S(1)}, bf16[128,2048]{1,0:T(8,128)(2,1)S(1)}, u32[]{:S(2)}, u32[]{:S(2)}) collective-permute-start(bf16[128,2048]{1,0:T(8,128)(2,1)S(1)} %get-tuple-element.55), channel_id=1, source_target_pairs={{0,1},{1,0},{2,3},{3,2},{4,5},{5,4},{6,7},{7,6},{8,9},{9,8},{10,11... | collective-permute-start | bytes 1572872 | tf_op jit(solution)/shard_map/ppermute | solution.py:121
  126.4 16.6 %collective-permute-start.32 = (bf16[128,2048]{1,0:T(8,128)(2,1)S(1)}, bf16[128,2048]{1,0:T(8,128)(2,1)S(1)}, u32[]{:S(2)}, u32[]{:S(2)}) collective-permute-start(bf16[128,2048]{1,0:T(8,128)(2,1)S(1)} %get-tuple-element.55), channel_id=1, source_target_pairs={{0,4},{4,0},{8,12},{12,8},{1,5},{5,1},{9,13},{13,9},{2,6},{6,2},{1... | collective-permute-start | bytes 1572872 | tf_op jit(solution)/shard_map/ppermute | solution.py:121
  130.2 14.9 %collective-permute-start.28 = (bf16[128,2048]{1,0:T(8,128)(2,1)S(1)}, bf16[128,2048]{1,0:T(8,128)(2,1)S(1)}, u32[]{:S(2)}, u32[]{:S(2)}) collective-permute-start(bf16[128,2048]{1,0:T(8,128)(2,1)S(1)} %get-tuple-element.54.refs_0_), channel_id=1, source_target_pairs={{0,2},{2,0},{1,3},{3,1},{4,6},{6,4},{5,7},{7,5},{8,10},{10,8},{9,1... | collective-permute-start | bytes 1572872 | tf_op jit(solution)/shard_map/ppermute | solution.py:121
  131.7 20.3 %collective-permute-start.37 = (bf16[128,2048]{1,0:T(8,128)(2,1)S(1)}, bf16[128,2048]{1,0:T(8,128)(2,1)S(1)}, u32[]{:S(2)}, u32[]{:S(2)}) collective-permute-start(bf16[128,2048]{1,0:T(8,128)(2,1)S(1)} %collective-permute-done.25), channel_id=1, source_target_pairs={{0,2},{2,0},{1,3},{3,1},{4,6},{6,4},{5,7},{7,5},{8,10},{10,8},{9,1... | collective-permute-start | bytes 1572872 | tf_op jit(solution)/shard_map/ppermute | solution.py:121
  132.2 19.7 %collective-permute-start.38 = (bf16[128,2048]{1,0:T(8,128)(2,1)S(1)}, bf16[128,2048]{1,0:T(8,128)(2,1)S(1)}, u32[]{:S(2)}, u32[]{:S(2)}) collective-permute-start(bf16[128,2048]{1,0:T(8,128)(2,1)S(1)} %collective-permute-done.26), channel_id=1, source_target_pairs={{0,4},{4,0},{8,12},{12,8},{1,5},{5,1},{9,13},{13,9},{2,6},{6,2},{1... | collective-permute-start | bytes 1572872 | tf_op jit(solution)/shard_map/ppermute | solution.py:121
  132.2 20.2 %collective-permute-start.33 = (bf16[128,2048]{1,0:T(8,128)(2,1)S(1)}, bf16[128,2048]{1,0:T(8,128)(2,1)S(1)}, u32[]{:S(2)}, u32[]{:S(2)}) collective-permute-start(bf16[128,2048]{1,0:T(8,128)(2,1)S(1)} %collective-permute-done.25), channel_id=1, source_target_pairs={{0,1},{1,0},{2,3},{3,2},{4,5},{5,4},{6,7},{7,6},{8,9},{9,8},{10,11... | collective-permute-start | bytes 1572872 | tf_op jit(solution)/shard_map/ppermute | solution.py:121
  145.0 11.5 %collective-permute-start.34 = (bf16[128,2048]{1,0:T(8,128)(2,1)S(1)}, bf16[128,2048]{1,0:T(8,128)(2,1)S(1)}, u32[]{:S(2)}, u32[]{:S(2)}) collective-permute-start(bf16[128,2048]{1,0:T(8,128)(2,1)S(1)} %collective-permute-done.32), channel_id=1, source_target_pairs={{0,1},{1,0},{2,3},{3,2},{4,5},{5,4},{6,7},{7,6},{8,9},{9,8},{10,11... | collective-permute-start | bytes 1572872 | tf_op jit(solution)/shard_map/ppermute | solution.py:121
  152.5 29.5 %collective-permute-start.29 = (bf16[128,2048]{1,0:T(8,128)(2,1)S(1)}, bf16[128,2048]{1,0:T(8,128)(2,1)S(1)}, u32[]{:S(2)}, u32[]{:S(2)}) collective-permute-start(bf16[128,2048]{1,0:T(8,128)(2,1)S(1)} %get-tuple-element.55), channel_id=1, source_target_pairs={{0,12},{12,0},{1,13},{13,1},{2,14},{14,2},{3,15},{15,3},{16,28},{2... | collective-permute-start | bytes 1572872 | tf_op jit(solution)/shard_map/ppermute | solution.py:686
  168.4 10.4 %collective-permute-start.42 = (bf16[64,2048]{1,0:T(8,128)(2,1)S(1)}, bf16[64,2048]{1,0:T(8,128)(2,1)}, u32[]{:S(2)}, u32[]{:S(2)}) collective-permute-start(bf16[64,2048]{1,0:T(8,128)(2,1)S(1)} %get-tuple-element.59), channel_id=1, source_target_pairs={{0,12},{4,8},{8,4},{12,0},{1,13},{5,9},{9,5},{13,1},{2,14},{6,10},... | collective-permute-start | bytes 786440 | tf_op jit(solution)/shard_map/ppermute | solution.py:121
  180.6 30.1 %collective-permute-start.45 = (bf16[128,2048]{1,0:T(8,128)(2,1)S(1)}, bf16[128,2048]{1,0:T(8,128)(2,1)S(1)}, u32[]{:S(2)}, u32[]{:S(2)}) collective-permute-start(bf16[128,2048]{1,0:T(8,128)(2,1)S(1)} %get-tuple-element.56.refs_0_), channel_id=1, source_target_pairs={{0,2},{2,0},{1,3},{3,1},{4,6},{6,4},{5,7},{7,5},{8,10},{10,8},{9,1... | collective-permute-start | bytes 1572872 | tf_op jit(solution)/shard_map/ppermute | solution.py:121
  194.3 14.9 %collective-permute-start.41 = (bf16[128,2048]{1,0:T(8,128)(2,1)S(1)}, bf16[128,2048]{1,0:T(8,128)(2,1)S(1)}, u32[]{:S(2)}, u32[]{:S(2)}) collective-permute-start(bf16[128,2048]{1,0:T(8,128)(2,1)S(1)} %broadcast_select_fusion.refs_2_), channel_id=1, source_target_pairs={{0,2},{2,0},{1,3},{3,1},{4,6},{6,4},{5,7},{7,5},{8,10},{10,8},{9,1... | collective-permute-start | bytes 1572872 | tf_op jit(solution)/shard_map/ppermute | solution.py:121
  195.9 19.0 %collective-permute-start.46 = (bf16[64,2048]{1,0:T(8,128)(2,1)}, bf16[64,2048]{1,0:T(8,128)(2,1)}, u32[]{:S(2)}, u32[]{:S(2)}) collective-permute-start(bf16[64,2048]{1,0:T(8,128)(2,1)} %collective-permute-done.42.refs_2_), channel_id=1, source_target_pairs={{0,2},{2,0},{1,3},{3,1},{4,6},{6,4},{5,7},{7,5},{8,10},{10,8},{9,1... | collective-permute-start | bytes 786440 | tf_op jit(solution)/shard_map/ppermute | solution.py:121
  202.8 16.7 %collective-permute-start.51 = (f32[2,8,128]{2,1,0:T(8,128)S(1)}, f32[2,8,128]{2,1,0:T(8,128)S(1)}, u32[]{:S(2)}, u32[]{:S(2)}) collective-permute-start(f32[2,8,128]{2,1,0:T(8,128)S(1)} %pad_maximum_fusion.2), channel_id=1, source_target_pairs={{0,2},{2,0},{1,3},{3,1},{4,6},{6,4},{5,7},{7,5},{8,10},{10,8},{9,1... | collective-permute-start | bytes 24584 | tf_op jit(solution)/shard_map/ppermute | solution.py:121
  209.2 11.3 %collective-permute-start.44 = (bf16[64,2048]{1,0:T(8,128)(2,1)}, bf16[64,2048]{1,0:T(8,128)(2,1)S(1)}, u32[]{:S(2)}, u32[]{:S(2)}) collective-permute-start(bf16[64,2048]{1,0:T(8,128)(2,1)} %copy-done.19), channel_id=1, source_target_pairs={{0,2},{2,0},{1,3},{3,1},{4,6},{6,4},{5,7},{7,5},{8,10},{10,8},{9,1... | collective-permute-start | bytes 786440 | tf_op jit(solution)/shard_map/ppermute | solution.py:121
  (45 other events, 378.2 us)

commit v15 on v12

--- a/solution.py
+++ b/solution.py
@@ -599,11 +599,12 @@
     far_core = across(far, "sub", 1)
     near_a_core = across(near_a, "sub", 1)
 
-    near_b = across(after(own[1], far_z, far_core, near_a_core), "blk", 1)
-    far_zx = across(far_z, "ops", 1)
-    operators = after(operators, far_z)
+    operators = after(operators, mix_b)
     operators_core = across(operators, "sub", 1)
     turned = arrange(right, operators, operators_core)
+    next_b, far_z = after((own[1], far_z), far_core, near_a_core, turned)
+    near_b = across(next_b, "blk", 1)
+    far_zx = across(far_z, "ops", 1)
     cols = (*cols, operators[-1, :16, :sectors].astype(jnp.int32))
     far_x_core = across(far_x, "sub", 1)
     far_z_core = across(far_z, "sub", 1)
@@ -713,7 +714,7 @@
     late_in = across(after(two_late, far_in), "blk", 3)
     far_in_x = across(after(far_in, near_in), "ops", 1)
     sums = stats_three + across(stats_three, "sub", 1)
-    other = jnp.where(middle, other_middle, after(other_end, sums))
+    other = jnp.where(middle, other_middle, after(other_end, two_near))
     other_x = across(other, "ops", 1)
     sums = after(sums, far_in)
     both = jnp.stack([sums + across(sums, "blk", 1), across(sums, "blk", 2) + across(sums, "blk", 3)])

time: 207 us -> 210 us (1.014)
  local copies, waits for them, and re-layouts: 10.5 us -> 15.6 us
    unnamed x52 -> x50, local copies, waits for them, and re-layouts: 10.3 us -> 15.5 us
  transfers between devices with their start and end apart: 52 -> 52, of which waited for: 25 -> 27; matrix products, arithmetic and copies ran while one was open for 2% -> 2% of each run, Pallas kernels for 15% -> 15%
where the time goes in v15:
time: 210 us; the launch traced here: 207 us
  waiting for transfers between devices  98 us (47%)
  starting transfers between devices  50.5 us (24%)
  Pallas kernels  38 us (18%)
  local copies, waits for them, and re-layouts  15.6 us (7%)
  other arithmetic  4.4 us (2%)
    ppermute x42, waiting for transfers between devices, across(): return lax.ppermute(value, axis, [(i, i ^ distance) for i in range(size)])  72.7 us
    ppermute x42, starting transfers between devices, across(): return lax.ppermute(value, axis, [(i, i ^ distance) for i in range(size)])  35.5 us
    pallas_call x2, Pallas kernels, operate(): pl.pallas_call(functools.partial(operate_kernel, first, plan), out_shape=...  24.8 us
    unnamed x50, local copies, waits for them, and re-layouts  15.5 us
    ppermute x1, waiting for transfers between devices, shards(): mix_b = lax.ppermute(mix_b, 'blk', [(0, 1), (1, 3), (3, 2), (2, 0)])  12.4 us
    ppermute x6, starting transfers between devices, share(): lax.ppermute(pair, axes, [(i, i ^ distance) for i in range(count)])  6.98 us
    ppermute x1, waiting for transfers between devices, shards(): mix_a = lax.ppermute(mix_a, 'blk', [(0, 2), (2, 3), (3, 1), (1, 0)])  6.69 us
    ppermute x6, waiting for transfers between devices, share(): lax.ppermute(pair, axes, [(i, i ^ distance) for i in range(count)])  6.17 us
  transfers between devices with their start and end apart: 52, of which 27 were waited for; matrix products, arithmetic and copies ran while one was open for 2% of the time, Pallas kernels for 15%

profile of v15, /device:TPU:0, one launch (start us, length us, event | category | flops | bytes accessed | tf_op | source)
XLA Modules:
  0.0 207.4 jit_solution(1450402375080836623)
XLA Ops:
  0.6 4.2 %prepare.1 = (bf16[128,2176]{1,0:T(8,128)(2,1)}, bf16[128,2176]{1,0:T(8,128)(2,1)}, bf16[31,128,128]{2,1,0:T(8,128)(2,1)}, f32[8,128]{1,0:T(8,128)}) custom-call(s32[16,16]{1,0:T(8,128)} %pattern.5, bf16[2,2,128,2048]{3,2,1,0:T(8,128)(2,1)} %bitcast.115, bf16[2,128,2048]{2,1,0:T(8,128)(2,1)} %bitcast.76, bf16[48,128,128]{2,1,0:T(8,128)(2,1)} %bitcast.80, ...), custom_call_target="tpu_custom_call" | custom-call | tf_op jit(solution)/shard_map/prepare/pallas_call | solution.py:435
  4.9 4.1 %collective-permute-start.1 = (bf16[128,2176]{1,0:T(8,128)(2,1)}, bf16[128,2176]{1,0:T(8,128)(2,1)S(1)}, u32[]{:S(2)}, u32[]{:S(2)}) collective-permute-start(bf16[128,2176]{1,0:T(8,128)(2,1)} %get-tuple-element.36), channel_id=1, source_target_pairs={{0,8},{8,12},{12,4},{4,0},{1,9},{9,13},{13,5},{5,1},{2,10},{10,14}... | collective-permute-start | bytes 1671176 | tf_op jit(solution)/shard_map/ppermute | solution.py:580
  9.0 1.5 collective-permute-start
  10.6 2.3 %bitcast_multiply_fusion.2 = (bf16[128,2048]{1,0:T(8,128)(2,1)}, bf16[128,2048]{1,0:T(8,128)(2,1)}) fusion(bf16[2,2,128,2048]{3,2,1,0:T(8,128)(2,1)} %bitcast.116, s32[]{:T(128)S(6)} %select_n.51, bf16[2048]{0:T(1024)(128)(2,1)S(1)} %get-tuple-element.81, bf16[2048]{0:T(1024)(128)(2,1)S(1)} %get-tuple-element.82), kind=kLoop, calls=%fused_computation.2 | loop fusion | flops 524288 | bytes 2105348 | tf_op jit(solution)/shard_map/mul | solution.py:586
  13.4 1.5 collective-permute-done.3
  15.7 6.7 %collective-permute-done.1.refs_16_ = bf16[128,2176]{1,0:T(8,128)(2,1)S(1)} collective-permute-done((bf16[128,2176]{1,0:T(8,128)(2,1)}, bf16[128,2176]{1,0:T(8,128)(2,1)S(1)}, u32[]{:S(2)}, u32[]{:S(2)}) %collective-permute-start.1) | collective-permute-done | bytes 557088 | tf_op jit(solution)/shard_map/ppermute | solution.py:580
  22.4 12.4 %collective-permute-done.2.refs_17_ = bf16[128,2176]{1,0:T(8,128)(2,1)S(1)} collective-permute-done((bf16[128,2176]{1,0:T(8,128)(2,1)}, bf16[128,2176]{1,0:T(8,128)(2,1)S(1)}, u32[]{:S(2)}, u32[]{:S(2)}) %collective-permute-start.2) | collective-permute-done | bytes 557088 | tf_op jit(solution)/shard_map/ppermute | solution.py:581
  39.2 1.7 arrange.1.right
  40.9 1.6 copy-done
  42.5 6.9 %collective-permute-done.6 = bf16[128,2048]{1,0:T(8,128)(2,1)} collective-permute-done((bf16[128,2048]{1,0:T(8,128)(2,1)S(1)}, bf16[128,2048]{1,0:T(8,128)(2,1)}, u32[]{:S(2)}, u32[]{:S(2)}) %collective-permute-start.6) | collective-permute-done | bytes 524320 | tf_op jit(solution)/shard_map/ppermute | solution.py:121
  53.8 11.1 %collective-permute-done.9 = bf16[128,2048]{1,0:T(8,128)(2,1)} collective-permute-done((bf16[128,2048]{1,0:T(8,128)(2,1)}, bf16[128,2048]{1,0:T(8,128)(2,1)}, u32[]{:S(2)}, u32[]{:S(2)}) %collective-permute-start.9) | collective-permute-done | bytes 524320 | tf_op jit(solution)/shard_map/ppermute | solution.py:121
  66.5 2.5 %collective-permute-start.16 = (bf16[128,2048]{1,0:T(8,128)(2,1)S(1)}, bf16[128,2048]{1,0:T(8,128)(2,1)S(1)}, u32[]{:S(2)}, u32[]{:S(2)}) collective-permute-start(bf16[128,2048]{1,0:T(8,128)(2,1)S(1)} %dynamic-slice_bitcast_fusion), channel_id=1, source_target_pairs={{0,12},{4,8},{8,4},{12,0},{1,13},{5,9},{9,5},{13,1},{2,14},{6,10},... | collective-permute-start | bytes 1572872 | tf_op jit(solution)/shard_map/ppermute | solution.py:121
  77.5 13.0 %operate_first.1 = (bf16[2,128,2048]{2,1,0:T(8,128)(2,1)}, bf16[2,128,2048]{2,1,0:T(8,128)(2,1)}, f32[8,128]{1,0:T(8,128)S(1)}) custom-call(s32[3,1,16]{2,1,0:T(1,128)S(1)} %bitcast.106, s32[3,1,16]{2,1,0:T(1,128)S(1)} %bitcast.109, s32[16,16]{1,0:T(8,128)S(1)} %bitcast_convert_fusion.cols_other, s32[16,16]{1,0:T(8,128)S(1)} %copy-done.20, ...), custom_call_target="tpu_custom_call" | custom-call | flops 3221225472 | bytes 16777216 | tf_op jit(solution)/shard_map/operate_first/pallas_call | solution.py:306
  93.6 1.7 collective-permute-start.20
  100.6 2.1 %update.1 = (f32[2,128,2048]{2,1,0:T(8,128)S(1)}, f32[8,128]{1,0:T(8,128)S(1)}) custom-call(bf16[2,128,2048]{2,1,0:T(8,128)(2,1)S(1)} %copy-done.2, bf16[2,128,2048]{2,1,0:T(8,128)(2,1)S(1)} %copy-done.5, bf16[2,128,2048]{2,1,0:T(8,128)(2,1)S(1)} %bitcast.79, bf16[128,2048]{1,0:T(8,128)(2,1)S(1)} %collective-permute-done.16.hd_far.refs_17_, ...), custom_call_target="tpu_custom_call" | custom-call | tf_op jit(solution)/shard_map/update/pallas_call | solution.py:644
  104.5 1.7 collective-permute-start.23
  108.2 2.6 %collective-permute-done.24.refs_3_ = f32[2,8,128]{2,1,0:T(8,128)S(1)} collective-permute-done((f32[2,8,128]{2,1,0:T(8,128)S(1)}, f32[2,8,128]{2,1,0:T(8,128)S(1)}, u32[]{:S(2)}, u32[]{:S(2)}) %collective-permute-start.24) | collective-permute-done | bytes 8224 | tf_op jit(solution)/shard_map/ppermute | solution.py:130
  114.5 9.2 %collective-permute-done.25 = bf16[128,2048]{1,0:T(8,128)(2,1)S(1)} collective-permute-done((bf16[128,2048]{1,0:T(8,128)(2,1)S(1)}, bf16[128,2048]{1,0:T(8,128)(2,1)S(1)}, u32[]{:S(2)}, u32[]{:S(2)}) %collective-permute-start.25) | collective-permute-done | bytes 524320 | tf_op jit(solution)/shard_map/ppermute | solution.py:121
  123.8 4.7 %collective-permute-start.32 = (bf16[128,2048]{1,0:T(8,128)(2,1)S(1)}, bf16[128,2048]{1,0:T(8,128)(2,1)S(1)}, u32[]{:S(2)}, u32[]{:S(2)}) collective-permute-start(bf16[128,2048]{1,0:T(8,128)(2,1)S(1)} %get-tuple-element.55), channel_id=1, source_target_pairs={{0,4},{4,0},{8,12},{12,8},{1,5},{5,1},{9,13},{13,9},{2,6},{6,2},{1... | collective-permute-start | bytes 1572872 | tf_op jit(solution)/shard_map/ppermute | solution.py:121
  130.7 10.7 %collective-permute-done.32 = bf16[128,2048]{1,0:T(8,128)(2,1)S(1)} collective-permute-done((bf16[128,2048]{1,0:T(8,128)(2,1)S(1)}, bf16[128,2048]{1,0:T(8,128)(2,1)S(1)}, u32[]{:S(2)}, u32[]{:S(2)}) %collective-permute-start.32) | collective-permute-done | bytes 524320 | tf_op jit(solution)/shard_map/ppermute | solution.py:121
  141.4 2.0 collective-permute-done.28.refs_1_
  143.4 6.9 %collective-permute-done.37 = bf16[128,2048]{1,0:T(8,128)(2,1)S(1)} collective-permute-done((bf16[128,2048]{1,0:T(8,128)(2,1)S(1)}, bf16[128,2048]{1,0:T(8,128)(2,1)S(1)}, u32[]{:S(2)}, u32[]{:S(2)}) %collective-permute-start.37) | collective-permute-done | bytes 524320 | tf_op jit(solution)/shard_map/ppermute | solution.py:121
  150.9 3.2 %collective-permute-start.29 = (bf16[128,2048]{1,0:T(8,128)(2,1)S(1)}, bf16[128,2048]{1,0:T(8,128)(2,1)S(1)}, u32[]{:S(2)}, u32[]{:S(2)}) collective-permute-start(bf16[128,2048]{1,0:T(8,128)(2,1)S(1)} %get-tuple-element.55), channel_id=1, source_target_pairs={{0,12},{12,0},{1,13},{13,1},{2,14},{14,2},{3,15},{15,3},{16,28},{2... | collective-permute-start | bytes 1572872 | tf_op jit(solution)/shard_map/ppermute | solution.py:686
  154.2 11.8 %operate_second.1 = (bf16[128,2048]{1,0:T(8,128)(2,1)S(1)}, bf16[64,2048]{1,0:T(8,128)(2,1)S(1)}, bf16[64,2048]{1,0:T(8,128)(2,1)S(1)}, f32[8,128]{1,0:T(8,128)S(1)}) custom-call(s32[3,1,16]{2,1,0:T(1,128)S(1)} %bitcast.107, s32[3,1,16]{2,1,0:T(1,128)S(1)} %bitcast.110, s32[16,16]{1,0:T(8,128)S(1)} %bitcast_convert_fusion.cols_other, ...), custom_call_target="tpu_custom_call" | custom-call | bytes 1024 | tf_op jit(solution)/shard_map/operate_second/pallas_call | solution.py:306
  166.0 2.6 %collective-permute-start.42 = (bf16[64,2048]{1,0:T(8,128)(2,1)S(1)}, bf16[64,2048]{1,0:T(8,128)(2,1)}, u32[]{:S(2)}, u32[]{:S(2)}) collective-permute-start(bf16[64,2048]{1,0:T(8,128)(2,1)S(1)} %get-tuple-element.59), channel_id=1, source_target_pairs={{0,12},{4,8},{8,4},{12,0},{1,13},{5,9},{9,5},{13,1},{2,14},{6,10},... | collective-permute-start | bytes 786440 | tf_op jit(solution)/shard_map/ppermute | solution.py:121
  169.7 6.7 %collective-permute-done.42.refs_2_ = bf16[64,2048]{1,0:T(8,128)(2,1)} collective-permute-done((bf16[64,2048]{1,0:T(8,128)(2,1)S(1)}, bf16[64,2048]{1,0:T(8,128)(2,1)}, u32[]{:S(2)}, u32[]{:S(2)}) %collective-permute-start.42) | collective-permute-done | bytes 262176 | tf_op jit(solution)/shard_map/ppermute | solution.py:121
  176.4 4.3 %collective-permute-start.48 = (f32[8,128]{1,0:T(8,128)S(1)}, f32[8,128]{1,0:T(8,128)S(1)}, u32[]{:S(2)}, u32[]{:S(2)}) collective-permute-start(f32[8,128]{1,0:T(8,128)S(1)} %add.66), channel_id=1, source_target_pairs={{0,4},{4,0},{8,12},{12,8},{1,5},{5,1},{9,13},{13,9},{2,6},{6,2},{1... | collective-permute-start | bytes 12296 | tf_op jit(solution)/shard_map/ppermute | solution.py:121
  181.5 2.4 %collective-permute-start.50 = (f32[8,128]{1,0:T(8,128)S(1)}, f32[8,128]{1,0:T(8,128)S(1)}, u32[]{:S(2)}, u32[]{:S(2)}) collective-permute-start(f32[8,128]{1,0:T(8,128)S(1)} %add.66), channel_id=1, source_target_pairs={{0,12},{4,8},{8,4},{12,0},{1,13},{5,9},{9,5},{13,1},{2,14},{6,10},... | collective-permute-start | bytes 12296 | tf_op jit(solution)/shard_map/ppermute | solution.py:121
  187.0 6.2 %collective-permute-done.43.refs_3_ = bf16[64,2048]{1,0:T(8,128)(2,1)} collective-permute-done((bf16[64,2048]{1,0:T(8,128)(2,1)S(1)}, bf16[64,2048]{1,0:T(8,128)(2,1)}, u32[]{:S(2)}, u32[]{:S(2)}) %collective-permute-start.43) | collective-permute-done | bytes 262176 | tf_op jit(solution)/shard_map/ppermute | solution.py:121
  195.2 1.5 collective-permute-start.44
  199.0 5.0 %collective-permute-done.46.refs_4_ = bf16[64,2048]{1,0:T(8,128)(2,1)} collective-permute-done((bf16[64,2048]{1,0:T(8,128)(2,1)}, bf16[64,2048]{1,0:T(8,128)(2,1)}, u32[]{:S(2)}, u32[]{:S(2)}) %collective-permute-start.46) | collective-permute-done | bytes 262176 | tf_op jit(solution)/shard_map/ppermute | solution.py:121
  204.0 2.4 %assemble.4.refs_1_ = bf16[2,2,128,2048]{3,2,1,0:T(8,128)(2,1)} custom-call(bf16[128,2048]{1,0:T(8,128)(2,1)S(1)} %get-tuple-element.56.refs_0_, bf16[128,2048]{1,0:T(8,128)(2,1)S(1)} %collective-permute-done.45.refs_1_, bf16[64,2048]{1,0:T(8,128)(2,1)} %collective-permute-done.42.refs_2_, bf16[64,2048]{1,0:T(8,128)(2,1)} %collective-permute-done.43.refs_3_, ...), custom_call_target="tpu_custom_call" | custom-call | tf_op jit(solution)/shard_map/assemble/pallas_call | solution.py:548
  (151 shorter events, 49.0 us)
Async XLA Ops:
  4.9 17.5 %collective-permute-start.1 = (bf16[128,2176]{1,0:T(8,128)(2,1)}, bf16[128,2176]{1,0:T(8,128)(2,1)S(1)}, u32[]{:S(2)}, u32[]{:S(2)}) collective-permute-start(bf16[128,2176]{1,0:T(8,128)(2,1)} %get-tuple-element.36), channel_id=1, source_target_pairs={{0,8},{8,12},{12,4},{4,0},{1,9},{9,13},{13,5},{5,1},{2,10},{10,14}... | collective-permute-start | bytes 1671176 | tf_op jit(solution)/shard_map/ppermute | solution.py:580
  9.0 25.8 %collective-permute-start.2 = (bf16[128,2176]{1,0:T(8,128)(2,1)}, bf16[128,2176]{1,0:T(8,128)(2,1)S(1)}, u32[]{:S(2)}, u32[]{:S(2)}) collective-permute-start(bf16[128,2176]{1,0:T(8,128)(2,1)} %get-tuple-element.37), channel_id=1, source_target_pairs={{0,4},{4,12},{12,8},{8,0},{1,5},{5,13},{13,9},{9,1},{2,6},{6,14},{... | collective-permute-start | bytes 1671176 | tf_op jit(solution)/shard_map/ppermute | solution.py:581
  9.0 25.8 %collective-permute-start = (bf16[31,128,128]{2,1,0:T(8,128)(2,1)}, bf16[31,128,128]{2,1,0:T(8,128)(2,1)S(1)}, u32[]{:S(2)}, u32[]{:S(2)}) collective-permute-start(bf16[31,128,128]{2,1,0:T(8,128)(2,1)} %get-tuple-element.35), channel_id=1, source_target_pairs={{0,2},{2,0},{1,3},{3,1},{4,6},{6,4},{5,7},{7,5},{8,10},{10,8},{9,1... | collective-permute-start | bytes 3047432 | tf_op jit(solution)/shard_map/ppermute | solution.py:121
  35.0 14.5 %collective-permute-start.6 = (bf16[128,2048]{1,0:T(8,128)(2,1)S(1)}, bf16[128,2048]{1,0:T(8,128)(2,1)}, u32[]{:S(2)}, u32[]{:S(2)}) collective-permute-start(bf16[128,2048]{1,0:T(8,128)(2,1)S(1)} %get-tuple-element.71), channel_id=1, source_target_pairs={{0,4},{4,0},{8,12},{12,8},{1,5},{5,1},{9,13},{13,9},{2,6},{6,2},{1... | collective-permute-start | bytes 1572872 | tf_op jit(solution)/shard_map/ppermute | solution.py:121
  35.7 13.7 %collective-permute-start.7 = (bf16[128,2048]{1,0:T(8,128)(2,1)S(1)}, bf16[128,2048]{1,0:T(8,128)(2,1)S(1)}, u32[]{:S(2)}, u32[]{:S(2)}) collective-permute-start(bf16[128,2048]{1,0:T(8,128)(2,1)S(1)} %get-tuple-element.71), channel_id=1, source_target_pairs={{0,1},{1,0},{2,3},{3,2},{4,5},{5,4},{6,7},{7,6},{8,9},{9,8},{10,11... | collective-permute-start | bytes 1572872 | tf_op jit(solution)/shard_map/ppermute | solution.py:121
  36.0 14.3 %collective-permute-start.8 = (bf16[128,2048]{1,0:T(8,128)(2,1)S(1)}, bf16[128,2048]{1,0:T(8,128)(2,1)S(1)}, u32[]{:S(2)}, u32[]{:S(2)}) collective-permute-start(bf16[128,2048]{1,0:T(8,128)(2,1)S(1)} %get-tuple-element.72), channel_id=1, source_target_pairs={{0,1},{1,0},{2,3},{3,2},{4,5},{5,4},{6,7},{7,6},{8,9},{9,8},{10,11... | collective-permute-start | bytes 1572872 | tf_op jit(solution)/shard_map/ppermute | solution.py:121
  36.3 17.0 %collective-permute-start.11 = (bf16[128,2048]{1,0:T(8,128)(2,1)S(1)}, bf16[128,2048]{1,0:T(8,128)(2,1)}, u32[]{:S(2)}, u32[]{:S(2)}) collective-permute-start(bf16[128,2048]{1,0:T(8,128)(2,1)S(1)} %get-tuple-element.71), channel_id=1, source_target_pairs={{0,2},{2,0},{1,3},{3,1},{4,6},{6,4},{5,7},{7,5},{8,10},{10,8},{9,1... | collective-permute-start | bytes 1572872 | tf_op jit(solution)/shard_map/ppermute | solution.py:121
  51.1 13.9 %collective-permute-start.9 = (bf16[128,2048]{1,0:T(8,128)(2,1)}, bf16[128,2048]{1,0:T(8,128)(2,1)}, u32[]{:S(2)}, u32[]{:S(2)}) collective-permute-start(bf16[128,2048]{1,0:T(8,128)(2,1)} %get-tuple-element.41), channel_id=1, source_target_pairs={{0,4},{4,0},{8,12},{12,8},{1,5},{5,1},{9,13},{13,9},{2,6},{6,2},{1... | collective-permute-start | bytes 1572872 | tf_op jit(solution)/shard_map/ppermute | solution.py:121
  51.8 13.6 %collective-permute-start.14 = (bf16[128,2048]{1,0:T(8,128)(2,1)}, bf16[128,2048]{1,0:T(8,128)(2,1)}, u32[]{:S(2)}, u32[]{:S(2)}) collective-permute-start(bf16[128,2048]{1,0:T(8,128)(2,1)} %collective-permute-done.6), channel_id=1, source_target_pairs={{0,2},{2,0},{1,3},{3,1},{4,6},{6,4},{5,7},{7,5},{8,10},{10,8},{9,1... | collective-permute-start | bytes 1572872 | tf_op jit(solution)/shard_map/ppermute | solution.py:121
  53.3 15.8 %collective-permute-start.12 = (bf16[128,2048]{1,0:T(8,128)(2,1)}, bf16[128,2048]{1,0:T(8,128)(2,1)}, u32[]{:S(2)}, u32[]{:S(2)}) collective-permute-start(bf16[128,2048]{1,0:T(8,128)(2,1)} %collective-permute-done.11), channel_id=1, source_target_pairs={{0,1},{1,0},{2,3},{3,2},{4,5},{5,4},{6,7},{7,6},{8,9},{9,8},{10,11... | collective-permute-start | bytes 1572872 | tf_op jit(solution)/shard_map/ppermute | solution.py:121
  53.3 15.8 %collective-permute-start.13 = (bf16[128,2048]{1,0:T(8,128)(2,1)}, bf16[128,2048]{1,0:T(8,128)(2,1)}, u32[]{:S(2)}, u32[]{:S(2)}) collective-permute-start(bf16[128,2048]{1,0:T(8,128)(2,1)} %collective-permute-done.6), channel_id=1, source_target_pairs={{0,1},{1,0},{2,3},{3,2},{4,5},{5,4},{6,7},{7,6},{8,9},{9,8},{10,11... | collective-permute-start | bytes 1572872 | tf_op jit(solution)/shard_map/ppermute | solution.py:121
  66.5 28.7 %collective-permute-start.16 = (bf16[128,2048]{1,0:T(8,128)(2,1)S(1)}, bf16[128,2048]{1,0:T(8,128)(2,1)S(1)}, u32[]{:S(2)}, u32[]{:S(2)}) collective-permute-start(bf16[128,2048]{1,0:T(8,128)(2,1)S(1)} %dynamic-slice_bitcast_fusion), channel_id=1, source_target_pairs={{0,12},{4,8},{8,4},{12,0},{1,13},{5,9},{9,5},{13,1},{2,14},{6,10},... | collective-permute-start | bytes 1572872 | tf_op jit(solution)/shard_map/ppermute | solution.py:121
  111.4 12.4 %collective-permute-start.25 = (bf16[128,2048]{1,0:T(8,128)(2,1)S(1)}, bf16[128,2048]{1,0:T(8,128)(2,1)S(1)}, u32[]{:S(2)}, u32[]{:S(2)}) collective-permute-start(bf16[128,2048]{1,0:T(8,128)(2,1)S(1)} %get-tuple-element.54.refs_0_), channel_id=1, source_target_pairs={{0,4},{4,0},{8,12},{12,8},{1,5},{5,1},{9,13},{13,9},{2,6},{6,2},{1... | collective-permute-start | bytes 1572872 | tf_op jit(solution)/shard_map/ppermute | solution.py:121
  111.8 12.0 %collective-permute-start.26 = (bf16[128,2048]{1,0:T(8,128)(2,1)S(1)}, bf16[128,2048]{1,0:T(8,128)(2,1)S(1)}, u32[]{:S(2)}, u32[]{:S(2)}) collective-permute-start(bf16[128,2048]{1,0:T(8,128)(2,1)S(1)} %get-tuple-element.55), channel_id=1, source_target_pairs={{0,2},{2,0},{1,3},{3,1},{4,6},{6,4},{5,7},{7,5},{8,10},{10,8},{9,1... | collective-permute-start | bytes 1572872 | tf_op jit(solution)/shard_map/ppermute | solution.py:121
  113.3 10.6 %collective-permute-start.27 = (bf16[128,2048]{1,0:T(8,128)(2,1)S(1)}, bf16[128,2048]{1,0:T(8,128)(2,1)S(1)}, u32[]{:S(2)}, u32[]{:S(2)}) collective-permute-start(bf16[128,2048]{1,0:T(8,128)(2,1)S(1)} %get-tuple-element.55), channel_id=1, source_target_pairs={{4,8},{8,4},{5,9},{9,5},{6,10},{10,6},{7,11},{11,7},{20,24},{24,20... | collective-permute-start | bytes 1572872 | tf_op jit(solution)/shard_map/ppermute | solution.py:674
  114.0 16.6 %collective-permute-start.30 = (bf16[128,2048]{1,0:T(8,128)(2,1)S(1)}, bf16[128,2048]{1,0:T(8,128)(2,1)S(1)}, u32[]{:S(2)}, u32[]{:S(2)}) collective-permute-start(bf16[128,2048]{1,0:T(8,128)(2,1)S(1)} %get-tuple-element.54.refs_0_), channel_id=1, source_target_pairs={{0,1},{1,0},{2,3},{3,2},{4,5},{5,4},{6,7},{7,6},{8,9},{9,8},{10,11... | collective-permute-start | bytes 1572872 | tf_op jit(solution)/shard_map/ppermute | solution.py:121
  114.0 16.6 %collective-permute-start.31 = (bf16[128,2048]{1,0:T(8,128)(2,1)S(1)}, bf16[128,2048]{1,0:T(8,128)(2,1)S(1)}, u32[]{:S(2)}, u32[]{:S(2)}) collective-permute-start(bf16[128,2048]{1,0:T(8,128)(2,1)S(1)} %get-tuple-element.55), channel_id=1, source_target_pairs={{0,1},{1,0},{2,3},{3,2},{4,5},{5,4},{6,7},{7,6},{8,9},{9,8},{10,11... | collective-permute-start | bytes 1572872 | tf_op jit(solution)/shard_map/ppermute | solution.py:121
  123.8 17.6 %collective-permute-start.32 = (bf16[128,2048]{1,0:T(8,128)(2,1)S(1)}, bf16[128,2048]{1,0:T(8,128)(2,1)S(1)}, u32[]{:S(2)}, u32[]{:S(2)}) collective-permute-start(bf16[128,2048]{1,0:T(8,128)(2,1)S(1)} %get-tuple-element.55), channel_id=1, source_target_pairs={{0,4},{4,0},{8,12},{12,8},{1,5},{5,1},{9,13},{13,9},{2,6},{6,2},{1... | collective-permute-start | bytes 1572872 | tf_op jit(solution)/shard_map/ppermute | solution.py:121
  128.6 14.9 %collective-permute-start.28 = (bf16[128,2048]{1,0:T(8,128)(2,1)S(1)}, bf16[128,2048]{1,0:T(8,128)(2,1)S(1)}, u32[]{:S(2)}, u32[]{:S(2)}) collective-permute-start(bf16[128,2048]{1,0:T(8,128)(2,1)S(1)} %get-tuple-element.54.refs_0_), channel_id=1, source_target_pairs={{0,2},{2,0},{1,3},{3,1},{4,6},{6,4},{5,7},{7,5},{8,10},{10,8},{9,1... | collective-permute-start | bytes 1572872 | tf_op jit(solution)/shard_map/ppermute | solution.py:121
  129.1 21.2 %collective-permute-start.37 = (bf16[128,2048]{1,0:T(8,128)(2,1)S(1)}, bf16[128,2048]{1,0:T(8,128)(2,1)S(1)}, u32[]{:S(2)}, u32[]{:S(2)}) collective-permute-start(bf16[128,2048]{1,0:T(8,128)(2,1)S(1)} %collective-permute-done.25), channel_id=1, source_target_pairs={{0,2},{2,0},{1,3},{3,1},{4,6},{6,4},{5,7},{7,5},{8,10},{10,8},{9,1... | collective-permute-start | bytes 1572872 | tf_op jit(solution)/shard_map/ppermute | solution.py:121
  130.6 19.7 %collective-permute-start.38 = (bf16[128,2048]{1,0:T(8,128)(2,1)S(1)}, bf16[128,2048]{1,0:T(8,128)(2,1)S(1)}, u32[]{:S(2)}, u32[]{:S(2)}) collective-permute-start(bf16[128,2048]{1,0:T(8,128)(2,1)S(1)} %collective-permute-done.26), channel_id=1, source_target_pairs={{0,4},{4,0},{8,12},{12,8},{1,5},{5,1},{9,13},{13,9},{2,6},{6,2},{1... | collective-permute-start | bytes 1572872 | tf_op jit(solution)/shard_map/ppermute | solution.py:121
  130.6 20.2 %collective-permute-start.33 = (bf16[128,2048]{1,0:T(8,128)(2,1)S(1)}, bf16[128,2048]{1,0:T(8,128)(2,1)S(1)}, u32[]{:S(2)}, u32[]{:S(2)}) collective-permute-start(bf16[128,2048]{1,0:T(8,128)(2,1)S(1)} %collective-permute-done.25), channel_id=1, source_target_pairs={{0,1},{1,0},{2,3},{3,2},{4,5},{5,4},{6,7},{7,6},{8,9},{9,8},{10,11... | collective-permute-start | bytes 1572872 | tf_op jit(solution)/shard_map/ppermute | solution.py:121
  141.4 9.5 %collective-permute-start.36 = (bf16[128,2048]{1,0:T(8,128)(2,1)S(1)}, bf16[128,2048]{1,0:T(8,128)(2,1)S(1)}, u32[]{:S(2)}, u32[]{:S(2)}) collective-permute-start(bf16[128,2048]{1,0:T(8,128)(2,1)S(1)} %collective-permute-done.26), channel_id=1, source_target_pairs={{0,1},{1,0},{2,3},{3,2},{4,5},{5,4},{6,7},{7,6},{8,9},{9,8},{10,11... | collective-permute-start | bytes 1572872 | tf_op jit(solution)/shard_map/ppermute | solution.py:121
  143.4 10.7 %collective-permute-start.34 = (bf16[128,2048]{1,0:T(8,128)(2,1)S(1)}, bf16[128,2048]{1,0:T(8,128)(2,1)S(1)}, u32[]{:S(2)}, u32[]{:S(2)}) collective-permute-start(bf16[128,2048]{1,0:T(8,128)(2,1)S(1)} %collective-permute-done.32), channel_id=1, source_target_pairs={{0,1},{1,0},{2,3},{3,2},{4,5},{5,4},{6,7},{7,6},{8,9},{9,8},{10,11... | collective-permute-start | bytes 1572872 | tf_op jit(solution)/shard_map/ppermute | solution.py:121
  150.9 18.2 %collective-permute-start.29 = (bf16[128,2048]{1,0:T(8,128)(2,1)S(1)}, bf16[128,2048]{1,0:T(8,128)(2,1)S(1)}, u32[]{:S(2)}, u32[]{:S(2)}) collective-permute-start(bf16[128,2048]{1,0:T(8,128)(2,1)S(1)} %get-tuple-element.55), channel_id=1, source_target_pairs={{0,12},{12,0},{1,13},{13,1},{2,14},{14,2},{3,15},{15,3},{16,28},{2... | collective-permute-start | bytes 1572872 | tf_op jit(solution)/shard_map/ppermute | solution.py:686
  166.0 10.5 %collective-permute-start.42 = (bf16[64,2048]{1,0:T(8,128)(2,1)S(1)}, bf16[64,2048]{1,0:T(8,128)(2,1)}, u32[]{:S(2)}, u32[]{:S(2)}) collective-permute-start(bf16[64,2048]{1,0:T(8,128)(2,1)S(1)} %get-tuple-element.59), channel_id=1, source_target_pairs={{0,12},{4,8},{8,4},{12,0},{1,13},{5,9},{9,5},{13,1},{2,14},{6,10},... | collective-permute-start | bytes 786440 | tf_op jit(solution)/shard_map/ppermute | solution.py:121
  168.6 26.1 %collective-permute-start.45 = (bf16[128,2048]{1,0:T(8,128)(2,1)S(1)}, bf16[128,2048]{1,0:T(8,128)(2,1)S(1)}, u32[]{:S(2)}, u32[]{:S(2)}) collective-permute-start(bf16[128,2048]{1,0:T(8,128)(2,1)S(1)} %get-tuple-element.56.refs_0_), channel_id=1, source_target_pairs={{0,2},{2,0},{1,3},{3,1},{4,6},{6,4},{5,7},{7,5},{8,10},{10,8},{9,1... | collective-permute-start | bytes 1572872 | tf_op jit(solution)/shard_map/ppermute | solution.py:121
  176.4 7.4 %collective-permute-start.48 = (f32[8,128]{1,0:T(8,128)S(1)}, f32[8,128]{1,0:T(8,128)S(1)}, u32[]{:S(2)}, u32[]{:S(2)}) collective-permute-start(f32[8,128]{1,0:T(8,128)S(1)} %add.66), channel_id=1, source_target_pairs={{0,4},{4,0},{8,12},{12,8},{1,5},{5,1},{9,13},{13,9},{2,6},{6,2},{1... | collective-permute-start | bytes 12296 | tf_op jit(solution)/shard_map/ppermute | solution.py:121
  180.8 14.4 %collective-permute-start.41 = (bf16[128,2048]{1,0:T(8,128)(2,1)S(1)}, bf16[128,2048]{1,0:T(8,128)(2,1)S(1)}, u32[]{:S(2)}, u32[]{:S(2)}) collective-permute-start(bf16[128,2048]{1,0:T(8,128)(2,1)S(1)} %broadcast_select_fusion.refs_2_), channel_id=1, source_target_pairs={{0,2},{2,0},{1,3},{3,1},{4,6},{6,4},{5,7},{7,5},{8,10},{10,8},{9,1... | collective-permute-start | bytes 1572872 | tf_op jit(solution)/shard_map/ppermute | solution.py:121
  183.8 9.4 %collective-permute-start.43 = (bf16[64,2048]{1,0:T(8,128)(2,1)S(1)}, bf16[64,2048]{1,0:T(8,128)(2,1)}, u32[]{:S(2)}, u32[]{:S(2)}) collective-permute-start(bf16[64,2048]{1,0:T(8,128)(2,1)S(1)} %get-tuple-element.60), channel_id=1, source_target_pairs={{0,12},{4,8},{8,4},{12,0},{1,13},{5,9},{9,5},{13,1},{2,14},{6,10},... | collective-permute-start | bytes 786440 | tf_op jit(solution)/shard_map/ppermute | solution.py:121
  194.7 9.4 %collective-permute-start.46 = (bf16[64,2048]{1,0:T(8,128)(2,1)}, bf16[64,2048]{1,0:T(8,128)(2,1)}, u32[]{:S(2)}, u32[]{:S(2)}) collective-permute-start(bf16[64,2048]{1,0:T(8,128)(2,1)} %collective-permute-done.42.refs_2_), channel_id=1, source_target_pairs={{0,2},{2,0},{1,3},{3,1},{4,6},{6,4},{5,7},{7,5},{8,10},{10,8},{9,1... | collective-permute-start | bytes 786440 | tf_op jit(solution)/shard_map/ppermute | solution.py:121
  195.2 11.5 %collective-permute-start.44 = (bf16[64,2048]{1,0:T(8,128)(2,1)}, bf16[64,2048]{1,0:T(8,128)(2,1)S(1)}, u32[]{:S(2)}, u32[]{:S(2)}) collective-permute-start(bf16[64,2048]{1,0:T(8,128)(2,1)} %collective-permute-done.43.refs_3_), channel_id=1, source_target_pairs={{0,2},{2,0},{1,3},{3,1},{4,6},{6,4},{5,7},{7,5},{8,10},{10,8},{9,1... | collective-permute-start | bytes 786440 | tf_op jit(solution)/shard_map/ppermute | solution.py:121
  (45 other events, 315.3 us)

commit v16 on v15

--- a/solution.py
+++ b/solution.py
@@ -159,7 +159,7 @@
     else:
         hd_own, hd_far, psi_in, off_in, stats_in, near_out, far_out, late_out, stats_out = refs[:9]
         refs = refs[9:]
-    field, images, left, diag, sems = refs
+    field, images, left, diag, parts, sems = refs
     z, x, c = place()
     sectors, block, width = field.shape
     table = right.shape[1]
@@ -177,19 +177,27 @@
     for at in range(2):
         begin(left_own.at[pl.ds(rows[at] * links, links)], left.at[0, pl.ds(at * links, links)])
     begin(left_other.at[pl.ds(table // 2, 2 * links)], left.at[1])
-    if not first:
+    if first:
+        for at, mix in enumerate((mix_a, mix_b)):
+            begin(mix.at[pl.ds(0, parts.shape[1]), pl.ds(width, LANES)], parts.at[at])
+    else:
         begin(hd_own.at[x], diag.at[0])
         begin(hd_far, diag.at[1])
 
     def allowed(a, q, value):
         return lax.select(pattern[a, q] != 0, value, jnp.zeros_like(value))
 
+    later = len(copies)
     for piece, offsets in zip(pieces, plan):
         for at, (dz, dx, dc, start, tall) in enumerate(offsets):
             row = row_of(dz, dx, dc)
+            if first:
+                begin(piece.at[at], field.at[row, pl.ds(start, tall)])
+                continue
             for line in range(0, tall, 16):
-                value = piece[at, line : line + 16, :]
-                field[row, start + line : start + line + 16, :] = value
+                field[row, start + line : start + line + 16, :] = piece[at, line : line + 16, :]
+    for copy in copies[later:]:
+        copy.wait()
 
     def right_col(term, b, j):
         return cols_other[j, b] if term else right_cols[j, 0, b]
@@ -231,7 +239,7 @@
         return carry
 
     lax.fori_loop(0, sectors // pair, image, 0, unroll=2)
-    for copy in copies:
+    for copy in copies[:later]:
         copy.wait()
 
     step = 2
@@ -281,7 +289,7 @@
 
     sums = list(lax.fori_loop(0, sectors // step, column, (zero,) * (2 if first else 3)))
     if first:
-        far_weight = sum(mix[0:48, width:].astype(jnp.float32) for mix in (mix_a, mix_b))
+        far_weight = (parts[0] + parts[1]).astype(jnp.float32)
         sums[1] += weight_own[...] + (far_weight[0:8] + far_weight[16:24] + far_weight[32:40])
     stats_out[...] = jnp.zeros_like(stats_out)
     for at, value in enumerate(sums):
@@ -300,22 +308,23 @@
     some = jax.ShapeDtypeStruct((block // 2, width), jnp.bfloat16)
     stats = jax.ShapeDtypeStruct((8, LANES), jnp.float32)
     out_shape = (rows, rows, stats) if first else (one, some, some, stats)
-    extra_specs = [VMEM] * 3 if first else [ANY, ANY, VMEM, VMEM, VMEM]
+    extra_specs = [ANY, ANY, VMEM] if first else [ANY, ANY, VMEM, VMEM, VMEM]
     inner = 2 * 2 * sectors * 2 * links * links * block * block * block
     outer = 2 * 2 * 2 * links * block * block * width
     return pl.pallas_call(
         functools.partial(operate_kernel, first, plan),
         out_shape=out_shape,
-        in_specs=[SMEM, SMEM, SMEM, SMEM, VMEM, ANY, ANY] + [VMEM] * len(pieces) + extra_specs,
+        in_specs=[SMEM, SMEM, SMEM, SMEM, VMEM, ANY, ANY] + [ANY if first else VMEM] * len(pieces) + extra_specs,
         out_specs=(VMEM,) * len(out_shape),
         scratch_shapes=[
             pltpu.VMEM((sectors, block, width), jnp.bfloat16),
             pltpu.VMEM((2, 2 * links * block, width), jnp.bfloat16),
             pltpu.VMEM((2, 2 * links, block, block), jnp.bfloat16),
             pltpu.VMEM((2, block, width), jnp.bfloat16),
-            pltpu.SemaphoreType.DMA((5,)),
+            pltpu.VMEM((2, 48, LANES), jnp.bfloat16),
+            pltpu.SemaphoreType.DMA((5 + len(plan),)),
         ],
-        compiler_params=pltpu.CompilerParams(vmem_limit_bytes=OPERATE_LIMIT),
+        compiler_params=pltpu.CompilerParams(vmem_limit_bytes=PREPARE_LIMIT if first else OPERATE_LIMIT),
         cost_estimate=pl.CostEstimate(
             flops=inner + outer if first else 0,
             bytes_accessed=16 * 1024 * 1024 if first else 1024,

time: 210 us -> 205 us (0.976)
  local copies, waits for them, and re-layouts: 15.6 us -> 6.5 us
  other arithmetic: 4.4 us -> 6.88 us
  Pallas kernels: 38 us -> 40.2 us
    unnamed x50 -> x42, local copies, waits for them, and re-layouts: 15.5 us -> 6.32 us
    pallas_call x2, Pallas kernels: 24.8 us -> 27 us  [operate(): pl.pallas_call(functools.partial(operate_kernel, first, plan), out_shape=...]
  transfers between devices with their start and end apart: 52 -> 52, of which waited for: 27 -> 27; matrix products, arithmetic and copies ran while one was open for 2% -> 3% of each run, Pallas kernels for 15% -> 16%
where the time goes in v16:
time: 205 us; the launch traced here: 203 us
  waiting for transfers between devices  97.6 us (48%)
  starting transfers between devices  50.3 us (25%)
  Pallas kernels  40.2 us (20%)
  other arithmetic  6.88 us (3%)
  local copies, waits for them, and re-layouts  6.5 us (3%)
    ppermute x42, waiting for transfers between devices, across(): return lax.ppermute(value, axis, [(i, i ^ distance) for i in range(size)])  71.7 us
    ppermute x42, starting transfers between devices, across(): return lax.ppermute(value, axis, [(i, i ^ distance) for i in range(size)])  35.3 us
    pallas_call x2, Pallas kernels, operate(): pl.pallas_call(functools.partial(operate_kernel, first, plan), out_shape=...  27 us
    ppermute x1, waiting for transfers between devices, shards(): mix_b = lax.ppermute(mix_b, 'blk', [(0, 1), (1, 3), (3, 2), (2, 0)])  12.6 us
    ppermute x1, waiting for transfers between devices, shards(): mix_a = lax.ppermute(mix_a, 'blk', [(0, 2), (2, 3), (3, 1), (1, 0)])  7.08 us
    ppermute x6, starting transfers between devices, share(): lax.ppermute(pair, axes, [(i, i ^ distance) for i in range(count)])  6.98 us
    unnamed x42, local copies, waits for them, and re-layouts  6.32 us
    ppermute x6, waiting for transfers between devices, share(): lax.ppermute(pair, axes, [(i, i ^ distance) for i in range(count)])  6.17 us
  transfers between devices with their start and end apart: 52, of which 27 were waited for; matrix products, arithmetic and copies ran while one was open for 3% of the time, Pallas kernels for 16%

profile of v16, /device:TPU:0, one launch (start us, length us, event | category | flops | bytes accessed | tf_op | source)
XLA Modules:
  0.0 202.5 jit_solution(7971441049802749555)
XLA Ops:
  0.6 4.3 %prepare.1 = (bf16[128,2176]{1,0:T(8,128)(2,1)}, bf16[128,2176]{1,0:T(8,128)(2,1)}, bf16[31,128,128]{2,1,0:T(8,128)(2,1)}, f32[8,128]{1,0:T(8,128)}) custom-call(s32[16,16]{1,0:T(8,128)} %pattern.5, bf16[2,2,128,2048]{3,2,1,0:T(8,128)(2,1)} %bitcast.109, bf16[2,128,2048]{2,1,0:T(8,128)(2,1)} %bitcast.76, bf16[48,128,128]{2,1,0:T(8,128)(2,1)} %bitcast.80, ...), custom_call_target="tpu_custom_call" | custom-call | tf_op jit(solution)/shard_map/prepare/pallas_call | solution.py:444
  4.9 4.1 %collective-permute-start.1 = (bf16[128,2176]{1,0:T(8,128)(2,1)}, bf16[128,2176]{1,0:T(8,128)(2,1)}, u32[]{:S(2)}, u32[]{:S(2)}) collective-permute-start(bf16[128,2176]{1,0:T(8,128)(2,1)} %get-tuple-element.36), channel_id=1, source_target_pairs={{0,8},{8,12},{12,4},{4,0},{1,9},{9,13},{13,5},{5,1},{2,10},{10,14}... | collective-permute-start | bytes 1671176 | tf_op jit(solution)/shard_map/ppermute | solution.py:589
  9.0 1.5 collective-permute-start
  13.0 1.5 collective-permute-done.3
  15.3 7.1 %collective-permute-done.1.refs_16_ = bf16[128,2176]{1,0:T(8,128)(2,1)} collective-permute-done((bf16[128,2176]{1,0:T(8,128)(2,1)}, bf16[128,2176]{1,0:T(8,128)(2,1)}, u32[]{:S(2)}, u32[]{:S(2)}) %collective-permute-start.1) | collective-permute-done | bytes 557088 | tf_op jit(solution)/shard_map/ppermute | solution.py:589
  22.4 12.6 %collective-permute-done.2.refs_17_ = bf16[128,2176]{1,0:T(8,128)(2,1)} collective-permute-done((bf16[128,2176]{1,0:T(8,128)(2,1)}, bf16[128,2176]{1,0:T(8,128)(2,1)}, u32[]{:S(2)}, u32[]{:S(2)}) %collective-permute-start.2) | collective-permute-done | bytes 557088 | tf_op jit(solution)/shard_map/ppermute | solution.py:590
  35.0 1.7 select_multiply_fusion
  40.9 1.7 arrange.1.right
  42.6 1.6 copy-done
  44.3 6.6 %collective-permute-done.6 = bf16[128,2048]{1,0:T(8,128)(2,1)} collective-permute-done((bf16[128,2048]{1,0:T(8,128)(2,1)S(1)}, bf16[128,2048]{1,0:T(8,128)(2,1)}, u32[]{:S(2)}, u32[]{:S(2)}) %collective-permute-start.6) | collective-permute-done | bytes 524320 | tf_op jit(solution)/shard_map/ppermute | solution.py:121
  53.6 10.6 %collective-permute-done.9 = bf16[128,2048]{1,0:T(8,128)(2,1)S(1)} collective-permute-done((bf16[128,2048]{1,0:T(8,128)(2,1)}, bf16[128,2048]{1,0:T(8,128)(2,1)S(1)}, u32[]{:S(2)}, u32[]{:S(2)}) %collective-permute-start.9) | collective-permute-done | bytes 524320 | tf_op jit(solution)/shard_map/ppermute | solution.py:121
  65.9 2.5 %collective-permute-start.16 = (bf16[128,2048]{1,0:T(8,128)(2,1)S(1)}, bf16[128,2048]{1,0:T(8,128)(2,1)S(1)}, u32[]{:S(2)}, u32[]{:S(2)}) collective-permute-start(bf16[128,2048]{1,0:T(8,128)(2,1)S(1)} %dynamic-slice_bitcast_fusion), channel_id=1, source_target_pairs={{0,12},{4,8},{8,4},{12,0},{1,13},{5,9},{9,5},{13,1},{2,14},{6,10},... | collective-permute-start | bytes 1572872 | tf_op jit(solution)/shard_map/ppermute | solution.py:121
  69.8 15.1 %operate_first.1 = (bf16[2,128,2048]{2,1,0:T(8,128)(2,1)}, bf16[2,128,2048]{2,1,0:T(8,128)(2,1)}, f32[8,128]{1,0:T(8,128)}) custom-call(s32[3,1,16]{2,1,0:T(1,128)} %bitcast.100, s32[3,1,16]{2,1,0:T(1,128)} %bitcast.103, s32[16,16]{1,0:T(8,128)} %bitcast_convert_fusion.cols_other, s32[16,16]{1,0:T(8,128)} %pattern.5, bf16[2,48,128,128]{3,2,1,0:T(8,128)(2,1)} %copy-done, ...), custom_call_target="tpu_custom_call" | custom-call | flops 3221225472 | bytes 16777216 | tf_op jit(solution)/shard_map/operate_first/pallas_call | solution.py:314
  87.1 1.5 collective-permute-start.18
  89.0 1.6 collective-permute-start.20
  96.0 2.1 %update.1 = (f32[2,128,2048]{2,1,0:T(8,128)S(1)}, f32[8,128]{1,0:T(8,128)S(1)}) custom-call(bf16[2,128,2048]{2,1,0:T(8,128)(2,1)S(1)} %copy-done.2, bf16[2,128,2048]{2,1,0:T(8,128)(2,1)S(1)} %copy-done.5, bf16[2,128,2048]{2,1,0:T(8,128)(2,1)S(1)} %bitcast.79, bf16[128,2048]{1,0:T(8,128)(2,1)S(1)} %collective-permute-done.16.hd_far.refs_17_, ...), custom_call_target="tpu_custom_call" | custom-call | tf_op jit(solution)/shard_map/update/pallas_call | solution.py:653
  100.0 1.6 collective-permute-start.23
  103.6 2.5 %collective-permute-done.24.refs_3_ = f32[2,8,128]{2,1,0:T(8,128)S(1)} collective-permute-done((f32[2,8,128]{2,1,0:T(8,128)S(1)}, f32[2,8,128]{2,1,0:T(8,128)S(1)}, u32[]{:S(2)}, u32[]{:S(2)}) %collective-permute-start.24) | collective-permute-done | bytes 8224 | tf_op jit(solution)/shard_map/ppermute | solution.py:130
  110.0 9.1 %collective-permute-done.25 = bf16[128,2048]{1,0:T(8,128)(2,1)S(1)} collective-permute-done((bf16[128,2048]{1,0:T(8,128)(2,1)S(1)}, bf16[128,2048]{1,0:T(8,128)(2,1)S(1)}, u32[]{:S(2)}, u32[]{:S(2)}) %collective-permute-start.25) | collective-permute-done | bytes 524320 | tf_op jit(solution)/shard_map/ppermute | solution.py:121
  119.3 4.7 %collective-permute-start.32 = (bf16[128,2048]{1,0:T(8,128)(2,1)S(1)}, bf16[128,2048]{1,0:T(8,128)(2,1)S(1)}, u32[]{:S(2)}, u32[]{:S(2)}) collective-permute-start(bf16[128,2048]{1,0:T(8,128)(2,1)S(1)} %get-tuple-element.55), channel_id=1, source_target_pairs={{0,4},{4,0},{8,12},{12,8},{1,5},{5,1},{9,13},{13,9},{2,6},{6,2},{1... | collective-permute-start | bytes 1572872 | tf_op jit(solution)/shard_map/ppermute | solution.py:121
  126.0 10.7 %collective-permute-done.32 = bf16[128,2048]{1,0:T(8,128)(2,1)S(1)} collective-permute-done((bf16[128,2048]{1,0:T(8,128)(2,1)S(1)}, bf16[128,2048]{1,0:T(8,128)(2,1)S(1)}, u32[]{:S(2)}, u32[]{:S(2)}) %collective-permute-start.32) | collective-permute-done | bytes 524320 | tf_op jit(solution)/shard_map/ppermute | solution.py:121
  136.8 2.0 collective-permute-done.28.refs_1_
  138.8 6.9 %collective-permute-done.37 = bf16[128,2048]{1,0:T(8,128)(2,1)S(1)} collective-permute-done((bf16[128,2048]{1,0:T(8,128)(2,1)S(1)}, bf16[128,2048]{1,0:T(8,128)(2,1)S(1)}, u32[]{:S(2)}, u32[]{:S(2)}) %collective-permute-start.37) | collective-permute-done | bytes 524320 | tf_op jit(solution)/shard_map/ppermute | solution.py:121
  146.3 3.3 %collective-permute-start.29 = (bf16[128,2048]{1,0:T(8,128)(2,1)S(1)}, bf16[128,2048]{1,0:T(8,128)(2,1)S(1)}, u32[]{:S(2)}, u32[]{:S(2)}) collective-permute-start(bf16[128,2048]{1,0:T(8,128)(2,1)S(1)} %get-tuple-element.55), channel_id=1, source_target_pairs={{0,12},{12,0},{1,13},{13,1},{2,14},{14,2},{3,15},{15,3},{16,28},{2... | collective-permute-start | bytes 1572872 | tf_op jit(solution)/shard_map/ppermute | solution.py:695
  149.6 11.9 %operate_second.1 = (bf16[128,2048]{1,0:T(8,128)(2,1)S(1)}, bf16[64,2048]{1,0:T(8,128)(2,1)S(1)}, bf16[64,2048]{1,0:T(8,128)(2,1)S(1)}, f32[8,128]{1,0:T(8,128)S(1)}) custom-call(s32[3,1,16]{2,1,0:T(1,128)S(1)} %bitcast.101, s32[3,1,16]{2,1,0:T(1,128)S(1)} %bitcast.104, s32[16,16]{1,0:T(8,128)S(1)} %copy-done.7, s32[16,16]{1,0:T(8,128)S(1)} %copy-done.6, ...), custom_call_target="tpu_custom_call" | custom-call | bytes 1024 | tf_op jit(solution)/shard_map/operate_second/pallas_call | solution.py:314
  161.6 2.5 %collective-permute-start.42 = (bf16[64,2048]{1,0:T(8,128)(2,1)S(1)}, bf16[64,2048]{1,0:T(8,128)(2,1)}, u32[]{:S(2)}, u32[]{:S(2)}) collective-permute-start(bf16[64,2048]{1,0:T(8,128)(2,1)S(1)} %get-tuple-element.59), channel_id=1, source_target_pairs={{0,12},{4,8},{8,4},{12,0},{1,13},{5,9},{9,5},{13,1},{2,14},{6,10},... | collective-permute-start | bytes 786440 | tf_op jit(solution)/shard_map/ppermute | solution.py:121
  165.3 6.8 %collective-permute-done.42.refs_2_ = bf16[64,2048]{1,0:T(8,128)(2,1)} collective-permute-done((bf16[64,2048]{1,0:T(8,128)(2,1)S(1)}, bf16[64,2048]{1,0:T(8,128)(2,1)}, u32[]{:S(2)}, u32[]{:S(2)}) %collective-permute-start.42) | collective-permute-done | bytes 262176 | tf_op jit(solution)/shard_map/ppermute | solution.py:121
  172.1 4.1 %collective-permute-start.48 = (f32[8,128]{1,0:T(8,128)S(1)}, f32[8,128]{1,0:T(8,128)S(1)}, u32[]{:S(2)}, u32[]{:S(2)}) collective-permute-start(f32[8,128]{1,0:T(8,128)S(1)} %add.66), channel_id=1, source_target_pairs={{0,4},{4,0},{8,12},{12,8},{1,5},{5,1},{9,13},{13,9},{2,6},{6,2},{1... | collective-permute-start | bytes 12296 | tf_op jit(solution)/shard_map/ppermute | solution.py:121
  176.8 2.4 %collective-permute-start.50 = (f32[8,128]{1,0:T(8,128)S(1)}, f32[8,128]{1,0:T(8,128)S(1)}, u32[]{:S(2)}, u32[]{:S(2)}) collective-permute-start(f32[8,128]{1,0:T(8,128)S(1)} %add.66), channel_id=1, source_target_pairs={{0,12},{4,8},{8,4},{12,0},{1,13},{5,9},{9,5},{13,1},{2,14},{6,10},... | collective-permute-start | bytes 12296 | tf_op jit(solution)/shard_map/ppermute | solution.py:121
  182.3 6.1 %collective-permute-done.43.refs_3_ = bf16[64,2048]{1,0:T(8,128)(2,1)} collective-permute-done((bf16[64,2048]{1,0:T(8,128)(2,1)S(1)}, bf16[64,2048]{1,0:T(8,128)(2,1)}, u32[]{:S(2)}, u32[]{:S(2)}) %collective-permute-start.43) | collective-permute-done | bytes 262176 | tf_op jit(solution)/shard_map/ppermute | solution.py:121
  194.2 4.9 %collective-permute-done.46.refs_4_ = bf16[64,2048]{1,0:T(8,128)(2,1)} collective-permute-done((bf16[64,2048]{1,0:T(8,128)(2,1)}, bf16[64,2048]{1,0:T(8,128)(2,1)}, u32[]{:S(2)}, u32[]{:S(2)}) %collective-permute-start.46) | collective-permute-done | bytes 262176 | tf_op jit(solution)/shard_map/ppermute | solution.py:121
  199.1 2.4 %assemble.4.refs_1_ = bf16[2,2,128,2048]{3,2,1,0:T(8,128)(2,1)} custom-call(bf16[128,2048]{1,0:T(8,128)(2,1)S(1)} %get-tuple-element.56.refs_0_, bf16[128,2048]{1,0:T(8,128)(2,1)S(1)} %collective-permute-done.45.refs_1_, bf16[64,2048]{1,0:T(8,128)(2,1)} %collective-permute-done.42.refs_2_, bf16[64,2048]{1,0:T(8,128)(2,1)} %collective-permute-done.43.refs_3_, ...), custom_call_target="tpu_custom_call" | custom-call | tf_op jit(solution)/shard_map/assemble/pallas_call | solution.py:557
  (143 shorter events, 43.7 us)
Async XLA Ops:
  4.9 17.5 %collective-permute-start.1 = (bf16[128,2176]{1,0:T(8,128)(2,1)}, bf16[128,2176]{1,0:T(8,128)(2,1)}, u32[]{:S(2)}, u32[]{:S(2)}) collective-permute-start(bf16[128,2176]{1,0:T(8,128)(2,1)} %get-tuple-element.36), channel_id=1, source_target_pairs={{0,8},{8,12},{12,4},{4,0},{1,9},{9,13},{13,5},{5,1},{2,10},{10,14}... | collective-permute-start | bytes 1671176 | tf_op jit(solution)/shard_map/ppermute | solution.py:589
  9.0 26.0 %collective-permute-start.2 = (bf16[128,2176]{1,0:T(8,128)(2,1)}, bf16[128,2176]{1,0:T(8,128)(2,1)}, u32[]{:S(2)}, u32[]{:S(2)}) collective-permute-start(bf16[128,2176]{1,0:T(8,128)(2,1)} %get-tuple-element.37), channel_id=1, source_target_pairs={{0,4},{4,12},{12,8},{8,0},{1,5},{5,13},{13,9},{9,1},{2,6},{6,14},{... | collective-permute-start | bytes 1671176 | tf_op jit(solution)/shard_map/ppermute | solution.py:590
  9.0 26.0 %collective-permute-start = (bf16[31,128,128]{2,1,0:T(8,128)(2,1)}, bf16[31,128,128]{2,1,0:T(8,128)(2,1)S(1)}, u32[]{:S(2)}, u32[]{:S(2)}) collective-permute-start(bf16[31,128,128]{2,1,0:T(8,128)(2,1)} %get-tuple-element.35), channel_id=1, source_target_pairs={{0,2},{2,0},{1,3},{3,1},{4,6},{6,4},{5,7},{7,5},{8,10},{10,8},{9,1... | collective-permute-start | bytes 3047432 | tf_op jit(solution)/shard_map/ppermute | solution.py:121
  36.7 14.1 %collective-permute-start.6 = (bf16[128,2048]{1,0:T(8,128)(2,1)S(1)}, bf16[128,2048]{1,0:T(8,128)(2,1)}, u32[]{:S(2)}, u32[]{:S(2)}) collective-permute-start(bf16[128,2048]{1,0:T(8,128)(2,1)S(1)} %get-tuple-element.71), channel_id=1, source_target_pairs={{0,4},{4,0},{8,12},{12,8},{1,5},{5,1},{9,13},{13,9},{2,6},{6,2},{1... | collective-permute-start | bytes 1572872 | tf_op jit(solution)/shard_map/ppermute | solution.py:121
  37.5 13.4 %collective-permute-start.7 = (bf16[128,2048]{1,0:T(8,128)(2,1)S(1)}, bf16[128,2048]{1,0:T(8,128)(2,1)S(1)}, u32[]{:S(2)}, u32[]{:S(2)}) collective-permute-start(bf16[128,2048]{1,0:T(8,128)(2,1)S(1)} %get-tuple-element.71), channel_id=1, source_target_pairs={{0,1},{1,0},{2,3},{3,2},{4,5},{5,4},{6,7},{7,6},{8,9},{9,8},{10,11... | collective-permute-start | bytes 1572872 | tf_op jit(solution)/shard_map/ppermute | solution.py:121
  37.5 13.4 %collective-permute-start.8 = (bf16[128,2048]{1,0:T(8,128)(2,1)S(1)}, bf16[128,2048]{1,0:T(8,128)(2,1)S(1)}, u32[]{:S(2)}, u32[]{:S(2)}) collective-permute-start(bf16[128,2048]{1,0:T(8,128)(2,1)S(1)} %get-tuple-element.72), channel_id=1, source_target_pairs={{0,1},{1,0},{2,3},{3,2},{4,5},{5,4},{6,7},{7,6},{8,9},{9,8},{10,11... | collective-permute-start | bytes 1572872 | tf_op jit(solution)/shard_map/ppermute | solution.py:121
  38.0 15.1 %collective-permute-start.11 = (bf16[128,2048]{1,0:T(8,128)(2,1)S(1)}, bf16[128,2048]{1,0:T(8,128)(2,1)}, u32[]{:S(2)}, u32[]{:S(2)}) collective-permute-start(bf16[128,2048]{1,0:T(8,128)(2,1)S(1)} %get-tuple-element.71), channel_id=1, source_target_pairs={{0,2},{2,0},{1,3},{3,1},{4,6},{6,4},{5,7},{7,5},{8,10},{10,8},{9,1... | collective-permute-start | bytes 1572872 | tf_op jit(solution)/shard_map/ppermute | solution.py:121
  50.9 13.4 %collective-permute-start.9 = (bf16[128,2048]{1,0:T(8,128)(2,1)}, bf16[128,2048]{1,0:T(8,128)(2,1)S(1)}, u32[]{:S(2)}, u32[]{:S(2)}) collective-permute-start(bf16[128,2048]{1,0:T(8,128)(2,1)} %get-tuple-element.41), channel_id=1, source_target_pairs={{0,4},{4,0},{8,12},{12,8},{1,5},{5,1},{9,13},{13,9},{2,6},{6,2},{1... | collective-permute-start | bytes 1572872 | tf_op jit(solution)/shard_map/ppermute | solution.py:121
  51.6 13.2 %collective-permute-start.14 = (bf16[128,2048]{1,0:T(8,128)(2,1)}, bf16[128,2048]{1,0:T(8,128)(2,1)}, u32[]{:S(2)}, u32[]{:S(2)}) collective-permute-start(bf16[128,2048]{1,0:T(8,128)(2,1)} %collective-permute-done.6), channel_id=1, source_target_pairs={{0,2},{2,0},{1,3},{3,1},{4,6},{6,4},{5,7},{7,5},{8,10},{10,8},{9,1... | collective-permute-start | bytes 1572872 | tf_op jit(solution)/shard_map/ppermute | solution.py:121
  53.1 15.9 %collective-permute-start.12 = (bf16[128,2048]{1,0:T(8,128)(2,1)}, bf16[128,2048]{1,0:T(8,128)(2,1)S(1)}, u32[]{:S(2)}, u32[]{:S(2)}) collective-permute-start(bf16[128,2048]{1,0:T(8,128)(2,1)} %collective-permute-done.11), channel_id=1, source_target_pairs={{0,1},{1,0},{2,3},{3,2},{4,5},{5,4},{6,7},{7,6},{8,9},{9,8},{10,11... | collective-permute-start | bytes 1572872 | tf_op jit(solution)/shard_map/ppermute | solution.py:121
  53.1 15.9 %collective-permute-start.13 = (bf16[128,2048]{1,0:T(8,128)(2,1)}, bf16[128,2048]{1,0:T(8,128)(2,1)}, u32[]{:S(2)}, u32[]{:S(2)}) collective-permute-start(bf16[128,2048]{1,0:T(8,128)(2,1)} %collective-permute-done.6), channel_id=1, source_target_pairs={{0,1},{1,0},{2,3},{3,2},{4,5},{5,4},{6,7},{7,6},{8,9},{9,8},{10,11... | collective-permute-start | bytes 1572872 | tf_op jit(solution)/shard_map/ppermute | solution.py:121
  65.9 24.6 %collective-permute-start.16 = (bf16[128,2048]{1,0:T(8,128)(2,1)S(1)}, bf16[128,2048]{1,0:T(8,128)(2,1)S(1)}, u32[]{:S(2)}, u32[]{:S(2)}) collective-permute-start(bf16[128,2048]{1,0:T(8,128)(2,1)S(1)} %dynamic-slice_bitcast_fusion), channel_id=1, source_target_pairs={{0,12},{4,8},{8,4},{12,0},{1,13},{5,9},{9,5},{13,1},{2,14},{6,10},... | collective-permute-start | bytes 1572872 | tf_op jit(solution)/shard_map/ppermute | solution.py:121
  106.7 12.4 %collective-permute-start.25 = (bf16[128,2048]{1,0:T(8,128)(2,1)S(1)}, bf16[128,2048]{1,0:T(8,128)(2,1)S(1)}, u32[]{:S(2)}, u32[]{:S(2)}) collective-permute-start(bf16[128,2048]{1,0:T(8,128)(2,1)S(1)} %get-tuple-element.54.refs_0_), channel_id=1, source_target_pairs={{0,4},{4,0},{8,12},{12,8},{1,5},{5,1},{9,13},{13,9},{2,6},{6,2},{1... | collective-permute-start | bytes 1572872 | tf_op jit(solution)/shard_map/ppermute | solution.py:121
  107.3 12.0 %collective-permute-start.26 = (bf16[128,2048]{1,0:T(8,128)(2,1)S(1)}, bf16[128,2048]{1,0:T(8,128)(2,1)S(1)}, u32[]{:S(2)}, u32[]{:S(2)}) collective-permute-start(bf16[128,2048]{1,0:T(8,128)(2,1)S(1)} %get-tuple-element.55), channel_id=1, source_target_pairs={{0,2},{2,0},{1,3},{3,1},{4,6},{6,4},{5,7},{7,5},{8,10},{10,8},{9,1... | collective-permute-start | bytes 1572872 | tf_op jit(solution)/shard_map/ppermute | solution.py:121
  108.7 10.5 %collective-permute-start.27 = (bf16[128,2048]{1,0:T(8,128)(2,1)S(1)}, bf16[128,2048]{1,0:T(8,128)(2,1)S(1)}, u32[]{:S(2)}, u32[]{:S(2)}) collective-permute-start(bf16[128,2048]{1,0:T(8,128)(2,1)S(1)} %get-tuple-element.55), channel_id=1, source_target_pairs={{4,8},{8,4},{5,9},{9,5},{6,10},{10,6},{7,11},{11,7},{20,24},{24,20... | collective-permute-start | bytes 1572872 | tf_op jit(solution)/shard_map/ppermute | solution.py:683
  109.4 16.5 %collective-permute-start.30 = (bf16[128,2048]{1,0:T(8,128)(2,1)S(1)}, bf16[128,2048]{1,0:T(8,128)(2,1)S(1)}, u32[]{:S(2)}, u32[]{:S(2)}) collective-permute-start(bf16[128,2048]{1,0:T(8,128)(2,1)S(1)} %get-tuple-element.54.refs_0_), channel_id=1, source_target_pairs={{0,1},{1,0},{2,3},{3,2},{4,5},{5,4},{6,7},{7,6},{8,9},{9,8},{10,11... | collective-permute-start | bytes 1572872 | tf_op jit(solution)/shard_map/ppermute | solution.py:121
  109.5 16.5 %collective-permute-start.31 = (bf16[128,2048]{1,0:T(8,128)(2,1)S(1)}, bf16[128,2048]{1,0:T(8,128)(2,1)S(1)}, u32[]{:S(2)}, u32[]{:S(2)}) collective-permute-start(bf16[128,2048]{1,0:T(8,128)(2,1)S(1)} %get-tuple-element.55), channel_id=1, source_target_pairs={{0,1},{1,0},{2,3},{3,2},{4,5},{5,4},{6,7},{7,6},{8,9},{9,8},{10,11... | collective-permute-start | bytes 1572872 | tf_op jit(solution)/shard_map/ppermute | solution.py:121
  119.3 17.5 %collective-permute-start.32 = (bf16[128,2048]{1,0:T(8,128)(2,1)S(1)}, bf16[128,2048]{1,0:T(8,128)(2,1)S(1)}, u32[]{:S(2)}, u32[]{:S(2)}) collective-permute-start(bf16[128,2048]{1,0:T(8,128)(2,1)S(1)} %get-tuple-element.55), channel_id=1, source_target_pairs={{0,4},{4,0},{8,12},{12,8},{1,5},{5,1},{9,13},{13,9},{2,6},{6,2},{1... | collective-permute-start | bytes 1572872 | tf_op jit(solution)/shard_map/ppermute | solution.py:121
  123.9 14.9 %collective-permute-start.28 = (bf16[128,2048]{1,0:T(8,128)(2,1)S(1)}, bf16[128,2048]{1,0:T(8,128)(2,1)S(1)}, u32[]{:S(2)}, u32[]{:S(2)}) collective-permute-start(bf16[128,2048]{1,0:T(8,128)(2,1)S(1)} %get-tuple-element.54.refs_0_), channel_id=1, source_target_pairs={{0,2},{2,0},{1,3},{3,1},{4,6},{6,4},{5,7},{7,5},{8,10},{10,8},{9,1... | collective-permute-start | bytes 1572872 | tf_op jit(solution)/shard_map/ppermute | solution.py:121
  124.5 21.2 %collective-permute-start.37 = (bf16[128,2048]{1,0:T(8,128)(2,1)S(1)}, bf16[128,2048]{1,0:T(8,128)(2,1)S(1)}, u32[]{:S(2)}, u32[]{:S(2)}) collective-permute-start(bf16[128,2048]{1,0:T(8,128)(2,1)S(1)} %collective-permute-done.25), channel_id=1, source_target_pairs={{0,2},{2,0},{1,3},{3,1},{4,6},{6,4},{5,7},{7,5},{8,10},{10,8},{9,1... | collective-permute-start | bytes 1572872 | tf_op jit(solution)/shard_map/ppermute | solution.py:121
  126.0 19.7 %collective-permute-start.38 = (bf16[128,2048]{1,0:T(8,128)(2,1)S(1)}, bf16[128,2048]{1,0:T(8,128)(2,1)S(1)}, u32[]{:S(2)}, u32[]{:S(2)}) collective-permute-start(bf16[128,2048]{1,0:T(8,128)(2,1)S(1)} %collective-permute-done.26), channel_id=1, source_target_pairs={{0,4},{4,0},{8,12},{12,8},{1,5},{5,1},{9,13},{13,9},{2,6},{6,2},{1... | collective-permute-start | bytes 1572872 | tf_op jit(solution)/shard_map/ppermute | solution.py:121
  126.0 20.2 %collective-permute-start.33 = (bf16[128,2048]{1,0:T(8,128)(2,1)S(1)}, bf16[128,2048]{1,0:T(8,128)(2,1)S(1)}, u32[]{:S(2)}, u32[]{:S(2)}) collective-permute-start(bf16[128,2048]{1,0:T(8,128)(2,1)S(1)} %collective-permute-done.25), channel_id=1, source_target_pairs={{0,1},{1,0},{2,3},{3,2},{4,5},{5,4},{6,7},{7,6},{8,9},{9,8},{10,11... | collective-permute-start | bytes 1572872 | tf_op jit(solution)/shard_map/ppermute | solution.py:121
  136.8 9.5 %collective-permute-start.36 = (bf16[128,2048]{1,0:T(8,128)(2,1)S(1)}, bf16[128,2048]{1,0:T(8,128)(2,1)S(1)}, u32[]{:S(2)}, u32[]{:S(2)}) collective-permute-start(bf16[128,2048]{1,0:T(8,128)(2,1)S(1)} %collective-permute-done.26), channel_id=1, source_target_pairs={{0,1},{1,0},{2,3},{3,2},{4,5},{5,4},{6,7},{7,6},{8,9},{9,8},{10,11... | collective-permute-start | bytes 1572872 | tf_op jit(solution)/shard_map/ppermute | solution.py:121
  138.8 10.8 %collective-permute-start.34 = (bf16[128,2048]{1,0:T(8,128)(2,1)S(1)}, bf16[128,2048]{1,0:T(8,128)(2,1)S(1)}, u32[]{:S(2)}, u32[]{:S(2)}) collective-permute-start(bf16[128,2048]{1,0:T(8,128)(2,1)S(1)} %collective-permute-done.32), channel_id=1, source_target_pairs={{0,1},{1,0},{2,3},{3,2},{4,5},{5,4},{6,7},{7,6},{8,9},{9,8},{10,11... | collective-permute-start | bytes 1572872 | tf_op jit(solution)/shard_map/ppermute | solution.py:121
  146.3 18.4 %collective-permute-start.29 = (bf16[128,2048]{1,0:T(8,128)(2,1)S(1)}, bf16[128,2048]{1,0:T(8,128)(2,1)S(1)}, u32[]{:S(2)}, u32[]{:S(2)}) collective-permute-start(bf16[128,2048]{1,0:T(8,128)(2,1)S(1)} %get-tuple-element.55), channel_id=1, source_target_pairs={{0,12},{12,0},{1,13},{13,1},{2,14},{14,2},{3,15},{15,3},{16,28},{2... | collective-permute-start | bytes 1572872 | tf_op jit(solution)/shard_map/ppermute | solution.py:695
  161.6 10.5 %collective-permute-start.42 = (bf16[64,2048]{1,0:T(8,128)(2,1)S(1)}, bf16[64,2048]{1,0:T(8,128)(2,1)}, u32[]{:S(2)}, u32[]{:S(2)}) collective-permute-start(bf16[64,2048]{1,0:T(8,128)(2,1)S(1)} %get-tuple-element.59), channel_id=1, source_target_pairs={{0,12},{4,8},{8,4},{12,0},{1,13},{5,9},{9,5},{13,1},{2,14},{6,10},... | collective-permute-start | bytes 786440 | tf_op jit(solution)/shard_map/ppermute | solution.py:121
  164.1 25.8 %collective-permute-start.45 = (bf16[128,2048]{1,0:T(8,128)(2,1)S(1)}, bf16[128,2048]{1,0:T(8,128)(2,1)S(1)}, u32[]{:S(2)}, u32[]{:S(2)}) collective-permute-start(bf16[128,2048]{1,0:T(8,128)(2,1)S(1)} %get-tuple-element.56.refs_0_), channel_id=1, source_target_pairs={{0,2},{2,0},{1,3},{3,1},{4,6},{6,4},{5,7},{7,5},{8,10},{10,8},{9,1... | collective-permute-start | bytes 1572872 | tf_op jit(solution)/shard_map/ppermute | solution.py:121
  172.1 7.1 %collective-permute-start.48 = (f32[8,128]{1,0:T(8,128)S(1)}, f32[8,128]{1,0:T(8,128)S(1)}, u32[]{:S(2)}, u32[]{:S(2)}) collective-permute-start(f32[8,128]{1,0:T(8,128)S(1)} %add.66), channel_id=1, source_target_pairs={{0,4},{4,0},{8,12},{12,8},{1,5},{5,1},{9,13},{13,9},{2,6},{6,2},{1... | collective-permute-start | bytes 12296 | tf_op jit(solution)/shard_map/ppermute | solution.py:121
  176.2 14.3 %collective-permute-start.41 = (bf16[128,2048]{1,0:T(8,128)(2,1)S(1)}, bf16[128,2048]{1,0:T(8,128)(2,1)S(1)}, u32[]{:S(2)}, u32[]{:S(2)}) collective-permute-start(bf16[128,2048]{1,0:T(8,128)(2,1)S(1)} %broadcast_select_fusion.refs_2_), channel_id=1, source_target_pairs={{0,2},{2,0},{1,3},{3,1},{4,6},{6,4},{5,7},{7,5},{8,10},{10,8},{9,1... | collective-permute-start | bytes 1572872 | tf_op jit(solution)/shard_map/ppermute | solution.py:121
  179.2 9.2 %collective-permute-start.43 = (bf16[64,2048]{1,0:T(8,128)(2,1)S(1)}, bf16[64,2048]{1,0:T(8,128)(2,1)}, u32[]{:S(2)}, u32[]{:S(2)}) collective-permute-start(bf16[64,2048]{1,0:T(8,128)(2,1)S(1)} %get-tuple-element.60), channel_id=1, source_target_pairs={{0,12},{4,8},{8,4},{12,0},{1,13},{5,9},{9,5},{13,1},{2,14},{6,10},... | collective-permute-start | bytes 786440 | tf_op jit(solution)/shard_map/ppermute | solution.py:121
  189.9 9.2 %collective-permute-start.46 = (bf16[64,2048]{1,0:T(8,128)(2,1)}, bf16[64,2048]{1,0:T(8,128)(2,1)}, u32[]{:S(2)}, u32[]{:S(2)}) collective-permute-start(bf16[64,2048]{1,0:T(8,128)(2,1)} %collective-permute-done.42.refs_2_), channel_id=1, source_target_pairs={{0,2},{2,0},{1,3},{3,1},{4,6},{6,4},{5,7},{7,5},{8,10},{10,8},{9,1... | collective-permute-start | bytes 786440 | tf_op jit(solution)/shard_map/ppermute | solution.py:121
  190.5 11.4 %collective-permute-start.44 = (bf16[64,2048]{1,0:T(8,128)(2,1)}, bf16[64,2048]{1,0:T(8,128)(2,1)S(1)}, u32[]{:S(2)}, u32[]{:S(2)}) collective-permute-start(bf16[64,2048]{1,0:T(8,128)(2,1)} %collective-permute-done.43.refs_3_), channel_id=1, source_target_pairs={{0,2},{2,0},{1,3},{3,1},{4,6},{6,4},{5,7},{7,5},{8,10},{10,8},{9,1... | collective-permute-start | bytes 786440 | tf_op jit(solution)/shard_map/ppermute | solution.py:121
  (41 other events, 495.7 us)

commit v17 on v16

--- a/solution.py
+++ b/solution.py
@@ -598,6 +598,7 @@
         masked(row_of(0, 2 + at, 0), lax.dynamic_slice(halves, (half, at, 0, 0), (1, 1, block, width))[0, 0])
         for at in range(2)
     ]
+    own = list(lax.optimization_barrier(tuple(own)))
     own_core = [across(value, "sub", 1) for value in own]
 
     mix_a, mix_b = after((mix_a, mix_b), *own_core)
@@ -611,10 +612,11 @@
     operators = after(operators, mix_b)
     operators_core = across(operators, "sub", 1)
     turned = arrange(right, operators, operators_core)
-    next_b, far_z = after((own[1], far_z), far_core, near_a_core, turned)
+    cols_other = operators[-1, :16, :sectors].astype(jnp.int32)
+    cols = (*cols, cols_other)
+    next_b, far_z = after((own[1], far_z), far_core, near_a_core, turned, cols_other)
     near_b = across(next_b, "blk", 1)
     far_zx = across(far_z, "ops", 1)
-    cols = (*cols, operators[-1, :16, :sectors].astype(jnp.int32))
     far_x_core = across(far_x, "sub", 1)
     far_z_core = across(far_z, "sub", 1)
     hd_far = lax.dynamic_index_in_dim(diag, x, 0, keepdims=False)

time: 205 us -> 204 us (level)
  no operation moved by 1% of the time
where the time goes in v17:
time: 204 us; the launch traced here: 201 us
  waiting for transfers between devices  96.7 us (47%)
  starting transfers between devices  50.4 us (25%)
  Pallas kernels  40.2 us (20%)
  local copies, waits for them, and re-layouts  6.62 us (3%)
  other arithmetic  5.81 us (3%)
    ppermute x42, waiting for transfers between devices, across(): return lax.ppermute(value, axis, [(i, i ^ distance) for i in range(size)])  70.9 us
    ppermute x42, starting transfers between devices, across(): return lax.ppermute(value, axis, [(i, i ^ distance) for i in range(size)])  35.4 us
    pallas_call x2, Pallas kernels, operate(): pl.pallas_call(functools.partial(operate_kernel, first, plan), out_shape=...  27 us
    ppermute x1, waiting for transfers between devices, shards(): mix_b = lax.ppermute(mix_b, 'blk', [(0, 1), (1, 3), (3, 2), (2, 0)])  12.6 us
    ppermute x1, waiting for transfers between devices, shards(): mix_a = lax.ppermute(mix_a, 'blk', [(0, 2), (2, 3), (3, 1), (1, 0)])  7.06 us
    ppermute x6, starting transfers between devices, share(): lax.ppermute(pair, axes, [(i, i ^ distance) for i in range(count)])  6.98 us
    unnamed x42, local copies, waits for them, and re-layouts  6.44 us
    ppermute x6, waiting for transfers between devices, share(): lax.ppermute(pair, axes, [(i, i ^ distance) for i in range(count)])  6.17 us
  transfers between devices with their start and end apart: 52, of which 27 were waited for; matrix products, arithmetic and copies ran while one was open for 3% of the time, Pallas kernels for 16%

profile of v17, /device:TPU:0, one launch (start us, length us, event | category | flops | bytes accessed | tf_op | source)
XLA Modules:
  0.0 200.8 jit_solution(12662251019826975450)
XLA Ops:
  0.6 4.3 %prepare.1 = (bf16[128,2176]{1,0:T(8,128)(2,1)}, bf16[128,2176]{1,0:T(8,128)(2,1)}, bf16[31,128,128]{2,1,0:T(8,128)(2,1)}, f32[8,128]{1,0:T(8,128)}) custom-call(s32[16,16]{1,0:T(8,128)} %pattern.5, bf16[2,2,128,2048]{3,2,1,0:T(8,128)(2,1)} %bitcast.108, bf16[2,128,2048]{2,1,0:T(8,128)(2,1)} %bitcast.74, bf16[48,128,128]{2,1,0:T(8,128)(2,1)} %bitcast.78, ...), custom_call_target="tpu_custom_call" | custom-call | tf_op jit(solution)/shard_map/prepare/pallas_call | solution.py:444
  4.9 4.1 %collective-permute-start.1 = (bf16[128,2176]{1,0:T(8,128)(2,1)}, bf16[128,2176]{1,0:T(8,128)(2,1)}, u32[]{:S(2)}, u32[]{:S(2)}) collective-permute-start(bf16[128,2176]{1,0:T(8,128)(2,1)} %get-tuple-element.38), channel_id=1, source_target_pairs={{0,8},{8,12},{12,4},{4,0},{1,9},{9,13},{13,5},{5,1},{2,10},{10,14}... | collective-permute-start | bytes 1671176 | tf_op jit(solution)/shard_map/ppermute | solution.py:589
  13.1 1.5 collective-permute-done.3
  15.4 7.1 %collective-permute-done.1.refs_16_ = bf16[128,2176]{1,0:T(8,128)(2,1)} collective-permute-done((bf16[128,2176]{1,0:T(8,128)(2,1)}, bf16[128,2176]{1,0:T(8,128)(2,1)}, u32[]{:S(2)}, u32[]{:S(2)}) %collective-permute-start.1) | collective-permute-done | bytes 557088 | tf_op jit(solution)/shard_map/ppermute | solution.py:589
  22.4 12.6 %collective-permute-done.2.refs_17_ = bf16[128,2176]{1,0:T(8,128)(2,1)} collective-permute-done((bf16[128,2176]{1,0:T(8,128)(2,1)}, bf16[128,2176]{1,0:T(8,128)(2,1)}, u32[]{:S(2)}, u32[]{:S(2)}) %collective-permute-start.2) | collective-permute-done | bytes 557088 | tf_op jit(solution)/shard_map/ppermute | solution.py:590
  35.0 1.7 select_multiply_fusion
  40.1 1.5 copy-done.4
  41.6 1.7 arrange.1.right
  43.3 1.6 copy-done
  44.9 5.9 %collective-permute-done.6 = bf16[128,2048]{1,0:T(8,128)(2,1)} collective-permute-done((bf16[128,2048]{1,0:T(8,128)(2,1)S(1)}, bf16[128,2048]{1,0:T(8,128)(2,1)}, u32[]{:S(2)}, u32[]{:S(2)}) %collective-permute-start.6) | collective-permute-done | bytes 524320 | tf_op jit(solution)/shard_map/ppermute | solution.py:121
  53.6 10.6 %collective-permute-done.9 = bf16[128,2048]{1,0:T(8,128)(2,1)S(1)} collective-permute-done((bf16[128,2048]{1,0:T(8,128)(2,1)}, bf16[128,2048]{1,0:T(8,128)(2,1)S(1)}, u32[]{:S(2)}, u32[]{:S(2)}) %collective-permute-start.9) | collective-permute-done | bytes 524320 | tf_op jit(solution)/shard_map/ppermute | solution.py:121
  64.8 2.5 %collective-permute-start.16 = (bf16[128,2048]{1,0:T(8,128)(2,1)S(1)}, bf16[128,2048]{1,0:T(8,128)(2,1)S(1)}, u32[]{:S(2)}, u32[]{:S(2)}) collective-permute-start(bf16[128,2048]{1,0:T(8,128)(2,1)S(1)} %dynamic-slice_bitcast_fusion), channel_id=1, source_target_pairs={{0,12},{4,8},{8,4},{12,0},{1,13},{5,9},{9,5},{13,1},{2,14},{6,10},... | collective-permute-start | bytes 1572872 | tf_op jit(solution)/shard_map/ppermute | solution.py:121
  68.2 15.1 %operate_first.1 = (bf16[2,128,2048]{2,1,0:T(8,128)(2,1)}, bf16[2,128,2048]{2,1,0:T(8,128)(2,1)}, f32[8,128]{1,0:T(8,128)}) custom-call(s32[3,1,16]{2,1,0:T(1,128)} %bitcast.98, s32[3,1,16]{2,1,0:T(1,128)} %bitcast.101, s32[16,16]{1,0:T(8,128)} %bitcast_convert_fusion.cols_other, s32[16,16]{1,0:T(8,128)} %pattern.5, bf16[2,48,128,128]{3,2,1,0:T(8,128)(2,1)} %copy-done, ...), custom_call_target="tpu_custom_call" | custom-call | flops 3221225472 | bytes 16777216 | tf_op jit(solution)/shard_map/operate_first/pallas_call | solution.py:314
  87.2 1.7 collective-permute-start.20
  94.2 2.1 %update.1 = (f32[2,128,2048]{2,1,0:T(8,128)S(1)}, f32[8,128]{1,0:T(8,128)S(1)}) custom-call(bf16[2,128,2048]{2,1,0:T(8,128)(2,1)S(1)} %copy-done.2, bf16[2,128,2048]{2,1,0:T(8,128)(2,1)S(1)} %copy-done.5, bf16[2,128,2048]{2,1,0:T(8,128)(2,1)S(1)} %bitcast.77, bf16[128,2048]{1,0:T(8,128)(2,1)S(1)} %collective-permute-done.16.hd_far.refs_17_, ...), custom_call_target="tpu_custom_call" | custom-call | tf_op jit(solution)/shard_map/update/pallas_call | solution.py:655
  98.2 1.7 collective-permute-start.23
  101.9 2.6 %collective-permute-done.24.refs_3_ = f32[2,8,128]{2,1,0:T(8,128)S(1)} collective-permute-done((f32[2,8,128]{2,1,0:T(8,128)S(1)}, f32[2,8,128]{2,1,0:T(8,128)S(1)}, u32[]{:S(2)}, u32[]{:S(2)}) %collective-permute-start.24) | collective-permute-done | bytes 8224 | tf_op jit(solution)/shard_map/ppermute | solution.py:130
  108.2 9.2 %collective-permute-done.25 = bf16[128,2048]{1,0:T(8,128)(2,1)S(1)} collective-permute-done((bf16[128,2048]{1,0:T(8,128)(2,1)S(1)}, bf16[128,2048]{1,0:T(8,128)(2,1)S(1)}, u32[]{:S(2)}, u32[]{:S(2)}) %collective-permute-start.25) | collective-permute-done | bytes 524320 | tf_op jit(solution)/shard_map/ppermute | solution.py:121
  117.5 4.7 %collective-permute-start.32 = (bf16[128,2048]{1,0:T(8,128)(2,1)S(1)}, bf16[128,2048]{1,0:T(8,128)(2,1)S(1)}, u32[]{:S(2)}, u32[]{:S(2)}) collective-permute-start(bf16[128,2048]{1,0:T(8,128)(2,1)S(1)} %get-tuple-element.59), channel_id=1, source_target_pairs={{0,4},{4,0},{8,12},{12,8},{1,5},{5,1},{9,13},{13,9},{2,6},{6,2},{1... | collective-permute-start | bytes 1572872 | tf_op jit(solution)/shard_map/ppermute | solution.py:121
  124.4 10.7 %collective-permute-done.32 = bf16[128,2048]{1,0:T(8,128)(2,1)S(1)} collective-permute-done((bf16[128,2048]{1,0:T(8,128)(2,1)S(1)}, bf16[128,2048]{1,0:T(8,128)(2,1)S(1)}, u32[]{:S(2)}, u32[]{:S(2)}) %collective-permute-start.32) | collective-permute-done | bytes 524320 | tf_op jit(solution)/shard_map/ppermute | solution.py:121
  135.1 2.0 %collective-permute-done.28.refs_1_ = bf16[128,2048]{1,0:T(8,128)(2,1)S(1)} collective-permute-done((bf16[128,2048]{1,0:T(8,128)(2,1)S(1)}, bf16[128,2048]{1,0:T(8,128)(2,1)S(1)}, u32[]{:S(2)}, u32[]{:S(2)}) %collective-permute-start.28) | collective-permute-done | bytes 524320 | tf_op jit(solution)/shard_map/ppermute | solution.py:121
  137.1 6.9 %collective-permute-done.37 = bf16[128,2048]{1,0:T(8,128)(2,1)S(1)} collective-permute-done((bf16[128,2048]{1,0:T(8,128)(2,1)S(1)}, bf16[128,2048]{1,0:T(8,128)(2,1)S(1)}, u32[]{:S(2)}, u32[]{:S(2)}) %collective-permute-start.37) | collective-permute-done | bytes 524320 | tf_op jit(solution)/shard_map/ppermute | solution.py:121
  144.6 3.3 %collective-permute-start.29 = (bf16[128,2048]{1,0:T(8,128)(2,1)S(1)}, bf16[128,2048]{1,0:T(8,128)(2,1)S(1)}, u32[]{:S(2)}, u32[]{:S(2)}) collective-permute-start(bf16[128,2048]{1,0:T(8,128)(2,1)S(1)} %get-tuple-element.59), channel_id=1, source_target_pairs={{0,12},{12,0},{1,13},{13,1},{2,14},{14,2},{3,15},{15,3},{16,28},{2... | collective-permute-start | bytes 1572872 | tf_op jit(solution)/shard_map/ppermute | solution.py:697
  148.0 12.0 %operate_second.1 = (bf16[128,2048]{1,0:T(8,128)(2,1)S(1)}, bf16[64,2048]{1,0:T(8,128)(2,1)S(1)}, bf16[64,2048]{1,0:T(8,128)(2,1)S(1)}, f32[8,128]{1,0:T(8,128)S(1)}) custom-call(s32[3,1,16]{2,1,0:T(1,128)S(1)} %bitcast.99, s32[3,1,16]{2,1,0:T(1,128)S(1)} %bitcast.102, s32[16,16]{1,0:T(8,128)S(1)} %copy-done.7, s32[16,16]{1,0:T(8,128)S(1)} %copy-done.6, ...), custom_call_target="tpu_custom_call" | custom-call | bytes 1024 | tf_op jit(solution)/shard_map/operate_second/pallas_call | solution.py:314
  159.9 2.6 %collective-permute-start.42 = (bf16[64,2048]{1,0:T(8,128)(2,1)S(1)}, bf16[64,2048]{1,0:T(8,128)(2,1)}, u32[]{:S(2)}, u32[]{:S(2)}) collective-permute-start(bf16[64,2048]{1,0:T(8,128)(2,1)S(1)} %get-tuple-element.63), channel_id=1, source_target_pairs={{0,12},{4,8},{8,4},{12,0},{1,13},{5,9},{9,5},{13,1},{2,14},{6,10},... | collective-permute-start | bytes 786440 | tf_op jit(solution)/shard_map/ppermute | solution.py:121
  163.7 6.7 %collective-permute-done.42.refs_2_ = bf16[64,2048]{1,0:T(8,128)(2,1)} collective-permute-done((bf16[64,2048]{1,0:T(8,128)(2,1)S(1)}, bf16[64,2048]{1,0:T(8,128)(2,1)}, u32[]{:S(2)}, u32[]{:S(2)}) %collective-permute-start.42) | collective-permute-done | bytes 262176 | tf_op jit(solution)/shard_map/ppermute | solution.py:121
  170.4 4.1 %collective-permute-start.48 = (f32[8,128]{1,0:T(8,128)S(1)}, f32[8,128]{1,0:T(8,128)S(1)}, u32[]{:S(2)}, u32[]{:S(2)}) collective-permute-start(f32[8,128]{1,0:T(8,128)S(1)} %add.66), channel_id=1, source_target_pairs={{0,4},{4,0},{8,12},{12,8},{1,5},{5,1},{9,13},{13,9},{2,6},{6,2},{1... | collective-permute-start | bytes 12296 | tf_op jit(solution)/shard_map/ppermute | solution.py:121
  175.3 2.2 %collective-permute-start.50 = (f32[8,128]{1,0:T(8,128)S(1)}, f32[8,128]{1,0:T(8,128)S(1)}, u32[]{:S(2)}, u32[]{:S(2)}) collective-permute-start(f32[8,128]{1,0:T(8,128)S(1)} %add.66), channel_id=1, source_target_pairs={{0,12},{4,8},{8,4},{12,0},{1,13},{5,9},{9,5},{13,1},{2,14},{6,10},... | collective-permute-start | bytes 12296 | tf_op jit(solution)/shard_map/ppermute | solution.py:121
  177.5 1.6 collective-permute-start.43
  180.8 5.9 %collective-permute-done.43.refs_3_ = bf16[64,2048]{1,0:T(8,128)(2,1)} collective-permute-done((bf16[64,2048]{1,0:T(8,128)(2,1)S(1)}, bf16[64,2048]{1,0:T(8,128)(2,1)}, u32[]{:S(2)}, u32[]{:S(2)}) %collective-permute-start.43) | collective-permute-done | bytes 262176 | tf_op jit(solution)/shard_map/ppermute | solution.py:121
  192.5 4.9 %collective-permute-done.46.refs_4_ = bf16[64,2048]{1,0:T(8,128)(2,1)} collective-permute-done((bf16[64,2048]{1,0:T(8,128)(2,1)}, bf16[64,2048]{1,0:T(8,128)(2,1)}, u32[]{:S(2)}, u32[]{:S(2)}) %collective-permute-start.46) | collective-permute-done | bytes 262176 | tf_op jit(solution)/shard_map/ppermute | solution.py:121
  197.4 2.4 %assemble.4.refs_1_ = bf16[2,2,128,2048]{3,2,1,0:T(8,128)(2,1)} custom-call(bf16[128,2048]{1,0:T(8,128)(2,1)S(1)} %get-tuple-element.60.refs_0_, bf16[128,2048]{1,0:T(8,128)(2,1)S(1)} %collective-permute-done.45.refs_1_, bf16[64,2048]{1,0:T(8,128)(2,1)} %collective-permute-done.42.refs_2_, bf16[64,2048]{1,0:T(8,128)(2,1)} %collective-permute-done.43.refs_3_, ...), custom_call_target="tpu_custom_call" | custom-call | tf_op jit(solution)/shard_map/assemble/pallas_call | solution.py:557
  (142 shorter events, 42.4 us)
Async XLA Ops:
  4.9 17.5 %collective-permute-start.1 = (bf16[128,2176]{1,0:T(8,128)(2,1)}, bf16[128,2176]{1,0:T(8,128)(2,1)}, u32[]{:S(2)}, u32[]{:S(2)}) collective-permute-start(bf16[128,2176]{1,0:T(8,128)(2,1)} %get-tuple-element.38), channel_id=1, source_target_pairs={{0,8},{8,12},{12,4},{4,0},{1,9},{9,13},{13,5},{5,1},{2,10},{10,14}... | collective-permute-start | bytes 1671176 | tf_op jit(solution)/shard_map/ppermute | solution.py:589
  9.0 26.0 %collective-permute-start.2 = (bf16[128,2176]{1,0:T(8,128)(2,1)}, bf16[128,2176]{1,0:T(8,128)(2,1)}, u32[]{:S(2)}, u32[]{:S(2)}) collective-permute-start(bf16[128,2176]{1,0:T(8,128)(2,1)} %get-tuple-element.39), channel_id=1, source_target_pairs={{0,4},{4,12},{12,8},{8,0},{1,5},{5,13},{13,9},{9,1},{2,6},{6,14},{... | collective-permute-start | bytes 1671176 | tf_op jit(solution)/shard_map/ppermute | solution.py:590
  9.0 26.0 %collective-permute-start = (bf16[31,128,128]{2,1,0:T(8,128)(2,1)}, bf16[31,128,128]{2,1,0:T(8,128)(2,1)S(1)}, u32[]{:S(2)}, u32[]{:S(2)}) collective-permute-start(bf16[31,128,128]{2,1,0:T(8,128)(2,1)} %get-tuple-element.37), channel_id=1, source_target_pairs={{0,2},{2,0},{1,3},{3,1},{4,6},{6,4},{5,7},{7,5},{8,10},{10,8},{9,1... | collective-permute-start | bytes 3047432 | tf_op jit(solution)/shard_map/ppermute | solution.py:121
  36.7 14.1 %collective-permute-start.6 = (bf16[128,2048]{1,0:T(8,128)(2,1)S(1)}, bf16[128,2048]{1,0:T(8,128)(2,1)}, u32[]{:S(2)}, u32[]{:S(2)}) collective-permute-start(bf16[128,2048]{1,0:T(8,128)(2,1)S(1)} %get-tuple-element.73), channel_id=1, source_target_pairs={{0,4},{4,0},{8,12},{12,8},{1,5},{5,1},{9,13},{13,9},{2,6},{6,2},{1... | collective-permute-start | bytes 1572872 | tf_op jit(solution)/shard_map/ppermute | solution.py:121
  37.5 13.4 %collective-permute-start.7 = (bf16[128,2048]{1,0:T(8,128)(2,1)S(1)}, bf16[128,2048]{1,0:T(8,128)(2,1)S(1)}, u32[]{:S(2)}, u32[]{:S(2)}) collective-permute-start(bf16[128,2048]{1,0:T(8,128)(2,1)S(1)} %get-tuple-element.73), channel_id=1, source_target_pairs={{0,1},{1,0},{2,3},{3,2},{4,5},{5,4},{6,7},{7,6},{8,9},{9,8},{10,11... | collective-permute-start | bytes 1572872 | tf_op jit(solution)/shard_map/ppermute | solution.py:121
  37.5 13.4 %collective-permute-start.8 = (bf16[128,2048]{1,0:T(8,128)(2,1)S(1)}, bf16[128,2048]{1,0:T(8,128)(2,1)S(1)}, u32[]{:S(2)}, u32[]{:S(2)}) collective-permute-start(bf16[128,2048]{1,0:T(8,128)(2,1)S(1)} %get-tuple-element.74), channel_id=1, source_target_pairs={{0,1},{1,0},{2,3},{3,2},{4,5},{5,4},{6,7},{7,6},{8,9},{9,8},{10,11... | collective-permute-start | bytes 1572872 | tf_op jit(solution)/shard_map/ppermute | solution.py:121
  38.0 15.1 %collective-permute-start.11 = (bf16[128,2048]{1,0:T(8,128)(2,1)S(1)}, bf16[128,2048]{1,0:T(8,128)(2,1)}, u32[]{:S(2)}, u32[]{:S(2)}) collective-permute-start(bf16[128,2048]{1,0:T(8,128)(2,1)S(1)} %get-tuple-element.73), channel_id=1, source_target_pairs={{0,2},{2,0},{1,3},{3,1},{4,6},{6,4},{5,7},{7,5},{8,10},{10,8},{9,1... | collective-permute-start | bytes 1572872 | tf_op jit(solution)/shard_map/ppermute | solution.py:121
  50.9 13.4 %collective-permute-start.9 = (bf16[128,2048]{1,0:T(8,128)(2,1)}, bf16[128,2048]{1,0:T(8,128)(2,1)S(1)}, u32[]{:S(2)}, u32[]{:S(2)}) collective-permute-start(bf16[128,2048]{1,0:T(8,128)(2,1)} %get-tuple-element.45), channel_id=1, source_target_pairs={{0,4},{4,0},{8,12},{12,8},{1,5},{5,1},{9,13},{13,9},{2,6},{6,2},{1... | collective-permute-start | bytes 1572872 | tf_op jit(solution)/shard_map/ppermute | solution.py:121
  51.6 13.1 %collective-permute-start.14 = (bf16[128,2048]{1,0:T(8,128)(2,1)}, bf16[128,2048]{1,0:T(8,128)(2,1)S(1)}, u32[]{:S(2)}, u32[]{:S(2)}) collective-permute-start(bf16[128,2048]{1,0:T(8,128)(2,1)} %collective-permute-done.6), channel_id=1, source_target_pairs={{0,2},{2,0},{1,3},{3,1},{4,6},{6,4},{5,7},{7,5},{8,10},{10,8},{9,1... | collective-permute-start | bytes 1572872 | tf_op jit(solution)/shard_map/ppermute | solution.py:121
  53.1 14.2 %collective-permute-start.12 = (bf16[128,2048]{1,0:T(8,128)(2,1)}, bf16[128,2048]{1,0:T(8,128)(2,1)S(1)}, u32[]{:S(2)}, u32[]{:S(2)}) collective-permute-start(bf16[128,2048]{1,0:T(8,128)(2,1)} %collective-permute-done.11), channel_id=1, source_target_pairs={{0,1},{1,0},{2,3},{3,2},{4,5},{5,4},{6,7},{7,6},{8,9},{9,8},{10,11... | collective-permute-start | bytes 1572872 | tf_op jit(solution)/shard_map/ppermute | solution.py:121
  53.1 14.2 %collective-permute-start.13 = (bf16[128,2048]{1,0:T(8,128)(2,1)}, bf16[128,2048]{1,0:T(8,128)(2,1)}, u32[]{:S(2)}, u32[]{:S(2)}) collective-permute-start(bf16[128,2048]{1,0:T(8,128)(2,1)} %collective-permute-done.6), channel_id=1, source_target_pairs={{0,1},{1,0},{2,3},{3,2},{4,5},{5,4},{6,7},{7,6},{8,9},{9,8},{10,11... | collective-permute-start | bytes 1572872 | tf_op jit(solution)/shard_map/ppermute | solution.py:121
  64.8 24.1 %collective-permute-start.16 = (bf16[128,2048]{1,0:T(8,128)(2,1)S(1)}, bf16[128,2048]{1,0:T(8,128)(2,1)S(1)}, u32[]{:S(2)}, u32[]{:S(2)}) collective-permute-start(bf16[128,2048]{1,0:T(8,128)(2,1)S(1)} %dynamic-slice_bitcast_fusion), channel_id=1, source_target_pairs={{0,12},{4,8},{8,4},{12,0},{1,13},{5,9},{9,5},{13,1},{2,14},{6,10},... | collective-permute-start | bytes 1572872 | tf_op jit(solution)/shard_map/ppermute | solution.py:121
  105.1 12.4 %collective-permute-start.25 = (bf16[128,2048]{1,0:T(8,128)(2,1)S(1)}, bf16[128,2048]{1,0:T(8,128)(2,1)S(1)}, u32[]{:S(2)}, u32[]{:S(2)}) collective-permute-start(bf16[128,2048]{1,0:T(8,128)(2,1)S(1)} %get-tuple-element.58.refs_0_), channel_id=1, source_target_pairs={{0,4},{4,0},{8,12},{12,8},{1,5},{5,1},{9,13},{13,9},{2,6},{6,2},{1... | collective-permute-start | bytes 1572872 | tf_op jit(solution)/shard_map/ppermute | solution.py:121
  105.5 12.0 %collective-permute-start.26 = (bf16[128,2048]{1,0:T(8,128)(2,1)S(1)}, bf16[128,2048]{1,0:T(8,128)(2,1)S(1)}, u32[]{:S(2)}, u32[]{:S(2)}) collective-permute-start(bf16[128,2048]{1,0:T(8,128)(2,1)S(1)} %get-tuple-element.59), channel_id=1, source_target_pairs={{0,2},{2,0},{1,3},{3,1},{4,6},{6,4},{5,7},{7,5},{8,10},{10,8},{9,1... | collective-permute-start | bytes 1572872 | tf_op jit(solution)/shard_map/ppermute | solution.py:121
  107.0 10.6 %collective-permute-start.27 = (bf16[128,2048]{1,0:T(8,128)(2,1)S(1)}, bf16[128,2048]{1,0:T(8,128)(2,1)S(1)}, u32[]{:S(2)}, u32[]{:S(2)}) collective-permute-start(bf16[128,2048]{1,0:T(8,128)(2,1)S(1)} %get-tuple-element.59), channel_id=1, source_target_pairs={{4,8},{8,4},{5,9},{9,5},{6,10},{10,6},{7,11},{11,7},{20,24},{24,20... | collective-permute-start | bytes 1572872 | tf_op jit(solution)/shard_map/ppermute | solution.py:685
  107.7 16.6 %collective-permute-start.30 = (bf16[128,2048]{1,0:T(8,128)(2,1)S(1)}, bf16[128,2048]{1,0:T(8,128)(2,1)S(1)}, u32[]{:S(2)}, u32[]{:S(2)}) collective-permute-start(bf16[128,2048]{1,0:T(8,128)(2,1)S(1)} %get-tuple-element.58.refs_0_), channel_id=1, source_target_pairs={{0,1},{1,0},{2,3},{3,2},{4,5},{5,4},{6,7},{7,6},{8,9},{9,8},{10,11... | collective-permute-start | bytes 1572872 | tf_op jit(solution)/shard_map/ppermute | solution.py:121
  107.7 16.6 %collective-permute-start.31 = (bf16[128,2048]{1,0:T(8,128)(2,1)S(1)}, bf16[128,2048]{1,0:T(8,128)(2,1)S(1)}, u32[]{:S(2)}, u32[]{:S(2)}) collective-permute-start(bf16[128,2048]{1,0:T(8,128)(2,1)S(1)} %get-tuple-element.59), channel_id=1, source_target_pairs={{0,1},{1,0},{2,3},{3,2},{4,5},{5,4},{6,7},{7,6},{8,9},{9,8},{10,11... | collective-permute-start | bytes 1572872 | tf_op jit(solution)/shard_map/ppermute | solution.py:121
  117.5 17.6 %collective-permute-start.32 = (bf16[128,2048]{1,0:T(8,128)(2,1)S(1)}, bf16[128,2048]{1,0:T(8,128)(2,1)S(1)}, u32[]{:S(2)}, u32[]{:S(2)}) collective-permute-start(bf16[128,2048]{1,0:T(8,128)(2,1)S(1)} %get-tuple-element.59), channel_id=1, source_target_pairs={{0,4},{4,0},{8,12},{12,8},{1,5},{5,1},{9,13},{13,9},{2,6},{6,2},{1... | collective-permute-start | bytes 1572872 | tf_op jit(solution)/shard_map/ppermute | solution.py:121
  122.3 14.9 %collective-permute-start.28 = (bf16[128,2048]{1,0:T(8,128)(2,1)S(1)}, bf16[128,2048]{1,0:T(8,128)(2,1)S(1)}, u32[]{:S(2)}, u32[]{:S(2)}) collective-permute-start(bf16[128,2048]{1,0:T(8,128)(2,1)S(1)} %get-tuple-element.58.refs_0_), channel_id=1, source_target_pairs={{0,2},{2,0},{1,3},{3,1},{4,6},{6,4},{5,7},{7,5},{8,10},{10,8},{9,1... | collective-permute-start | bytes 1572872 | tf_op jit(solution)/shard_map/ppermute | solution.py:121
  122.8 21.2 %collective-permute-start.37 = (bf16[128,2048]{1,0:T(8,128)(2,1)S(1)}, bf16[128,2048]{1,0:T(8,128)(2,1)S(1)}, u32[]{:S(2)}, u32[]{:S(2)}) collective-permute-start(bf16[128,2048]{1,0:T(8,128)(2,1)S(1)} %collective-permute-done.25), channel_id=1, source_target_pairs={{0,2},{2,0},{1,3},{3,1},{4,6},{6,4},{5,7},{7,5},{8,10},{10,8},{9,1... | collective-permute-start | bytes 1572872 | tf_op jit(solution)/shard_map/ppermute | solution.py:121
  124.3 19.7 %collective-permute-start.38 = (bf16[128,2048]{1,0:T(8,128)(2,1)S(1)}, bf16[128,2048]{1,0:T(8,128)(2,1)S(1)}, u32[]{:S(2)}, u32[]{:S(2)}) collective-permute-start(bf16[128,2048]{1,0:T(8,128)(2,1)S(1)} %collective-permute-done.26), channel_id=1, source_target_pairs={{0,4},{4,0},{8,12},{12,8},{1,5},{5,1},{9,13},{13,9},{2,6},{6,2},{1... | collective-permute-start | bytes 1572872 | tf_op jit(solution)/shard_map/ppermute | solution.py:121
  124.3 20.2 %collective-permute-start.33 = (bf16[128,2048]{1,0:T(8,128)(2,1)S(1)}, bf16[128,2048]{1,0:T(8,128)(2,1)S(1)}, u32[]{:S(2)}, u32[]{:S(2)}) collective-permute-start(bf16[128,2048]{1,0:T(8,128)(2,1)S(1)} %collective-permute-done.25), channel_id=1, source_target_pairs={{0,1},{1,0},{2,3},{3,2},{4,5},{5,4},{6,7},{7,6},{8,9},{9,8},{10,11... | collective-permute-start | bytes 1572872 | tf_op jit(solution)/shard_map/ppermute | solution.py:121
  135.1 9.5 %collective-permute-start.36 = (bf16[128,2048]{1,0:T(8,128)(2,1)S(1)}, bf16[128,2048]{1,0:T(8,128)(2,1)S(1)}, u32[]{:S(2)}, u32[]{:S(2)}) collective-permute-start(bf16[128,2048]{1,0:T(8,128)(2,1)S(1)} %collective-permute-done.26), channel_id=1, source_target_pairs={{0,1},{1,0},{2,3},{3,2},{4,5},{5,4},{6,7},{7,6},{8,9},{9,8},{10,11... | collective-permute-start | bytes 1572872 | tf_op jit(solution)/shard_map/ppermute | solution.py:121
  137.1 10.8 %collective-permute-start.34 = (bf16[128,2048]{1,0:T(8,128)(2,1)S(1)}, bf16[128,2048]{1,0:T(8,128)(2,1)S(1)}, u32[]{:S(2)}, u32[]{:S(2)}) collective-permute-start(bf16[128,2048]{1,0:T(8,128)(2,1)S(1)} %collective-permute-done.32), channel_id=1, source_target_pairs={{0,1},{1,0},{2,3},{3,2},{4,5},{5,4},{6,7},{7,6},{8,9},{9,8},{10,11... | collective-permute-start | bytes 1572872 | tf_op jit(solution)/shard_map/ppermute | solution.py:121
  144.6 18.4 %collective-permute-start.29 = (bf16[128,2048]{1,0:T(8,128)(2,1)S(1)}, bf16[128,2048]{1,0:T(8,128)(2,1)S(1)}, u32[]{:S(2)}, u32[]{:S(2)}) collective-permute-start(bf16[128,2048]{1,0:T(8,128)(2,1)S(1)} %get-tuple-element.59), channel_id=1, source_target_pairs={{0,12},{12,0},{1,13},{13,1},{2,14},{14,2},{3,15},{15,3},{16,28},{2... | collective-permute-start | bytes 1572872 | tf_op jit(solution)/shard_map/ppermute | solution.py:697
  159.9 10.5 %collective-permute-start.42 = (bf16[64,2048]{1,0:T(8,128)(2,1)S(1)}, bf16[64,2048]{1,0:T(8,128)(2,1)}, u32[]{:S(2)}, u32[]{:S(2)}) collective-permute-start(bf16[64,2048]{1,0:T(8,128)(2,1)S(1)} %get-tuple-element.63), channel_id=1, source_target_pairs={{0,12},{4,8},{8,4},{12,0},{1,13},{5,9},{9,5},{13,1},{2,14},{6,10},... | collective-permute-start | bytes 786440 | tf_op jit(solution)/shard_map/ppermute | solution.py:121
  162.5 25.7 %collective-permute-start.45 = (bf16[128,2048]{1,0:T(8,128)(2,1)S(1)}, bf16[128,2048]{1,0:T(8,128)(2,1)S(1)}, u32[]{:S(2)}, u32[]{:S(2)}) collective-permute-start(bf16[128,2048]{1,0:T(8,128)(2,1)S(1)} %get-tuple-element.60.refs_0_), channel_id=1, source_target_pairs={{0,2},{2,0},{1,3},{3,1},{4,6},{6,4},{5,7},{7,5},{8,10},{10,8},{9,1... | collective-permute-start | bytes 1572872 | tf_op jit(solution)/shard_map/ppermute | solution.py:121
  170.4 7.1 %collective-permute-start.48 = (f32[8,128]{1,0:T(8,128)S(1)}, f32[8,128]{1,0:T(8,128)S(1)}, u32[]{:S(2)}, u32[]{:S(2)}) collective-permute-start(f32[8,128]{1,0:T(8,128)S(1)} %add.66), channel_id=1, source_target_pairs={{0,4},{4,0},{8,12},{12,8},{1,5},{5,1},{9,13},{13,9},{2,6},{6,2},{1... | collective-permute-start | bytes 12296 | tf_op jit(solution)/shard_map/ppermute | solution.py:121
  174.5 14.3 %collective-permute-start.41 = (bf16[128,2048]{1,0:T(8,128)(2,1)S(1)}, bf16[128,2048]{1,0:T(8,128)(2,1)S(1)}, u32[]{:S(2)}, u32[]{:S(2)}) collective-permute-start(bf16[128,2048]{1,0:T(8,128)(2,1)S(1)} %broadcast_select_fusion.refs_2_), channel_id=1, source_target_pairs={{0,2},{2,0},{1,3},{3,1},{4,6},{6,4},{5,7},{7,5},{8,10},{10,8},{9,1... | collective-permute-start | bytes 1572872 | tf_op jit(solution)/shard_map/ppermute | solution.py:121
  177.5 9.2 %collective-permute-start.43 = (bf16[64,2048]{1,0:T(8,128)(2,1)S(1)}, bf16[64,2048]{1,0:T(8,128)(2,1)}, u32[]{:S(2)}, u32[]{:S(2)}) collective-permute-start(bf16[64,2048]{1,0:T(8,128)(2,1)S(1)} %get-tuple-element.64), channel_id=1, source_target_pairs={{0,12},{4,8},{8,4},{12,0},{1,13},{5,9},{9,5},{13,1},{2,14},{6,10},... | collective-permute-start | bytes 786440 | tf_op jit(solution)/shard_map/ppermute | solution.py:121
  188.2 9.2 %collective-permute-start.46 = (bf16[64,2048]{1,0:T(8,128)(2,1)}, bf16[64,2048]{1,0:T(8,128)(2,1)}, u32[]{:S(2)}, u32[]{:S(2)}) collective-permute-start(bf16[64,2048]{1,0:T(8,128)(2,1)} %collective-permute-done.42.refs_2_), channel_id=1, source_target_pairs={{0,2},{2,0},{1,3},{3,1},{4,6},{6,4},{5,7},{7,5},{8,10},{10,8},{9,1... | collective-permute-start | bytes 786440 | tf_op jit(solution)/shard_map/ppermute | solution.py:121
  188.8 11.3 %collective-permute-start.44 = (bf16[64,2048]{1,0:T(8,128)(2,1)}, bf16[64,2048]{1,0:T(8,128)(2,1)S(1)}, u32[]{:S(2)}, u32[]{:S(2)}) collective-permute-start(bf16[64,2048]{1,0:T(8,128)(2,1)} %collective-permute-done.43.refs_3_), channel_id=1, source_target_pairs={{0,2},{2,0},{1,3},{3,1},{4,6},{6,4},{5,7},{7,5},{8,10},{10,8},{9,1... | collective-permute-start | bytes 786440 | tf_op jit(solution)/shard_map/ppermute | solution.py:121
  (41 other events, 449.8 us)

commit v18 on v17

--- a/solution.py
+++ b/solution.py
@@ -461,12 +461,14 @@
     return jnp.sum(rows, axis=1, keepdims=True)
 
 
-def update_kernel(psi, off, hd_own, hd_far, *refs):
-    stats, (t_out, stats_out, diag, sems) = refs[:4], refs[4:]
+def update_kernel(psi_ref, off_ref, hd_own, hd_far, *refs):
+    stats, (t_out, stats_out, psi, off, diag, sems) = refs[:4], refs[4:]
     z, x, c = place()
     copies = [
         pltpu.make_async_copy(hd_own.at[x], diag.at[0], sems.at[0]),
         pltpu.make_async_copy(hd_far, diag.at[1], sems.at[1]),
+        pltpu.make_async_copy(psi_ref, psi, sems.at[2]),
+        pltpu.make_async_copy(off_ref, off, sems.at[3]),
     ]
     for copy in copies:
         copy.start()
@@ -605,7 +607,8 @@
     far = masked(row_of(2, 0, 0), jnp.where(middle, mix_a[:, :width], mix_b[:, :width]))
     far_z = across(far, "blk", 1)
     far_x = across(far, "ops", 1)
-    near_a = masked(row_of(1, 2, 0), jnp.where(middle, mix_b[:, :width], mix_a[:, :width]))
+    late_a, late_b = after((mix_a, mix_b), far)
+    near_a = masked(row_of(1, 2, 0), jnp.where(middle, late_b[:, :width], late_a[:, :width]))
     far_core = across(far, "sub", 1)
     near_a_core = across(near_a, "sub", 1)
 
@@ -658,11 +661,13 @@
             jax.ShapeDtypeStruct((2, block, width), jnp.float32),
             jax.ShapeDtypeStruct((8, LANES), jnp.float32),
         ),
-        in_specs=[VMEM, VMEM, ANY, ANY] + [VMEM] * 4,
+        in_specs=[ANY] * 4 + [VMEM] * 4,
         out_specs=(VMEM, VMEM),
         scratch_shapes=[
             pltpu.VMEM((2, block, width), jnp.bfloat16),
-            pltpu.SemaphoreType.DMA((2,)),
+            pltpu.VMEM((2, block, width), jnp.bfloat16),
+            pltpu.VMEM((2, block, width), jnp.bfloat16),
+            pltpu.SemaphoreType.DMA((4,)),
         ],
         compiler_params=pltpu.CompilerParams(vmem_limit_bytes=VMEM_LIMIT),
         name="update",

time: 204 us -> 206 us (level)
    mul x2 -> x3, other arithmetic: 2.73 us -> 4.16 us  [masked(): return value * jnp.repeat(line, block)[None, :]]
  transfers between devices with their start and end apart: 52 -> 52, of which waited for: 27 -> 27; matrix products, arithmetic and copies ran while one was open for 3% -> 4% of each run, Pallas kernels for 16% -> 16%
where the time goes in v18:
time: 206 us; the launch traced here: 203 us
  waiting for transfers between devices  97.6 us (47%)
  starting transfers between devices  50.1 us (24%)
  Pallas kernels  40.4 us (20%)
  other arithmetic  7.24 us (4%)
  local copies, waits for them, and re-layouts  6.67 us (3%)
    ppermute x42, waiting for transfers between devices, across(): return lax.ppermute(value, axis, [(i, i ^ distance) for i in range(size)])  71.8 us
    ppermute x42, starting transfers between devices, across(): return lax.ppermute(value, axis, [(i, i ^ distance) for i in range(size)])  35.1 us
    pallas_call x2, Pallas kernels, operate(): pl.pallas_call(functools.partial(operate_kernel, first, plan), out_shape=...  27 us
    ppermute x1, waiting for transfers between devices, shards(): mix_b = lax.ppermute(mix_b, 'blk', [(0, 1), (1, 3), (3, 2), (2, 0)])  12.6 us
    ppermute x1, waiting for transfers between devices, shards(): mix_a = lax.ppermute(mix_a, 'blk', [(0, 2), (2, 3), (3, 1), (1, 0)])  7.05 us
    ppermute x6, starting transfers between devices, share(): lax.ppermute(pair, axes, [(i, i ^ distance) for i in range(count)])  6.98 us
    unnamed x42, local copies, waits for them, and re-layouts  6.42 us
    ppermute x6, waiting for transfers between devices, share(): lax.ppermute(pair, axes, [(i, i ^ distance) for i in range(count)])  6.17 us
  transfers between devices with their start and end apart: 52, of which 27 were waited for; matrix products, arithmetic and copies ran while one was open for 4% of the time, Pallas kernels for 16%

profile of v18, /device:TPU:0, one launch (start us, length us, event | category | flops | bytes accessed | tf_op | source)
XLA Modules:
  0.0 203.0 jit_solution(4225164583965251405)
XLA Ops:
  0.6 4.3 %prepare.1 = (bf16[128,2176]{1,0:T(8,128)(2,1)}, bf16[128,2176]{1,0:T(8,128)(2,1)}, bf16[31,128,128]{2,1,0:T(8,128)(2,1)}, f32[8,128]{1,0:T(8,128)}) custom-call(s32[16,16]{1,0:T(8,128)} %pattern.5, bf16[2,2,128,2048]{3,2,1,0:T(8,128)(2,1)} %bitcast.108, bf16[2,128,2048]{2,1,0:T(8,128)(2,1)} %bitcast.74, bf16[48,128,128]{2,1,0:T(8,128)(2,1)} %bitcast.78, ...), custom_call_target="tpu_custom_call" | custom-call | tf_op jit(solution)/shard_map/prepare/pallas_call | solution.py:444
  4.9 4.1 %collective-permute-start.1 = (bf16[128,2176]{1,0:T(8,128)(2,1)}, bf16[128,2176]{1,0:T(8,128)(2,1)}, u32[]{:S(2)}, u32[]{:S(2)}) collective-permute-start(bf16[128,2176]{1,0:T(8,128)(2,1)} %get-tuple-element.40), channel_id=1, source_target_pairs={{0,8},{8,12},{12,4},{4,0},{1,9},{9,13},{13,5},{5,1},{2,10},{10,14}... | collective-permute-start | bytes 1671176 | tf_op jit(solution)/shard_map/ppermute | solution.py:591
  9.0 1.5 collective-permute-start
  15.4 7.0 %collective-permute-done.1.refs_16_ = bf16[128,2176]{1,0:T(8,128)(2,1)} collective-permute-done((bf16[128,2176]{1,0:T(8,128)(2,1)}, bf16[128,2176]{1,0:T(8,128)(2,1)}, u32[]{:S(2)}, u32[]{:S(2)}) %collective-permute-start.1) | collective-permute-done | bytes 557088 | tf_op jit(solution)/shard_map/ppermute | solution.py:591
  22.4 12.6 %collective-permute-done.2.refs_17_ = bf16[128,2176]{1,0:T(8,128)(2,1)} collective-permute-done((bf16[128,2176]{1,0:T(8,128)(2,1)}, bf16[128,2176]{1,0:T(8,128)(2,1)}, u32[]{:S(2)}, u32[]{:S(2)}) %collective-permute-start.2) | collective-permute-done | bytes 557088 | tf_op jit(solution)/shard_map/ppermute | solution.py:592
  35.0 1.6 select_multiply_fusion.1
  41.2 1.5 copy-done.4
  42.7 1.7 arrange.1.right
  44.5 1.6 copy-done
  46.1 6.6 %collective-permute-done.6 = bf16[128,2048]{1,0:T(8,128)(2,1)} collective-permute-done((bf16[128,2048]{1,0:T(8,128)(2,1)S(1)}, bf16[128,2048]{1,0:T(8,128)(2,1)}, u32[]{:S(2)}, u32[]{:S(2)}) %collective-permute-start.6) | collective-permute-done | bytes 524320 | tf_op jit(solution)/shard_map/ppermute | solution.py:121
  55.3 10.9 %collective-permute-done.9 = bf16[128,2048]{1,0:T(8,128)(2,1)S(1)} collective-permute-done((bf16[128,2048]{1,0:T(8,128)(2,1)}, bf16[128,2048]{1,0:T(8,128)(2,1)S(1)}, u32[]{:S(2)}, u32[]{:S(2)}) %collective-permute-start.9) | collective-permute-done | bytes 524320 | tf_op jit(solution)/shard_map/ppermute | solution.py:121
  66.8 2.5 %collective-permute-start.16 = (bf16[128,2048]{1,0:T(8,128)(2,1)S(1)}, bf16[128,2048]{1,0:T(8,128)(2,1)S(1)}, u32[]{:S(2)}, u32[]{:S(2)}) collective-permute-start(bf16[128,2048]{1,0:T(8,128)(2,1)S(1)} %dynamic-slice_bitcast_fusion), channel_id=1, source_target_pairs={{0,12},{4,8},{8,4},{12,0},{1,13},{5,9},{9,5},{13,1},{2,14},{6,10},... | collective-permute-start | bytes 1572872 | tf_op jit(solution)/shard_map/ppermute | solution.py:121
  70.2 15.1 %operate_first.1 = (bf16[2,128,2048]{2,1,0:T(8,128)(2,1)}, bf16[2,128,2048]{2,1,0:T(8,128)(2,1)}, f32[8,128]{1,0:T(8,128)}) custom-call(s32[3,1,16]{2,1,0:T(1,128)} %bitcast.98, s32[3,1,16]{2,1,0:T(1,128)} %bitcast.101, s32[16,16]{1,0:T(8,128)} %bitcast_convert_fusion.cols_other, s32[16,16]{1,0:T(8,128)} %pattern.5, bf16[2,48,128,128]{3,2,1,0:T(8,128)(2,1)} %copy-done, ...), custom_call_target="tpu_custom_call" | custom-call | flops 3221225472 | bytes 16777216 | tf_op jit(solution)/shard_map/operate_first/pallas_call | solution.py:314
  89.2 1.7 collective-permute-start.20
  96.2 2.3 %update.1 = (f32[2,128,2048]{2,1,0:T(8,128)S(1)}, f32[8,128]{1,0:T(8,128)S(1)}) custom-call(bf16[2,128,2048]{2,1,0:T(8,128)(2,1)S(1)} %copy-done.2, bf16[2,128,2048]{2,1,0:T(8,128)(2,1)S(1)} %copy-done.5, bf16[2,128,2048]{2,1,0:T(8,128)(2,1)S(1)} %bitcast.77, bf16[128,2048]{1,0:T(8,128)(2,1)S(1)} %collective-permute-done.16.hd_far.refs_17_, ...), custom_call_target="tpu_custom_call" | custom-call | tf_op jit(solution)/shard_map/update/pallas_call | solution.py:658
  100.4 1.7 collective-permute-start.23
  104.0 2.6 %collective-permute-done.24.refs_3_ = f32[2,8,128]{2,1,0:T(8,128)S(1)} collective-permute-done((f32[2,8,128]{2,1,0:T(8,128)S(1)}, f32[2,8,128]{2,1,0:T(8,128)S(1)}, u32[]{:S(2)}, u32[]{:S(2)}) %collective-permute-start.24) | collective-permute-done | bytes 8224 | tf_op jit(solution)/shard_map/ppermute | solution.py:130
  110.4 9.2 %collective-permute-done.25 = bf16[128,2048]{1,0:T(8,128)(2,1)S(1)} collective-permute-done((bf16[128,2048]{1,0:T(8,128)(2,1)S(1)}, bf16[128,2048]{1,0:T(8,128)(2,1)S(1)}, u32[]{:S(2)}, u32[]{:S(2)}) %collective-permute-start.25) | collective-permute-done | bytes 524320 | tf_op jit(solution)/shard_map/ppermute | solution.py:121
  119.7 4.7 %collective-permute-start.32 = (bf16[128,2048]{1,0:T(8,128)(2,1)S(1)}, bf16[128,2048]{1,0:T(8,128)(2,1)S(1)}, u32[]{:S(2)}, u32[]{:S(2)}) collective-permute-start(bf16[128,2048]{1,0:T(8,128)(2,1)S(1)} %get-tuple-element.63), channel_id=1, source_target_pairs={{0,4},{4,0},{8,12},{12,8},{1,5},{5,1},{9,13},{13,9},{2,6},{6,2},{1... | collective-permute-start | bytes 1572872 | tf_op jit(solution)/shard_map/ppermute | solution.py:121
  126.5 10.7 %collective-permute-done.32 = bf16[128,2048]{1,0:T(8,128)(2,1)S(1)} collective-permute-done((bf16[128,2048]{1,0:T(8,128)(2,1)S(1)}, bf16[128,2048]{1,0:T(8,128)(2,1)S(1)}, u32[]{:S(2)}, u32[]{:S(2)}) %collective-permute-start.32) | collective-permute-done | bytes 524320 | tf_op jit(solution)/shard_map/ppermute | solution.py:121
  137.2 2.0 collective-permute-done.28.refs_1_
  139.2 6.9 %collective-permute-done.37 = bf16[128,2048]{1,0:T(8,128)(2,1)S(1)} collective-permute-done((bf16[128,2048]{1,0:T(8,128)(2,1)S(1)}, bf16[128,2048]{1,0:T(8,128)(2,1)S(1)}, u32[]{:S(2)}, u32[]{:S(2)}) %collective-permute-start.37) | collective-permute-done | bytes 524320 | tf_op jit(solution)/shard_map/ppermute | solution.py:121
  146.7 3.3 %collective-permute-start.29 = (bf16[128,2048]{1,0:T(8,128)(2,1)S(1)}, bf16[128,2048]{1,0:T(8,128)(2,1)S(1)}, u32[]{:S(2)}, u32[]{:S(2)}) collective-permute-start(bf16[128,2048]{1,0:T(8,128)(2,1)S(1)} %get-tuple-element.63), channel_id=1, source_target_pairs={{0,12},{12,0},{1,13},{13,1},{2,14},{14,2},{3,15},{15,3},{16,28},{2... | collective-permute-start | bytes 1572872 | tf_op jit(solution)/shard_map/ppermute | solution.py:702
  150.1 11.9 %operate_second.1 = (bf16[128,2048]{1,0:T(8,128)(2,1)S(1)}, bf16[64,2048]{1,0:T(8,128)(2,1)S(1)}, bf16[64,2048]{1,0:T(8,128)(2,1)S(1)}, f32[8,128]{1,0:T(8,128)S(1)}) custom-call(s32[3,1,16]{2,1,0:T(1,128)S(1)} %bitcast.99, s32[3,1,16]{2,1,0:T(1,128)S(1)} %bitcast.102, s32[16,16]{1,0:T(8,128)S(1)} %copy-done.7, s32[16,16]{1,0:T(8,128)S(1)} %copy-done.6, ...), custom_call_target="tpu_custom_call" | custom-call | bytes 1024 | tf_op jit(solution)/shard_map/operate_second/pallas_call | solution.py:314
  162.1 2.5 %collective-permute-start.42 = (bf16[64,2048]{1,0:T(8,128)(2,1)S(1)}, bf16[64,2048]{1,0:T(8,128)(2,1)}, u32[]{:S(2)}, u32[]{:S(2)}) collective-permute-start(bf16[64,2048]{1,0:T(8,128)(2,1)S(1)} %get-tuple-element.67), channel_id=1, source_target_pairs={{0,12},{4,8},{8,4},{12,0},{1,13},{5,9},{9,5},{13,1},{2,14},{6,10},... | collective-permute-start | bytes 786440 | tf_op jit(solution)/shard_map/ppermute | solution.py:121
  165.7 6.8 %collective-permute-done.42.refs_2_ = bf16[64,2048]{1,0:T(8,128)(2,1)} collective-permute-done((bf16[64,2048]{1,0:T(8,128)(2,1)S(1)}, bf16[64,2048]{1,0:T(8,128)(2,1)}, u32[]{:S(2)}, u32[]{:S(2)}) %collective-permute-start.42) | collective-permute-done | bytes 262176 | tf_op jit(solution)/shard_map/ppermute | solution.py:121
  172.5 4.1 %collective-permute-start.48 = (f32[8,128]{1,0:T(8,128)S(1)}, f32[8,128]{1,0:T(8,128)S(1)}, u32[]{:S(2)}, u32[]{:S(2)}) collective-permute-start(f32[8,128]{1,0:T(8,128)S(1)} %add.66), channel_id=1, source_target_pairs={{0,4},{4,0},{8,12},{12,8},{1,5},{5,1},{9,13},{13,9},{2,6},{6,2},{1... | collective-permute-start | bytes 12296 | tf_op jit(solution)/shard_map/ppermute | solution.py:121
  177.5 2.2 %collective-permute-start.50 = (f32[8,128]{1,0:T(8,128)S(1)}, f32[8,128]{1,0:T(8,128)S(1)}, u32[]{:S(2)}, u32[]{:S(2)}) collective-permute-start(f32[8,128]{1,0:T(8,128)S(1)} %add.66), channel_id=1, source_target_pairs={{0,12},{4,8},{8,4},{12,0},{1,13},{5,9},{9,5},{13,1},{2,14},{6,10},... | collective-permute-start | bytes 12296 | tf_op jit(solution)/shard_map/ppermute | solution.py:121
  179.7 1.7 collective-permute-start.43
  183.0 5.9 %collective-permute-done.43.refs_3_ = bf16[64,2048]{1,0:T(8,128)(2,1)} collective-permute-done((bf16[64,2048]{1,0:T(8,128)(2,1)S(1)}, bf16[64,2048]{1,0:T(8,128)(2,1)}, u32[]{:S(2)}, u32[]{:S(2)}) %collective-permute-start.43) | collective-permute-done | bytes 262176 | tf_op jit(solution)/shard_map/ppermute | solution.py:121
  194.7 4.9 %collective-permute-done.46.refs_4_ = bf16[64,2048]{1,0:T(8,128)(2,1)} collective-permute-done((bf16[64,2048]{1,0:T(8,128)(2,1)}, bf16[64,2048]{1,0:T(8,128)(2,1)}, u32[]{:S(2)}, u32[]{:S(2)}) %collective-permute-start.46) | collective-permute-done | bytes 262176 | tf_op jit(solution)/shard_map/ppermute | solution.py:121
  199.6 2.4 %assemble.4.refs_1_ = bf16[2,2,128,2048]{3,2,1,0:T(8,128)(2,1)} custom-call(bf16[128,2048]{1,0:T(8,128)(2,1)S(1)} %get-tuple-element.64.refs_0_, bf16[128,2048]{1,0:T(8,128)(2,1)S(1)} %collective-permute-done.45.refs_1_, bf16[64,2048]{1,0:T(8,128)(2,1)} %collective-permute-done.42.refs_2_, bf16[64,2048]{1,0:T(8,128)(2,1)} %collective-permute-done.43.refs_3_, ...), custom_call_target="tpu_custom_call" | custom-call | tf_op jit(solution)/shard_map/assemble/pallas_call | solution.py:559
  (144 shorter events, 43.5 us)
Async XLA Ops:
  4.9 17.5 %collective-permute-start.1 = (bf16[128,2176]{1,0:T(8,128)(2,1)}, bf16[128,2176]{1,0:T(8,128)(2,1)}, u32[]{:S(2)}, u32[]{:S(2)}) collective-permute-start(bf16[128,2176]{1,0:T(8,128)(2,1)} %get-tuple-element.40), channel_id=1, source_target_pairs={{0,8},{8,12},{12,4},{4,0},{1,9},{9,13},{13,5},{5,1},{2,10},{10,14}... | collective-permute-start | bytes 1671176 | tf_op jit(solution)/shard_map/ppermute | solution.py:591
  9.0 26.0 %collective-permute-start.2 = (bf16[128,2176]{1,0:T(8,128)(2,1)}, bf16[128,2176]{1,0:T(8,128)(2,1)}, u32[]{:S(2)}, u32[]{:S(2)}) collective-permute-start(bf16[128,2176]{1,0:T(8,128)(2,1)} %get-tuple-element.41), channel_id=1, source_target_pairs={{0,4},{4,12},{12,8},{8,0},{1,5},{5,13},{13,9},{9,1},{2,6},{6,14},{... | collective-permute-start | bytes 1671176 | tf_op jit(solution)/shard_map/ppermute | solution.py:592
  9.0 26.0 %collective-permute-start = (bf16[31,128,128]{2,1,0:T(8,128)(2,1)}, bf16[31,128,128]{2,1,0:T(8,128)(2,1)S(1)}, u32[]{:S(2)}, u32[]{:S(2)}) collective-permute-start(bf16[31,128,128]{2,1,0:T(8,128)(2,1)} %get-tuple-element.39), channel_id=1, source_target_pairs={{0,2},{2,0},{1,3},{3,1},{4,6},{6,4},{5,7},{7,5},{8,10},{10,8},{9,1... | collective-permute-start | bytes 3047432 | tf_op jit(solution)/shard_map/ppermute | solution.py:121
  38.1 8.0 %collective-permute-start.8 = (bf16[128,2048]{1,0:T(8,128)(2,1)S(1)}, bf16[128,2048]{1,0:T(8,128)(2,1)S(1)}, u32[]{:S(2)}, u32[]{:S(2)}) collective-permute-start(bf16[128,2048]{1,0:T(8,128)(2,1)S(1)} %select_multiply_fusion), channel_id=1, source_target_pairs={{0,1},{1,0},{2,3},{3,2},{4,5},{5,4},{6,7},{7,6},{8,9},{9,8},{10,11... | collective-permute-start | bytes 1572872 | tf_op jit(solution)/shard_map/ppermute | solution.py:121
  38.3 14.3 %collective-permute-start.6 = (bf16[128,2048]{1,0:T(8,128)(2,1)S(1)}, bf16[128,2048]{1,0:T(8,128)(2,1)}, u32[]{:S(2)}, u32[]{:S(2)}) collective-permute-start(bf16[128,2048]{1,0:T(8,128)(2,1)S(1)} %select_multiply_fusion.1), channel_id=1, source_target_pairs={{0,4},{4,0},{8,12},{12,8},{1,5},{5,1},{9,13},{13,9},{2,6},{6,2},{1... | collective-permute-start | bytes 1572872 | tf_op jit(solution)/shard_map/ppermute | solution.py:121
  39.0 13.6 %collective-permute-start.7 = (bf16[128,2048]{1,0:T(8,128)(2,1)S(1)}, bf16[128,2048]{1,0:T(8,128)(2,1)S(1)}, u32[]{:S(2)}, u32[]{:S(2)}) collective-permute-start(bf16[128,2048]{1,0:T(8,128)(2,1)S(1)} %select_multiply_fusion.1), channel_id=1, source_target_pairs={{0,1},{1,0},{2,3},{3,2},{4,5},{5,4},{6,7},{7,6},{8,9},{9,8},{10,11... | collective-permute-start | bytes 1572872 | tf_op jit(solution)/shard_map/ppermute | solution.py:121
  39.1 15.7 %collective-permute-start.11 = (bf16[128,2048]{1,0:T(8,128)(2,1)S(1)}, bf16[128,2048]{1,0:T(8,128)(2,1)}, u32[]{:S(2)}, u32[]{:S(2)}) collective-permute-start(bf16[128,2048]{1,0:T(8,128)(2,1)S(1)} %select_multiply_fusion.1), channel_id=1, source_target_pairs={{0,2},{2,0},{1,3},{3,1},{4,6},{6,4},{5,7},{7,5},{8,10},{10,8},{9,1... | collective-permute-start | bytes 1572872 | tf_op jit(solution)/shard_map/ppermute | solution.py:121
  52.6 13.6 %collective-permute-start.9 = (bf16[128,2048]{1,0:T(8,128)(2,1)}, bf16[128,2048]{1,0:T(8,128)(2,1)S(1)}, u32[]{:S(2)}, u32[]{:S(2)}) collective-permute-start(bf16[128,2048]{1,0:T(8,128)(2,1)} %get-tuple-element.49), channel_id=1, source_target_pairs={{0,4},{4,0},{8,12},{12,8},{1,5},{5,1},{9,13},{13,9},{2,6},{6,2},{1... | collective-permute-start | bytes 1572872 | tf_op jit(solution)/shard_map/ppermute | solution.py:121
  53.4 13.3 %collective-permute-start.14 = (bf16[128,2048]{1,0:T(8,128)(2,1)}, bf16[128,2048]{1,0:T(8,128)(2,1)S(1)}, u32[]{:S(2)}, u32[]{:S(2)}) collective-permute-start(bf16[128,2048]{1,0:T(8,128)(2,1)} %collective-permute-done.6), channel_id=1, source_target_pairs={{0,2},{2,0},{1,3},{3,1},{4,6},{6,4},{5,7},{7,5},{8,10},{10,8},{9,1... | collective-permute-start | bytes 1572872 | tf_op jit(solution)/shard_map/ppermute | solution.py:121
  54.8 14.5 %collective-permute-start.12 = (bf16[128,2048]{1,0:T(8,128)(2,1)}, bf16[128,2048]{1,0:T(8,128)(2,1)S(1)}, u32[]{:S(2)}, u32[]{:S(2)}) collective-permute-start(bf16[128,2048]{1,0:T(8,128)(2,1)} %collective-permute-done.11), channel_id=1, source_target_pairs={{0,1},{1,0},{2,3},{3,2},{4,5},{5,4},{6,7},{7,6},{8,9},{9,8},{10,11... | collective-permute-start | bytes 1572872 | tf_op jit(solution)/shard_map/ppermute | solution.py:121
  54.8 14.5 %collective-permute-start.13 = (bf16[128,2048]{1,0:T(8,128)(2,1)}, bf16[128,2048]{1,0:T(8,128)(2,1)}, u32[]{:S(2)}, u32[]{:S(2)}) collective-permute-start(bf16[128,2048]{1,0:T(8,128)(2,1)} %collective-permute-done.6), channel_id=1, source_target_pairs={{0,1},{1,0},{2,3},{3,2},{4,5},{5,4},{6,7},{7,6},{8,9},{9,8},{10,11... | collective-permute-start | bytes 1572872 | tf_op jit(solution)/shard_map/ppermute | solution.py:121
  66.8 24.1 %collective-permute-start.16 = (bf16[128,2048]{1,0:T(8,128)(2,1)S(1)}, bf16[128,2048]{1,0:T(8,128)(2,1)S(1)}, u32[]{:S(2)}, u32[]{:S(2)}) collective-permute-start(bf16[128,2048]{1,0:T(8,128)(2,1)S(1)} %dynamic-slice_bitcast_fusion), channel_id=1, source_target_pairs={{0,12},{4,8},{8,4},{12,0},{1,13},{5,9},{9,5},{13,1},{2,14},{6,10},... | collective-permute-start | bytes 1572872 | tf_op jit(solution)/shard_map/ppermute | solution.py:121
  107.2 12.4 %collective-permute-start.25 = (bf16[128,2048]{1,0:T(8,128)(2,1)S(1)}, bf16[128,2048]{1,0:T(8,128)(2,1)S(1)}, u32[]{:S(2)}, u32[]{:S(2)}) collective-permute-start(bf16[128,2048]{1,0:T(8,128)(2,1)S(1)} %get-tuple-element.62.refs_0_), channel_id=1, source_target_pairs={{0,4},{4,0},{8,12},{12,8},{1,5},{5,1},{9,13},{13,9},{2,6},{6,2},{1... | collective-permute-start | bytes 1572872 | tf_op jit(solution)/shard_map/ppermute | solution.py:121
  107.6 12.0 %collective-permute-start.26 = (bf16[128,2048]{1,0:T(8,128)(2,1)S(1)}, bf16[128,2048]{1,0:T(8,128)(2,1)S(1)}, u32[]{:S(2)}, u32[]{:S(2)}) collective-permute-start(bf16[128,2048]{1,0:T(8,128)(2,1)S(1)} %get-tuple-element.63), channel_id=1, source_target_pairs={{0,2},{2,0},{1,3},{3,1},{4,6},{6,4},{5,7},{7,5},{8,10},{10,8},{9,1... | collective-permute-start | bytes 1572872 | tf_op jit(solution)/shard_map/ppermute | solution.py:121
  109.1 10.6 %collective-permute-start.27 = (bf16[128,2048]{1,0:T(8,128)(2,1)S(1)}, bf16[128,2048]{1,0:T(8,128)(2,1)S(1)}, u32[]{:S(2)}, u32[]{:S(2)}) collective-permute-start(bf16[128,2048]{1,0:T(8,128)(2,1)S(1)} %get-tuple-element.63), channel_id=1, source_target_pairs={{4,8},{8,4},{5,9},{9,5},{6,10},{10,6},{7,11},{11,7},{20,24},{24,20... | collective-permute-start | bytes 1572872 | tf_op jit(solution)/shard_map/ppermute | solution.py:690
  109.8 16.6 %collective-permute-start.30 = (bf16[128,2048]{1,0:T(8,128)(2,1)S(1)}, bf16[128,2048]{1,0:T(8,128)(2,1)S(1)}, u32[]{:S(2)}, u32[]{:S(2)}) collective-permute-start(bf16[128,2048]{1,0:T(8,128)(2,1)S(1)} %get-tuple-element.62.refs_0_), channel_id=1, source_target_pairs={{0,1},{1,0},{2,3},{3,2},{4,5},{5,4},{6,7},{7,6},{8,9},{9,8},{10,11... | collective-permute-start | bytes 1572872 | tf_op jit(solution)/shard_map/ppermute | solution.py:121
  109.9 16.6 %collective-permute-start.31 = (bf16[128,2048]{1,0:T(8,128)(2,1)S(1)}, bf16[128,2048]{1,0:T(8,128)(2,1)S(1)}, u32[]{:S(2)}, u32[]{:S(2)}) collective-permute-start(bf16[128,2048]{1,0:T(8,128)(2,1)S(1)} %get-tuple-element.63), channel_id=1, source_target_pairs={{0,1},{1,0},{2,3},{3,2},{4,5},{5,4},{6,7},{7,6},{8,9},{9,8},{10,11... | collective-permute-start | bytes 1572872 | tf_op jit(solution)/shard_map/ppermute | solution.py:121
  119.7 17.6 %collective-permute-start.32 = (bf16[128,2048]{1,0:T(8,128)(2,1)S(1)}, bf16[128,2048]{1,0:T(8,128)(2,1)S(1)}, u32[]{:S(2)}, u32[]{:S(2)}) collective-permute-start(bf16[128,2048]{1,0:T(8,128)(2,1)S(1)} %get-tuple-element.63), channel_id=1, source_target_pairs={{0,4},{4,0},{8,12},{12,8},{1,5},{5,1},{9,13},{13,9},{2,6},{6,2},{1... | collective-permute-start | bytes 1572872 | tf_op jit(solution)/shard_map/ppermute | solution.py:121
  124.4 14.9 %collective-permute-start.28 = (bf16[128,2048]{1,0:T(8,128)(2,1)S(1)}, bf16[128,2048]{1,0:T(8,128)(2,1)S(1)}, u32[]{:S(2)}, u32[]{:S(2)}) collective-permute-start(bf16[128,2048]{1,0:T(8,128)(2,1)S(1)} %get-tuple-element.62.refs_0_), channel_id=1, source_target_pairs={{0,2},{2,0},{1,3},{3,1},{4,6},{6,4},{5,7},{7,5},{8,10},{10,8},{9,1... | collective-permute-start | bytes 1572872 | tf_op jit(solution)/shard_map/ppermute | solution.py:121
  125.0 21.2 %collective-permute-start.37 = (bf16[128,2048]{1,0:T(8,128)(2,1)S(1)}, bf16[128,2048]{1,0:T(8,128)(2,1)S(1)}, u32[]{:S(2)}, u32[]{:S(2)}) collective-permute-start(bf16[128,2048]{1,0:T(8,128)(2,1)S(1)} %collective-permute-done.25), channel_id=1, source_target_pairs={{0,2},{2,0},{1,3},{3,1},{4,6},{6,4},{5,7},{7,5},{8,10},{10,8},{9,1... | collective-permute-start | bytes 1572872 | tf_op jit(solution)/shard_map/ppermute | solution.py:121
  126.4 19.7 %collective-permute-start.38 = (bf16[128,2048]{1,0:T(8,128)(2,1)S(1)}, bf16[128,2048]{1,0:T(8,128)(2,1)S(1)}, u32[]{:S(2)}, u32[]{:S(2)}) collective-permute-start(bf16[128,2048]{1,0:T(8,128)(2,1)S(1)} %collective-permute-done.26), channel_id=1, source_target_pairs={{0,4},{4,0},{8,12},{12,8},{1,5},{5,1},{9,13},{13,9},{2,6},{6,2},{1... | collective-permute-start | bytes 1572872 | tf_op jit(solution)/shard_map/ppermute | solution.py:121
  126.4 20.2 %collective-permute-start.33 = (bf16[128,2048]{1,0:T(8,128)(2,1)S(1)}, bf16[128,2048]{1,0:T(8,128)(2,1)S(1)}, u32[]{:S(2)}, u32[]{:S(2)}) collective-permute-start(bf16[128,2048]{1,0:T(8,128)(2,1)S(1)} %collective-permute-done.25), channel_id=1, source_target_pairs={{0,1},{1,0},{2,3},{3,2},{4,5},{5,4},{6,7},{7,6},{8,9},{9,8},{10,11... | collective-permute-start | bytes 1572872 | tf_op jit(solution)/shard_map/ppermute | solution.py:121
  137.2 9.5 %collective-permute-start.36 = (bf16[128,2048]{1,0:T(8,128)(2,1)S(1)}, bf16[128,2048]{1,0:T(8,128)(2,1)S(1)}, u32[]{:S(2)}, u32[]{:S(2)}) collective-permute-start(bf16[128,2048]{1,0:T(8,128)(2,1)S(1)} %collective-permute-done.26), channel_id=1, source_target_pairs={{0,1},{1,0},{2,3},{3,2},{4,5},{5,4},{6,7},{7,6},{8,9},{9,8},{10,11... | collective-permute-start | bytes 1572872 | tf_op jit(solution)/shard_map/ppermute | solution.py:121
  139.2 10.8 %collective-permute-start.34 = (bf16[128,2048]{1,0:T(8,128)(2,1)S(1)}, bf16[128,2048]{1,0:T(8,128)(2,1)S(1)}, u32[]{:S(2)}, u32[]{:S(2)}) collective-permute-start(bf16[128,2048]{1,0:T(8,128)(2,1)S(1)} %collective-permute-done.32), channel_id=1, source_target_pairs={{0,1},{1,0},{2,3},{3,2},{4,5},{5,4},{6,7},{7,6},{8,9},{9,8},{10,11... | collective-permute-start | bytes 1572872 | tf_op jit(solution)/shard_map/ppermute | solution.py:121
  146.7 18.4 %collective-permute-start.29 = (bf16[128,2048]{1,0:T(8,128)(2,1)S(1)}, bf16[128,2048]{1,0:T(8,128)(2,1)S(1)}, u32[]{:S(2)}, u32[]{:S(2)}) collective-permute-start(bf16[128,2048]{1,0:T(8,128)(2,1)S(1)} %get-tuple-element.63), channel_id=1, source_target_pairs={{0,12},{12,0},{1,13},{13,1},{2,14},{14,2},{3,15},{15,3},{16,28},{2... | collective-permute-start | bytes 1572872 | tf_op jit(solution)/shard_map/ppermute | solution.py:702
  162.1 10.5 %collective-permute-start.42 = (bf16[64,2048]{1,0:T(8,128)(2,1)S(1)}, bf16[64,2048]{1,0:T(8,128)(2,1)}, u32[]{:S(2)}, u32[]{:S(2)}) collective-permute-start(bf16[64,2048]{1,0:T(8,128)(2,1)S(1)} %get-tuple-element.67), channel_id=1, source_target_pairs={{0,12},{4,8},{8,4},{12,0},{1,13},{5,9},{9,5},{13,1},{2,14},{6,10},... | collective-permute-start | bytes 786440 | tf_op jit(solution)/shard_map/ppermute | solution.py:121
  164.6 25.8 %collective-permute-start.45 = (bf16[128,2048]{1,0:T(8,128)(2,1)S(1)}, bf16[128,2048]{1,0:T(8,128)(2,1)S(1)}, u32[]{:S(2)}, u32[]{:S(2)}) collective-permute-start(bf16[128,2048]{1,0:T(8,128)(2,1)S(1)} %get-tuple-element.64.refs_0_), channel_id=1, source_target_pairs={{0,2},{2,0},{1,3},{3,1},{4,6},{6,4},{5,7},{7,5},{8,10},{10,8},{9,1... | collective-permute-start | bytes 1572872 | tf_op jit(solution)/shard_map/ppermute | solution.py:121
  172.5 7.1 %collective-permute-start.48 = (f32[8,128]{1,0:T(8,128)S(1)}, f32[8,128]{1,0:T(8,128)S(1)}, u32[]{:S(2)}, u32[]{:S(2)}) collective-permute-start(f32[8,128]{1,0:T(8,128)S(1)} %add.66), channel_id=1, source_target_pairs={{0,4},{4,0},{8,12},{12,8},{1,5},{5,1},{9,13},{13,9},{2,6},{6,2},{1... | collective-permute-start | bytes 12296 | tf_op jit(solution)/shard_map/ppermute | solution.py:121
  176.7 14.3 %collective-permute-start.41 = (bf16[128,2048]{1,0:T(8,128)(2,1)S(1)}, bf16[128,2048]{1,0:T(8,128)(2,1)S(1)}, u32[]{:S(2)}, u32[]{:S(2)}) collective-permute-start(bf16[128,2048]{1,0:T(8,128)(2,1)S(1)} %broadcast_select_fusion.refs_2_), channel_id=1, source_target_pairs={{0,2},{2,0},{1,3},{3,1},{4,6},{6,4},{5,7},{7,5},{8,10},{10,8},{9,1... | collective-permute-start | bytes 1572872 | tf_op jit(solution)/shard_map/ppermute | solution.py:121
  179.7 9.3 %collective-permute-start.43 = (bf16[64,2048]{1,0:T(8,128)(2,1)S(1)}, bf16[64,2048]{1,0:T(8,128)(2,1)}, u32[]{:S(2)}, u32[]{:S(2)}) collective-permute-start(bf16[64,2048]{1,0:T(8,128)(2,1)S(1)} %get-tuple-element.68), channel_id=1, source_target_pairs={{0,12},{4,8},{8,4},{12,0},{1,13},{5,9},{9,5},{13,1},{2,14},{6,10},... | collective-permute-start | bytes 786440 | tf_op jit(solution)/shard_map/ppermute | solution.py:121
  190.4 9.2 %collective-permute-start.46 = (bf16[64,2048]{1,0:T(8,128)(2,1)}, bf16[64,2048]{1,0:T(8,128)(2,1)}, u32[]{:S(2)}, u32[]{:S(2)}) collective-permute-start(bf16[64,2048]{1,0:T(8,128)(2,1)} %collective-permute-done.42.refs_2_), channel_id=1, source_target_pairs={{0,2},{2,0},{1,3},{3,1},{4,6},{6,4},{5,7},{7,5},{8,10},{10,8},{9,1... | collective-permute-start | bytes 786440 | tf_op jit(solution)/shard_map/ppermute | solution.py:121
  190.9 11.4 %collective-permute-start.44 = (bf16[64,2048]{1,0:T(8,128)(2,1)}, bf16[64,2048]{1,0:T(8,128)(2,1)S(1)}, u32[]{:S(2)}, u32[]{:S(2)}) collective-permute-start(bf16[64,2048]{1,0:T(8,128)(2,1)} %collective-permute-done.43.refs_3_), channel_id=1, source_target_pairs={{0,2},{2,0},{1,3},{3,1},{4,6},{6,4},{5,7},{7,5},{8,10},{10,8},{9,1... | collective-permute-start | bytes 786440 | tf_op jit(solution)/shard_map/ppermute | solution.py:121
  (41 other events, 462.6 us)
